TPU v7x, 32 devices: a whole 2x2x4 slice. The times are simulated.
32 devices in a mesh: dp: 4 (over y, core), seq: 8 (over z, x).
Axes of the slice: x: 2, y: 2, z: 4, core: 2. Of those that a mesh axis runs over, the one named last changes fastest.
Arguments:
- frames_x: bfloat16 [32, 128, 1152], P(('dp', 'seq')), may hold values from -6 to 6
- grad_y: bfloat16 [32, 128, 1152], P(('dp', 'seq')), may hold values from -6 to 6
- clip_ids: int32 [4, 8], P('dp'), may hold values from 0 to 3, never falling along the last dimension, each value on 1 to 4 neighbouring positions
- clip_patches: int32 [4, 4], P('dp'), may hold values from 32 to 128, as said below
- clip_step: int32 [4, 4], P('dp'), may hold values from 0 to 15
- mod_table: float32 [16, 3456], replicated, may hold values from -3 to 3
- w_qkv: bfloat16 [1152, 3456], P('seq'), may hold values from -2 to 2
- w_out: bfloat16 [1152, 1152], P('seq'), may hold values from -0.1875 to 0.1875
Outputs:
- out_y: bfloat16 [32, 128, 1152], P(('dp', 'seq'))
- grad_x: bfloat16 [32, 128, 1152], P(('dp', 'seq'))
- grad_w_out: float32 [1152, 1152], P('seq', 'dp')
Inputs may be any that keep to these rules, and one draw needn't show every extreme that they name: `clip_patches`: in every group some clip uses all 128 patch slots. `clip_ids`: frame slots of a group are numbered by clip and never fall; every clip from 0 to 3 holds 1 to 4 frames, one clip exactly 4.
All inputs are finite; a program needn't handle non-finite values.
Results may differ from a plain program's by a relative error of at most 0.0085.
The roundings to bfloat16 on the way count: a program that leaves them out, or rounds other values in their place, can miss the bound.
Values may be sent and summed in bfloat16 or wider, within the bound.
No kernel may reach another device: no remote copies, remote signals or barrier semaphores. Data moves between devices by JAX's collectives and lax.ppermute only.
A program may use at most 128 MiB of HBM per device.

v0:
```python
import math

import jax
import jax.numpy as jnp
from jax import lax
from jax.sharding import PartitionSpec as P

HEADS = 16


def normalize(inputs):
    values = inputs.astype(jnp.float32)
    centred = values - jnp.mean(values, axis=-1, keepdims=True)
    inv_sigma = lax.rsqrt(jnp.mean(centred * centred, axis=-1, keepdims=True) + 1e-06)
    return (centred * inv_sigma, inv_sigma)


def matmul(left_rows, right_rows):
    return jnp.dot(left_rows, right_rows, preferred_element_type=jnp.float32)


def matmul_t(left_rows, weight):
    return lax.dot_general(
        left_rows, weight, (((1,), (1,)), ((), ())), preferred_element_type=jnp.float32
    )


def flatten(matrix):
    return matrix.reshape(-1, matrix.shape[-1])


def split_heads(triple, num_heads):
    frames_all, columns, three_width = triple.shape
    head_size = three_width // 3 // num_heads
    pieces = triple.reshape(frames_all, columns, 3, num_heads, head_size)
    return (pieces[:, :, 0], pieces[:, :, 1], pieces[:, :, 2], head_size)


def attend_forward(triple, clip_rows, frame_patch, patch_start, num_heads):
    frames_all, columns, three_width = triple.shape
    queries, key_heads, values, head_size = split_heads(triple, num_heads)
    scores = jnp.einsum(
        "fphe,gphe->phfg", queries, key_heads, preferred_element_type=jnp.float32
    ) / math.sqrt(head_size)
    position = patch_start + jnp.arange(columns)
    is_valid = position[None, :] < frame_patch[:, None]
    same_clip = clip_rows[:, None] == clip_rows[None, :]
    diag_mask = jnp.arange(frames_all)[:, None] == jnp.arange(frames_all)[None, :]
    allowed = same_clip[None] & (jnp.transpose(is_valid)[:, None, :] | diag_mask[None])
    scores = jnp.where(allowed[:, None], scores, -jnp.inf)
    largest = jnp.max(scores, axis=-1, keepdims=True)
    exponent = jnp.exp(scores - largest)
    weights = exponent / jnp.sum(exponent, axis=-1, keepdims=True)
    weights_low = weights.astype(jnp.bfloat16)
    output = jnp.einsum("phfg,gphe->fphe", weights_low, values, preferred_element_type=jnp.float32)
    output = output.astype(jnp.bfloat16).reshape(frames_all, columns, three_width // 3)
    return (output, weights, weights_low)


def attend_backward(triple, weights, weights_low, grad_out, num_heads):
    frames_all, columns, three_width = triple.shape
    queries, key_heads, values, head_size = split_heads(triple, num_heads)
    grad_heads = grad_out.reshape(frames_all, columns, num_heads, head_size)
    grad_weights = jnp.einsum(
        "fphe,gphe->phfg", grad_heads, values, preferred_element_type=jnp.float32
    )
    grad_values = jnp.einsum(
        "phfg,fphe->gphe", weights_low, grad_heads, preferred_element_type=jnp.float32
    ).astype(jnp.bfloat16)
    inner = jnp.sum(weights * grad_weights, axis=-1, keepdims=True)
    grad_scores = (weights * (grad_weights - inner) / math.sqrt(head_size)).astype(jnp.bfloat16)
    grad_queries = jnp.einsum(
        "phfg,gphe->fphe", grad_scores, key_heads, preferred_element_type=jnp.float32
    ).astype(jnp.bfloat16)
    grad_keys = jnp.einsum(
        "phfg,fphe->gphe", grad_scores, queries, preferred_element_type=jnp.float32
    ).astype(jnp.bfloat16)
    stacked = jnp.stack([grad_queries, grad_keys, grad_values], axis=2)
    return stacked.reshape(frames_all, columns, three_width)


def local(frames_x, grad_y, clip_ids, clip_patches, clip_step, mod_table, w_qkv, w_out):
    seq_size = lax.axis_size("seq")
    seq_index = lax.axis_index("seq")
    frame_count, patches, model_width = frames_x.shape
    columns = patches // seq_size
    clip_rows = clip_ids[0]
    frames_all = clip_rows.shape[0]
    own_rows = lax.dynamic_slice_in_dim(clip_rows, seq_index * frame_count, frame_count)
    clip_range = jnp.arange(clip_step.shape[1])
    own_hot = (own_rows[:, None] == clip_range[None, :]).astype(jnp.int32)
    all_hot = (clip_rows[:, None] == clip_range[None, :]).astype(jnp.int32)
    own_step = jnp.sum(own_hot * clip_step[0][None, :], axis=1)
    own_patch = jnp.sum(own_hot * clip_patches[0][None, :], axis=1)
    all_patch = jnp.sum(all_hot * clip_patches[0][None, :], axis=1)
    step_hot = (own_step[:, None] == jnp.arange(mod_table.shape[0])[None, :]).astype(jnp.float32)
    modulate = jnp.dot(step_hot, mod_table, precision=lax.Precision.HIGHEST)
    shift_mod = modulate[:, :model_width][:, None, :]
    scale_mod = modulate[:, model_width : 2 * model_width][:, None, :]
    gate_mod = modulate[:, 2 * model_width :][:, None, :]
    normed, inv_sigma = normalize(frames_x)
    hidden = (normed * (1.0 + scale_mod) + shift_mod).astype(jnp.bfloat16)
    w_qkv_full, w_out_full = (
        lax.all_gather(w_qkv, "seq", axis=0, tiled=True),
        lax.all_gather(w_out, "seq", axis=0, tiled=True),
    )
    patch_start = seq_index * columns
    triple = (
        matmul(flatten(hidden), w_qkv_full)
        .astype(jnp.bfloat16)
        .reshape(frame_count, patches, 3 * model_width)
    )
    triple_pos = lax.all_to_all(triple, "seq", split_axis=1, concat_axis=0, tiled=True)
    output_pos, weights, weights_low = attend_forward(
        triple_pos, clip_rows, all_patch, patch_start, HEADS
    )
    attended = lax.all_to_all(output_pos, "seq", split_axis=0, concat_axis=1, tiled=True)
    projected = (
        matmul(flatten(attended), w_out_full)
        .astype(jnp.bfloat16)
        .reshape(frame_count, patches, model_width)
    )
    is_valid = jnp.arange(patches)[None, :] < own_patch[:, None]
    factor = jnp.where(is_valid[:, :, None], gate_mod, jnp.float32(0.0))
    out_y = (frames_x.astype(jnp.float32) + factor * projected.astype(jnp.float32)).astype(
        jnp.bfloat16
    )
    grad_proj = (factor * grad_y.astype(jnp.float32)).astype(jnp.bfloat16)
    grad_attn = (
        matmul_t(flatten(grad_proj), w_out_full)
        .astype(jnp.bfloat16)
        .reshape(frame_count, patches, model_width)
    )
    grad_attn_pos = lax.all_to_all(grad_attn, "seq", split_axis=1, concat_axis=0, tiled=True)
    grad_triple_pos = attend_backward(triple_pos, weights, weights_low, grad_attn_pos, HEADS)
    grad_triple = lax.all_to_all(grad_triple_pos, "seq", split_axis=0, concat_axis=1, tiled=True)
    grad_hidden = (
        matmul_t(flatten(grad_triple), w_qkv_full)
        .astype(jnp.bfloat16)
        .reshape(frame_count, patches, model_width)
    )
    left_rows = flatten(attended)
    right_rows = flatten(grad_proj)
    grad_norm = grad_hidden.astype(jnp.float32) * (1.0 + scale_mod)
    first_mean = jnp.mean(grad_norm, axis=-1, keepdims=True)
    second_mean = jnp.mean(grad_norm * normed, axis=-1, keepdims=True)
    grad_x = grad_y.astype(jnp.float32) + inv_sigma * (
        grad_norm - first_mean - normed * second_mean
    )
    full_term = lax.dot_general(
        left_rows, right_rows, (((0,), (0,)), ((), ())), preferred_element_type=jnp.float32
    )
    column_part = lax.psum_scatter(full_term, "dp", scatter_dimension=1, tiled=True)
    grad_w = lax.psum_scatter(column_part, "seq", scatter_dimension=0, tiled=True)
    grad_scale = 1.0 / math.sqrt(lax.axis_size("dp") * frames_all * patches)
    grad_w_out = grad_w * jnp.float32(grad_scale)
    return (out_y, grad_x.astype(jnp.bfloat16), grad_w_out)


def solution(mesh):
    return jax.shard_map(
        local,
        mesh=mesh,
        in_specs=(
            P(("dp", "seq"), None, None),
            P(("dp", "seq"), None, None),
            P("dp", None),
            P("dp", None),
            P("dp", None),
            P(),
            P("seq", None),
            P("seq", None),
        ),
        out_specs=(P(("dp", "seq"), None, None), P(("dp", "seq"), None, None), P("seq", "dp")),
        check_vma=False,
    )
```

profile of v0, /device:TPU:4, one launch (start us, length us, event | category | flops | bytes accessed | tf_op | source)
XLA Modules:
  0.0 344.4 jit_solution(4347991252997346110)
XLA Ops:
  7.2 0.0 all-gather.3.cloned.1.call-start
  7.2 0.7 all-gather.3.cloned.1.call-update
  7.9 0.0 all-gather.5.cloned.1.call-start
  8.0 0.7 all-gather.5.cloned.1.call-update
  8.7 1.1 convert_reduce_fusion
  9.8 1.2 constant_dynamic-slice_fusion
  11.0 1.9 fusion.60
  12.9 0.8 fusion.56
  13.8 1.2 fusion.33
  15.0 116.0 %all-gather.3.cloned.1.call-done = bf16[1152,3456]{1,0:T(8,128)(2,1)} async-done(((bf16[144,3456]{1,0:T(8,128)(2,1)}), bf16[1152,3456]{1,0:T(8,128)(2,1)}) %all-gather.3.cloned.1.call-update) | async-done | bytes 7962640 | tf_op jit(solution)/shard_map/all_gather | solution.py:104
  131.0 4.8 %fusion.2 = bf16[1,128,3456]{2,1,0:T(8,128)(2,1)S(1)} fusion(bf16[1152,3456]{1,0:T(8,128)(2,1)} %all-gather.3.cloned.1.call-done, bf16[1,128,1152]{2,1,0:T(8,128)(2,1)} %param.8, f32[1152]{0:T(1024)S(1)} %get-tuple-element.20, f32[1152]{0:T(1024)S(1)} %get-tuple-element.19, f32[128]{0:T(128)S(1)} %add_rsqrt_fusion, f32[128]{0:T(128)S(1)} %broadcast_multiply_fusion.3), kind=kOutput, calls=%fused_computation.3 | convolution fusion | flops 1020542976 | bytes 9152512 | tf_op jit(solution)/shard_map/dot_general | solution.py:19
  135.8 1.4 copy.86
  137.2 0.5 broadcast.215
  137.8 6.2 %reduce.17 = bf16[128,3456]{1,0:T(8,128)(2,1)S(1)} reduce(bf16[128,1,3456]{2,1,0:T(2,128)(2,1)S(1)} %bitcast.82, bf16[]{:T(256)} %broadcast.215), dimensions={1}, to_apply=%bitcast.80.reduce_sub_computation | reduce | bytes 1769474
  144.0 1.3 reshape.296
  145.3 3.7 %all-to-all-start = ((bf16[8,2,27648]{2,1,0:T(2,128)(2,1)}), bf16[8,2,27648]{2,1,0:T(2,128)(2,1)S(1)}, u32[]{:S(2)}, u32[]{:S(2)}) async-start(bf16[8,2,27648]{2,1,0:T(2,128)(2,1)} %reshape.296), calls=%async_computation | async-start | bytes 1769472 | tf_op jit(solution)/shard_map/all_to_all | solution.py:113
  149.0 0.1 select_reduce_fusion
  149.1 0.1 iota_compare_fusion
  149.2 0.1 broadcast_compare_fusion
  149.3 0.1 or_and_fusion
  149.4 35.5 %all-to-all-done = bf16[8,2,27648]{2,1,0:T(2,128)(2,1)S(1)} async-done(((bf16[8,2,27648]{2,1,0:T(2,128)(2,1)}), bf16[8,2,27648]{2,1,0:T(2,128)(2,1)S(1)}, u32[]{:S(2)}, u32[]{:S(2)}) %all-to-all-start) | async-done | bytes 884768 | tf_op jit(solution)/shard_map/all_to_all | solution.py:113
  184.9 0.8 reshape.297
  185.7 5.1 %bitcast_reduce_fusion = bf16[128,3456]{1,0:T(8,128)(2,1)S(1)} fusion(bf16[128,1,3456]{2,1,0:T(2,128)(2,1)S(1)} %reshape.297), kind=kLoop, calls=%fused_computation.102 | loop fusion | bytes 1769472 | tf_op jit(solution)/shard_map/all_to_all | solution.py:113
  190.7 2.8 reshape.278
  193.6 0.4 fusion.69
  194.0 2.1 fusion.70
  196.2 1.9 fusion.18
  198.1 0.1 copy.53
  198.2 1.2 reshape.279
  199.4 3.4 all-to-all-start.1
  202.8 0.3 reduce-scatter.5.cloned.1.call-start
  203.1 1.3 fusion.59
  204.4 0.6 iota_compare_fusion.2
  205.0 6.8 %all-to-all-done.1 = bf16[8,16,1152]{2,1,0:T(8,128)(2,1)S(1)} async-done(((bf16[8,16,1152]{2,1,0:T(8,128)(2,1)}), bf16[8,16,1152]{2,1,0:T(8,128)(2,1)S(1)}, u32[]{:S(2)}, u32[]{:S(2)}) %all-to-all-start.1) | async-done | bytes 294944 | tf_op jit(solution)/shard_map/all_to_all | solution.py:117
  211.8 3.3 fusion.52
  215.1 0.0 reduce-scatter.5.cloned.1.call-update
  215.1 0.0 all-gather.5.cloned.1.call-done
  215.2 2.7 fusion.10
  217.9 0.5 copy.87
  218.3 2.4 reduce.18
  220.8 0.1 reshape.298
  220.8 13.2 %all_to_all.16 = bf16[8,2,9216]{2,1,0:T(2,128)(2,1)S(1)} all-to-all(bf16[8,2,9216]{2,1,0:T(2,128)(2,1)S(1)} %reshape.298), channel_id=1, replica_groups=mesh['dp'=4,'seq'=8] {'seq'}, dimensions={0} | all-to-all | bytes 589824 | tf_op jit(solution)/shard_map/all_to_all | solution.py:134
  234.1 0.2 reshape.299
  234.3 1.7 bitcast_reduce_fusion.1
  236.0 0.9 reshape.283
  237.0 0.7 fusion.40
  237.7 3.5 %fusion.20 = bf16[8,16,1,16,72]{4,0,3,1,2:T(8,128)(2,1)} fusion(f32[16,16,8,8]{2,3,1,0:T(8,128)S(1)} %fusion.40, bf16[8,16,1,16,72]{4,3,2,1,0:T(8,128)(2,1)S(1)} %copy-done.8, f32[16,16,8,8]{2,3,1,0:T(8,128)} %get-tuple-element.25, f32[16,16,8]{2,1,0:T(8,128)} %copy-done.12), kind=kOutput, calls=%fused_computation.30 | convolution fusion | flops 2623495 | bytes 729088 | tf_op jit(solution)/shard_map/phfg,fphe->gphe/dot_general | solution.py:75
  241.1 2.7 fusion.19
  243.8 1.9 fusion.21
  245.7 0.4 pad_maximum_fusion
  246.1 0.2 copy.58
  246.3 2.6 reshape.284
  248.9 4.2 %all-to-all-start.3 = ((bf16[8,16,3456]{2,1,0:T(8,128)(2,1)}), bf16[8,16,3456]{2,1,0:T(8,128)(2,1)}, u32[]{:S(2)}, u32[]{:S(2)}) async-start(bf16[8,16,3456]{2,1,0:T(8,128)(2,1)} %reshape.284), calls=%async_computation.3 | async-start | bytes 1769472 | tf_op jit(solution)/shard_map/all_to_all | solution.py:136
  253.2 0.3 reduce-scatter.7.cloned.1.call-start
  253.5 11.5 %reduce-scatter.5.cloned.1.call-done = f32[1152,288]{0,1:T(8,128)} async-done(((f32[1152,1152]{0,1:T(8,128)}), f32[1152,288]{0,1:T(8,128)}) %reduce-scatter.5.cloned.1.call-update) | async-done | bytes 1327120 | tf_op jit(solution)/shard_map/reduce_scatter | solution.py:153
  265.0 3.1 copy.62
  268.2 1.3 fusion.9
  269.5 4.8 %all-to-all-done.3 = bf16[8,16,3456]{2,1,0:T(8,128)(2,1)} async-done(((bf16[8,16,3456]{2,1,0:T(8,128)(2,1)}), bf16[8,16,3456]{2,1,0:T(8,128)(2,1)}, u32[]{:S(2)}, u32[]{:S(2)}) %all-to-all-start.3) | async-done | bytes 884768 | tf_op jit(solution)/shard_map/all_to_all | solution.py:136
  274.3 6.3 %fusion.30 = (f32[128]{0:T(128)S(1)}, f32[128,1152]{1,0:T(8,128)S(1)}) fusion(bf16[1,128,1152]{2,1,0:T(8,128)(2,1)S(1)} %copy-done.1, f32[128]{0:T(128)S(1)} %add_rsqrt_fusion, f32[128]{0:T(128)S(1)} %broadcast_multiply_fusion.3, f32[1152]{0:T(1024)S(1)} %get-tuple-element.19, bf16[128,3456]{1,0:T(8,128)(2,1)} %bitcast.20, ...), kind=kOutput, calls=%fused_computation.45 | convolution fusion | flops 1020395392 | bytes 9738240 | tf_op jit(solution)/shard_map/dot_general | solution.py:23
  280.6 0.1 reduce_sum.88
  280.8 1.0 fusion.35
  281.8 54.2 %reduce-scatter.7.cloned.1.call-done = f32[144,288]{1,0:T(8,128)} async-done(((f32[1152,288]{1,0:T(8,128)}), f32[144,288]{1,0:T(8,128)}) %reduce-scatter.7.cloned.1.call-update) | async-done | bytes 165904
  335.9 1.1 copy.63
  337.0 0.8 copy.59
  (36 shorter events, 0.2 us)
Async XLA Ops:
  7.2 5.8 %copy-start = (f32[16,3456]{1,0:T(8,128)S(1)}, f32[16,3456]{1,0:T(8,128)}, u32[]{:S(2)}) copy-start(f32[16,3456]{1,0:T(8,128)} %param.13) | copy-start | bytes 663556
  7.2 123.9 %all-gather.3.cloned.1.call-start = ((), (), s32[]{:S(2)}) async-start(), calls=%async_computation.6 | async-start | bytes 8957952 | tf_op jit(solution)/shard_map/all_gather | solution.py:104
  7.9 207.2 %all-gather.5.cloned.1.call-start = ((), (), s32[]{:S(2)}) async-start(), calls=%async_computation.7 | async-start | bytes 2985984 | tf_op jit(solution)/shard_map/all_gather | solution.py:105
  137.8 11.2 %copy-start.10 = (s32[1,8]{1,0:T(1,128)S(1)}, s32[1,8]{1,0:T(1,128)}, u32[]{:S(2)}) copy-start(s32[1,8]{1,0:T(1,128)} %param.10) | copy-start | bytes 100
  137.8 11.3 %copy-start.11 = (s32[1,4]{1,0:T(1,128)S(1)}, s32[1,4]{1,0:T(1,128)}, u32[]{:S(2)}) copy-start(s32[1,4]{1,0:T(1,128)} %param.11) | copy-start | bytes 52
  145.3 39.6 %all-to-all-start = ((bf16[8,2,27648]{2,1,0:T(2,128)(2,1)}), bf16[8,2,27648]{2,1,0:T(2,128)(2,1)S(1)}, u32[]{:S(2)}, u32[]{:S(2)}) async-start(bf16[8,2,27648]{2,1,0:T(2,128)(2,1)} %reshape.296), calls=%async_computation | async-start | bytes 1769472 | tf_op jit(solution)/shard_map/all_to_all | solution.py:113
  194.0 4.1 %copy-start.5 = (bf16[8,16,1,16,72]{4,3,2,1,0:T(8,128)(2,1)}, bf16[8,16,1,16,72]{4,3,2,1,0:T(8,128)(2,1)S(1)}, u32[]{:S(2)}) copy-start(bf16[8,16,1,16,72]{4,3,2,1,0:T(8,128)(2,1)S(1)} %get-tuple-element.21) | copy-start | bytes 884740
  194.0 4.1 %copy-start.7 = (bf16[8,16,1,16,72]{4,3,2,1,0:T(8,128)(2,1)}, bf16[8,16,1,16,72]{4,3,2,1,0:T(8,128)(2,1)S(1)}, u32[]{:S(2)}) copy-start(bf16[8,16,1,16,72]{4,3,2,1,0:T(8,128)(2,1)S(1)} %get-tuple-element.22) | copy-start | bytes 884740
  196.2 2.0 copy-start.12
  196.2 15.6 %copy-start.3 = (bf16[1,128,1152]{2,1,0:T(8,128)(2,1)S(1)}, bf16[1,128,1152]{2,1,0:T(8,128)(2,1)}, u32[]{:S(2)}) copy-start(bf16[1,128,1152]{2,1,0:T(8,128)(2,1)} %param.9) | copy-start | bytes 884740
  199.4 12.4 %all-to-all-start.1 = ((bf16[8,16,1152]{2,1,0:T(8,128)(2,1)}), bf16[8,16,1152]{2,1,0:T(8,128)(2,1)S(1)}, u32[]{:S(2)}, u32[]{:S(2)}) async-start(bf16[8,16,1152]{2,1,0:T(8,128)(2,1)} %reshape.279), calls=%async_computation.1 | async-start | bytes 589824 | tf_op jit(solution)/shard_map/all_to_all | solution.py:117
  202.8 62.2 %reduce-scatter.5.cloned.1.call-start = ((), (), s32[]{:S(2)}) async-start(), calls=%async_computation.8 | async-start | bytes 6635520 | tf_op jit(solution)/shard_map/reduce_scatter | solution.py:153
  234.1 3.6 %copy-start.8 = (bf16[8,16,1,16,72]{4,3,2,1,0:T(8,128)(2,1)S(1)}, bf16[8,16,1,16,72]{4,3,2,1,0:T(8,128)(2,1)}, u32[]{:S(2)}) copy-start(bf16[8,16,1,16,72]{4,3,2,1,0:T(8,128)(2,1)} %copy-done.7) | copy-start | bytes 884740
  237.6 3.5 %copy-start.6 = (bf16[8,16,1,16,72]{4,3,2,1,0:T(8,128)(2,1)S(1)}, bf16[8,16,1,16,72]{4,3,2,1,0:T(8,128)(2,1)}, u32[]{:S(2)}) copy-start(bf16[8,16,1,16,72]{4,3,2,1,0:T(8,128)(2,1)} %copy-done.5) | copy-start | bytes 884740
  241.1 2.7 copy-start.13
  243.8 1.9 copy-start.9
  248.9 25.4 %all-to-all-start.3 = ((bf16[8,16,3456]{2,1,0:T(8,128)(2,1)}), bf16[8,16,3456]{2,1,0:T(8,128)(2,1)}, u32[]{:S(2)}, u32[]{:S(2)}) async-start(bf16[8,16,3456]{2,1,0:T(8,128)(2,1)} %reshape.284), calls=%async_computation.3 | async-start | bytes 1769472 | tf_op jit(solution)/shard_map/all_to_all | solution.py:136
  253.1 15.0 %copy-start.1 = (bf16[1,128,1152]{2,1,0:T(8,128)(2,1)S(1)}, bf16[1,128,1152]{2,1,0:T(8,128)(2,1)}, u32[]{:S(2)}) copy-start(bf16[1,128,1152]{2,1,0:T(8,128)(2,1)} %param.8) | copy-start | bytes 884740
  253.2 15.0 %copy-start.2 = (bf16[1152,1152]{1,0:T(8,128)(2,1)S(1)}, bf16[1152,1152]{1,0:T(8,128)(2,1)}, u32[]{:S(2)}) copy-start(bf16[1152,1152]{1,0:T(8,128)(2,1)} %all-gather.5.cloned.1.call-done) | copy-start | bytes 7962628
  253.2 82.8 %reduce-scatter.7.cloned.1.call-start = ((), (), s32[]{:S(2)}) async-start(), calls=%async_computation.9 | async-start | bytes 1990656
  274.3 6.5 %copy-start.4 = (bf16[1,128,1152]{2,1,0:T(8,128)(2,1)S(1)}, bf16[1,128,1152]{2,1,0:T(8,128)(2,1)}, u32[]{:S(2)}) copy-start(bf16[1,128,1152]{2,1,0:T(8,128)(2,1)} %param.9) | copy-start | bytes 884740
Sparse Core Ops, SparseCore 0:
  10.2 120.7 all-gather.2
  133.2 62.1 all-gather.4
  215.2 49.6 reduce-scatter.4
  268.7 67.1 reduce-scatter.6
where the time goes:
time: 347 us; the launch traced here: 344 us
  waiting for transfers between devices  230 us (66%)
  matrix products  32 us (9%)
  local copies, waits for them, and re-layouts  26.1 us (8%)
  other arithmetic  16.7 us (5%)
  between operations  14.2 us (4%)
  blocking collectives  13.2 us (4%)
  starting transfers between devices  12 us (3%)
    all_gather x1, waiting for transfers between devices, local(): lax.all_gather(w_qkv, 'seq', axis=0, tiled=True)  116 us
    unnamed x5, waiting for transfers between devices  55.6 us
    all_to_all x1, waiting for transfers between devices, local(): lax.all_to_all(triple, 'seq', split_axis=1, concat_axis=0, tiled=True)  35.5 us
    all_to_all x1, blocking collectives, local(): lax.all_to_all(grad_attn, 'seq', split_axis=1, concat_axis=0, tiled=True)  13.2 us
    reduce_scatter x1, waiting for transfers between devices, local(): lax.psum_scatter(full_term, 'dp', scatter_dimension=1, tiled=True)  11.5 us
    dot_general x2, matrix products, matmul_t(): lax.dot_general(left_rows, weight, (((1,), (1,)), ((), ())), preferred_el...  8.99 us
    unnamed x2, other arithmetic  8.67 us
    unnamed x36, local copies, waits for them, and re-layouts  7.97 us
  transfers between devices with their start and end apart: 7, of which 6 were waited for; matrix products, arithmetic and copies ran while one was open for 21% of the time, Pallas kernels for 0%

commit v1 on v0

v1 whole, which is shorter than its diff:
```python
import functools
import math

import jax
import jax.numpy as jnp
from jax import lax
from jax.experimental import pallas as pl
from jax.experimental.pallas import tpu as pltpu
from jax.sharding import Mesh, PartitionSpec as P

HEADS = 16
CORES = 2
AXES = ("y", "c", "z", "x")
BLOCK = 16
VMEM_LIMIT = 56 * 1024 * 1024
BF16 = jnp.bfloat16
F32 = jnp.float32


def dot(left, right):
    return jnp.dot(left, right, preferred_element_type=F32)


def dot_t(left, right):
    return lax.dot_general(left, right, (((1,), (1,)), ((), ())), preferred_element_type=F32)


def t_dot(left, right):
    return lax.dot_general(left, right, (((0,), (0,)), ((), ())), preferred_element_type=F32)


def normalize(values):
    centred = values - jnp.mean(values, axis=-1, keepdims=True)
    inv_sigma = lax.rsqrt(jnp.mean(centred * centred, axis=-1, keepdims=True) + 1e-06)
    return centred * inv_sigma, inv_sigma


class Layout:
    def __init__(self, mesh):
        groups, seq = mesh.shape["dp"], mesh.shape["seq"]
        self.nc = CORES
        self.ny = groups // CORES
        self.nz = groups
        self.nx = seq // self.nz
        self.chips = self.ny * self.nx
        self.frames = seq

    def linear(self, y, c, z, x):
        return ((y * self.nc + c) * self.nz + z) * self.nx + x

    def perm(self, move):
        pairs = []
        for y in range(self.ny):
            for c in range(self.nc):
                for z in range(self.nz):
                    for x in range(self.nx):
                        pairs.append((self.linear(y, c, z, x), self.linear(*move(y, c, z, x))))
        return pairs

    def to_plane(self, k):
        return self.perm(lambda y, c, z, x: (z % self.ny, (z // self.ny) ^ k, c * self.ny + y, x))

    def from_plane(self, k):
        return [(target, source) for source, target in self.to_plane(k)]

    def swap(self, ky=0, kc=0, kz=0, kx=0):
        return self.perm(lambda y, c, z, x: (y ^ ky, c ^ kc, z ^ kz, x ^ kx))

    def chip_of(self, k):
        return k // self.nx, k % self.nx

    def slots(self):
        return [(k, j) for k in range(self.chips) for j in range(self.nc)]


def slot_scalars(lay, pos_ref, info_ref, slot):
    k, j = slot
    ky, kx = lay.chip_of(k)
    z_frame = (pos_ref[1] ^ j) * lay.ny + (pos_ref[0] ^ ky)
    frame = z_frame * lay.nx + (pos_ref[3] ^ kx)
    clip = info_ref[frame]
    clips = (info_ref.shape[0] - lay.frames) // 2
    return clip, info_ref[lay.frames + clip], info_ref[lay.frames + clips + clip]


def table_row(mod_ref, step, part, width):
    return mod_ref[pl.ds(step, 1), part * width : (part + 1) * width]


def allowed_pairs(lay, pos_ref, info_ref, patch_base):
    rows = lay.frames * BLOCK
    row_slot = lax.broadcasted_iota(jnp.int32, (rows, 1), 0) // BLOCK
    col_slot = lax.broadcasted_iota(jnp.int32, (1, rows), 1) // BLOCK
    row_clip = jnp.zeros((rows, 1), jnp.int32)
    col_clip = jnp.zeros((1, rows), jnp.int32)
    col_limit = jnp.zeros((1, rows), jnp.int32)
    for t, slot in enumerate(lay.slots()):
        clip, limit, _ = slot_scalars(lay, pos_ref, info_ref, slot)
        row_clip = jnp.where(row_slot == t, clip, row_clip)
        col_clip = jnp.where(col_slot == t, clip, col_clip)
        col_limit = jnp.where(col_slot == t, limit, col_limit)
    row_patch = lax.broadcasted_iota(jnp.int32, (rows, 1), 0) % BLOCK
    col_patch = lax.broadcasted_iota(jnp.int32, (1, rows), 1) % BLOCK
    row_key = row_clip * BLOCK + row_patch
    col_key = col_clip * BLOCK + col_patch
    col_valid = (patch_base + col_patch < col_limit).astype(jnp.int32)
    row_index = lax.broadcasted_iota(jnp.int32, (rows, rows), 0)
    col_index = lax.broadcasted_iota(jnp.int32, (rows, rows), 1)
    return (row_key == col_key) & ((col_valid > 0) | (row_index == col_index))


def head_mask(values, head, head_size):
    lane = lax.broadcasted_iota(jnp.int32, (1, values.shape[1]), 1)
    inside = (lane >= head * head_size) & (lane < (head + 1) * head_size)
    return jnp.where(inside, values, jnp.zeros_like(values))


def softmax(scores, allowed):
    scores = jnp.where(allowed, scores, -jnp.inf)
    exponent = jnp.exp(scores - jnp.max(scores, axis=-1, keepdims=True))
    return exponent / jnp.sum(exponent, axis=-1, keepdims=True)


def fill_weights(lay, pos_ref, w_refs, w_scr):
    halves = w_scr.shape[0]
    rows = w_refs[0].shape[0]
    for h in range(halves):
        half = (pos_ref[1] ^ h) if halves > 1 else 0
        for k in range(lay.nz):
            start = pl.multiple_of((pos_ref[2] ^ k) * rows, 16)
            w_scr[half, pl.ds(start, rows), :] = w_refs[h * lay.nz + k][...]


def forward_kernel(lay, halves, half_heads, pos_ref, info_ref, *refs):
    x_refs, refs = refs[: lay.frames], refs[lay.frames :]
    w_refs, refs = refs[: halves * lay.nz], refs[halves * lay.nz :]
    mod_ref, q_ref, k_ref, v_ref, *refs = refs
    att_refs, (w_scr, hid_scr) = refs[: lay.chips], refs[lay.chips :]
    width = hid_scr.shape[1]
    cols = w_scr.shape[2] // 3
    head_size = cols // half_heads
    patches = q_ref.shape[2] * pl.num_programs(0)

    @pl.when(pl.program_id(0) == 0)
    def _():
        fill_weights(lay, pos_ref, w_refs, w_scr)

    for t, slot in enumerate(lay.slots()):
        _, _, step = slot_scalars(lay, pos_ref, info_ref, slot)
        normed, _ = normalize(x_refs[t][...].astype(F32))
        shift, scale = table_row(mod_ref, step, 0, width), table_row(mod_ref, step, 1, width)
        hid_scr[t * BLOCK : (t + 1) * BLOCK, :] = (normed * (1.0 + scale) + shift).astype(BF16)

    patch_base = pos_ref[1] * patches + pl.program_id(0) * BLOCK
    allowed = allowed_pairs(lay, pos_ref, info_ref, patch_base)
    outputs = []
    for h in range(halves):
        triple = dot(hid_scr[...], w_scr[h])
        queries = triple[:, :cols].astype(BF16)
        keys = triple[:, cols : 2 * cols].astype(BF16)
        values = triple[:, 2 * cols :].astype(BF16)
        q_ref[h] = queries.reshape(q_ref.shape[1:])
        k_ref[h] = keys.reshape(k_ref.shape[1:])
        v_ref[h] = values.reshape(v_ref.shape[1:])
        output = jnp.zeros(queries.shape, F32)
        for head in range(half_heads):
            scores = dot_t(head_mask(queries, head, head_size), keys) * (1.0 / math.sqrt(head_size))
            weights = softmax(scores, allowed).astype(BF16)
            output = output + dot(weights, head_mask(values, head, head_size))
        outputs.append(output)
    attended = jnp.concatenate(outputs, axis=1) if halves > 1 else outputs[0]
    attended = attended.astype(BF16).reshape(lay.frames, BLOCK, attended.shape[1])
    for k in range(lay.chips):
        att_refs[k][...] = attended[k * lay.nc : (k + 1) * lay.nc]


def backward_kernel(lay, halves, half_heads, pos_ref, info_ref, *refs):
    g_refs, refs = refs[: lay.frames], refs[lay.frames :]
    w_refs, refs = refs[: halves * lay.nz], refs[halves * lay.nz :]
    mod_ref, wo_ref, q_ref, k_ref, v_ref, *refs = refs
    att_refs, refs = refs[: lay.chips], refs[lay.chips :]
    gh_refs, refs = refs[: lay.chips], refs[lay.chips :]
    gw_ref, w_scr, gp_scr, acc_scr = refs
    width = gp_scr.shape[1]
    cols = w_scr.shape[2] // 3
    head_size = cols // half_heads
    patches = q_ref.shape[2] * pl.num_programs(0)
    rows = gp_scr.shape[0]

    @pl.when(pl.program_id(0) == 0)
    def _():
        fill_weights(lay, pos_ref, w_refs, w_scr)
        acc_scr[...] = jnp.zeros_like(acc_scr)

    patch_base = pos_ref[1] * patches + pl.program_id(0) * BLOCK
    patch = patch_base + lax.broadcasted_iota(jnp.int32, (BLOCK, 1), 0)
    for t, slot in enumerate(lay.slots()):
        _, limit, step = slot_scalars(lay, pos_ref, info_ref, slot)
        factor = jnp.where(patch < limit, table_row(mod_ref, step, 2, width), 0.0)
        grad_proj = factor * g_refs[t][...].astype(F32)
        gp_scr[t * BLOCK : (t + 1) * BLOCK, :] = grad_proj.astype(BF16)

    attended = jnp.concatenate([ref[...] for ref in att_refs], axis=0).reshape(rows, -1)
    acc_scr[...] += t_dot(attended, gp_scr[...])
    grad_attn = dot_t(gp_scr[...], wo_ref[0])

    allowed = allowed_pairs(lay, pos_ref, info_ref, patch_base)
    scaling = 1.0 / math.sqrt(head_size)
    total = jnp.zeros((rows, width), F32)
    for h in range(halves):
        queries = q_ref[h].reshape(rows, cols)
        keys = k_ref[h].reshape(rows, cols)
        values = v_ref[h].reshape(rows, cols)
        grad_out = grad_attn[:, h * cols : (h + 1) * cols].astype(BF16)
        grad_queries = jnp.zeros((rows, cols), F32)
        grad_keys = jnp.zeros((rows, cols), F32)
        grad_values = jnp.zeros((rows, cols), F32)
        for head in range(half_heads):
            q_head = head_mask(queries, head, head_size)
            g_head = head_mask(grad_out, head, head_size)
            weights = softmax(dot_t(q_head, keys) * scaling, allowed)
            grad_weights = dot_t(g_head, values)
            grad_values = grad_values + t_dot(weights.astype(BF16), g_head)
            inner = jnp.sum(weights * grad_weights, axis=-1, keepdims=True)
            grad_scores = (weights * (grad_weights - inner) * scaling).astype(BF16)
            grad_queries = grad_queries + dot(grad_scores, head_mask(keys, head, head_size))
            grad_keys = grad_keys + t_dot(grad_scores, q_head)
        grad_triple = jnp.concatenate([grad_queries, grad_keys, grad_values], axis=1).astype(BF16)
        total = total + dot_t(grad_triple, w_scr[h])
    total = total.reshape(lay.frames, BLOCK, width)
    for k in range(lay.chips):
        gh_refs[k][...] = total[k * lay.nc : (k + 1) * lay.nc].astype(gh_refs[k].dtype)

    @pl.when(pl.program_id(0) == pl.num_programs(0) - 1)
    def _():
        part = gw_ref.shape[2]
        for d in range(gw_ref.shape[0]):
            gw_ref[d] = acc_scr[:, d * part : (d + 1) * part]


def output_kernel(lay, pos_ref, info_ref, *refs):
    x_refs, refs = refs[: lay.nc], refs[lay.nc :]
    att_refs, refs = refs[: lay.chips], refs[lay.chips :]
    wo_ref, mod_ref, *out_refs = refs
    _, patches, width = att_refs[0].shape
    own_chip = pos_ref[0] * lay.nx + pos_ref[3]
    model = x_refs[0].shape[1]
    total = jnp.zeros((lay.nc * patches, model), F32)
    for k in range(lay.chips):
        total = total + dot(att_refs[k][...].reshape(lay.nc * patches, width), wo_ref[own_chip ^ k])
    patch = pos_ref[1] * patches + lax.broadcasted_iota(jnp.int32, (patches, 1), 0)
    for j in range(lay.nc):
        _, limit, step = slot_scalars(lay, pos_ref, info_ref, (0, j))
        factor = jnp.where(patch < limit, table_row(mod_ref, step, 2, model), 0.0)
        projected = total[j * patches : (j + 1) * patches].astype(BF16).astype(F32)
        out_refs[j][...] = (x_refs[j][...].astype(F32) + factor * projected).astype(BF16)


def input_grad_kernel(lay, pos_ref, info_ref, *refs):
    x_refs, refs = refs[: lay.nc], refs[lay.nc :]
    g_refs, refs = refs[: lay.nc], refs[lay.nc :]
    gh_refs, refs = refs[: lay.chips], refs[lay.chips :]
    mod_ref, *out_refs = refs
    model = x_refs[0].shape[1]
    for j in range(lay.nc):
        _, _, step = slot_scalars(lay, pos_ref, info_ref, (0, j))
        grad_hidden = gh_refs[0][j]
        for k in range(1, lay.chips):
            grad_hidden = grad_hidden + gh_refs[k][j].astype(F32)
        grad_hidden = grad_hidden.astype(BF16).astype(F32)
        normed, inv_sigma = normalize(x_refs[j][...].astype(F32))
        grad_norm = grad_hidden * (1.0 + table_row(mod_ref, step, 1, model))
        first_mean = jnp.mean(grad_norm, axis=-1, keepdims=True)
        second_mean = jnp.mean(grad_norm * normed, axis=-1, keepdims=True)
        grad_x = g_refs[j][...].astype(F32) + inv_sigma * (
            grad_norm - first_mean - normed * second_mean
        )
        out_refs[j][...] = grad_x.astype(BF16)


def whole_spec(shape):
    return pl.BlockSpec(shape, lambda *_: (0,) * len(shape))


def params():
    return pltpu.CompilerParams(vmem_limit_bytes=VMEM_LIMIT)


def struct(shape, dtype=BF16):
    return jax.ShapeDtypeStruct(shape, dtype)


def pieces_of(lay, own, indices, axis_swap, count):
    return [own] + [lax.ppermute(own, AXES, axis_swap(k)) for k in range(1, count)]


def local(lay, frames_x, grad_y, clip_ids, clip_patches, clip_step, mod_table, w_qkv, w_out):
    y, c, z, x = (lax.axis_index(name) for name in AXES)
    _, patches, model = frames_x.shape
    half = patches // lay.nc
    chips, nc, nx, ny, nz = lay.chips, lay.nc, lay.nx, lay.ny, lay.nz
    chip_heads = HEADS // chips
    head_size = model // HEADS
    halves = 2 if chip_heads % 2 == 0 else 1
    half_heads = chip_heads // halves
    cols = half_heads * head_size
    chip_width = chip_heads * head_size
    rows = w_qkv.shape[0]
    blocks = half // BLOCK

    def to_plane(frame):
        own_half = z // ny
        return [
            lax.ppermute(
                lax.dynamic_slice_in_dim(frame[0], (own_half ^ k) * half, half),
                AXES,
                lay.to_plane(k),
            )
            for k in range(nc)
        ]

    def from_plane(parts):
        own_half = z // ny
        got = [lax.ppermute(part, AXES, lay.from_plane(k)) for k, part in enumerate(parts)]
        first = jnp.where(own_half == 0, got[0], got[1])
        second = jnp.where(own_half == 0, got[1], got[0])
        return jnp.concatenate([first, second], axis=0)[None]

    def chip_swap(k):
        ky, kx = lay.chip_of(k)
        return lay.swap(ky=ky, kx=kx)

    def over_chips(parts):
        return list(parts) + [
            lax.ppermute(part, AXES, chip_swap(k)) for k in range(1, chips) for part in parts
        ]

    info = jnp.concatenate([clip_ids[0], clip_patches[0], clip_step[0]])[None]
    info = lax.ppermute(info, AXES, lay.to_plane(0))[0]
    pos = jnp.stack([y, c, z, x]).astype(jnp.int32)
    x_own = to_plane(frames_x)
    x_all = over_chips(x_own)

    split = w_qkv.reshape(rows, 3, chips, halves, cols)
    mine = c if halves > 1 else 0

    def columns_of(chip):
        part = lax.dynamic_index_in_dim(split, chip, axis=2, keepdims=False)
        return lax.dynamic_index_in_dim(part, mine, axis=2, keepdims=False).reshape(rows, 3 * cols)

    by_x = [columns_of(y * nx + x)] + [
        lax.ppermute(columns_of(y * nx + (x ^ kx)), AXES, lay.swap(kx=kx)) for kx in range(1, nx)
    ]
    stacked = jnp.stack(by_x)
    ordered = [
        lax.dynamic_index_in_dim(stacked, x ^ i, axis=0, keepdims=False) for i in range(nx)
    ]
    w_own = jnp.concatenate(ordered, axis=0)
    w_pieces = [w_own] + [lax.ppermute(w_own, AXES, lay.swap(kz=kz)) for kz in range(1, nz)]
    if halves > 1:
        w_pieces = w_pieces + [lax.ppermute(piece, AXES, lay.swap(kc=1)) for piece in w_pieces]

    groups = ny * nc
    quarter = model // groups
    wo = lax.dynamic_slice_in_dim(w_out, (y * nc + c) * quarter, quarter, axis=1)
    wo = lax.all_gather(wo, ("z", "x"), axis=0, tiled=True)
    wo = lax.all_gather(wo, ("y", "c"), axis=1, tiled=True)
    wo = wo.reshape(chips, chip_width, model)

    g_own = to_plane(grad_y)
    g_all = over_chips(g_own)

    frame_spec = pl.BlockSpec((BLOCK, model), lambda i, *_: (i, 0))
    triple_spec = pl.BlockSpec((halves, lay.frames, BLOCK, cols), lambda i, *_: (0, 0, i, 0))
    att_spec = pl.BlockSpec((nc, BLOCK, chip_width), lambda i, *_: (0, i, 0))
    gh_spec = pl.BlockSpec((nc, BLOCK, model), lambda i, *_: (0, i, 0))
    w_specs = [whole_spec(piece.shape) for piece in w_pieces]
    w_scratch = pltpu.VMEM((halves, model, 3 * cols), BF16)
    triple_shape = struct((halves, lay.frames, half, cols))
    tokens = lay.frames * BLOCK

    queries, keys, values, *att = pl.pallas_call(
        functools.partial(forward_kernel, lay, halves, half_heads),
        grid_spec=pltpu.PrefetchScalarGridSpec(
            num_scalar_prefetch=2,
            grid=(blocks,),
            in_specs=[frame_spec] * lay.frames + w_specs + [whole_spec(mod_table.shape)],
            out_specs=[triple_spec] * 3 + [att_spec] * chips,
            scratch_shapes=[w_scratch, pltpu.VMEM((tokens, model), BF16)],
        ),
        out_shape=[triple_shape] * 3 + [struct((nc, half, chip_width))] * chips,
        compiler_params=params(),
        name="forward",
    )(pos, info, *x_all, *w_pieces, mod_table)

    att_own = [att[0]] + [
        lax.ppermute(att[k], AXES, chip_swap(k)) for k in range(1, chips)
    ]

    *partial_sums, grad_w = pl.pallas_call(
        functools.partial(backward_kernel, lay, halves, half_heads),
        grid_spec=pltpu.PrefetchScalarGridSpec(
            num_scalar_prefetch=2,
            grid=(blocks,),
            in_specs=[frame_spec] * lay.frames
            + w_specs
            + [
                whole_spec(mod_table.shape),
                pl.BlockSpec(
                    (1, chip_width, model), lambda i, pos_ref, _: (pos_ref[0] * nx + pos_ref[3], 0, 0)
                ),
            ]
            + [triple_spec] * 3
            + [att_spec] * chips,
            out_specs=[gh_spec] * chips + [whole_spec((groups, chip_width, quarter))],
            scratch_shapes=[
                w_scratch,
                pltpu.VMEM((tokens, model), BF16),
                pltpu.VMEM((chip_width, model), F32),
            ],
        ),
        out_shape=[struct((nc, half, model), F32)]
        + [struct((nc, half, model))] * (chips - 1)
        + [struct((groups, chip_width, quarter), F32)],
        compiler_params=params(),
        name="backward",
    )(pos, info, *g_all, *w_pieces, mod_table, wo, queries, keys, values, *att)

    gh_own = [partial_sums[0]] + [
        lax.ppermute(partial_sums[k], AXES, chip_swap(k)) for k in range(1, chips)
    ]

    flat_spec = whole_spec((half, model))
    out_parts = pl.pallas_call(
        functools.partial(output_kernel, lay),
        grid_spec=pltpu.PrefetchScalarGridSpec(
            num_scalar_prefetch=2,
            grid=(1,),
            in_specs=[flat_spec] * nc
            + [whole_spec((nc, half, chip_width))] * chips
            + [whole_spec(wo.shape), whole_spec(mod_table.shape)],
            out_specs=[flat_spec] * nc,
        ),
        out_shape=[struct((half, model))] * nc,
        compiler_params=params(),
        name="output",
    )(pos, info, *x_own, *att_own, wo, mod_table)
    out_y = from_plane(out_parts)

    grad_parts = pl.pallas_call(
        functools.partial(input_grad_kernel, lay),
        grid_spec=pltpu.PrefetchScalarGridSpec(
            num_scalar_prefetch=2,
            grid=(blocks,),
            in_specs=[frame_spec] * (2 * nc) + [gh_spec] * chips + [whole_spec(mod_table.shape)],
            out_specs=[frame_spec] * nc,
        ),
        out_shape=[struct((half, model))] * nc,
        compiler_params=params(),
        name="input_grad",
    )(pos, info, *x_own, *g_own, *gh_own, mod_table)
    grad_x = from_plane(grad_parts)

    grad_w = grad_w.reshape(ny, nc, chip_width, quarter)
    kept = lax.dynamic_index_in_dim(grad_w, c, axis=1, keepdims=False)
    sent = lax.dynamic_index_in_dim(grad_w, 1 - c, axis=1, keepdims=False)
    grad_w = kept + lax.ppermute(sent, AXES, lay.swap(kc=1))
    by_y = [lax.dynamic_index_in_dim(grad_w, y, axis=0, keepdims=False)] + [
        lax.ppermute(
            lax.dynamic_index_in_dim(grad_w, y ^ ky, axis=0, keepdims=False), AXES, lay.swap(ky=ky)
        )
        for ky in range(1, ny)
    ]
    by_y = jnp.stack(by_y).reshape(ny, nc, rows, quarter)
    if nx == nc:
        kept = lax.dynamic_index_in_dim(by_y, x, axis=1, keepdims=False)
        sent = lax.dynamic_index_in_dim(by_y, 1 - x, axis=1, keepdims=False)
        got = lax.ppermute(sent, AXES, lay.swap(kx=1))
        both = jnp.stack([kept, got], axis=1)
        pick = lambda m: m ^ x
    else:
        both = lax.all_gather(by_y, "x", axis=1, tiled=False)
        both = both.reshape(ny, nc, nx, rows, quarter)
        both = lax.dynamic_index_in_dim(both, x, axis=2, keepdims=False)
        pick = lambda m: m

    def for_plane(target):
        source_y, m = target // nc, target % nc
        return both[y ^ source_y, pick(m)]

    total = for_plane(z)
    for kz in range(1, nz):
        total = total + lax.ppermute(for_plane(z ^ kz), AXES, lay.swap(kz=kz))
    grad_w_out = total * jnp.float32(1.0 / math.sqrt(groups * lay.frames * patches))
    return out_y, grad_x, grad_w_out


def solution(mesh):
    lay = Layout(mesh)
    grid = Mesh(mesh.devices.reshape(lay.ny, lay.nc, lay.nz, lay.nx), AXES)
    rows, cols = ("z", "x"), ("y", "c")
    frame = P(AXES, None, None)
    group = P(cols, None)
    return jax.shard_map(
        functools.partial(local, lay),
        mesh=grid,
        in_specs=(frame, frame, group, group, group, P(), P(rows, None), P(rows, None)),
        out_specs=(frame, frame, P(rows, cols)),
        check_vma=False,
    )
```

time: 347 us -> 229 us (0.66)
  waiting for transfers between devices: 230 us -> 60.8 us
  starting transfers between devices: 12 us -> 58.4 us
  Pallas kernels: 0 us -> 37.6 us
  matrix products: 32 us -> 0 us
  blocking collectives: 13.2 us -> 32.6 us
  other arithmetic: 16.7 us -> 3.5 us
  local copies, waits for them, and re-layouts: 26.1 us -> 17.6 us
    all_gather x2 -> x1, waiting for transfers between devices: 116 us -> 0.02 us  [local(): wo = lax.all_gather(wo, ('y', 'c'), axis=1, tiled=True)]
    ppermute x0 -> x41, waiting for transfers between devices: none -> 60.8 us  [the longest x4 18.3 us: from_plane(): lax.ppermute(part, AXES, lay.from_plane(k))]
    ppermute x0 -> x41, starting transfers between devices: none -> 58.3 us  [the longest x12 15.3 us: over_chips(): lax.ppermute(part, AXES, chip_swap(k))]
    unnamed x5 -> x1, waiting for transfers between devices: 55.6 us -> 0.02 us
    all_to_all x3 -> x0, waiting for transfers between devices: 47.1 us -> none  [the longest x1 35.5 us: local(): lax.all_to_all(triple, 'seq', split_axis=1, concat_axis=0, tiled=True)]
    pallas_call x0 -> x4, Pallas kernels: none -> 37.6 us  [the longest x1 16.2 us: local(): pl.pallas_call(functools.partial(backward_kernel, lay, halves, half_heads...]
    all_gather x0 -> x1, blocking collectives: none -> 32.6 us  [local(): wo = lax.all_gather(wo, ('z', 'x'), axis=0, tiled=True)]
    dot_general x11 -> x0, matrix products: 29.9 us -> none  [the longest x2 8.99 us: matmul_t(): lax.dot_general(left_rows, weight, (((1,), (1,)), ((), ())), preferred_el...]
  transfers between devices with their start and end apart: 7 -> 42, of which waited for: 6 -> 13; matrix products, arithmetic and copies ran while one was open for 21% -> 6% of each run, Pallas kernels for 0% -> 10%
where the time goes in v1:
time: 229 us; the launch traced here: 225 us
  waiting for transfers between devices  60.8 us (27%)
  starting transfers between devices  58.4 us (26%)
  Pallas kernels  37.6 us (16%)
  blocking collectives  32.6 us (14%)
  local copies, waits for them, and re-layouts  17.6 us (8%)
  between operations  14.7 us (6%)
  other arithmetic  3.5 us (2%)
    all_gather x1, blocking collectives, local(): wo = lax.all_gather(wo, ('z', 'x'), axis=0, tiled=True)  32.6 us
    ppermute x4, waiting for transfers between devices, from_plane(): lax.ppermute(part, AXES, lay.from_plane(k))  18.3 us
    pallas_call x1, Pallas kernels, local(): pl.pallas_call(functools.partial(backward_kernel, lay, halves, half_heads...  16.2 us
    ppermute x12, starting transfers between devices, over_chips(): lax.ppermute(part, AXES, chip_swap(k))  15.3 us
    ppermute x3, waiting for transfers between devices, local(): total = total + lax.ppermute(for_plane(z ^ kz), AXES, lay.swap(kz=kz))  13.7 us
    ppermute x12, waiting for transfers between devices, over_chips(): lax.ppermute(part, AXES, chip_swap(k))  12.7 us
    pallas_call x1, Pallas kernels, local(): pl.pallas_call(functools.partial(forward_kernel, lay, halves, half_heads)...  12.3 us
    ppermute x4, starting transfers between devices, from_plane(): lax.ppermute(part, AXES, lay.from_plane(k))  9.95 us
  transfers between devices with their start and end apart: 42, of which 13 were waited for; matrix products, arithmetic and copies ran while one was open for 6% of the time, Pallas kernels for 10%

profile of v1, /device:TPU:4, one launch (start us, length us, event | category | flops | bytes accessed | tf_op | source)
XLA Modules:
  0.0 225.1 jit_solution(5924282109966835532)
XLA Ops:
  7.2 0.9 copy-done
  8.2 32.6 %all_gather.6 = bf16[1152,288]{1,0:T(8,128)(2,1)S(1)} all-gather(bf16[144,288]{1,0:T(8,128)(2,1)S(1)} %constant_dynamic-slice_fusion.1), channel_id=1, replica_groups=mesh['y'=2,'c'=2,'z'=4,'x'=2] {'z','x'}, dimensions={0}, use_global_device_ids=true | all-gather | bytes 746496 | tf_op jit(solution)/shard_map/all_gather | solution.py:366
  40.9 1.2 copy.25
  42.1 2.4 %reshape.32 = bf16[144,3,4,2,144]{4,3,2,1,0:T(2,128)(2,1)S(1)} reshape(bf16[144,3456]{1,0:T(8,128)(2,1)S(1)} %copy-done.12) | data formatting | bytes 1990656 | tf_op jit(solution)/shard_map/reshape | solution.py:344
  44.5 0.9 constant_dynamic-slice_fusion.2
  45.5 0.7 copy.28
  46.2 1.6 collective-permute-start.9
  47.8 1.9 collective-permute-start.1
  49.8 2.2 collective-permute-start.2
  52.0 5.6 %collective-permute-start = (s32[1,16]{1,0:T(1,128)S(1)}, s32[1,16]{1,0:T(1,128)S(1)}, u32[]{:S(2)}, u32[]{:S(2)}) collective-permute-start(s32[1,16]{1,0:T(1,128)S(1)} %add_bitcast_fusion), channel_id=1, source_target_pairs={{0,0},{1,1},{2,16},{3,17},{4,8},{5,9},{6,24},{7,25},{8,4},{9,5},{1... | collective-permute-start | bytes 200 | tf_op jit(solution)/shard_map/ppermute | solution.py:339
  57.7 1.0 dynamic-slice_bitcast_fusion.2
  58.7 1.9 collective-permute-start.22
  60.6 0.7 copy.27
  61.3 0.2 collective-permute-start.23
  61.6 0.2 collective-permute-start.3
  61.8 0.2 fusion.4
  62.2 2.7 %collective-permute-done = s32[1,16]{1,0:T(1,128)S(1)} collective-permute-done((s32[1,16]{1,0:T(1,128)S(1)}, s32[1,16]{1,0:T(1,128)S(1)}, u32[]{:S(2)}, u32[]{:S(2)}) %collective-permute-start) | collective-permute-done | bytes 96 | tf_op jit(solution)/shard_map/ppermute | solution.py:339
  64.9 0.1 collective-permute-start.4
  65.1 3.3 %collective-permute-done.22.refs_0_.refs_2_ = bf16[64,1152]{1,0:T(8,128)(2,1)S(1)} collective-permute-done((bf16[64,1152]{1,0:T(8,128)(2,1)S(1)}, bf16[64,1152]{1,0:T(8,128)(2,1)S(1)}, u32[]{:S(2)}, u32[]{:S(2)}) %collective-permute-start.22) | collective-permute-done | bytes 147488 | tf_op jit(solution)/shard_map/ppermute | solution.py:314
  68.4 0.9 collective-permute-start.10
  69.3 0.9 collective-permute-done.23.refs_1_.refs_3_
  70.2 2.6 %collective-permute-start.12 = (bf16[288,432]{1,0:T(8,128)(2,1)S(1)}, bf16[288,432]{1,0:T(8,128)(2,1)S(1)}, u32[]{:S(2)}, u32[]{:S(2)}) collective-permute-start(bf16[288,432]{1,0:T(8,128)(2,1)S(1)} %pad_maximum_fusion.refs_8_), channel_id=1, source_target_pairs={{0,6},{1,7},{2,4},{3,5},{4,2},{5,3},{6,0},{7,1},{8,14},{9,15},{10,... | collective-permute-start | bytes 746504 | tf_op jit(solution)/shard_map/ppermute | solution.py:359
  72.8 8.5 %collective-permute-start.6 = (bf16[64,1152]{1,0:T(8,128)(2,1)S(1)}, bf16[64,1152]{1,0:T(8,128)(2,1)S(1)}, u32[]{:S(2)}, u32[]{:S(2)}) collective-permute-start(bf16[64,1152]{1,0:T(8,128)(2,1)S(1)} %collective-permute-done.2.refs_1_), channel_id=1, source_target_pairs={{0,16},{1,17},{2,18},{3,19},{4,20},{5,21},{6,22},{7,23},{8,24},{9,... | collective-permute-start | bytes 442376 | tf_op jit(solution)/shard_map/ppermute | solution.py:335
  81.3 7.0 %collective-permute-done.6.refs_5_ = bf16[64,1152]{1,0:T(8,128)(2,1)S(1)} collective-permute-done((bf16[64,1152]{1,0:T(8,128)(2,1)S(1)}, bf16[64,1152]{1,0:T(8,128)(2,1)S(1)}, u32[]{:S(2)}, u32[]{:S(2)}) %collective-permute-start.6) | collective-permute-done | bytes 147488 | tf_op jit(solution)/shard_map/ppermute | solution.py:335
  88.3 0.7 collective-permute-start.8
  89.1 0.6 copy-done.23
  89.7 1.8 collective-permute-done.11.refs_10_
  91.5 4.2 %collective-permute-start.15 = (bf16[288,432]{1,0:T(8,128)(2,1)S(1)}, bf16[288,432]{1,0:T(8,128)(2,1)S(1)}, u32[]{:S(2)}, u32[]{:S(2)}) collective-permute-start(bf16[288,432]{1,0:T(8,128)(2,1)S(1)} %collective-permute-done.11.refs_10_), channel_id=1, source_target_pairs={{0,8},{1,9},{2,10},{3,11},{4,12},{5,13},{6,14},{7,15},{8,0},{9,1},... | collective-permute-start | bytes 746504 | tf_op jit(solution)/shard_map/ppermute | solution.py:361
  95.7 0.5 collective-permute-start.24
  96.3 5.7 %collective-permute-done.24.refs_2_ = bf16[64,1152]{1,0:T(8,128)(2,1)S(1)} collective-permute-done((bf16[64,1152]{1,0:T(8,128)(2,1)S(1)}, bf16[64,1152]{1,0:T(8,128)(2,1)S(1)}, u32[]{:S(2)}, u32[]{:S(2)}) %collective-permute-start.24) | collective-permute-done | bytes 147488 | tf_op jit(solution)/shard_map/ppermute | solution.py:335
  102.0 0.4 collective-permute-start.25
  102.4 1.9 collective-permute-start.27
  104.3 1.2 collective-permute-start.28
  105.6 1.8 collective-permute-start.29
  107.3 0.6 pad_add_fusion.pos_ref
  108.1 12.3 %forward.1 = (bf16[2,8,64,144]{3,2,1,0:T(8,128)(2,1)}, bf16[2,8,64,144]{3,2,1,0:T(8,128)(2,1)}, bf16[2,8,64,144]{3,2,1,0:T(8,128)(2,1)}, bf16[2,64,288]{2,1,0:T(...) custom-call(s32[4]{0:T(128)} %pad_add_fusion.pos_ref, ...), custom_call_target="tpu_custom_call" | custom-call | tf_op jit(solution)/shard_map/forward/pallas_call | solution.py:382
  120.3 5.2 %copy.26 = bf16[1152,1152]{1,0:T(8,128)(2,1)} copy(bf16[1152,1152]{0,1:T(8,128)(2,1)} %all-gather.2.cloned.1.call-done) | data formatting | bytes 5308416 | tf_op jit(solution)/shard_map/all_gather | solution.py:367
  125.6 16.2 %backward.1 = (f32[2,64,1152]{2,1,0:T(8,128)}, bf16[2,64,1152]{2,1,0:T(8,128)(2,1)}, bf16[2,64,1152]{2,1,0:T(8,128)(2,1)}, bf16[2,64,1152]{2,1,0:T(8,128)(2,1)}, f32[4,288,288]{2,1,0:T(8,128)}) custom-call(s32[4]{0:T(128)} %pad_add_fusion.pos_ref, s32[16]{0:T(128)} %bitcast.70, bf16[64,1152]{1,0:T(8,128)(2,1)} %copy-done.13, bf16[64,1152]{1,0:T(8,128)(2,1)} %copy-done.14, ...), custom_call_target="tpu_custom_call" | custom-call | tf_op jit(solution)/shard_map/backward/pallas_call | solution.py:400
  141.9 1.3 dynamic-slice_bitcast_fusion
  143.3 1.8 collective-permute-start.17
  145.1 1.7 collective-permute-start.19
  146.8 1.7 collective-permute-start.30
  148.5 0.2 collective-permute-start.31
  148.8 4.0 %collective-permute-done.18.refs_4_ = bf16[2,64,288]{2,1,0:T(8,128)(2,1)S(1)} collective-permute-done((bf16[2,64,288]{2,1,0:T(8,128)(2,1)S(1)}, bf16[2,64,288]{2,1,0:T(8,128)(2,1)S(1)}, u32[]{:S(2)}, u32[]{:S(2)}) %collective-permute-start.18) | collective-permute-done | bytes 73760 | tf_op jit(solution)/shard_map/ppermute | solution.py:397
  152.8 0.6 copy-done.30
  153.4 0.6 copy-done.31
  154.1 4.3 %output.1 = (bf16[64,1152]{1,0:T(8,128)(2,1)}, bf16[64,1152]{1,0:T(8,128)(2,1)}) custom-call(s32[4]{0:T(128)} %pad_add_fusion.pos_ref, s32[16]{0:T(128)} %bitcast.71, bf16[64,1152]{1,0:T(8,128)(2,1)} %copy-done.3, bf16[64,1152]{1,0:T(8,128)(2,1)} %copy-done.4, bf16[2,64,288]{2,1,0:T(8,128)(2,1)} %get-tuple-element.19.refs_2_.refs_21_, ...), custom_call_target="tpu_custom_call" | custom-call | tf_op jit(solution)/shard_map/output/pallas_call | solution.py:434
  158.4 6.1 %collective-permute-start.20 = (bf16[64,1152]{1,0:T(8,128)(2,1)}, bf16[64,1152]{1,0:T(8,128)(2,1)S(1)}, u32[]{:S(2)}, u32[]{:S(2)}) collective-permute-start(bf16[64,1152]{1,0:T(8,128)(2,1)} %get-tuple-element.23), channel_id=1, source_target_pairs={{0,0},{1,1},{16,2},{17,3},{8,4},{9,5},{24,6},{25,7},{4,8},{5,9},{2... | collective-permute-start | bytes 442376 | tf_op jit(solution)/shard_map/ppermute | solution.py:324
  164.8 9.8 %collective-permute-done.20 = bf16[64,1152]{1,0:T(8,128)(2,1)S(1)} collective-permute-done((bf16[64,1152]{1,0:T(8,128)(2,1)}, bf16[64,1152]{1,0:T(8,128)(2,1)S(1)}, u32[]{:S(2)}, u32[]{:S(2)}) %collective-permute-start.20) | collective-permute-done | bytes 147488 | tf_op jit(solution)/shard_map/ppermute | solution.py:324
  174.5 0.7 collective-permute-done.21
  175.4 0.7 copy-done.16
  176.2 4.8 %input_grad.1 = (bf16[64,1152]{1,0:T(8,128)(2,1)}, bf16[64,1152]{1,0:T(8,128)(2,1)}) custom-call(s32[4]{0:T(128)} %pad_add_fusion.pos_ref, s32[16]{0:T(128)} %bitcast.72, bf16[64,1152]{1,0:T(8,128)(2,1)} %copy-done.3, bf16[64,1152]{1,0:T(8,128)(2,1)} %copy-done.4, bf16[64,1152]{1,0:T(8,128)(2,1)} %copy-done.13, bf16[64,1152]{1,0:T(8,128)(2,1)} %copy-done.14, ...), custom_call_target="tpu_custom_call" | custom-call | tf_op jit(solution)/shard_map/input_grad/pallas_call | solution.py:450
  181.1 1.9 collective-permute-start.33
  183.0 1.9 collective-permute-start.34
  184.9 0.7 maximum_bitcast_fusion
  185.7 1.8 collective-permute-start.37
  187.4 7.8 %collective-permute-done.33 = bf16[64,1152]{1,0:T(8,128)(2,1)S(1)} collective-permute-done((bf16[64,1152]{1,0:T(8,128)(2,1)}, bf16[64,1152]{1,0:T(8,128)(2,1)S(1)}, u32[]{:S(2)}, u32[]{:S(2)}) %collective-permute-start.33) | collective-permute-done | bytes 147488 | tf_op jit(solution)/shard_map/ppermute | solution.py:324
  195.3 3.3 %collective-permute-done.37 = f32[2,144,288]{2,1,0:T(8,128)S(1)} collective-permute-done((f32[2,144,288]{2,1,0:T(8,128)S(1)}, f32[2,144,288]{2,1,0:T(8,128)S(1)}, u32[]{:S(2)}, u32[]{:S(2)}) %collective-permute-start.37) | collective-permute-done | bytes 331808 | tf_op jit(solution)/shard_map/ppermute | solution.py:478
  198.8 0.2 collective-permute-start.39
  198.9 4.2 %collective-permute-start.40 = (f32[144,288]{1,0:T(8,128)S(1)}, f32[144,288]{1,0:T(8,128)S(1)}, u32[]{:S(2)}, u32[]{:S(2)}) collective-permute-start(f32[144,288]{1,0:T(8,128)S(1)} %get-tuple-element.39), channel_id=1, source_target_pairs={{0,6},{1,7},{2,4},{3,5},{4,2},{5,3},{6,0},{7,1},{8,14},{9,15},{10,... | collective-permute-start | bytes 497672 | tf_op jit(solution)/shard_map/ppermute | solution.py:493
  203.1 0.7 maximum_bitcast_fusion.1
  203.9 4.8 %collective-permute-done.38 = f32[144,288]{1,0:T(8,128)S(1)} collective-permute-done((f32[144,288]{1,0:T(8,128)S(1)}, f32[144,288]{1,0:T(8,128)S(1)}, u32[]{:S(2)}, u32[]{:S(2)}) %collective-permute-start.38) | collective-permute-done | bytes 165920 | tf_op jit(solution)/shard_map/ppermute | solution.py:493
  208.7 8.9 %collective-permute-done.39 = f32[144,288]{1,0:T(8,128)S(1)} collective-permute-done((f32[144,288]{1,0:T(8,128)S(1)}, f32[144,288]{1,0:T(8,128)S(1)}, u32[]{:S(2)}, u32[]{:S(2)}) %collective-permute-start.39) | collective-permute-done | bytes 165920 | tf_op jit(solution)/shard_map/ppermute | solution.py:493
  217.5 0.8 fusion.12
  (127 shorter events, 1.8 us)
Async XLA Ops:
  7.2 34.9 %copy-start.12 = (bf16[144,3456]{1,0:T(8,128)(2,1)S(1)}, bf16[144,3456]{1,0:T(8,128)(2,1)}, u32[]{:S(2)}) copy-start(bf16[144,3456]{1,0:T(8,128)(2,1)} %param.14) | copy-start | bytes 2985988
  7.2 113.1 %all-gather.2.cloned.1.call-start = ((), (), s32[]{:S(2)}) async-start(), calls=%async_computation | async-start | bytes 3317760 | tf_op jit(solution)/shard_map/all_gather | solution.py:367
  44.5 7.4 %copy-start.33 = (s32[1,4]{1,0:T(1,128)S(1)}, s32[1,4]{1,0:T(1,128)}, u32[]{:S(2)}) copy-start(s32[1,4]{1,0:T(1,128)} %param.12) | copy-start | bytes 52
  44.5 7.4 %copy-start.34 = (s32[1,4]{1,0:T(1,128)S(1)}, s32[1,4]{1,0:T(1,128)}, u32[]{:S(2)}) copy-start(s32[1,4]{1,0:T(1,128)} %param.11) | copy-start | bytes 52
  44.5 7.4 %copy-start.35 = (s32[1,8]{1,0:T(1,128)S(1)}, s32[1,8]{1,0:T(1,128)}, u32[]{:S(2)}) copy-start(s32[1,8]{1,0:T(1,128)} %param.10) | copy-start | bytes 100
  46.2 15.1 %collective-permute-start.9 = (bf16[144,432]{0,1:T(8,128)(2,1)S(1)}, bf16[144,432]{0,1:T(8,128)(2,1)S(1)}, u32[]{:S(2)}, u32[]{:S(2)}) collective-permute-start(bf16[144,432]{0,1:T(8,128)(2,1)S(1)} %bitcast.68), channel_id=1, source_target_pairs={{0,1},{1,0},{2,3},{3,2},{4,5},{5,4},{6,7},{7,6},{8,9},{9,8},{10,11... | collective-permute-start | bytes 373256 | tf_op jit(solution)/shard_map/ppermute | solution.py:352
  47.8 13.8 %collective-permute-start.1 = (bf16[64,1152]{1,0:T(8,128)(2,1)S(1)}, bf16[64,1152]{1,0:T(8,128)(2,1)S(1)}, u32[]{:S(2)}, u32[]{:S(2)}) collective-permute-start(bf16[64,1152]{1,0:T(8,128)(2,1)S(1)} %get-tuple-element.53), channel_id=1, source_target_pairs={{0,0},{1,1},{2,16},{3,17},{4,8},{5,9},{6,24},{7,25},{8,4},{9,5},{1... | collective-permute-start | bytes 442376 | tf_op jit(solution)/shard_map/ppermute | solution.py:314
  49.8 15.1 %collective-permute-start.2 = (bf16[64,1152]{1,0:T(8,128)(2,1)S(1)}, bf16[64,1152]{1,0:T(8,128)(2,1)S(1)}, u32[]{:S(2)}, u32[]{:S(2)}) collective-permute-start(bf16[64,1152]{1,0:T(8,128)(2,1)S(1)} %get-tuple-element.52), channel_id=1, source_target_pairs={{0,8},{1,9},{2,24},{3,25},{4,0},{5,1},{6,16},{7,17},{8,12},{9,13},... | collective-permute-start | bytes 442376 | tf_op jit(solution)/shard_map/ppermute | solution.py:314
  52.0 12.9 %collective-permute-start = (s32[1,16]{1,0:T(1,128)S(1)}, s32[1,16]{1,0:T(1,128)S(1)}, u32[]{:S(2)}, u32[]{:S(2)}) collective-permute-start(s32[1,16]{1,0:T(1,128)S(1)} %add_bitcast_fusion), channel_id=1, source_target_pairs={{0,0},{1,1},{2,16},{3,17},{4,8},{5,9},{6,24},{7,25},{8,4},{9,5},{1... | collective-permute-start | bytes 200 | tf_op jit(solution)/shard_map/ppermute | solution.py:339
  58.7 9.7 %collective-permute-start.22 = (bf16[64,1152]{1,0:T(8,128)(2,1)S(1)}, bf16[64,1152]{1,0:T(8,128)(2,1)S(1)}, u32[]{:S(2)}, u32[]{:S(2)}) collective-permute-start(bf16[64,1152]{1,0:T(8,128)(2,1)S(1)} %get-tuple-element.49), channel_id=1, source_target_pairs={{0,0},{1,1},{2,16},{3,17},{4,8},{5,9},{6,24},{7,25},{8,4},{9,5},{1... | collective-permute-start | bytes 442376 | tf_op jit(solution)/shard_map/ppermute | solution.py:314
  61.3 8.9 %collective-permute-start.23 = (bf16[64,1152]{1,0:T(8,128)(2,1)S(1)}, bf16[64,1152]{1,0:T(8,128)(2,1)S(1)}, u32[]{:S(2)}, u32[]{:S(2)}) collective-permute-start(bf16[64,1152]{1,0:T(8,128)(2,1)S(1)} %get-tuple-element.48), channel_id=1, source_target_pairs={{0,8},{1,9},{2,24},{3,25},{4,0},{5,1},{6,16},{7,17},{8,12},{9,13},... | collective-permute-start | bytes 442376 | tf_op jit(solution)/shard_map/ppermute | solution.py:314
  61.6 46.4 %copy-start.3 = (bf16[64,1152]{1,0:T(8,128)(2,1)}, bf16[64,1152]{1,0:T(8,128)(2,1)S(1)}, u32[]{:S(2)}) copy-start(bf16[64,1152]{1,0:T(8,128)(2,1)S(1)} %collective-permute-done.1.refs_0_) | copy-start | bytes 442372
  61.6 8.6 %collective-permute-start.3 = (bf16[64,1152]{1,0:T(8,128)(2,1)S(1)}, bf16[64,1152]{1,0:T(8,128)(2,1)S(1)}, u32[]{:S(2)}, u32[]{:S(2)}) collective-permute-start(bf16[64,1152]{1,0:T(8,128)(2,1)S(1)} %collective-permute-done.1.refs_0_), channel_id=1, source_target_pairs={{0,1},{1,0},{2,3},{3,2},{4,5},{5,4},{6,7},{7,6},{8,9},{9,8},{10,11... | collective-permute-start | bytes 442376 | tf_op jit(solution)/shard_map/ppermute | solution.py:335
  64.9 43.1 %copy-start.32 = (s32[1,16]{1,0:T(1,128)}, s32[1,16]{1,0:T(1,128)S(1)}, u32[]{:S(2)}) copy-start(s32[1,16]{1,0:T(1,128)S(1)} %collective-permute-done) | copy-start | bytes 196
  64.9 16.4 %collective-permute-start.5 = (bf16[64,1152]{1,0:T(8,128)(2,1)S(1)}, bf16[64,1152]{1,0:T(8,128)(2,1)S(1)}, u32[]{:S(2)}, u32[]{:S(2)}) collective-permute-start(bf16[64,1152]{1,0:T(8,128)(2,1)S(1)} %collective-permute-done.1.refs_0_), channel_id=1, source_target_pairs={{0,16},{1,17},{2,18},{3,19},{4,20},{5,21},{6,22},{7,23},{8,24},{9,... | collective-permute-start | bytes 442376 | tf_op jit(solution)/shard_map/ppermute | solution.py:335
  64.9 43.1 %copy-start.4 = (bf16[64,1152]{1,0:T(8,128)(2,1)}, bf16[64,1152]{1,0:T(8,128)(2,1)S(1)}, u32[]{:S(2)}) copy-start(bf16[64,1152]{1,0:T(8,128)(2,1)S(1)} %collective-permute-done.2.refs_1_) | copy-start | bytes 442372
  64.9 7.9 %collective-permute-start.4 = (bf16[64,1152]{1,0:T(8,128)(2,1)S(1)}, bf16[64,1152]{1,0:T(8,128)(2,1)S(1)}, u32[]{:S(2)}, u32[]{:S(2)}) collective-permute-start(bf16[64,1152]{1,0:T(8,128)(2,1)S(1)} %collective-permute-done.2.refs_1_), channel_id=1, source_target_pairs={{0,1},{1,0},{2,3},{3,2},{4,5},{5,4},{6,7},{7,6},{8,9},{9,8},{10,11... | collective-permute-start | bytes 442376 | tf_op jit(solution)/shard_map/ppermute | solution.py:335
  65.1 42.9 %copy-start.1 = (bf16[288,432]{1,0:T(8,128)(2,1)}, bf16[288,432]{1,0:T(8,128)(2,1)S(1)}, u32[]{:S(2)}) copy-start(bf16[288,432]{1,0:T(8,128)(2,1)S(1)} %pad_maximum_fusion.refs_8_) | copy-start | bytes 746500
  68.4 57.2 %copy-start.13 = (bf16[64,1152]{1,0:T(8,128)(2,1)}, bf16[64,1152]{1,0:T(8,128)(2,1)S(1)}, u32[]{:S(2)}) copy-start(bf16[64,1152]{1,0:T(8,128)(2,1)S(1)} %collective-permute-done.22.refs_0_.refs_2_) | copy-start | bytes 442372
  68.4 21.2 %collective-permute-start.10 = (bf16[288,432]{1,0:T(8,128)(2,1)S(1)}, bf16[288,432]{1,0:T(8,128)(2,1)S(1)}, u32[]{:S(2)}, u32[]{:S(2)}) collective-permute-start(bf16[288,432]{1,0:T(8,128)(2,1)S(1)} %pad_maximum_fusion.refs_8_), channel_id=1, source_target_pairs={{0,2},{1,3},{2,0},{3,1},{4,6},{5,7},{6,4},{7,5},{8,10},{9,11},{10,... | collective-permute-start | bytes 746504 | tf_op jit(solution)/shard_map/ppermute | solution.py:359
  70.2 55.4 %copy-start.14 = (bf16[64,1152]{1,0:T(8,128)(2,1)}, bf16[64,1152]{1,0:T(8,128)(2,1)S(1)}, u32[]{:S(2)}) copy-start(bf16[64,1152]{1,0:T(8,128)(2,1)S(1)} %collective-permute-done.23.refs_1_.refs_3_) | copy-start | bytes 442372
  70.2 21.2 %collective-permute-start.11 = (bf16[288,432]{1,0:T(8,128)(2,1)S(1)}, bf16[288,432]{1,0:T(8,128)(2,1)S(1)}, u32[]{:S(2)}, u32[]{:S(2)}) collective-permute-start(bf16[288,432]{1,0:T(8,128)(2,1)S(1)} %pad_maximum_fusion.refs_8_), channel_id=1, source_target_pairs={{0,4},{1,5},{2,6},{3,7},{4,0},{5,1},{6,2},{7,3},{8,12},{9,13},{10,... | collective-permute-start | bytes 746504 | tf_op jit(solution)/shard_map/ppermute | solution.py:359
  70.2 37.7 %copy-start.19 = (bf16[64,1152]{1,0:T(8,128)(2,1)}, bf16[64,1152]{1,0:T(8,128)(2,1)S(1)}, u32[]{:S(2)}) copy-start(bf16[64,1152]{1,0:T(8,128)(2,1)S(1)} %collective-permute-done.3.refs_2_) | copy-start | bytes 442372
  70.2 25.4 %collective-permute-start.12 = (bf16[288,432]{1,0:T(8,128)(2,1)S(1)}, bf16[288,432]{1,0:T(8,128)(2,1)S(1)}, u32[]{:S(2)}, u32[]{:S(2)}) collective-permute-start(bf16[288,432]{1,0:T(8,128)(2,1)S(1)} %pad_maximum_fusion.refs_8_), channel_id=1, source_target_pairs={{0,6},{1,7},{2,4},{3,5},{4,2},{5,3},{6,0},{7,1},{8,14},{9,15},{10,... | collective-permute-start | bytes 746504 | tf_op jit(solution)/shard_map/ppermute | solution.py:359
  72.8 16.2 %copy-start.21 = (bf16[64,1152]{1,0:T(8,128)(2,1)}, bf16[64,1152]{1,0:T(8,128)(2,1)S(1)}, u32[]{:S(2)}) copy-start(bf16[64,1152]{1,0:T(8,128)(2,1)S(1)} %collective-permute-done.4.refs_3_) | copy-start | bytes 442372
  72.8 15.5 %collective-permute-start.6 = (bf16[64,1152]{1,0:T(8,128)(2,1)S(1)}, bf16[64,1152]{1,0:T(8,128)(2,1)S(1)}, u32[]{:S(2)}, u32[]{:S(2)}) collective-permute-start(bf16[64,1152]{1,0:T(8,128)(2,1)S(1)} %collective-permute-done.2.refs_1_), channel_id=1, source_target_pairs={{0,16},{1,17},{2,18},{3,19},{4,20},{5,21},{6,22},{7,23},{8,24},{9,... | collective-permute-start | bytes 442376 | tf_op jit(solution)/shard_map/ppermute | solution.py:335
  81.3 7.7 %copy-start.20 = (bf16[64,1152]{1,0:T(8,128)(2,1)}, bf16[64,1152]{1,0:T(8,128)(2,1)S(1)}, u32[]{:S(2)}) copy-start(bf16[64,1152]{1,0:T(8,128)(2,1)S(1)} %collective-permute-done.5.refs_4_) | copy-start | bytes 442372
  81.3 7.7 %collective-permute-start.7 = (bf16[64,1152]{1,0:T(8,128)(2,1)S(1)}, bf16[64,1152]{1,0:T(8,128)(2,1)S(1)}, u32[]{:S(2)}, u32[]{:S(2)}) collective-permute-start(bf16[64,1152]{1,0:T(8,128)(2,1)S(1)} %collective-permute-done.1.refs_0_), channel_id=1, source_target_pairs={{0,17},{1,16},{2,19},{3,18},{4,21},{5,20},{6,23},{7,22},{8,25},{9,... | collective-permute-start | bytes 442376 | tf_op jit(solution)/shard_map/ppermute | solution.py:335
  88.3 7.5 %collective-permute-start.8 = (bf16[64,1152]{1,0:T(8,128)(2,1)S(1)}, bf16[64,1152]{1,0:T(8,128)(2,1)S(1)}, u32[]{:S(2)}, u32[]{:S(2)}) collective-permute-start(bf16[64,1152]{1,0:T(8,128)(2,1)S(1)} %collective-permute-done.2.refs_1_), channel_id=1, source_target_pairs={{0,17},{1,16},{2,19},{3,18},{4,21},{5,20},{6,23},{7,22},{8,25},{9,... | collective-permute-start | bytes 442376 | tf_op jit(solution)/shard_map/ppermute | solution.py:335
  89.0 13.0 %collective-permute-start.13 = (bf16[288,432]{1,0:T(8,128)(2,1)S(1)}, bf16[288,432]{1,0:T(8,128)(2,1)S(1)}, u32[]{:S(2)}, u32[]{:S(2)}) collective-permute-start(bf16[288,432]{1,0:T(8,128)(2,1)S(1)} %pad_maximum_fusion.refs_8_), channel_id=1, source_target_pairs={{0,8},{1,9},{2,10},{3,11},{4,12},{5,13},{6,14},{7,15},{8,0},{9,1},... | collective-permute-start | bytes 746504 | tf_op jit(solution)/shard_map/ppermute | solution.py:361
  89.7 18.3 %copy-start.5 = (bf16[288,432]{1,0:T(8,128)(2,1)}, bf16[288,432]{1,0:T(8,128)(2,1)S(1)}, u32[]{:S(2)}) copy-start(bf16[288,432]{1,0:T(8,128)(2,1)S(1)} %collective-permute-done.10.refs_9_) | copy-start | bytes 746500
  89.7 12.7 %collective-permute-start.14 = (bf16[288,432]{1,0:T(8,128)(2,1)S(1)}, bf16[288,432]{1,0:T(8,128)(2,1)S(1)}, u32[]{:S(2)}, u32[]{:S(2)}) collective-permute-start(bf16[288,432]{1,0:T(8,128)(2,1)S(1)} %collective-permute-done.10.refs_9_), channel_id=1, source_target_pairs={{0,8},{1,9},{2,10},{3,11},{4,12},{5,13},{6,14},{7,15},{8,0},{9,1},... | collective-permute-start | bytes 746504 | tf_op jit(solution)/shard_map/ppermute | solution.py:361
  91.5 16.5 %copy-start.6 = (bf16[288,432]{1,0:T(8,128)(2,1)}, bf16[288,432]{1,0:T(8,128)(2,1)S(1)}, u32[]{:S(2)}) copy-start(bf16[288,432]{1,0:T(8,128)(2,1)S(1)} %collective-permute-done.11.refs_10_) | copy-start | bytes 746500
  91.5 12.9 %collective-permute-start.15 = (bf16[288,432]{1,0:T(8,128)(2,1)S(1)}, bf16[288,432]{1,0:T(8,128)(2,1)S(1)}, u32[]{:S(2)}, u32[]{:S(2)}) collective-permute-start(bf16[288,432]{1,0:T(8,128)(2,1)S(1)} %collective-permute-done.11.refs_10_), channel_id=1, source_target_pairs={{0,8},{1,9},{2,10},{3,11},{4,12},{5,13},{6,14},{7,15},{8,0},{9,1},... | collective-permute-start | bytes 746504 | tf_op jit(solution)/shard_map/ppermute | solution.py:361
  95.7 12.3 %copy-start.7 = (bf16[288,432]{1,0:T(8,128)(2,1)}, bf16[288,432]{1,0:T(8,128)(2,1)S(1)}, u32[]{:S(2)}) copy-start(bf16[288,432]{1,0:T(8,128)(2,1)S(1)} %collective-permute-done.12.refs_11_) | copy-start | bytes 746500
  95.7 9.9 %collective-permute-start.16 = (bf16[288,432]{1,0:T(8,128)(2,1)S(1)}, bf16[288,432]{1,0:T(8,128)(2,1)S(1)}, u32[]{:S(2)}, u32[]{:S(2)}) collective-permute-start(bf16[288,432]{1,0:T(8,128)(2,1)S(1)} %collective-permute-done.12.refs_11_), channel_id=1, source_target_pairs={{0,8},{1,9},{2,10},{3,11},{4,12},{5,13},{6,14},{7,15},{8,0},{9,1},... | collective-permute-start | bytes 746504 | tf_op jit(solution)/shard_map/ppermute | solution.py:361
  95.7 9.8 %copy-start.24 = (bf16[64,1152]{1,0:T(8,128)(2,1)}, bf16[64,1152]{1,0:T(8,128)(2,1)S(1)}, u32[]{:S(2)}) copy-start(bf16[64,1152]{1,0:T(8,128)(2,1)S(1)} %collective-permute-done.8.refs_7_) | copy-start | bytes 442372
  95.7 6.2 %collective-permute-start.24 = (bf16[64,1152]{1,0:T(8,128)(2,1)S(1)}, bf16[64,1152]{1,0:T(8,128)(2,1)S(1)}, u32[]{:S(2)}, u32[]{:S(2)}) collective-permute-start(bf16[64,1152]{1,0:T(8,128)(2,1)S(1)} %collective-permute-done.22.refs_0_.refs_2_), channel_id=1, source_target_pairs={{0,1},{1,0},{2,3},{3,2},{4,5},{5,4},{6,7},{7,6},{8,9},{9,8},{10,11... | collective-permute-start | bytes 442376 | tf_op jit(solution)/shard_map/ppermute | solution.py:335
  102.0 23.6 %collective-permute-start.26 = (bf16[64,1152]{1,0:T(8,128)(2,1)S(1)}, bf16[64,1152]{1,0:T(8,128)(2,1)}, u32[]{:S(2)}, u32[]{:S(2)}) collective-permute-start(bf16[64,1152]{1,0:T(8,128)(2,1)S(1)} %collective-permute-done.22.refs_0_.refs_2_), channel_id=1, source_target_pairs={{0,16},{1,17},{2,18},{3,19},{4,20},{5,21},{6,22},{7,23},{8,24},{9,... | collective-permute-start | bytes 442376 | tf_op jit(solution)/shard_map/ppermute | solution.py:335
  102.0 6.1 %copy-start.8 = (bf16[288,432]{1,0:T(8,128)(2,1)}, bf16[288,432]{1,0:T(8,128)(2,1)S(1)}, u32[]{:S(2)}) copy-start(bf16[288,432]{1,0:T(8,128)(2,1)S(1)} %collective-permute-done.13.refs_12_) | copy-start | bytes 746500
  102.0 23.6 %collective-permute-start.25 = (bf16[64,1152]{1,0:T(8,128)(2,1)S(1)}, bf16[64,1152]{1,0:T(8,128)(2,1)}, u32[]{:S(2)}, u32[]{:S(2)}) collective-permute-start(bf16[64,1152]{1,0:T(8,128)(2,1)S(1)} %collective-permute-done.23.refs_1_.refs_3_), channel_id=1, source_target_pairs={{0,1},{1,0},{2,3},{3,2},{4,5},{5,4},{6,7},{7,6},{8,9},{9,8},{10,11... | collective-permute-start | bytes 442376 | tf_op jit(solution)/shard_map/ppermute | solution.py:335
  102.4 5.7 %copy-start.9 = (bf16[288,432]{1,0:T(8,128)(2,1)}, bf16[288,432]{1,0:T(8,128)(2,1)S(1)}, u32[]{:S(2)}) copy-start(bf16[288,432]{1,0:T(8,128)(2,1)S(1)} %collective-permute-done.14.refs_13_) | copy-start | bytes 746500
  102.4 23.2 %collective-permute-start.27 = (bf16[64,1152]{1,0:T(8,128)(2,1)S(1)}, bf16[64,1152]{1,0:T(8,128)(2,1)}, u32[]{:S(2)}, u32[]{:S(2)}) collective-permute-start(bf16[64,1152]{1,0:T(8,128)(2,1)S(1)} %collective-permute-done.23.refs_1_.refs_3_), channel_id=1, source_target_pairs={{0,16},{1,17},{2,18},{3,19},{4,20},{5,21},{6,22},{7,23},{8,24},{9,... | collective-permute-start | bytes 442376 | tf_op jit(solution)/shard_map/ppermute | solution.py:335
  104.3 21.3 %collective-permute-start.28 = (bf16[64,1152]{1,0:T(8,128)(2,1)S(1)}, bf16[64,1152]{1,0:T(8,128)(2,1)}, u32[]{:S(2)}, u32[]{:S(2)}) collective-permute-start(bf16[64,1152]{1,0:T(8,128)(2,1)S(1)} %collective-permute-done.22.refs_0_.refs_2_), channel_id=1, source_target_pairs={{0,17},{1,16},{2,19},{3,18},{4,21},{5,20},{6,23},{7,22},{8,25},{9,... | collective-permute-start | bytes 442376 | tf_op jit(solution)/shard_map/ppermute | solution.py:335
  105.6 20.0 %collective-permute-start.29 = (bf16[64,1152]{1,0:T(8,128)(2,1)S(1)}, bf16[64,1152]{1,0:T(8,128)(2,1)}, u32[]{:S(2)}, u32[]{:S(2)}) collective-permute-start(bf16[64,1152]{1,0:T(8,128)(2,1)S(1)} %collective-permute-done.23.refs_1_.refs_3_), channel_id=1, source_target_pairs={{0,17},{1,16},{2,19},{3,18},{4,21},{5,20},{6,23},{7,22},{8,25},{9,... | collective-permute-start | bytes 442376 | tf_op jit(solution)/shard_map/ppermute | solution.py:335
  141.9 6.7 %copy-start.37 = (bf16[2,64,1152]{2,1,0:T(8,128)(2,1)S(1)}, bf16[2,64,1152]{2,1,0:T(8,128)(2,1)}, u32[]{:S(2)}) copy-start(bf16[2,64,1152]{2,1,0:T(8,128)(2,1)} %get-tuple-element.30) | copy-start | bytes 884740
  141.9 10.9 %copy-start.36 = (bf16[2,64,1152]{2,1,0:T(8,128)(2,1)S(1)}, bf16[2,64,1152]{2,1,0:T(8,128)(2,1)}, u32[]{:S(2)}) copy-start(bf16[2,64,1152]{2,1,0:T(8,128)(2,1)} %get-tuple-element.31) | copy-start | bytes 884740
  143.2 21.3 %collective-permute-start.35 = (f32[2,288,288]{2,1,0:T(8,128)S(1)}, f32[2,288,288]{2,1,0:T(8,128)S(1)}, u32[]{:S(2)}, u32[]{:S(2)}) collective-permute-start(f32[2,288,288]{2,1,0:T(8,128)S(1)} %dynamic-slice_bitcast_fusion), channel_id=1, source_target_pairs={{0,8},{1,9},{2,10},{3,11},{4,12},{5,13},{6,14},{7,15},{8,0},{9,1},... | collective-permute-start | bytes 1990664 | tf_op jit(solution)/shard_map/ppermute | solution.py:467
  143.3 5.3 %collective-permute-start.17 = (bf16[2,64,288]{2,1,0:T(8,128)(2,1)S(1)}, bf16[2,64,288]{2,1,0:T(8,128)(2,1)S(1)}, u32[]{:S(2)}, u32[]{:S(2)}) collective-permute-start(bf16[2,64,288]{2,1,0:T(8,128)(2,1)S(1)} %copy-done.28), channel_id=1, source_target_pairs={{0,1},{1,0},{2,3},{3,2},{4,5},{5,4},{6,7},{7,6},{8,9},{9,8},{10,11... | collective-permute-start | bytes 221192 | tf_op jit(solution)/shard_map/ppermute | solution.py:397
  145.0 7.7 %collective-permute-start.18 = (bf16[2,64,288]{2,1,0:T(8,128)(2,1)S(1)}, bf16[2,64,288]{2,1,0:T(8,128)(2,1)S(1)}, u32[]{:S(2)}, u32[]{:S(2)}) collective-permute-start(bf16[2,64,288]{2,1,0:T(8,128)(2,1)S(1)} %copy-done.27), channel_id=1, source_target_pairs={{0,16},{1,17},{2,18},{3,19},{4,20},{5,21},{6,22},{7,23},{8,24},{9,... | collective-permute-start | bytes 221192 | tf_op jit(solution)/shard_map/ppermute | solution.py:397
  145.1 7.7 %collective-permute-start.19 = (bf16[2,64,288]{2,1,0:T(8,128)(2,1)S(1)}, bf16[2,64,288]{2,1,0:T(8,128)(2,1)S(1)}, u32[]{:S(2)}, u32[]{:S(2)}) collective-permute-start(bf16[2,64,288]{2,1,0:T(8,128)(2,1)S(1)} %copy-done.26), channel_id=1, source_target_pairs={{0,17},{1,16},{2,19},{3,18},{4,21},{5,20},{6,23},{7,22},{8,25},{9,... | collective-permute-start | bytes 221192 | tf_op jit(solution)/shard_map/ppermute | solution.py:397
  146.8 28.5 %collective-permute-start.30 = (bf16[2,64,1152]{2,1,0:T(8,128)(2,1)}, bf16[2,64,1152]{2,1,0:T(8,128)(2,1)S(1)}, u32[]{:S(2)}, u32[]{:S(2)}) collective-permute-start(bf16[2,64,1152]{2,1,0:T(8,128)(2,1)} %get-tuple-element.29), channel_id=1, source_target_pairs={{0,1},{1,0},{2,3},{3,2},{4,5},{5,4},{6,7},{7,6},{8,9},{9,8},{10,11... | collective-permute-start | bytes 884744 | tf_op jit(solution)/shard_map/ppermute | solution.py:430
  148.5 26.8 %collective-permute-start.31 = (bf16[2,64,1152]{2,1,0:T(8,128)(2,1)S(1)}, bf16[2,64,1152]{2,1,0:T(8,128)(2,1)S(1)}, u32[]{:S(2)}, u32[]{:S(2)}) collective-permute-start(bf16[2,64,1152]{2,1,0:T(8,128)(2,1)S(1)} %copy-done.37), channel_id=1, source_target_pairs={{0,16},{1,17},{2,18},{3,19},{4,20},{5,21},{6,22},{7,23},{8,24},{9,... | collective-permute-start | bytes 884744 | tf_op jit(solution)/shard_map/ppermute | solution.py:430
  152.8 11.8 %copy-start.2 = (f32[4,288,288]{2,1,0:T(8,128)S(1)}, f32[4,288,288]{2,1,0:T(8,128)}, u32[]{:S(2)}) copy-start(f32[4,288,288]{2,1,0:T(8,128)} %get-tuple-element.34) | copy-start | bytes 3981316
  152.8 22.6 %collective-permute-start.32 = (bf16[2,64,1152]{2,1,0:T(8,128)(2,1)S(1)}, bf16[2,64,1152]{2,1,0:T(8,128)(2,1)S(1)}, u32[]{:S(2)}, u32[]{:S(2)}) collective-permute-start(bf16[2,64,1152]{2,1,0:T(8,128)(2,1)S(1)} %copy-done.36), channel_id=1, source_target_pairs={{0,17},{1,16},{2,19},{3,18},{4,21},{5,20},{6,23},{7,22},{8,25},{9,... | collective-permute-start | bytes 884744 | tf_op jit(solution)/shard_map/ppermute | solution.py:430
  158.4 16.1 %collective-permute-start.20 = (bf16[64,1152]{1,0:T(8,128)(2,1)}, bf16[64,1152]{1,0:T(8,128)(2,1)S(1)}, u32[]{:S(2)}, u32[]{:S(2)}) collective-permute-start(bf16[64,1152]{1,0:T(8,128)(2,1)} %get-tuple-element.23), channel_id=1, source_target_pairs={{0,0},{1,1},{16,2},{17,3},{8,4},{9,5},{24,6},{25,7},{4,8},{5,9},{2... | collective-permute-start | bytes 442376 | tf_op jit(solution)/shard_map/ppermute | solution.py:324
  164.5 10.8 %collective-permute-start.21 = (bf16[64,1152]{1,0:T(8,128)(2,1)}, bf16[64,1152]{1,0:T(8,128)(2,1)S(1)}, u32[]{:S(2)}, u32[]{:S(2)}) collective-permute-start(bf16[64,1152]{1,0:T(8,128)(2,1)} %get-tuple-element.24), channel_id=1, source_target_pairs={{8,0},{9,1},{24,2},{25,3},{0,4},{1,5},{16,6},{17,7},{12,8},{13,9},... | collective-permute-start | bytes 442376 | tf_op jit(solution)/shard_map/ppermute | solution.py:324
  174.5 11.1 %collective-permute-start.36 = (f32[288,288]{1,0:T(8,128)S(1)}, f32[288,288]{1,0:T(8,128)S(1)}, u32[]{:S(2)}, u32[]{:S(2)}) collective-permute-start(f32[288,288]{1,0:T(8,128)S(1)} %get-tuple-element.42), channel_id=1, source_target_pairs={{0,16},{1,17},{2,18},{3,19},{4,20},{5,21},{6,22},{7,23},{8,24},{9,... | collective-permute-start | bytes 995336 | tf_op jit(solution)/shard_map/ppermute | solution.py:469
  181.1 14.2 %collective-permute-start.33 = (bf16[64,1152]{1,0:T(8,128)(2,1)}, bf16[64,1152]{1,0:T(8,128)(2,1)S(1)}, u32[]{:S(2)}, u32[]{:S(2)}) collective-permute-start(bf16[64,1152]{1,0:T(8,128)(2,1)} %get-tuple-element.32), channel_id=1, source_target_pairs={{0,0},{1,1},{16,2},{17,3},{8,4},{9,5},{24,6},{25,7},{4,8},{5,9},{2... | collective-permute-start | bytes 442376 | tf_op jit(solution)/shard_map/ppermute | solution.py:324
  183.0 12.3 %collective-permute-start.34 = (bf16[64,1152]{1,0:T(8,128)(2,1)}, bf16[64,1152]{1,0:T(8,128)(2,1)S(1)}, u32[]{:S(2)}, u32[]{:S(2)}) collective-permute-start(bf16[64,1152]{1,0:T(8,128)(2,1)} %get-tuple-element.33), channel_id=1, source_target_pairs={{8,0},{9,1},{24,2},{25,3},{0,4},{1,5},{16,6},{17,7},{12,8},{13,9},... | collective-permute-start | bytes 442376 | tf_op jit(solution)/shard_map/ppermute | solution.py:324
  185.7 12.9 %collective-permute-start.37 = (f32[2,144,288]{2,1,0:T(8,128)S(1)}, f32[2,144,288]{2,1,0:T(8,128)S(1)}, u32[]{:S(2)}, u32[]{:S(2)}) collective-permute-start(f32[2,144,288]{2,1,0:T(8,128)S(1)} %get-tuple-element.40), channel_id=1, source_target_pairs={{0,1},{1,0},{2,3},{3,2},{4,5},{5,4},{6,7},{7,6},{8,9},{9,8},{10,11... | collective-permute-start | bytes 995336 | tf_op jit(solution)/shard_map/ppermute | solution.py:478
  198.7 10.0 %collective-permute-start.38 = (f32[144,288]{1,0:T(8,128)S(1)}, f32[144,288]{1,0:T(8,128)S(1)}, u32[]{:S(2)}, u32[]{:S(2)}) collective-permute-start(f32[144,288]{1,0:T(8,128)S(1)} %get-tuple-element.37), channel_id=1, source_target_pairs={{0,2},{1,3},{2,0},{3,1},{4,6},{5,7},{6,4},{7,5},{8,10},{9,11},{10,... | collective-permute-start | bytes 497672 | tf_op jit(solution)/shard_map/ppermute | solution.py:493
  198.8 18.8 %collective-permute-start.39 = (f32[144,288]{1,0:T(8,128)S(1)}, f32[144,288]{1,0:T(8,128)S(1)}, u32[]{:S(2)}, u32[]{:S(2)}) collective-permute-start(f32[144,288]{1,0:T(8,128)S(1)} %get-tuple-element.38), channel_id=1, source_target_pairs={{0,4},{1,5},{2,6},{3,7},{4,0},{5,1},{6,2},{7,3},{8,12},{9,13},{10,... | collective-permute-start | bytes 497672 | tf_op jit(solution)/shard_map/ppermute | solution.py:493
  198.9 18.6 %collective-permute-start.40 = (f32[144,288]{1,0:T(8,128)S(1)}, f32[144,288]{1,0:T(8,128)S(1)}, u32[]{:S(2)}, u32[]{:S(2)}) collective-permute-start(f32[144,288]{1,0:T(8,128)S(1)} %get-tuple-element.39), channel_id=1, source_target_pairs={{0,6},{1,7},{2,4},{3,5},{4,2},{5,3},{6,0},{7,1},{8,14},{9,15},{10,... | collective-permute-start | bytes 497672 | tf_op jit(solution)/shard_map/ppermute | solution.py:493
  (16 other events, 31.4 us)
Sparse Core Ops, SparseCore 0:
  42.2 44.3 all-gather.1

commit v2 on v1

v2 whole, which is shorter than its diff:
```python
import functools
import math

import jax
import jax.numpy as jnp
from jax import lax
from jax.experimental import pallas as pl
from jax.experimental.pallas import tpu as pltpu
from jax.sharding import Mesh, PartitionSpec as P

HEADS = 16
CORES = 2
AXES = ("y", "c", "z", "x")
BLOCK = 16
VMEM_LIMIT = 56 * 1024 * 1024
BF16 = jnp.bfloat16
F32 = jnp.float32


def dot(left, right):
    return jnp.dot(left, right, preferred_element_type=F32)


def dot_t(left, right):
    return lax.dot_general(left, right, (((1,), (1,)), ((), ())), preferred_element_type=F32)


def t_dot(left, right):
    return lax.dot_general(left, right, (((0,), (0,)), ((), ())), preferred_element_type=F32)


def normalize(values):
    centred = values - jnp.mean(values, axis=-1, keepdims=True)
    inv_sigma = lax.rsqrt(jnp.mean(centred * centred, axis=-1, keepdims=True) + 1e-06)
    return centred * inv_sigma, inv_sigma


class Layout:
    def __init__(self, mesh):
        groups, seq = mesh.shape["dp"], mesh.shape["seq"]
        self.nc = CORES
        self.ny = groups // CORES
        self.nz = groups
        self.nx = seq // self.nz
        self.chips = self.ny * self.nx
        self.frames = seq

    def linear(self, y, c, z, x):
        return ((y * self.nc + c) * self.nz + z) * self.nx + x

    def perm(self, move):
        pairs = []
        for y in range(self.ny):
            for c in range(self.nc):
                for z in range(self.nz):
                    for x in range(self.nx):
                        pairs.append((self.linear(y, c, z, x), self.linear(*move(y, c, z, x))))
        return pairs

    def to_plane(self, k):
        return self.perm(lambda y, c, z, x: (z % self.ny, (z // self.ny) ^ k, c * self.ny + y, x))

    def from_plane(self, k):
        return [(target, source) for source, target in self.to_plane(k)]

    def swap(self, ky=0, kc=0, kz=0, kx=0):
        return self.perm(lambda y, c, z, x: (y ^ ky, c ^ kc, z ^ kz, x ^ kx))

    def rows_to_chip(self):
        def move(y, c, z, x):
            s = z * self.nx + x
            chip, core = s // self.nc, s % self.nc
            return chip // self.nx, core, c * self.ny + y, chip % self.nx

        return self.perm(move)

    def to_owner(self, j):
        def move(y, c, z, x):
            s = self.nc * (y * self.nx + x) + c
            d = z ^ j
            return d // self.nc, d % self.nc, s // self.nx, s % self.nx

        return self.perm(move)

    def chip_of(self, k):
        return k // self.nx, k % self.nx

    def slots(self):
        return [(k, j) for k in range(self.chips) for j in range(self.nc)]


def slot_scalars(lay, pos_ref, info_ref, slot):
    k, j = slot
    ky, kx = lay.chip_of(k)
    z_frame = (pos_ref[1] ^ j) * lay.ny + (pos_ref[0] ^ ky)
    frame = z_frame * lay.nx + (pos_ref[3] ^ kx)
    clip = info_ref[frame]
    clips = (info_ref.shape[0] - lay.frames) // 2
    return clip, info_ref[lay.frames + clip], info_ref[lay.frames + clips + clip]


def table_row(mod_ref, step, part, width):
    return mod_ref[pl.ds(step, 1), part * width : (part + 1) * width]


def allowed_pairs(lay, pos_ref, info_ref, patch_base):
    rows = lay.frames * BLOCK
    row_slot = lax.broadcasted_iota(jnp.int32, (rows, 1), 0) // BLOCK
    col_slot = lax.broadcasted_iota(jnp.int32, (1, rows), 1) // BLOCK
    row_clip = jnp.zeros((rows, 1), jnp.int32)
    row_limit = jnp.zeros((rows, 1), jnp.int32)
    col_clip = jnp.zeros((1, rows), jnp.int32)
    for t, slot in enumerate(lay.slots()):
        clip, limit, _ = slot_scalars(lay, pos_ref, info_ref, slot)
        row_clip = jnp.where(row_slot == t, clip, row_clip)
        row_limit = jnp.where(row_slot == t, limit, row_limit)
        col_clip = jnp.where(col_slot == t, clip, col_clip)
    row_patch = lax.broadcasted_iota(jnp.int32, (rows, 1), 0) % BLOCK
    col_patch = lax.broadcasted_iota(jnp.int32, (1, rows), 1) % BLOCK
    row_key = row_clip * BLOCK + row_patch
    col_key = col_clip * BLOCK + col_patch
    row_valid = (patch_base + row_patch < row_limit).astype(jnp.int32)
    row_index = lax.broadcasted_iota(jnp.int32, (rows, rows), 0)
    col_index = lax.broadcasted_iota(jnp.int32, (rows, rows), 1)
    return (row_key == col_key) & ((row_valid > 0) | (row_index == col_index))


def head_mask(values, head, head_size):
    lane = lax.broadcasted_iota(jnp.int32, (1, values.shape[1]), 1)
    inside = (lane >= head * head_size) & (lane < (head + 1) * head_size)
    return jnp.where(inside, values, jnp.zeros_like(values))


def softmax(scores, allowed):
    scores = jnp.where(allowed, scores, -jnp.inf)
    exponent = jnp.exp(scores - jnp.max(scores, axis=0, keepdims=True))
    return exponent / jnp.sum(exponent, axis=0, keepdims=True)


def patch_blocks(array, block):
    part = array[:, block * BLOCK : (block + 1) * BLOCK, :]
    return part.reshape(part.shape[0] * BLOCK, part.shape[2])


def pick_kernel(lay, halves, cols, pos_ref, w_ref, *out_refs):
    model = w_ref.shape[1] // 3
    for k, out_ref in enumerate(out_refs):
        chip = pos_ref[0] * lay.nx + (pos_ref[3] ^ k)
        want = chip * halves + (pos_ref[1] if halves > 1 else 0)
        for v in range(lay.chips * halves):

            @pl.when(want == v)
            def _(v=v, out_ref=out_ref):
                parts = [
                    w_ref[:, p * model + v * cols : p * model + (v + 1) * cols].astype(F32)
                    for p in range(3)
                ]
                out_ref[...] = jnp.concatenate(parts, axis=1).astype(BF16)


def forward_kernel(lay, halves, half_heads, pos_ref, info_ref, *refs):
    x_refs, refs = refs[: lay.frames], refs[lay.frames :]
    w_refs, refs = refs[:halves], refs[halves:]
    mod_ref, q_ref, k_ref, v_ref, *refs = refs
    att_refs, (hid_scr,) = refs[: lay.chips], refs[lay.chips :]
    model = hid_scr.shape[1]
    cols = w_refs[0].shape[1] // 3
    head_size = cols // half_heads
    step_patches = x_refs[0].shape[0]
    patches = step_patches * pl.num_programs(0)

    for t, slot in enumerate(lay.slots()):
        _, _, step = slot_scalars(lay, pos_ref, info_ref, slot)
        normed, _ = normalize(x_refs[t][...].astype(F32))
        shift, scale = table_row(mod_ref, step, 0, model), table_row(mod_ref, step, 1, model)
        hid_scr[t * step_patches : (t + 1) * step_patches, :] = (
            normed * (1.0 + scale) + shift
        ).astype(BF16)

    for h in range(halves):
        triple = dot(hid_scr[...], w_refs[h][...])
        for n, ref in enumerate((q_ref, k_ref, v_ref)):
            ref[h] = triple[:, n * cols : (n + 1) * cols].astype(BF16).reshape(ref.shape[1:])

    for b in range(step_patches // BLOCK):
        patch_base = pos_ref[1] * patches + pl.program_id(0) * step_patches + b * BLOCK
        allowed = allowed_pairs(lay, pos_ref, info_ref, patch_base)
        outputs = []
        for h in range(halves):
            queries, keys, values = (patch_blocks(ref[h], b) for ref in (q_ref, k_ref, v_ref))
            output = jnp.zeros(queries.shape, F32)
            for head in range(half_heads):
                scores = dot_t(head_mask(keys, head, head_size), queries)
                weights = softmax(scores * (1.0 / math.sqrt(head_size)), allowed).astype(BF16)
                output = output + t_dot(weights, head_mask(values, head, head_size))
            outputs.append(output)
        if halves > 1:
            first = jnp.where(pos_ref[1] == 0, outputs[0], outputs[1])
            second = jnp.where(pos_ref[1] == 0, outputs[1], outputs[0])
            outputs = [jnp.concatenate([first, second], axis=1)]
        attended = outputs[0].astype(BF16).reshape(lay.frames, BLOCK, halves * cols)
        for k in range(lay.chips):
            att_refs[k][:, b * BLOCK : (b + 1) * BLOCK, :] = attended[k * lay.nc : (k + 1) * lay.nc]


def projection_grad_kernel(lay, halves, pos_ref, info_ref, *refs):
    g_refs, refs = refs[: lay.frames], refs[lay.frames :]
    att_refs, refs = refs[: lay.chips], refs[lay.chips :]
    wo_refs, refs = refs[: lay.nc], refs[lay.nc :]
    mod_ref, ga_ref, kept_ref, sent_ref, gp_scr, wo_scr, acc_scr = refs
    rows, model = gp_scr.shape
    step_patches = g_refs[0].shape[0]
    patches = step_patches * pl.num_programs(0)
    width = att_refs[0].shape[2]
    block_rows = width // lay.nc
    is_first = pos_ref[1] == 0

    @pl.when(pl.program_id(0) == 0)
    def _():
        acc_scr[...] = jnp.zeros_like(acc_scr)
        own, other = wo_refs[0][...].astype(F32), wo_refs[1][...].astype(F32)
        both = [jnp.where(is_first, own, other), jnp.where(is_first, other, own)]
        wo_scr[...] = jnp.concatenate(both, axis=0).astype(BF16)

    patch_base = pos_ref[1] * patches + pl.program_id(0) * step_patches
    patch = patch_base + lax.broadcasted_iota(jnp.int32, (step_patches, 1), 0)
    for t, slot in enumerate(lay.slots()):
        _, limit, step = slot_scalars(lay, pos_ref, info_ref, slot)
        factor = jnp.where(patch < limit, table_row(mod_ref, step, 2, model), 0.0)
        grad_proj = factor * g_refs[t][...].astype(F32)
        gp_scr[t * step_patches : (t + 1) * step_patches, :] = grad_proj.astype(BF16)

    attended = jnp.concatenate([ref[...] for ref in att_refs], axis=0).reshape(rows, width)
    acc_scr[...] += t_dot(attended, gp_scr[...])
    grad_attn = dot_t(gp_scr[...], wo_scr[...])
    part = width // halves
    for h in range(halves):
        ga_ref[h] = grad_attn[:, h * part : (h + 1) * part].astype(BF16).reshape(ga_ref.shape[1:])

    @pl.when(pl.program_id(0) == pl.num_programs(0) - 1)
    def _():
        first, second = acc_scr[:block_rows, :], acc_scr[block_rows:, :]
        kept_ref[...] = jnp.where(is_first, first, second)
        sent_ref[...] = jnp.where(is_first, second, first)


def spread_kernel(lay, pos_ref, kept_ref, got_ref, *refs):
    out_refs, scr = refs[:-1], refs[-1]
    total = kept_ref[...] + got_ref[...]
    part = scr.shape[2]
    for d in range(scr.shape[0]):
        scr[d] = total[:, d * part : (d + 1) * part]
    for j, ref in enumerate(out_refs):
        ref[...] = scr[pos_ref[2] ^ j]


def backward_kernel(lay, halves, half_heads, pos_ref, info_ref, *refs):
    w_refs, refs = refs[:halves], refs[halves:]
    q_ref, k_ref, v_ref, ga_ref, *refs = refs
    gh_refs, (gt_scr,) = refs[: lay.chips], refs[lay.chips :]
    _, frames, step_patches, cols = q_ref.shape
    model = w_refs[0].shape[0]
    head_size = cols // half_heads
    patches = step_patches * pl.num_programs(0)
    scaling = 1.0 / math.sqrt(head_size)

    for b in range(step_patches // BLOCK):
        patch_base = pos_ref[1] * patches + pl.program_id(0) * step_patches + b * BLOCK
        allowed = allowed_pairs(lay, pos_ref, info_ref, patch_base)
        for h in range(halves):
            queries, keys, values = (patch_blocks(ref[h], b) for ref in (q_ref, k_ref, v_ref))
            grad_out = patch_blocks(ga_ref[(pos_ref[1] ^ h) if halves > 1 else 0], b)
            grad_queries = jnp.zeros(queries.shape, F32)
            grad_keys = jnp.zeros(queries.shape, F32)
            grad_values = jnp.zeros(queries.shape, F32)
            for head in range(half_heads):
                k_head = head_mask(keys, head, head_size)
                g_head = head_mask(grad_out, head, head_size)
                weights = softmax(dot_t(k_head, queries) * scaling, allowed)
                grad_weights = dot_t(values, g_head)
                grad_values = grad_values + dot(weights.astype(BF16), g_head)
                inner = jnp.sum(weights * grad_weights, axis=0, keepdims=True)
                grad_scores = (weights * (grad_weights - inner) * scaling).astype(BF16)
                grad_queries = grad_queries + t_dot(grad_scores, k_head)
                grad_keys = grad_keys + dot(grad_scores, head_mask(queries, head, head_size))
            grads = jnp.concatenate([grad_queries, grad_keys, grad_values], axis=1).astype(BF16)
            gt_scr[h, :, b * BLOCK : (b + 1) * BLOCK, :] = grads.reshape(frames, BLOCK, 3 * cols)

    rows = lay.nc * step_patches
    for k in range(lay.chips):
        total = jnp.zeros((rows, model), F32)
        for h in range(halves):
            part = gt_scr[h, k * lay.nc : (k + 1) * lay.nc].reshape(rows, 3 * cols)
            total = total + dot_t(part, w_refs[h][...])
        gh_refs[k][...] = total.reshape(gh_refs[k].shape).astype(gh_refs[k].dtype)


def output_kernel(lay, pos_ref, info_ref, *refs):
    x_refs, refs = refs[: lay.nc], refs[lay.nc :]
    att_refs, refs = refs[: lay.chips], refs[lay.chips :]
    wo_ref, mod_ref, *out_refs = refs
    _, patches, width = att_refs[0].shape
    own_chip = pos_ref[0] * lay.nx + pos_ref[3]
    model = x_refs[0].shape[1]
    total = jnp.zeros((lay.nc * patches, model), F32)
    for k in range(lay.chips):
        total = total + dot(att_refs[k][...].reshape(lay.nc * patches, width), wo_ref[own_chip ^ k])
    patch = pos_ref[1] * patches + lax.broadcasted_iota(jnp.int32, (patches, 1), 0)
    for j in range(lay.nc):
        _, limit, step = slot_scalars(lay, pos_ref, info_ref, (0, j))
        factor = jnp.where(patch < limit, table_row(mod_ref, step, 2, model), 0.0)
        projected = total[j * patches : (j + 1) * patches].astype(BF16).astype(F32)
        out_refs[j][...] = (x_refs[j][...].astype(F32) + factor * projected).astype(BF16)


def input_grad_kernel(lay, pos_ref, info_ref, *refs):
    x_refs, refs = refs[: lay.nc], refs[lay.nc :]
    g_refs, refs = refs[: lay.nc], refs[lay.nc :]
    gh_refs, refs = refs[: lay.chips], refs[lay.chips :]
    mod_ref, *out_refs = refs
    model = x_refs[0].shape[1]
    for j in range(lay.nc):
        _, _, step = slot_scalars(lay, pos_ref, info_ref, (0, j))
        grad_hidden = gh_refs[0][j]
        for k in range(1, lay.chips):
            grad_hidden = grad_hidden + gh_refs[k][j].astype(F32)
        grad_hidden = grad_hidden.astype(BF16).astype(F32)
        normed, inv_sigma = normalize(x_refs[j][...].astype(F32))
        grad_norm = grad_hidden * (1.0 + table_row(mod_ref, step, 1, model))
        first_mean = jnp.mean(grad_norm, axis=-1, keepdims=True)
        second_mean = jnp.mean(grad_norm * normed, axis=-1, keepdims=True)
        grad_x = g_refs[j][...].astype(F32) + inv_sigma * (
            grad_norm - first_mean - normed * second_mean
        )
        out_refs[j][...] = grad_x.astype(BF16)


def whole_spec(shape):
    return pl.BlockSpec(shape, lambda *_: (0,) * len(shape))


def struct(shape, dtype=BF16):
    return jax.ShapeDtypeStruct(shape, dtype)


def local(lay, frames_x, grad_y, clip_ids, clip_patches, clip_step, mod_table, w_qkv, w_out):
    y, c, z, x = (lax.axis_index(name) for name in AXES)
    _, patches, model = frames_x.shape
    half = patches // lay.nc
    chips, nc, nx = lay.chips, lay.nc, lay.nx
    chip_heads = HEADS // chips
    head_size = model // HEADS
    halves = 2 if chip_heads % 2 == 0 else 1
    half_heads = chip_heads // halves
    cols = half_heads * head_size
    chip_width = chip_heads * head_size
    rows = w_qkv.shape[0]
    groups = lay.nz
    quarter = model // groups
    step_patches = max(BLOCK, min(half, 512 // lay.frames))
    steps = half // step_patches
    tokens = lay.frames * step_patches

    def call(kernel, name, in_specs, out_specs, out_shape, scratch=(), grid=(1,), prefetch=2):
        return pl.pallas_call(
            kernel,
            grid_spec=pltpu.PrefetchScalarGridSpec(
                num_scalar_prefetch=prefetch,
                grid=grid,
                in_specs=in_specs,
                out_specs=out_specs,
                scratch_shapes=list(scratch),
            ),
            out_shape=out_shape,
            compiler_params=pltpu.CompilerParams(vmem_limit_bytes=VMEM_LIMIT),
            name=name,
        )

    def chip_swap(k):
        ky, kx = lay.chip_of(k)
        return lay.swap(ky=ky, kx=kx)

    def over_chips(parts):
        own = [parts[0]]
        return own + [lax.ppermute(parts[k], AXES, chip_swap(k)) for k in range(1, chips)]

    def from_plane(parts):
        got = [lax.ppermute(part, AXES, lay.from_plane(k)) for k, part in enumerate(parts)]
        first = jnp.where(z // lay.ny == 0, got[0], got[1])
        second = jnp.where(z // lay.ny == 0, got[1], got[0])
        return jnp.concatenate([first, second], axis=0)[None]

    info = jnp.concatenate([clip_ids[0], clip_patches[0], clip_step[0]])[None]
    info = lax.ppermute(info, AXES, lay.to_plane(0))[0]
    pos = jnp.stack([y, c, z, x]).astype(jnp.int32)
    own = []
    for k in range(nc):
        start = ((z // lay.ny) ^ k) * half
        pair = [lax.dynamic_slice_in_dim(frame[0], start, half) for frame in (frames_x, grad_y)]
        own.append(lax.ppermute(jnp.concatenate(pair, axis=0), AXES, lay.to_plane(k)))
    by_slot = [over_chips([part] * chips) for part in own]
    frames = [by_slot[j][k] for k, j in lay.slots()]

    picked = call(
        functools.partial(pick_kernel, lay, halves, cols),
        "pick",
        [whole_spec(w_qkv.shape)],
        [whole_spec((rows, 3 * cols))] * nx,
        [struct((rows, 3 * cols))] * nx,
        prefetch=1,
    )(pos, w_qkv)
    by_x = [picked[0]] + [
        lax.ppermute(picked[kx], AXES, lay.swap(kx=kx)) for kx in range(1, nx)
    ]
    if nx == 2:
        ordered = [jnp.where(x == i, by_x[0], by_x[1]) for i in range(nx)]
    else:
        stacked = jnp.stack(by_x)
        ordered = [lax.dynamic_index_in_dim(stacked, x ^ i, 0, keepdims=False) for i in range(nx)]
    w_own = lax.all_gather(jnp.concatenate(ordered, axis=0), "z", axis=0, tiled=True)
    w_halves = [w_own]
    if halves > 1:
        w_halves.append(lax.ppermute(w_own, AXES, lay.swap(kc=1)))

    wo_own = lax.ppermute(w_out, AXES, lay.rows_to_chip())
    wo_rows = [wo_own, lax.ppermute(wo_own, AXES, lay.swap(kc=1))]
    late_w_out, _ = lax.optimization_barrier((w_out, w_own))
    wo = lax.all_gather(late_w_out, ("z", "x"), axis=0, tiled=True)
    wo = wo.reshape(chips, chip_width, model)

    x_spec = pl.BlockSpec((step_patches, model), lambda i, *_: (i, 0))
    g_spec = pl.BlockSpec((step_patches, model), lambda i, *_: (steps + i, 0))
    triple_spec = pl.BlockSpec((halves, lay.frames, step_patches, cols), lambda i, *_: (0, 0, i, 0))
    att_spec = pl.BlockSpec((nc, step_patches, chip_width), lambda i, *_: (0, i, 0))
    gh_spec = pl.BlockSpec((nc, step_patches, model), lambda i, *_: (0, i, 0))
    w_specs = [whole_spec((model, 3 * cols))] * halves
    mod_spec = whole_spec(mod_table.shape)
    triple_shape = struct((halves, lay.frames, half, cols))

    queries, keys, values, *att = call(
        functools.partial(forward_kernel, lay, halves, half_heads),
        "forward",
        [x_spec] * lay.frames + w_specs + [mod_spec],
        [triple_spec] * 3 + [att_spec] * chips,
        [triple_shape] * 3 + [struct((nc, half, chip_width))] * chips,
        [pltpu.VMEM((tokens, model), BF16)],
        (steps,),
    )(pos, info, *frames, *w_halves, mod_table)

    grad_attn, kept, sent = call(
        functools.partial(projection_grad_kernel, lay, halves),
        "projection_grad",
        [g_spec] * lay.frames + [att_spec] * chips + [whole_spec(w_out.shape)] * nc + [mod_spec],
        [triple_spec] + [whole_spec((rows, model))] * 2,
        [triple_shape] + [struct((rows, model), F32)] * 2,
        [
            pltpu.VMEM((tokens, model), BF16),
            pltpu.VMEM((chip_width, model), BF16),
            pltpu.VMEM((chip_width, model), F32),
        ],
        (steps,),
    )(pos, info, *frames, *att, *wo_rows, mod_table)
    got = lax.ppermute(sent, AXES, lay.swap(kc=1))
    att_own = over_chips(att)

    partial_sums = call(
        functools.partial(backward_kernel, lay, halves, half_heads),
        "backward",
        w_specs + [triple_spec] * 4,
        [gh_spec] * chips,
        [struct((nc, half, model), F32)] + [struct((nc, half, model))] * (chips - 1),
        [pltpu.VMEM((halves, lay.frames, step_patches, 3 * cols), BF16)],
        (steps,),
    )(pos, info, *w_halves, queries, keys, values, grad_attn)
    gh_own = over_chips(partial_sums)

    pieces = call(
        functools.partial(spread_kernel, lay),
        "spread",
        [whole_spec((rows, model))] * 2,
        [whole_spec((rows, quarter))] * groups,
        [struct((rows, quarter), F32)] * groups,
        [pltpu.VMEM((groups, rows, quarter), F32)],
        prefetch=1,
    )(pos, kept, got)
    pieces = [lax.ppermute(piece, AXES, lay.to_owner(j)) for j, piece in enumerate(pieces)]
    grad_w_out = sum(pieces[1:], pieces[0]) * jnp.float32(
        1.0 / math.sqrt(groups * lay.frames * patches)
    )

    def half_spec(start):
        return pl.BlockSpec((half, model), lambda *_: (start, 0))

    out_parts = call(
        functools.partial(output_kernel, lay),
        "output",
        [half_spec(0)] * nc
        + [whole_spec((nc, half, chip_width))] * chips
        + [whole_spec(wo.shape), mod_spec],
        [half_spec(0)] * nc,
        [struct((half, model))] * nc,
    )(pos, info, *own, *att_own, wo, mod_table)
    out_y = from_plane(out_parts)

    grad_parts = call(
        functools.partial(input_grad_kernel, lay),
        "input_grad",
        [x_spec] * nc + [g_spec] * nc + [gh_spec] * chips + [mod_spec],
        [x_spec] * nc,
        [struct((half, model))] * nc,
        grid=(steps,),
    )(pos, info, *own, *own, *gh_own, mod_table)
    grad_x = from_plane(grad_parts)
    return out_y, grad_x, grad_w_out


def solution(mesh):
    lay = Layout(mesh)
    grid = Mesh(mesh.devices.reshape(lay.ny, lay.nc, lay.nz, lay.nx), AXES)
    rows, cols = ("z", "x"), ("y", "c")
    frame = P(AXES, None, None)
    group = P(cols, None)
    return jax.shard_map(
        functools.partial(local, lay),
        mesh=grid,
        in_specs=(frame, frame, group, group, group, P(), P(rows, None), P(rows, None)),
        out_specs=(frame, frame, P(rows, cols)),
        check_vma=False,
    )
```

time: 229 us -> 264 us (1.15); the launches traced: 225 us -> 263 us
  waiting for transfers between devices: 60.8 us -> 138 us
  starting transfers between devices: 58.4 us -> 41.4 us
  local copies, waits for them, and re-layouts: 17.6 us -> 6.11 us
  blocking collectives: 32.6 us -> 24.4 us
    ppermute x36 -> x23, waiting for transfers between devices: 39.7 us -> 112 us  [the longest x4 48.8 us: local(): lax.ppermute(piece, AXES, lay.to_owner(j))]
    ppermute x36 -> x23, starting transfers between devices: 42.7 us -> 27.3 us  [the longest x12 10.3 us: over_chips(): lax.ppermute(parts[k], AXES, chip_swap(k))]
    ppermute x1, waiting for transfers between devices: 2.7 us -> 14.3 us  [local(): info = lax.ppermute(info, AXES, lay.to_plane(0))[0]]
    all_gather x1, blocking collectives: 32.6 us -> 24.4 us  [local(): lax.all_gather(jnp.concatenate(ordered, axis=0), 'z', axis=0, tiled=True)]
    ppermute x4, waiting for transfers between devices: 18.3 us -> 11.4 us  [from_plane(): lax.ppermute(part, AXES, lay.from_plane(k))]
    all_gather x2 -> x1, local copies, waits for them, and re-layouts: 6.4 us -> 1.53 us  [local(): lax.all_gather(jnp.concatenate(ordered, axis=0), 'z', axis=0, tiled=True)]
    pallas_call x4 -> x7, Pallas kernels: 37.6 us -> 35.1 us  [the longest x1 9.7 us: local(): call(functools.partial(backward_kernel, lay, halves, half_heads), 'backwa...]
  transfers between devices with their start and end apart: 42 -> 29, of which waited for: 13 -> 14; matrix products, arithmetic and copies ran while one was open for 6% -> 2% of each run, Pallas kernels for 10% -> 12%
where the time goes in v2:
time: 264 us; the launch traced here: 263 us
  waiting for transfers between devices  138 us (52%)
  starting transfers between devices  41.4 us (16%)
  Pallas kernels  35.1 us (13%)
  blocking collectives  24.4 us (9%)
  between operations  14.4 us (5%)
  local copies, waits for them, and re-layouts  6.11 us (2%)
  other arithmetic  4.04 us (2%)
    ppermute x4, waiting for transfers between devices, local(): lax.ppermute(piece, AXES, lay.to_owner(j))  48.8 us
    ppermute x12, waiting for transfers between devices, over_chips(): lax.ppermute(parts[k], AXES, chip_swap(k))  40.3 us
    all_gather x1, blocking collectives, local(): lax.all_gather(jnp.concatenate(ordered, axis=0), 'z', axis=0, tiled=True)  24.4 us
    ppermute x2, waiting for transfers between devices, local(): lax.ppermute(jnp.concatenate(pair, axis=0), AXES, lay.to_plane(k))  18.6 us
    ppermute x1, waiting for transfers between devices, local(): info = lax.ppermute(info, AXES, lay.to_plane(0))[0]  14.3 us
    ppermute x4, waiting for transfers between devices, from_plane(): lax.ppermute(part, AXES, lay.from_plane(k))  11.4 us
    ppermute x4, starting transfers between devices, from_plane(): lax.ppermute(part, AXES, lay.from_plane(k))  10.9 us
    ppermute x12, starting transfers between devices, over_chips(): lax.ppermute(parts[k], AXES, chip_swap(k))  10.3 us
  transfers between devices with their start and end apart: 29, of which 14 were waited for; matrix products, arithmetic and copies ran while one was open for 2% of the time, Pallas kernels for 12%

profile of v2, /device:TPU:4, one launch (start us, length us, event | category | flops | bytes accessed | tf_op | source)
XLA Modules:
  0.0 263.2 jit_solution(8110113171622338492)
XLA Ops:
  7.2 0.0 all-gather.2.cloned.1.call-start
  7.2 0.7 pad_add_fusion.pos_ref
  7.9 2.9 %pick.1 = (bf16[144,432]{1,0:T(8,128)(2,1)}, bf16[144,432]{1,0:T(8,128)(2,1)}) custom-call(s32[4]{0:T(128)} %pad_add_fusion.pos_ref, bf16[144,3456]{1,0:T(8,128)(2,1)} %w_ref.1), custom_call_target="tpu_custom_call" | custom-call | tf_op jit(solution)/shard_map/pick/pallas_call | solution.py:404
  10.8 1.5 collective-permute-start.9
  12.2 4.3 %collective-permute-done.9 = bf16[144,432]{1,0:T(8,128)(2,1)S(1)} collective-permute-done((bf16[144,432]{1,0:T(8,128)(2,1)}, bf16[144,432]{1,0:T(8,128)(2,1)S(1)}, u32[]{:S(2)}, u32[]{:S(2)}) %collective-permute-start.9) | collective-permute-done | bytes 124448 | tf_op jit(solution)/shard_map/ppermute | solution.py:413
  16.6 0.9 broadcast_select_fusion.1
  17.5 0.0 copy-start.10
  17.5 24.4 %all_gather.6.refs_8_.refs_0_ = bf16[1152,432]{1,0:T(8,128)(2,1)S(1)} all-gather(bf16[288,432]{1,0:T(8,128)(2,1)S(1)} %pad_maximum_fusion.2), channel_id=1, replica_groups=mesh['y'=2,'c'=2,'z'=4,'x'=2] {'z'}, dimensions={0}, use_global_device_ids=true | all-gather | bytes 1244160 | tf_op jit(solution)/shard_map/all_gather | solution.py:420
  41.9 0.0 all-gather.2.cloned.1.call-update
  42.0 0.0 copy-start.11
  42.0 0.0 copy-start.12
  42.0 2.1 collective-permute-start.16
  44.1 1.5 copy.11
  45.7 2.4 collective-permute-start.10
  48.1 0.7 collective-permute-start.2
  48.9 3.8 %collective-permute-start.1 = (bf16[128,1152]{1,0:T(8,128)(2,1)S(1)}, bf16[128,1152]{1,0:T(8,128)(2,1)S(1)}, u32[]{:S(2)}, u32[]{:S(2)}) collective-permute-start(bf16[128,1152]{1,0:T(8,128)(2,1)S(1)} %pad_maximum_fusion), channel_id=1, source_target_pairs={{0,0},{1,1},{2,16},{3,17},{4,8},{5,9},{6,24},{7,25},{8,4},{9,5},{1... | collective-permute-start | bytes 884744 | tf_op jit(solution)/shard_map/ppermute | solution.py:400
  52.7 0.1 add_bitcast_fusion
  52.8 3.1 %collective-permute-start = (s32[1,16]{1,0:T(1,128)S(1)}, s32[1,16]{1,0:T(1,128)S(1)}, u32[]{:S(2)}, u32[]{:S(2)}) collective-permute-start(s32[1,16]{1,0:T(1,128)S(1)} %add_bitcast_fusion), channel_id=1, source_target_pairs={{0,0},{1,1},{2,16},{3,17},{4,8},{5,9},{6,24},{7,25},{8,4},{9,5},{1... | collective-permute-start | bytes 200 | tf_op jit(solution)/shard_map/ppermute | solution.py:394
  55.9 18.6 %collective-permute-done.2.refs_1_.refs_3_ = bf16[128,1152]{1,0:T(8,128)(2,1)S(1)} collective-permute-done((bf16[128,1152]{1,0:T(8,128)(2,1)S(1)}, bf16[128,1152]{1,0:T(8,128)(2,1)S(1)}, u32[]{:S(2)}, u32[]{:S(2)}) %collective-permute-start.2) | collective-permute-done | bytes 294944 | tf_op jit(solution)/shard_map/ppermute | solution.py:400
  74.5 0.0 collective-permute-start.4
  74.5 14.3 %collective-permute-done = s32[1,16]{1,0:T(1,128)S(1)} collective-permute-done((s32[1,16]{1,0:T(1,128)S(1)}, s32[1,16]{1,0:T(1,128)S(1)}, u32[]{:S(2)}, u32[]{:S(2)}) %collective-permute-start) | collective-permute-done | bytes 96 | tf_op jit(solution)/shard_map/ppermute | solution.py:394
  88.9 0.0 collective-permute-start.6
  88.9 0.0 collective-permute-done.16.refs_12_
  88.9 0.1 collective-permute-start.17
  89.0 0.0 copy-start.2
  89.0 0.1 collective-permute-start.8
  89.1 3.4 %collective-permute-start.3 = (bf16[128,1152]{1,0:T(8,128)(2,1)S(1)}, bf16[128,1152]{1,0:T(8,128)(2,1)S(1)}, u32[]{:S(2)}, u32[]{:S(2)}) collective-permute-start(bf16[128,1152]{1,0:T(8,128)(2,1)S(1)} %collective-permute-done.1.refs_0_.refs_2_), channel_id=1, source_target_pairs={{0,1},{1,0},{2,3},{3,2},{4,5},{5,4},{6,7},{7,6},{8,9},{9,8},{10,11... | collective-permute-start | bytes 884744 | tf_op jit(solution)/shard_map/ppermute | solution.py:385
  92.5 5.6 %collective-permute-done.6.refs_5_ = bf16[128,1152]{1,0:T(8,128)(2,1)S(1)} collective-permute-done((bf16[128,1152]{1,0:T(8,128)(2,1)S(1)}, bf16[128,1152]{1,0:T(8,128)(2,1)S(1)}, u32[]{:S(2)}, u32[]{:S(2)}) %collective-permute-start.6) | collective-permute-done | bytes 294944 | tf_op jit(solution)/shard_map/ppermute | solution.py:385
  98.1 1.7 collective-permute-start.7
  99.8 1.6 copy.12.refs_9_.refs_1_
  101.4 4.7 %collective-permute-done.8.refs_7_ = bf16[128,1152]{1,0:T(8,128)(2,1)S(1)} collective-permute-done((bf16[128,1152]{1,0:T(8,128)(2,1)S(1)}, bf16[128,1152]{1,0:T(8,128)(2,1)S(1)}, u32[]{:S(2)}, u32[]{:S(2)}) %collective-permute-start.8) | collective-permute-done | bytes 294944 | tf_op jit(solution)/shard_map/ppermute | solution.py:385
  106.1 11.4 %collective-permute-done.3.refs_2_ = bf16[128,1152]{1,0:T(8,128)(2,1)S(1)} collective-permute-done((bf16[128,1152]{1,0:T(8,128)(2,1)S(1)}, bf16[128,1152]{1,0:T(8,128)(2,1)S(1)}, u32[]{:S(2)}, u32[]{:S(2)}) %collective-permute-start.3) | collective-permute-done | bytes 294944 | tf_op jit(solution)/shard_map/ppermute | solution.py:385
  117.5 4.7 %collective-permute-done.7.refs_6_ = bf16[128,1152]{1,0:T(8,128)(2,1)S(1)} collective-permute-done((bf16[128,1152]{1,0:T(8,128)(2,1)S(1)}, bf16[128,1152]{1,0:T(8,128)(2,1)S(1)}, u32[]{:S(2)}, u32[]{:S(2)}) %collective-permute-start.7) | collective-permute-done | bytes 294944 | tf_op jit(solution)/shard_map/ppermute | solution.py:385
  122.3 0.6 copy-done.8
  122.9 6.8 %forward.1 = (bf16[2,8,64,144]{3,2,1,0:T(8,128)(2,1)}, bf16[2,8,64,144]{3,2,1,0:T(8,128)(2,1)}, bf16[2,8,64,144]{3,2,1,0:T(8,128)(2,1)}, bf16[2,64,288]{2,1,0:T(...) custom-call(s32[4]{0:T(128)} %pad_add_fusion.pos_ref, ...), custom_call_target="tpu_custom_call" | custom-call | tf_op jit(solution)/shard_map/forward/pallas_call | solution.py:440
  129.7 4.6 %projection_grad.1 = (bf16[2,8,64,144]{3,2,1,0:T(8,128)(2,1)}, f32[144,1152]{1,0:T(8,128)}, f32[144,1152]{1,0:T(8,128)}) custom-call(s32[4]{0:T(128)} %pad_add_fusion.pos_ref, s32[16]{0:T(128)} %bitcast.25, bf16[128,1152]{1,0:T(8,128)(2,1)} %copy-done.2, bf16[128,1152]{1,0:T(8,128)(2,1)} %copy-done.1, bf16[128,1152]{1,0:T(8,128)(2,1)} %copy-done.6, ...), custom_call_target="tpu_custom_call" | custom-call | tf_op jit(solution)/shard_map/projection_grad/pallas_call | solution.py:450
  134.3 9.7 %backward.1 = (f32[2,64,1152]{2,1,0:T(8,128)}, bf16[2,64,1152]{2,1,0:T(8,128)(2,1)}, bf16[2,64,1152]{2,1,0:T(8,128)(2,1)}, bf16[2,64,1152]{2,1,0:T(8,128)(2,1)}) custom-call(s32[4]{0:T(128)} %pad_add_fusion.pos_ref, s32[16]{0:T(128)} %bitcast.26, bf16[1152,432]{1,0:T(8,128)(2,1)} %copy-done, bf16[1152,432]{1,0:T(8,128)(2,1)} %copy.12.refs_9_.refs_1_, ...), custom_call_target="tpu_custom_call" | custom-call | tf_op jit(solution)/shard_map/backward/pallas_call | solution.py:466
  144.0 1.2 collective-permute-start.18
  145.2 1.9 collective-permute-start.19
  147.1 1.5 collective-permute-start.20
  148.6 0.2 collective-permute-start.23
  148.8 5.3 %collective-permute-done.18.refs_5_ = bf16[2,64,1152]{2,1,0:T(8,128)(2,1)S(1)} collective-permute-done((bf16[2,64,1152]{2,1,0:T(8,128)(2,1)}, bf16[2,64,1152]{2,1,0:T(8,128)(2,1)S(1)}, u32[]{:S(2)}, u32[]{:S(2)}) %collective-permute-start.18) | collective-permute-done | bytes 294944 | tf_op jit(solution)/shard_map/ppermute | solution.py:385
  154.1 6.8 %collective-permute-done.19.refs_6_ = bf16[2,64,1152]{2,1,0:T(8,128)(2,1)S(1)} collective-permute-done((bf16[2,64,1152]{2,1,0:T(8,128)(2,1)}, bf16[2,64,1152]{2,1,0:T(8,128)(2,1)S(1)}, u32[]{:S(2)}, u32[]{:S(2)}) %collective-permute-start.19) | collective-permute-done | bytes 294944 | tf_op jit(solution)/shard_map/ppermute | solution.py:385
  160.9 1.8 collective-permute-done.20.refs_7_
  162.7 0.7 copy-done.15
  163.5 3.7 %input_grad.1 = (bf16[64,1152]{1,0:T(8,128)(2,1)}, bf16[64,1152]{1,0:T(8,128)(2,1)}) custom-call(s32[4]{0:T(128)} %pad_add_fusion.pos_ref, s32[16]{0:T(128)} %bitcast.27, bf16[128,1152]{1,0:T(8,128)(2,1)} %copy-done.2, bf16[128,1152]{1,0:T(8,128)(2,1)} %copy-done.1, bf16[128,1152]{1,0:T(8,128)(2,1)} %copy-done.2, bf16[128,1152]{1,0:T(8,128)(2,1)} %copy-done.1, ...), custom_call_target="tpu_custom_call" | custom-call | tf_op jit(solution)/shard_map/input_grad/pallas_call | solution.py:505
  167.1 2.1 collective-permute-start.21
  169.2 4.1 %collective-permute-start.22 = (bf16[64,1152]{1,0:T(8,128)(2,1)}, bf16[64,1152]{1,0:T(8,128)(2,1)S(1)}, u32[]{:S(2)}, u32[]{:S(2)}) collective-permute-start(bf16[64,1152]{1,0:T(8,128)(2,1)} %get-tuple-element.46), channel_id=1, source_target_pairs={{8,0},{9,1},{24,2},{25,3},{0,4},{1,5},{16,6},{17,7},{12,8},{13,9},... | collective-permute-start | bytes 442376 | tf_op jit(solution)/shard_map/ppermute | solution.py:388
  173.3 0.5 collective-permute-start.11
  173.8 9.5 %collective-permute-done.21 = bf16[64,1152]{1,0:T(8,128)(2,1)S(1)} collective-permute-done((bf16[64,1152]{1,0:T(8,128)(2,1)}, bf16[64,1152]{1,0:T(8,128)(2,1)S(1)}, u32[]{:S(2)}, u32[]{:S(2)}) %collective-permute-start.21) | collective-permute-done | bytes 147488 | tf_op jit(solution)/shard_map/ppermute | solution.py:388
  183.4 0.8 copy-done.9
  184.2 3.1 %spread.1 = (f32[144,288]{1,0:T(8,128)}, f32[144,288]{1,0:T(8,128)}, f32[144,288]{1,0:T(8,128)}, f32[144,288]{1,0:T(8,128)}) custom-call(s32[4]{0:T(128)} %pad_add_fusion.pos_ref, f32[144,1152]{1,0:T(8,128)} %get-tuple-element.47.kept_ref, f32[144,1152]{1,0:T(8,128)} %copy-done.9), custom_call_target="tpu_custom_call" | custom-call | tf_op jit(solution)/shard_map/spread/pallas_call | solution.py:477
  187.4 1.9 collective-permute-start.24
  189.3 4.3 %collective-permute-start.25 = (f32[144,288]{1,0:T(8,128)}, f32[144,288]{1,0:T(8,128)S(1)}, u32[]{:S(2)}, u32[]{:S(2)}) collective-permute-start(f32[144,288]{1,0:T(8,128)} %get-tuple-element.50), channel_id=1, source_target_pairs={{0,8},{1,10},{2,0},{3,2},{4,24},{5,26},{6,16},{7,18},{8,9},{9,11},... | collective-permute-start | bytes 497672 | tf_op jit(solution)/shard_map/ppermute | solution.py:486
  193.6 0.1 collective-permute-start.27
  193.7 0.7 maximum_bitcast_fusion.1
  194.4 0.6 copy-done.21
  195.1 4.3 %output.1 = (bf16[64,1152]{1,0:T(8,128)(2,1)}, bf16[64,1152]{1,0:T(8,128)(2,1)}) custom-call(s32[4]{0:T(128)} %pad_add_fusion.pos_ref, s32[16]{0:T(128)} %bitcast.28, bf16[128,1152]{1,0:T(8,128)(2,1)} %copy-done.2, bf16[128,1152]{1,0:T(8,128)(2,1)} %copy-done.1, bf16[2,64,288]{2,1,0:T(8,128)(2,1)} %get-tuple-element.30.refs_2_.refs_8_, ...), custom_call_target="tpu_custom_call" | custom-call | tf_op jit(solution)/shard_map/output/pallas_call | solution.py:494
  199.4 4.8 %collective-permute-start.14 = (bf16[64,1152]{1,0:T(8,128)(2,1)}, bf16[64,1152]{1,0:T(8,128)(2,1)S(1)}, u32[]{:S(2)}, u32[]{:S(2)}) collective-permute-start(bf16[64,1152]{1,0:T(8,128)(2,1)} %get-tuple-element.35), channel_id=1, source_target_pairs={{0,0},{1,1},{16,2},{17,3},{8,4},{9,5},{24,6},{25,7},{4,8},{5,9},{2... | collective-permute-start | bytes 442376 | tf_op jit(solution)/shard_map/ppermute | solution.py:388
  204.2 12.7 %collective-permute-done.24 = f32[144,288]{1,0:T(8,128)S(1)} collective-permute-done((f32[144,288]{1,0:T(8,128)}, f32[144,288]{1,0:T(8,128)S(1)}, u32[]{:S(2)}, u32[]{:S(2)}) %collective-permute-start.24) | collective-permute-done | bytes 165920 | tf_op jit(solution)/shard_map/ppermute | solution.py:486
  216.9 36.1 %collective-permute-done.27 = f32[144,288]{1,0:T(8,128)S(1)} collective-permute-done((f32[144,288]{1,0:T(8,128)}, f32[144,288]{1,0:T(8,128)S(1)}, u32[]{:S(2)}, u32[]{:S(2)}) %collective-permute-start.27) | collective-permute-done | bytes 165920 | tf_op jit(solution)/shard_map/ppermute | solution.py:486
  253.0 0.7 add_multiply_fusion
  253.7 1.9 collective-permute-done.14
  255.6 0.7 maximum_bitcast_fusion
  (71 shorter events, 0.3 us)
Async XLA Ops:
  7.2 187.3 %all-gather.2.cloned.1.call-start = ((), (), s32[]{:S(2)}) async-start(), calls=%async_computation | async-start | bytes 2985984 | tf_op jit(solution)/shard_map/all_gather | solution.py:428
  10.8 5.8 %collective-permute-start.9 = (bf16[144,432]{1,0:T(8,128)(2,1)}, bf16[144,432]{1,0:T(8,128)(2,1)S(1)}, u32[]{:S(2)}, u32[]{:S(2)}) collective-permute-start(bf16[144,432]{1,0:T(8,128)(2,1)} %get-tuple-element.29), channel_id=1, source_target_pairs={{0,1},{1,0},{2,3},{3,2},{4,5},{5,4},{6,7},{7,6},{8,9},{9,8},{10,11... | collective-permute-start | bytes 373256 | tf_op jit(solution)/shard_map/ppermute | solution.py:413
  17.5 24.5 %copy-start.10 = (bf16[144,1152]{1,0:T(8,128)(2,1)S(1)}, bf16[144,1152]{1,0:T(8,128)(2,1)}, u32[]{:S(2)}) copy-start(bf16[144,1152]{1,0:T(8,128)(2,1)} %param.15) | copy-start | bytes 995332
  41.9 3.7 %copy-start = (bf16[1152,432]{1,0:T(8,128)(2,1)}, bf16[1152,432]{1,0:T(8,128)(2,1)S(1)}, u32[]{:S(2)}) copy-start(bf16[1152,432]{1,0:T(8,128)(2,1)S(1)} %all_gather.6.refs_8_.refs_0_) | copy-start | bytes 2985988
  42.0 6.1 %copy-start.11 = (bf16[1,128,1152]{2,1,0:T(8,128)(2,1)S(1)}, bf16[1,128,1152]{2,1,0:T(8,128)(2,1)}, u32[]{:S(2)}) copy-start(bf16[1,128,1152]{2,1,0:T(8,128)(2,1)} %param.9) | copy-start | bytes 884740
  42.0 6.0 %copy-start.12 = (bf16[1,128,1152]{2,1,0:T(8,128)(2,1)S(1)}, bf16[1,128,1152]{2,1,0:T(8,128)(2,1)}, u32[]{:S(2)}) copy-start(bf16[1,128,1152]{2,1,0:T(8,128)(2,1)} %param.8) | copy-start | bytes 884740
  42.0 46.9 %collective-permute-start.16 = (bf16[144,1152]{1,0:T(8,128)(2,1)S(1)}, bf16[144,1152]{1,0:T(8,128)(2,1)}, u32[]{:S(2)}, u32[]{:S(2)}) collective-permute-start(bf16[144,1152]{1,0:T(8,128)(2,1)S(1)} %copy-done.10), channel_id=1, source_target_pairs={{0,0},{1,8},{2,1},{3,9},{4,16},{5,24},{6,17},{7,25},{8,4},{9,12},{... | collective-permute-start | bytes 995336 | tf_op jit(solution)/shard_map/ppermute | solution.py:425
  45.7 7.1 %copy-start.23 = (s32[1,4]{1,0:T(1,128)S(1)}, s32[1,4]{1,0:T(1,128)}, u32[]{:S(2)}) copy-start(s32[1,4]{1,0:T(1,128)} %param.12) | copy-start | bytes 52
  45.7 7.1 %copy-start.24 = (s32[1,4]{1,0:T(1,128)S(1)}, s32[1,4]{1,0:T(1,128)}, u32[]{:S(2)}) copy-start(s32[1,4]{1,0:T(1,128)} %param.11) | copy-start | bytes 52
  45.7 7.1 %copy-start.25 = (s32[1,8]{1,0:T(1,128)S(1)}, s32[1,8]{1,0:T(1,128)}, u32[]{:S(2)}) copy-start(s32[1,8]{1,0:T(1,128)} %param.10) | copy-start | bytes 100
  45.7 52.4 %collective-permute-start.10 = (bf16[1152,432]{0,1:T(8,128)(2,1)}, bf16[1152,432]{0,1:T(8,128)(2,1)S(1)}, u32[]{:S(2)}, u32[]{:S(2)}) collective-permute-start(bf16[1152,432]{0,1:T(8,128)(2,1)} %copy.11), channel_id=1, source_target_pairs={{0,8},{1,9},{2,10},{3,11},{4,12},{5,13},{6,14},{7,15},{8,0},{9,1},... | collective-permute-start | bytes 2985992 | tf_op jit(solution)/shard_map/ppermute | solution.py:423
  48.1 26.4 %collective-permute-start.2 = (bf16[128,1152]{1,0:T(8,128)(2,1)S(1)}, bf16[128,1152]{1,0:T(8,128)(2,1)S(1)}, u32[]{:S(2)}, u32[]{:S(2)}) collective-permute-start(bf16[128,1152]{1,0:T(8,128)(2,1)S(1)} %pad_maximum_fusion.1), channel_id=1, source_target_pairs={{0,8},{1,9},{2,24},{3,25},{4,0},{5,1},{6,16},{7,17},{8,12},{9,13},... | collective-permute-start | bytes 884744 | tf_op jit(solution)/shard_map/ppermute | solution.py:400
  48.9 40.1 %collective-permute-start.1 = (bf16[128,1152]{1,0:T(8,128)(2,1)S(1)}, bf16[128,1152]{1,0:T(8,128)(2,1)S(1)}, u32[]{:S(2)}, u32[]{:S(2)}) collective-permute-start(bf16[128,1152]{1,0:T(8,128)(2,1)S(1)} %pad_maximum_fusion), channel_id=1, source_target_pairs={{0,0},{1,1},{2,16},{3,17},{4,8},{5,9},{6,24},{7,25},{8,4},{9,5},{1... | collective-permute-start | bytes 884744 | tf_op jit(solution)/shard_map/ppermute | solution.py:400
  52.8 36.1 %collective-permute-start = (s32[1,16]{1,0:T(1,128)S(1)}, s32[1,16]{1,0:T(1,128)S(1)}, u32[]{:S(2)}, u32[]{:S(2)}) collective-permute-start(s32[1,16]{1,0:T(1,128)S(1)} %add_bitcast_fusion), channel_id=1, source_target_pairs={{0,0},{1,1},{2,16},{3,17},{4,8},{5,9},{6,24},{7,25},{8,4},{9,5},{1... | collective-permute-start | bytes 200 | tf_op jit(solution)/shard_map/ppermute | solution.py:394
  74.5 47.7 %copy-start.1 = (bf16[128,1152]{1,0:T(8,128)(2,1)}, bf16[128,1152]{1,0:T(8,128)(2,1)S(1)}, u32[]{:S(2)}) copy-start(bf16[128,1152]{1,0:T(8,128)(2,1)S(1)} %collective-permute-done.2.refs_1_.refs_3_) | copy-start | bytes 884740
  74.5 14.5 %collective-permute-start.4 = (bf16[128,1152]{1,0:T(8,128)(2,1)S(1)}, bf16[128,1152]{1,0:T(8,128)(2,1)S(1)}, u32[]{:S(2)}, u32[]{:S(2)}) collective-permute-start(bf16[128,1152]{1,0:T(8,128)(2,1)S(1)} %collective-permute-done.2.refs_1_.refs_3_), channel_id=1, source_target_pairs={{0,1},{1,0},{2,3},{3,2},{4,5},{5,4},{6,7},{7,6},{8,9},{9,8},{10,11... | collective-permute-start | bytes 884744 | tf_op jit(solution)/shard_map/ppermute | solution.py:385
  88.9 33.3 %copy-start.22 = (s32[1,16]{1,0:T(1,128)}, s32[1,16]{1,0:T(1,128)S(1)}, u32[]{:S(2)}) copy-start(s32[1,16]{1,0:T(1,128)S(1)} %collective-permute-done) | copy-start | bytes 196
  88.9 9.2 %collective-permute-start.6 = (bf16[128,1152]{1,0:T(8,128)(2,1)S(1)}, bf16[128,1152]{1,0:T(8,128)(2,1)S(1)}, u32[]{:S(2)}, u32[]{:S(2)}) collective-permute-start(bf16[128,1152]{1,0:T(8,128)(2,1)S(1)} %collective-permute-done.2.refs_1_.refs_3_), channel_id=1, source_target_pairs={{0,16},{1,17},{2,18},{3,19},{4,20},{5,21},{6,22},{7,23},{8,24},{9,... | collective-permute-start | bytes 884744 | tf_op jit(solution)/shard_map/ppermute | solution.py:385
  88.9 40.8 %collective-permute-start.17 = (bf16[144,1152]{1,0:T(8,128)(2,1)}, bf16[144,1152]{1,0:T(8,128)(2,1)}, u32[]{:S(2)}, u32[]{:S(2)}) collective-permute-start(bf16[144,1152]{1,0:T(8,128)(2,1)} %collective-permute-done.16.refs_12_), channel_id=1, source_target_pairs={{0,8},{1,9},{2,10},{3,11},{4,12},{5,13},{6,14},{7,15},{8,0},{9,1},... | collective-permute-start | bytes 995336 | tf_op jit(solution)/shard_map/ppermute | solution.py:426
  89.0 33.2 %copy-start.2 = (bf16[128,1152]{1,0:T(8,128)(2,1)}, bf16[128,1152]{1,0:T(8,128)(2,1)S(1)}, u32[]{:S(2)}) copy-start(bf16[128,1152]{1,0:T(8,128)(2,1)S(1)} %collective-permute-done.1.refs_0_.refs_2_) | copy-start | bytes 884740
  89.0 17.1 %collective-permute-start.8 = (bf16[128,1152]{1,0:T(8,128)(2,1)S(1)}, bf16[128,1152]{1,0:T(8,128)(2,1)S(1)}, u32[]{:S(2)}, u32[]{:S(2)}) collective-permute-start(bf16[128,1152]{1,0:T(8,128)(2,1)S(1)} %collective-permute-done.2.refs_1_.refs_3_), channel_id=1, source_target_pairs={{0,17},{1,16},{2,19},{3,18},{4,21},{5,20},{6,23},{7,22},{8,25},{9,... | collective-permute-start | bytes 884744 | tf_op jit(solution)/shard_map/ppermute | solution.py:385
  89.1 33.1 %copy-start.3 = (bf16[128,1152]{1,0:T(8,128)(2,1)}, bf16[128,1152]{1,0:T(8,128)(2,1)S(1)}, u32[]{:S(2)}) copy-start(bf16[128,1152]{1,0:T(8,128)(2,1)S(1)} %collective-permute-done.4.refs_3_) | copy-start | bytes 884740
  89.1 28.4 %collective-permute-start.3 = (bf16[128,1152]{1,0:T(8,128)(2,1)S(1)}, bf16[128,1152]{1,0:T(8,128)(2,1)S(1)}, u32[]{:S(2)}, u32[]{:S(2)}) collective-permute-start(bf16[128,1152]{1,0:T(8,128)(2,1)S(1)} %collective-permute-done.1.refs_0_.refs_2_), channel_id=1, source_target_pairs={{0,1},{1,0},{2,3},{3,2},{4,5},{5,4},{6,7},{7,6},{8,9},{9,8},{10,11... | collective-permute-start | bytes 884744 | tf_op jit(solution)/shard_map/ppermute | solution.py:385
  98.1 24.1 %copy-start.4 = (bf16[128,1152]{1,0:T(8,128)(2,1)}, bf16[128,1152]{1,0:T(8,128)(2,1)S(1)}, u32[]{:S(2)}) copy-start(bf16[128,1152]{1,0:T(8,128)(2,1)S(1)} %collective-permute-done.6.refs_5_) | copy-start | bytes 884740
  98.1 19.5 %collective-permute-start.5 = (bf16[128,1152]{1,0:T(8,128)(2,1)S(1)}, bf16[128,1152]{1,0:T(8,128)(2,1)S(1)}, u32[]{:S(2)}, u32[]{:S(2)}) collective-permute-start(bf16[128,1152]{1,0:T(8,128)(2,1)S(1)} %collective-permute-done.1.refs_0_.refs_2_), channel_id=1, source_target_pairs={{0,16},{1,17},{2,18},{3,19},{4,20},{5,21},{6,22},{7,23},{8,24},{9,... | collective-permute-start | bytes 884744 | tf_op jit(solution)/shard_map/ppermute | solution.py:385
  98.1 24.1 %collective-permute-start.7 = (bf16[128,1152]{1,0:T(8,128)(2,1)S(1)}, bf16[128,1152]{1,0:T(8,128)(2,1)S(1)}, u32[]{:S(2)}, u32[]{:S(2)}) collective-permute-start(bf16[128,1152]{1,0:T(8,128)(2,1)S(1)} %collective-permute-done.1.refs_0_.refs_2_), channel_id=1, source_target_pairs={{0,17},{1,16},{2,19},{3,18},{4,21},{5,20},{6,23},{7,22},{8,25},{9,... | collective-permute-start | bytes 884744 | tf_op jit(solution)/shard_map/ppermute | solution.py:385
  106.1 16.1 %copy-start.5 = (bf16[128,1152]{1,0:T(8,128)(2,1)}, bf16[128,1152]{1,0:T(8,128)(2,1)S(1)}, u32[]{:S(2)}) copy-start(bf16[128,1152]{1,0:T(8,128)(2,1)S(1)} %collective-permute-done.8.refs_7_) | copy-start | bytes 884740
  117.5 4.7 %copy-start.6 = (bf16[128,1152]{1,0:T(8,128)(2,1)}, bf16[128,1152]{1,0:T(8,128)(2,1)S(1)}, u32[]{:S(2)}) copy-start(bf16[128,1152]{1,0:T(8,128)(2,1)S(1)} %collective-permute-done.3.refs_2_) | copy-start | bytes 884740
  117.5 4.7 %copy-start.7 = (bf16[128,1152]{1,0:T(8,128)(2,1)}, bf16[128,1152]{1,0:T(8,128)(2,1)S(1)}, u32[]{:S(2)}) copy-start(bf16[128,1152]{1,0:T(8,128)(2,1)S(1)} %collective-permute-done.5.refs_4_) | copy-start | bytes 884740
  122.2 0.7 copy-start.8
  134.3 14.3 %copy-start.26 = (f32[144,1152]{1,0:T(8,128)S(1)}, f32[144,1152]{1,0:T(8,128)}, u32[]{:S(2)}) copy-start(f32[144,1152]{1,0:T(8,128)} %get-tuple-element.48) | copy-start | bytes 1990660
  144.0 10.1 %collective-permute-start.18 = (bf16[2,64,1152]{2,1,0:T(8,128)(2,1)}, bf16[2,64,1152]{2,1,0:T(8,128)(2,1)S(1)}, u32[]{:S(2)}, u32[]{:S(2)}) collective-permute-start(bf16[2,64,1152]{2,1,0:T(8,128)(2,1)} %get-tuple-element.42), channel_id=1, source_target_pairs={{0,1},{1,0},{2,3},{3,2},{4,5},{5,4},{6,7},{7,6},{8,9},{9,8},{10,11... | collective-permute-start | bytes 884744 | tf_op jit(solution)/shard_map/ppermute | solution.py:385
  145.2 15.7 %collective-permute-start.19 = (bf16[2,64,1152]{2,1,0:T(8,128)(2,1)}, bf16[2,64,1152]{2,1,0:T(8,128)(2,1)S(1)}, u32[]{:S(2)}, u32[]{:S(2)}) collective-permute-start(bf16[2,64,1152]{2,1,0:T(8,128)(2,1)} %get-tuple-element.43), channel_id=1, source_target_pairs={{0,16},{1,17},{2,18},{3,19},{4,20},{5,21},{6,22},{7,23},{8,24},{9,... | collective-permute-start | bytes 884744 | tf_op jit(solution)/shard_map/ppermute | solution.py:385
  147.1 15.6 %collective-permute-start.20 = (bf16[2,64,1152]{2,1,0:T(8,128)(2,1)}, bf16[2,64,1152]{2,1,0:T(8,128)(2,1)S(1)}, u32[]{:S(2)}, u32[]{:S(2)}) collective-permute-start(bf16[2,64,1152]{2,1,0:T(8,128)(2,1)} %get-tuple-element.44), channel_id=1, source_target_pairs={{0,17},{1,16},{2,19},{3,18},{4,21},{5,20},{6,23},{7,22},{8,25},{9,... | collective-permute-start | bytes 884744 | tf_op jit(solution)/shard_map/ppermute | solution.py:385
  148.6 34.7 %collective-permute-start.23 = (f32[144,1152]{1,0:T(8,128)S(1)}, f32[144,1152]{1,0:T(8,128)S(1)}, u32[]{:S(2)}, u32[]{:S(2)}) collective-permute-start(f32[144,1152]{1,0:T(8,128)S(1)} %copy-done.26), channel_id=1, source_target_pairs={{0,8},{1,9},{2,10},{3,11},{4,12},{5,13},{6,14},{7,15},{8,0},{9,1},... | collective-permute-start | bytes 1990664 | tf_op jit(solution)/shard_map/ppermute | solution.py:463
  154.1 8.6 %copy-start.13 = (bf16[2,64,1152]{2,1,0:T(8,128)(2,1)}, bf16[2,64,1152]{2,1,0:T(8,128)(2,1)S(1)}, u32[]{:S(2)}) copy-start(bf16[2,64,1152]{2,1,0:T(8,128)(2,1)S(1)} %collective-permute-done.18.refs_5_) | copy-start | bytes 884740
  160.9 1.8 copy-start.14
  162.7 0.7 copy-start.15
  163.4 9.8 %copy-start.18 = (bf16[2,64,288]{2,1,0:T(8,128)(2,1)S(1)}, bf16[2,64,288]{2,1,0:T(8,128)(2,1)}, u32[]{:S(2)}) copy-start(bf16[2,64,288]{2,1,0:T(8,128)(2,1)} %get-tuple-element.31.refs_9_) | copy-start | bytes 221188
  163.4 10.4 %copy-start.17 = (bf16[2,64,288]{2,1,0:T(8,128)(2,1)S(1)}, bf16[2,64,288]{2,1,0:T(8,128)(2,1)}, u32[]{:S(2)}) copy-start(bf16[2,64,288]{2,1,0:T(8,128)(2,1)} %get-tuple-element.32.refs_10_) | copy-start | bytes 221188
  163.5 19.9 %copy-start.16 = (bf16[2,64,288]{2,1,0:T(8,128)(2,1)S(1)}, bf16[2,64,288]{2,1,0:T(8,128)(2,1)}, u32[]{:S(2)}) copy-start(bf16[2,64,288]{2,1,0:T(8,128)(2,1)} %get-tuple-element.33.refs_11_) | copy-start | bytes 221188
  167.1 16.2 %collective-permute-start.21 = (bf16[64,1152]{1,0:T(8,128)(2,1)}, bf16[64,1152]{1,0:T(8,128)(2,1)S(1)}, u32[]{:S(2)}, u32[]{:S(2)}) collective-permute-start(bf16[64,1152]{1,0:T(8,128)(2,1)} %get-tuple-element.45), channel_id=1, source_target_pairs={{0,0},{1,1},{16,2},{17,3},{8,4},{9,5},{24,6},{25,7},{4,8},{5,9},{2... | collective-permute-start | bytes 442376 | tf_op jit(solution)/shard_map/ppermute | solution.py:388
  169.2 14.1 %collective-permute-start.22 = (bf16[64,1152]{1,0:T(8,128)(2,1)}, bf16[64,1152]{1,0:T(8,128)(2,1)S(1)}, u32[]{:S(2)}, u32[]{:S(2)}) collective-permute-start(bf16[64,1152]{1,0:T(8,128)(2,1)} %get-tuple-element.46), channel_id=1, source_target_pairs={{8,0},{9,1},{24,2},{25,3},{0,4},{1,5},{16,6},{17,7},{12,8},{13,9},... | collective-permute-start | bytes 442376 | tf_op jit(solution)/shard_map/ppermute | solution.py:388
  173.3 20.3 %collective-permute-start.11 = (bf16[2,64,288]{2,1,0:T(8,128)(2,1)S(1)}, bf16[2,64,288]{2,1,0:T(8,128)(2,1)S(1)}, u32[]{:S(2)}, u32[]{:S(2)}) collective-permute-start(bf16[2,64,288]{2,1,0:T(8,128)(2,1)S(1)} %copy-done.18), channel_id=1, source_target_pairs={{0,1},{1,0},{2,3},{3,2},{4,5},{5,4},{6,7},{7,6},{8,9},{9,8},{10,11... | collective-permute-start | bytes 221192 | tf_op jit(solution)/shard_map/ppermute | solution.py:385
  173.8 19.8 %collective-permute-start.12 = (bf16[2,64,288]{2,1,0:T(8,128)(2,1)S(1)}, bf16[2,64,288]{2,1,0:T(8,128)(2,1)S(1)}, u32[]{:S(2)}, u32[]{:S(2)}) collective-permute-start(bf16[2,64,288]{2,1,0:T(8,128)(2,1)S(1)} %copy-done.17), channel_id=1, source_target_pairs={{0,16},{1,17},{2,18},{3,19},{4,20},{5,21},{6,22},{7,23},{8,24},{9,... | collective-permute-start | bytes 221192 | tf_op jit(solution)/shard_map/ppermute | solution.py:385
  183.3 11.1 %collective-permute-start.13 = (bf16[2,64,288]{2,1,0:T(8,128)(2,1)S(1)}, bf16[2,64,288]{2,1,0:T(8,128)(2,1)S(1)}, u32[]{:S(2)}, u32[]{:S(2)}) collective-permute-start(bf16[2,64,288]{2,1,0:T(8,128)(2,1)S(1)} %copy-done.16), channel_id=1, source_target_pairs={{0,17},{1,16},{2,19},{3,18},{4,21},{5,20},{6,23},{7,22},{8,25},{9,... | collective-permute-start | bytes 221192 | tf_op jit(solution)/shard_map/ppermute | solution.py:385
  183.4 0.9 copy-start.9
  187.4 29.5 %collective-permute-start.24 = (f32[144,288]{1,0:T(8,128)}, f32[144,288]{1,0:T(8,128)S(1)}, u32[]{:S(2)}, u32[]{:S(2)}) collective-permute-start(f32[144,288]{1,0:T(8,128)} %get-tuple-element.49), channel_id=1, source_target_pairs={{0,0},{1,2},{2,8},{3,10},{4,16},{5,18},{6,24},{7,26},{8,1},{9,3},{... | collective-permute-start | bytes 497672 | tf_op jit(solution)/shard_map/ppermute | solution.py:486
  189.3 27.6 %collective-permute-start.25 = (f32[144,288]{1,0:T(8,128)}, f32[144,288]{1,0:T(8,128)S(1)}, u32[]{:S(2)}, u32[]{:S(2)}) collective-permute-start(f32[144,288]{1,0:T(8,128)} %get-tuple-element.50), channel_id=1, source_target_pairs={{0,8},{1,10},{2,0},{3,2},{4,24},{5,26},{6,16},{7,18},{8,9},{9,11},... | collective-permute-start | bytes 497672 | tf_op jit(solution)/shard_map/ppermute | solution.py:486
  193.6 0.8 copy-start.19
  193.6 23.3 %collective-permute-start.26 = (f32[144,288]{1,0:T(8,128)}, f32[144,288]{1,0:T(8,128)S(1)}, u32[]{:S(2)}, u32[]{:S(2)}) collective-permute-start(f32[144,288]{1,0:T(8,128)} %get-tuple-element.51), channel_id=1, source_target_pairs={{0,16},{1,18},{2,24},{3,26},{4,0},{5,2},{6,8},{7,10},{8,17},{9,19}... | collective-permute-start | bytes 497672 | tf_op jit(solution)/shard_map/ppermute | solution.py:486
  193.6 0.8 copy-start.20
  193.6 59.4 %collective-permute-start.27 = (f32[144,288]{1,0:T(8,128)}, f32[144,288]{1,0:T(8,128)S(1)}, u32[]{:S(2)}, u32[]{:S(2)}) collective-permute-start(f32[144,288]{1,0:T(8,128)} %get-tuple-element.52), channel_id=1, source_target_pairs={{0,24},{1,26},{2,16},{3,18},{4,8},{5,10},{6,0},{7,2},{8,25},{9,27}... | collective-permute-start | bytes 497672 | tf_op jit(solution)/shard_map/ppermute | solution.py:486
  194.4 0.6 copy-start.21
  199.4 56.2 %collective-permute-start.14 = (bf16[64,1152]{1,0:T(8,128)(2,1)}, bf16[64,1152]{1,0:T(8,128)(2,1)S(1)}, u32[]{:S(2)}, u32[]{:S(2)}) collective-permute-start(bf16[64,1152]{1,0:T(8,128)(2,1)} %get-tuple-element.35), channel_id=1, source_target_pairs={{0,0},{1,1},{16,2},{17,3},{8,4},{9,5},{24,6},{25,7},{4,8},{5,9},{2... | collective-permute-start | bytes 442376 | tf_op jit(solution)/shard_map/ppermute | solution.py:388
  216.9 38.7 %collective-permute-start.15 = (bf16[64,1152]{1,0:T(8,128)(2,1)}, bf16[64,1152]{1,0:T(8,128)(2,1)S(1)}, u32[]{:S(2)}, u32[]{:S(2)}) collective-permute-start(bf16[64,1152]{1,0:T(8,128)(2,1)} %get-tuple-element.36), channel_id=1, source_target_pairs={{8,0},{9,1},{24,2},{25,3},{0,4},{1,5},{16,6},{17,7},{12,8},{13,9},... | collective-permute-start | bytes 442376 | tf_op jit(solution)/shard_map/ppermute | solution.py:388
Sparse Core Ops, SparseCore 0:
  42.1 86.2 all-gather.1

commit v3 on v2

v3 whole, which is shorter than its diff:
```python
import functools
import math

import jax
import jax.numpy as jnp
from jax import lax
from jax.experimental import pallas as pl
from jax.experimental.pallas import tpu as pltpu
from jax.sharding import Mesh, PartitionSpec as P

HEADS = 16
CORES = 2
AXES = ("y", "c", "z", "x")
BLOCK = 16
VMEM_LIMIT = 56 * 1024 * 1024
BF16 = jnp.bfloat16
F32 = jnp.float32


def dot(left, right):
    return jnp.dot(left, right, preferred_element_type=F32)


def dot_t(left, right):
    return lax.dot_general(left, right, (((1,), (1,)), ((), ())), preferred_element_type=F32)


def t_dot(left, right):
    return lax.dot_general(left, right, (((0,), (0,)), ((), ())), preferred_element_type=F32)


def normalize(values):
    centred = values - jnp.mean(values, axis=-1, keepdims=True)
    inv_sigma = lax.rsqrt(jnp.mean(centred * centred, axis=-1, keepdims=True) + 1e-06)
    return centred * inv_sigma, inv_sigma


class Layout:
    def __init__(self, mesh):
        groups, seq = mesh.shape["dp"], mesh.shape["seq"]
        self.nc = CORES
        self.ny = groups // CORES
        self.nz = groups
        self.nx = seq // self.nz
        self.chips = self.ny * self.nx
        self.frames = seq
        self.chip_heads = HEADS // self.chips
        self.halves = 2 if self.chip_heads % 2 == 0 else 1
        self.half_heads = self.chip_heads // self.halves

    def linear(self, y, c, z, x):
        return ((y * self.nc + c) * self.nz + z) * self.nx + x

    def perm(self, move):
        pairs = []
        for y in range(self.ny):
            for c in range(self.nc):
                for z in range(self.nz):
                    for x in range(self.nx):
                        pairs.append((self.linear(y, c, z, x), self.linear(*move(y, c, z, x))))
        return pairs

    def to_plane(self, k):
        return self.perm(lambda y, c, z, x: (z % self.ny, (z // self.ny) ^ k, c * self.ny + y, x))

    def from_plane(self, k):
        return [(target, source) for source, target in self.to_plane(k)]

    def swap(self, ky=0, kc=0, kz=0, kx=0):
        return self.perm(lambda y, c, z, x: (y ^ ky, c ^ kc, z ^ kz, x ^ kx))

    def row_block(self, y, x, i):
        if self.halves > 1:
            return (i * self.ny + y) * self.nx + x
        return self.nc * (y * self.nx + x) + i

    def rows_to_chip(self):
        reader = {
            self.row_block(y, x, i): (y, x, i)
            for y in range(self.ny)
            for x in range(self.nx)
            for i in range(self.nc)
        }

        def move(y, c, z, x):
            chip_y, chip_x, i = reader[z * self.nx + x]
            return chip_y, i, c * self.ny + y, chip_x

        return self.perm(move)

    def to_owner(self, j):
        def move(y, c, z, x):
            s = self.row_block(y, x, c)
            d = z ^ j
            return d // self.nc, d % self.nc, s // self.nx, s % self.nx

        return self.perm(move)

    def chip_of(self, k):
        return k // self.nx, k % self.nx

    def slots(self):
        return [(k, j) for k in range(self.chips) for j in range(self.nc)]


def slot_scalars(lay, pos_ref, info_ref, slot):
    k, j = slot
    ky, kx = lay.chip_of(k)
    z_frame = (pos_ref[1] ^ j) * lay.ny + (pos_ref[0] ^ ky)
    frame = z_frame * lay.nx + (pos_ref[3] ^ kx)
    clip = info_ref[frame]
    clips = (info_ref.shape[0] - lay.frames) // 2
    return clip, info_ref[lay.frames + clip], info_ref[lay.frames + clips + clip]


def table_row(mod_ref, step, part, width):
    return mod_ref[pl.ds(step, 1), part * width : (part + 1) * width]


def allowed_pairs(lay, pos_ref, info_ref, patch_base):
    rows = lay.frames * BLOCK
    row_slot = lax.broadcasted_iota(jnp.int32, (rows, 1), 0) // BLOCK
    col_slot = lax.broadcasted_iota(jnp.int32, (1, rows), 1) // BLOCK
    row_clip = jnp.zeros((rows, 1), jnp.int32)
    row_limit = jnp.zeros((rows, 1), jnp.int32)
    col_clip = jnp.zeros((1, rows), jnp.int32)
    for t, slot in enumerate(lay.slots()):
        clip, limit, _ = slot_scalars(lay, pos_ref, info_ref, slot)
        row_clip = jnp.where(row_slot == t, clip, row_clip)
        row_limit = jnp.where(row_slot == t, limit, row_limit)
        col_clip = jnp.where(col_slot == t, clip, col_clip)
    row_patch = lax.broadcasted_iota(jnp.int32, (rows, 1), 0) % BLOCK
    col_patch = lax.broadcasted_iota(jnp.int32, (1, rows), 1) % BLOCK
    row_key = row_clip * BLOCK + row_patch
    col_key = col_clip * BLOCK + col_patch
    row_valid = (patch_base + row_patch < row_limit).astype(jnp.int32)
    row_index = lax.broadcasted_iota(jnp.int32, (rows, rows), 0)
    col_index = lax.broadcasted_iota(jnp.int32, (rows, rows), 1)
    return (row_key == col_key) & ((row_valid > 0) | (row_index == col_index))


def head_mask(values, head, head_size):
    lane = lax.broadcasted_iota(jnp.int32, (1, values.shape[1]), 1)
    inside = (lane >= head * head_size) & (lane < (head + 1) * head_size)
    return jnp.where(inside, values, jnp.zeros_like(values))


def patch_blocks(array, block):
    part = array[:, block * BLOCK : (block + 1) * BLOCK, :]
    return part.reshape(part.shape[0] * BLOCK, part.shape[2])


def pick_kernel(lay, cols, pos_ref, w_ref, *out_refs):
    model = w_ref.shape[1] // 3
    for k, out_ref in enumerate(out_refs):
        chip_x = pos_ref[3] ^ k
        if lay.halves > 1:
            want = lay.row_block(pos_ref[0], chip_x, pos_ref[1])
        else:
            want = pos_ref[0] * lay.nx + chip_x
        for v in range(lay.chips * lay.halves):

            @pl.when(want == v)
            def _(v=v, out_ref=out_ref):
                parts = [
                    w_ref[:, p * model + v * cols : p * model + (v + 1) * cols].astype(F32)
                    for p in range(3)
                ]
                out_ref[...] = jnp.concatenate(parts, axis=1).astype(BF16)


def fill_weights(lay, pos_ref, w_refs, w_scr):
    rows = w_refs[0].shape[0]
    for h in range(lay.halves):
        for k in range(lay.nz):
            start = pl.multiple_of((pos_ref[2] ^ k) * rows, 16)
            w_scr[h, pl.ds(start, rows), :] = w_refs[h * lay.nz + k][...]


def heads_stacked(lay, values):
    head_size = values.shape[1] // lay.half_heads
    parts = [head_mask(values, head, head_size) for head in range(lay.half_heads)]
    return jnp.concatenate(parts, axis=0) if len(parts) > 1 else parts[0]


def beside(lay, weights):
    return jnp.concatenate([weights[head] for head in range(lay.half_heads)], axis=1)


def attention_weights(lay, keys_stacked, queries, allowed, scaling):
    scores = dot_t(keys_stacked, queries) * scaling
    scores = jnp.where(allowed, scores.reshape((lay.half_heads,) + allowed.shape), -jnp.inf)
    exponent = jnp.exp(scores - jnp.max(scores, axis=1, keepdims=True))
    return exponent / jnp.sum(exponent, axis=1, keepdims=True)


def forward_kernel(lay, pos_ref, info_ref, *refs):
    x_refs, refs = refs[: lay.frames], refs[lay.frames :]
    w_refs, refs = refs[: lay.halves * lay.nz], refs[lay.halves * lay.nz :]
    mod_ref, q_ref, k_ref, v_ref, att_ref, w_scr, hid_scr = refs
    model = hid_scr.shape[1]
    cols = w_scr.shape[2] // 3
    scaling = 1.0 / math.sqrt(cols // lay.half_heads)
    step_patches = x_refs[0].shape[0]
    patches = step_patches * pl.num_programs(0)

    @pl.when(pl.program_id(0) == 0)
    def _():
        fill_weights(lay, pos_ref, w_refs, w_scr)

    for t, slot in enumerate(lay.slots()):
        _, _, step = slot_scalars(lay, pos_ref, info_ref, slot)
        normed, _ = normalize(x_refs[t][...].astype(F32))
        shift, scale = table_row(mod_ref, step, 0, model), table_row(mod_ref, step, 1, model)
        hid_scr[t * step_patches : (t + 1) * step_patches, :] = (
            normed * (1.0 + scale) + shift
        ).astype(BF16)

    for h in range(lay.halves):
        triple = dot(hid_scr[...], w_scr[h])
        for n, ref in enumerate((q_ref, k_ref, v_ref)):
            ref[h] = triple[:, n * cols : (n + 1) * cols].astype(BF16).reshape(ref.shape[1:])

    for b in range(step_patches // BLOCK):
        patch_base = pos_ref[1] * patches + pl.program_id(0) * step_patches + b * BLOCK
        allowed = allowed_pairs(lay, pos_ref, info_ref, patch_base)
        outputs = []
        for h in range(lay.halves):
            queries, keys, values = (patch_blocks(ref[h], b) for ref in (q_ref, k_ref, v_ref))
            weights = attention_weights(lay, heads_stacked(lay, keys), queries, allowed, scaling)
            weights = weights.astype(BF16).reshape(-1, allowed.shape[1])
            outputs.append(t_dot(weights, heads_stacked(lay, values)))
        if lay.halves > 1:
            first = jnp.where(pos_ref[1] == 0, outputs[0], outputs[1])
            second = jnp.where(pos_ref[1] == 0, outputs[1], outputs[0])
            outputs = [jnp.concatenate([first, second], axis=1)]
        attended = outputs[0].astype(BF16)
        att_ref[:, b * BLOCK : (b + 1) * BLOCK, :] = attended.reshape(lay.frames, BLOCK, -1)


def weight_grad_kernel(lay, pos_ref, info_ref, *refs):
    g_refs, refs = refs[: lay.frames], refs[lay.frames :]
    att_ref, mod_ref, gp_ref, kept_ref, sent_ref, acc_scr = refs
    _, step_patches, model = gp_ref.shape
    tokens = lay.frames * step_patches
    patches = step_patches * pl.num_programs(0)
    groups, block_rows, part = kept_ref.shape
    is_first = pos_ref[1] == 0

    @pl.when(pl.program_id(0) == 0)
    def _():
        acc_scr[...] = jnp.zeros_like(acc_scr)

    patch_base = pos_ref[1] * patches + pl.program_id(0) * step_patches
    patch = patch_base + lax.broadcasted_iota(jnp.int32, (step_patches, 1), 0)
    for t, slot in enumerate(lay.slots()):
        _, limit, step = slot_scalars(lay, pos_ref, info_ref, slot)
        factor = jnp.where(patch < limit, table_row(mod_ref, step, 2, model), 0.0)
        gp_ref[t] = (factor * g_refs[t][...].astype(F32)).astype(BF16)

    attended = att_ref[...].reshape(tokens, -1)
    acc_scr[...] += t_dot(attended, gp_ref[...].reshape(tokens, model))

    @pl.when(pl.program_id(0) == pl.num_programs(0) - 1)
    def _():
        first, second = acc_scr[:block_rows, :], acc_scr[block_rows:, :]
        kept = jnp.where(is_first, first, second)
        sent = jnp.where(is_first, second, first)
        for d in range(groups):
            kept_ref[pos_ref[2] ^ d] = kept[:, d * part : (d + 1) * part]
            sent_ref[pos_ref[2] ^ d] = sent[:, d * part : (d + 1) * part]


def projection_kernel(lay, pos_ref, gp_ref, att_ref, *refs):
    wo_refs, refs = refs[: lay.nc], refs[lay.nc :]
    ga_ref, *refs = refs
    pr_refs, (wo_scr,) = refs[: lay.chips], refs[lay.chips :]
    _, step_patches, model = gp_ref.shape
    tokens = lay.frames * step_patches
    is_first = pos_ref[1] == 0

    @pl.when(pl.program_id(0) == 0)
    def _():
        own, other = wo_refs[0][...].astype(F32), wo_refs[1][...].astype(F32)
        both = [jnp.where(is_first, own, other), jnp.where(is_first, other, own)]
        wo_scr[...] = jnp.concatenate(both, axis=0).astype(BF16)

    grad_attn = dot_t(gp_ref[...].reshape(tokens, model), wo_scr[...])
    part = wo_scr.shape[0] // lay.halves
    for h in range(lay.halves):
        ga_ref[h] = grad_attn[:, h * part : (h + 1) * part].astype(BF16).reshape(ga_ref.shape[1:])
    attended = att_ref[...].reshape(tokens, -1)
    projected = dot(attended, wo_scr[...]).reshape(lay.chips, lay.nc, step_patches, model)
    for k in range(lay.chips):
        pr_refs[k][...] = projected[k].astype(pr_refs[k].dtype)


def backward_kernel(lay, pos_ref, info_ref, *refs):
    w_refs, refs = refs[: lay.halves * lay.nz], refs[lay.halves * lay.nz :]
    q_ref, k_ref, v_ref, ga_ref, *refs = refs
    gh_refs, (w_scr, gt_scr) = refs[: lay.chips], refs[lay.chips :]
    _, frames, step_patches, cols = q_ref.shape
    model = w_scr.shape[1]
    patches = step_patches * pl.num_programs(0)
    scaling = 1.0 / math.sqrt(cols // lay.half_heads)

    @pl.when(pl.program_id(0) == 0)
    def _():
        fill_weights(lay, pos_ref, w_refs, w_scr)

    for b in range(step_patches // BLOCK):
        patch_base = pos_ref[1] * patches + pl.program_id(0) * step_patches + b * BLOCK
        allowed = allowed_pairs(lay, pos_ref, info_ref, patch_base)
        for h in range(lay.halves):
            queries, keys, values = (patch_blocks(ref[h], b) for ref in (q_ref, k_ref, v_ref))
            grad_out = patch_blocks(ga_ref[(pos_ref[1] ^ h) if lay.halves > 1 else 0], b)
            keys = heads_stacked(lay, keys)
            weights = attention_weights(lay, keys, queries, allowed, scaling)
            grad_weights = dot_t(heads_stacked(lay, values), grad_out).reshape(weights.shape)
            grad_values = dot(beside(lay, weights.astype(BF16)), heads_stacked(lay, grad_out))
            inner = jnp.sum(weights * grad_weights, axis=1, keepdims=True)
            grad_scores = (weights * (grad_weights - inner) * scaling).astype(BF16)
            grad_queries = t_dot(grad_scores.reshape(-1, grad_scores.shape[2]), keys)
            grad_keys = dot(beside(lay, grad_scores), heads_stacked(lay, queries))
            grads = jnp.concatenate([grad_queries, grad_keys, grad_values], axis=1).astype(BF16)
            gt_scr[h, :, b * BLOCK : (b + 1) * BLOCK, :] = grads.reshape(frames, BLOCK, 3 * cols)

    rows = lay.nc * step_patches
    for k in range(lay.chips):
        total = jnp.zeros((rows, model), F32)
        for h in range(lay.halves):
            part = gt_scr[h, k * lay.nc : (k + 1) * lay.nc].reshape(rows, 3 * cols)
            total = total + dot_t(part, w_scr[h])
        gh_refs[k][...] = total.reshape(gh_refs[k].shape).astype(gh_refs[k].dtype)


def output_kernel(lay, pos_ref, info_ref, *refs):
    x_refs, refs = refs[: lay.nc], refs[lay.nc :]
    pr_refs, refs = refs[: lay.chips], refs[lay.chips :]
    mod_ref, *out_refs = refs
    step_patches, model = x_refs[0].shape
    patches = step_patches * pl.num_programs(0)
    patch_base = pos_ref[1] * patches + pl.program_id(0) * step_patches
    patch = patch_base + lax.broadcasted_iota(jnp.int32, (step_patches, 1), 0)
    for j in range(lay.nc):
        _, limit, step = slot_scalars(lay, pos_ref, info_ref, (0, j))
        factor = jnp.where(patch < limit, table_row(mod_ref, step, 2, model), 0.0)
        projected = pr_refs[0][j]
        for k in range(1, lay.chips):
            projected = projected + pr_refs[k][j].astype(F32)
        projected = projected.astype(BF16).astype(F32)
        out_refs[j][...] = (x_refs[j][...].astype(F32) + factor * projected).astype(BF16)


def input_grad_kernel(lay, pos_ref, info_ref, *refs):
    x_refs, refs = refs[: lay.nc], refs[lay.nc :]
    g_refs, refs = refs[: lay.nc], refs[lay.nc :]
    gh_refs, refs = refs[: lay.chips], refs[lay.chips :]
    mod_ref, *out_refs = refs
    model = x_refs[0].shape[1]
    for j in range(lay.nc):
        _, _, step = slot_scalars(lay, pos_ref, info_ref, (0, j))
        grad_hidden = gh_refs[0][j]
        for k in range(1, lay.chips):
            grad_hidden = grad_hidden + gh_refs[k][j].astype(F32)
        grad_hidden = grad_hidden.astype(BF16).astype(F32)
        normed, inv_sigma = normalize(x_refs[j][...].astype(F32))
        grad_norm = grad_hidden * (1.0 + table_row(mod_ref, step, 1, model))
        first_mean = jnp.mean(grad_norm, axis=-1, keepdims=True)
        second_mean = jnp.mean(grad_norm * normed, axis=-1, keepdims=True)
        grad_x = g_refs[j][...].astype(F32) + inv_sigma * (
            grad_norm - first_mean - normed * second_mean
        )
        out_refs[j][...] = grad_x.astype(BF16)


def whole_spec(shape):
    return pl.BlockSpec(shape, lambda *_: (0,) * len(shape))


def struct(shape, dtype=BF16):
    return jax.ShapeDtypeStruct(shape, dtype)


def local(lay, frames_x, grad_y, clip_ids, clip_patches, clip_step, mod_table, w_qkv, w_out):
    y, c, z, x = (lax.axis_index(name) for name in AXES)
    _, patches, model = frames_x.shape
    half = patches // lay.nc
    chips, nc, nx = lay.chips, lay.nc, lay.nx
    head_size = model // HEADS
    halves = lay.halves
    cols = lay.half_heads * head_size
    chip_width = lay.chip_heads * head_size
    rows = w_qkv.shape[0]
    groups = lay.nz
    quarter = model // groups
    step_patches = max(BLOCK, min(half, 512 // lay.frames))
    steps = half // step_patches
    tokens = lay.frames * step_patches

    def call(kernel, name, in_specs, out_specs, out_shape, scratch=(), grid=(1,), prefetch=2):
        return pl.pallas_call(
            kernel,
            grid_spec=pltpu.PrefetchScalarGridSpec(
                num_scalar_prefetch=prefetch,
                grid=grid,
                in_specs=in_specs,
                out_specs=out_specs,
                scratch_shapes=list(scratch),
            ),
            out_shape=out_shape,
            compiler_params=pltpu.CompilerParams(vmem_limit_bytes=VMEM_LIMIT),
            name=name,
        )

    def chip_swap(k):
        ky, kx = lay.chip_of(k)
        return lay.swap(ky=ky, kx=kx)

    def over_chips(parts):
        own = [parts[0]]
        return own + [lax.ppermute(parts[k], AXES, chip_swap(k)) for k in range(1, chips)]

    def from_plane(parts):
        got = [lax.ppermute(part, AXES, lay.from_plane(k)) for k, part in enumerate(parts)]
        first = jnp.where(z // lay.ny == 0, got[0], got[1])
        second = jnp.where(z // lay.ny == 0, got[1], got[0])
        return jnp.concatenate([first, second], axis=0)[None]

    info = jnp.concatenate([clip_ids[0], clip_patches[0], clip_step[0]])[None]
    info = lax.ppermute(info, AXES, lay.to_plane(0))[0]
    pos = jnp.stack([y, c, z, x]).astype(jnp.int32)
    own = []
    for k in range(nc):
        start = ((z // lay.ny) ^ k) * half
        pair = [lax.dynamic_slice_in_dim(frame[0], start, half) for frame in (frames_x, grad_y)]
        own.append(lax.ppermute(jnp.concatenate(pair, axis=0), AXES, lay.to_plane(k)))
    by_slot = [over_chips([part] * chips) for part in own]
    frames = [by_slot[j][k] for k, j in lay.slots()]

    picked = call(
        functools.partial(pick_kernel, lay, cols),
        "pick",
        [whole_spec(w_qkv.shape)],
        [whole_spec((rows, 3 * cols))] * nx,
        [struct((rows, 3 * cols))] * nx,
        prefetch=1,
    )(pos, w_qkv)
    by_x = [picked[0]] + [
        lax.ppermute(picked[kx], AXES, lay.swap(kx=kx)) for kx in range(1, nx)
    ]
    if nx == 2:
        ordered = [jnp.where(x == i, by_x[0], by_x[1]) for i in range(nx)]
    else:
        stacked = jnp.stack(by_x)
        ordered = [lax.dynamic_index_in_dim(stacked, x ^ i, 0, keepdims=False) for i in range(nx)]
    w_own = jnp.concatenate(ordered, axis=0)
    w_pieces = [w_own] + [lax.ppermute(w_own, AXES, lay.swap(kz=kz)) for kz in range(1, lay.nz)]
    if halves > 1:
        w_pieces += [lax.ppermute(piece, AXES, lay.swap(kc=1)) for piece in w_pieces]

    wo_own = lax.ppermute(w_out, AXES, lay.rows_to_chip())
    wo_rows = [wo_own, lax.ppermute(wo_own, AXES, lay.swap(kc=1))]

    x_spec = pl.BlockSpec((step_patches, model), lambda i, *_: (i, 0))
    g_spec = pl.BlockSpec((step_patches, model), lambda i, *_: (steps + i, 0))
    triple_spec = pl.BlockSpec((halves, lay.frames, step_patches, cols), lambda i, *_: (0, 0, i, 0))
    att_spec = pl.BlockSpec((lay.frames, step_patches, chip_width), lambda i, *_: (0, i, 0))
    gp_spec = pl.BlockSpec((lay.frames, step_patches, model), lambda i, *_: (0, i, 0))
    part_spec = pl.BlockSpec((nc, step_patches, model), lambda i, *_: (0, i, 0))
    w_specs = [whole_spec(piece.shape) for piece in w_pieces]
    w_scratch = pltpu.VMEM((halves, model, 3 * cols), BF16)
    mod_spec = whole_spec(mod_table.shape)
    triple_shape = struct((halves, lay.frames, half, cols))
    part_shapes = [struct((nc, half, model), F32)] + [struct((nc, half, model))] * (chips - 1)

    queries, keys, values, attended = call(
        functools.partial(forward_kernel, lay),
        "forward",
        [x_spec] * lay.frames + w_specs + [mod_spec],
        [triple_spec] * 3 + [att_spec],
        [triple_shape] * 3 + [struct((lay.frames, half, chip_width))],
        [w_scratch, pltpu.VMEM((tokens, model), BF16)],
        (steps,),
    )(pos, info, *frames, *w_pieces, mod_table)

    piece_shape = (groups, rows, quarter)
    grad_proj, kept, sent = call(
        functools.partial(weight_grad_kernel, lay),
        "weight_grad",
        [g_spec] * lay.frames + [att_spec, mod_spec],
        [gp_spec] + [whole_spec(piece_shape)] * 2,
        [struct((lay.frames, half, model))] + [struct(piece_shape, F32)] * 2,
        [pltpu.VMEM((chip_width, model), F32)],
        (steps,),
    )(pos, info, *frames, attended, mod_table)
    got = lax.ppermute(sent, AXES, lay.swap(kc=1))

    grad_attn, *projected = call(
        functools.partial(projection_kernel, lay),
        "projection",
        [gp_spec, att_spec] + [whole_spec(w_out.shape)] * nc,
        [triple_spec] + [part_spec] * chips,
        [triple_shape] + part_shapes,
        [pltpu.VMEM((chip_width, model), BF16)],
        (steps,),
        prefetch=1,
    )(pos, grad_proj, attended, *wo_rows)

    pieces = [kept[j] + got[j] for j in range(groups)]
    grad_attn, *pieces = lax.optimization_barrier((grad_attn, *pieces))
    pieces = [lax.ppermute(piece, AXES, lay.to_owner(j)) for j, piece in enumerate(pieces)]
    grad_w_out = sum(pieces[1:], pieces[0]) * jnp.float32(
        1.0 / math.sqrt(groups * lay.frames * patches)
    )
    projected = over_chips(projected)

    partial_sums = call(
        functools.partial(backward_kernel, lay),
        "backward",
        w_specs + [triple_spec] * 4,
        [part_spec] * chips,
        part_shapes,
        [w_scratch, pltpu.VMEM((halves, lay.frames, step_patches, 3 * cols), BF16)],
        (steps,),
    )(pos, info, *w_pieces, queries, keys, values, grad_attn)
    grad_hidden = over_chips(partial_sums)

    out_parts = call(
        functools.partial(output_kernel, lay),
        "output",
        [x_spec] * nc + [part_spec] * chips + [mod_spec],
        [x_spec] * nc,
        [struct((half, model))] * nc,
        grid=(steps,),
    )(pos, info, *own, *projected, mod_table)
    out_y = from_plane(out_parts)

    grad_parts = call(
        functools.partial(input_grad_kernel, lay),
        "input_grad",
        [x_spec] * nc + [g_spec] * nc + [part_spec] * chips + [mod_spec],
        [x_spec] * nc,
        [struct((half, model))] * nc,
        grid=(steps,),
    )(pos, info, *own, *own, *grad_hidden, mod_table)
    grad_x = from_plane(grad_parts)
    return out_y, grad_x, grad_w_out


def solution(mesh):
    lay = Layout(mesh)
    grid = Mesh(mesh.devices.reshape(lay.ny, lay.nc, lay.nz, lay.nx), AXES)
    rows, cols = ("z", "x"), ("y", "c")
    frame = P(AXES, None, None)
    group = P(cols, None)
    return jax.shard_map(
        functools.partial(local, lay),
        mesh=grid,
        in_specs=(frame, frame, group, group, group, P(), P(rows, None), P(rows, None)),
        out_specs=(frame, frame, P(rows, cols)),
        check_vma=False,
    )
```

time: 264 us -> 185 us (0.70)
  waiting for transfers between devices: 138 us -> 95 us
  blocking collectives: 24.4 us -> 0 us
  between operations: 14.4 us -> 1.08 us
    ppermute x4, waiting for transfers between devices: 48.8 us -> 0.64 us  [local(): lax.ppermute(piece, AXES, lay.to_owner(j))]
    all_gather x1 -> x0, blocking collectives: 24.4 us -> none  [local(): lax.all_gather(jnp.concatenate(ordered, axis=0), 'z', axis=0, tiled=True)]
    ppermute x2, waiting for transfers between devices: 18.6 us -> 0.01 us  [local(): lax.ppermute(jnp.concatenate(pair, axis=0), AXES, lay.to_plane(k))]
    ppermute x12, waiting for transfers between devices: 40.3 us -> 57.3 us  [over_chips(): lax.ppermute(parts[k], AXES, chip_swap(k))]
    ppermute x1, waiting for transfers between devices: 14.3 us -> 21.3 us  [local(): info = lax.ppermute(info, AXES, lay.to_plane(0))[0]]
    ppermute x1 -> x7, waiting for transfers between devices: 0.01 us -> 4.85 us  [the longest x3 3.32 us: local(): lax.ppermute(w_own, AXES, lay.swap(kz=kz))]
    ppermute x4, waiting for transfers between devices: 11.4 us -> 7.61 us  [from_plane(): lax.ppermute(part, AXES, lay.from_plane(k))]
    ppermute x1, waiting for transfers between devices: 4.32 us -> 0.93 us  [local(): lax.ppermute(picked[kx], AXES, lay.swap(kx=kx))]
  transfers between devices with their start and end apart: 29 -> 34, of which waited for: 14 -> 14; matrix products, arithmetic and copies ran while one was open for 2% -> 2% of each run, Pallas kernels for 12% -> 20%
where the time goes in v3:
time: 185 us
  waiting for transfers between devices  95 us (51%)
  starting transfers between devices  43.8 us (24%)
  Pallas kernels  36.9 us (20%)
  local copies, waits for them, and re-layouts  4.08 us (2%)
  other arithmetic  4.05 us (2%)
    ppermute x12, waiting for transfers between devices, over_chips(): lax.ppermute(parts[k], AXES, chip_swap(k))  57.3 us
    ppermute x1, waiting for transfers between devices, local(): info = lax.ppermute(info, AXES, lay.to_plane(0))[0]  21.3 us
    ppermute x12, starting transfers between devices, over_chips(): lax.ppermute(parts[k], AXES, chip_swap(k))  13.5 us
    ppermute x4, starting transfers between devices, from_plane(): lax.ppermute(part, AXES, lay.from_plane(k))  10.5 us
    pallas_call x1, Pallas kernels, local(): call(functools.partial(backward_kernel, lay), 'backward', w_specs + [trip...  9.62 us
    pallas_call x1, Pallas kernels, local(): call(functools.partial(forward_kernel, lay), 'forward', [x_spec] * lay.fr...  8.56 us
    ppermute x4, waiting for transfers between devices, from_plane(): lax.ppermute(part, AXES, lay.from_plane(k))  7.61 us
    pallas_call x1, Pallas kernels, local(): call(functools.partial(projection_kernel, lay), 'projection', [gp_spec, a...  4.77 us
  transfers between devices with their start and end apart: 34, of which 14 were waited for; matrix products, arithmetic and copies ran while one was open for 2% of the time, Pallas kernels for 20%

profile of v3, /device:TPU:4, one launch (start us, length us, event | category | flops | bytes accessed | tf_op | source)
XLA Modules:
  0.0 184.9 jit_solution(8843851852729662156)
XLA Ops:
  0.7 1.2 dynamic-slice_bitcast_fusion
  1.9 1.0 collective-permute-start.2
  2.9 0.6 pad_add_fusion.pos_ref
  3.5 3.0 %pick.1 = (bf16[144,432]{1,0:T(8,128)(2,1)}, bf16[144,432]{1,0:T(8,128)(2,1)}) custom-call(s32[4]{0:T(128)} %pad_add_fusion.pos_ref, bf16[144,3456]{1,0:T(8,128)(2,1)} %w_ref.1), custom_call_target="tpu_custom_call" | custom-call | tf_op jit(solution)/shard_map/pick/pallas_call | solution.py:441
  6.5 1.5 collective-permute-start.9
  8.0 3.3 %collective-permute-start.1 = (bf16[128,1152]{1,0:T(8,128)(2,1)S(1)}, bf16[128,1152]{1,0:T(8,128)(2,1)S(1)}, u32[]{:S(2)}, u32[]{:S(2)}) collective-permute-start(bf16[128,1152]{1,0:T(8,128)(2,1)S(1)} %pad_maximum_fusion), channel_id=1, source_target_pairs={{0,0},{1,1},{2,16},{3,17},{4,8},{5,9},{6,24},{7,25},{8,4},{9,5},{1... | collective-permute-start | bytes 884744 | tf_op jit(solution)/shard_map/ppermute | solution.py:437
  11.3 0.9 collective-permute-done.9
  12.3 0.9 broadcast_select_fusion.1
  13.2 0.7 collective-permute-start.10
  14.0 0.1 add_bitcast_fusion
  14.1 3.5 %collective-permute-start = (s32[1,16]{1,0:T(1,128)S(1)}, s32[1,16]{1,0:T(1,128)S(1)}, u32[]{:S(2)}, u32[]{:S(2)}) collective-permute-start(s32[1,16]{1,0:T(1,128)S(1)} %add_bitcast_fusion), channel_id=1, source_target_pairs={{0,0},{1,1},{2,16},{3,17},{4,8},{5,9},{6,24},{7,25},{8,4},{9,5},{1... | collective-permute-start | bytes 200 | tf_op jit(solution)/shard_map/ppermute | solution.py:431
  17.6 1.7 collective-permute-start.11
  19.3 21.3 %collective-permute-done = s32[1,16]{1,0:T(1,128)S(1)} collective-permute-done((s32[1,16]{1,0:T(1,128)S(1)}, s32[1,16]{1,0:T(1,128)S(1)}, u32[]{:S(2)}, u32[]{:S(2)}) %collective-permute-start) | collective-permute-done | bytes 96 | tf_op jit(solution)/shard_map/ppermute | solution.py:431
  40.6 0.0 collective-permute-start.12
  40.6 0.1 collective-permute-start.13
  40.7 0.0 copy-start.1
  40.7 1.6 collective-permute-start.4
  42.3 3.5 %collective-permute-start.6 = (bf16[128,1152]{1,0:T(8,128)(2,1)S(1)}, bf16[128,1152]{1,0:T(8,128)(2,1)S(1)}, u32[]{:S(2)}, u32[]{:S(2)}) collective-permute-start(bf16[128,1152]{1,0:T(8,128)(2,1)S(1)} %collective-permute-done.2.refs_1_.refs_3_), channel_id=1, source_target_pairs={{0,16},{1,17},{2,18},{3,19},{4,20},{5,21},{6,22},{7,23},{8,24},{9,... | collective-permute-start | bytes 884744 | tf_op jit(solution)/shard_map/ppermute | solution.py:422
  45.7 0.1 collective-permute-start.8
  45.8 3.3 %collective-permute-done.12.refs_11_.refs_3_ = bf16[288,432]{1,0:T(8,128)(2,1)S(1)} collective-permute-done((bf16[288,432]{1,0:T(8,128)(2,1)S(1)}, bf16[288,432]{1,0:T(8,128)(2,1)S(1)}, u32[]{:S(2)}, u32[]{:S(2)}) %collective-permute-start.12) | collective-permute-done | bytes 248864 | tf_op jit(solution)/shard_map/ppermute | solution.py:458
  49.1 1.5 collective-permute-start.3
  50.6 2.9 %collective-permute-start.17 = (bf16[144,1152]{1,0:T(8,128)(2,1)S(1)}, bf16[144,1152]{1,0:T(8,128)(2,1)S(1)}, u32[]{:S(2)}, u32[]{:S(2)}) collective-permute-start(bf16[144,1152]{1,0:T(8,128)(2,1)S(1)} %copy-done.29), channel_id=1, source_target_pairs={{0,0},{1,1},{2,16},{3,17},{4,8},{5,9},{6,24},{7,25},{8,4},{9,5},{1... | collective-permute-start | bytes 995336 | tf_op jit(solution)/shard_map/ppermute | solution.py:462
  53.5 10.6 %collective-permute-done.6.refs_5_ = bf16[128,1152]{1,0:T(8,128)(2,1)S(1)} collective-permute-done((bf16[128,1152]{1,0:T(8,128)(2,1)S(1)}, bf16[128,1152]{1,0:T(8,128)(2,1)S(1)}, u32[]{:S(2)}, u32[]{:S(2)}) %collective-permute-start.6) | collective-permute-done | bytes 294944 | tf_op jit(solution)/shard_map/ppermute | solution.py:422
  64.1 0.1 collective-permute-start.14
  64.2 0.0 copy-start.13
  64.3 0.5 collective-permute-start.15
  64.7 14.0 %collective-permute-done.5.refs_4_ = bf16[128,1152]{1,0:T(8,128)(2,1)S(1)} collective-permute-done((bf16[128,1152]{1,0:T(8,128)(2,1)S(1)}, bf16[128,1152]{1,0:T(8,128)(2,1)S(1)}, u32[]{:S(2)}, u32[]{:S(2)}) %collective-permute-start.5) | collective-permute-done | bytes 294944 | tf_op jit(solution)/shard_map/ppermute | solution.py:422
  78.8 1.5 collective-permute-done.16.refs_15_.refs_7_
  80.5 0.6 copy-done.9
  81.1 8.6 %forward.1 = (bf16[2,8,64,144]{3,2,1,0:T(8,128)(2,1)}, bf16[2,8,64,144]{3,2,1,0:T(8,128)(2,1)}, bf16[2,8,64,144]{3,2,1,0:T(8,128)(2,1)}, bf16[8,64,288]{2,1,0:T(8,128)(2,1)}) custom-call(s32[4]{0:T(128)} %pad_add_fusion.pos_ref, s32[16]{0:T(128)} %bitcast.30, bf16[128,1152]{1,0:T(8,128)(2,1)} %copy-done.1, bf16[128,1152]{1,0:T(8,128)(2,1)} %copy-done, ...), custom_call_target="tpu_custom_call" | custom-call | tf_op jit(solution)/shard_map/forward/pallas_call | solution.py:477
  89.6 4.3 %weight_grad.1 = (bf16[8,64,1152]{2,1,0:T(8,128)(2,1)}, f32[4,144,288]{2,1,0:T(8,128)}, f32[4,144,288]{2,1,0:T(8,128)}) custom-call(s32[4]{0:T(128)} %pad_add_fusion.pos_ref, s32[16]{0:T(128)} %bitcast.31, bf16[128,1152]{1,0:T(8,128)(2,1)} %copy-done.1, bf16[128,1152]{1,0:T(8,128)(2,1)} %copy-done, bf16[128,1152]{1,0:T(8,128)(2,1)} %copy-done.13, ...), custom_call_target="tpu_custom_call" | custom-call | tf_op jit(solution)/shard_map/weight_grad/pallas_call | solution.py:488
  94.0 0.1 collective-permute-start.24
  94.1 0.4 collective-permute-start.18
  94.5 2.4 %collective-permute-done.18.refs_1_ = bf16[144,1152]{1,0:T(8,128)(2,1)S(1)} collective-permute-done((bf16[144,1152]{1,0:T(8,128)(2,1)S(1)}, bf16[144,1152]{1,0:T(8,128)(2,1)S(1)}, u32[]{:S(2)}, u32[]{:S(2)}) %collective-permute-start.18) | collective-permute-done | bytes 331808 | tf_op jit(solution)/shard_map/ppermute | solution.py:463
  96.9 0.7 copy-done.18
  97.6 4.8 %projection.1 = (bf16[2,8,64,144]{3,2,1,0:T(8,128)(2,1)}, f32[2,64,1152]{2,1,0:T(8,128)}, bf16[2,64,1152]{2,1,0:T(8,128)(2,1)}, bf16[2,64,1152]{2,1,0:T(8,128)(2,1)}, bf16[2,64,1152]{2,1,0:T(8,128)(2,1)}) custom-call(s32[4]{0:T(128)} %pad_add_fusion.pos_ref, bf16[8,64,1152]{2,1,0:T(8,128)(2,1)} %get-tuple-element.33.gp_ref, ...), custom_call_target="tpu_custom_call" | custom-call | tf_op jit(solution)/shard_map/projection/pallas_call | solution.py:499
  102.4 0.5 collective-permute-start.19
  102.9 3.0 %collective-permute-start.21 = (bf16[2,64,1152]{2,1,0:T(8,128)(2,1)}, bf16[2,64,1152]{2,1,0:T(8,128)(2,1)S(1)}, u32[]{:S(2)}, u32[]{:S(2)}) collective-permute-start(bf16[2,64,1152]{2,1,0:T(8,128)(2,1)} %get-tuple-element.37), channel_id=1, source_target_pairs={{0,17},{1,16},{2,19},{3,18},{4,21},{5,20},{6,23},{7,22},{8,25},{9,... | collective-permute-start | bytes 884744 | tf_op jit(solution)/shard_map/ppermute | solution.py:422
  105.8 6.6 %collective-permute-done.19.refs_3_ = bf16[2,64,1152]{2,1,0:T(8,128)(2,1)S(1)} collective-permute-done((bf16[2,64,1152]{2,1,0:T(8,128)(2,1)}, bf16[2,64,1152]{2,1,0:T(8,128)(2,1)S(1)}, u32[]{:S(2)}, u32[]{:S(2)}) %collective-permute-start.19) | collective-permute-done | bytes 294944 | tf_op jit(solution)/shard_map/ppermute | solution.py:422
  112.4 5.8 %collective-permute-done.20.refs_4_ = bf16[2,64,1152]{2,1,0:T(8,128)(2,1)S(1)} collective-permute-done((bf16[2,64,1152]{2,1,0:T(8,128)(2,1)}, bf16[2,64,1152]{2,1,0:T(8,128)(2,1)S(1)}, u32[]{:S(2)}, u32[]{:S(2)}) %collective-permute-start.20) | collective-permute-done | bytes 294944 | tf_op jit(solution)/shard_map/ppermute | solution.py:422
  118.2 0.7 copy-done.23
  118.9 0.1 copy-done.24
  119.0 3.1 %output.1 = (bf16[64,1152]{1,0:T(8,128)(2,1)}, bf16[64,1152]{1,0:T(8,128)(2,1)}) custom-call(s32[4]{0:T(128)} %pad_add_fusion.pos_ref, s32[16]{0:T(128)} %bitcast.32, bf16[128,1152]{1,0:T(8,128)(2,1)} %copy-done.1, bf16[128,1152]{1,0:T(8,128)(2,1)} %copy-done, f32[2,64,1152]{2,1,0:T(8,128)} %get-tuple-element.34.refs_2_, bf16[2,64,1152]{2,1,0:T(8,128)(2,1)} %copy-done.22, ...), custom_call_target="tpu_custom_call" | custom-call | tf_op jit(solution)/shard_map/output/pallas_call | solution.py:529
  122.1 1.9 %collective-permute-start.22 = (bf16[64,1152]{1,0:T(8,128)(2,1)}, bf16[64,1152]{1,0:T(8,128)(2,1)S(1)}, u32[]{:S(2)}, u32[]{:S(2)}) collective-permute-start(bf16[64,1152]{1,0:T(8,128)(2,1)} %get-tuple-element.38), channel_id=1, source_target_pairs={{0,0},{1,1},{16,2},{17,3},{8,4},{9,5},{24,6},{25,7},{4,8},{5,9},{2... | collective-permute-start | bytes 442376 | tf_op jit(solution)/shard_map/ppermute | solution.py:425
  124.0 3.5 %collective-permute-start.23 = (bf16[64,1152]{1,0:T(8,128)(2,1)}, bf16[64,1152]{1,0:T(8,128)(2,1)S(1)}, u32[]{:S(2)}, u32[]{:S(2)}) collective-permute-start(bf16[64,1152]{1,0:T(8,128)(2,1)} %get-tuple-element.39), channel_id=1, source_target_pairs={{8,0},{9,1},{24,2},{25,3},{0,4},{1,5},{16,6},{17,7},{12,8},{13,9},... | collective-permute-start | bytes 442376 | tf_op jit(solution)/shard_map/ppermute | solution.py:425
  127.6 0.1 fusion
  127.6 9.6 %backward.1 = (f32[2,64,1152]{2,1,0:T(8,128)}, bf16[2,64,1152]{2,1,0:T(8,128)(2,1)}, bf16[2,64,1152]{2,1,0:T(8,128)(2,1)}, bf16[2,64,1152]{2,1,0:T(8,128)(2,1)}) custom-call(s32[4]{0:T(128)} %pad_add_fusion.pos_ref, s32[16]{0:T(128)} %bitcast.33, bf16[288,432]{1,0:T(8,128)(2,1)} %copy-done.2, bf16[288,432]{1,0:T(8,128)(2,1)} %copy-done.3, ...), custom_call_target="tpu_custom_call" | custom-call | tf_op jit(solution)/shard_map/backward/pallas_call | solution.py:518
  137.3 1.5 collective-permute-start.25
  138.8 2.0 %collective-permute-start.27 = (bf16[2,64,1152]{2,1,0:T(8,128)(2,1)}, bf16[2,64,1152]{2,1,0:T(8,128)(2,1)S(1)}, u32[]{:S(2)}, u32[]{:S(2)}) collective-permute-start(bf16[2,64,1152]{2,1,0:T(8,128)(2,1)} %get-tuple-element.50), channel_id=1, source_target_pairs={{0,17},{1,16},{2,19},{3,18},{4,21},{5,20},{6,23},{7,22},{8,25},{9,... | collective-permute-start | bytes 884744 | tf_op jit(solution)/shard_map/ppermute | solution.py:422
  140.8 1.9 %collective-permute-start.30 = (f32[144,288]{1,0:T(8,128)S(1)}, f32[144,288]{1,0:T(8,128)S(1)}, u32[]{:S(2)}, u32[]{:S(2)}) collective-permute-start(f32[144,288]{1,0:T(8,128)S(1)} %get-tuple-element.53), channel_id=1, source_target_pairs={{0,0},{1,1},{2,8},{3,9},{4,16},{5,17},{6,24},{7,25},{8,4},{9,5},{1... | collective-permute-start | bytes 497672 | tf_op jit(solution)/shard_map/ppermute | solution.py:512
  142.7 0.1 collective-permute-start.31
  142.8 4.6 %collective-permute-done.25.refs_5_ = bf16[2,64,1152]{2,1,0:T(8,128)(2,1)S(1)} collective-permute-done((bf16[2,64,1152]{2,1,0:T(8,128)(2,1)}, bf16[2,64,1152]{2,1,0:T(8,128)(2,1)S(1)}, u32[]{:S(2)}, u32[]{:S(2)}) %collective-permute-start.25) | collective-permute-done | bytes 294944 | tf_op jit(solution)/shard_map/ppermute | solution.py:422
  147.4 15.7 %collective-permute-done.26.refs_6_ = bf16[2,64,1152]{2,1,0:T(8,128)(2,1)S(1)} collective-permute-done((bf16[2,64,1152]{2,1,0:T(8,128)(2,1)}, bf16[2,64,1152]{2,1,0:T(8,128)(2,1)S(1)}, u32[]{:S(2)}, u32[]{:S(2)}) %collective-permute-start.26) | collective-permute-done | bytes 294944 | tf_op jit(solution)/shard_map/ppermute | solution.py:422
  163.1 1.9 %collective-permute-start.33 = (f32[144,288]{1,0:T(8,128)S(1)}, f32[144,288]{1,0:T(8,128)S(1)}, u32[]{:S(2)}, u32[]{:S(2)}) collective-permute-start(f32[144,288]{1,0:T(8,128)S(1)} %get-tuple-element.56), channel_id=1, source_target_pairs={{0,24},{1,25},{2,16},{3,17},{4,8},{5,9},{6,0},{7,1},{8,28},{9,29},... | collective-permute-start | bytes 497672 | tf_op jit(solution)/shard_map/ppermute | solution.py:512
  165.0 0.7 maximum_bitcast_fusion
  165.8 0.7 copy-done.21
  166.5 3.5 %input_grad.1 = (bf16[64,1152]{1,0:T(8,128)(2,1)}, bf16[64,1152]{1,0:T(8,128)(2,1)}) custom-call(s32[4]{0:T(128)} %pad_add_fusion.pos_ref, s32[16]{0:T(128)} %bitcast.34, bf16[128,1152]{1,0:T(8,128)(2,1)} %copy-done.1, bf16[128,1152]{1,0:T(8,128)(2,1)} %copy-done, bf16[128,1152]{1,0:T(8,128)(2,1)} %copy-done.1, bf16[128,1152]{1,0:T(8,128)(2,1)} %copy-done, ...), custom_call_target="tpu_custom_call" | custom-call | tf_op jit(solution)/shard_map/input_grad/pallas_call | solution.py:539
  170.0 4.8 %collective-permute-start.28 = (bf16[64,1152]{1,0:T(8,128)(2,1)}, bf16[64,1152]{1,0:T(8,128)(2,1)S(1)}, u32[]{:S(2)}, u32[]{:S(2)}) collective-permute-start(bf16[64,1152]{1,0:T(8,128)(2,1)} %get-tuple-element.51), channel_id=1, source_target_pairs={{0,0},{1,1},{16,2},{17,3},{8,4},{9,5},{24,6},{25,7},{4,8},{5,9},{2... | collective-permute-start | bytes 442376 | tf_op jit(solution)/shard_map/ppermute | solution.py:425
  174.9 0.3 collective-permute-start.29
  175.2 0.6 collective-permute-done.33
  175.8 0.7 add_multiply_fusion
  176.5 7.5 %collective-permute-done.28 = bf16[64,1152]{1,0:T(8,128)(2,1)S(1)} collective-permute-done((bf16[64,1152]{1,0:T(8,128)(2,1)}, bf16[64,1152]{1,0:T(8,128)(2,1)S(1)}, u32[]{:S(2)}, u32[]{:S(2)}) %collective-permute-start.28) | collective-permute-done | bytes 147488 | tf_op jit(solution)/shard_map/ppermute | solution.py:425
  184.0 0.1 collective-permute-done.29
  184.2 0.7 maximum_bitcast_fusion.1
  (84 shorter events, 0.3 us)
Async XLA Ops:
  1.9 38.7 %collective-permute-start.2 = (bf16[128,1152]{1,0:T(8,128)(2,1)S(1)}, bf16[128,1152]{1,0:T(8,128)(2,1)S(1)}, u32[]{:S(2)}, u32[]{:S(2)}) collective-permute-start(bf16[128,1152]{1,0:T(8,128)(2,1)S(1)} %pad_maximum_fusion.1), channel_id=1, source_target_pairs={{0,8},{1,9},{2,24},{3,25},{4,0},{5,1},{6,16},{7,17},{8,12},{9,13},... | collective-permute-start | bytes 884744 | tf_op jit(solution)/shard_map/ppermute | solution.py:437
  3.5 10.5 %copy-start.26 = (s32[1,4]{1,0:T(1,128)S(1)}, s32[1,4]{1,0:T(1,128)}, u32[]{:S(2)}) copy-start(s32[1,4]{1,0:T(1,128)} %param.12) | copy-start | bytes 52
  3.5 10.5 %copy-start.27 = (s32[1,4]{1,0:T(1,128)S(1)}, s32[1,4]{1,0:T(1,128)}, u32[]{:S(2)}) copy-start(s32[1,4]{1,0:T(1,128)} %param.11) | copy-start | bytes 52
  3.5 10.5 %copy-start.28 = (s32[1,8]{1,0:T(1,128)S(1)}, s32[1,8]{1,0:T(1,128)}, u32[]{:S(2)}) copy-start(s32[1,8]{1,0:T(1,128)} %param.10) | copy-start | bytes 100
  3.5 47.1 %copy-start.29 = (bf16[144,1152]{1,0:T(8,128)(2,1)S(1)}, bf16[144,1152]{1,0:T(8,128)(2,1)}, u32[]{:S(2)}) copy-start(bf16[144,1152]{1,0:T(8,128)(2,1)} %param.15) | copy-start | bytes 995332
  6.5 5.7 %collective-permute-start.9 = (bf16[144,432]{1,0:T(8,128)(2,1)}, bf16[144,432]{1,0:T(8,128)(2,1)S(1)}, u32[]{:S(2)}, u32[]{:S(2)}) collective-permute-start(bf16[144,432]{1,0:T(8,128)(2,1)} %get-tuple-element.31), channel_id=1, source_target_pairs={{0,1},{1,0},{2,3},{3,2},{4,5},{5,4},{6,7},{7,6},{8,9},{9,8},{10,11... | collective-permute-start | bytes 373256 | tf_op jit(solution)/shard_map/ppermute | solution.py:450
  8.0 32.7 %collective-permute-start.1 = (bf16[128,1152]{1,0:T(8,128)(2,1)S(1)}, bf16[128,1152]{1,0:T(8,128)(2,1)S(1)}, u32[]{:S(2)}, u32[]{:S(2)}) collective-permute-start(bf16[128,1152]{1,0:T(8,128)(2,1)S(1)} %pad_maximum_fusion), channel_id=1, source_target_pairs={{0,0},{1,1},{2,16},{3,17},{4,8},{5,9},{6,24},{7,25},{8,4},{9,5},{1... | collective-permute-start | bytes 884744 | tf_op jit(solution)/shard_map/ppermute | solution.py:437
  13.2 67.1 %copy-start.2 = (bf16[288,432]{1,0:T(8,128)(2,1)}, bf16[288,432]{1,0:T(8,128)(2,1)S(1)}, u32[]{:S(2)}) copy-start(bf16[288,432]{1,0:T(8,128)(2,1)S(1)} %pad_maximum_fusion.2.refs_8_.refs_0_) | copy-start | bytes 746500
  13.2 29.0 %collective-permute-start.10 = (bf16[288,432]{1,0:T(8,128)(2,1)S(1)}, bf16[288,432]{1,0:T(8,128)(2,1)S(1)}, u32[]{:S(2)}, u32[]{:S(2)}) collective-permute-start(bf16[288,432]{1,0:T(8,128)(2,1)S(1)} %pad_maximum_fusion.2.refs_8_.refs_0_), channel_id=1, source_target_pairs={{0,2},{1,3},{2,0},{3,1},{4,6},{5,7},{6,4},{7,5},{8,10},{9,11},{10,... | collective-permute-start | bytes 746504 | tf_op jit(solution)/shard_map/ppermute | solution.py:458
  14.1 26.5 %collective-permute-start = (s32[1,16]{1,0:T(1,128)S(1)}, s32[1,16]{1,0:T(1,128)S(1)}, u32[]{:S(2)}, u32[]{:S(2)}) collective-permute-start(s32[1,16]{1,0:T(1,128)S(1)} %add_bitcast_fusion), channel_id=1, source_target_pairs={{0,0},{1,1},{2,16},{3,17},{4,8},{5,9},{6,24},{7,25},{8,4},{9,5},{1... | collective-permute-start | bytes 200 | tf_op jit(solution)/shard_map/ppermute | solution.py:431
  17.6 28.1 %collective-permute-start.11 = (bf16[288,432]{1,0:T(8,128)(2,1)S(1)}, bf16[288,432]{1,0:T(8,128)(2,1)S(1)}, u32[]{:S(2)}, u32[]{:S(2)}) collective-permute-start(bf16[288,432]{1,0:T(8,128)(2,1)S(1)} %pad_maximum_fusion.2.refs_8_.refs_0_), channel_id=1, source_target_pairs={{0,4},{1,5},{2,6},{3,7},{4,0},{5,1},{6,2},{7,3},{8,12},{9,13},{10,... | collective-permute-start | bytes 746504 | tf_op jit(solution)/shard_map/ppermute | solution.py:458
  40.6 39.8 %copy-start.25 = (s32[1,16]{1,0:T(1,128)}, s32[1,16]{1,0:T(1,128)S(1)}, u32[]{:S(2)}) copy-start(s32[1,16]{1,0:T(1,128)S(1)} %collective-permute-done) | copy-start | bytes 196
  40.6 8.5 %collective-permute-start.12 = (bf16[288,432]{1,0:T(8,128)(2,1)S(1)}, bf16[288,432]{1,0:T(8,128)(2,1)S(1)}, u32[]{:S(2)}, u32[]{:S(2)}) collective-permute-start(bf16[288,432]{1,0:T(8,128)(2,1)S(1)} %pad_maximum_fusion.2.refs_8_.refs_0_), channel_id=1, source_target_pairs={{0,6},{1,7},{2,4},{3,5},{4,2},{5,3},{6,0},{7,1},{8,14},{9,15},{10,... | collective-permute-start | bytes 746504 | tf_op jit(solution)/shard_map/ppermute | solution.py:458
  40.6 39.8 %copy-start = (bf16[128,1152]{1,0:T(8,128)(2,1)}, bf16[128,1152]{1,0:T(8,128)(2,1)S(1)}, u32[]{:S(2)}) copy-start(bf16[128,1152]{1,0:T(8,128)(2,1)S(1)} %collective-permute-done.2.refs_1_.refs_3_) | copy-start | bytes 884740
  40.6 10.0 %collective-permute-start.13 = (bf16[288,432]{1,0:T(8,128)(2,1)S(1)}, bf16[288,432]{1,0:T(8,128)(2,1)S(1)}, u32[]{:S(2)}, u32[]{:S(2)}) collective-permute-start(bf16[288,432]{1,0:T(8,128)(2,1)S(1)} %pad_maximum_fusion.2.refs_8_.refs_0_), channel_id=1, source_target_pairs={{0,8},{1,9},{2,10},{3,11},{4,12},{5,13},{6,14},{7,15},{8,0},{9,1},... | collective-permute-start | bytes 746504 | tf_op jit(solution)/shard_map/ppermute | solution.py:460
  40.7 39.7 %copy-start.1 = (bf16[128,1152]{1,0:T(8,128)(2,1)}, bf16[128,1152]{1,0:T(8,128)(2,1)S(1)}, u32[]{:S(2)}) copy-start(bf16[128,1152]{1,0:T(8,128)(2,1)S(1)} %collective-permute-done.1.refs_0_.refs_2_) | copy-start | bytes 884740
  40.7 9.9 %collective-permute-start.4 = (bf16[128,1152]{1,0:T(8,128)(2,1)S(1)}, bf16[128,1152]{1,0:T(8,128)(2,1)S(1)}, u32[]{:S(2)}, u32[]{:S(2)}) collective-permute-start(bf16[128,1152]{1,0:T(8,128)(2,1)S(1)} %collective-permute-done.2.refs_1_.refs_3_), channel_id=1, source_target_pairs={{0,1},{1,0},{2,3},{3,2},{4,5},{5,4},{6,7},{7,6},{8,9},{9,8},{10,11... | collective-permute-start | bytes 884744 | tf_op jit(solution)/shard_map/ppermute | solution.py:422
  42.3 38.1 %copy-start.3 = (bf16[288,432]{1,0:T(8,128)(2,1)}, bf16[288,432]{1,0:T(8,128)(2,1)S(1)}, u32[]{:S(2)}) copy-start(bf16[288,432]{1,0:T(8,128)(2,1)S(1)} %collective-permute-done.10.refs_9_.refs_1_) | copy-start | bytes 746500
  42.3 21.9 %collective-permute-start.6 = (bf16[128,1152]{1,0:T(8,128)(2,1)S(1)}, bf16[128,1152]{1,0:T(8,128)(2,1)S(1)}, u32[]{:S(2)}, u32[]{:S(2)}) collective-permute-start(bf16[128,1152]{1,0:T(8,128)(2,1)S(1)} %collective-permute-done.2.refs_1_.refs_3_), channel_id=1, source_target_pairs={{0,16},{1,17},{2,18},{3,19},{4,20},{5,21},{6,22},{7,23},{8,24},{9,... | collective-permute-start | bytes 884744 | tf_op jit(solution)/shard_map/ppermute | solution.py:422
  45.7 34.7 %copy-start.4 = (bf16[288,432]{1,0:T(8,128)(2,1)}, bf16[288,432]{1,0:T(8,128)(2,1)S(1)}, u32[]{:S(2)}) copy-start(bf16[288,432]{1,0:T(8,128)(2,1)S(1)} %collective-permute-done.11.refs_10_.refs_2_) | copy-start | bytes 746500
  45.7 18.4 %collective-permute-start.8 = (bf16[128,1152]{1,0:T(8,128)(2,1)S(1)}, bf16[128,1152]{1,0:T(8,128)(2,1)S(1)}, u32[]{:S(2)}, u32[]{:S(2)}) collective-permute-start(bf16[128,1152]{1,0:T(8,128)(2,1)S(1)} %collective-permute-done.2.refs_1_.refs_3_), channel_id=1, source_target_pairs={{0,17},{1,16},{2,19},{3,18},{4,21},{5,20},{6,23},{7,22},{8,25},{9,... | collective-permute-start | bytes 884744 | tf_op jit(solution)/shard_map/ppermute | solution.py:422
  49.1 31.3 %copy-start.5 = (bf16[288,432]{1,0:T(8,128)(2,1)}, bf16[288,432]{1,0:T(8,128)(2,1)S(1)}, u32[]{:S(2)}) copy-start(bf16[288,432]{1,0:T(8,128)(2,1)S(1)} %collective-permute-done.12.refs_11_.refs_3_) | copy-start | bytes 746500
  49.1 15.1 %collective-permute-start.3 = (bf16[128,1152]{1,0:T(8,128)(2,1)S(1)}, bf16[128,1152]{1,0:T(8,128)(2,1)S(1)}, u32[]{:S(2)}, u32[]{:S(2)}) collective-permute-start(bf16[128,1152]{1,0:T(8,128)(2,1)S(1)} %collective-permute-done.1.refs_0_.refs_2_), channel_id=1, source_target_pairs={{0,1},{1,0},{2,3},{3,2},{4,5},{5,4},{6,7},{7,6},{8,9},{9,8},{10,11... | collective-permute-start | bytes 884744 | tf_op jit(solution)/shard_map/ppermute | solution.py:422
  50.6 29.8 %copy-start.6 = (bf16[288,432]{1,0:T(8,128)(2,1)}, bf16[288,432]{1,0:T(8,128)(2,1)S(1)}, u32[]{:S(2)}) copy-start(bf16[288,432]{1,0:T(8,128)(2,1)S(1)} %collective-permute-done.13.refs_12_.refs_4_) | copy-start | bytes 746500
  50.6 28.2 %collective-permute-start.5 = (bf16[128,1152]{1,0:T(8,128)(2,1)S(1)}, bf16[128,1152]{1,0:T(8,128)(2,1)S(1)}, u32[]{:S(2)}, u32[]{:S(2)}) collective-permute-start(bf16[128,1152]{1,0:T(8,128)(2,1)S(1)} %collective-permute-done.1.refs_0_.refs_2_), channel_id=1, source_target_pairs={{0,16},{1,17},{2,18},{3,19},{4,20},{5,21},{6,22},{7,23},{8,24},{9,... | collective-permute-start | bytes 884744 | tf_op jit(solution)/shard_map/ppermute | solution.py:422
  50.6 29.8 %copy-start.10 = (bf16[128,1152]{1,0:T(8,128)(2,1)}, bf16[128,1152]{1,0:T(8,128)(2,1)S(1)}, u32[]{:S(2)}) copy-start(bf16[128,1152]{1,0:T(8,128)(2,1)S(1)} %collective-permute-done.4.refs_3_) | copy-start | bytes 884740
  50.6 43.5 %collective-permute-start.17 = (bf16[144,1152]{1,0:T(8,128)(2,1)S(1)}, bf16[144,1152]{1,0:T(8,128)(2,1)S(1)}, u32[]{:S(2)}, u32[]{:S(2)}) collective-permute-start(bf16[144,1152]{1,0:T(8,128)(2,1)S(1)} %copy-done.29), channel_id=1, source_target_pairs={{0,0},{1,1},{2,16},{3,17},{4,8},{5,9},{6,24},{7,25},{8,4},{9,5},{1... | collective-permute-start | bytes 995336 | tf_op jit(solution)/shard_map/ppermute | solution.py:462
  64.1 16.3 %copy-start.11 = (bf16[128,1152]{1,0:T(8,128)(2,1)}, bf16[128,1152]{1,0:T(8,128)(2,1)S(1)}, u32[]{:S(2)}) copy-start(bf16[128,1152]{1,0:T(8,128)(2,1)S(1)} %collective-permute-done.6.refs_5_) | copy-start | bytes 884740
  64.1 14.7 %collective-permute-start.7 = (bf16[128,1152]{1,0:T(8,128)(2,1)S(1)}, bf16[128,1152]{1,0:T(8,128)(2,1)S(1)}, u32[]{:S(2)}, u32[]{:S(2)}) collective-permute-start(bf16[128,1152]{1,0:T(8,128)(2,1)S(1)} %collective-permute-done.1.refs_0_.refs_2_), channel_id=1, source_target_pairs={{0,17},{1,16},{2,19},{3,18},{4,21},{5,20},{6,23},{7,22},{8,25},{9,... | collective-permute-start | bytes 884744 | tf_op jit(solution)/shard_map/ppermute | solution.py:422
  64.1 16.3 %copy-start.12 = (bf16[128,1152]{1,0:T(8,128)(2,1)}, bf16[128,1152]{1,0:T(8,128)(2,1)S(1)}, u32[]{:S(2)}) copy-start(bf16[128,1152]{1,0:T(8,128)(2,1)S(1)} %collective-permute-done.8.refs_7_) | copy-start | bytes 884740
  64.1 14.7 %collective-permute-start.14 = (bf16[288,432]{1,0:T(8,128)(2,1)S(1)}, bf16[288,432]{1,0:T(8,128)(2,1)S(1)}, u32[]{:S(2)}, u32[]{:S(2)}) collective-permute-start(bf16[288,432]{1,0:T(8,128)(2,1)S(1)} %collective-permute-done.10.refs_9_.refs_1_), channel_id=1, source_target_pairs={{0,8},{1,9},{2,10},{3,11},{4,12},{5,13},{6,14},{7,15},{8,0},{9,1},... | collective-permute-start | bytes 746504 | tf_op jit(solution)/shard_map/ppermute | solution.py:460
  64.2 16.2 %copy-start.13 = (bf16[128,1152]{1,0:T(8,128)(2,1)}, bf16[128,1152]{1,0:T(8,128)(2,1)S(1)}, u32[]{:S(2)}) copy-start(bf16[128,1152]{1,0:T(8,128)(2,1)S(1)} %collective-permute-done.3.refs_2_) | copy-start | bytes 884740
  64.3 14.6 %collective-permute-start.15 = (bf16[288,432]{1,0:T(8,128)(2,1)S(1)}, bf16[288,432]{1,0:T(8,128)(2,1)S(1)}, u32[]{:S(2)}, u32[]{:S(2)}) collective-permute-start(bf16[288,432]{1,0:T(8,128)(2,1)S(1)} %collective-permute-done.11.refs_10_.refs_2_), channel_id=1, source_target_pairs={{0,8},{1,9},{2,10},{3,11},{4,12},{5,13},{6,14},{7,15},{8,0},{9,1},... | collective-permute-start | bytes 746504 | tf_op jit(solution)/shard_map/ppermute | solution.py:460
  78.8 1.7 copy-start.14
  78.8 1.6 collective-permute-start.16
  78.8 1.7 copy-start.15
  78.8 1.7 copy-start.7
  78.8 1.7 copy-start.8
  80.4 0.7 copy-start.9
  94.0 33.6 %collective-permute-start.24 = (f32[4,144,288]{2,1,0:T(8,128)}, f32[4,144,288]{2,1,0:T(8,128)S(1)}, u32[]{:S(2)}, u32[]{:S(2)}) collective-permute-start(f32[4,144,288]{2,1,0:T(8,128)} %get-tuple-element.45), channel_id=1, source_target_pairs={{0,8},{1,9},{2,10},{3,11},{4,12},{5,13},{6,14},{7,15},{8,0},{9,1},... | collective-permute-start | bytes 1990664 | tf_op jit(solution)/shard_map/ppermute | solution.py:497
  94.1 2.8 %copy-start.17 = (bf16[144,1152]{1,0:T(8,128)(2,1)}, bf16[144,1152]{1,0:T(8,128)(2,1)S(1)}, u32[]{:S(2)}) copy-start(bf16[144,1152]{1,0:T(8,128)(2,1)S(1)} %collective-permute-done.17.refs_0_) | copy-start | bytes 995332
  94.1 2.8 %collective-permute-start.18 = (bf16[144,1152]{1,0:T(8,128)(2,1)S(1)}, bf16[144,1152]{1,0:T(8,128)(2,1)S(1)}, u32[]{:S(2)}, u32[]{:S(2)}) collective-permute-start(bf16[144,1152]{1,0:T(8,128)(2,1)S(1)} %collective-permute-done.17.refs_0_), channel_id=1, source_target_pairs={{0,8},{1,9},{2,10},{3,11},{4,12},{5,13},{6,14},{7,15},{8,0},{9,1},... | collective-permute-start | bytes 995336 | tf_op jit(solution)/shard_map/ppermute | solution.py:463
  96.9 0.7 copy-start.18
  102.3 25.2 %copy-start.16 = (f32[4,144,288]{2,1,0:T(8,128)S(1)}, f32[4,144,288]{2,1,0:T(8,128)}, u32[]{:S(2)}) copy-start(f32[4,144,288]{2,1,0:T(8,128)} %get-tuple-element.44) | copy-start | bytes 1990660
  102.4 10.1 %collective-permute-start.19 = (bf16[2,64,1152]{2,1,0:T(8,128)(2,1)}, bf16[2,64,1152]{2,1,0:T(8,128)(2,1)S(1)}, u32[]{:S(2)}, u32[]{:S(2)}) collective-permute-start(bf16[2,64,1152]{2,1,0:T(8,128)(2,1)} %get-tuple-element.35), channel_id=1, source_target_pairs={{0,1},{1,0},{2,3},{3,2},{4,5},{5,4},{6,7},{7,6},{8,9},{9,8},{10,11... | collective-permute-start | bytes 884744 | tf_op jit(solution)/shard_map/ppermute | solution.py:422
  102.9 15.3 %collective-permute-start.20 = (bf16[2,64,1152]{2,1,0:T(8,128)(2,1)}, bf16[2,64,1152]{2,1,0:T(8,128)(2,1)S(1)}, u32[]{:S(2)}, u32[]{:S(2)}) collective-permute-start(bf16[2,64,1152]{2,1,0:T(8,128)(2,1)} %get-tuple-element.36), channel_id=1, source_target_pairs={{0,16},{1,17},{2,18},{3,19},{4,20},{5,21},{6,22},{7,23},{8,24},{9,... | collective-permute-start | bytes 884744 | tf_op jit(solution)/shard_map/ppermute | solution.py:422
  102.9 15.3 %collective-permute-start.21 = (bf16[2,64,1152]{2,1,0:T(8,128)(2,1)}, bf16[2,64,1152]{2,1,0:T(8,128)(2,1)S(1)}, u32[]{:S(2)}, u32[]{:S(2)}) collective-permute-start(bf16[2,64,1152]{2,1,0:T(8,128)(2,1)} %get-tuple-element.37), channel_id=1, source_target_pairs={{0,17},{1,16},{2,19},{3,18},{4,21},{5,20},{6,23},{7,22},{8,25},{9,... | collective-permute-start | bytes 884744 | tf_op jit(solution)/shard_map/ppermute | solution.py:422
  112.4 5.8 %copy-start.22 = (bf16[2,64,1152]{2,1,0:T(8,128)(2,1)}, bf16[2,64,1152]{2,1,0:T(8,128)(2,1)S(1)}, u32[]{:S(2)}) copy-start(bf16[2,64,1152]{2,1,0:T(8,128)(2,1)S(1)} %collective-permute-done.19.refs_3_) | copy-start | bytes 884740
  118.2 0.7 copy-start.23
  118.2 0.8 copy-start.24
  122.1 18.7 %collective-permute-start.22 = (bf16[64,1152]{1,0:T(8,128)(2,1)}, bf16[64,1152]{1,0:T(8,128)(2,1)S(1)}, u32[]{:S(2)}, u32[]{:S(2)}) collective-permute-start(bf16[64,1152]{1,0:T(8,128)(2,1)} %get-tuple-element.38), channel_id=1, source_target_pairs={{0,0},{1,1},{16,2},{17,3},{8,4},{9,5},{24,6},{25,7},{4,8},{5,9},{2... | collective-permute-start | bytes 442376 | tf_op jit(solution)/shard_map/ppermute | solution.py:425
  124.0 16.8 %collective-permute-start.23 = (bf16[64,1152]{1,0:T(8,128)(2,1)}, bf16[64,1152]{1,0:T(8,128)(2,1)S(1)}, u32[]{:S(2)}, u32[]{:S(2)}) collective-permute-start(bf16[64,1152]{1,0:T(8,128)(2,1)} %get-tuple-element.39), channel_id=1, source_target_pairs={{8,0},{9,1},{24,2},{25,3},{0,4},{1,5},{16,6},{17,7},{12,8},{13,9},... | collective-permute-start | bytes 442376 | tf_op jit(solution)/shard_map/ppermute | solution.py:425
  137.3 10.1 %collective-permute-start.25 = (bf16[2,64,1152]{2,1,0:T(8,128)(2,1)}, bf16[2,64,1152]{2,1,0:T(8,128)(2,1)S(1)}, u32[]{:S(2)}, u32[]{:S(2)}) collective-permute-start(bf16[2,64,1152]{2,1,0:T(8,128)(2,1)} %get-tuple-element.48), channel_id=1, source_target_pairs={{0,1},{1,0},{2,3},{3,2},{4,5},{5,4},{6,7},{7,6},{8,9},{9,8},{10,11... | collective-permute-start | bytes 884744 | tf_op jit(solution)/shard_map/ppermute | solution.py:422
  138.8 24.4 %collective-permute-start.26 = (bf16[2,64,1152]{2,1,0:T(8,128)(2,1)}, bf16[2,64,1152]{2,1,0:T(8,128)(2,1)S(1)}, u32[]{:S(2)}, u32[]{:S(2)}) collective-permute-start(bf16[2,64,1152]{2,1,0:T(8,128)(2,1)} %get-tuple-element.49), channel_id=1, source_target_pairs={{0,16},{1,17},{2,18},{3,19},{4,20},{5,21},{6,22},{7,23},{8,24},{9,... | collective-permute-start | bytes 884744 | tf_op jit(solution)/shard_map/ppermute | solution.py:422
  138.8 27.0 %collective-permute-start.27 = (bf16[2,64,1152]{2,1,0:T(8,128)(2,1)}, bf16[2,64,1152]{2,1,0:T(8,128)(2,1)S(1)}, u32[]{:S(2)}, u32[]{:S(2)}) collective-permute-start(bf16[2,64,1152]{2,1,0:T(8,128)(2,1)} %get-tuple-element.50), channel_id=1, source_target_pairs={{0,17},{1,16},{2,19},{3,18},{4,21},{5,20},{6,23},{7,22},{8,25},{9,... | collective-permute-start | bytes 884744 | tf_op jit(solution)/shard_map/ppermute | solution.py:422
  140.8 34.1 %collective-permute-start.30 = (f32[144,288]{1,0:T(8,128)S(1)}, f32[144,288]{1,0:T(8,128)S(1)}, u32[]{:S(2)}, u32[]{:S(2)}) collective-permute-start(f32[144,288]{1,0:T(8,128)S(1)} %get-tuple-element.53), channel_id=1, source_target_pairs={{0,0},{1,1},{2,8},{3,9},{4,16},{5,17},{6,24},{7,25},{8,4},{9,5},{1... | collective-permute-start | bytes 497672 | tf_op jit(solution)/shard_map/ppermute | solution.py:512
  142.7 32.4 %collective-permute-start.31 = (f32[144,288]{1,0:T(8,128)S(1)}, f32[144,288]{1,0:T(8,128)S(1)}, u32[]{:S(2)}, u32[]{:S(2)}) collective-permute-start(f32[144,288]{1,0:T(8,128)S(1)} %get-tuple-element.54), channel_id=1, source_target_pairs={{0,8},{1,9},{2,0},{3,1},{4,24},{5,25},{6,16},{7,17},{8,12},{9,13},... | collective-permute-start | bytes 497672 | tf_op jit(solution)/shard_map/ppermute | solution.py:512
  147.4 18.4 %copy-start.19 = (bf16[2,64,1152]{2,1,0:T(8,128)(2,1)}, bf16[2,64,1152]{2,1,0:T(8,128)(2,1)S(1)}, u32[]{:S(2)}) copy-start(bf16[2,64,1152]{2,1,0:T(8,128)(2,1)S(1)} %collective-permute-done.25.refs_5_) | copy-start | bytes 884740
  147.4 27.8 %collective-permute-start.32 = (f32[144,288]{1,0:T(8,128)S(1)}, f32[144,288]{1,0:T(8,128)S(1)}, u32[]{:S(2)}, u32[]{:S(2)}) collective-permute-start(f32[144,288]{1,0:T(8,128)S(1)} %get-tuple-element.55), channel_id=1, source_target_pairs={{0,16},{1,17},{2,24},{3,25},{4,0},{5,1},{6,8},{7,9},{8,20},{9,21},... | collective-permute-start | bytes 497672 | tf_op jit(solution)/shard_map/ppermute | solution.py:512
  163.1 2.7 %copy-start.20 = (bf16[2,64,1152]{2,1,0:T(8,128)(2,1)}, bf16[2,64,1152]{2,1,0:T(8,128)(2,1)S(1)}, u32[]{:S(2)}) copy-start(bf16[2,64,1152]{2,1,0:T(8,128)(2,1)S(1)} %collective-permute-done.26.refs_6_) | copy-start | bytes 884740
  163.1 12.6 %collective-permute-start.33 = (f32[144,288]{1,0:T(8,128)S(1)}, f32[144,288]{1,0:T(8,128)S(1)}, u32[]{:S(2)}, u32[]{:S(2)}) collective-permute-start(f32[144,288]{1,0:T(8,128)S(1)} %get-tuple-element.56), channel_id=1, source_target_pairs={{0,24},{1,25},{2,16},{3,17},{4,8},{5,9},{6,0},{7,1},{8,28},{9,29},... | collective-permute-start | bytes 497672 | tf_op jit(solution)/shard_map/ppermute | solution.py:512
  165.8 0.7 copy-start.21
  170.0 14.0 %collective-permute-start.28 = (bf16[64,1152]{1,0:T(8,128)(2,1)}, bf16[64,1152]{1,0:T(8,128)(2,1)S(1)}, u32[]{:S(2)}, u32[]{:S(2)}) collective-permute-start(bf16[64,1152]{1,0:T(8,128)(2,1)} %get-tuple-element.51), channel_id=1, source_target_pairs={{0,0},{1,1},{16,2},{17,3},{8,4},{9,5},{24,6},{25,7},{4,8},{5,9},{2... | collective-permute-start | bytes 442376 | tf_op jit(solution)/shard_map/ppermute | solution.py:425
  174.9 9.3 %collective-permute-start.29 = (bf16[64,1152]{1,0:T(8,128)(2,1)}, bf16[64,1152]{1,0:T(8,128)(2,1)S(1)}, u32[]{:S(2)}, u32[]{:S(2)}) collective-permute-start(bf16[64,1152]{1,0:T(8,128)(2,1)} %get-tuple-element.52), channel_id=1, source_target_pairs={{8,0},{9,1},{24,2},{25,3},{0,4},{1,5},{16,6},{17,7},{12,8},{13,9},... | collective-permute-start | bytes 442376 | tf_op jit(solution)/shard_map/ppermute | solution.py:425

commit v4 on v3

--- a/solution.py
+++ b/solution.py
@@ -88,16 +88,31 @@
 
         return self.perm(move)
 
-    def to_owner(self, j):
+    def to_owner(self):
         def move(y, c, z, x):
             s = self.row_block(y, x, c)
-            d = z ^ j
-            return d // self.nc, d % self.nc, s // self.nx, s % self.nx
+            return z // self.nc, z % self.nc, s // self.nx, s % self.nx
 
         return self.perm(move)
 
     def chip_of(self, k):
         return k // self.nx, k % self.nx
+
+    def bits(self, count):
+        return [1 << b for b in range(count.bit_length() - 1)]
+
+    def chip_bits(self, j):
+        bits = self.bits(self.chips)
+        return bits if j % 2 == 0 else bits[::-1]
+
+    def doubled(self, bits):
+        held = [0]
+        for bit in bits:
+            held = held + [k ^ bit for k in held]
+        return held
+
+    def halved(self, bit):
+        return [k for k in range(self.chips) if not k & bit]
 
     def slots(self):
         return [(k, j) for k in range(self.chips) for j in range(self.nc)]
@@ -170,11 +185,13 @@
 
 
 def fill_weights(lay, pos_ref, w_refs, w_scr):
-    rows = w_refs[0].shape[0]
+    rows = w_scr.shape[1] // lay.nz
+    order = lay.doubled(lay.bits(lay.nz)[::-1])
     for h in range(lay.halves):
-        for k in range(lay.nz):
+        for n, k in enumerate(order):
+            ref, place = w_refs[2 * h + (2 * n) // lay.nz], n % (lay.nz // 2)
             start = pl.multiple_of((pos_ref[2] ^ k) * rows, 16)
-            w_scr[h, pl.ds(start, rows), :] = w_refs[h * lay.nz + k][...]
+            w_scr[h, pl.ds(start, rows), :] = ref[place]
 
 
 def heads_stacked(lay, values):
@@ -191,33 +208,41 @@
     scores = dot_t(keys_stacked, queries) * scaling
     scores = jnp.where(allowed, scores.reshape((lay.half_heads,) + allowed.shape), -jnp.inf)
     exponent = jnp.exp(scores - jnp.max(scores, axis=1, keepdims=True))
-    return exponent / jnp.sum(exponent, axis=1, keepdims=True)
-
-
-def forward_kernel(lay, pos_ref, info_ref, *refs):
-    x_refs, refs = refs[: lay.frames], refs[lay.frames :]
-    w_refs, refs = refs[: lay.halves * lay.nz], refs[lay.halves * lay.nz :]
-    mod_ref, q_ref, k_ref, v_ref, att_ref, w_scr, hid_scr = refs
-    model = hid_scr.shape[1]
+    return exponent * (1.0 / jnp.sum(exponent, axis=1, keepdims=True))
+
+
+def prepare_kernel(lay, pos_ref, info_ref, *refs):
+    pair_refs, (mod_ref, hid_ref, gp_ref) = refs[: 2 * lay.nc], refs[2 * lay.nc :]
+    _, step_patches, model = hid_ref.shape
+    patches = step_patches * pl.num_programs(0)
+    patch_base = pos_ref[1] * patches + pl.program_id(0) * step_patches
+    patch = patch_base + lax.broadcasted_iota(jnp.int32, (step_patches, 1), 0)
+    for t, (k, j) in enumerate(lay.slots()):
+        _, limit, step = slot_scalars(lay, pos_ref, info_ref, (k, j))
+        n = lay.doubled(lay.chip_bits(j)).index(k)
+        ref, place = pair_refs[2 * j + (2 * n) // lay.chips], n % (lay.chips // 2)
+        normed, _ = normalize(ref[place, 0].astype(F32))
+        shift, scale = table_row(mod_ref, step, 0, model), table_row(mod_ref, step, 1, model)
+        hid_ref[t] = (normed * (1.0 + scale) + shift).astype(BF16)
+        factor = jnp.where(patch < limit, table_row(mod_ref, step, 2, model), 0.0)
+        gp_ref[t] = (factor * ref[place, 1].astype(F32)).astype(BF16)
+
+
+def forward_kernel(lay, pos_ref, info_ref, hid_ref, *refs):
+    w_refs, refs = refs[: 2 * lay.halves], refs[2 * lay.halves :]
+    q_ref, k_ref, v_ref, att_ref, w_scr = refs
+    _, step_patches, model = hid_ref.shape
     cols = w_scr.shape[2] // 3
     scaling = 1.0 / math.sqrt(cols // lay.half_heads)
-    step_patches = x_refs[0].shape[0]
     patches = step_patches * pl.num_programs(0)
 
     @pl.when(pl.program_id(0) == 0)
     def _():
         fill_weights(lay, pos_ref, w_refs, w_scr)
 
-    for t, slot in enumerate(lay.slots()):
-        _, _, step = slot_scalars(lay, pos_ref, info_ref, slot)
-        normed, _ = normalize(x_refs[t][...].astype(F32))
-        shift, scale = table_row(mod_ref, step, 0, model), table_row(mod_ref, step, 1, model)
-        hid_scr[t * step_patches : (t + 1) * step_patches, :] = (
-            normed * (1.0 + scale) + shift
-        ).astype(BF16)
-
+    hidden = hid_ref[...].reshape(lay.frames * step_patches, model)
     for h in range(lay.halves):
-        triple = dot(hid_scr[...], w_scr[h])
+        triple = dot(hidden, w_scr[h])
         for n, ref in enumerate((q_ref, k_ref, v_ref)):
             ref[h] = triple[:, n * cols : (n + 1) * cols].astype(BF16).reshape(ref.shape[1:])
 
@@ -238,25 +263,15 @@
         att_ref[:, b * BLOCK : (b + 1) * BLOCK, :] = attended.reshape(lay.frames, BLOCK, -1)
 
 
-def weight_grad_kernel(lay, pos_ref, info_ref, *refs):
-    g_refs, refs = refs[: lay.frames], refs[lay.frames :]
-    att_ref, mod_ref, gp_ref, kept_ref, sent_ref, acc_scr = refs
+def weight_grad_kernel(lay, pos_ref, gp_ref, att_ref, kept_ref, sent_ref, acc_scr):
     _, step_patches, model = gp_ref.shape
     tokens = lay.frames * step_patches
-    patches = step_patches * pl.num_programs(0)
     groups, block_rows, part = kept_ref.shape
     is_first = pos_ref[1] == 0
 
     @pl.when(pl.program_id(0) == 0)
     def _():
         acc_scr[...] = jnp.zeros_like(acc_scr)
-
-    patch_base = pos_ref[1] * patches + pl.program_id(0) * step_patches
-    patch = patch_base + lax.broadcasted_iota(jnp.int32, (step_patches, 1), 0)
-    for t, slot in enumerate(lay.slots()):
-        _, limit, step = slot_scalars(lay, pos_ref, info_ref, slot)
-        factor = jnp.where(patch < limit, table_row(mod_ref, step, 2, model), 0.0)
-        gp_ref[t] = (factor * g_refs[t][...].astype(F32)).astype(BF16)
 
     attended = att_ref[...].reshape(tokens, -1)
     acc_scr[...] += t_dot(attended, gp_ref[...].reshape(tokens, model))
@@ -267,14 +282,14 @@
         kept = jnp.where(is_first, first, second)
         sent = jnp.where(is_first, second, first)
         for d in range(groups):
-            kept_ref[pos_ref[2] ^ d] = kept[:, d * part : (d + 1) * part]
-            sent_ref[pos_ref[2] ^ d] = sent[:, d * part : (d + 1) * part]
+            kept_ref[d] = kept[:, d * part : (d + 1) * part]
+            sent_ref[d] = sent[:, d * part : (d + 1) * part]
 
 
 def projection_kernel(lay, pos_ref, gp_ref, att_ref, *refs):
     wo_refs, refs = refs[: lay.nc], refs[lay.nc :]
-    ga_ref, *refs = refs
-    pr_refs, (wo_scr,) = refs[: lay.chips], refs[lay.chips :]
+    ga_ref, own_ref, sent_ref, wo_scr = refs
+    own_chip = pos_ref[0] * lay.nx + pos_ref[3]
     _, step_patches, model = gp_ref.shape
     tokens = lay.frames * step_patches
     is_first = pos_ref[1] == 0
@@ -291,14 +306,16 @@
         ga_ref[h] = grad_attn[:, h * part : (h + 1) * part].astype(BF16).reshape(ga_ref.shape[1:])
     attended = att_ref[...].reshape(tokens, -1)
     projected = dot(attended, wo_scr[...]).reshape(lay.chips, lay.nc, step_patches, model)
+    own_ref[...] = projected[0]
     for k in range(lay.chips):
-        pr_refs[k][...] = projected[k].astype(pr_refs[k].dtype)
+        sent_ref[own_chip ^ k] = projected[k].astype(BF16)
 
 
 def backward_kernel(lay, pos_ref, info_ref, *refs):
-    w_refs, refs = refs[: lay.halves * lay.nz], refs[lay.halves * lay.nz :]
+    w_refs, refs = refs[: 2 * lay.halves], refs[2 * lay.halves :]
     q_ref, k_ref, v_ref, ga_ref, *refs = refs
-    gh_refs, (w_scr, gt_scr) = refs[: lay.chips], refs[lay.chips :]
+    kept_refs, refs = refs[: lay.nc], refs[lay.nc :]
+    sent_refs, (w_scr, gt_scr) = refs[: lay.nc], refs[lay.nc :]
     _, frames, step_patches, cols = q_ref.shape
     model = w_scr.shape[1]
     patches = step_patches * pl.num_programs(0)
@@ -331,44 +348,56 @@
         for h in range(lay.halves):
             part = gt_scr[h, k * lay.nc : (k + 1) * lay.nc].reshape(rows, 3 * cols)
             total = total + dot_t(part, w_scr[h])
-        gh_refs[k][...] = total.reshape(gh_refs[k].shape).astype(gh_refs[k].dtype)
+        total = total.reshape(lay.nc, step_patches, model)
+        for j in range(lay.nc):
+            first = lay.chip_bits(j)[0]
+            place = lay.halved(first).index(k & ~first)
+            if k & first:
+                sent_refs[j][place] = total[j].astype(BF16)
+            else:
+                kept_refs[j][place] = total[j]
 
 
 def output_kernel(lay, pos_ref, info_ref, *refs):
-    x_refs, refs = refs[: lay.nc], refs[lay.nc :]
-    pr_refs, refs = refs[: lay.chips], refs[lay.chips :]
-    mod_ref, *out_refs = refs
-    step_patches, model = x_refs[0].shape
+    pair_refs, refs = refs[: lay.nc], refs[lay.nc :]
+    own_ref, got_ref, refs = refs[0], refs[1], refs[2:]
+    kept_refs, refs = refs[: lay.nc], refs[lay.nc :]
+    add_refs, refs = refs[: lay.nc], refs[lay.nc :]
+    mod_ref, *refs = refs
+    out_refs, sum_refs = refs[: lay.nc], refs[lay.nc :]
+    own_chip = pos_ref[0] * lay.nx + pos_ref[3]
+    step_patches, model = out_refs[0].shape
     patches = step_patches * pl.num_programs(0)
     patch_base = pos_ref[1] * patches + pl.program_id(0) * step_patches
     patch = patch_base + lax.broadcasted_iota(jnp.int32, (step_patches, 1), 0)
     for j in range(lay.nc):
         _, limit, step = slot_scalars(lay, pos_ref, info_ref, (0, j))
         factor = jnp.where(patch < limit, table_row(mod_ref, step, 2, model), 0.0)
-        projected = pr_refs[0][j]
+        projected = own_ref[j]
         for k in range(1, lay.chips):
-            projected = projected + pr_refs[k][j].astype(F32)
+            projected = projected + got_ref[own_chip ^ k, j].astype(F32)
         projected = projected.astype(BF16).astype(F32)
-        out_refs[j][...] = (x_refs[j][...].astype(F32) + factor * projected).astype(BF16)
+        out_refs[j][...] = (pair_refs[j][0, 0].astype(F32) + factor * projected).astype(BF16)
+        sum_refs[j][...] = (kept_refs[j][1] + add_refs[j][1].astype(F32)).astype(BF16)
 
 
 def input_grad_kernel(lay, pos_ref, info_ref, *refs):
-    x_refs, refs = refs[: lay.nc], refs[lay.nc :]
-    g_refs, refs = refs[: lay.nc], refs[lay.nc :]
-    gh_refs, refs = refs[: lay.chips], refs[lay.chips :]
+    pair_refs, refs = refs[: lay.nc], refs[lay.nc :]
+    kept_refs, refs = refs[: lay.nc], refs[lay.nc :]
+    add_refs, refs = refs[: lay.nc], refs[lay.nc :]
+    last_refs, refs = refs[: lay.nc], refs[lay.nc :]
     mod_ref, *out_refs = refs
-    model = x_refs[0].shape[1]
+    model = out_refs[0].shape[1]
     for j in range(lay.nc):
         _, _, step = slot_scalars(lay, pos_ref, info_ref, (0, j))
-        grad_hidden = gh_refs[0][j]
-        for k in range(1, lay.chips):
-            grad_hidden = grad_hidden + gh_refs[k][j].astype(F32)
+        grad_hidden = kept_refs[j][0] + add_refs[j][0].astype(F32)
+        grad_hidden = grad_hidden + last_refs[j][...].astype(F32)
         grad_hidden = grad_hidden.astype(BF16).astype(F32)
-        normed, inv_sigma = normalize(x_refs[j][...].astype(F32))
+        normed, inv_sigma = normalize(pair_refs[j][0, 0].astype(F32))
         grad_norm = grad_hidden * (1.0 + table_row(mod_ref, step, 1, model))
         first_mean = jnp.mean(grad_norm, axis=-1, keepdims=True)
         second_mean = jnp.mean(grad_norm * normed, axis=-1, keepdims=True)
-        grad_x = g_refs[j][...].astype(F32) + inv_sigma * (
+        grad_x = pair_refs[j][0, 1].astype(F32) + inv_sigma * (
             grad_norm - first_mean - normed * second_mean
         )
         out_refs[j][...] = grad_x.astype(BF16)
@@ -398,7 +427,7 @@
     steps = half // step_patches
     tokens = lay.frames * step_patches
 
-    def call(kernel, name, in_specs, out_specs, out_shape, scratch=(), grid=(1,), prefetch=2):
+    def call(kernel, name, cost, in_specs, out_specs, out_shape, scratch=(), grid=(1,), prefetch=2):
         return pl.pallas_call(
             kernel,
             grid_spec=pltpu.PrefetchScalarGridSpec(
@@ -410,12 +439,20 @@
             ),
             out_shape=out_shape,
             compiler_params=pltpu.CompilerParams(vmem_limit_bytes=VMEM_LIMIT),
+            cost_estimate=pl.CostEstimate(
+                flops=cost * tokens * steps, bytes_accessed=4 * model * tokens, transcendentals=0
+            ),
             name=name,
         )
 
     def chip_swap(k):
         ky, kx = lay.chip_of(k)
         return lay.swap(ky=ky, kx=kx)
+
+    def doubling(held, bits, swap):
+        for bit in bits[:-1]:
+            held = jnp.concatenate([held, lax.ppermute(held, AXES, swap(bit))], axis=0)
+        return [held, lax.ppermute(held, AXES, swap(bits[-1]))]
 
     def over_chips(parts):
         own = [parts[0]]
@@ -433,14 +470,16 @@
     own = []
     for k in range(nc):
         start = ((z // lay.ny) ^ k) * half
-        pair = [lax.dynamic_slice_in_dim(frame[0], start, half) for frame in (frames_x, grad_y)]
-        own.append(lax.ppermute(jnp.concatenate(pair, axis=0), AXES, lay.to_plane(k)))
-    by_slot = [over_chips([part] * chips) for part in own]
-    frames = [by_slot[j][k] for k, j in lay.slots()]
+        pair = [lax.dynamic_slice_in_dim(frame, start, half, axis=1) for frame in (frames_x, grad_y)]
+        own.append(lax.ppermute(jnp.stack(pair, axis=1), AXES, lay.to_plane(k)))
+    pairs = []
+    for j in range(nc):
+        pairs += doubling(own[j], lay.chip_bits(j), chip_swap)
 
     picked = call(
         functools.partial(pick_kernel, lay, cols),
         "pick",
+        2 * model * 1000,
         [whole_spec(w_qkv.shape)],
         [whole_spec((rows, 3 * cols))] * nx,
         [struct((rows, 3 * cols))] * nx,
@@ -454,16 +493,20 @@
     else:
         stacked = jnp.stack(by_x)
         ordered = [lax.dynamic_index_in_dim(stacked, x ^ i, 0, keepdims=False) for i in range(nx)]
-    w_own = jnp.concatenate(ordered, axis=0)
-    w_pieces = [w_own] + [lax.ppermute(w_own, AXES, lay.swap(kz=kz)) for kz in range(1, lay.nz)]
+    w_own = jnp.concatenate(ordered, axis=0)[None]
+    w_pieces = doubling(w_own, lay.bits(lay.nz)[::-1], lambda kz: lay.swap(kz=kz))
     if halves > 1:
         w_pieces += [lax.ppermute(piece, AXES, lay.swap(kc=1)) for piece in w_pieces]
 
-    wo_own = lax.ppermute(w_out, AXES, lay.rows_to_chip())
+    late_w_out, _ = lax.optimization_barrier((w_out, w_pieces[:2]))
+    wo_own = lax.ppermute(late_w_out, AXES, lay.rows_to_chip())
     wo_rows = [wo_own, lax.ppermute(wo_own, AXES, lay.swap(kc=1))]
 
     x_spec = pl.BlockSpec((step_patches, model), lambda i, *_: (i, 0))
-    g_spec = pl.BlockSpec((step_patches, model), lambda i, *_: (steps + i, 0))
+
+    def pair_spec(count):
+        return pl.BlockSpec((count, 2, step_patches, model), lambda i, *_: (0, 0, i, 0))
+
     triple_spec = pl.BlockSpec((halves, lay.frames, step_patches, cols), lambda i, *_: (0, 0, i, 0))
     att_spec = pl.BlockSpec((lay.frames, step_patches, chip_width), lambda i, *_: (0, i, 0))
     gp_spec = pl.BlockSpec((lay.frames, step_patches, model), lambda i, *_: (0, i, 0))
@@ -472,78 +515,121 @@
     w_scratch = pltpu.VMEM((halves, model, 3 * cols), BF16)
     mod_spec = whole_spec(mod_table.shape)
     triple_shape = struct((halves, lay.frames, half, cols))
-    part_shapes = [struct((nc, half, model), F32)] + [struct((nc, half, model))] * (chips - 1)
+
+    hidden, grad_proj = call(
+        functools.partial(prepare_kernel, lay),
+        "prepare",
+        3 * model * 1000,
+        [pair_spec(chips // 2)] * (2 * nc) + [mod_spec],
+        [gp_spec] * 2,
+        [struct((lay.frames, half, model))] * 2,
+        grid=(steps,),
+    )(pos, info, *pairs, mod_table)
 
     queries, keys, values, attended = call(
         functools.partial(forward_kernel, lay),
         "forward",
-        [x_spec] * lay.frames + w_specs + [mod_spec],
+        8 * model * 1000,
+        [gp_spec] + w_specs,
         [triple_spec] * 3 + [att_spec],
         [triple_shape] * 3 + [struct((lay.frames, half, chip_width))],
-        [w_scratch, pltpu.VMEM((tokens, model), BF16)],
+        [w_scratch],
         (steps,),
-    )(pos, info, *frames, *w_pieces, mod_table)
+    )(pos, info, hidden, *w_pieces)
 
     piece_shape = (groups, rows, quarter)
-    grad_proj, kept, sent = call(
+    kept, sent = call(
         functools.partial(weight_grad_kernel, lay),
         "weight_grad",
-        [g_spec] * lay.frames + [att_spec, mod_spec],
-        [gp_spec] + [whole_spec(piece_shape)] * 2,
-        [struct((lay.frames, half, model))] + [struct(piece_shape, F32)] * 2,
+        4 * model * 1000,
+        [gp_spec, att_spec],
+        [whole_spec(piece_shape)] * 2,
+        [struct(piece_shape, F32)] * 2,
         [pltpu.VMEM((chip_width, model), F32)],
         (steps,),
-    )(pos, info, *frames, attended, mod_table)
+        prefetch=1,
+    )(pos, grad_proj, attended)
     got = lax.ppermute(sent, AXES, lay.swap(kc=1))
 
-    grad_attn, *projected = call(
+    grad_attn, projected, sent = call(
         functools.partial(projection_kernel, lay),
         "projection",
+        4 * model * 1000,
         [gp_spec, att_spec] + [whole_spec(w_out.shape)] * nc,
-        [triple_spec] + [part_spec] * chips,
-        [triple_shape] + part_shapes,
+        [
+            triple_spec,
+            part_spec,
+            pl.BlockSpec((chips, nc, step_patches, model), lambda i, *_: (0, 0, i, 0)),
+        ],
+        [triple_shape, struct((nc, half, model), F32), struct((chips, nc, half, model))],
         [pltpu.VMEM((chip_width, model), BF16)],
         (steps,),
         prefetch=1,
     )(pos, grad_proj, attended, *wo_rows)
-
-    pieces = [kept[j] + got[j] for j in range(groups)]
-    grad_attn, *pieces = lax.optimization_barrier((grad_attn, *pieces))
-    pieces = [lax.ppermute(piece, AXES, lay.to_owner(j)) for j, piece in enumerate(pieces)]
-    grad_w_out = sum(pieces[1:], pieces[0]) * jnp.float32(
+    others = lax.all_to_all(sent, ("y", "x"), split_axis=0, concat_axis=0, tiled=True)
+
+    cut = kept + got
+    grad_attn, cut = lax.optimization_barrier((grad_attn, cut))
+    cut = lax.all_to_all(cut, "z", split_axis=0, concat_axis=0, tiled=True)
+    grad_w_out = lax.ppermute(jnp.sum(cut, axis=0), AXES, lay.to_owner()) * jnp.float32(
         1.0 / math.sqrt(groups * lay.frames * patches)
     )
-    projected = over_chips(projected)
-
-    partial_sums = call(
+
+    def side_spec(count):
+        return pl.BlockSpec((count, step_patches, model), lambda i, *_: (0, i, 0))
+
+    side = chips // 2
+    sums = call(
         functools.partial(backward_kernel, lay),
         "backward",
+        10 * model * 1000,
         w_specs + [triple_spec] * 4,
-        [part_spec] * chips,
-        part_shapes,
+        [side_spec(side)] * (2 * nc),
+        [struct((side, half, model), F32)] * nc + [struct((side, half, model))] * nc,
         [w_scratch, pltpu.VMEM((halves, lay.frames, step_patches, 3 * cols), BF16)],
         (steps,),
     )(pos, info, *w_pieces, queries, keys, values, grad_attn)
-    grad_hidden = over_chips(partial_sums)
-
-    out_parts = call(
+    held, added = list(sums[:nc]), []
+    for j in range(nc):
+        bits = lay.chip_bits(j)
+        keys_held = lay.halved(bits[0])
+        added.append(lax.ppermute(sums[nc + j], AXES, chip_swap(bits[0])))
+        for bit in bits[1:-1]:
+            total = held[j] + added[j].astype(F32)
+            out_at = [n for n, k in enumerate(keys_held) if k & bit]
+            in_at = [n for n, k in enumerate(keys_held) if not k & bit]
+            out_part = jnp.stack([total[n] for n in out_at]).astype(BF16)
+            held[j] = jnp.stack([total[n] for n in in_at])
+            added[j] = lax.ppermute(out_part, AXES, chip_swap(bit))
+            keys_held = [keys_held[n] for n in in_at]
+
+    *out_parts, last0, last1 = call(
         functools.partial(output_kernel, lay),
         "output",
-        [x_spec] * nc + [part_spec] * chips + [mod_spec],
+        3 * model * 1000,
+        [pair_spec(1)] * nc
+        + [part_spec, pl.BlockSpec((chips, nc, step_patches, model), lambda i, *_: (0, 0, i, 0))]
+        + [side_spec(2)] * (2 * nc)
+        + [mod_spec],
+        [x_spec] * (2 * nc),
+        [struct((half, model))] * (2 * nc),
+        grid=(steps,),
+    )(pos, info, *own, projected, others, *held, *added, mod_table)
+    last = [
+        lax.ppermute(part, AXES, chip_swap(lay.chip_bits(j)[-1]))
+        for j, part in enumerate((last0, last1))
+    ]
+    out_y = from_plane(out_parts)
+
+    grad_parts = call(
+        functools.partial(input_grad_kernel, lay),
+        "input_grad",
+        3 * model * 1000,
+        [pair_spec(1)] * nc + [side_spec(1)] * (2 * nc) + [x_spec] * nc + [mod_spec],
         [x_spec] * nc,
         [struct((half, model))] * nc,
         grid=(steps,),
-    )(pos, info, *own, *projected, mod_table)
-    out_y = from_plane(out_parts)
-
-    grad_parts = call(
-        functools.partial(input_grad_kernel, lay),
-        "input_grad",
-        [x_spec] * nc + [g_spec] * nc + [part_spec] * chips + [mod_spec],
-        [x_spec] * nc,
-        [struct((half, model))] * nc,
-        grid=(steps,),
-    )(pos, info, *own, *own, *grad_hidden, mod_table)
+    )(pos, info, *own, *held, *added, *last, mod_table)
     grad_x = from_plane(grad_parts)
     return out_y, grad_x, grad_w_out
 

time: 185 us -> 170 us (0.919)
  waiting for transfers between devices: 95 us -> 68.6 us
  Pallas kernels: 36.9 us -> 41.6 us
  starting transfers between devices: 43.8 us -> 46.5 us
  local copies, waits for them, and re-layouts: 4.08 us -> 6.61 us
    ppermute x22 -> x14, waiting for transfers between devices: 61.3 us -> 43.5 us  [the longest x3 11.7 us: doubling(): return [held, lax.ppermute(held, AXES, swap(bits[-1]))]]
    ppermute x1, waiting for transfers between devices: 21.3 us -> 3.53 us  [local(): info = lax.ppermute(info, AXES, lay.to_plane(0))[0]]
    ppermute x4, waiting for transfers between devices: 7.61 us -> 18.1 us  [from_plane(): lax.ppermute(part, AXES, lay.from_plane(k))]
    all_to_all x0 -> x2, starting transfers between devices: none -> 8.12 us  [the longest x1 4.29 us: local(): cut = lax.all_to_all(cut, 'z', split_axis=0, concat_axis=0, tiled=True)]
    ppermute x22 -> x14, starting transfers between devices: 27.1 us -> 19.3 us  [the longest x2 4.31 us: local(): own.append(lax.ppermute(jnp.stack(pair, axis=1), AXES, lay.to_plane(k)))]
    pallas_call x7 -> x8, Pallas kernels: 36.9 us -> 41.6 us  [the longest x1 9.7 us: local(): call(functools.partial(backward_kernel, lay), 'backward', 10 * model * 10...]
    unnamed x60 -> x52, local copies, waits for them, and re-layouts: 2.9 us -> 5.37 us
    ppermute x1, starting transfers between devices: 0.14 us -> 2.37 us  [local(): got = lax.ppermute(sent, AXES, lay.swap(kc=1))]
  transfers between devices with their start and end apart: 34 -> 26, of which waited for: 14 -> 11; matrix products, arithmetic and copies ran while one was open for 2% -> 3% of each run, Pallas kernels for 20% -> 22%
where the time goes in v4:
time: 170 us; the launch traced here: 169 us
  waiting for transfers between devices  68.6 us (40%)
  starting transfers between devices  46.5 us (27%)
  Pallas kernels  41.6 us (24%)
  local copies, waits for them, and re-layouts  6.61 us (4%)
  other arithmetic  5.15 us (3%)
    ppermute x4, waiting for transfers between devices, from_plane(): lax.ppermute(part, AXES, lay.from_plane(k))  18.1 us
    ppermute x4, starting transfers between devices, from_plane(): lax.ppermute(part, AXES, lay.from_plane(k))  12.3 us
    ppermute x3, waiting for transfers between devices, doubling(): return [held, lax.ppermute(held, AXES, swap(bits[-1]))]  11.7 us
    pallas_call x1, Pallas kernels, local(): call(functools.partial(backward_kernel, lay), 'backward', 10 * model * 10...  9.7 us
    ppermute x2, waiting for transfers between devices, local(): own.append(lax.ppermute(jnp.stack(pair, axis=1), AXES, lay.to_plane(k)))  9.67 us
    ppermute x2, waiting for transfers between devices, local(): added.append(lax.ppermute(sums[nc + j], AXES, chip_swap(bits[0])))  8.62 us
    pallas_call x1, Pallas kernels, local(): call(functools.partial(forward_kernel, lay), 'forward', 8 * model * 1000,...  7.82 us
    ppermute x1, waiting for transfers between devices, local(): lax.ppermute(jnp.sum(cut, axis=0), AXES, lay.to_owner())  6.96 us
  transfers between devices with their start and end apart: 26, of which 11 were waited for; matrix products, arithmetic and copies ran while one was open for 3% of the time, Pallas kernels for 22%

profile of v4, /device:TPU:4, one launch (start us, length us, event | category | flops | bytes accessed | tf_op | source)
XLA Modules:
  0.0 169.5 jit_solution(14509374259312990701)
XLA Ops:
  0.7 1.2 dynamic-slice_bitcast_fusion
  1.9 1.0 collective-permute-start.2
  2.9 0.7 pad_add_fusion.pos_ref
  3.6 2.9 %pick.1 = (bf16[144,432]{1,0:T(8,128)(2,1)}, bf16[144,432]{1,0:T(8,128)(2,1)}) custom-call(s32[4]{0:T(128)} %pad_add_fusion.pos_ref, bf16[144,3456]{1,0:T(8,128)(2,1)} %w_ref.1), custom_call_target="tpu_custom_call" | custom-call | flops 1179648000 | bytes 2359296 | tf_op jit(solution)/shard_map/pick/pallas_call | solution.py:479
  6.4 1.5 collective-permute-start.7
  8.0 3.3 %collective-permute-start.1 = (bf16[1,2,64,1152]{3,2,1,0:T(8,128)(2,1)S(1)}, bf16[1,2,64,1152]{3,2,1,0:T(8,128)(2,1)S(1)}, u32[]{:S(2)}, u32[]{:S(2)}) collective-permute-start(bf16[1,2,64,1152]{3,2,1,0:T(8,128)(2,1)S(1)} %pad_maximum_fusion.1), channel_id=1, source_target_pairs={{0,0},{1,1},{2,16},{3,17},{4,8},{5,9},{6,24},{7,25},{8,4},{9,5},{1... | collective-permute-start | bytes 884744 | tf_op jit(solution)/shard_map/ppermute | solution.py:474
  11.3 0.9 collective-permute-done.7
  12.2 0.9 broadcast_select_fusion.1
  13.2 3.0 %collective-permute-start.8 = (bf16[1,288,432]{2,1,0:T(8,128)(2,1)S(1)}, bf16[1,288,432]{2,1,0:T(8,128)(2,1)S(1)}, u32[]{:S(2)}, u32[]{:S(2)}) collective-permute-start(bf16[1,288,432]{2,1,0:T(8,128)(2,1)S(1)} %maximum_bitcast_fusion), channel_id=1, source_target_pairs={{0,4},{1,5},{2,6},{3,7},{4,0},{5,1},{6,2},{7,3},{8,12},{9,13},{10,... | collective-permute-start | bytes 746504 | tf_op jit(solution)/shard_map/ppermute | solution.py:454
  16.2 0.1 collective-permute-start.5
  16.3 9.7 %collective-permute-done.1.refs_0_ = bf16[1,2,64,1152]{3,2,1,0:T(8,128)(2,1)S(1)} collective-permute-done((bf16[1,2,64,1152]{3,2,1,0:T(8,128)(2,1)S(1)}, bf16[1,2,64,1152]{3,2,1,0:T(8,128)(2,1)S(1)}, u32[]{:S(2)}, u32[]{:S(2)}) %collective-permute-start.1) | collective-permute-done | bytes 294944 | tf_op jit(solution)/shard_map/ppermute | solution.py:474
  26.0 1.2 collective-permute-start.3
  27.2 0.0 copy-start.7
  27.3 6.5 %collective-permute-done.8 = bf16[1,288,432]{2,1,0:T(8,128)(2,1)S(1)} collective-permute-done((bf16[1,288,432]{2,1,0:T(8,128)(2,1)S(1)}, bf16[1,288,432]{2,1,0:T(8,128)(2,1)S(1)}, u32[]{:S(2)}, u32[]{:S(2)}) %collective-permute-start.8) | collective-permute-done | bytes 248864 | tf_op jit(solution)/shard_map/ppermute | solution.py:454
  33.8 0.1 pad_maximum_fusion.refs_0_
  33.9 0.1 collective-permute-start.9
  34.0 0.6 collective-permute-start.6
  34.7 0.9 collective-permute-start.4
  35.6 11.7 %collective-permute-done.9.refs_1_ = bf16[2,288,432]{2,1,0:T(8,128)(2,1)S(1)} collective-permute-done((bf16[2,288,432]{2,1,0:T(8,128)(2,1)S(1)}, bf16[2,288,432]{2,1,0:T(8,128)(2,1)S(1)}, u32[]{:S(2)}, u32[]{:S(2)}) %collective-permute-start.9) | collective-permute-done | bytes 497696 | tf_op jit(solution)/shard_map/ppermute | solution.py:455
  47.3 0.1 add_bitcast_fusion
  47.4 2.8 %collective-permute-start = (s32[1,16]{1,0:T(1,128)S(1)}, s32[1,16]{1,0:T(1,128)S(1)}, u32[]{:S(2)}, u32[]{:S(2)}) collective-permute-start(s32[1,16]{1,0:T(1,128)S(1)} %add_bitcast_fusion), channel_id=1, source_target_pairs={{0,0},{1,1},{2,16},{3,17},{4,8},{5,9},{6,24},{7,25},{8,4},{9,5},{1... | collective-permute-start | bytes 200 | tf_op jit(solution)/shard_map/ppermute | solution.py:468
  50.2 3.5 %collective-permute-done = s32[1,16]{1,0:T(1,128)S(1)} collective-permute-done((s32[1,16]{1,0:T(1,128)S(1)}, s32[1,16]{1,0:T(1,128)S(1)}, u32[]{:S(2)}, u32[]{:S(2)}) %collective-permute-start) | collective-permute-done | bytes 96 | tf_op jit(solution)/shard_map/ppermute | solution.py:468
  53.7 2.8 %collective-permute-start.12 = (bf16[144,1152]{1,0:T(8,128)(2,1)S(1)}, bf16[144,1152]{1,0:T(8,128)(2,1)S(1)}, u32[]{:S(2)}, u32[]{:S(2)}) collective-permute-start(bf16[144,1152]{1,0:T(8,128)(2,1)S(1)} %copy-done.15), channel_id=1, source_target_pairs={{0,0},{1,1},{2,16},{3,17},{4,8},{5,9},{6,24},{7,25},{8,4},{9,5},{1... | collective-permute-start | bytes 995336 | tf_op jit(solution)/shard_map/ppermute | solution.py:502
  56.6 0.8 copy-done.13
  57.4 0.2 copy-done.14
  57.6 5.0 %prepare.1 = (bf16[8,64,1152]{2,1,0:T(8,128)(2,1)}, bf16[8,64,1152]{2,1,0:T(8,128)(2,1)}) custom-call(s32[4]{0:T(128)} %pad_add_fusion.pos_ref, s32[16]{0:T(128)} %bitcast.27, bf16[2,2,64,1152]{3,2,1,0:T(8,128)(2,1)} %copy-done.6, bf16[2,2,64,1152]{3,2,1,0:T(8,128)(2,1)} %copy-done.14, bf16[2,2,64,1152]{3,2,1,0:T(8,128)(2,1)} %copy-done.5, ...), custom_call_target="tpu_custom_call" | custom-call | flops 1769472000 | bytes 2359296 | tf_op jit(solution)/shard_map/prepare/pallas_call | solution.py:519
  62.6 0.8 copy-done.11
  63.4 0.2 copy-done.12
  63.6 7.8 %forward.1 = (bf16[2,8,64,144]{3,2,1,0:T(8,128)(2,1)}, bf16[2,8,64,144]{3,2,1,0:T(8,128)(2,1)}, bf16[2,8,64,144]{3,2,1,0:T(8,128)(2,1)}, bf16[8,64,288]{2,1,0:T(8,128)(2,1)}) custom-call(s32[4]{0:T(128)} %pad_add_fusion.pos_ref, s32[16]{0:T(128)} %bitcast.28, bf16[8,64,1152]{2,1,0:T(8,128)(2,1)} %get-tuple-element.30.hid_ref, ...), custom_call_target="tpu_custom_call" | custom-call | flops 4718592000 | bytes 2359296 | tf_op jit(solution)/shard_map/forward/pallas_call | solution.py:529
  71.4 4.1 %weight_grad.1 = (f32[4,144,288]{2,1,0:T(8,128)}, f32[4,144,288]{2,1,0:T(8,128)}) custom-call(s32[4]{0:T(128)} %pad_add_fusion.pos_ref, bf16[8,64,1152]{2,1,0:T(8,128)(2,1)} %get-tuple-element.29.gp_ref, bf16[8,64,288]{2,1,0:T(8,128)(2,1)} %get-tuple-element.33.att_ref), custom_call_target="tpu_custom_call" | custom-call | flops 2359296000 | bytes 2359296 | tf_op jit(solution)/shard_map/weight_grad/pallas_call | solution.py:541
  75.5 2.4 %collective-permute-start.14 = (f32[4,144,288]{2,1,0:T(8,128)}, f32[4,144,288]{2,1,0:T(8,128)S(1)}, u32[]{:S(2)}, u32[]{:S(2)}) collective-permute-start(f32[4,144,288]{2,1,0:T(8,128)} %get-tuple-element.42), channel_id=1, source_target_pairs={{0,8},{1,9},{2,10},{3,11},{4,12},{5,13},{6,14},{7,15},{8,0},{9,1},... | collective-permute-start | bytes 1990664 | tf_op jit(solution)/shard_map/ppermute | solution.py:552
  77.9 0.1 collective-permute-start.13
  78.0 2.4 %collective-permute-done.13.refs_1_ = bf16[144,1152]{1,0:T(8,128)(2,1)S(1)} collective-permute-done((bf16[144,1152]{1,0:T(8,128)(2,1)S(1)}, bf16[144,1152]{1,0:T(8,128)(2,1)S(1)}, u32[]{:S(2)}, u32[]{:S(2)}) %collective-permute-start.13) | collective-permute-done | bytes 331808 | tf_op jit(solution)/shard_map/ppermute | solution.py:503
  80.4 0.7 copy-done.17
  81.1 4.9 %projection.1 = (bf16[2,8,64,144]{3,2,1,0:T(8,128)(2,1)}, f32[2,64,1152]{2,1,0:T(8,128)}, bf16[4,2,64,1152]{3,2,1,0:T(8,128)(2,1)}) custom-call(s32[4]{0:T(128)} %pad_add_fusion.pos_ref, bf16[8,64,1152]{2,1,0:T(8,128)(2,1)} %get-tuple-element.29.gp_ref, bf16[8,64,288]{2,1,0:T(8,128)(2,1)} %get-tuple-element.33.att_ref, bf16[144,1152]{1,0:T(8,128)(2,1)} %copy-done.16, ...), custom_call_target="tpu_custom_call" | custom-call | flops 2359296000 | bytes 2359296 | tf_op jit(solution)/shard_map/projection/pallas_call | solution.py:554
  86.1 3.8 %all-to-all-start = ((bf16[4,2,64,1152]{3,2,1,0:T(8,128)(2,1)}), bf16[4,2,64,1152]{3,2,1,0:T(8,128)(2,1)S(1)}, u32[]{:S(2)}, u32[]{:S(2)}) async-start(bf16[4,2,64,1152]{3,2,1,0:T(8,128)(2,1)} %get-tuple-element.36), calls=%async_computation | async-start | bytes 2359296 | tf_op jit(solution)/shard_map/all_to_all | solution.py:569
  89.9 1.0 add.14
  90.9 9.7 %backward.1 = (f32[2,64,1152]{2,1,0:T(8,128)}, f32[2,64,1152]{2,1,0:T(8,128)}, bf16[2,64,1152]{2,1,0:T(8,128)(2,1)}, bf16[2,64,1152]{2,1,0:T(8,128)(2,1)}) custom-call(s32[4]{0:T(128)} %pad_add_fusion.pos_ref, s32[16]{0:T(128)} %bitcast.29, bf16[2,288,432]{2,1,0:T(8,128)(2,1)} %copy-done.2, bf16[2,288,432]{2,1,0:T(8,128)(2,1)} %copy-done.10, ...), custom_call_target="tpu_custom_call" | custom-call | flops 5898240000 | bytes 2359296 | tf_op jit(solution)/shard_map/backward/pallas_call | solution.py:582
  100.6 1.3 collective-permute-start.15
  101.9 0.6 collective-permute-start.16
  102.5 8.6 %collective-permute-done.15.refs_6_.refs_4_ = bf16[2,64,1152]{2,1,0:T(8,128)(2,1)S(1)} collective-permute-done((bf16[2,64,1152]{2,1,0:T(8,128)(2,1)}, bf16[2,64,1152]{2,1,0:T(8,128)(2,1)S(1)}, u32[]{:S(2)}, u32[]{:S(2)}) %collective-permute-start.15) | collective-permute-done | bytes 294944 | tf_op jit(solution)/shard_map/ppermute | solution.py:596
  111.1 0.7 copy-done.18
  111.8 0.1 copy-done.19
  112.0 0.4 copy-done
  112.4 3.9 %output.1 = (bf16[64,1152]{1,0:T(8,128)(2,1)}, bf16[64,1152]{1,0:T(8,128)(2,1)}, bf16[64,1152]{1,0:T(8,128)(2,1)}, bf16[64,1152]{1,0:T(8,128)(2,1)}) custom-call(s32[4]{0:T(128)} %pad_add_fusion.pos_ref, s32[16]{0:T(128)} %bitcast.30, bf16[1,2,64,1152]{3,2,1,0:T(8,128)(2,1)} %copy-done.4, bf16[1,2,64,1152]{3,2,1,0:T(8,128)(2,1)} %copy-done.3, ...), custom_call_target="tpu_custom_call" | custom-call | flops 1769472000 | bytes 2359296 | tf_op jit(solution)/shard_map/output/pallas_call | solution.py:606
  116.3 1.1 collective-permute-start.19
  117.4 1.4 collective-permute-start.20
  118.8 4.3 %all-to-all-start.1 = ((f32[4,144,288]{2,1,0:T(8,128)}), f32[4,144,288]{2,1,0:T(8,128)S(1)}, u32[]{:S(2)}, u32[]{:S(2)}) async-start(f32[4,144,288]{2,1,0:T(8,128)} %add.14), calls=%async_computation.1 | async-start | bytes 1769472 | tf_op jit(solution)/shard_map/all_to_all | solution.py:573
  123.1 4.0 %collective-permute-start.17 = (bf16[64,1152]{1,0:T(8,128)(2,1)S(1)}, bf16[64,1152]{1,0:T(8,128)(2,1)S(1)}, u32[]{:S(2)}, u32[]{:S(2)}) collective-permute-start(bf16[64,1152]{1,0:T(8,128)(2,1)S(1)} %copy-done.21), channel_id=1, source_target_pairs={{0,0},{1,1},{16,2},{17,3},{8,4},{9,5},{24,6},{25,7},{4,8},{5,9},{2... | collective-permute-start | bytes 442376 | tf_op jit(solution)/shard_map/ppermute | solution.py:462
  127.2 1.9 %collective-permute-start.18 = (bf16[64,1152]{1,0:T(8,128)(2,1)S(1)}, bf16[64,1152]{1,0:T(8,128)(2,1)S(1)}, u32[]{:S(2)}, u32[]{:S(2)}) collective-permute-start(bf16[64,1152]{1,0:T(8,128)(2,1)S(1)} %copy-done.20), channel_id=1, source_target_pairs={{8,0},{9,1},{24,2},{25,3},{0,4},{1,5},{16,6},{17,7},{12,8},{13,9},... | collective-permute-start | bytes 442376 | tf_op jit(solution)/shard_map/ppermute | solution.py:462
  129.1 0.7 copy-done.22
  129.7 0.6 copy-done.23
  130.4 3.3 %input_grad.1 = (bf16[64,1152]{1,0:T(8,128)(2,1)}, bf16[64,1152]{1,0:T(8,128)(2,1)}) custom-call(s32[4]{0:T(128)} %pad_add_fusion.pos_ref, s32[16]{0:T(128)} %bitcast.31, bf16[1,2,64,1152]{3,2,1,0:T(8,128)(2,1)} %copy-done.4, bf16[1,2,64,1152]{3,2,1,0:T(8,128)(2,1)} %copy-done.3, f32[2,64,1152]{2,1,0:T(8,128)} %get-tuple-element.44.refs_4_.refs_2_, ...), custom_call_target="tpu_custom_call" | custom-call | flops 1769472000 | bytes 2359296 | tf_op jit(solution)/shard_map/input_grad/pallas_call | solution.py:624
  133.7 2.4 %collective-permute-start.21 = (bf16[64,1152]{1,0:T(8,128)(2,1)}, bf16[64,1152]{1,0:T(8,128)(2,1)S(1)}, u32[]{:S(2)}, u32[]{:S(2)}) collective-permute-start(bf16[64,1152]{1,0:T(8,128)(2,1)} %get-tuple-element.52), channel_id=1, source_target_pairs={{0,0},{1,1},{16,2},{17,3},{8,4},{9,5},{24,6},{25,7},{4,8},{5,9},{2... | collective-permute-start | bytes 442376 | tf_op jit(solution)/shard_map/ppermute | solution.py:462
  136.1 4.0 %collective-permute-start.22 = (bf16[64,1152]{1,0:T(8,128)(2,1)}, bf16[64,1152]{1,0:T(8,128)(2,1)S(1)}, u32[]{:S(2)}, u32[]{:S(2)}) collective-permute-start(bf16[64,1152]{1,0:T(8,128)(2,1)} %get-tuple-element.53), channel_id=1, source_target_pairs={{8,0},{9,1},{24,2},{25,3},{0,4},{1,5},{16,6},{17,7},{12,8},{13,9},... | collective-permute-start | bytes 442376 | tf_op jit(solution)/shard_map/ppermute | solution.py:462
  140.1 1.8 %collective-permute-done.17 = bf16[64,1152]{1,0:T(8,128)(2,1)S(1)} collective-permute-done((bf16[64,1152]{1,0:T(8,128)(2,1)S(1)}, bf16[64,1152]{1,0:T(8,128)(2,1)S(1)}, u32[]{:S(2)}, u32[]{:S(2)}) %collective-permute-start.17) | collective-permute-done | bytes 147488 | tf_op jit(solution)/shard_map/ppermute | solution.py:462
  141.9 3.2 %collective-permute-done.18 = bf16[64,1152]{1,0:T(8,128)(2,1)S(1)} collective-permute-done((bf16[64,1152]{1,0:T(8,128)(2,1)S(1)}, bf16[64,1152]{1,0:T(8,128)(2,1)S(1)}, u32[]{:S(2)}, u32[]{:S(2)}) %collective-permute-start.18) | collective-permute-done | bytes 147488 | tf_op jit(solution)/shard_map/ppermute | solution.py:462
  145.2 0.7 maximum_bitcast_fusion.1
  145.9 13.2 %collective-permute-done.21 = bf16[64,1152]{1,0:T(8,128)(2,1)S(1)} collective-permute-done((bf16[64,1152]{1,0:T(8,128)(2,1)}, bf16[64,1152]{1,0:T(8,128)(2,1)S(1)}, u32[]{:S(2)}, u32[]{:S(2)}) %collective-permute-start.21) | collective-permute-done | bytes 147488 | tf_op jit(solution)/shard_map/ppermute | solution.py:462
  159.1 0.1 reduce_sum.9
  159.2 1.9 %collective-permute-start.23 = (f32[144,288]{1,0:T(8,128)S(1)}, f32[144,288]{1,0:T(8,128)S(1)}, u32[]{:S(2)}, u32[]{:S(2)}) collective-permute-start(f32[144,288]{1,0:T(8,128)S(1)} %reduce_sum.9), channel_id=1, source_target_pairs={{0,0},{1,1},{2,8},{3,9},{4,16},{5,17},{6,24},{7,25},{8,4},{9,5},{1... | collective-permute-start | bytes 497672 | tf_op jit(solution)/shard_map/ppermute | solution.py:574
  161.1 0.7 maximum_bitcast_fusion.2
  161.8 7.0 %collective-permute-done.23 = f32[144,288]{1,0:T(8,128)S(1)} collective-permute-done((f32[144,288]{1,0:T(8,128)S(1)}, f32[144,288]{1,0:T(8,128)S(1)}, u32[]{:S(2)}, u32[]{:S(2)}) %collective-permute-start.23) | collective-permute-done | bytes 165920 | tf_op jit(solution)/shard_map/ppermute | solution.py:574
  168.8 0.7 broadcast_multiply_fusion
  (65 shorter events, 0.4 us)
Async XLA Ops:
  1.9 14.3 %collective-permute-start.2 = (bf16[1,2,64,1152]{3,2,1,0:T(8,128)(2,1)S(1)}, bf16[1,2,64,1152]{3,2,1,0:T(8,128)(2,1)S(1)}, u32[]{:S(2)}, u32[]{:S(2)}) collective-permute-start(bf16[1,2,64,1152]{3,2,1,0:T(8,128)(2,1)S(1)} %pad_maximum_fusion.2), channel_id=1, source_target_pairs={{0,8},{1,9},{2,24},{3,25},{4,0},{5,1},{6,16},{7,17},{8,12},{9,13},... | collective-permute-start | bytes 884744 | tf_op jit(solution)/shard_map/ppermute | solution.py:474
  6.4 5.7 %collective-permute-start.7 = (bf16[144,432]{1,0:T(8,128)(2,1)}, bf16[144,432]{1,0:T(8,128)(2,1)S(1)}, u32[]{:S(2)}, u32[]{:S(2)}) collective-permute-start(bf16[144,432]{1,0:T(8,128)(2,1)} %get-tuple-element.32), channel_id=1, source_target_pairs={{0,1},{1,0},{2,3},{3,2},{4,5},{5,4},{6,7},{7,6},{8,9},{9,8},{10,11... | collective-permute-start | bytes 373256 | tf_op jit(solution)/shard_map/ppermute | solution.py:489
  8.0 18.0 %collective-permute-start.1 = (bf16[1,2,64,1152]{3,2,1,0:T(8,128)(2,1)S(1)}, bf16[1,2,64,1152]{3,2,1,0:T(8,128)(2,1)S(1)}, u32[]{:S(2)}, u32[]{:S(2)}) collective-permute-start(bf16[1,2,64,1152]{3,2,1,0:T(8,128)(2,1)S(1)} %pad_maximum_fusion.1), channel_id=1, source_target_pairs={{0,0},{1,1},{2,16},{3,17},{4,8},{5,9},{6,24},{7,25},{8,4},{9,5},{1... | collective-permute-start | bytes 884744 | tf_op jit(solution)/shard_map/ppermute | solution.py:474
  13.2 20.6 %collective-permute-start.8 = (bf16[1,288,432]{2,1,0:T(8,128)(2,1)S(1)}, bf16[1,288,432]{2,1,0:T(8,128)(2,1)S(1)}, u32[]{:S(2)}, u32[]{:S(2)}) collective-permute-start(bf16[1,288,432]{2,1,0:T(8,128)(2,1)S(1)} %maximum_bitcast_fusion), channel_id=1, source_target_pairs={{0,4},{1,5},{2,6},{3,7},{4,0},{5,1},{6,2},{7,3},{8,12},{9,13},{10,... | collective-permute-start | bytes 746504 | tf_op jit(solution)/shard_map/ppermute | solution.py:454
  16.2 17.7 %copy-start.3 = (bf16[1,2,64,1152]{3,2,1,0:T(8,128)(2,1)}, bf16[1,2,64,1152]{3,2,1,0:T(8,128)(2,1)S(1)}, u32[]{:S(2)}) copy-start(bf16[1,2,64,1152]{3,2,1,0:T(8,128)(2,1)S(1)} %collective-permute-done.2.refs_1_) | copy-start | bytes 884740
  16.2 17.8 %collective-permute-start.5 = (bf16[1,2,64,1152]{3,2,1,0:T(8,128)(2,1)S(1)}, bf16[1,2,64,1152]{3,2,1,0:T(8,128)(2,1)S(1)}, u32[]{:S(2)}, u32[]{:S(2)}) collective-permute-start(bf16[1,2,64,1152]{3,2,1,0:T(8,128)(2,1)S(1)} %collective-permute-done.2.refs_1_), channel_id=1, source_target_pairs={{0,16},{1,17},{2,18},{3,19},{4,20},{5,21},{6,22},{7,23},{8,24},{9,... | collective-permute-start | bytes 884744 | tf_op jit(solution)/shard_map/ppermute | solution.py:454
  26.0 8.1 %copy-start.4 = (bf16[1,2,64,1152]{3,2,1,0:T(8,128)(2,1)}, bf16[1,2,64,1152]{3,2,1,0:T(8,128)(2,1)S(1)}, u32[]{:S(2)}) copy-start(bf16[1,2,64,1152]{3,2,1,0:T(8,128)(2,1)S(1)} %collective-permute-done.1.refs_0_) | copy-start | bytes 884740
  26.0 8.7 %collective-permute-start.3 = (bf16[1,2,64,1152]{3,2,1,0:T(8,128)(2,1)S(1)}, bf16[1,2,64,1152]{3,2,1,0:T(8,128)(2,1)S(1)}, u32[]{:S(2)}, u32[]{:S(2)}) collective-permute-start(bf16[1,2,64,1152]{3,2,1,0:T(8,128)(2,1)S(1)} %collective-permute-done.1.refs_0_), channel_id=1, source_target_pairs={{0,1},{1,0},{2,3},{3,2},{4,5},{5,4},{6,7},{7,6},{8,9},{9,8},{10,11... | collective-permute-start | bytes 884744 | tf_op jit(solution)/shard_map/ppermute | solution.py:454
  27.2 20.1 %copy-start.7 = (s32[1,4]{1,0:T(1,128)S(1)}, s32[1,4]{1,0:T(1,128)}, u32[]{:S(2)}) copy-start(s32[1,4]{1,0:T(1,128)} %param.12) | copy-start | bytes 52
  27.2 20.1 %copy-start.8 = (s32[1,4]{1,0:T(1,128)S(1)}, s32[1,4]{1,0:T(1,128)}, u32[]{:S(2)}) copy-start(s32[1,4]{1,0:T(1,128)} %param.11) | copy-start | bytes 52
  27.2 20.1 %copy-start.9 = (s32[1,8]{1,0:T(1,128)S(1)}, s32[1,8]{1,0:T(1,128)}, u32[]{:S(2)}) copy-start(s32[1,8]{1,0:T(1,128)} %param.10) | copy-start | bytes 100
  27.3 26.5 %copy-start.15 = (bf16[144,1152]{1,0:T(8,128)(2,1)S(1)}, bf16[144,1152]{1,0:T(8,128)(2,1)}, u32[]{:S(2)}) copy-start(bf16[144,1152]{1,0:T(8,128)(2,1)} %param.15) | copy-start | bytes 995332
  33.9 28.7 %copy-start.2 = (bf16[2,288,432]{2,1,0:T(8,128)(2,1)}, bf16[2,288,432]{2,1,0:T(8,128)(2,1)S(1)}, u32[]{:S(2)}) copy-start(bf16[2,288,432]{2,1,0:T(8,128)(2,1)S(1)} %pad_maximum_fusion.refs_0_) | copy-start | bytes 1492996
  33.9 13.4 %collective-permute-start.9 = (bf16[2,288,432]{2,1,0:T(8,128)(2,1)S(1)}, bf16[2,288,432]{2,1,0:T(8,128)(2,1)S(1)}, u32[]{:S(2)}, u32[]{:S(2)}) collective-permute-start(bf16[2,288,432]{2,1,0:T(8,128)(2,1)S(1)} %pad_maximum_fusion.refs_0_), channel_id=1, source_target_pairs={{0,2},{1,3},{2,0},{3,1},{4,6},{5,7},{6,4},{7,5},{8,10},{9,11},{10,... | collective-permute-start | bytes 1493000 | tf_op jit(solution)/shard_map/ppermute | solution.py:455
  34.0 22.5 %copy-start.5 = (bf16[2,2,64,1152]{3,2,1,0:T(8,128)(2,1)}, bf16[2,2,64,1152]{3,2,1,0:T(8,128)(2,1)S(1)}, u32[]{:S(2)}) copy-start(bf16[2,2,64,1152]{3,2,1,0:T(8,128)(2,1)S(1)} %constant_dynamic-update-slice_fusion.2.refs_2_) | copy-start | bytes 1769476
  34.0 22.5 %collective-permute-start.6 = (bf16[2,2,64,1152]{3,2,1,0:T(8,128)(2,1)S(1)}, bf16[2,2,64,1152]{3,2,1,0:T(8,128)(2,1)S(1)}, u32[]{:S(2)}, u32[]{:S(2)}) collective-permute-start(bf16[2,2,64,1152]{3,2,1,0:T(8,128)(2,1)S(1)} %constant_dynamic-update-slice_fusion.2.refs_2_), channel_id=1, source_target_pairs={{0,1},{1,0},{2,3},{3,2},{4,5},{5,4},{6,7},{7,6},{8,9},{9,8},{10,11... | collective-permute-start | bytes 1769480 | tf_op jit(solution)/shard_map/ppermute | solution.py:455
  34.7 21.9 %copy-start.6 = (bf16[2,2,64,1152]{3,2,1,0:T(8,128)(2,1)}, bf16[2,2,64,1152]{3,2,1,0:T(8,128)(2,1)S(1)}, u32[]{:S(2)}) copy-start(bf16[2,2,64,1152]{3,2,1,0:T(8,128)(2,1)S(1)} %constant_dynamic-update-slice_fusion.refs_0_) | copy-start | bytes 1769476
  34.7 21.9 %collective-permute-start.4 = (bf16[2,2,64,1152]{3,2,1,0:T(8,128)(2,1)S(1)}, bf16[2,2,64,1152]{3,2,1,0:T(8,128)(2,1)S(1)}, u32[]{:S(2)}, u32[]{:S(2)}) collective-permute-start(bf16[2,2,64,1152]{3,2,1,0:T(8,128)(2,1)S(1)} %constant_dynamic-update-slice_fusion.refs_0_), channel_id=1, source_target_pairs={{0,16},{1,17},{2,18},{3,19},{4,20},{5,21},{6,22},{7,23},{8,24},{9,... | collective-permute-start | bytes 1769480 | tf_op jit(solution)/shard_map/ppermute | solution.py:455
  35.6 27.0 %collective-permute-start.10 = (bf16[2,288,432]{2,1,0:T(8,128)(2,1)S(1)}, bf16[2,288,432]{2,1,0:T(8,128)(2,1)S(1)}, u32[]{:S(2)}, u32[]{:S(2)}) collective-permute-start(bf16[2,288,432]{2,1,0:T(8,128)(2,1)S(1)} %pad_maximum_fusion.refs_0_), channel_id=1, source_target_pairs={{0,8},{1,9},{2,10},{3,11},{4,12},{5,13},{6,14},{7,15},{8,0},{9,1},... | collective-permute-start | bytes 1493000 | tf_op jit(solution)/shard_map/ppermute | solution.py:499
  47.3 15.3 %copy-start.10 = (bf16[2,288,432]{2,1,0:T(8,128)(2,1)}, bf16[2,288,432]{2,1,0:T(8,128)(2,1)S(1)}, u32[]{:S(2)}) copy-start(bf16[2,288,432]{2,1,0:T(8,128)(2,1)S(1)} %collective-permute-done.9.refs_1_) | copy-start | bytes 1492996
  47.3 15.3 %collective-permute-start.11 = (bf16[2,288,432]{2,1,0:T(8,128)(2,1)S(1)}, bf16[2,288,432]{2,1,0:T(8,128)(2,1)S(1)}, u32[]{:S(2)}, u32[]{:S(2)}) collective-permute-start(bf16[2,288,432]{2,1,0:T(8,128)(2,1)S(1)} %collective-permute-done.9.refs_1_), channel_id=1, source_target_pairs={{0,8},{1,9},{2,10},{3,11},{4,12},{5,13},{6,14},{7,15},{8,0},{9,1},... | collective-permute-start | bytes 1493000 | tf_op jit(solution)/shard_map/ppermute | solution.py:499
  47.4 6.3 %collective-permute-start = (s32[1,16]{1,0:T(1,128)S(1)}, s32[1,16]{1,0:T(1,128)S(1)}, u32[]{:S(2)}, u32[]{:S(2)}) collective-permute-start(s32[1,16]{1,0:T(1,128)S(1)} %add_bitcast_fusion), channel_id=1, source_target_pairs={{0,0},{1,1},{2,16},{3,17},{4,8},{5,9},{6,24},{7,25},{8,4},{9,5},{1... | collective-permute-start | bytes 200 | tf_op jit(solution)/shard_map/ppermute | solution.py:468
  53.7 2.9 %copy-start.24 = (s32[1,16]{1,0:T(1,128)}, s32[1,16]{1,0:T(1,128)S(1)}, u32[]{:S(2)}) copy-start(s32[1,16]{1,0:T(1,128)S(1)} %collective-permute-done) | copy-start | bytes 196
  53.7 24.2 %collective-permute-start.12 = (bf16[144,1152]{1,0:T(8,128)(2,1)S(1)}, bf16[144,1152]{1,0:T(8,128)(2,1)S(1)}, u32[]{:S(2)}, u32[]{:S(2)}) collective-permute-start(bf16[144,1152]{1,0:T(8,128)(2,1)S(1)} %copy-done.15), channel_id=1, source_target_pairs={{0,0},{1,1},{2,16},{3,17},{4,8},{5,9},{6,24},{7,25},{8,4},{9,5},{1... | collective-permute-start | bytes 995336 | tf_op jit(solution)/shard_map/ppermute | solution.py:502
  56.5 0.8 copy-start.13
  56.6 1.0 copy-start.14
  62.6 0.8 copy-start.11
  62.6 1.0 copy-start.12
  75.5 14.4 %collective-permute-start.14 = (f32[4,144,288]{2,1,0:T(8,128)}, f32[4,144,288]{2,1,0:T(8,128)S(1)}, u32[]{:S(2)}, u32[]{:S(2)}) collective-permute-start(f32[4,144,288]{2,1,0:T(8,128)} %get-tuple-element.42), channel_id=1, source_target_pairs={{0,8},{1,9},{2,10},{3,11},{4,12},{5,13},{6,14},{7,15},{8,0},{9,1},... | collective-permute-start | bytes 1990664 | tf_op jit(solution)/shard_map/ppermute | solution.py:552
  77.9 2.5 %copy-start.16 = (bf16[144,1152]{1,0:T(8,128)(2,1)}, bf16[144,1152]{1,0:T(8,128)(2,1)S(1)}, u32[]{:S(2)}) copy-start(bf16[144,1152]{1,0:T(8,128)(2,1)S(1)} %collective-permute-done.12.refs_0_) | copy-start | bytes 995332
  77.9 2.5 %collective-permute-start.13 = (bf16[144,1152]{1,0:T(8,128)(2,1)S(1)}, bf16[144,1152]{1,0:T(8,128)(2,1)S(1)}, u32[]{:S(2)}, u32[]{:S(2)}) collective-permute-start(bf16[144,1152]{1,0:T(8,128)(2,1)S(1)} %collective-permute-done.12.refs_0_), channel_id=1, source_target_pairs={{0,8},{1,9},{2,10},{3,11},{4,12},{5,13},{6,14},{7,15},{8,0},{9,1},... | collective-permute-start | bytes 995336 | tf_op jit(solution)/shard_map/ppermute | solution.py:503
  80.4 0.7 copy-start.17
  86.1 3.9 %copy-start.1 = (f32[4,144,288]{2,1,0:T(8,128)S(1)}, f32[4,144,288]{2,1,0:T(8,128)}, u32[]{:S(2)}) copy-start(f32[4,144,288]{2,1,0:T(8,128)} %get-tuple-element.41) | copy-start | bytes 1990660
  86.1 25.1 %all-to-all-start = ((bf16[4,2,64,1152]{3,2,1,0:T(8,128)(2,1)}), bf16[4,2,64,1152]{3,2,1,0:T(8,128)(2,1)S(1)}, u32[]{:S(2)}, u32[]{:S(2)}) async-start(bf16[4,2,64,1152]{3,2,1,0:T(8,128)(2,1)} %get-tuple-element.36), calls=%async_computation | async-start | bytes 2359296 | tf_op jit(solution)/shard_map/all_to_all | solution.py:569
  100.6 10.5 %collective-permute-start.15 = (bf16[2,64,1152]{2,1,0:T(8,128)(2,1)}, bf16[2,64,1152]{2,1,0:T(8,128)(2,1)S(1)}, u32[]{:S(2)}, u32[]{:S(2)}) collective-permute-start(bf16[2,64,1152]{2,1,0:T(8,128)(2,1)} %get-tuple-element.46), channel_id=1, source_target_pairs={{0,1},{1,0},{2,3},{3,2},{4,5},{5,4},{6,7},{7,6},{8,9},{9,8},{10,11... | collective-permute-start | bytes 884744 | tf_op jit(solution)/shard_map/ppermute | solution.py:596
  101.9 9.2 %collective-permute-start.16 = (bf16[2,64,1152]{2,1,0:T(8,128)(2,1)}, bf16[2,64,1152]{2,1,0:T(8,128)(2,1)S(1)}, u32[]{:S(2)}, u32[]{:S(2)}) collective-permute-start(bf16[2,64,1152]{2,1,0:T(8,128)(2,1)} %get-tuple-element.47), channel_id=1, source_target_pairs={{0,16},{1,17},{2,18},{3,19},{4,20},{5,21},{6,22},{7,23},{8,24},{9,... | collective-permute-start | bytes 884744 | tf_op jit(solution)/shard_map/ppermute | solution.py:596
  111.1 0.7 copy-start.18
  111.1 0.8 copy-start.19
  111.1 1.3 copy-start
  116.3 6.9 %copy-start.21 = (bf16[64,1152]{1,0:T(8,128)(2,1)S(1)}, bf16[64,1152]{1,0:T(8,128)(2,1)}, u32[]{:S(2)}) copy-start(bf16[64,1152]{1,0:T(8,128)(2,1)} %get-tuple-element.48) | copy-start | bytes 442372
  116.3 10.9 %copy-start.20 = (bf16[64,1152]{1,0:T(8,128)(2,1)S(1)}, bf16[64,1152]{1,0:T(8,128)(2,1)}, u32[]{:S(2)}) copy-start(bf16[64,1152]{1,0:T(8,128)(2,1)} %get-tuple-element.49) | copy-start | bytes 442372
  116.3 12.8 %collective-permute-start.19 = (bf16[64,1152]{1,0:T(8,128)(2,1)}, bf16[64,1152]{1,0:T(8,128)(2,1)S(1)}, u32[]{:S(2)}, u32[]{:S(2)}) collective-permute-start(bf16[64,1152]{1,0:T(8,128)(2,1)} %get-tuple-element.50), channel_id=1, source_target_pairs={{0,16},{1,17},{2,18},{3,19},{4,20},{5,21},{6,22},{7,23},{8,24},{9,... | collective-permute-start | bytes 442376 | tf_op jit(solution)/shard_map/ppermute | solution.py:619
  117.4 11.7 %collective-permute-start.20 = (bf16[64,1152]{1,0:T(8,128)(2,1)}, bf16[64,1152]{1,0:T(8,128)(2,1)S(1)}, u32[]{:S(2)}, u32[]{:S(2)}) collective-permute-start(bf16[64,1152]{1,0:T(8,128)(2,1)} %get-tuple-element.51), channel_id=1, source_target_pairs={{0,1},{1,0},{2,3},{3,2},{4,5},{5,4},{6,7},{7,6},{8,9},{9,8},{10,11... | collective-permute-start | bytes 442376 | tf_op jit(solution)/shard_map/ppermute | solution.py:619
  118.8 40.2 %all-to-all-start.1 = ((f32[4,144,288]{2,1,0:T(8,128)}), f32[4,144,288]{2,1,0:T(8,128)S(1)}, u32[]{:S(2)}, u32[]{:S(2)}) async-start(f32[4,144,288]{2,1,0:T(8,128)} %add.14), calls=%async_computation.1 | async-start | bytes 1769472 | tf_op jit(solution)/shard_map/all_to_all | solution.py:573
  123.1 18.8 %collective-permute-start.17 = (bf16[64,1152]{1,0:T(8,128)(2,1)S(1)}, bf16[64,1152]{1,0:T(8,128)(2,1)S(1)}, u32[]{:S(2)}, u32[]{:S(2)}) collective-permute-start(bf16[64,1152]{1,0:T(8,128)(2,1)S(1)} %copy-done.21), channel_id=1, source_target_pairs={{0,0},{1,1},{16,2},{17,3},{8,4},{9,5},{24,6},{25,7},{4,8},{5,9},{2... | collective-permute-start | bytes 442376 | tf_op jit(solution)/shard_map/ppermute | solution.py:462
  127.2 17.9 %collective-permute-start.18 = (bf16[64,1152]{1,0:T(8,128)(2,1)S(1)}, bf16[64,1152]{1,0:T(8,128)(2,1)S(1)}, u32[]{:S(2)}, u32[]{:S(2)}) collective-permute-start(bf16[64,1152]{1,0:T(8,128)(2,1)S(1)} %copy-done.20), channel_id=1, source_target_pairs={{8,0},{9,1},{24,2},{25,3},{0,4},{1,5},{16,6},{17,7},{12,8},{13,9},... | collective-permute-start | bytes 442376 | tf_op jit(solution)/shard_map/ppermute | solution.py:462
  129.1 0.7 copy-start.22
  129.7 0.6 copy-start.23
  133.7 25.3 %collective-permute-start.21 = (bf16[64,1152]{1,0:T(8,128)(2,1)}, bf16[64,1152]{1,0:T(8,128)(2,1)S(1)}, u32[]{:S(2)}, u32[]{:S(2)}) collective-permute-start(bf16[64,1152]{1,0:T(8,128)(2,1)} %get-tuple-element.52), channel_id=1, source_target_pairs={{0,0},{1,1},{16,2},{17,3},{8,4},{9,5},{24,6},{25,7},{4,8},{5,9},{2... | collective-permute-start | bytes 442376 | tf_op jit(solution)/shard_map/ppermute | solution.py:462
  136.1 23.0 %collective-permute-start.22 = (bf16[64,1152]{1,0:T(8,128)(2,1)}, bf16[64,1152]{1,0:T(8,128)(2,1)S(1)}, u32[]{:S(2)}, u32[]{:S(2)}) collective-permute-start(bf16[64,1152]{1,0:T(8,128)(2,1)} %get-tuple-element.53), channel_id=1, source_target_pairs={{8,0},{9,1},{24,2},{25,3},{0,4},{1,5},{16,6},{17,7},{12,8},{13,9},... | collective-permute-start | bytes 442376 | tf_op jit(solution)/shard_map/ppermute | solution.py:462
  159.2 9.6 %collective-permute-start.23 = (f32[144,288]{1,0:T(8,128)S(1)}, f32[144,288]{1,0:T(8,128)S(1)}, u32[]{:S(2)}, u32[]{:S(2)}) collective-permute-start(f32[144,288]{1,0:T(8,128)S(1)} %reduce_sum.9), channel_id=1, source_target_pairs={{0,0},{1,1},{2,8},{3,9},{4,16},{5,17},{6,24},{7,25},{8,4},{9,5},{1... | collective-permute-start | bytes 497672 | tf_op jit(solution)/shard_map/ppermute | solution.py:574

commit v5 on v4

--- a/solution.py
+++ b/solution.py
@@ -61,7 +61,16 @@
         return pairs
 
     def to_plane(self, k):
-        return self.perm(lambda y, c, z, x: (z % self.ny, (z // self.ny) ^ k, c * self.ny + y, x))
+        return self.perm(
+            lambda y, c, z, x: ((z % self.ny) ^ c, (z // self.ny) ^ k, c * self.ny + y, x)
+        )
+
+    def to_plane_from_neighbour(self, k):
+        def move(y, c, z, x):
+            y = y ^ 1
+            return (z % self.ny) ^ c, (z // self.ny) ^ k, c * self.ny + y, x
+
+        return self.perm(move)
 
     def from_plane(self, k):
         return [(target, source) for source, target in self.to_plane(k)]
@@ -84,7 +93,7 @@
 
         def move(y, c, z, x):
             chip_y, chip_x, i = reader[z * self.nx + x]
-            return chip_y, i, c * self.ny + y, chip_x
+            return chip_y, i, c * self.ny + (y ^ (z & 1)), chip_x
 
         return self.perm(move)
 
@@ -121,7 +130,7 @@
 def slot_scalars(lay, pos_ref, info_ref, slot):
     k, j = slot
     ky, kx = lay.chip_of(k)
-    z_frame = (pos_ref[1] ^ j) * lay.ny + (pos_ref[0] ^ ky)
+    z_frame = (pos_ref[1] ^ j) * lay.ny + (pos_ref[0] ^ ky ^ (pos_ref[2] // lay.ny))
     frame = z_frame * lay.nx + (pos_ref[3] ^ kx)
     clip = info_ref[frame]
     clips = (info_ref.shape[0] - lay.frames) // 2
@@ -178,20 +187,22 @@
             @pl.when(want == v)
             def _(v=v, out_ref=out_ref):
                 parts = [
-                    w_ref[:, p * model + v * cols : p * model + (v + 1) * cols].astype(F32)
+                    w_ref[:, p * model + v * cols : p * model + (v + 1) * cols]
                     for p in range(3)
                 ]
-                out_ref[...] = jnp.concatenate(parts, axis=1).astype(BF16)
+                out_ref[...] = jnp.concatenate(parts, axis=1)
 
 
 def fill_weights(lay, pos_ref, w_refs, w_scr):
-    rows = w_scr.shape[1] // lay.nz
     order = lay.doubled(lay.bits(lay.nz)[::-1])
+    block = w_scr.shape[1] // lay.nz
+    rows, width = w_refs[0].shape[1], w_scr.shape[2]
     for h in range(lay.halves):
         for n, k in enumerate(order):
             ref, place = w_refs[2 * h + (2 * n) // lay.nz], n % (lay.nz // 2)
-            start = pl.multiple_of((pos_ref[2] ^ k) * rows, 16)
-            w_scr[h, pl.ds(start, rows), :] = ref[place]
+            for m in range(block // rows):
+                start = pl.multiple_of((pos_ref[2] ^ k) * block + m * rows, 16)
+                w_scr[h, pl.ds(start, rows), :] = ref[place, :, m * width : (m + 1) * width]
 
 
 def heads_stacked(lay, values):
@@ -263,10 +274,13 @@
         att_ref[:, b * BLOCK : (b + 1) * BLOCK, :] = attended.reshape(lay.frames, BLOCK, -1)
 
 
-def weight_grad_kernel(lay, pos_ref, gp_ref, att_ref, kept_ref, sent_ref, acc_scr):
+def weight_grad_kernel(lay, pos_ref, gp_ref, att_ref, kept_ref, sent_ref, acc_scr, cut_scr):
     _, step_patches, model = gp_ref.shape
     tokens = lay.frames * step_patches
-    groups, block_rows, part = kept_ref.shape
+    groups, chunk_rows, chunk_width = kept_ref.shape
+    block_rows, part = acc_scr.shape[0] // lay.nc, model // groups
+    fold = chunk_width // part
+    order = lay.doubled(lay.bits(lay.nz)[::-1])
     is_first = pos_ref[1] == 0
 
     @pl.when(pl.program_id(0) == 0)
@@ -281,15 +295,21 @@
         first, second = acc_scr[:block_rows, :], acc_scr[block_rows:, :]
         kept = jnp.where(is_first, first, second)
         sent = jnp.where(is_first, second, first)
-        for d in range(groups):
-            kept_ref[d] = kept[:, d * part : (d + 1) * part]
-            sent_ref[d] = sent[:, d * part : (d + 1) * part]
+        for ref, rows in ((kept_ref, kept), (sent_ref, sent)):
+            for d in range(groups):
+                chunk = [
+                    rows[m * chunk_rows : (m + 1) * chunk_rows, d * part : (d + 1) * part]
+                    for m in range(fold)
+                ]
+                cut_scr[d] = jnp.concatenate(chunk, axis=1) if fold > 1 else chunk[0]
+            for n, k in enumerate(order):
+                ref[n] = cut_scr[pos_ref[2] ^ k]
 
 
 def projection_kernel(lay, pos_ref, gp_ref, att_ref, *refs):
     wo_refs, refs = refs[: lay.nc], refs[lay.nc :]
-    ga_ref, own_ref, sent_ref, wo_scr = refs
-    own_chip = pos_ref[0] * lay.nx + pos_ref[3]
+    ga_ref, *refs = refs
+    pr_refs, (wo_scr,) = refs[: lay.chips], refs[lay.chips :]
     _, step_patches, model = gp_ref.shape
     tokens = lay.frames * step_patches
     is_first = pos_ref[1] == 0
@@ -306,9 +326,8 @@
         ga_ref[h] = grad_attn[:, h * part : (h + 1) * part].astype(BF16).reshape(ga_ref.shape[1:])
     attended = att_ref[...].reshape(tokens, -1)
     projected = dot(attended, wo_scr[...]).reshape(lay.chips, lay.nc, step_patches, model)
-    own_ref[...] = projected[0]
     for k in range(lay.chips):
-        sent_ref[own_chip ^ k] = projected[k].astype(BF16)
+        pr_refs[k][...] = projected[k].astype(pr_refs[k].dtype)
 
 
 def backward_kernel(lay, pos_ref, info_ref, *refs):
@@ -360,12 +379,11 @@
 
 def output_kernel(lay, pos_ref, info_ref, *refs):
     pair_refs, refs = refs[: lay.nc], refs[lay.nc :]
-    own_ref, got_ref, refs = refs[0], refs[1], refs[2:]
+    pr_refs, refs = refs[: lay.chips], refs[lay.chips :]
     kept_refs, refs = refs[: lay.nc], refs[lay.nc :]
     add_refs, refs = refs[: lay.nc], refs[lay.nc :]
     mod_ref, *refs = refs
     out_refs, sum_refs = refs[: lay.nc], refs[lay.nc :]
-    own_chip = pos_ref[0] * lay.nx + pos_ref[3]
     step_patches, model = out_refs[0].shape
     patches = step_patches * pl.num_programs(0)
     patch_base = pos_ref[1] * patches + pl.program_id(0) * step_patches
@@ -373,9 +391,9 @@
     for j in range(lay.nc):
         _, limit, step = slot_scalars(lay, pos_ref, info_ref, (0, j))
         factor = jnp.where(patch < limit, table_row(mod_ref, step, 2, model), 0.0)
-        projected = own_ref[j]
+        projected = pr_refs[0][j]
         for k in range(1, lay.chips):
-            projected = projected + got_ref[own_chip ^ k, j].astype(F32)
+            projected = projected + pr_refs[k][j].astype(F32)
         projected = projected.astype(BF16).astype(F32)
         out_refs[j][...] = (pair_refs[j][0, 0].astype(F32) + factor * projected).astype(BF16)
         sum_refs[j][...] = (kept_refs[j][1] + add_refs[j][1].astype(F32)).astype(BF16)
@@ -454,10 +472,6 @@
             held = jnp.concatenate([held, lax.ppermute(held, AXES, swap(bit))], axis=0)
         return [held, lax.ppermute(held, AXES, swap(bits[-1]))]
 
-    def over_chips(parts):
-        own = [parts[0]]
-        return own + [lax.ppermute(parts[k], AXES, chip_swap(k)) for k in range(1, chips)]
-
     def from_plane(parts):
         got = [lax.ppermute(part, AXES, lay.from_plane(k)) for k, part in enumerate(parts)]
         first = jnp.where(z // lay.ny == 0, got[0], got[1])
@@ -471,7 +485,13 @@
     for k in range(nc):
         start = ((z // lay.ny) ^ k) * half
         pair = [lax.dynamic_slice_in_dim(frame, start, half, axis=1) for frame in (frames_x, grad_y)]
-        own.append(lax.ppermute(jnp.stack(pair, axis=1), AXES, lay.to_plane(k)))
+        pair = jnp.stack(pair, axis=1)
+        if k == 0:
+            own.append(lax.ppermute(pair, AXES, lay.to_plane(k)))
+        else:
+            pair = lax.ppermute(pair, AXES, lay.swap(ky=1))
+            own.append(lax.ppermute(pair, AXES, lay.to_plane_from_neighbour(k)))
+    own[0], info = lax.optimization_barrier((own[0], info))
     pairs = []
     for j in range(nc):
         pairs += doubling(own[j], lay.chip_bits(j), chip_swap)
@@ -493,7 +513,7 @@
     else:
         stacked = jnp.stack(by_x)
         ordered = [lax.dynamic_index_in_dim(stacked, x ^ i, 0, keepdims=False) for i in range(nx)]
-    w_own = jnp.concatenate(ordered, axis=0)[None]
+    w_own = jnp.concatenate(ordered, axis=1 if rows % 16 == 0 else 0)[None]
     w_pieces = doubling(w_own, lay.bits(lay.nz)[::-1], lambda kz: lay.swap(kz=kz))
     if halves > 1:
         w_pieces += [lax.ppermute(piece, AXES, lay.swap(kc=1)) for piece in w_pieces]
@@ -537,7 +557,8 @@
         (steps,),
     )(pos, info, hidden, *w_pieces)
 
-    piece_shape = (groups, rows, quarter)
+    fold = 3 if rows % 24 == 0 else 1
+    piece_shape = (groups, rows // fold, quarter * fold)
     kept, sent = call(
         functools.partial(weight_grad_kernel, lay),
         "weight_grad",
@@ -545,35 +566,31 @@
         [gp_spec, att_spec],
         [whole_spec(piece_shape)] * 2,
         [struct(piece_shape, F32)] * 2,
-        [pltpu.VMEM((chip_width, model), F32)],
+        [pltpu.VMEM((chip_width, model), F32), pltpu.VMEM(piece_shape, F32)],
         (steps,),
         prefetch=1,
     )(pos, grad_proj, attended)
     got = lax.ppermute(sent, AXES, lay.swap(kc=1))
 
-    grad_attn, projected, sent = call(
+    grad_attn, *projected = call(
         functools.partial(projection_kernel, lay),
         "projection",
         4 * model * 1000,
         [gp_spec, att_spec] + [whole_spec(w_out.shape)] * nc,
-        [
-            triple_spec,
-            part_spec,
-            pl.BlockSpec((chips, nc, step_patches, model), lambda i, *_: (0, 0, i, 0)),
-        ],
-        [triple_shape, struct((nc, half, model), F32), struct((chips, nc, half, model))],
+        [triple_spec] + [part_spec] * chips,
+        [triple_shape, struct((nc, half, model), F32)] + [struct((nc, half, model))] * (chips - 1),
         [pltpu.VMEM((chip_width, model), BF16)],
         (steps,),
         prefetch=1,
     )(pos, grad_proj, attended, *wo_rows)
-    others = lax.all_to_all(sent, ("y", "x"), split_axis=0, concat_axis=0, tiled=True)
-
-    cut = kept + got
-    grad_attn, cut = lax.optimization_barrier((grad_attn, cut))
-    cut = lax.all_to_all(cut, "z", split_axis=0, concat_axis=0, tiled=True)
-    grad_w_out = lax.ppermute(jnp.sum(cut, axis=0), AXES, lay.to_owner()) * jnp.float32(
-        1.0 / math.sqrt(groups * lay.frames * patches)
-    )
+    projected = [projected[0]] + [
+        lax.ppermute(projected[k], AXES, chip_swap(k)) for k in range(1, chips)
+    ]
+
+    middle = groups // 2
+    cut, away = kept[:middle] + got[:middle], kept[middle:] + got[middle:]
+    grad_attn, cut, away = lax.optimization_barrier((grad_attn, cut, away))
+    first_away = lax.ppermute(away, AXES, lay.swap(kz=1))
 
     def side_spec(count):
         return pl.BlockSpec((count, step_patches, model), lambda i, *_: (0, i, 0))
@@ -589,6 +606,18 @@
         [w_scratch, pltpu.VMEM((halves, lay.frames, step_patches, 3 * cols), BF16)],
         (steps,),
     )(pos, info, *w_pieces, queries, keys, values, grad_attn)
+    sums, first_away, projected = lax.optimization_barrier((sums, first_away, projected))
+    cut = cut + first_away
+    for bit in lay.bits(lay.nz)[1:]:
+        middle = middle // 2
+        cut = cut[:middle] + lax.ppermute(cut[middle:], AXES, lay.swap(kz=bit))
+    projected, cut = lax.optimization_barrier((projected, cut))
+    grad_w = lax.ppermute(cut[0], AXES, lay.to_owner())
+    grad_w = jnp.concatenate(
+        [grad_w[:, m * quarter : (m + 1) * quarter] for m in range(fold)], axis=0
+    )
+    grad_w_out = grad_w * jnp.float32(1.0 / math.sqrt(groups * lay.frames * patches))
+
     held, added = list(sums[:nc]), []
     for j in range(nc):
         bits = lay.chip_bits(j)
@@ -608,13 +637,13 @@
         "output",
         3 * model * 1000,
         [pair_spec(1)] * nc
-        + [part_spec, pl.BlockSpec((chips, nc, step_patches, model), lambda i, *_: (0, 0, i, 0))]
+        + [part_spec] * chips
         + [side_spec(2)] * (2 * nc)
         + [mod_spec],
         [x_spec] * (2 * nc),
         [struct((half, model))] * (2 * nc),
         grid=(steps,),
-    )(pos, info, *own, projected, others, *held, *added, mod_table)
+    )(pos, info, *own, *projected, *held, *added, mod_table)
     last = [
         lax.ppermute(part, AXES, chip_swap(lay.chip_bits(j)[-1]))
         for j, part in enumerate((last0, last1))

time: 170 us -> 154 us (0.906); the launches traced: 169 us -> 152 us
  waiting for transfers between devices: 68.6 us -> 29.9 us
  starting transfers between devices: 46.5 us -> 68.2 us
    ppermute x3 -> x9, starting transfers between devices: 6.23 us -> 22.9 us  [the longest x1 7.49 us: local(): own.append(lax.ppermute(pair, AXES, lay.to_plane_from_neighbour(k)))]
    ppermute x4, waiting for transfers between devices: 18.1 us -> 5.24 us  [from_plane(): lax.ppermute(part, AXES, lay.from_plane(k))]
    ppermute x3, waiting for transfers between devices: 11.7 us -> 0.72 us  [doubling(): return [held, lax.ppermute(held, AXES, swap(bits[-1]))]]
    ppermute x2, waiting for transfers between devices: 8.62 us -> 0.01 us  [local(): added.append(lax.ppermute(sums[nc + j], AXES, chip_swap(bits[0])))]
    all_to_all x2 -> x0, starting transfers between devices: 8.12 us -> none  [the longest x1 4.29 us: local(): cut = lax.all_to_all(cut, 'z', split_axis=0, concat_axis=0, tiled=True)]
    ppermute x1, starting transfers between devices: 2.78 us -> 8.67 us  [local(): wo_own = lax.ppermute(late_w_out, AXES, lay.rows_to_chip())]
    ppermute x3, starting transfers between devices: 1.55 us -> 6.9 us  [doubling(): return [held, lax.ppermute(held, AXES, swap(bits[-1]))]]
    ppermute x3 -> x9, waiting for transfers between devices: 16.6 us -> 12.4 us  [the longest x1 6.01 us: local(): cut = cut[:middle] + lax.ppermute(cut[middle:], AXES, lay.swap(kz=bit))]
  transfers between devices with their start and end apart: 26 -> 30, of which waited for: 11 -> 9; matrix products, arithmetic and copies ran while one was open for 3% -> 2% of each run, Pallas kernels for 22% -> 27%
where the time goes in v5:
time: 154 us; the launch traced here: 152 us
  starting transfers between devices  68.2 us (44%)
  Pallas kernels  41.4 us (27%)
  waiting for transfers between devices  29.9 us (19%)
  local copies, waits for them, and re-layouts  6.84 us (4%)
  other arithmetic  4.29 us (3%)
    ppermute x4, starting transfers between devices, from_plane(): lax.ppermute(part, AXES, lay.from_plane(k))  11.7 us
    pallas_call x1, Pallas kernels, local(): call(functools.partial(backward_kernel, lay), 'backward', 10 * model * 10...  9.71 us
    ppermute x1, starting transfers between devices, local(): wo_own = lax.ppermute(late_w_out, AXES, lay.rows_to_chip())  8.67 us
    pallas_call x1, Pallas kernels, local(): call(functools.partial(forward_kernel, lay), 'forward', 8 * model * 1000,...  7.99 us
    ppermute x1, starting transfers between devices, local(): own.append(lax.ppermute(pair, AXES, lay.to_plane_from_neighbour(k)))  7.49 us
    ppermute x3, starting transfers between devices, doubling(): return [held, lax.ppermute(held, AXES, swap(bits[-1]))]  6.9 us
    ppermute x1, waiting for transfers between devices, local(): cut = cut[:middle] + lax.ppermute(cut[middle:], AXES, lay.swap(kz=bit))  6.01 us
    ppermute x1, waiting for transfers between devices, local(): own.append(lax.ppermute(pair, AXES, lay.to_plane_from_neighbour(k)))  5.81 us
  transfers between devices with their start and end apart: 30, of which 9 were waited for; matrix products, arithmetic and copies ran while one was open for 2% of the time, Pallas kernels for 27%

profile of v5, /device:TPU:4, one launch (start us, length us, event | category | flops | bytes accessed | tf_op | source)
XLA Modules:
  0.0 151.6 jit_solution(9174189561282890864)
XLA Ops:
  0.7 1.2 dynamic-slice_bitcast_fusion
  1.9 0.1 collective-permute-start.2
  2.0 0.7 pad_add_fusion.pos_ref
  2.6 2.9 %pick.1 = (bf16[144,432]{1,0:T(8,128)(2,1)}, bf16[144,432]{1,0:T(8,128)(2,1)}) custom-call(s32[4]{0:T(128)} %pad_add_fusion.pos_ref, bf16[144,3456]{1,0:T(8,128)(2,1)} %w_ref.1), custom_call_target="tpu_custom_call" | custom-call | flops 1179648000 | bytes 2359296 | tf_op jit(solution)/shard_map/pick/pallas_call | solution.py:499
  5.5 2.0 %collective-permute-start.4 = (bf16[144,432]{1,0:T(8,128)(2,1)}, bf16[144,432]{1,0:T(8,128)(2,1)S(1)}, u32[]{:S(2)}, u32[]{:S(2)}) collective-permute-start(bf16[144,432]{1,0:T(8,128)(2,1)} %get-tuple-element.51), channel_id=1, source_target_pairs={{0,1},{1,0},{2,3},{3,2},{4,5},{5,4},{6,7},{7,6},{8,9},{9,8},{10,11... | collective-permute-start | bytes 373256 | tf_op jit(solution)/shard_map/ppermute | solution.py:509
  7.6 4.4 %collective-permute-start = (bf16[1,2,64,1152]{3,2,1,0:T(8,128)(2,1)S(1)}, bf16[1,2,64,1152]{3,2,1,0:T(8,128)(2,1)S(1)}, u32[]{:S(2)}, u32[]{:S(2)}) collective-permute-start(bf16[1,2,64,1152]{3,2,1,0:T(8,128)(2,1)S(1)} %pad_maximum_fusion.1), channel_id=1, source_target_pairs={{0,0},{1,1},{2,16},{3,17},{4,8},{5,9},{6,24},{7,25},{8,20},{9,21},... | collective-permute-start | bytes 884744 | tf_op jit(solution)/shard_map/ppermute | solution.py:490
  12.0 0.9 broadcast_select_fusion.1
  12.9 0.1 maximum_bitcast_fusion.2
  13.1 2.2 %collective-permute-start.5 = (bf16[1,144,864]{2,1,0:T(8,128)(2,1)S(1)}, bf16[1,144,864]{2,1,0:T(8,128)(2,1)S(1)}, u32[]{:S(2)}, u32[]{:S(2)}) collective-permute-start(bf16[1,144,864]{2,1,0:T(8,128)(2,1)S(1)} %maximum_bitcast_fusion.2), channel_id=1, source_target_pairs={{0,4},{1,5},{2,6},{3,7},{4,0},{5,1},{6,2},{7,3},{8,12},{9,13},{10,... | collective-permute-start | bytes 746504 | tf_op jit(solution)/shard_map/ppermute | solution.py:472
  15.3 0.1 add_bitcast_fusion
  15.3 4.4 %collective-permute-start.1 = (s32[1,16]{1,0:T(1,128)S(1)}, s32[1,16]{1,0:T(1,128)S(1)}, u32[]{:S(2)}, u32[]{:S(2)}) collective-permute-start(s32[1,16]{1,0:T(1,128)S(1)} %add_bitcast_fusion), channel_id=1, source_target_pairs={{0,0},{1,1},{2,16},{3,17},{4,8},{5,9},{6,24},{7,25},{8,20},{9,21},... | collective-permute-start | bytes 200 | tf_op jit(solution)/shard_map/ppermute | solution.py:482
  19.8 4.7 %collective-permute-done.1 = s32[1,16]{1,0:T(1,128)S(1)} collective-permute-done((s32[1,16]{1,0:T(1,128)S(1)}, s32[1,16]{1,0:T(1,128)S(1)}, u32[]{:S(2)}, u32[]{:S(2)}) %collective-permute-start.1) | collective-permute-done | bytes 96 | tf_op jit(solution)/shard_map/ppermute | solution.py:482
  24.5 0.5 collective-permute-start.9
  25.1 7.5 %collective-permute-start.3 = (bf16[1,2,64,1152]{3,2,1,0:T(8,128)(2,1)S(1)}, bf16[1,2,64,1152]{3,2,1,0:T(8,128)(2,1)S(1)}, u32[]{:S(2)}, u32[]{:S(2)}) collective-permute-start(bf16[1,2,64,1152]{3,2,1,0:T(8,128)(2,1)S(1)} %collective-permute-done.2), channel_id=1, source_target_pairs={{0,10},{1,11},{2,26},{3,27},{4,2},{5,3},{6,18},{7,19},{8,30},{9,31... | collective-permute-start | bytes 884744 | tf_op jit(solution)/shard_map/ppermute | solution.py:493
  32.6 0.1 pad_maximum_fusion.refs_0_
  32.7 1.3 collective-permute-start.6
  34.0 5.8 %collective-permute-done.3.refs_1_ = bf16[1,2,64,1152]{3,2,1,0:T(8,128)(2,1)S(1)} collective-permute-done((bf16[1,2,64,1152]{3,2,1,0:T(8,128)(2,1)S(1)}, bf16[1,2,64,1152]{3,2,1,0:T(8,128)(2,1)S(1)}, u32[]{:S(2)}, u32[]{:S(2)}) %collective-permute-start.3) | collective-permute-done | bytes 294944 | tf_op jit(solution)/shard_map/ppermute | solution.py:493
  39.8 0.5 collective-permute-start.11
  40.4 1.6 %collective-permute-start.10 = (bf16[2,2,64,1152]{3,2,1,0:T(8,128)(2,1)S(1)}, bf16[2,2,64,1152]{3,2,1,0:T(8,128)(2,1)S(1)}, u32[]{:S(2)}, u32[]{:S(2)}) collective-permute-start(bf16[2,2,64,1152]{3,2,1,0:T(8,128)(2,1)S(1)} %constant_dynamic-update-slice_fusion.refs_0_), channel_id=1, source_target_pairs={{0,16},{1,17},{2,18},{3,19},{4,20},{5,21},{6,22},{7,23},{8,24},{9,... | collective-permute-start | bytes 1769480 | tf_op jit(solution)/shard_map/ppermute | solution.py:473
  42.0 4.6 %collective-permute-done.11 = bf16[1,2,64,1152]{3,2,1,0:T(8,128)(2,1)S(1)} collective-permute-done((bf16[1,2,64,1152]{3,2,1,0:T(8,128)(2,1)S(1)}, bf16[1,2,64,1152]{3,2,1,0:T(8,128)(2,1)S(1)}, u32[]{:S(2)}, u32[]{:S(2)}) %collective-permute-start.11) | collective-permute-done | bytes 294944 | tf_op jit(solution)/shard_map/ppermute | solution.py:472
  46.7 4.0 %collective-permute-start.12 = (bf16[2,2,64,1152]{3,2,1,0:T(8,128)(2,1)S(1)}, bf16[2,2,64,1152]{3,2,1,0:T(8,128)(2,1)S(1)}, u32[]{:S(2)}, u32[]{:S(2)}) collective-permute-start(bf16[2,2,64,1152]{3,2,1,0:T(8,128)(2,1)S(1)} %constant_dynamic-update-slice_fusion.2.refs_2_), channel_id=1, source_target_pairs={{0,1},{1,0},{2,3},{3,2},{4,5},{5,4},{6,7},{7,6},{8,9},{9,8},{10,11... | collective-permute-start | bytes 1769480 | tf_op jit(solution)/shard_map/ppermute | solution.py:473
  50.7 2.5 %collective-permute-start.7 = (bf16[2,144,864]{2,1,0:T(8,128)(2,1)S(1)}, bf16[2,144,864]{2,1,0:T(8,128)(2,1)S(1)}, u32[]{:S(2)}, u32[]{:S(2)}) collective-permute-start(bf16[2,144,864]{2,1,0:T(8,128)(2,1)S(1)} %pad_maximum_fusion.refs_0_), channel_id=1, source_target_pairs={{0,8},{1,9},{2,10},{3,11},{4,12},{5,13},{6,14},{7,15},{8,0},{9,1},... | collective-permute-start | bytes 1493000 | tf_op jit(solution)/shard_map/ppermute | solution.py:519
  53.1 0.1 collective-permute-start.8
  53.2 8.7 %collective-permute-start.13 = (bf16[144,1152]{1,0:T(8,128)(2,1)S(1)}, bf16[144,1152]{1,0:T(8,128)(2,1)S(1)}, u32[]{:S(2)}, u32[]{:S(2)}) collective-permute-start(bf16[144,1152]{1,0:T(8,128)(2,1)S(1)} %copy-done.14), channel_id=1, source_target_pairs={{0,0},{1,1},{2,18},{3,19},{4,8},{5,9},{6,26},{7,27},{8,4},{9,5},{1... | collective-permute-start | bytes 995336 | tf_op jit(solution)/shard_map/ppermute | solution.py:522
  61.9 0.7 collective-permute-done.12.refs_3_
  62.6 0.1 copy-done.9
  62.8 0.8 copy-done.10
  63.6 5.0 %prepare.1 = (bf16[8,64,1152]{2,1,0:T(8,128)(2,1)}, bf16[8,64,1152]{2,1,0:T(8,128)(2,1)}) custom-call(s32[4]{0:T(128)} %pad_add_fusion.pos_ref, s32[16]{0:T(128)} %bitcast.29, bf16[2,2,64,1152]{3,2,1,0:T(8,128)(2,1)} %copy-done.4, bf16[2,2,64,1152]{3,2,1,0:T(8,128)(2,1)} %copy-done.9, bf16[2,2,64,1152]{3,2,1,0:T(8,128)(2,1)} %copy-done.5, ...), custom_call_target="tpu_custom_call" | custom-call | flops 1769472000 | bytes 2359296 | tf_op jit(solution)/shard_map/prepare/pallas_call | solution.py:539
  68.6 0.7 copy-done.12
  69.4 0.2 copy-done.13
  69.6 8.0 %forward.1 = (bf16[2,8,64,144]{3,2,1,0:T(8,128)(2,1)}, bf16[2,8,64,144]{3,2,1,0:T(8,128)(2,1)}, bf16[2,8,64,144]{3,2,1,0:T(8,128)(2,1)}, bf16[8,64,288]{2,1,0:T(8,128)(2,1)}) custom-call(s32[4]{0:T(128)} %pad_add_fusion.pos_ref, s32[16]{0:T(128)} %bitcast.30, bf16[8,64,1152]{2,1,0:T(8,128)(2,1)} %get-tuple-element.52.hid_ref, ...), custom_call_target="tpu_custom_call" | custom-call | flops 4718592000 | bytes 2359296 | tf_op jit(solution)/shard_map/forward/pallas_call | solution.py:549
  77.6 3.9 %weight_grad.1 = (f32[4,48,864]{2,1,0:T(8,128)}, f32[4,48,864]{2,1,0:T(8,128)}) custom-call(s32[4]{0:T(128)} %pad_add_fusion.pos_ref, bf16[8,64,1152]{2,1,0:T(8,128)(2,1)} %get-tuple-element.56.gp_ref, bf16[8,64,288]{2,1,0:T(8,128)(2,1)} %get-tuple-element.57.att_ref), custom_call_target="tpu_custom_call" | custom-call | flops 2359296000 | bytes 2359296 | tf_op jit(solution)/shard_map/weight_grad/pallas_call | solution.py:562
  81.5 2.2 %collective-permute-start.15 = (f32[4,48,864]{2,1,0:T(8,128)}, f32[4,48,864]{2,1,0:T(8,128)S(1)}, u32[]{:S(2)}, u32[]{:S(2)}) collective-permute-start(f32[4,48,864]{2,1,0:T(8,128)} %get-tuple-element.61), channel_id=1, source_target_pairs={{0,8},{1,9},{2,10},{3,11},{4,12},{5,13},{6,14},{7,15},{8,0},{9,1},... | collective-permute-start | bytes 1990664 | tf_op jit(solution)/shard_map/ppermute | solution.py:573
  83.8 0.1 collective-permute-start.14
  83.8 2.2 %collective-permute-done.14.refs_1_ = bf16[144,1152]{1,0:T(8,128)(2,1)S(1)} collective-permute-done((bf16[144,1152]{1,0:T(8,128)(2,1)S(1)}, bf16[144,1152]{1,0:T(8,128)(2,1)S(1)}, u32[]{:S(2)}, u32[]{:S(2)}) %collective-permute-start.14) | collective-permute-done | bytes 331808 | tf_op jit(solution)/shard_map/ppermute | solution.py:523
  86.0 0.8 copy-done.16
  86.8 4.8 %projection.1 = (bf16[2,8,64,144]{3,2,1,0:T(8,128)(2,1)}, f32[2,64,1152]{2,1,0:T(8,128)}, bf16[2,64,1152]{2,1,0:T(8,128)(2,1)}, bf16[2,64,1152]{2,1,0:T(8,128)(2,1)}, bf16[2,64,1152]{2,1,0:T(8,128)(2,1)}) custom-call(s32[4]{0:T(128)} %pad_add_fusion.pos_ref, bf16[8,64,1152]{2,1,0:T(8,128)(2,1)} %get-tuple-element.56.gp_ref, ...), custom_call_target="tpu_custom_call" | custom-call | flops 2359296000 | bytes 2359296 | tf_op jit(solution)/shard_map/projection/pallas_call | solution.py:575
  91.5 2.0 %collective-permute-start.17 = (bf16[2,64,1152]{2,1,0:T(8,128)(2,1)}, bf16[2,64,1152]{2,1,0:T(8,128)(2,1)S(1)}, u32[]{:S(2)}, u32[]{:S(2)}) collective-permute-start(bf16[2,64,1152]{2,1,0:T(8,128)(2,1)} %get-tuple-element.69), channel_id=1, source_target_pairs={{0,1},{1,0},{2,3},{3,2},{4,5},{5,4},{6,7},{7,6},{8,9},{9,8},{10,11... | collective-permute-start | bytes 884744 | tf_op jit(solution)/shard_map/ppermute | solution.py:587
  93.6 1.5 collective-permute-start.19
  95.1 0.1 slice_add_fusion
  95.1 3.7 %collective-permute-start.16 = (f32[2,48,864]{2,1,0:T(8,128)S(1)}, f32[2,48,864]{2,1,0:T(8,128)S(1)}, u32[]{:S(2)}, u32[]{:S(2)}) collective-permute-start(f32[2,48,864]{2,1,0:T(8,128)S(1)} %get-tuple-element.67), channel_id=1, source_target_pairs={{0,2},{1,3},{2,0},{3,1},{4,6},{5,7},{6,4},{7,5},{8,10},{9,11},{10,... | collective-permute-start | bytes 995336 | tf_op jit(solution)/shard_map/ppermute | solution.py:593
  98.8 9.7 %backward.1 = (f32[2,64,1152]{2,1,0:T(8,128)}, f32[2,64,1152]{2,1,0:T(8,128)}, bf16[2,64,1152]{2,1,0:T(8,128)(2,1)}, bf16[2,64,1152]{2,1,0:T(8,128)(2,1)}) custom-call(s32[4]{0:T(128)} %pad_add_fusion.pos_ref, s32[16]{0:T(128)} %bitcast.31, bf16[2,144,864]{2,1,0:T(8,128)(2,1)} %copy-done.1, bf16[2,144,864]{2,1,0:T(8,128)(2,1)} %copy-done.11, ...), custom_call_target="tpu_custom_call" | custom-call | flops 5898240000 | bytes 2359296 | tf_op jit(solution)/shard_map/backward/pallas_call | solution.py:599
  108.6 0.5 collective-permute-done.18.refs_4_
  109.2 1.8 %collective-permute-start.20 = (f32[1,48,864]{2,1,0:T(8,128)S(1)}, f32[1,48,864]{2,1,0:T(8,128)S(1)}, u32[]{:S(2)}, u32[]{:S(2)}) collective-permute-start(f32[1,48,864]{2,1,0:T(8,128)S(1)} %slice.39), channel_id=1, source_target_pairs={{0,4},{1,5},{2,6},{3,7},{4,0},{5,1},{6,2},{7,3},{8,12},{9,13},{10,... | collective-permute-start | bytes 497672 | tf_op jit(solution)/shard_map/ppermute | solution.py:613
  111.0 1.2 collective-permute-start.21
  112.2 1.1 collective-permute-start.22
  113.3 6.0 %collective-permute-done.20 = f32[1,48,864]{2,1,0:T(8,128)S(1)} collective-permute-done((f32[1,48,864]{2,1,0:T(8,128)S(1)}, f32[1,48,864]{2,1,0:T(8,128)S(1)}, u32[]{:S(2)}, u32[]{:S(2)}) %collective-permute-start.20) | collective-permute-done | bytes 165920 | tf_op jit(solution)/shard_map/ppermute | solution.py:613
  119.4 1.9 %collective-permute-start.29 = (f32[48,864]{1,0:T(8,128)S(1)}, f32[48,864]{1,0:T(8,128)S(1)}, u32[]{:S(2)}, u32[]{:S(2)}) collective-permute-start(f32[48,864]{1,0:T(8,128)S(1)} %bitcast.25), channel_id=1, source_target_pairs={{0,0},{1,1},{2,8},{3,9},{4,16},{5,17},{6,24},{7,25},{8,4},{9,5},{1... | collective-permute-start | bytes 497672 | tf_op jit(solution)/shard_map/ppermute | solution.py:615
  121.4 0.7 copy-done.20
  122.0 0.7 copy-done.21
  122.7 3.8 %output.1 = (bf16[64,1152]{1,0:T(8,128)(2,1)}, bf16[64,1152]{1,0:T(8,128)(2,1)}, bf16[64,1152]{1,0:T(8,128)(2,1)}, bf16[64,1152]{1,0:T(8,128)(2,1)}) custom-call(s32[4]{0:T(128)} %pad_add_fusion.pos_ref, s32[16]{0:T(128)} %bitcast.32, bf16[1,2,64,1152]{3,2,1,0:T(8,128)(2,1)} %copy-done.2, bf16[1,2,64,1152]{3,2,1,0:T(8,128)(2,1)} %copy-done.3, ...), custom_call_target="tpu_custom_call" | custom-call | flops 1769472000 | bytes 2359296 | tf_op jit(solution)/shard_map/output/pallas_call | solution.py:635
  126.5 1.1 collective-permute-start.26
  127.6 3.5 %collective-permute-start.23 = (bf16[64,1152]{1,0:T(8,128)(2,1)}, bf16[64,1152]{1,0:T(8,128)(2,1)S(1)}, u32[]{:S(2)}, u32[]{:S(2)}) collective-permute-start(bf16[64,1152]{1,0:T(8,128)(2,1)} %get-tuple-element.86), channel_id=1, source_target_pairs={{0,0},{1,1},{16,2},{17,3},{8,4},{9,5},{24,6},{25,7},{20,8},{21,9},... | collective-permute-start | bytes 442376 | tf_op jit(solution)/shard_map/ppermute | solution.py:476
  131.0 4.2 %collective-permute-start.24 = (bf16[64,1152]{1,0:T(8,128)(2,1)}, bf16[64,1152]{1,0:T(8,128)(2,1)S(1)}, u32[]{:S(2)}, u32[]{:S(2)}) collective-permute-start(bf16[64,1152]{1,0:T(8,128)(2,1)} %get-tuple-element.87), channel_id=1, source_target_pairs={{8,0},{9,1},{24,2},{25,3},{0,4},{1,5},{16,6},{17,7},{28,8},{29,9},... | collective-permute-start | bytes 442376 | tf_op jit(solution)/shard_map/ppermute | solution.py:476
  135.2 0.1 fusion
  135.3 0.7 maximum_multiply_fusion
  136.0 0.6 copy-done.24
  136.7 0.7 copy-done.25
  137.3 3.4 %input_grad.1 = (bf16[64,1152]{1,0:T(8,128)(2,1)}, bf16[64,1152]{1,0:T(8,128)(2,1)}) custom-call(s32[4]{0:T(128)} %pad_add_fusion.pos_ref, s32[16]{0:T(128)} %bitcast.33, bf16[1,2,64,1152]{3,2,1,0:T(8,128)(2,1)} %copy-done.2, bf16[1,2,64,1152]{3,2,1,0:T(8,128)(2,1)} %copy-done.3, f32[2,64,1152]{2,1,0:T(8,128)} %get-tuple-element.82.refs_6_.refs_2_, ...), custom_call_target="tpu_custom_call" | custom-call | flops 1769472000 | bytes 2359296 | tf_op jit(solution)/shard_map/input_grad/pallas_call | solution.py:653
  140.7 4.0 %collective-permute-start.27 = (bf16[64,1152]{1,0:T(8,128)(2,1)}, bf16[64,1152]{1,0:T(8,128)(2,1)S(1)}, u32[]{:S(2)}, u32[]{:S(2)}) collective-permute-start(bf16[64,1152]{1,0:T(8,128)(2,1)} %get-tuple-element.90), channel_id=1, source_target_pairs={{0,0},{1,1},{16,2},{17,3},{8,4},{9,5},{24,6},{25,7},{20,8},{21,9},... | collective-permute-start | bytes 442376 | tf_op jit(solution)/shard_map/ppermute | solution.py:476
  144.9 0.7 maximum_bitcast_fusion
  145.6 3.3 %collective-permute-done.27 = bf16[64,1152]{1,0:T(8,128)(2,1)S(1)} collective-permute-done((bf16[64,1152]{1,0:T(8,128)(2,1)}, bf16[64,1152]{1,0:T(8,128)(2,1)S(1)}, u32[]{:S(2)}, u32[]{:S(2)}) %collective-permute-start.27) | collective-permute-done | bytes 147488 | tf_op jit(solution)/shard_map/ppermute | solution.py:476
  148.9 1.9 %collective-permute-done.28 = bf16[64,1152]{1,0:T(8,128)(2,1)S(1)} collective-permute-done((bf16[64,1152]{1,0:T(8,128)(2,1)}, bf16[64,1152]{1,0:T(8,128)(2,1)S(1)}, u32[]{:S(2)}, u32[]{:S(2)}) %collective-permute-start.28) | collective-permute-done | bytes 147488 | tf_op jit(solution)/shard_map/ppermute | solution.py:476
  150.9 0.7 maximum_bitcast_fusion.1
  (80 shorter events, 0.5 us)
Async XLA Ops:
  1.9 23.2 %collective-permute-start.2 = (bf16[1,2,64,1152]{3,2,1,0:T(8,128)(2,1)S(1)}, bf16[1,2,64,1152]{3,2,1,0:T(8,128)(2,1)S(1)}, u32[]{:S(2)}, u32[]{:S(2)}) collective-permute-start(bf16[1,2,64,1152]{3,2,1,0:T(8,128)(2,1)S(1)} %pad_maximum_fusion.2), channel_id=1, source_target_pairs={{0,16},{1,17},{2,18},{3,19},{4,20},{5,21},{6,22},{7,23},{8,24},{9,... | collective-permute-start | bytes 884744 | tf_op jit(solution)/shard_map/ppermute | solution.py:492
  5.5 9.8 %copy-start.6 = (s32[1,4]{1,0:T(1,128)S(1)}, s32[1,4]{1,0:T(1,128)}, u32[]{:S(2)}) copy-start(s32[1,4]{1,0:T(1,128)} %param.12) | copy-start | bytes 52
  5.5 9.8 %copy-start.7 = (s32[1,4]{1,0:T(1,128)S(1)}, s32[1,4]{1,0:T(1,128)}, u32[]{:S(2)}) copy-start(s32[1,4]{1,0:T(1,128)} %param.11) | copy-start | bytes 52
  5.5 9.8 %copy-start.8 = (s32[1,8]{1,0:T(1,128)S(1)}, s32[1,8]{1,0:T(1,128)}, u32[]{:S(2)}) copy-start(s32[1,8]{1,0:T(1,128)} %param.10) | copy-start | bytes 100
  5.5 6.5 %collective-permute-start.4 = (bf16[144,432]{1,0:T(8,128)(2,1)}, bf16[144,432]{1,0:T(8,128)(2,1)S(1)}, u32[]{:S(2)}, u32[]{:S(2)}) collective-permute-start(bf16[144,432]{1,0:T(8,128)(2,1)} %get-tuple-element.51), channel_id=1, source_target_pairs={{0,1},{1,0},{2,3},{3,2},{4,5},{5,4},{6,7},{7,6},{8,9},{9,8},{10,11... | collective-permute-start | bytes 373256 | tf_op jit(solution)/shard_map/ppermute | solution.py:509
  7.6 17.0 %collective-permute-start = (bf16[1,2,64,1152]{3,2,1,0:T(8,128)(2,1)S(1)}, bf16[1,2,64,1152]{3,2,1,0:T(8,128)(2,1)S(1)}, u32[]{:S(2)}, u32[]{:S(2)}) collective-permute-start(bf16[1,2,64,1152]{3,2,1,0:T(8,128)(2,1)S(1)} %pad_maximum_fusion.1), channel_id=1, source_target_pairs={{0,0},{1,1},{2,16},{3,17},{4,8},{5,9},{6,24},{7,25},{8,20},{9,21},... | collective-permute-start | bytes 884744 | tf_op jit(solution)/shard_map/ppermute | solution.py:490
  13.1 19.5 %collective-permute-start.5 = (bf16[1,144,864]{2,1,0:T(8,128)(2,1)S(1)}, bf16[1,144,864]{2,1,0:T(8,128)(2,1)S(1)}, u32[]{:S(2)}, u32[]{:S(2)}) collective-permute-start(bf16[1,144,864]{2,1,0:T(8,128)(2,1)S(1)} %maximum_bitcast_fusion.2), channel_id=1, source_target_pairs={{0,4},{1,5},{2,6},{3,7},{4,0},{5,1},{6,2},{7,3},{8,12},{9,13},{10,... | collective-permute-start | bytes 746504 | tf_op jit(solution)/shard_map/ppermute | solution.py:472
  15.3 9.2 %collective-permute-start.1 = (s32[1,16]{1,0:T(1,128)S(1)}, s32[1,16]{1,0:T(1,128)S(1)}, u32[]{:S(2)}, u32[]{:S(2)}) collective-permute-start(s32[1,16]{1,0:T(1,128)S(1)} %add_bitcast_fusion), channel_id=1, source_target_pairs={{0,0},{1,1},{2,16},{3,17},{4,8},{5,9},{6,24},{7,25},{8,20},{9,21},... | collective-permute-start | bytes 200 | tf_op jit(solution)/shard_map/ppermute | solution.py:482
  24.5 17.5 %copy-start.26 = (s32[1,16]{1,0:T(1,128)}, s32[1,16]{1,0:T(1,128)S(1)}, u32[]{:S(2)}) copy-start(s32[1,16]{1,0:T(1,128)S(1)} %collective-permute-done.1) | copy-start | bytes 196
  24.5 17.5 %copy-start.2 = (bf16[1,2,64,1152]{3,2,1,0:T(8,128)(2,1)}, bf16[1,2,64,1152]{3,2,1,0:T(8,128)(2,1)S(1)}, u32[]{:S(2)}) copy-start(bf16[1,2,64,1152]{3,2,1,0:T(8,128)(2,1)S(1)} %collective-permute-done.refs_0_) | copy-start | bytes 884740
  24.5 15.9 %collective-permute-start.9 = (bf16[1,2,64,1152]{3,2,1,0:T(8,128)(2,1)S(1)}, bf16[1,2,64,1152]{3,2,1,0:T(8,128)(2,1)S(1)}, u32[]{:S(2)}, u32[]{:S(2)}) collective-permute-start(bf16[1,2,64,1152]{3,2,1,0:T(8,128)(2,1)S(1)} %collective-permute-done.refs_0_), channel_id=1, source_target_pairs={{0,1},{1,0},{2,3},{3,2},{4,5},{5,4},{6,7},{7,6},{8,9},{9,8},{10,11... | collective-permute-start | bytes 884744 | tf_op jit(solution)/shard_map/ppermute | solution.py:472
  25.1 14.8 %collective-permute-start.3 = (bf16[1,2,64,1152]{3,2,1,0:T(8,128)(2,1)S(1)}, bf16[1,2,64,1152]{3,2,1,0:T(8,128)(2,1)S(1)}, u32[]{:S(2)}, u32[]{:S(2)}) collective-permute-start(bf16[1,2,64,1152]{3,2,1,0:T(8,128)(2,1)S(1)} %collective-permute-done.2), channel_id=1, source_target_pairs={{0,10},{1,11},{2,26},{3,27},{4,2},{5,3},{6,18},{7,19},{8,30},{9,31... | collective-permute-start | bytes 884744 | tf_op jit(solution)/shard_map/ppermute | solution.py:493
  32.6 20.6 %copy-start.14 = (bf16[144,1152]{1,0:T(8,128)(2,1)S(1)}, bf16[144,1152]{1,0:T(8,128)(2,1)}, u32[]{:S(2)}) copy-start(bf16[144,1152]{1,0:T(8,128)(2,1)} %param.15) | copy-start | bytes 995332
  32.7 35.9 %copy-start.1 = (bf16[2,144,864]{2,1,0:T(8,128)(2,1)}, bf16[2,144,864]{2,1,0:T(8,128)(2,1)S(1)}, u32[]{:S(2)}) copy-start(bf16[2,144,864]{2,1,0:T(8,128)(2,1)S(1)} %pad_maximum_fusion.refs_0_) | copy-start | bytes 1492996
  32.7 20.4 %collective-permute-start.6 = (bf16[2,144,864]{2,1,0:T(8,128)(2,1)S(1)}, bf16[2,144,864]{2,1,0:T(8,128)(2,1)S(1)}, u32[]{:S(2)}, u32[]{:S(2)}) collective-permute-start(bf16[2,144,864]{2,1,0:T(8,128)(2,1)S(1)} %pad_maximum_fusion.refs_0_), channel_id=1, source_target_pairs={{0,2},{1,3},{2,0},{3,1},{4,6},{5,7},{6,4},{7,5},{8,10},{9,11},{10,... | collective-permute-start | bytes 1493000 | tf_op jit(solution)/shard_map/ppermute | solution.py:473
  39.8 28.7 %copy-start.3 = (bf16[1,2,64,1152]{3,2,1,0:T(8,128)(2,1)}, bf16[1,2,64,1152]{3,2,1,0:T(8,128)(2,1)S(1)}, u32[]{:S(2)}) copy-start(bf16[1,2,64,1152]{3,2,1,0:T(8,128)(2,1)S(1)} %collective-permute-done.3.refs_1_) | copy-start | bytes 884740
  39.8 6.8 %collective-permute-start.11 = (bf16[1,2,64,1152]{3,2,1,0:T(8,128)(2,1)S(1)}, bf16[1,2,64,1152]{3,2,1,0:T(8,128)(2,1)S(1)}, u32[]{:S(2)}, u32[]{:S(2)}) collective-permute-start(bf16[1,2,64,1152]{3,2,1,0:T(8,128)(2,1)S(1)} %collective-permute-done.3.refs_1_), channel_id=1, source_target_pairs={{0,16},{1,17},{2,18},{3,19},{4,20},{5,21},{6,22},{7,23},{8,24},{9,... | collective-permute-start | bytes 884744 | tf_op jit(solution)/shard_map/ppermute | solution.py:472
  40.4 22.2 %copy-start.4 = (bf16[2,2,64,1152]{3,2,1,0:T(8,128)(2,1)}, bf16[2,2,64,1152]{3,2,1,0:T(8,128)(2,1)S(1)}, u32[]{:S(2)}) copy-start(bf16[2,2,64,1152]{3,2,1,0:T(8,128)(2,1)S(1)} %constant_dynamic-update-slice_fusion.refs_0_) | copy-start | bytes 1769476
  40.4 21.5 %collective-permute-start.10 = (bf16[2,2,64,1152]{3,2,1,0:T(8,128)(2,1)S(1)}, bf16[2,2,64,1152]{3,2,1,0:T(8,128)(2,1)S(1)}, u32[]{:S(2)}, u32[]{:S(2)}) collective-permute-start(bf16[2,2,64,1152]{3,2,1,0:T(8,128)(2,1)S(1)} %constant_dynamic-update-slice_fusion.refs_0_), channel_id=1, source_target_pairs={{0,16},{1,17},{2,18},{3,19},{4,20},{5,21},{6,22},{7,23},{8,24},{9,... | collective-permute-start | bytes 1769480 | tf_op jit(solution)/shard_map/ppermute | solution.py:473
  46.6 16.0 %copy-start.5 = (bf16[2,2,64,1152]{3,2,1,0:T(8,128)(2,1)}, bf16[2,2,64,1152]{3,2,1,0:T(8,128)(2,1)S(1)}, u32[]{:S(2)}) copy-start(bf16[2,2,64,1152]{3,2,1,0:T(8,128)(2,1)S(1)} %constant_dynamic-update-slice_fusion.2.refs_2_) | copy-start | bytes 1769476
  46.7 16.0 %collective-permute-start.12 = (bf16[2,2,64,1152]{3,2,1,0:T(8,128)(2,1)S(1)}, bf16[2,2,64,1152]{3,2,1,0:T(8,128)(2,1)S(1)}, u32[]{:S(2)}, u32[]{:S(2)}) collective-permute-start(bf16[2,2,64,1152]{3,2,1,0:T(8,128)(2,1)S(1)} %constant_dynamic-update-slice_fusion.2.refs_2_), channel_id=1, source_target_pairs={{0,1},{1,0},{2,3},{3,2},{4,5},{5,4},{6,7},{7,6},{8,9},{9,8},{10,11... | collective-permute-start | bytes 1769480 | tf_op jit(solution)/shard_map/ppermute | solution.py:473
  50.7 17.9 %collective-permute-start.7 = (bf16[2,144,864]{2,1,0:T(8,128)(2,1)S(1)}, bf16[2,144,864]{2,1,0:T(8,128)(2,1)S(1)}, u32[]{:S(2)}, u32[]{:S(2)}) collective-permute-start(bf16[2,144,864]{2,1,0:T(8,128)(2,1)S(1)} %pad_maximum_fusion.refs_0_), channel_id=1, source_target_pairs={{0,8},{1,9},{2,10},{3,11},{4,12},{5,13},{6,14},{7,15},{8,0},{9,1},... | collective-permute-start | bytes 1493000 | tf_op jit(solution)/shard_map/ppermute | solution.py:519
  53.1 15.5 %copy-start.11 = (bf16[2,144,864]{2,1,0:T(8,128)(2,1)}, bf16[2,144,864]{2,1,0:T(8,128)(2,1)S(1)}, u32[]{:S(2)}) copy-start(bf16[2,144,864]{2,1,0:T(8,128)(2,1)S(1)} %collective-permute-done.6.refs_1_) | copy-start | bytes 1492996
  53.1 15.5 %collective-permute-start.8 = (bf16[2,144,864]{2,1,0:T(8,128)(2,1)S(1)}, bf16[2,144,864]{2,1,0:T(8,128)(2,1)S(1)}, u32[]{:S(2)}, u32[]{:S(2)}) collective-permute-start(bf16[2,144,864]{2,1,0:T(8,128)(2,1)S(1)} %collective-permute-done.6.refs_1_), channel_id=1, source_target_pairs={{0,8},{1,9},{2,10},{3,11},{4,12},{5,13},{6,14},{7,15},{8,0},{9,1},... | collective-permute-start | bytes 1493000 | tf_op jit(solution)/shard_map/ppermute | solution.py:519
  53.2 30.5 %collective-permute-start.13 = (bf16[144,1152]{1,0:T(8,128)(2,1)S(1)}, bf16[144,1152]{1,0:T(8,128)(2,1)S(1)}, u32[]{:S(2)}, u32[]{:S(2)}) collective-permute-start(bf16[144,1152]{1,0:T(8,128)(2,1)S(1)} %copy-done.14), channel_id=1, source_target_pairs={{0,0},{1,1},{2,18},{3,19},{4,8},{5,9},{6,26},{7,27},{8,4},{9,5},{1... | collective-permute-start | bytes 995336 | tf_op jit(solution)/shard_map/ppermute | solution.py:522
  61.9 0.8 copy-start.9
  62.8 0.8 copy-start.10
  68.6 0.8 copy-start.12
  68.6 1.0 copy-start.13
  81.5 13.5 %copy-start = (f32[4,48,864]{2,1,0:T(8,128)S(1)}, f32[4,48,864]{2,1,0:T(8,128)}, u32[]{:S(2)}) copy-start(f32[4,48,864]{2,1,0:T(8,128)} %get-tuple-element.60) | copy-start | bytes 1990660
  81.5 13.5 %collective-permute-start.15 = (f32[4,48,864]{2,1,0:T(8,128)}, f32[4,48,864]{2,1,0:T(8,128)S(1)}, u32[]{:S(2)}, u32[]{:S(2)}) collective-permute-start(f32[4,48,864]{2,1,0:T(8,128)} %get-tuple-element.61), channel_id=1, source_target_pairs={{0,8},{1,9},{2,10},{3,11},{4,12},{5,13},{6,14},{7,15},{8,0},{9,1},... | collective-permute-start | bytes 1990664 | tf_op jit(solution)/shard_map/ppermute | solution.py:573
  83.8 2.2 %copy-start.15 = (bf16[144,1152]{1,0:T(8,128)(2,1)}, bf16[144,1152]{1,0:T(8,128)(2,1)S(1)}, u32[]{:S(2)}) copy-start(bf16[144,1152]{1,0:T(8,128)(2,1)S(1)} %collective-permute-done.13.refs_0_) | copy-start | bytes 995332
  83.8 2.2 %collective-permute-start.14 = (bf16[144,1152]{1,0:T(8,128)(2,1)S(1)}, bf16[144,1152]{1,0:T(8,128)(2,1)S(1)}, u32[]{:S(2)}, u32[]{:S(2)}) collective-permute-start(bf16[144,1152]{1,0:T(8,128)(2,1)S(1)} %collective-permute-done.13.refs_0_), channel_id=1, source_target_pairs={{0,8},{1,9},{2,10},{3,11},{4,12},{5,13},{6,14},{7,15},{8,0},{9,1},... | collective-permute-start | bytes 995336 | tf_op jit(solution)/shard_map/ppermute | solution.py:523
  86.0 0.8 copy-start.16
  91.5 17.0 %collective-permute-start.17 = (bf16[2,64,1152]{2,1,0:T(8,128)(2,1)}, bf16[2,64,1152]{2,1,0:T(8,128)(2,1)S(1)}, u32[]{:S(2)}, u32[]{:S(2)}) collective-permute-start(bf16[2,64,1152]{2,1,0:T(8,128)(2,1)} %get-tuple-element.69), channel_id=1, source_target_pairs={{0,1},{1,0},{2,3},{3,2},{4,5},{5,4},{6,7},{7,6},{8,9},{9,8},{10,11... | collective-permute-start | bytes 884744 | tf_op jit(solution)/shard_map/ppermute | solution.py:587
  93.6 15.5 %collective-permute-start.18 = (bf16[2,64,1152]{2,1,0:T(8,128)(2,1)}, bf16[2,64,1152]{2,1,0:T(8,128)(2,1)S(1)}, u32[]{:S(2)}, u32[]{:S(2)}) collective-permute-start(bf16[2,64,1152]{2,1,0:T(8,128)(2,1)} %get-tuple-element.70), channel_id=1, source_target_pairs={{0,16},{1,17},{2,18},{3,19},{4,20},{5,21},{6,22},{7,23},{8,24},{9,... | collective-permute-start | bytes 884744 | tf_op jit(solution)/shard_map/ppermute | solution.py:587
  93.6 15.5 %collective-permute-start.19 = (bf16[2,64,1152]{2,1,0:T(8,128)(2,1)}, bf16[2,64,1152]{2,1,0:T(8,128)(2,1)S(1)}, u32[]{:S(2)}, u32[]{:S(2)}) collective-permute-start(bf16[2,64,1152]{2,1,0:T(8,128)(2,1)} %get-tuple-element.71), channel_id=1, source_target_pairs={{0,17},{1,16},{2,19},{3,18},{4,21},{5,20},{6,23},{7,22},{8,25},{9,... | collective-permute-start | bytes 884744 | tf_op jit(solution)/shard_map/ppermute | solution.py:587
  95.1 14.0 %collective-permute-start.16 = (f32[2,48,864]{2,1,0:T(8,128)S(1)}, f32[2,48,864]{2,1,0:T(8,128)S(1)}, u32[]{:S(2)}, u32[]{:S(2)}) collective-permute-start(f32[2,48,864]{2,1,0:T(8,128)S(1)} %get-tuple-element.67), channel_id=1, source_target_pairs={{0,2},{1,3},{2,0},{3,1},{4,6},{5,7},{6,4},{7,5},{8,10},{9,11},{10,... | collective-permute-start | bytes 995336 | tf_op jit(solution)/shard_map/ppermute | solution.py:593
  108.5 2.5 %copy-start.23 = (bf16[2,64,1152]{2,1,0:T(8,128)(2,1)S(1)}, bf16[2,64,1152]{2,1,0:T(8,128)(2,1)}, u32[]{:S(2)}) copy-start(bf16[2,64,1152]{2,1,0:T(8,128)(2,1)} %get-tuple-element.84) | copy-start | bytes 884740
  108.5 3.7 %copy-start.22 = (bf16[2,64,1152]{2,1,0:T(8,128)(2,1)S(1)}, bf16[2,64,1152]{2,1,0:T(8,128)(2,1)}, u32[]{:S(2)}) copy-start(bf16[2,64,1152]{2,1,0:T(8,128)(2,1)} %get-tuple-element.85) | copy-start | bytes 884740
  108.5 12.8 %copy-start.17 = (bf16[2,64,1152]{2,1,0:T(8,128)(2,1)}, bf16[2,64,1152]{2,1,0:T(8,128)(2,1)S(1)}, u32[]{:S(2)}) copy-start(bf16[2,64,1152]{2,1,0:T(8,128)(2,1)S(1)} %collective-permute-done.17.refs_3_) | copy-start | bytes 884740
  109.1 12.2 %copy-start.18 = (bf16[2,64,1152]{2,1,0:T(8,128)(2,1)}, bf16[2,64,1152]{2,1,0:T(8,128)(2,1)S(1)}, u32[]{:S(2)}) copy-start(bf16[2,64,1152]{2,1,0:T(8,128)(2,1)S(1)} %collective-permute-done.18.refs_4_) | copy-start | bytes 884740
  109.1 12.2 %copy-start.19 = (bf16[2,64,1152]{2,1,0:T(8,128)(2,1)}, bf16[2,64,1152]{2,1,0:T(8,128)(2,1)S(1)}, u32[]{:S(2)}) copy-start(bf16[2,64,1152]{2,1,0:T(8,128)(2,1)S(1)} %collective-permute-done.19.refs_5_) | copy-start | bytes 884740
  109.2 10.2 %collective-permute-start.20 = (f32[1,48,864]{2,1,0:T(8,128)S(1)}, f32[1,48,864]{2,1,0:T(8,128)S(1)}, u32[]{:S(2)}, u32[]{:S(2)}) collective-permute-start(f32[1,48,864]{2,1,0:T(8,128)S(1)} %slice.39), channel_id=1, source_target_pairs={{0,4},{1,5},{2,6},{3,7},{4,0},{5,1},{6,2},{7,3},{8,12},{9,13},{10,... | collective-permute-start | bytes 497672 | tf_op jit(solution)/shard_map/ppermute | solution.py:613
  111.0 10.3 %collective-permute-start.21 = (bf16[2,64,1152]{2,1,0:T(8,128)(2,1)S(1)}, bf16[2,64,1152]{2,1,0:T(8,128)(2,1)S(1)}, u32[]{:S(2)}, u32[]{:S(2)}) collective-permute-start(bf16[2,64,1152]{2,1,0:T(8,128)(2,1)S(1)} %copy-done.23), channel_id=1, source_target_pairs={{0,1},{1,0},{2,3},{3,2},{4,5},{5,4},{6,7},{7,6},{8,9},{9,8},{10,11... | collective-permute-start | bytes 884744 | tf_op jit(solution)/shard_map/ppermute | solution.py:625
  112.2 9.1 %collective-permute-start.22 = (bf16[2,64,1152]{2,1,0:T(8,128)(2,1)S(1)}, bf16[2,64,1152]{2,1,0:T(8,128)(2,1)S(1)}, u32[]{:S(2)}, u32[]{:S(2)}) collective-permute-start(bf16[2,64,1152]{2,1,0:T(8,128)(2,1)S(1)} %copy-done.22), channel_id=1, source_target_pairs={{0,16},{1,17},{2,18},{3,19},{4,20},{5,21},{6,22},{7,23},{8,24},{9,... | collective-permute-start | bytes 884744 | tf_op jit(solution)/shard_map/ppermute | solution.py:625
  119.4 15.8 %collective-permute-start.29 = (f32[48,864]{1,0:T(8,128)S(1)}, f32[48,864]{1,0:T(8,128)S(1)}, u32[]{:S(2)}, u32[]{:S(2)}) collective-permute-start(f32[48,864]{1,0:T(8,128)S(1)} %bitcast.25), channel_id=1, source_target_pairs={{0,0},{1,1},{2,8},{3,9},{4,16},{5,17},{6,24},{7,25},{8,4},{9,5},{1... | collective-permute-start | bytes 497672 | tf_op jit(solution)/shard_map/ppermute | solution.py:615
  121.3 0.7 copy-start.20
  122.0 0.7 copy-start.21
  126.5 9.5 %collective-permute-start.25 = (bf16[64,1152]{1,0:T(8,128)(2,1)}, bf16[64,1152]{1,0:T(8,128)(2,1)S(1)}, u32[]{:S(2)}, u32[]{:S(2)}) collective-permute-start(bf16[64,1152]{1,0:T(8,128)(2,1)} %get-tuple-element.88), channel_id=1, source_target_pairs={{0,16},{1,17},{2,18},{3,19},{4,20},{5,21},{6,22},{7,23},{8,24},{9,... | collective-permute-start | bytes 442376 | tf_op jit(solution)/shard_map/ppermute | solution.py:648
  126.5 9.5 %collective-permute-start.26 = (bf16[64,1152]{1,0:T(8,128)(2,1)}, bf16[64,1152]{1,0:T(8,128)(2,1)S(1)}, u32[]{:S(2)}, u32[]{:S(2)}) collective-permute-start(bf16[64,1152]{1,0:T(8,128)(2,1)} %get-tuple-element.89), channel_id=1, source_target_pairs={{0,1},{1,0},{2,3},{3,2},{4,5},{5,4},{6,7},{7,6},{8,9},{9,8},{10,11... | collective-permute-start | bytes 442376 | tf_op jit(solution)/shard_map/ppermute | solution.py:648
  127.6 17.2 %collective-permute-start.23 = (bf16[64,1152]{1,0:T(8,128)(2,1)}, bf16[64,1152]{1,0:T(8,128)(2,1)S(1)}, u32[]{:S(2)}, u32[]{:S(2)}) collective-permute-start(bf16[64,1152]{1,0:T(8,128)(2,1)} %get-tuple-element.86), channel_id=1, source_target_pairs={{0,0},{1,1},{16,2},{17,3},{8,4},{9,5},{24,6},{25,7},{20,8},{21,9},... | collective-permute-start | bytes 442376 | tf_op jit(solution)/shard_map/ppermute | solution.py:476
  131.0 13.8 %collective-permute-start.24 = (bf16[64,1152]{1,0:T(8,128)(2,1)}, bf16[64,1152]{1,0:T(8,128)(2,1)S(1)}, u32[]{:S(2)}, u32[]{:S(2)}) collective-permute-start(bf16[64,1152]{1,0:T(8,128)(2,1)} %get-tuple-element.87), channel_id=1, source_target_pairs={{8,0},{9,1},{24,2},{25,3},{0,4},{1,5},{16,6},{17,7},{28,8},{29,9},... | collective-permute-start | bytes 442376 | tf_op jit(solution)/shard_map/ppermute | solution.py:476
  136.0 0.7 copy-start.24
  136.7 0.7 copy-start.25
  140.7 8.2 %collective-permute-start.27 = (bf16[64,1152]{1,0:T(8,128)(2,1)}, bf16[64,1152]{1,0:T(8,128)(2,1)S(1)}, u32[]{:S(2)}, u32[]{:S(2)}) collective-permute-start(bf16[64,1152]{1,0:T(8,128)(2,1)} %get-tuple-element.90), channel_id=1, source_target_pairs={{0,0},{1,1},{16,2},{17,3},{8,4},{9,5},{24,6},{25,7},{20,8},{21,9},... | collective-permute-start | bytes 442376 | tf_op jit(solution)/shard_map/ppermute | solution.py:476
  144.7 6.1 %collective-permute-start.28 = (bf16[64,1152]{1,0:T(8,128)(2,1)}, bf16[64,1152]{1,0:T(8,128)(2,1)S(1)}, u32[]{:S(2)}, u32[]{:S(2)}) collective-permute-start(bf16[64,1152]{1,0:T(8,128)(2,1)} %get-tuple-element.91), channel_id=1, source_target_pairs={{8,0},{9,1},{24,2},{25,3},{0,4},{1,5},{16,6},{17,7},{28,8},{29,9},... | collective-permute-start | bytes 442376 | tf_op jit(solution)/shard_map/ppermute | solution.py:476

commit v6 on v5

--- a/solution.py
+++ b/solution.py
@@ -65,13 +65,6 @@
             lambda y, c, z, x: ((z % self.ny) ^ c, (z // self.ny) ^ k, c * self.ny + y, x)
         )
 
-    def to_plane_from_neighbour(self, k):
-        def move(y, c, z, x):
-            y = y ^ 1
-            return (z % self.ny) ^ c, (z // self.ny) ^ k, c * self.ny + y, x
-
-        return self.perm(move)
-
     def from_plane(self, k):
         return [(target, source) for source, target in self.to_plane(k)]
 
@@ -119,9 +112,6 @@
         for bit in bits:
             held = held + [k ^ bit for k in held]
         return held
-
-    def halved(self, bit):
-        return [k for k in range(self.chips) if not k & bit]
 
     def slots(self):
         return [(k, j) for k in range(self.chips) for j in range(self.nc)]
@@ -239,17 +229,25 @@
         gp_ref[t] = (factor * ref[place, 1].astype(F32)).astype(BF16)
 
 
-def forward_kernel(lay, pos_ref, info_ref, hid_ref, *refs):
+def forward_kernel(lay, pos_ref, info_ref, hid_ref, gp_ref, *refs):
     w_refs, refs = refs[: 2 * lay.halves], refs[2 * lay.halves :]
-    q_ref, k_ref, v_ref, att_ref, w_scr = refs
+    wo_refs, refs = refs[: lay.nc], refs[lay.nc :]
+    q_ref, k_ref, v_ref, ga_ref, kept_ref, sent_ref, *refs = refs
+    pr_refs, (w_scr, att_scr, wo_scr, acc_scr, cut_scr) = refs[: lay.chips], refs[lay.chips :]
     _, step_patches, model = hid_ref.shape
+    tokens = lay.frames * step_patches
     cols = w_scr.shape[2] // 3
     scaling = 1.0 / math.sqrt(cols // lay.half_heads)
     patches = step_patches * pl.num_programs(0)
+    is_first = pos_ref[1] == 0
 
     @pl.when(pl.program_id(0) == 0)
     def _():
         fill_weights(lay, pos_ref, w_refs, w_scr)
+        own, other = wo_refs[0][...].astype(F32), wo_refs[1][...].astype(F32)
+        both = [jnp.where(is_first, own, other), jnp.where(is_first, other, own)]
+        wo_scr[...] = jnp.concatenate(both, axis=0).astype(BF16)
+        acc_scr[...] = jnp.zeros_like(acc_scr)
 
     hidden = hid_ref[...].reshape(lay.frames * step_patches, model)
     for h in range(lay.halves):
@@ -271,27 +269,24 @@
             second = jnp.where(pos_ref[1] == 0, outputs[1], outputs[0])
             outputs = [jnp.concatenate([first, second], axis=1)]
         attended = outputs[0].astype(BF16)
-        att_ref[:, b * BLOCK : (b + 1) * BLOCK, :] = attended.reshape(lay.frames, BLOCK, -1)
-
-
-def weight_grad_kernel(lay, pos_ref, gp_ref, att_ref, kept_ref, sent_ref, acc_scr, cut_scr):
-    _, step_patches, model = gp_ref.shape
-    tokens = lay.frames * step_patches
-    groups, chunk_rows, chunk_width = kept_ref.shape
-    block_rows, part = acc_scr.shape[0] // lay.nc, model // groups
-    fold = chunk_width // part
-    order = lay.doubled(lay.bits(lay.nz)[::-1])
-    is_first = pos_ref[1] == 0
-
-    @pl.when(pl.program_id(0) == 0)
-    def _():
-        acc_scr[...] = jnp.zeros_like(acc_scr)
-
-    attended = att_ref[...].reshape(tokens, -1)
-    acc_scr[...] += t_dot(attended, gp_ref[...].reshape(tokens, model))
+        att_scr[:, b * BLOCK : (b + 1) * BLOCK, :] = attended.reshape(lay.frames, BLOCK, -1)
+
+    attended = att_scr[...].reshape(tokens, -1)
+    grad_proj = gp_ref[...].reshape(tokens, model)
+    acc_scr[...] += t_dot(attended, grad_proj)
+    grad_attn = dot_t(grad_proj, wo_scr[...])
+    part = wo_scr.shape[0] // lay.halves
+    for h in range(lay.halves):
+        ga_ref[h] = grad_attn[:, h * part : (h + 1) * part].astype(BF16).reshape(ga_ref.shape[1:])
+    projected = dot(attended, wo_scr[...]).reshape(lay.chips, lay.nc, step_patches, model)
+    for k in range(lay.chips):
+        pr_refs[k][...] = projected[k].astype(pr_refs[k].dtype)
 
     @pl.when(pl.program_id(0) == pl.num_programs(0) - 1)
     def _():
+        groups, chunk_rows, chunk_width = kept_ref.shape
+        block_rows, part = acc_scr.shape[0] // lay.nc, model // groups
+        order = lay.doubled(lay.bits(lay.nz)[::-1])
         first, second = acc_scr[:block_rows, :], acc_scr[block_rows:, :]
         kept = jnp.where(is_first, first, second)
         sent = jnp.where(is_first, second, first)
@@ -299,42 +294,17 @@
             for d in range(groups):
                 chunk = [
                     rows[m * chunk_rows : (m + 1) * chunk_rows, d * part : (d + 1) * part]
-                    for m in range(fold)
+                    for m in range(chunk_width // part)
                 ]
-                cut_scr[d] = jnp.concatenate(chunk, axis=1) if fold > 1 else chunk[0]
+                cut_scr[d] = jnp.concatenate(chunk, axis=1) if len(chunk) > 1 else chunk[0]
             for n, k in enumerate(order):
                 ref[n] = cut_scr[pos_ref[2] ^ k]
-
-
-def projection_kernel(lay, pos_ref, gp_ref, att_ref, *refs):
-    wo_refs, refs = refs[: lay.nc], refs[lay.nc :]
-    ga_ref, *refs = refs
-    pr_refs, (wo_scr,) = refs[: lay.chips], refs[lay.chips :]
-    _, step_patches, model = gp_ref.shape
-    tokens = lay.frames * step_patches
-    is_first = pos_ref[1] == 0
-
-    @pl.when(pl.program_id(0) == 0)
-    def _():
-        own, other = wo_refs[0][...].astype(F32), wo_refs[1][...].astype(F32)
-        both = [jnp.where(is_first, own, other), jnp.where(is_first, other, own)]
-        wo_scr[...] = jnp.concatenate(both, axis=0).astype(BF16)
-
-    grad_attn = dot_t(gp_ref[...].reshape(tokens, model), wo_scr[...])
-    part = wo_scr.shape[0] // lay.halves
-    for h in range(lay.halves):
-        ga_ref[h] = grad_attn[:, h * part : (h + 1) * part].astype(BF16).reshape(ga_ref.shape[1:])
-    attended = att_ref[...].reshape(tokens, -1)
-    projected = dot(attended, wo_scr[...]).reshape(lay.chips, lay.nc, step_patches, model)
-    for k in range(lay.chips):
-        pr_refs[k][...] = projected[k].astype(pr_refs[k].dtype)
 
 
 def backward_kernel(lay, pos_ref, info_ref, *refs):
     w_refs, refs = refs[: 2 * lay.halves], refs[2 * lay.halves :]
     q_ref, k_ref, v_ref, ga_ref, *refs = refs
-    kept_refs, refs = refs[: lay.nc], refs[lay.nc :]
-    sent_refs, (w_scr, gt_scr) = refs[: lay.nc], refs[lay.nc :]
+    gh_refs, (w_scr, gt_scr) = refs[: lay.chips], refs[lay.chips :]
     _, frames, step_patches, cols = q_ref.shape
     model = w_scr.shape[1]
     patches = step_patches * pl.num_programs(0)
@@ -367,23 +337,13 @@
         for h in range(lay.halves):
             part = gt_scr[h, k * lay.nc : (k + 1) * lay.nc].reshape(rows, 3 * cols)
             total = total + dot_t(part, w_scr[h])
-        total = total.reshape(lay.nc, step_patches, model)
-        for j in range(lay.nc):
-            first = lay.chip_bits(j)[0]
-            place = lay.halved(first).index(k & ~first)
-            if k & first:
-                sent_refs[j][place] = total[j].astype(BF16)
-            else:
-                kept_refs[j][place] = total[j]
+        gh_refs[k][...] = total.reshape(gh_refs[k].shape).astype(gh_refs[k].dtype)
 
 
 def output_kernel(lay, pos_ref, info_ref, *refs):
     pair_refs, refs = refs[: lay.nc], refs[lay.nc :]
     pr_refs, refs = refs[: lay.chips], refs[lay.chips :]
-    kept_refs, refs = refs[: lay.nc], refs[lay.nc :]
-    add_refs, refs = refs[: lay.nc], refs[lay.nc :]
-    mod_ref, *refs = refs
-    out_refs, sum_refs = refs[: lay.nc], refs[lay.nc :]
+    mod_ref, *out_refs = refs
     step_patches, model = out_refs[0].shape
     patches = step_patches * pl.num_programs(0)
     patch_base = pos_ref[1] * patches + pl.program_id(0) * step_patches
@@ -396,20 +356,18 @@
             projected = projected + pr_refs[k][j].astype(F32)
         projected = projected.astype(BF16).astype(F32)
         out_refs[j][...] = (pair_refs[j][0, 0].astype(F32) + factor * projected).astype(BF16)
-        sum_refs[j][...] = (kept_refs[j][1] + add_refs[j][1].astype(F32)).astype(BF16)
 
 
 def input_grad_kernel(lay, pos_ref, info_ref, *refs):
     pair_refs, refs = refs[: lay.nc], refs[lay.nc :]
-    kept_refs, refs = refs[: lay.nc], refs[lay.nc :]
-    add_refs, refs = refs[: lay.nc], refs[lay.nc :]
-    last_refs, refs = refs[: lay.nc], refs[lay.nc :]
+    gh_refs, refs = refs[: lay.chips], refs[lay.chips :]
     mod_ref, *out_refs = refs
     model = out_refs[0].shape[1]
     for j in range(lay.nc):
         _, _, step = slot_scalars(lay, pos_ref, info_ref, (0, j))
-        grad_hidden = kept_refs[j][0] + add_refs[j][0].astype(F32)
-        grad_hidden = grad_hidden + last_refs[j][...].astype(F32)
+        grad_hidden = gh_refs[0][j]
+        for k in range(1, lay.chips):
+            grad_hidden = grad_hidden + gh_refs[k][j].astype(F32)
         grad_hidden = grad_hidden.astype(BF16).astype(F32)
         normed, inv_sigma = normalize(pair_refs[j][0, 0].astype(F32))
         grad_norm = grad_hidden * (1.0 + table_row(mod_ref, step, 1, model))
@@ -467,10 +425,15 @@
         ky, kx = lay.chip_of(k)
         return lay.swap(ky=ky, kx=kx)
 
-    def doubling(held, bits, swap):
+    def doubling(held, bits, swap, after=()):
         for bit in bits[:-1]:
             held = jnp.concatenate([held, lax.ppermute(held, AXES, swap(bit))], axis=0)
+        held, _ = lax.optimization_barrier((held, after))
         return [held, lax.ppermute(held, AXES, swap(bits[-1]))]
+
+    def over_chips(parts):
+        got = [lax.ppermute(parts[k], AXES, chip_swap(k)) for k in range(1, chips)]
+        return [parts[0]] + got
 
     def from_plane(parts):
         got = [lax.ppermute(part, AXES, lay.from_plane(k)) for k, part in enumerate(parts)]
@@ -487,11 +450,8 @@
         pair = [lax.dynamic_slice_in_dim(frame, start, half, axis=1) for frame in (frames_x, grad_y)]
         pair = jnp.stack(pair, axis=1)
         if k == 0:
-            own.append(lax.ppermute(pair, AXES, lay.to_plane(k)))
-        else:
-            pair = lax.ppermute(pair, AXES, lay.swap(ky=1))
-            own.append(lax.ppermute(pair, AXES, lay.to_plane_from_neighbour(k)))
-    own[0], info = lax.optimization_barrier((own[0], info))
+            pair, info = lax.optimization_barrier((pair, info))
+        own.append(lax.ppermute(pair, AXES, lay.to_plane(k)))
     pairs = []
     for j in range(nc):
         pairs += doubling(own[j], lay.chip_bits(j), chip_swap)
@@ -514,151 +474,117 @@
         stacked = jnp.stack(by_x)
         ordered = [lax.dynamic_index_in_dim(stacked, x ^ i, 0, keepdims=False) for i in range(nx)]
     w_own = jnp.concatenate(ordered, axis=1 if rows % 16 == 0 else 0)[None]
-    w_pieces = doubling(w_own, lay.bits(lay.nz)[::-1], lambda kz: lay.swap(kz=kz))
+    w_pieces = doubling(w_own, lay.bits(lay.nz)[::-1], lambda kz: lay.swap(kz=kz), pairs[::2])
     if halves > 1:
         w_pieces += [lax.ppermute(piece, AXES, lay.swap(kc=1)) for piece in w_pieces]
 
     late_w_out, _ = lax.optimization_barrier((w_out, w_pieces[:2]))
     wo_own = lax.ppermute(late_w_out, AXES, lay.rows_to_chip())
-    wo_rows = [wo_own, lax.ppermute(wo_own, AXES, lay.swap(kc=1))]
-
-    x_spec = pl.BlockSpec((step_patches, model), lambda i, *_: (i, 0))
-
-    def pair_spec(count):
-        return pl.BlockSpec((count, 2, step_patches, model), lambda i, *_: (0, 0, i, 0))
-
+
+    def spread(count, width, patches_at_once):
+        return pl.BlockSpec((count, patches_at_once, width), lambda i, *_: (0, i, 0))
+
+    def pair_spec(count, patches_at_once):
+        return pl.BlockSpec((count, 2, patches_at_once, model), lambda i, *_: (0, 0, i, 0))
+
+    few = max(BLOCK, step_patches // 2)
+    few_steps = half // few
+    x_spec = pl.BlockSpec((few, model), lambda i, *_: (i, 0))
     triple_spec = pl.BlockSpec((halves, lay.frames, step_patches, cols), lambda i, *_: (0, 0, i, 0))
-    att_spec = pl.BlockSpec((lay.frames, step_patches, chip_width), lambda i, *_: (0, i, 0))
-    gp_spec = pl.BlockSpec((lay.frames, step_patches, model), lambda i, *_: (0, i, 0))
-    part_spec = pl.BlockSpec((nc, step_patches, model), lambda i, *_: (0, i, 0))
     w_specs = [whole_spec(piece.shape) for piece in w_pieces]
     w_scratch = pltpu.VMEM((halves, model, 3 * cols), BF16)
     mod_spec = whole_spec(mod_table.shape)
     triple_shape = struct((halves, lay.frames, half, cols))
+    part_specs = [spread(nc, model, step_patches)] * chips
+    part_shapes = [struct((nc, half, model), F32)] + [struct((nc, half, model))] * (chips - 1)
 
     hidden, grad_proj = call(
         functools.partial(prepare_kernel, lay),
         "prepare",
         3 * model * 1000,
-        [pair_spec(chips // 2)] * (2 * nc) + [mod_spec],
-        [gp_spec] * 2,
+        [pair_spec(chips // 2, few)] * (2 * nc) + [mod_spec],
+        [spread(lay.frames, model, few)] * 2,
         [struct((lay.frames, half, model))] * 2,
-        grid=(steps,),
+        grid=(few_steps,),
     )(pos, info, *pairs, mod_table)
-
-    queries, keys, values, attended = call(
+    wo_own, _ = lax.optimization_barrier((wo_own, hidden))
+    wo_rows = [wo_own, lax.ppermute(wo_own, AXES, lay.swap(kc=1))]
+
+    fold = 3 if rows % 24 == 0 else 1
+    piece_shape = (groups, rows // fold, quarter * fold)
+    queries, keys, values, grad_attn, kept, sent, *projected = call(
         functools.partial(forward_kernel, lay),
         "forward",
-        8 * model * 1000,
-        [gp_spec] + w_specs,
-        [triple_spec] * 3 + [att_spec],
-        [triple_shape] * 3 + [struct((lay.frames, half, chip_width))],
-        [w_scratch],
+        14 * model * 1000,
+        [spread(lay.frames, model, step_patches)] * 2
+        + w_specs
+        + [whole_spec(w_out.shape)] * nc,
+        [triple_spec] * 4 + [whole_spec(piece_shape)] * 2 + part_specs,
+        [triple_shape] * 4 + [struct(piece_shape, F32)] * 2 + part_shapes,
+        [
+            w_scratch,
+            pltpu.VMEM((lay.frames, step_patches, chip_width), BF16),
+            pltpu.VMEM((chip_width, model), BF16),
+            pltpu.VMEM((chip_width, model), F32),
+            pltpu.VMEM(piece_shape, F32),
+        ],
         (steps,),
-    )(pos, info, hidden, *w_pieces)
-
-    fold = 3 if rows % 24 == 0 else 1
-    piece_shape = (groups, rows // fold, quarter * fold)
-    kept, sent = call(
-        functools.partial(weight_grad_kernel, lay),
-        "weight_grad",
-        4 * model * 1000,
-        [gp_spec, att_spec],
-        [whole_spec(piece_shape)] * 2,
-        [struct(piece_shape, F32)] * 2,
-        [pltpu.VMEM((chip_width, model), F32), pltpu.VMEM(piece_shape, F32)],
-        (steps,),
-        prefetch=1,
-    )(pos, grad_proj, attended)
+    )(pos, info, hidden, grad_proj, *w_pieces, *wo_rows)
     got = lax.ppermute(sent, AXES, lay.swap(kc=1))
-
-    grad_attn, *projected = call(
-        functools.partial(projection_kernel, lay),
-        "projection",
-        4 * model * 1000,
-        [gp_spec, att_spec] + [whole_spec(w_out.shape)] * nc,
-        [triple_spec] + [part_spec] * chips,
-        [triple_shape, struct((nc, half, model), F32)] + [struct((nc, half, model))] * (chips - 1),
-        [pltpu.VMEM((chip_width, model), BF16)],
-        (steps,),
-        prefetch=1,
-    )(pos, grad_proj, attended, *wo_rows)
-    projected = [projected[0]] + [
-        lax.ppermute(projected[k], AXES, chip_swap(k)) for k in range(1, chips)
-    ]
+    projected = over_chips(projected)
 
     middle = groups // 2
     cut, away = kept[:middle] + got[:middle], kept[middle:] + got[middle:]
     grad_attn, cut, away = lax.optimization_barrier((grad_attn, cut, away))
     first_away = lax.ppermute(away, AXES, lay.swap(kz=1))
 
-    def side_spec(count):
-        return pl.BlockSpec((count, step_patches, model), lambda i, *_: (0, i, 0))
-
-    side = chips // 2
     sums = call(
         functools.partial(backward_kernel, lay),
         "backward",
         10 * model * 1000,
         w_specs + [triple_spec] * 4,
-        [side_spec(side)] * (2 * nc),
-        [struct((side, half, model), F32)] * nc + [struct((side, half, model))] * nc,
+        part_specs,
+        part_shapes,
         [w_scratch, pltpu.VMEM((halves, lay.frames, step_patches, 3 * cols), BF16)],
         (steps,),
     )(pos, info, *w_pieces, queries, keys, values, grad_attn)
     sums, first_away, projected = lax.optimization_barrier((sums, first_away, projected))
+    grad_hidden = over_chips(sums)
+    projected, _ = lax.optimization_barrier((projected, grad_hidden[1]))
+
+    out_parts = call(
+        functools.partial(output_kernel, lay),
+        "output",
+        3 * model * 1000,
+        [pair_spec(1, few)] * nc + [spread(nc, model, few)] * chips + [mod_spec],
+        [x_spec] * nc,
+        [struct((half, model))] * nc,
+        grid=(few_steps,),
+    )(pos, info, *own, *projected, mod_table)
+
     cut = cut + first_away
     for bit in lay.bits(lay.nz)[1:]:
         middle = middle // 2
-        cut = cut[:middle] + lax.ppermute(cut[middle:], AXES, lay.swap(kz=bit))
-    projected, cut = lax.optimization_barrier((projected, cut))
+        away = lax.ppermute(cut[middle:], AXES, lay.swap(kz=bit))
+        away, _ = lax.optimization_barrier((away, out_parts))
+        cut = cut[:middle] + away
     grad_w = lax.ppermute(cut[0], AXES, lay.to_owner())
     grad_w = jnp.concatenate(
         [grad_w[:, m * quarter : (m + 1) * quarter] for m in range(fold)], axis=0
     )
     grad_w_out = grad_w * jnp.float32(1.0 / math.sqrt(groups * lay.frames * patches))
 
-    held, added = list(sums[:nc]), []
-    for j in range(nc):
-        bits = lay.chip_bits(j)
-        keys_held = lay.halved(bits[0])
-        added.append(lax.ppermute(sums[nc + j], AXES, chip_swap(bits[0])))
-        for bit in bits[1:-1]:
-            total = held[j] + added[j].astype(F32)
-            out_at = [n for n, k in enumerate(keys_held) if k & bit]
-            in_at = [n for n, k in enumerate(keys_held) if not k & bit]
-            out_part = jnp.stack([total[n] for n in out_at]).astype(BF16)
-            held[j] = jnp.stack([total[n] for n in in_at])
-            added[j] = lax.ppermute(out_part, AXES, chip_swap(bit))
-            keys_held = [keys_held[n] for n in in_at]
-
-    *out_parts, last0, last1 = call(
-        functools.partial(output_kernel, lay),
-        "output",
-        3 * model * 1000,
-        [pair_spec(1)] * nc
-        + [part_spec] * chips
-        + [side_spec(2)] * (2 * nc)
-        + [mod_spec],
-        [x_spec] * (2 * nc),
-        [struct((half, model))] * (2 * nc),
-        grid=(steps,),
-    )(pos, info, *own, *projected, *held, *added, mod_table)
-    last = [
-        lax.ppermute(part, AXES, chip_swap(lay.chip_bits(j)[-1]))
-        for j, part in enumerate((last0, last1))
-    ]
     out_y = from_plane(out_parts)
 
     grad_parts = call(
         functools.partial(input_grad_kernel, lay),
         "input_grad",
         3 * model * 1000,
-        [pair_spec(1)] * nc + [side_spec(1)] * (2 * nc) + [x_spec] * nc + [mod_spec],
+        [pair_spec(1, few)] * nc + [spread(nc, model, few)] * chips + [mod_spec],
         [x_spec] * nc,
         [struct((half, model))] * nc,
-        grid=(steps,),
-    )(pos, info, *own, *held, *added, *last, mod_table)
+        grid=(few_steps,),
+    )(pos, info, *own, *grad_hidden, mod_table)
     grad_x = from_plane(grad_parts)
     return out_y, grad_x, grad_w_out
 

time: 154 us -> 138 us (0.90)
  starting transfers between devices: 68.2 us -> 45.6 us
  waiting for transfers between devices: 29.9 us -> 44.8 us
  Pallas kernels: 41.4 us -> 34.7 us
  local copies, waits for them, and re-layouts: 6.84 us -> 4.01 us
    ppermute x1 -> x2, waiting for transfers between devices: 0.01 us -> 14.3 us  [local(): own.append(lax.ppermute(pair, AXES, lay.to_plane(k)))]
    ppermute x3, waiting for transfers between devices: 0.72 us -> 11.5 us  [doubling(): return [held, lax.ppermute(held, AXES, swap(bits[-1]))]]
    ppermute x10 -> x7, starting transfers between devices: 16.3 us -> 7.55 us  [the longest x6 7.1 us: over_chips(): got = [lax.ppermute(parts[k], AXES, chip_swap(k)) for k in range(1, chips)]]
    ppermute x10 -> x7, waiting for transfers between devices: 12.4 us -> 6.43 us  [the longest x6 6.43 us: over_chips(): got = [lax.ppermute(parts[k], AXES, chip_swap(k)) for k in range(1, chips)]]
    pallas_call x3 -> x1, Pallas kernels: 16.7 us -> 11.2 us  [local(): call(functools.partial(forward_kernel, lay), 'forward', 14 * model * 1000...]
    ppermute x1, starting transfers between devices: 8.67 us -> 3.33 us  [local(): wo_own = lax.ppermute(late_w_out, AXES, lay.rows_to_chip())]
    ppermute x1, waiting for transfers between devices: 4.72 us -> 0.01 us  [local(): info = lax.ppermute(info, AXES, lay.to_plane(0))[0]]
    ppermute x3, starting transfers between devices: 3.28 us -> 0.62 us  [doubling(): held = jnp.concatenate([held, lax.ppermute(held, AXES, swap(bit))], axis=0)]
  transfers between devices with their start and end apart: 30 -> 28, of which waited for: 9 -> 11; matrix products, arithmetic and copies ran while one was open for 2% -> 3% of each run, Pallas kernels for 27% -> 17%
where the time goes in v6:
time: 138 us; the launch traced here: 135 us
  starting transfers between devices  45.6 us (33%)
  waiting for transfers between devices  44.8 us (32%)
  Pallas kernels  34.7 us (25%)
  other arithmetic  5.28 us (4%)
  local copies, waits for them, and re-layouts  4.01 us (3%)
    ppermute x2, waiting for transfers between devices, local(): own.append(lax.ppermute(pair, AXES, lay.to_plane(k)))  14.3 us
    ppermute x3, waiting for transfers between devices, doubling(): return [held, lax.ppermute(held, AXES, swap(bits[-1]))]  11.5 us
    pallas_call x1, Pallas kernels, local(): call(functools.partial(forward_kernel, lay), 'forward', 14 * model * 1000...  11.2 us
    ppermute x4, starting transfers between devices, from_plane(): lax.ppermute(part, AXES, lay.from_plane(k))  10.9 us
    pallas_call x1, Pallas kernels, local(): call(functools.partial(backward_kernel, lay), 'backward', 10 * model * 10...  9.56 us
    ppermute x6, starting transfers between devices, over_chips(): got = [lax.ppermute(parts[k], AXES, chip_swap(k)) for k in range(1, chips)]  7.1 us
    ppermute x6, waiting for transfers between devices, over_chips(): got = [lax.ppermute(parts[k], AXES, chip_swap(k)) for k in range(1, chips)]  6.43 us
    ppermute x2, starting transfers between devices, local(): own.append(lax.ppermute(pair, AXES, lay.to_plane(k)))  6.42 us
  transfers between devices with their start and end apart: 28, of which 11 were waited for; matrix products, arithmetic and copies ran while one was open for 3% of the time, Pallas kernels for 17%

profile of v6, /device:TPU:4, one launch (start us, length us, event | category | flops | bytes accessed | tf_op | source)
XLA Modules:
  0.0 135.4 jit_solution(3208567845330630371)
XLA Ops:
  0.6 0.8 add_bitcast_fusion
  1.4 3.4 %collective-permute-start = (s32[1,16]{1,0:T(1,128)S(1)}, s32[1,16]{1,0:T(1,128)S(1)}, u32[]{:S(2)}, u32[]{:S(2)}) collective-permute-start(s32[1,16]{1,0:T(1,128)S(1)} %add_bitcast_fusion), channel_id=1, source_target_pairs={{0,0},{1,1},{2,16},{3,17},{4,8},{5,9},{6,24},{7,25},{8,20},{9,21},... | collective-permute-start | bytes 200 | tf_op jit(solution)/shard_map/ppermute | solution.py:445
  4.8 0.7 pad_add_fusion.pos_ref
  5.5 3.0 %pick.1 = (bf16[144,432]{1,0:T(8,128)(2,1)}, bf16[144,432]{1,0:T(8,128)(2,1)}) custom-call(s32[4]{0:T(128)} %pad_add_fusion.pos_ref, bf16[144,3456]{1,0:T(8,128)(2,1)} %w_ref.1), custom_call_target="tpu_custom_call" | custom-call | flops 1179648000 | bytes 2359296 | tf_op jit(solution)/shard_map/pick/pallas_call | solution.py:459
  8.5 1.5 %collective-permute-start.3 = (bf16[144,432]{1,0:T(8,128)(2,1)}, bf16[144,432]{1,0:T(8,128)(2,1)S(1)}, u32[]{:S(2)}, u32[]{:S(2)}) collective-permute-start(bf16[144,432]{1,0:T(8,128)(2,1)} %get-tuple-element.50), channel_id=1, source_target_pairs={{0,1},{1,0},{2,3},{3,2},{4,5},{5,4},{6,7},{7,6},{8,9},{9,8},{10,11... | collective-permute-start | bytes 373256 | tf_op jit(solution)/shard_map/ppermute | solution.py:469
  10.1 1.1 collective-permute-start.2
  11.2 0.0 collective-permute-done
  11.2 5.3 %collective-permute-start.1 = (bf16[1,2,64,1152]{3,2,1,0:T(8,128)(2,1)S(1)}, bf16[1,2,64,1152]{3,2,1,0:T(8,128)(2,1)S(1)}, u32[]{:S(2)}, u32[]{:S(2)}) collective-permute-start(bf16[1,2,64,1152]{3,2,1,0:T(8,128)(2,1)S(1)} %pad_maximum_fusion.3), channel_id=1, source_target_pairs={{0,0},{1,1},{2,16},{3,17},{4,8},{5,9},{6,24},{7,25},{8,20},{9,21},... | collective-permute-start | bytes 884744 | tf_op jit(solution)/shard_map/ppermute | solution.py:454
  16.6 0.1 maximum_bitcast_fusion.2
  16.7 0.1 collective-permute-start.4
  16.8 6.0 %collective-permute-done.2.refs_1_ = bf16[1,2,64,1152]{3,2,1,0:T(8,128)(2,1)S(1)} collective-permute-done((bf16[1,2,64,1152]{3,2,1,0:T(8,128)(2,1)S(1)}, bf16[1,2,64,1152]{3,2,1,0:T(8,128)(2,1)S(1)}, u32[]{:S(2)}, u32[]{:S(2)}) %collective-permute-start.2) | collective-permute-done | bytes 294944 | tf_op jit(solution)/shard_map/ppermute | solution.py:454
  22.8 0.0 collective-permute-start.6
  22.8 8.3 %collective-permute-done.1.refs_0_ = bf16[1,2,64,1152]{3,2,1,0:T(8,128)(2,1)S(1)} collective-permute-done((bf16[1,2,64,1152]{3,2,1,0:T(8,128)(2,1)S(1)}, bf16[1,2,64,1152]{3,2,1,0:T(8,128)(2,1)S(1)}, u32[]{:S(2)}, u32[]{:S(2)}) %collective-permute-start.1) | collective-permute-done | bytes 294944 | tf_op jit(solution)/shard_map/ppermute | solution.py:454
  31.1 0.5 collective-permute-start.5
  31.7 5.8 %collective-permute-done.4 = bf16[1,144,864]{2,1,0:T(8,128)(2,1)S(1)} collective-permute-done((bf16[1,144,864]{2,1,0:T(8,128)(2,1)S(1)}, bf16[1,144,864]{2,1,0:T(8,128)(2,1)S(1)}, u32[]{:S(2)}, u32[]{:S(2)}) %collective-permute-start.4) | collective-permute-done | bytes 248864 | tf_op jit(solution)/shard_map/ppermute | solution.py:430
  37.5 0.1 pad_maximum_fusion.2.refs_0_
  37.6 0.0 copy-start.13
  37.6 0.0 collective-permute-done.6
  37.6 0.1 pad_maximum_fusion.1.refs_2_
  37.7 0.1 collective-permute-done.5
  37.9 0.1 pad_maximum_fusion.refs_0_
  38.0 4.5 %collective-permute-start.7 = (bf16[2,144,864]{2,1,0:T(8,128)(2,1)S(1)}, bf16[2,144,864]{2,1,0:T(8,128)(2,1)S(1)}, u32[]{:S(2)}, u32[]{:S(2)}) collective-permute-start(bf16[2,144,864]{2,1,0:T(8,128)(2,1)S(1)} %pad_maximum_fusion.2.refs_0_), channel_id=1, source_target_pairs={{0,2},{1,3},{2,0},{3,1},{4,6},{5,7},{6,4},{7,5},{8,10},{9,11},{10,... | collective-permute-start | bytes 1493000 | tf_op jit(solution)/shard_map/ppermute | solution.py:432
  42.4 0.6 collective-permute-start.11
  43.0 0.0 collective-permute-start.10
  43.0 11.5 %collective-permute-done.7.refs_1_ = bf16[2,144,864]{2,1,0:T(8,128)(2,1)S(1)} collective-permute-done((bf16[2,144,864]{2,1,0:T(8,128)(2,1)S(1)}, bf16[2,144,864]{2,1,0:T(8,128)(2,1)S(1)}, u32[]{:S(2)}, u32[]{:S(2)}) %collective-permute-start.7) | collective-permute-done | bytes 497696 | tf_op jit(solution)/shard_map/ppermute | solution.py:432
  54.5 3.3 %collective-permute-start.12 = (bf16[144,1152]{1,0:T(8,128)(2,1)S(1)}, bf16[144,1152]{1,0:T(8,128)(2,1)S(1)}, u32[]{:S(2)}, u32[]{:S(2)}) collective-permute-start(bf16[144,1152]{1,0:T(8,128)(2,1)S(1)} %copy-done.13), channel_id=1, source_target_pairs={{0,0},{1,1},{2,18},{3,19},{4,8},{5,9},{6,26},{7,27},{8,4},{9,5},{1... | collective-permute-start | bytes 995336 | tf_op jit(solution)/shard_map/ppermute | solution.py:482
  57.8 0.1 collective-permute-start.8
  57.9 0.5 collective-permute-start.9
  58.5 0.8 copy-done.8
  59.3 0.8 copy-done.9
  60.1 4.4 %prepare.1 = (bf16[8,64,1152]{2,1,0:T(8,128)(2,1)}, bf16[8,64,1152]{2,1,0:T(8,128)(2,1)}) custom-call(s32[4]{0:T(128)} %pad_add_fusion.pos_ref, s32[16]{0:T(128)} %bitcast.29, bf16[2,2,64,1152]{3,2,1,0:T(8,128)(2,1)} %copy-done.1, bf16[2,2,64,1152]{3,2,1,0:T(8,128)(2,1)} %copy-done.9, bf16[2,2,64,1152]{3,2,1,0:T(8,128)(2,1)} %copy-done, ...), custom_call_target="tpu_custom_call" | custom-call | flops 1769472000 | bytes 2359296 | tf_op jit(solution)/shard_map/prepare/pallas_call | solution.py:501
  64.5 1.5 %collective-permute-done.12.refs_4_ = bf16[144,1152]{1,0:T(8,128)(2,1)S(1)} collective-permute-done((bf16[144,1152]{1,0:T(8,128)(2,1)S(1)}, bf16[144,1152]{1,0:T(8,128)(2,1)S(1)}, u32[]{:S(2)}, u32[]{:S(2)}) %collective-permute-start.12) | collective-permute-done | bytes 331808 | tf_op jit(solution)/shard_map/ppermute | solution.py:482
  66.0 1.8 %collective-permute-start.13 = (bf16[144,1152]{1,0:T(8,128)(2,1)S(1)}, bf16[144,1152]{1,0:T(8,128)(2,1)S(1)}, u32[]{:S(2)}, u32[]{:S(2)}) collective-permute-start(bf16[144,1152]{1,0:T(8,128)(2,1)S(1)} %collective-permute-done.12.refs_4_), channel_id=1, source_target_pairs={{0,8},{1,9},{2,10},{3,11},{4,12},{5,13},{6,14},{7,15},{8,0},{9,1},... | collective-permute-start | bytes 995336 | tf_op jit(solution)/shard_map/ppermute | solution.py:511
  67.8 0.0 collective-permute-done.9.refs_3_
  67.8 1.2 collective-permute-done.13.refs_5_
  69.0 0.7 copy-done.15
  69.8 11.2 %forward.1 = (bf16[2,8,64,144]{3,2,1,0:T(8,128)(2,1)}, bf16[2,8,64,144]{3,2,1,0:T(8,128)(2,1)}, bf16[2,8,64,144]{3,2,1,0:T(8,128)(2,1)}, bf16[2,8,64,144]{3,2,1,...) custom-call(s32[4]{0:T(128)} %pad_add_fusion.pos_ref, ...), custom_call_target="tpu_custom_call" | custom-call | flops 8257536000 | bytes 2359296 | tf_op jit(solution)/shard_map/forward/pallas_call | solution.py:515
  81.0 0.4 collective-permute-start.14
  81.4 0.5 collective-permute-start.16
  81.9 3.0 %collective-permute-start.18 = (bf16[2,64,1152]{2,1,0:T(8,128)(2,1)}, bf16[2,64,1152]{2,1,0:T(8,128)(2,1)S(1)}, u32[]{:S(2)}, u32[]{:S(2)}) collective-permute-start(bf16[2,64,1152]{2,1,0:T(8,128)(2,1)} %get-tuple-element.71), channel_id=1, source_target_pairs={{0,17},{1,16},{2,19},{3,18},{4,21},{5,20},{6,23},{7,22},{8,25},{9,... | collective-permute-start | bytes 884744 | tf_op jit(solution)/shard_map/ppermute | solution.py:435
  84.9 1.2 slice_add_fusion
  86.0 1.3 collective-permute-start.15
  87.3 9.6 %backward.1 = (f32[2,64,1152]{2,1,0:T(8,128)}, bf16[2,64,1152]{2,1,0:T(8,128)(2,1)}, bf16[2,64,1152]{2,1,0:T(8,128)(2,1)}, bf16[2,64,1152]{2,1,0:T(8,128)(2,1)}) custom-call(s32[4]{0:T(128)} %pad_add_fusion.pos_ref, s32[16]{0:T(128)} %bitcast.31, bf16[2,144,864]{2,1,0:T(8,128)(2,1)} %copy-done.2, bf16[2,144,864]{2,1,0:T(8,128)(2,1)} %copy-done.10, ...), custom_call_target="tpu_custom_call" | custom-call | flops 5898240000 | bytes 2359296 | tf_op jit(solution)/shard_map/backward/pallas_call | solution.py:541
  96.9 0.3 collective-permute-done.17.refs_4_
  97.2 1.6 %collective-permute-start.19 = (bf16[2,64,1152]{2,1,0:T(8,128)(2,1)}, bf16[2,64,1152]{2,1,0:T(8,128)(2,1)S(1)}, u32[]{:S(2)}, u32[]{:S(2)}) collective-permute-start(bf16[2,64,1152]{2,1,0:T(8,128)(2,1)} %get-tuple-element.76), channel_id=1, source_target_pairs={{0,1},{1,0},{2,3},{3,2},{4,5},{5,4},{6,7},{7,6},{8,9},{9,8},{10,11... | collective-permute-start | bytes 884744 | tf_op jit(solution)/shard_map/ppermute | solution.py:435
  98.8 0.4 collective-permute-start.26
  99.3 0.2 collective-permute-start.22
  99.5 1.8 %collective-permute-start.23 = (bf16[2,64,1152]{2,1,0:T(8,128)(2,1)S(1)}, bf16[2,64,1152]{2,1,0:T(8,128)(2,1)S(1)}, u32[]{:S(2)}, u32[]{:S(2)}) collective-permute-start(bf16[2,64,1152]{2,1,0:T(8,128)(2,1)S(1)} %copy-done.16), channel_id=1, source_target_pairs={{0,17},{1,16},{2,19},{3,18},{4,21},{5,20},{6,23},{7,22},{8,25},{9,... | collective-permute-start | bytes 884744 | tf_op jit(solution)/shard_map/ppermute | solution.py:435
  101.3 6.1 %collective-permute-done.19.refs_3_ = bf16[2,64,1152]{2,1,0:T(8,128)(2,1)S(1)} collective-permute-done((bf16[2,64,1152]{2,1,0:T(8,128)(2,1)}, bf16[2,64,1152]{2,1,0:T(8,128)(2,1)S(1)}, u32[]{:S(2)}, u32[]{:S(2)}) %collective-permute-start.19) | collective-permute-done | bytes 294944 | tf_op jit(solution)/shard_map/ppermute | solution.py:435
  107.4 3.1 %output.1 = (bf16[64,1152]{1,0:T(8,128)(2,1)}, bf16[64,1152]{1,0:T(8,128)(2,1)}) custom-call(s32[4]{0:T(128)} %pad_add_fusion.pos_ref, s32[16]{0:T(128)} %bitcast.32, bf16[1,2,64,1152]{3,2,1,0:T(8,128)(2,1)} %copy-done.6, bf16[1,2,64,1152]{3,2,1,0:T(8,128)(2,1)} %copy-done.5, f32[2,64,1152]{2,1,0:T(8,128)} %get-tuple-element.77.refs_2_, ...), custom_call_target="tpu_custom_call" | custom-call | flops 1769472000 | bytes 2359296 | tf_op jit(solution)/shard_map/output/pallas_call | solution.py:555
  110.5 3.9 %collective-permute-start.20 = (bf16[64,1152]{1,0:T(8,128)(2,1)}, bf16[64,1152]{1,0:T(8,128)(2,1)S(1)}, u32[]{:S(2)}, u32[]{:S(2)}) collective-permute-start(bf16[64,1152]{1,0:T(8,128)(2,1)} %get-tuple-element.81), channel_id=1, source_target_pairs={{0,0},{1,1},{16,2},{17,3},{8,4},{9,5},{24,6},{25,7},{20,8},{21,9},... | collective-permute-start | bytes 442376 | tf_op jit(solution)/shard_map/ppermute | solution.py:439
  114.5 0.1 collective-permute-start.21
  114.6 2.8 %collective-permute-start.27 = (f32[48,864]{1,0:T(8,128)S(1)}, f32[48,864]{1,0:T(8,128)S(1)}, u32[]{:S(2)}, u32[]{:S(2)}) collective-permute-start(f32[48,864]{1,0:T(8,128)S(1)} %fusion), channel_id=1, source_target_pairs={{0,0},{1,1},{2,8},{3,9},{4,16},{5,17},{6,24},{7,25},{8,4},{9,5},{1... | collective-permute-start | bytes 497672 | tf_op jit(solution)/shard_map/ppermute | solution.py:571
  117.4 0.7 copy-done.22
  118.1 0.7 copy-done.23
  118.9 3.4 %input_grad.1 = (bf16[64,1152]{1,0:T(8,128)(2,1)}, bf16[64,1152]{1,0:T(8,128)(2,1)}) custom-call(s32[4]{0:T(128)} %pad_add_fusion.pos_ref, s32[16]{0:T(128)} %bitcast.33, bf16[1,2,64,1152]{3,2,1,0:T(8,128)(2,1)} %copy-done.6, bf16[1,2,64,1152]{3,2,1,0:T(8,128)(2,1)} %copy-done.5, f32[2,64,1152]{2,1,0:T(8,128)} %get-tuple-element.83.refs_2_, ...), custom_call_target="tpu_custom_call" | custom-call | flops 1769472000 | bytes 2359296 | tf_op jit(solution)/shard_map/input_grad/pallas_call | solution.py:579
  122.3 1.9 %collective-permute-start.24 = (bf16[64,1152]{1,0:T(8,128)(2,1)}, bf16[64,1152]{1,0:T(8,128)(2,1)S(1)}, u32[]{:S(2)}, u32[]{:S(2)}) collective-permute-start(bf16[64,1152]{1,0:T(8,128)(2,1)} %get-tuple-element.86), channel_id=1, source_target_pairs={{0,0},{1,1},{16,2},{17,3},{8,4},{9,5},{24,6},{25,7},{20,8},{21,9},... | collective-permute-start | bytes 442376 | tf_op jit(solution)/shard_map/ppermute | solution.py:439
  124.2 5.1 %collective-permute-start.25 = (bf16[64,1152]{1,0:T(8,128)(2,1)}, bf16[64,1152]{1,0:T(8,128)(2,1)S(1)}, u32[]{:S(2)}, u32[]{:S(2)}) collective-permute-start(bf16[64,1152]{1,0:T(8,128)(2,1)} %get-tuple-element.87), channel_id=1, source_target_pairs={{8,0},{9,1},{24,2},{25,3},{0,4},{1,5},{16,6},{17,7},{28,8},{29,9},... | collective-permute-start | bytes 442376 | tf_op jit(solution)/shard_map/ppermute | solution.py:439
  129.3 0.7 maximum_bitcast_fusion
  130.0 1.5 %collective-permute-done.24 = bf16[64,1152]{1,0:T(8,128)(2,1)S(1)} collective-permute-done((bf16[64,1152]{1,0:T(8,128)(2,1)}, bf16[64,1152]{1,0:T(8,128)(2,1)S(1)}, u32[]{:S(2)}, u32[]{:S(2)}) %collective-permute-start.24) | collective-permute-done | bytes 147488 | tf_op jit(solution)/shard_map/ppermute | solution.py:439
  131.5 2.3 %collective-permute-done.25 = bf16[64,1152]{1,0:T(8,128)(2,1)S(1)} collective-permute-done((bf16[64,1152]{1,0:T(8,128)(2,1)}, bf16[64,1152]{1,0:T(8,128)(2,1)S(1)}, u32[]{:S(2)}, u32[]{:S(2)}) %collective-permute-start.25) | collective-permute-done | bytes 147488 | tf_op jit(solution)/shard_map/ppermute | solution.py:439
  133.9 0.7 maximum_bitcast_fusion.1
  134.6 0.1 fusion.1
  134.7 0.7 maximum_multiply_fusion
  (68 shorter events, 0.4 us)
Async XLA Ops:
  1.4 9.8 %collective-permute-start = (s32[1,16]{1,0:T(1,128)S(1)}, s32[1,16]{1,0:T(1,128)S(1)}, u32[]{:S(2)}, u32[]{:S(2)}) collective-permute-start(s32[1,16]{1,0:T(1,128)S(1)} %add_bitcast_fusion), channel_id=1, source_target_pairs={{0,0},{1,1},{2,16},{3,17},{4,8},{5,9},{6,24},{7,25},{8,20},{9,21},... | collective-permute-start | bytes 200 | tf_op jit(solution)/shard_map/ppermute | solution.py:445
  5.5 4.5 %copy-start.3 = (bf16[1,128,1152]{2,1,0:T(8,128)(2,1)S(1)}, bf16[1,128,1152]{2,1,0:T(8,128)(2,1)}, u32[]{:S(2)}) copy-start(bf16[1,128,1152]{2,1,0:T(8,128)(2,1)} %param.9) | copy-start | bytes 884740
  5.5 4.5 %copy-start.4 = (bf16[1,128,1152]{2,1,0:T(8,128)(2,1)S(1)}, bf16[1,128,1152]{2,1,0:T(8,128)(2,1)}, u32[]{:S(2)}) copy-start(bf16[1,128,1152]{2,1,0:T(8,128)(2,1)} %param.8) | copy-start | bytes 884740
  8.5 8.1 %collective-permute-start.3 = (bf16[144,432]{1,0:T(8,128)(2,1)}, bf16[144,432]{1,0:T(8,128)(2,1)S(1)}, u32[]{:S(2)}, u32[]{:S(2)}) collective-permute-start(bf16[144,432]{1,0:T(8,128)(2,1)} %get-tuple-element.50), channel_id=1, source_target_pairs={{0,1},{1,0},{2,3},{3,2},{4,5},{5,4},{6,7},{7,6},{8,9},{9,8},{10,11... | collective-permute-start | bytes 373256 | tf_op jit(solution)/shard_map/ppermute | solution.py:469
  10.0 6.6 %copy-start.7 = (bf16[144,432]{1,0:T(8,128)(2,1)S(1)}, bf16[144,432]{1,0:T(8,128)(2,1)}, u32[]{:S(2)}) copy-start(bf16[144,432]{1,0:T(8,128)(2,1)} %get-tuple-element.49) | copy-start | bytes 373252
  10.1 12.8 %collective-permute-start.2 = (bf16[1,2,64,1152]{3,2,1,0:T(8,128)(2,1)S(1)}, bf16[1,2,64,1152]{3,2,1,0:T(8,128)(2,1)S(1)}, u32[]{:S(2)}, u32[]{:S(2)}) collective-permute-start(bf16[1,2,64,1152]{3,2,1,0:T(8,128)(2,1)S(1)} %pad_maximum_fusion.4), channel_id=1, source_target_pairs={{0,8},{1,9},{2,24},{3,25},{4,0},{5,1},{6,16},{7,17},{8,28},{9,29},... | collective-permute-start | bytes 884744 | tf_op jit(solution)/shard_map/ppermute | solution.py:454
  11.2 26.5 %copy-start.24 = (s32[1,16]{1,0:T(1,128)}, s32[1,16]{1,0:T(1,128)S(1)}, u32[]{:S(2)}) copy-start(s32[1,16]{1,0:T(1,128)S(1)} %collective-permute-done) | copy-start | bytes 196
  11.2 19.9 %collective-permute-start.1 = (bf16[1,2,64,1152]{3,2,1,0:T(8,128)(2,1)S(1)}, bf16[1,2,64,1152]{3,2,1,0:T(8,128)(2,1)S(1)}, u32[]{:S(2)}, u32[]{:S(2)}) collective-permute-start(bf16[1,2,64,1152]{3,2,1,0:T(8,128)(2,1)S(1)} %pad_maximum_fusion.3), channel_id=1, source_target_pairs={{0,0},{1,1},{2,16},{3,17},{4,8},{5,9},{6,24},{7,25},{8,20},{9,21},... | collective-permute-start | bytes 884744 | tf_op jit(solution)/shard_map/ppermute | solution.py:454
  16.7 20.8 %collective-permute-start.4 = (bf16[1,144,864]{2,1,0:T(8,128)(2,1)S(1)}, bf16[1,144,864]{2,1,0:T(8,128)(2,1)S(1)}, u32[]{:S(2)}, u32[]{:S(2)}) collective-permute-start(bf16[1,144,864]{2,1,0:T(8,128)(2,1)S(1)} %maximum_bitcast_fusion.2), channel_id=1, source_target_pairs={{0,4},{1,5},{2,6},{3,7},{4,0},{5,1},{6,2},{7,3},{8,12},{9,13},{10,... | collective-permute-start | bytes 746504 | tf_op jit(solution)/shard_map/ppermute | solution.py:430
  22.8 15.1 %copy-start.5 = (bf16[1,2,64,1152]{3,2,1,0:T(8,128)(2,1)}, bf16[1,2,64,1152]{3,2,1,0:T(8,128)(2,1)S(1)}, u32[]{:S(2)}) copy-start(bf16[1,2,64,1152]{3,2,1,0:T(8,128)(2,1)S(1)} %collective-permute-done.2.refs_1_) | copy-start | bytes 884740
  22.8 14.8 %collective-permute-start.6 = (bf16[1,2,64,1152]{3,2,1,0:T(8,128)(2,1)S(1)}, bf16[1,2,64,1152]{3,2,1,0:T(8,128)(2,1)S(1)}, u32[]{:S(2)}, u32[]{:S(2)}) collective-permute-start(bf16[1,2,64,1152]{3,2,1,0:T(8,128)(2,1)S(1)} %collective-permute-done.2.refs_1_), channel_id=1, source_target_pairs={{0,16},{1,17},{2,18},{3,19},{4,20},{5,21},{6,22},{7,23},{8,24},{9,... | collective-permute-start | bytes 884744 | tf_op jit(solution)/shard_map/ppermute | solution.py:430
  31.1 6.8 %copy-start.6 = (bf16[1,2,64,1152]{3,2,1,0:T(8,128)(2,1)}, bf16[1,2,64,1152]{3,2,1,0:T(8,128)(2,1)S(1)}, u32[]{:S(2)}) copy-start(bf16[1,2,64,1152]{3,2,1,0:T(8,128)(2,1)S(1)} %collective-permute-done.1.refs_0_) | copy-start | bytes 884740
  31.1 6.7 %collective-permute-start.5 = (bf16[1,2,64,1152]{3,2,1,0:T(8,128)(2,1)S(1)}, bf16[1,2,64,1152]{3,2,1,0:T(8,128)(2,1)S(1)}, u32[]{:S(2)}, u32[]{:S(2)}) collective-permute-start(bf16[1,2,64,1152]{3,2,1,0:T(8,128)(2,1)S(1)} %collective-permute-done.1.refs_0_), channel_id=1, source_target_pairs={{0,1},{1,0},{2,3},{3,2},{4,5},{5,4},{6,7},{7,6},{8,9},{9,8},{10,11... | collective-permute-start | bytes 884744 | tf_op jit(solution)/shard_map/ppermute | solution.py:430
  37.6 20.2 %copy-start.2 = (bf16[2,144,864]{2,1,0:T(8,128)(2,1)}, bf16[2,144,864]{2,1,0:T(8,128)(2,1)S(1)}, u32[]{:S(2)}) copy-start(bf16[2,144,864]{2,1,0:T(8,128)(2,1)S(1)} %pad_maximum_fusion.2.refs_0_) | copy-start | bytes 1492996
  37.6 16.9 %copy-start.13 = (bf16[144,1152]{1,0:T(8,128)(2,1)S(1)}, bf16[144,1152]{1,0:T(8,128)(2,1)}, u32[]{:S(2)}) copy-start(bf16[144,1152]{1,0:T(8,128)(2,1)} %param.15) | copy-start | bytes 995332
  37.7 20.7 %copy-start = (bf16[2,2,64,1152]{3,2,1,0:T(8,128)(2,1)}, bf16[2,2,64,1152]{3,2,1,0:T(8,128)(2,1)S(1)}, u32[]{:S(2)}) copy-start(bf16[2,2,64,1152]{3,2,1,0:T(8,128)(2,1)S(1)} %pad_maximum_fusion.1.refs_2_) | copy-start | bytes 1769476
  37.9 20.5 %copy-start.1 = (bf16[2,2,64,1152]{3,2,1,0:T(8,128)(2,1)}, bf16[2,2,64,1152]{3,2,1,0:T(8,128)(2,1)S(1)}, u32[]{:S(2)}) copy-start(bf16[2,2,64,1152]{3,2,1,0:T(8,128)(2,1)S(1)} %pad_maximum_fusion.refs_0_) | copy-start | bytes 1769476
  38.0 16.5 %collective-permute-start.7 = (bf16[2,144,864]{2,1,0:T(8,128)(2,1)S(1)}, bf16[2,144,864]{2,1,0:T(8,128)(2,1)S(1)}, u32[]{:S(2)}, u32[]{:S(2)}) collective-permute-start(bf16[2,144,864]{2,1,0:T(8,128)(2,1)S(1)} %pad_maximum_fusion.2.refs_0_), channel_id=1, source_target_pairs={{0,2},{1,3},{2,0},{3,1},{4,6},{5,7},{6,4},{7,5},{8,10},{9,11},{10,... | collective-permute-start | bytes 1493000 | tf_op jit(solution)/shard_map/ppermute | solution.py:432
  42.4 16.0 %collective-permute-start.11 = (bf16[2,2,64,1152]{3,2,1,0:T(8,128)(2,1)S(1)}, bf16[2,2,64,1152]{3,2,1,0:T(8,128)(2,1)S(1)}, u32[]{:S(2)}, u32[]{:S(2)}) collective-permute-start(bf16[2,2,64,1152]{3,2,1,0:T(8,128)(2,1)S(1)} %pad_maximum_fusion.1.refs_2_), channel_id=1, source_target_pairs={{0,1},{1,0},{2,3},{3,2},{4,5},{5,4},{6,7},{7,6},{8,9},{9,8},{10,11... | collective-permute-start | bytes 1769480 | tf_op jit(solution)/shard_map/ppermute | solution.py:432
  43.0 15.4 %collective-permute-start.10 = (bf16[2,2,64,1152]{3,2,1,0:T(8,128)(2,1)S(1)}, bf16[2,2,64,1152]{3,2,1,0:T(8,128)(2,1)S(1)}, u32[]{:S(2)}, u32[]{:S(2)}) collective-permute-start(bf16[2,2,64,1152]{3,2,1,0:T(8,128)(2,1)S(1)} %pad_maximum_fusion.refs_0_), channel_id=1, source_target_pairs={{0,16},{1,17},{2,18},{3,19},{4,20},{5,21},{6,22},{7,23},{8,24},{9,... | collective-permute-start | bytes 1769480 | tf_op jit(solution)/shard_map/ppermute | solution.py:432
  54.5 14.5 %copy-start.10 = (bf16[2,144,864]{2,1,0:T(8,128)(2,1)}, bf16[2,144,864]{2,1,0:T(8,128)(2,1)S(1)}, u32[]{:S(2)}) copy-start(bf16[2,144,864]{2,1,0:T(8,128)(2,1)S(1)} %collective-permute-done.7.refs_1_) | copy-start | bytes 1492996
  54.5 11.5 %collective-permute-start.12 = (bf16[144,1152]{1,0:T(8,128)(2,1)S(1)}, bf16[144,1152]{1,0:T(8,128)(2,1)S(1)}, u32[]{:S(2)}, u32[]{:S(2)}) collective-permute-start(bf16[144,1152]{1,0:T(8,128)(2,1)S(1)} %copy-done.13), channel_id=1, source_target_pairs={{0,0},{1,1},{2,18},{3,19},{4,8},{5,9},{6,26},{7,27},{8,4},{9,5},{1... | collective-permute-start | bytes 995336 | tf_op jit(solution)/shard_map/ppermute | solution.py:482
  57.8 9.9 %collective-permute-start.8 = (bf16[2,144,864]{2,1,0:T(8,128)(2,1)S(1)}, bf16[2,144,864]{2,1,0:T(8,128)(2,1)S(1)}, u32[]{:S(2)}, u32[]{:S(2)}) collective-permute-start(bf16[2,144,864]{2,1,0:T(8,128)(2,1)S(1)} %pad_maximum_fusion.2.refs_0_), channel_id=1, source_target_pairs={{0,8},{1,9},{2,10},{3,11},{4,12},{5,13},{6,14},{7,15},{8,0},{9,1},... | collective-permute-start | bytes 1493000 | tf_op jit(solution)/shard_map/ppermute | solution.py:479
  57.9 9.8 %collective-permute-start.9 = (bf16[2,144,864]{2,1,0:T(8,128)(2,1)S(1)}, bf16[2,144,864]{2,1,0:T(8,128)(2,1)S(1)}, u32[]{:S(2)}, u32[]{:S(2)}) collective-permute-start(bf16[2,144,864]{2,1,0:T(8,128)(2,1)S(1)} %collective-permute-done.7.refs_1_), channel_id=1, source_target_pairs={{0,8},{1,9},{2,10},{3,11},{4,12},{5,13},{6,14},{7,15},{8,0},{9,1},... | collective-permute-start | bytes 1493000 | tf_op jit(solution)/shard_map/ppermute | solution.py:479
  58.4 0.8 copy-start.8
  59.3 0.8 copy-start.9
  66.0 3.0 %copy-start.14 = (bf16[144,1152]{1,0:T(8,128)(2,1)}, bf16[144,1152]{1,0:T(8,128)(2,1)S(1)}, u32[]{:S(2)}) copy-start(bf16[144,1152]{1,0:T(8,128)(2,1)S(1)} %collective-permute-done.12.refs_4_) | copy-start | bytes 995332
  66.0 3.0 %collective-permute-start.13 = (bf16[144,1152]{1,0:T(8,128)(2,1)S(1)}, bf16[144,1152]{1,0:T(8,128)(2,1)S(1)}, u32[]{:S(2)}, u32[]{:S(2)}) collective-permute-start(bf16[144,1152]{1,0:T(8,128)(2,1)S(1)} %collective-permute-done.12.refs_4_), channel_id=1, source_target_pairs={{0,8},{1,9},{2,10},{3,11},{4,12},{5,13},{6,14},{7,15},{8,0},{9,1},... | collective-permute-start | bytes 995336 | tf_op jit(solution)/shard_map/ppermute | solution.py:511
  67.8 1.3 copy-start.11
  67.8 1.3 copy-start.12
  69.0 0.7 copy-start.15
  81.0 3.9 %collective-permute-start.14 = (f32[4,48,864]{2,1,0:T(8,128)}, f32[4,48,864]{2,1,0:T(8,128)S(1)}, u32[]{:S(2)}, u32[]{:S(2)}) collective-permute-start(f32[4,48,864]{2,1,0:T(8,128)} %get-tuple-element.61), channel_id=1, source_target_pairs={{0,8},{1,9},{2,10},{3,11},{4,12},{5,13},{6,14},{7,15},{8,0},{9,1},... | collective-permute-start | bytes 1990664 | tf_op jit(solution)/shard_map/ppermute | solution.py:533
  81.4 15.5 %collective-permute-start.16 = (bf16[2,64,1152]{2,1,0:T(8,128)(2,1)}, bf16[2,64,1152]{2,1,0:T(8,128)(2,1)S(1)}, u32[]{:S(2)}, u32[]{:S(2)}) collective-permute-start(bf16[2,64,1152]{2,1,0:T(8,128)(2,1)} %get-tuple-element.69), channel_id=1, source_target_pairs={{0,1},{1,0},{2,3},{3,2},{4,5},{5,4},{6,7},{7,6},{8,9},{9,8},{10,11... | collective-permute-start | bytes 884744 | tf_op jit(solution)/shard_map/ppermute | solution.py:435
  81.9 15.3 %collective-permute-start.17 = (bf16[2,64,1152]{2,1,0:T(8,128)(2,1)}, bf16[2,64,1152]{2,1,0:T(8,128)(2,1)S(1)}, u32[]{:S(2)}, u32[]{:S(2)}) collective-permute-start(bf16[2,64,1152]{2,1,0:T(8,128)(2,1)} %get-tuple-element.70), channel_id=1, source_target_pairs={{0,16},{1,17},{2,18},{3,19},{4,20},{5,21},{6,22},{7,23},{8,24},{9,... | collective-permute-start | bytes 884744 | tf_op jit(solution)/shard_map/ppermute | solution.py:435
  81.9 15.3 %collective-permute-start.18 = (bf16[2,64,1152]{2,1,0:T(8,128)(2,1)}, bf16[2,64,1152]{2,1,0:T(8,128)(2,1)S(1)}, u32[]{:S(2)}, u32[]{:S(2)}) collective-permute-start(bf16[2,64,1152]{2,1,0:T(8,128)(2,1)} %get-tuple-element.71), channel_id=1, source_target_pairs={{0,17},{1,16},{2,19},{3,18},{4,21},{5,20},{6,23},{7,22},{8,25},{9,... | collective-permute-start | bytes 884744 | tf_op jit(solution)/shard_map/ppermute | solution.py:435
  86.0 11.2 %collective-permute-start.15 = (f32[2,48,864]{2,1,0:T(8,128)S(1)}, f32[2,48,864]{2,1,0:T(8,128)S(1)}, u32[]{:S(2)}, u32[]{:S(2)}) collective-permute-start(f32[2,48,864]{2,1,0:T(8,128)S(1)} %get-tuple-element.67), channel_id=1, source_target_pairs={{0,2},{1,3},{2,0},{3,1},{4,6},{5,7},{6,4},{7,5},{8,10},{9,11},{10,... | collective-permute-start | bytes 995336 | tf_op jit(solution)/shard_map/ppermute | solution.py:539
  96.8 2.4 %copy-start.18 = (bf16[2,64,1152]{2,1,0:T(8,128)(2,1)S(1)}, bf16[2,64,1152]{2,1,0:T(8,128)(2,1)}, u32[]{:S(2)}) copy-start(bf16[2,64,1152]{2,1,0:T(8,128)(2,1)} %get-tuple-element.84) | copy-start | bytes 884740
  96.8 2.7 %copy-start.16 = (bf16[2,64,1152]{2,1,0:T(8,128)(2,1)S(1)}, bf16[2,64,1152]{2,1,0:T(8,128)(2,1)}, u32[]{:S(2)}) copy-start(bf16[2,64,1152]{2,1,0:T(8,128)(2,1)} %get-tuple-element.85) | copy-start | bytes 884740
  96.8 10.6 %copy-start.17 = (bf16[2,64,1152]{2,1,0:T(8,128)(2,1)}, bf16[2,64,1152]{2,1,0:T(8,128)(2,1)S(1)}, u32[]{:S(2)}) copy-start(bf16[2,64,1152]{2,1,0:T(8,128)(2,1)S(1)} %collective-permute-done.16.refs_3_) | copy-start | bytes 884740
  97.2 10.2 %copy-start.19 = (bf16[2,64,1152]{2,1,0:T(8,128)(2,1)}, bf16[2,64,1152]{2,1,0:T(8,128)(2,1)S(1)}, u32[]{:S(2)}) copy-start(bf16[2,64,1152]{2,1,0:T(8,128)(2,1)S(1)} %collective-permute-done.17.refs_4_) | copy-start | bytes 884740
  97.2 10.2 %copy-start.20 = (bf16[2,64,1152]{2,1,0:T(8,128)(2,1)}, bf16[2,64,1152]{2,1,0:T(8,128)(2,1)S(1)}, u32[]{:S(2)}) copy-start(bf16[2,64,1152]{2,1,0:T(8,128)(2,1)S(1)} %collective-permute-done.18.refs_5_) | copy-start | bytes 884740
  97.2 10.2 %collective-permute-start.19 = (bf16[2,64,1152]{2,1,0:T(8,128)(2,1)}, bf16[2,64,1152]{2,1,0:T(8,128)(2,1)S(1)}, u32[]{:S(2)}, u32[]{:S(2)}) collective-permute-start(bf16[2,64,1152]{2,1,0:T(8,128)(2,1)} %get-tuple-element.76), channel_id=1, source_target_pairs={{0,1},{1,0},{2,3},{3,2},{4,5},{5,4},{6,7},{7,6},{8,9},{9,8},{10,11... | collective-permute-start | bytes 884744 | tf_op jit(solution)/shard_map/ppermute | solution.py:435
  98.8 15.7 %collective-permute-start.26 = (f32[1,48,864]{2,1,0:T(8,128)S(1)}, f32[1,48,864]{2,1,0:T(8,128)S(1)}, u32[]{:S(2)}, u32[]{:S(2)}) collective-permute-start(f32[1,48,864]{2,1,0:T(8,128)S(1)} %slice.39), channel_id=1, source_target_pairs={{0,4},{1,5},{2,6},{3,7},{4,0},{5,1},{6,2},{7,3},{8,12},{9,13},{10,... | collective-permute-start | bytes 497672 | tf_op jit(solution)/shard_map/ppermute | solution.py:568
  99.3 18.1 %collective-permute-start.22 = (bf16[2,64,1152]{2,1,0:T(8,128)(2,1)S(1)}, bf16[2,64,1152]{2,1,0:T(8,128)(2,1)S(1)}, u32[]{:S(2)}, u32[]{:S(2)}) collective-permute-start(bf16[2,64,1152]{2,1,0:T(8,128)(2,1)S(1)} %copy-done.18), channel_id=1, source_target_pairs={{0,16},{1,17},{2,18},{3,19},{4,20},{5,21},{6,22},{7,23},{8,24},{9,... | collective-permute-start | bytes 884744 | tf_op jit(solution)/shard_map/ppermute | solution.py:435
  99.5 17.9 %collective-permute-start.23 = (bf16[2,64,1152]{2,1,0:T(8,128)(2,1)S(1)}, bf16[2,64,1152]{2,1,0:T(8,128)(2,1)S(1)}, u32[]{:S(2)}, u32[]{:S(2)}) collective-permute-start(bf16[2,64,1152]{2,1,0:T(8,128)(2,1)S(1)} %copy-done.16), channel_id=1, source_target_pairs={{0,17},{1,16},{2,19},{3,18},{4,21},{5,20},{6,23},{7,22},{8,25},{9,... | collective-permute-start | bytes 884744 | tf_op jit(solution)/shard_map/ppermute | solution.py:435
  107.4 3.1 %copy-start.21 = (bf16[2,64,1152]{2,1,0:T(8,128)(2,1)}, bf16[2,64,1152]{2,1,0:T(8,128)(2,1)S(1)}, u32[]{:S(2)}) copy-start(bf16[2,64,1152]{2,1,0:T(8,128)(2,1)S(1)} %collective-permute-done.19.refs_3_) | copy-start | bytes 884740
  110.5 18.7 %collective-permute-start.20 = (bf16[64,1152]{1,0:T(8,128)(2,1)}, bf16[64,1152]{1,0:T(8,128)(2,1)S(1)}, u32[]{:S(2)}, u32[]{:S(2)}) collective-permute-start(bf16[64,1152]{1,0:T(8,128)(2,1)} %get-tuple-element.81), channel_id=1, source_target_pairs={{0,0},{1,1},{16,2},{17,3},{8,4},{9,5},{24,6},{25,7},{20,8},{21,9},... | collective-permute-start | bytes 442376 | tf_op jit(solution)/shard_map/ppermute | solution.py:439
  114.5 14.8 %collective-permute-start.21 = (bf16[64,1152]{1,0:T(8,128)(2,1)}, bf16[64,1152]{1,0:T(8,128)(2,1)S(1)}, u32[]{:S(2)}, u32[]{:S(2)}) collective-permute-start(bf16[64,1152]{1,0:T(8,128)(2,1)} %get-tuple-element.82), channel_id=1, source_target_pairs={{8,0},{9,1},{24,2},{25,3},{0,4},{1,5},{16,6},{17,7},{28,8},{29,9},... | collective-permute-start | bytes 442376 | tf_op jit(solution)/shard_map/ppermute | solution.py:439
  114.6 20.0 %collective-permute-start.27 = (f32[48,864]{1,0:T(8,128)S(1)}, f32[48,864]{1,0:T(8,128)S(1)}, u32[]{:S(2)}, u32[]{:S(2)}) collective-permute-start(f32[48,864]{1,0:T(8,128)S(1)} %fusion), channel_id=1, source_target_pairs={{0,0},{1,1},{2,8},{3,9},{4,16},{5,17},{6,24},{7,25},{8,4},{9,5},{1... | collective-permute-start | bytes 497672 | tf_op jit(solution)/shard_map/ppermute | solution.py:571
  117.4 0.7 copy-start.22
  118.1 0.7 copy-start.23
  122.3 9.2 %collective-permute-start.24 = (bf16[64,1152]{1,0:T(8,128)(2,1)}, bf16[64,1152]{1,0:T(8,128)(2,1)S(1)}, u32[]{:S(2)}, u32[]{:S(2)}) collective-permute-start(bf16[64,1152]{1,0:T(8,128)(2,1)} %get-tuple-element.86), channel_id=1, source_target_pairs={{0,0},{1,1},{16,2},{17,3},{8,4},{9,5},{24,6},{25,7},{20,8},{21,9},... | collective-permute-start | bytes 442376 | tf_op jit(solution)/shard_map/ppermute | solution.py:439
  124.2 9.7 %collective-permute-start.25 = (bf16[64,1152]{1,0:T(8,128)(2,1)}, bf16[64,1152]{1,0:T(8,128)(2,1)S(1)}, u32[]{:S(2)}, u32[]{:S(2)}) collective-permute-start(bf16[64,1152]{1,0:T(8,128)(2,1)} %get-tuple-element.87), channel_id=1, source_target_pairs={{8,0},{9,1},{24,2},{25,3},{0,4},{1,5},{16,6},{17,7},{28,8},{29,9},... | collective-permute-start | bytes 442376 | tf_op jit(solution)/shard_map/ppermute | solution.py:439

commit v7 on v6

--- a/solution.py
+++ b/solution.py
@@ -164,7 +164,13 @@
     return part.reshape(part.shape[0] * BLOCK, part.shape[2])
 
 
-def pick_kernel(lay, cols, pos_ref, w_ref, *out_refs):
+def start_kernel(lay, cols, pos_ref, x_ref, g_ref, w_ref, *refs):
+    pair_refs, out_refs = refs[: lay.nc], refs[lay.nc :]
+    half = x_ref.shape[1] // lay.nc
+    for k, ref in enumerate(pair_refs):
+        first = pl.multiple_of(((pos_ref[2] // lay.ny) ^ k) * half, 16)
+        ref[0, 0] = x_ref[0, pl.ds(first, half), :]
+        ref[0, 1] = g_ref[0, pl.ds(first, half), :]
     model = w_ref.shape[1] // 3
     for k, out_ref in enumerate(out_refs):
         chip_x = pos_ref[3] ^ k
@@ -184,15 +190,14 @@
 
 
 def fill_weights(lay, pos_ref, w_refs, w_scr):
-    order = lay.doubled(lay.bits(lay.nz)[::-1])
     block = w_scr.shape[1] // lay.nz
-    rows, width = w_refs[0].shape[1], w_scr.shape[2]
+    rows, width = w_refs[0].shape[0], w_scr.shape[2]
     for h in range(lay.halves):
-        for n, k in enumerate(order):
-            ref, place = w_refs[2 * h + (2 * n) // lay.nz], n % (lay.nz // 2)
+        for k in range(lay.nz):
+            ref = w_refs[h * lay.nz + k]
             for m in range(block // rows):
                 start = pl.multiple_of((pos_ref[2] ^ k) * block + m * rows, 16)
-                w_scr[h, pl.ds(start, rows), :] = ref[place, :, m * width : (m + 1) * width]
+                w_scr[h, pl.ds(start, rows), :] = ref[:, m * width : (m + 1) * width]
 
 
 def heads_stacked(lay, values):
@@ -230,7 +235,7 @@
 
 
 def forward_kernel(lay, pos_ref, info_ref, hid_ref, gp_ref, *refs):
-    w_refs, refs = refs[: 2 * lay.halves], refs[2 * lay.halves :]
+    w_refs, refs = refs[: lay.halves * lay.nz], refs[lay.halves * lay.nz :]
     wo_refs, refs = refs[: lay.nc], refs[lay.nc :]
     q_ref, k_ref, v_ref, ga_ref, kept_ref, sent_ref, *refs = refs
     pr_refs, (w_scr, att_scr, wo_scr, acc_scr, cut_scr) = refs[: lay.chips], refs[lay.chips :]
@@ -302,7 +307,7 @@
 
 
 def backward_kernel(lay, pos_ref, info_ref, *refs):
-    w_refs, refs = refs[: 2 * lay.halves], refs[2 * lay.halves :]
+    w_refs, refs = refs[: lay.halves * lay.nz], refs[lay.halves * lay.nz :]
     q_ref, k_ref, v_ref, ga_ref, *refs = refs
     gh_refs, (w_scr, gt_scr) = refs[: lay.chips], refs[lay.chips :]
     _, frames, step_patches, cols = q_ref.shape
@@ -425,7 +430,7 @@
         ky, kx = lay.chip_of(k)
         return lay.swap(ky=ky, kx=kx)
 
-    def doubling(held, bits, swap, after=()):
+    def doubling(held, bits, swap, after):
         for bit in bits[:-1]:
             held = jnp.concatenate([held, lax.ppermute(held, AXES, swap(bit))], axis=0)
         held, _ = lax.optimization_barrier((held, after))
@@ -442,29 +447,29 @@
         return jnp.concatenate([first, second], axis=0)[None]
 
     info = jnp.concatenate([clip_ids[0], clip_patches[0], clip_step[0]])[None]
-    info = lax.ppermute(info, AXES, lay.to_plane(0))[0]
+    by_core = jnp.concatenate([info, lax.ppermute(info, AXES, lay.swap(kc=1))], axis=0)
+    info = [by_core] + [
+        lax.ppermute(by_core, AXES, lay.swap(ky=ky)) for ky in range(1, lay.ny)
+    ]
+    group_y, group_c = z % lay.ny, z // lay.ny
+    info = sum(
+        jnp.where((y ^ ky == group_y) & (c ^ kc == group_c), info[ky][kc], 0)
+        for ky in range(lay.ny)
+        for kc in range(nc)
+    )
     pos = jnp.stack([y, c, z, x]).astype(jnp.int32)
-    own = []
-    for k in range(nc):
-        start = ((z // lay.ny) ^ k) * half
-        pair = [lax.dynamic_slice_in_dim(frame, start, half, axis=1) for frame in (frames_x, grad_y)]
-        pair = jnp.stack(pair, axis=1)
-        if k == 0:
-            pair, info = lax.optimization_barrier((pair, info))
-        own.append(lax.ppermute(pair, AXES, lay.to_plane(k)))
-    pairs = []
-    for j in range(nc):
-        pairs += doubling(own[j], lay.chip_bits(j), chip_swap)
-
-    picked = call(
-        functools.partial(pick_kernel, lay, cols),
-        "pick",
+    pair_shape = (1, 2, half, model)
+    outputs = call(
+        functools.partial(start_kernel, lay, cols),
+        "start",
         2 * model * 1000,
-        [whole_spec(w_qkv.shape)],
-        [whole_spec((rows, 3 * cols))] * nx,
-        [struct((rows, 3 * cols))] * nx,
+        [whole_spec(frames_x.shape)] * 2 + [whole_spec(w_qkv.shape)],
+        [whole_spec(pair_shape)] * nc + [whole_spec((rows, 3 * cols))] * nx,
+        [struct(pair_shape)] * nc + [struct((rows, 3 * cols))] * nx,
         prefetch=1,
-    )(pos, w_qkv)
+    )(pos, frames_x, grad_y, w_qkv)
+    pairs, picked = outputs[:nc], outputs[nc:]
+    own = [lax.ppermute(pair, AXES, lay.to_plane(k)) for k, pair in enumerate(pairs)]
     by_x = [picked[0]] + [
         lax.ppermute(picked[kx], AXES, lay.swap(kx=kx)) for kx in range(1, nx)
     ]
@@ -473,12 +478,27 @@
     else:
         stacked = jnp.stack(by_x)
         ordered = [lax.dynamic_index_in_dim(stacked, x ^ i, 0, keepdims=False) for i in range(nx)]
-    w_own = jnp.concatenate(ordered, axis=1 if rows % 16 == 0 else 0)[None]
-    w_pieces = doubling(w_own, lay.bits(lay.nz)[::-1], lambda kz: lay.swap(kz=kz), pairs[::2])
+    w_own = jnp.concatenate(ordered, axis=1 if rows % 16 == 0 else 0)
+    own[0], _ = lax.optimization_barrier((own[0], w_own))
+    w_pieces = {0: w_own}
+    for bit in lay.bits(lay.nz):
+        w_pieces[bit] = lax.ppermute(w_own, AXES, lay.swap(kz=bit))
+    early = [w_pieces[bit] for bit in lay.bits(lay.nz)]
+    for k in range(1, lay.nz):
+        if k not in w_pieces:
+            bit = k & -k
+            w_pieces[k] = lax.ppermute(w_pieces[k ^ bit], AXES, lay.swap(kz=bit))
+    w_pieces = [w_pieces[k] for k in range(lay.nz)]
+    late = w_pieces[-1]
     if halves > 1:
         w_pieces += [lax.ppermute(piece, AXES, lay.swap(kc=1)) for piece in w_pieces]
 
-    late_w_out, _ = lax.optimization_barrier((w_out, w_pieces[:2]))
+    pairs = []
+    for j in range(nc):
+        pairs += doubling(own[j], lay.chip_bits(j), chip_swap, early if j else info)
+    pairs, _ = lax.optimization_barrier((pairs, [late] + w_pieces[lay.nz : -1]))
+
+    late_w_out, _ = lax.optimization_barrier((w_out, own))
     wo_own = lax.ppermute(late_w_out, AXES, lay.rows_to_chip())
 
     def spread(count, width, patches_at_once):
@@ -550,8 +570,8 @@
     )(pos, info, *w_pieces, queries, keys, values, grad_attn)
     sums, first_away, projected = lax.optimization_barrier((sums, first_away, projected))
     grad_hidden = over_chips(sums)
+
     projected, _ = lax.optimization_barrier((projected, grad_hidden[1]))
-
     out_parts = call(
         functools.partial(output_kernel, lay),
         "output",
@@ -565,16 +585,8 @@
     cut = cut + first_away
     for bit in lay.bits(lay.nz)[1:]:
         middle = middle // 2
-        away = lax.ppermute(cut[middle:], AXES, lay.swap(kz=bit))
-        away, _ = lax.optimization_barrier((away, out_parts))
-        cut = cut[:middle] + away
-    grad_w = lax.ppermute(cut[0], AXES, lay.to_owner())
-    grad_w = jnp.concatenate(
-        [grad_w[:, m * quarter : (m + 1) * quarter] for m in range(fold)], axis=0
-    )
-    grad_w_out = grad_w * jnp.float32(1.0 / math.sqrt(groups * lay.frames * patches))
-
-    out_y = from_plane(out_parts)
+        cut = cut[:middle] + lax.ppermute(cut[middle:], AXES, lay.swap(kz=bit))
+
 
     grad_parts = call(
         functools.partial(input_grad_kernel, lay),
@@ -586,6 +598,15 @@
         grid=(few_steps,),
     )(pos, info, *own, *grad_hidden, mod_table)
     grad_x = from_plane(grad_parts)
+    out_parts, _ = lax.optimization_barrier((out_parts, grad_parts))
+    out_y = from_plane(out_parts)
+
+    cut, _ = lax.optimization_barrier((cut, grad_parts))
+    grad_w = lax.ppermute(cut[0], AXES, lay.to_owner())
+    grad_w = jnp.concatenate(
+        [grad_w[:, m * quarter : (m + 1) * quarter] for m in range(fold)], axis=0
+    )
+    grad_w_out = grad_w * jnp.float32(1.0 / math.sqrt(groups * lay.frames * patches))
     return out_y, grad_x, grad_w_out
 
 

time: 138 us -> 153 us (1.11)
  waiting for transfers between devices: 44.8 us -> 57.6 us
    ppermute x4 -> x8, waiting for transfers between devices: 14.3 us -> 30.1 us  [the longest x2 16.5 us: local(): lax.ppermute(pair, AXES, lay.to_plane(k))]
    ppermute x3 -> x2, waiting for transfers between devices: 11.5 us -> 4.45 us  [doubling(): return [held, lax.ppermute(held, AXES, swap(bits[-1]))]]
    ppermute x1, starting transfers between devices: 1.26 us -> 6.06 us  [local(): first_away = lax.ppermute(away, AXES, lay.swap(kz=1))]
    ppermute x1, waiting for transfers between devices: 0.01 us -> 4.41 us  [local(): grad_w = lax.ppermute(cut[0], AXES, lay.to_owner())]
    ppermute x6, waiting for transfers between devices: 6.43 us -> 10.1 us  [over_chips(): got = [lax.ppermute(parts[k], AXES, chip_swap(k)) for k in range(1, chips)]]
    ppermute x3 -> x2, waiting for transfers between devices: 5.98 us -> 2.92 us  [doubling(): held = jnp.concatenate([held, lax.ppermute(held, AXES, swap(bit))], axis=0)]
    ppermute x3 -> x2, starting transfers between devices: 5.05 us -> 2.06 us  [doubling(): return [held, lax.ppermute(held, AXES, swap(bits[-1]))]]
    ppermute x2 -> x4, waiting for transfers between devices: 0.01 us -> 2.42 us  [local(): lax.ppermute(piece, AXES, lay.swap(kc=1))]
  transfers between devices with their start and end apart: 28 -> 32, of which waited for: 11 -> 18; matrix products, arithmetic and copies ran while one was open for 3% -> 3% of each run, Pallas kernels for 17% -> 14%
where the time goes in v7:
time: 153 us; the launch traced here: 151 us
  waiting for transfers between devices  57.6 us (38%)
  starting transfers between devices  47 us (31%)
  Pallas kernels  35.7 us (23%)
  other arithmetic  5.99 us (4%)
  local copies, waits for them, and re-layouts  3.25 us (2%)
    ppermute x2, waiting for transfers between devices, local(): lax.ppermute(pair, AXES, lay.to_plane(k))  16.5 us
    ppermute x4, starting transfers between devices, from_plane(): lax.ppermute(part, AXES, lay.from_plane(k))  11.9 us
    pallas_call x1, Pallas kernels, local(): call(functools.partial(forward_kernel, lay), 'forward', 14 * model * 1000...  11.3 us
    ppermute x6, waiting for transfers between devices, over_chips(): got = [lax.ppermute(parts[k], AXES, chip_swap(k)) for k in range(1, chips)]  10.1 us
    pallas_call x1, Pallas kernels, local(): call(functools.partial(backward_kernel, lay), 'backward', 10 * model * 10...  9.72 us
    ppermute x2, waiting for transfers between devices, local(): w_pieces[bit] = lax.ppermute(w_own, AXES, lay.swap(kz=bit))  8.18 us
    ppermute x6, starting transfers between devices, over_chips(): got = [lax.ppermute(parts[k], AXES, chip_swap(k)) for k in range(1, chips)]  7.06 us
    ppermute x1, starting transfers between devices, local(): first_away = lax.ppermute(away, AXES, lay.swap(kz=1))  6.06 us
  transfers between devices with their start and end apart: 32, of which 18 were waited for; matrix products, arithmetic and copies ran while one was open for 3% of the time, Pallas kernels for 14%

profile of v7, /device:TPU:4, one launch (start us, length us, event | category | flops | bytes accessed | tf_op | source)
XLA Modules:
  0.0 150.6 jit_solution(14281893317736086113)
XLA Ops:
  0.6 0.7 pad_add_fusion.1.pos_ref
  1.3 3.4 %start.1 = (bf16[1,2,64,1152]{3,2,1,0:T(8,128)(2,1)}, bf16[1,2,64,1152]{3,2,1,0:T(8,128)(2,1)}, bf16[144,432]{1,0:T(8,128)(2,1)}, bf16[144,432]{1,0:T(8,128)(2,1)}) custom-call(s32[4]{0:T(128)} %pad_add_fusion.1.pos_ref, bf16[1,128,1152]{2,1,0:T(8,128)(2,1)} %x_ref.1, bf16[1,128,1152]{2,1,0:T(8,128)(2,1)} %g_ref.1, bf16[144,3456]{1,0:T(8,128)(2,1)} %w_ref.1), custom_call_target="tpu_custom_call" | custom-call | flops 1179648000 | bytes 2359296 | tf_op jit(solution)/shard_map/start/pallas_call | solution.py:462
  4.7 1.5 collective-permute-start.3
  6.3 3.4 %collective-permute-start.2 = (bf16[1,2,64,1152]{3,2,1,0:T(8,128)(2,1)}, bf16[1,2,64,1152]{3,2,1,0:T(8,128)(2,1)S(1)}, u32[]{:S(2)}, u32[]{:S(2)}) collective-permute-start(bf16[1,2,64,1152]{3,2,1,0:T(8,128)(2,1)} %get-tuple-element.55), channel_id=1, source_target_pairs={{0,0},{1,1},{2,16},{3,17},{4,8},{5,9},{6,24},{7,25},{8,20},{9,21},... | collective-permute-start | bytes 884744 | tf_op jit(solution)/shard_map/ppermute | solution.py:472
  9.7 1.4 collective-permute-start.4
  11.1 0.9 broadcast_select_fusion.1
  12.0 0.1 pad_maximum_fusion.2.refs_0_
  12.2 16.5 %collective-permute-done.2.refs_0_ = bf16[1,2,64,1152]{3,2,1,0:T(8,128)(2,1)S(1)} collective-permute-done((bf16[1,2,64,1152]{3,2,1,0:T(8,128)(2,1)}, bf16[1,2,64,1152]{3,2,1,0:T(8,128)(2,1)S(1)}, u32[]{:S(2)}, u32[]{:S(2)}) %collective-permute-start.2) | collective-permute-done | bytes 294944 | tf_op jit(solution)/shard_map/ppermute | solution.py:472
  28.7 0.1 collective-permute-start.12
  29.0 2.0 %collective-permute-start.14 = (bf16[1,2,64,1152]{3,2,1,0:T(8,128)(2,1)S(1)}, bf16[1,2,64,1152]{3,2,1,0:T(8,128)(2,1)S(1)}, u32[]{:S(2)}, u32[]{:S(2)}) collective-permute-start(bf16[1,2,64,1152]{3,2,1,0:T(8,128)(2,1)S(1)} %collective-permute-done.4.refs_1_), channel_id=1, source_target_pairs={{0,16},{1,17},{2,18},{3,19},{4,20},{5,21},{6,22},{7,23},{8,24},{9,... | collective-permute-start | bytes 884744 | tf_op jit(solution)/shard_map/ppermute | solution.py:435
  31.0 1.5 %collective-permute-done.1 = s32[2,16]{1,0:T(2,128)S(1)} collective-permute-done((s32[2,16]{1,0:T(2,128)S(1)}, s32[2,16]{1,0:T(2,128)S(1)}, u32[]{:S(2)}, u32[]{:S(2)}) %collective-permute-start.1) | collective-permute-done | bytes 160 | tf_op jit(solution)/shard_map/ppermute | solution.py:452
  32.5 0.6 fusion.2.info_ref
  33.1 2.2 %collective-permute-start.5 = (bf16[144,864]{1,0:T(8,128)(2,1)S(1)}, bf16[144,864]{1,0:T(8,128)(2,1)S(1)}, u32[]{:S(2)}, u32[]{:S(2)}) collective-permute-start(bf16[144,864]{1,0:T(8,128)(2,1)S(1)} %pad_maximum_fusion.2.refs_0_), channel_id=1, source_target_pairs={{0,2},{1,3},{2,0},{3,1},{4,6},{5,7},{6,4},{7,5},{8,10},{9,11},{10,... | collective-permute-start | bytes 746504 | tf_op jit(solution)/shard_map/ppermute | solution.py:485
  35.3 0.1 collective-permute-done.12
  35.5 2.8 %collective-permute-done.14 = bf16[1,2,64,1152]{3,2,1,0:T(8,128)(2,1)S(1)} collective-permute-done((bf16[1,2,64,1152]{3,2,1,0:T(8,128)(2,1)S(1)}, bf16[1,2,64,1152]{3,2,1,0:T(8,128)(2,1)S(1)}, u32[]{:S(2)}, u32[]{:S(2)}) %collective-permute-start.14) | collective-permute-done | bytes 294944 | tf_op jit(solution)/shard_map/ppermute | solution.py:435
  38.4 8.0 %collective-permute-done.6.refs_2_ = bf16[144,864]{1,0:T(8,128)(2,1)S(1)} collective-permute-done((bf16[144,864]{1,0:T(8,128)(2,1)S(1)}, bf16[144,864]{1,0:T(8,128)(2,1)S(1)}, u32[]{:S(2)}, u32[]{:S(2)}) %collective-permute-start.6) | collective-permute-done | bytes 248864 | tf_op jit(solution)/shard_map/ppermute | solution.py:485
  46.4 0.2 collective-permute-done.5.refs_1_
  46.6 0.7 collective-permute-start.15
  47.3 1.4 collective-permute-start.13
  48.7 0.5 collective-permute-start.10
  49.2 0.3 collective-permute-start.7
  49.5 0.7 collective-permute-done.8.refs_4_
  50.2 0.1 collective-permute-start.9
  50.3 0.2 collective-permute-done.10.refs_6_
  50.6 2.9 %collective-permute-start.16 = (bf16[144,1152]{1,0:T(8,128)(2,1)S(1)}, bf16[144,1152]{1,0:T(8,128)(2,1)S(1)}, u32[]{:S(2)}, u32[]{:S(2)}) collective-permute-start(bf16[144,1152]{1,0:T(8,128)(2,1)S(1)} %copy-done.10), channel_id=1, source_target_pairs={{0,0},{1,1},{2,18},{3,19},{4,8},{5,9},{6,26},{7,27},{8,4},{9,5},{1... | collective-permute-start | bytes 995336 | tf_op jit(solution)/shard_map/ppermute | solution.py:502
  53.4 3.9 %collective-permute-done.7.refs_3_ = bf16[144,864]{1,0:T(8,128)(2,1)S(1)} collective-permute-done((bf16[144,864]{1,0:T(8,128)(2,1)S(1)}, bf16[144,864]{1,0:T(8,128)(2,1)S(1)}, u32[]{:S(2)}, u32[]{:S(2)}) %collective-permute-start.7) | collective-permute-done | bytes 248864 | tf_op jit(solution)/shard_map/ppermute | solution.py:490
  57.3 4.4 %collective-permute-done.15.refs_3_ = bf16[2,2,64,1152]{3,2,1,0:T(8,128)(2,1)S(1)} collective-permute-done((bf16[2,2,64,1152]{3,2,1,0:T(8,128)(2,1)S(1)}, bf16[2,2,64,1152]{3,2,1,0:T(8,128)(2,1)S(1)}, u32[]{:S(2)}, u32[]{:S(2)}) %collective-permute-start.15) | collective-permute-done | bytes 589856 | tf_op jit(solution)/shard_map/ppermute | solution.py:437
  61.8 0.7 copy-done.8
  62.5 0.8 copy-done.9
  63.3 4.6 %prepare.1 = (bf16[8,64,1152]{2,1,0:T(8,128)(2,1)}, bf16[8,64,1152]{2,1,0:T(8,128)(2,1)}) custom-call(s32[4]{0:T(128)} %pad_add_fusion.1.pos_ref, s32[16]{0:T(128)} %fusion.2.info_ref, bf16[2,2,64,1152]{3,2,1,0:T(8,128)(2,1)} %copy-done, bf16[2,2,64,1152]{3,2,1,0:T(8,128)(2,1)} %copy-done.9, bf16[2,2,64,1152]{3,2,1,0:T(8,128)(2,1)} %copy-done.1, ...), custom_call_target="tpu_custom_call" | custom-call | flops 1769472000 | bytes 2359296 | tf_op jit(solution)/shard_map/prepare/pallas_call | solution.py:521
  68.0 0.5 collective-permute-start.11
  68.5 1.5 collective-permute-done.11.refs_7_
  70.1 0.6 copy-done.25
  70.7 0.1 copy-done.12
  70.8 11.3 %forward.1 = (bf16[2,8,64,144]{3,2,1,0:T(8,128)(2,1)}, bf16[2,8,64,144]{3,2,1,0:T(8,128)(2,1)}, bf16[2,8,64,144]{3,2,1,0:T(8,128)(2,1)}, bf16[2,8,64,144]{3,2,1,...) custom-call(s32[4]{0:T(128)} %pad_add_fusion.1.pos_ref, ...), custom_call_target="tpu_custom_call" | custom-call | flops 8257536000 | bytes 2359296 | tf_op jit(solution)/shard_map/forward/pallas_call | solution.py:535
  82.1 0.1 collective-permute-start.18
  82.3 0.9 collective-permute-start.20
  83.2 0.6 collective-permute-start.21
  83.8 2.0 %collective-permute-start.22 = (bf16[2,64,1152]{2,1,0:T(8,128)(2,1)}, bf16[2,64,1152]{2,1,0:T(8,128)(2,1)S(1)}, u32[]{:S(2)}, u32[]{:S(2)}) collective-permute-start(bf16[2,64,1152]{2,1,0:T(8,128)(2,1)} %get-tuple-element.85), channel_id=1, source_target_pairs={{0,17},{1,16},{2,19},{3,18},{4,21},{5,20},{6,23},{7,22},{8,25},{9,... | collective-permute-start | bytes 884744 | tf_op jit(solution)/shard_map/ppermute | solution.py:440
  85.8 1.2 slice_add_fusion
  87.0 6.1 %collective-permute-start.19 = (f32[2,48,864]{2,1,0:T(8,128)S(1)}, f32[2,48,864]{2,1,0:T(8,128)S(1)}, u32[]{:S(2)}, u32[]{:S(2)}) collective-permute-start(f32[2,48,864]{2,1,0:T(8,128)S(1)} %get-tuple-element.81), channel_id=1, source_target_pairs={{0,2},{1,3},{2,0},{3,1},{4,6},{5,7},{6,4},{7,5},{8,10},{9,11},{10,... | collective-permute-start | bytes 995336 | tf_op jit(solution)/shard_map/ppermute | solution.py:559
  93.0 9.7 %backward.1 = (f32[2,64,1152]{2,1,0:T(8,128)}, bf16[2,64,1152]{2,1,0:T(8,128)(2,1)}, bf16[2,64,1152]{2,1,0:T(8,128)(2,1)}, bf16[2,64,1152]{2,1,0:T(8,128)(2,1)}) custom-call(s32[4]{0:T(128)} %pad_add_fusion.1.pos_ref, s32[16]{0:T(128)} %fusion.2.info_ref, bf16[144,864]{1,0:T(8,128)(2,1)} %copy-done.4, bf16[144,864]{1,0:T(8,128)(2,1)} %copy-done.20, ...), custom_call_target="tpu_custom_call" | custom-call | flops 5898240000 | bytes 2359296 | tf_op jit(solution)/shard_map/backward/pallas_call | solution.py:561
  102.8 1.3 collective-permute-start.23
  104.1 2.0 %collective-permute-start.24 = (bf16[2,64,1152]{2,1,0:T(8,128)(2,1)}, bf16[2,64,1152]{2,1,0:T(8,128)(2,1)S(1)}, u32[]{:S(2)}, u32[]{:S(2)}) collective-permute-start(bf16[2,64,1152]{2,1,0:T(8,128)(2,1)} %get-tuple-element.98), channel_id=1, source_target_pairs={{0,16},{1,17},{2,18},{3,19},{4,20},{5,21},{6,22},{7,23},{8,24},{9,... | collective-permute-start | bytes 884744 | tf_op jit(solution)/shard_map/ppermute | solution.py:440
  106.1 0.3 collective-permute-start.25
  106.4 2.5 %collective-permute-start.30 = (f32[1,48,864]{2,1,0:T(8,128)S(1)}, f32[1,48,864]{2,1,0:T(8,128)S(1)}, u32[]{:S(2)}, u32[]{:S(2)}) collective-permute-start(f32[1,48,864]{2,1,0:T(8,128)S(1)} %slice.47), channel_id=1, source_target_pairs={{0,4},{1,5},{2,6},{3,7},{4,0},{5,1},{6,2},{7,3},{8,12},{9,13},{10,... | collective-permute-start | bytes 497672 | tf_op jit(solution)/shard_map/ppermute | solution.py:588
  108.9 4.1 %collective-permute-done.23.refs_3_ = bf16[2,64,1152]{2,1,0:T(8,128)(2,1)S(1)} collective-permute-done((bf16[2,64,1152]{2,1,0:T(8,128)(2,1)}, bf16[2,64,1152]{2,1,0:T(8,128)(2,1)S(1)}, u32[]{:S(2)}, u32[]{:S(2)}) %collective-permute-start.23) | collective-permute-done | bytes 294944 | tf_op jit(solution)/shard_map/ppermute | solution.py:440
  113.0 5.1 %collective-permute-done.24.refs_4_ = bf16[2,64,1152]{2,1,0:T(8,128)(2,1)S(1)} collective-permute-done((bf16[2,64,1152]{2,1,0:T(8,128)(2,1)}, bf16[2,64,1152]{2,1,0:T(8,128)(2,1)S(1)}, u32[]{:S(2)}, u32[]{:S(2)}) %collective-permute-start.24) | collective-permute-done | bytes 294944 | tf_op jit(solution)/shard_map/ppermute | solution.py:440
  118.1 0.9 collective-permute-done.25.refs_5_
  119.0 0.7 copy-done.18
  119.7 3.4 %input_grad.1 = (bf16[64,1152]{1,0:T(8,128)(2,1)}, bf16[64,1152]{1,0:T(8,128)(2,1)}) custom-call(s32[4]{0:T(128)} %pad_add_fusion.1.pos_ref, s32[16]{0:T(128)} %fusion.2.info_ref, bf16[1,2,64,1152]{3,2,1,0:T(8,128)(2,1)} %copy-done.2, bf16[1,2,64,1152]{3,2,1,0:T(8,128)(2,1)} %copy-done.3, f32[2,64,1152]{2,1,0:T(8,128)} %get-tuple-element.97.refs_2_, ...), custom_call_target="tpu_custom_call" | custom-call | flops 1769472000 | bytes 2359296 | tf_op jit(solution)/shard_map/input_grad/pallas_call | solution.py:591
  123.2 3.2 %output.1 = (bf16[64,1152]{1,0:T(8,128)(2,1)}, bf16[64,1152]{1,0:T(8,128)(2,1)}) custom-call(s32[4]{0:T(128)} %pad_add_fusion.1.pos_ref, s32[16]{0:T(128)} %fusion.2.info_ref, bf16[1,2,64,1152]{3,2,1,0:T(8,128)(2,1)} %copy-done.2, bf16[1,2,64,1152]{3,2,1,0:T(8,128)(2,1)} %copy-done.3, f32[2,64,1152]{2,1,0:T(8,128)} %get-tuple-element.91.refs_2_, ...), custom_call_target="tpu_custom_call" | custom-call | flops 1769472000 | bytes 2359296 | tf_op jit(solution)/shard_map/output/pallas_call | solution.py:575
  126.4 5.4 %collective-permute-start.26 = (bf16[64,1152]{1,0:T(8,128)(2,1)}, bf16[64,1152]{1,0:T(8,128)(2,1)S(1)}, u32[]{:S(2)}, u32[]{:S(2)}) collective-permute-start(bf16[64,1152]{1,0:T(8,128)(2,1)} %get-tuple-element.102), channel_id=1, source_target_pairs={{0,0},{1,1},{16,2},{17,3},{8,4},{9,5},{24,6},{25,7},{20,8},{21,9},... | collective-permute-start | bytes 442376 | tf_op jit(solution)/shard_map/ppermute | solution.py:444
  131.8 1.9 %collective-permute-start.27 = (bf16[64,1152]{1,0:T(8,128)(2,1)}, bf16[64,1152]{1,0:T(8,128)(2,1)S(1)}, u32[]{:S(2)}, u32[]{:S(2)}) collective-permute-start(bf16[64,1152]{1,0:T(8,128)(2,1)} %get-tuple-element.103), channel_id=1, source_target_pairs={{8,0},{9,1},{24,2},{25,3},{0,4},{1,5},{16,6},{17,7},{28,8},{29,9},... | collective-permute-start | bytes 442376 | tf_op jit(solution)/shard_map/ppermute | solution.py:444
  133.8 1.9 %collective-permute-start.28 = (bf16[64,1152]{1,0:T(8,128)(2,1)S(1)}, bf16[64,1152]{1,0:T(8,128)(2,1)S(1)}, u32[]{:S(2)}, u32[]{:S(2)}) collective-permute-start(bf16[64,1152]{1,0:T(8,128)(2,1)S(1)} %copy-done.27), channel_id=1, source_target_pairs={{0,0},{1,1},{16,2},{17,3},{8,4},{9,5},{24,6},{25,7},{20,8},{21,9},... | collective-permute-start | bytes 442376 | tf_op jit(solution)/shard_map/ppermute | solution.py:444
  135.7 2.7 %collective-permute-start.29 = (bf16[64,1152]{1,0:T(8,128)(2,1)S(1)}, bf16[64,1152]{1,0:T(8,128)(2,1)S(1)}, u32[]{:S(2)}, u32[]{:S(2)}) collective-permute-start(bf16[64,1152]{1,0:T(8,128)(2,1)S(1)} %copy-done.26), channel_id=1, source_target_pairs={{8,0},{9,1},{24,2},{25,3},{0,4},{1,5},{16,6},{17,7},{28,8},{29,9},... | collective-permute-start | bytes 442376 | tf_op jit(solution)/shard_map/ppermute | solution.py:444
  138.4 2.2 %collective-permute-start.31 = (f32[48,864]{1,0:T(8,128)S(1)}, f32[48,864]{1,0:T(8,128)S(1)}, u32[]{:S(2)}, u32[]{:S(2)}) collective-permute-start(f32[48,864]{1,0:T(8,128)S(1)} %bitcast.26), channel_id=1, source_target_pairs={{0,0},{1,1},{2,8},{3,9},{4,16},{5,17},{6,24},{7,25},{8,4},{9,5},{1... | collective-permute-start | bytes 497672 | tf_op jit(solution)/shard_map/ppermute | solution.py:605
  140.7 0.7 maximum_bitcast_fusion
  141.4 1.4 collective-permute-done.28
  142.8 1.8 %collective-permute-done.29 = bf16[64,1152]{1,0:T(8,128)(2,1)S(1)} collective-permute-done((bf16[64,1152]{1,0:T(8,128)(2,1)S(1)}, bf16[64,1152]{1,0:T(8,128)(2,1)S(1)}, u32[]{:S(2)}, u32[]{:S(2)}) %collective-permute-start.29) | collective-permute-done | bytes 147488 | tf_op jit(solution)/shard_map/ppermute | solution.py:444
  144.6 0.7 maximum_bitcast_fusion.1
  145.4 4.4 %collective-permute-done.31 = f32[48,864]{1,0:T(8,128)S(1)} collective-permute-done((f32[48,864]{1,0:T(8,128)S(1)}, f32[48,864]{1,0:T(8,128)S(1)}, u32[]{:S(2)}, u32[]{:S(2)}) %collective-permute-start.31) | collective-permute-done | bytes 165920 | tf_op jit(solution)/shard_map/ppermute | solution.py:605
  149.8 0.1 fusion.6
  149.9 0.7 maximum_multiply_fusion
  (80 shorter events, 0.7 us)
Async XLA Ops:
  1.3 4.9 %copy-start.5 = (s32[1,4]{1,0:T(1,128)S(1)}, s32[1,4]{1,0:T(1,128)}, u32[]{:S(2)}) copy-start(s32[1,4]{1,0:T(1,128)} %param.12) | copy-start | bytes 52
  1.3 4.9 %copy-start.6 = (s32[1,4]{1,0:T(1,128)S(1)}, s32[1,4]{1,0:T(1,128)}, u32[]{:S(2)}) copy-start(s32[1,4]{1,0:T(1,128)} %param.11) | copy-start | bytes 52
  1.3 4.9 %copy-start.7 = (s32[1,8]{1,0:T(1,128)S(1)}, s32[1,8]{1,0:T(1,128)}, u32[]{:S(2)}) copy-start(s32[1,8]{1,0:T(1,128)} %param.10) | copy-start | bytes 100
  4.7 6.4 %collective-permute-start.3 = (bf16[144,432]{1,0:T(8,128)(2,1)}, bf16[144,432]{1,0:T(8,128)(2,1)S(1)}, u32[]{:S(2)}, u32[]{:S(2)}) collective-permute-start(bf16[144,432]{1,0:T(8,128)(2,1)} %get-tuple-element.57), channel_id=1, source_target_pairs={{0,1},{1,0},{2,3},{3,2},{4,5},{5,4},{6,7},{7,6},{8,9},{9,8},{10,11... | collective-permute-start | bytes 373256 | tf_op jit(solution)/shard_map/ppermute | solution.py:474
  6.3 22.5 %collective-permute-start = (s32[1,16]{1,0:T(1,128)S(1)}, s32[1,16]{1,0:T(1,128)S(1)}, u32[]{:S(2)}, u32[]{:S(2)}) collective-permute-start(s32[1,16]{1,0:T(1,128)S(1)} %fusion.7), channel_id=1, source_target_pairs={{0,8},{1,9},{2,10},{3,11},{4,12},{5,13},{6,14},{7,15},{8,0},{9,1},... | collective-permute-start | bytes 200 | tf_op jit(solution)/shard_map/ppermute | solution.py:450
  6.3 22.4 %collective-permute-start.2 = (bf16[1,2,64,1152]{3,2,1,0:T(8,128)(2,1)}, bf16[1,2,64,1152]{3,2,1,0:T(8,128)(2,1)S(1)}, u32[]{:S(2)}, u32[]{:S(2)}) collective-permute-start(bf16[1,2,64,1152]{3,2,1,0:T(8,128)(2,1)} %get-tuple-element.55), channel_id=1, source_target_pairs={{0,0},{1,1},{2,16},{3,17},{4,8},{5,9},{6,24},{7,25},{8,20},{9,21},... | collective-permute-start | bytes 884744 | tf_op jit(solution)/shard_map/ppermute | solution.py:472
  9.7 19.2 %collective-permute-start.4 = (bf16[1,2,64,1152]{3,2,1,0:T(8,128)(2,1)}, bf16[1,2,64,1152]{3,2,1,0:T(8,128)(2,1)S(1)}, u32[]{:S(2)}, u32[]{:S(2)}) collective-permute-start(bf16[1,2,64,1152]{3,2,1,0:T(8,128)(2,1)} %get-tuple-element.59), channel_id=1, source_target_pairs={{0,8},{1,9},{2,24},{3,25},{4,0},{5,1},{6,16},{7,17},{8,28},{9,29},... | collective-permute-start | bytes 884744 | tf_op jit(solution)/shard_map/ppermute | solution.py:472
  12.2 36.5 %copy-start.4 = (bf16[144,864]{1,0:T(8,128)(2,1)}, bf16[144,864]{1,0:T(8,128)(2,1)S(1)}, u32[]{:S(2)}) copy-start(bf16[144,864]{1,0:T(8,128)(2,1)S(1)} %pad_maximum_fusion.2.refs_0_) | copy-start | bytes 746500
  28.7 9.7 %copy-start.2 = (bf16[1,2,64,1152]{3,2,1,0:T(8,128)(2,1)}, bf16[1,2,64,1152]{3,2,1,0:T(8,128)(2,1)S(1)}, u32[]{:S(2)}) copy-start(bf16[1,2,64,1152]{3,2,1,0:T(8,128)(2,1)S(1)} %collective-permute-done.2.refs_0_) | copy-start | bytes 884740
  28.7 6.7 %collective-permute-start.12 = (bf16[1,2,64,1152]{3,2,1,0:T(8,128)(2,1)S(1)}, bf16[1,2,64,1152]{3,2,1,0:T(8,128)(2,1)S(1)}, u32[]{:S(2)}, u32[]{:S(2)}) collective-permute-start(bf16[1,2,64,1152]{3,2,1,0:T(8,128)(2,1)S(1)} %collective-permute-done.2.refs_0_), channel_id=1, source_target_pairs={{0,1},{1,0},{2,3},{3,2},{4,5},{5,4},{6,7},{7,6},{8,9},{9,8},{10,11... | collective-permute-start | bytes 884744 | tf_op jit(solution)/shard_map/ppermute | solution.py:435
  28.9 3.6 %collective-permute-start.1 = (s32[2,16]{1,0:T(2,128)S(1)}, s32[2,16]{1,0:T(2,128)S(1)}, u32[]{:S(2)}, u32[]{:S(2)}) collective-permute-start(s32[2,16]{1,0:T(2,128)S(1)} %pad_add_fusion), channel_id=1, source_target_pairs={{0,16},{1,17},{2,18},{3,19},{4,20},{5,21},{6,22},{7,23},{8,24},{9,... | collective-permute-start | bytes 392 | tf_op jit(solution)/shard_map/ppermute | solution.py:452
  28.9 9.4 %copy-start.3 = (bf16[1,2,64,1152]{3,2,1,0:T(8,128)(2,1)}, bf16[1,2,64,1152]{3,2,1,0:T(8,128)(2,1)S(1)}, u32[]{:S(2)}) copy-start(bf16[1,2,64,1152]{3,2,1,0:T(8,128)(2,1)S(1)} %collective-permute-done.4.refs_1_) | copy-start | bytes 884740
  29.0 9.4 %collective-permute-start.14 = (bf16[1,2,64,1152]{3,2,1,0:T(8,128)(2,1)S(1)}, bf16[1,2,64,1152]{3,2,1,0:T(8,128)(2,1)S(1)}, u32[]{:S(2)}, u32[]{:S(2)}) collective-permute-start(bf16[1,2,64,1152]{3,2,1,0:T(8,128)(2,1)S(1)} %collective-permute-done.4.refs_1_), channel_id=1, source_target_pairs={{0,16},{1,17},{2,18},{3,19},{4,20},{5,21},{6,22},{7,23},{8,24},{9,... | collective-permute-start | bytes 884744 | tf_op jit(solution)/shard_map/ppermute | solution.py:435
  33.1 17.4 %copy-start.10 = (bf16[144,1152]{1,0:T(8,128)(2,1)S(1)}, bf16[144,1152]{1,0:T(8,128)(2,1)}, u32[]{:S(2)}) copy-start(bf16[144,1152]{1,0:T(8,128)(2,1)} %param.15) | copy-start | bytes 995332
  33.1 13.3 %collective-permute-start.6 = (bf16[144,864]{1,0:T(8,128)(2,1)S(1)}, bf16[144,864]{1,0:T(8,128)(2,1)S(1)}, u32[]{:S(2)}, u32[]{:S(2)}) collective-permute-start(bf16[144,864]{1,0:T(8,128)(2,1)S(1)} %pad_maximum_fusion.2.refs_0_), channel_id=1, source_target_pairs={{0,4},{1,5},{2,6},{3,7},{4,0},{5,1},{6,2},{7,3},{8,12},{9,13},{10,... | collective-permute-start | bytes 746504 | tf_op jit(solution)/shard_map/ppermute | solution.py:485
  33.1 13.5 %collective-permute-start.5 = (bf16[144,864]{1,0:T(8,128)(2,1)S(1)}, bf16[144,864]{1,0:T(8,128)(2,1)S(1)}, u32[]{:S(2)}, u32[]{:S(2)}) collective-permute-start(bf16[144,864]{1,0:T(8,128)(2,1)S(1)} %pad_maximum_fusion.2.refs_0_), channel_id=1, source_target_pairs={{0,2},{1,3},{2,0},{3,1},{4,6},{5,7},{6,4},{7,5},{8,10},{9,11},{10,... | collective-permute-start | bytes 746504 | tf_op jit(solution)/shard_map/ppermute | solution.py:485
  35.5 26.3 %copy-start = (bf16[2,2,64,1152]{3,2,1,0:T(8,128)(2,1)}, bf16[2,2,64,1152]{3,2,1,0:T(8,128)(2,1)S(1)}, u32[]{:S(2)}) copy-start(bf16[2,2,64,1152]{3,2,1,0:T(8,128)(2,1)S(1)} %pad_maximum_fusion.refs_0_) | copy-start | bytes 1769476
  38.4 23.4 %copy-start.1 = (bf16[2,2,64,1152]{3,2,1,0:T(8,128)(2,1)}, bf16[2,2,64,1152]{3,2,1,0:T(8,128)(2,1)S(1)}, u32[]{:S(2)}) copy-start(bf16[2,2,64,1152]{3,2,1,0:T(8,128)(2,1)S(1)} %pad_maximum_fusion.1.refs_2_) | copy-start | bytes 1769476
  46.4 23.6 %copy-start.19 = (bf16[144,864]{1,0:T(8,128)(2,1)}, bf16[144,864]{1,0:T(8,128)(2,1)S(1)}, u32[]{:S(2)}) copy-start(bf16[144,864]{1,0:T(8,128)(2,1)S(1)} %collective-permute-done.6.refs_2_) | copy-start | bytes 746500
  46.6 23.4 %copy-start.20 = (bf16[144,864]{1,0:T(8,128)(2,1)}, bf16[144,864]{1,0:T(8,128)(2,1)S(1)}, u32[]{:S(2)}) copy-start(bf16[144,864]{1,0:T(8,128)(2,1)S(1)} %collective-permute-done.5.refs_1_) | copy-start | bytes 746500
  46.6 15.1 %collective-permute-start.15 = (bf16[2,2,64,1152]{3,2,1,0:T(8,128)(2,1)S(1)}, bf16[2,2,64,1152]{3,2,1,0:T(8,128)(2,1)S(1)}, u32[]{:S(2)}, u32[]{:S(2)}) collective-permute-start(bf16[2,2,64,1152]{3,2,1,0:T(8,128)(2,1)S(1)} %pad_maximum_fusion.1.refs_2_), channel_id=1, source_target_pairs={{0,1},{1,0},{2,3},{3,2},{4,5},{5,4},{6,7},{7,6},{8,9},{9,8},{10,11... | collective-permute-start | bytes 1769480 | tf_op jit(solution)/shard_map/ppermute | solution.py:437
  47.3 14.5 %collective-permute-start.13 = (bf16[2,2,64,1152]{3,2,1,0:T(8,128)(2,1)S(1)}, bf16[2,2,64,1152]{3,2,1,0:T(8,128)(2,1)S(1)}, u32[]{:S(2)}, u32[]{:S(2)}) collective-permute-start(bf16[2,2,64,1152]{3,2,1,0:T(8,128)(2,1)S(1)} %pad_maximum_fusion.refs_0_), channel_id=1, source_target_pairs={{0,16},{1,17},{2,18},{3,19},{4,20},{5,21},{6,22},{7,23},{8,24},{9,... | collective-permute-start | bytes 1769480 | tf_op jit(solution)/shard_map/ppermute | solution.py:437
  48.7 1.5 %collective-permute-start.8 = (bf16[144,864]{1,0:T(8,128)(2,1)S(1)}, bf16[144,864]{1,0:T(8,128)(2,1)S(1)}, u32[]{:S(2)}, u32[]{:S(2)}) collective-permute-start(bf16[144,864]{1,0:T(8,128)(2,1)S(1)} %pad_maximum_fusion.2.refs_0_), channel_id=1, source_target_pairs={{0,8},{1,9},{2,10},{3,11},{4,12},{5,13},{6,14},{7,15},{8,0},{9,1},... | collective-permute-start | bytes 746504 | tf_op jit(solution)/shard_map/ppermute | solution.py:494
  48.7 1.9 %collective-permute-start.10 = (bf16[144,864]{1,0:T(8,128)(2,1)S(1)}, bf16[144,864]{1,0:T(8,128)(2,1)S(1)}, u32[]{:S(2)}, u32[]{:S(2)}) collective-permute-start(bf16[144,864]{1,0:T(8,128)(2,1)S(1)} %collective-permute-done.6.refs_2_), channel_id=1, source_target_pairs={{0,8},{1,9},{2,10},{3,11},{4,12},{5,13},{6,14},{7,15},{8,0},{9,1},... | collective-permute-start | bytes 746504 | tf_op jit(solution)/shard_map/ppermute | solution.py:494
  49.2 8.1 %collective-permute-start.7 = (bf16[144,864]{1,0:T(8,128)(2,1)S(1)}, bf16[144,864]{1,0:T(8,128)(2,1)S(1)}, u32[]{:S(2)}, u32[]{:S(2)}) collective-permute-start(bf16[144,864]{1,0:T(8,128)(2,1)S(1)} %collective-permute-done.6.refs_2_), channel_id=1, source_target_pairs={{0,2},{1,3},{2,0},{3,1},{4,6},{5,7},{6,4},{7,5},{8,10},{9,11},{10,... | collective-permute-start | bytes 746504 | tf_op jit(solution)/shard_map/ppermute | solution.py:490
  50.2 19.8 %copy-start.21 = (bf16[144,864]{1,0:T(8,128)(2,1)}, bf16[144,864]{1,0:T(8,128)(2,1)S(1)}, u32[]{:S(2)}) copy-start(bf16[144,864]{1,0:T(8,128)(2,1)S(1)} %collective-permute-done.8.refs_4_) | copy-start | bytes 746500
  50.2 7.1 %collective-permute-start.9 = (bf16[144,864]{1,0:T(8,128)(2,1)S(1)}, bf16[144,864]{1,0:T(8,128)(2,1)S(1)}, u32[]{:S(2)}, u32[]{:S(2)}) collective-permute-start(bf16[144,864]{1,0:T(8,128)(2,1)S(1)} %collective-permute-done.5.refs_1_), channel_id=1, source_target_pairs={{0,8},{1,9},{2,10},{3,11},{4,12},{5,13},{6,14},{7,15},{8,0},{9,1},... | collective-permute-start | bytes 746504 | tf_op jit(solution)/shard_map/ppermute | solution.py:494
  50.6 19.5 %copy-start.22 = (bf16[144,864]{1,0:T(8,128)(2,1)}, bf16[144,864]{1,0:T(8,128)(2,1)S(1)}, u32[]{:S(2)}) copy-start(bf16[144,864]{1,0:T(8,128)(2,1)S(1)} %collective-permute-done.10.refs_6_) | copy-start | bytes 746500
  50.6 17.4 %collective-permute-start.16 = (bf16[144,1152]{1,0:T(8,128)(2,1)S(1)}, bf16[144,1152]{1,0:T(8,128)(2,1)S(1)}, u32[]{:S(2)}, u32[]{:S(2)}) collective-permute-start(bf16[144,1152]{1,0:T(8,128)(2,1)S(1)} %copy-done.10), channel_id=1, source_target_pairs={{0,0},{1,1},{2,18},{3,19},{4,8},{5,9},{6,26},{7,27},{8,4},{9,5},{1... | collective-permute-start | bytes 995336 | tf_op jit(solution)/shard_map/ppermute | solution.py:502
  57.3 12.8 %copy-start.23 = (bf16[144,864]{1,0:T(8,128)(2,1)}, bf16[144,864]{1,0:T(8,128)(2,1)S(1)}, u32[]{:S(2)}) copy-start(bf16[144,864]{1,0:T(8,128)(2,1)S(1)} %collective-permute-done.7.refs_3_) | copy-start | bytes 746500
  57.3 12.8 %copy-start.24 = (bf16[144,864]{1,0:T(8,128)(2,1)}, bf16[144,864]{1,0:T(8,128)(2,1)S(1)}, u32[]{:S(2)}) copy-start(bf16[144,864]{1,0:T(8,128)(2,1)S(1)} %collective-permute-done.9.refs_5_) | copy-start | bytes 746500
  61.7 0.8 copy-start.8
  62.5 0.8 copy-start.9
  67.9 2.1 %copy-start.11 = (bf16[144,1152]{1,0:T(8,128)(2,1)}, bf16[144,1152]{1,0:T(8,128)(2,1)S(1)}, u32[]{:S(2)}) copy-start(bf16[144,1152]{1,0:T(8,128)(2,1)S(1)} %collective-permute-done.16.refs_8_) | copy-start | bytes 995332
  67.9 2.1 %collective-permute-start.17 = (bf16[144,1152]{1,0:T(8,128)(2,1)S(1)}, bf16[144,1152]{1,0:T(8,128)(2,1)S(1)}, u32[]{:S(2)}, u32[]{:S(2)}) collective-permute-start(bf16[144,1152]{1,0:T(8,128)(2,1)S(1)} %collective-permute-done.16.refs_8_), channel_id=1, source_target_pairs={{0,8},{1,9},{2,10},{3,11},{4,12},{5,13},{6,14},{7,15},{8,0},{9,1},... | collective-permute-start | bytes 995336 | tf_op jit(solution)/shard_map/ppermute | solution.py:531
  68.0 2.0 %collective-permute-start.11 = (bf16[144,864]{1,0:T(8,128)(2,1)S(1)}, bf16[144,864]{1,0:T(8,128)(2,1)S(1)}, u32[]{:S(2)}, u32[]{:S(2)}) collective-permute-start(bf16[144,864]{1,0:T(8,128)(2,1)S(1)} %collective-permute-done.7.refs_3_), channel_id=1, source_target_pairs={{0,8},{1,9},{2,10},{3,11},{4,12},{5,13},{6,14},{7,15},{8,0},{9,1},... | collective-permute-start | bytes 746504 | tf_op jit(solution)/shard_map/ppermute | solution.py:494
  70.0 0.7 copy-start.25
  70.0 0.8 copy-start.12
  82.1 3.6 %collective-permute-start.18 = (f32[4,48,864]{2,1,0:T(8,128)}, f32[4,48,864]{2,1,0:T(8,128)S(1)}, u32[]{:S(2)}, u32[]{:S(2)}) collective-permute-start(f32[4,48,864]{2,1,0:T(8,128)} %get-tuple-element.75), channel_id=1, source_target_pairs={{0,8},{1,9},{2,10},{3,11},{4,12},{5,13},{6,14},{7,15},{8,0},{9,1},... | collective-permute-start | bytes 1990664 | tf_op jit(solution)/shard_map/ppermute | solution.py:553
  82.3 20.4 %collective-permute-start.20 = (bf16[2,64,1152]{2,1,0:T(8,128)(2,1)}, bf16[2,64,1152]{2,1,0:T(8,128)(2,1)S(1)}, u32[]{:S(2)}, u32[]{:S(2)}) collective-permute-start(bf16[2,64,1152]{2,1,0:T(8,128)(2,1)} %get-tuple-element.83), channel_id=1, source_target_pairs={{0,1},{1,0},{2,3},{3,2},{4,5},{5,4},{6,7},{7,6},{8,9},{9,8},{10,11... | collective-permute-start | bytes 884744 | tf_op jit(solution)/shard_map/ppermute | solution.py:440
  83.2 19.5 %collective-permute-start.21 = (bf16[2,64,1152]{2,1,0:T(8,128)(2,1)}, bf16[2,64,1152]{2,1,0:T(8,128)(2,1)S(1)}, u32[]{:S(2)}, u32[]{:S(2)}) collective-permute-start(bf16[2,64,1152]{2,1,0:T(8,128)(2,1)} %get-tuple-element.84), channel_id=1, source_target_pairs={{0,16},{1,17},{2,18},{3,19},{4,20},{5,21},{6,22},{7,23},{8,24},{9,... | collective-permute-start | bytes 884744 | tf_op jit(solution)/shard_map/ppermute | solution.py:440
  83.8 19.0 %collective-permute-start.22 = (bf16[2,64,1152]{2,1,0:T(8,128)(2,1)}, bf16[2,64,1152]{2,1,0:T(8,128)(2,1)S(1)}, u32[]{:S(2)}, u32[]{:S(2)}) collective-permute-start(bf16[2,64,1152]{2,1,0:T(8,128)(2,1)} %get-tuple-element.85), channel_id=1, source_target_pairs={{0,17},{1,16},{2,19},{3,18},{4,21},{5,20},{6,23},{7,22},{8,25},{9,... | collective-permute-start | bytes 884744 | tf_op jit(solution)/shard_map/ppermute | solution.py:440
  87.0 15.8 %collective-permute-start.19 = (f32[2,48,864]{2,1,0:T(8,128)S(1)}, f32[2,48,864]{2,1,0:T(8,128)S(1)}, u32[]{:S(2)}, u32[]{:S(2)}) collective-permute-start(f32[2,48,864]{2,1,0:T(8,128)S(1)} %get-tuple-element.81), channel_id=1, source_target_pairs={{0,2},{1,3},{2,0},{3,1},{4,6},{5,7},{6,4},{7,5},{8,10},{9,11},{10,... | collective-permute-start | bytes 995336 | tf_op jit(solution)/shard_map/ppermute | solution.py:559
  102.7 20.4 %copy-start.13 = (bf16[2,64,1152]{2,1,0:T(8,128)(2,1)}, bf16[2,64,1152]{2,1,0:T(8,128)(2,1)S(1)}, u32[]{:S(2)}) copy-start(bf16[2,64,1152]{2,1,0:T(8,128)(2,1)S(1)} %collective-permute-done.20.refs_3_) | copy-start | bytes 884740
  102.7 20.4 %copy-start.14 = (bf16[2,64,1152]{2,1,0:T(8,128)(2,1)}, bf16[2,64,1152]{2,1,0:T(8,128)(2,1)S(1)}, u32[]{:S(2)}) copy-start(bf16[2,64,1152]{2,1,0:T(8,128)(2,1)S(1)} %collective-permute-done.21.refs_4_) | copy-start | bytes 884740
  102.8 20.4 %copy-start.15 = (bf16[2,64,1152]{2,1,0:T(8,128)(2,1)}, bf16[2,64,1152]{2,1,0:T(8,128)(2,1)S(1)}, u32[]{:S(2)}) copy-start(bf16[2,64,1152]{2,1,0:T(8,128)(2,1)S(1)} %collective-permute-done.22.refs_5_) | copy-start | bytes 884740
  102.8 10.2 %collective-permute-start.23 = (bf16[2,64,1152]{2,1,0:T(8,128)(2,1)}, bf16[2,64,1152]{2,1,0:T(8,128)(2,1)S(1)}, u32[]{:S(2)}, u32[]{:S(2)}) collective-permute-start(bf16[2,64,1152]{2,1,0:T(8,128)(2,1)} %get-tuple-element.90), channel_id=1, source_target_pairs={{0,1},{1,0},{2,3},{3,2},{4,5},{5,4},{6,7},{7,6},{8,9},{9,8},{10,11... | collective-permute-start | bytes 884744 | tf_op jit(solution)/shard_map/ppermute | solution.py:440
  104.1 14.0 %collective-permute-start.24 = (bf16[2,64,1152]{2,1,0:T(8,128)(2,1)}, bf16[2,64,1152]{2,1,0:T(8,128)(2,1)S(1)}, u32[]{:S(2)}, u32[]{:S(2)}) collective-permute-start(bf16[2,64,1152]{2,1,0:T(8,128)(2,1)} %get-tuple-element.98), channel_id=1, source_target_pairs={{0,16},{1,17},{2,18},{3,19},{4,20},{5,21},{6,22},{7,23},{8,24},{9,... | collective-permute-start | bytes 884744 | tf_op jit(solution)/shard_map/ppermute | solution.py:440
  106.1 12.9 %collective-permute-start.25 = (bf16[2,64,1152]{2,1,0:T(8,128)(2,1)}, bf16[2,64,1152]{2,1,0:T(8,128)(2,1)S(1)}, u32[]{:S(2)}, u32[]{:S(2)}) collective-permute-start(bf16[2,64,1152]{2,1,0:T(8,128)(2,1)} %get-tuple-element.99), channel_id=1, source_target_pairs={{0,17},{1,16},{2,19},{3,18},{4,21},{5,20},{6,23},{7,22},{8,25},{9,... | collective-permute-start | bytes 884744 | tf_op jit(solution)/shard_map/ppermute | solution.py:440
  106.4 27.3 %collective-permute-start.30 = (f32[1,48,864]{2,1,0:T(8,128)S(1)}, f32[1,48,864]{2,1,0:T(8,128)S(1)}, u32[]{:S(2)}, u32[]{:S(2)}) collective-permute-start(f32[1,48,864]{2,1,0:T(8,128)S(1)} %slice.47), channel_id=1, source_target_pairs={{0,4},{1,5},{2,6},{3,7},{4,0},{5,1},{6,2},{7,3},{8,12},{9,13},{10,... | collective-permute-start | bytes 497672 | tf_op jit(solution)/shard_map/ppermute | solution.py:588
  113.0 6.0 %copy-start.16 = (bf16[2,64,1152]{2,1,0:T(8,128)(2,1)}, bf16[2,64,1152]{2,1,0:T(8,128)(2,1)S(1)}, u32[]{:S(2)}) copy-start(bf16[2,64,1152]{2,1,0:T(8,128)(2,1)S(1)} %collective-permute-done.23.refs_3_) | copy-start | bytes 884740
  118.1 0.9 copy-start.17
  119.0 0.7 copy-start.18
  123.1 10.6 %copy-start.27 = (bf16[64,1152]{1,0:T(8,128)(2,1)S(1)}, bf16[64,1152]{1,0:T(8,128)(2,1)}, u32[]{:S(2)}) copy-start(bf16[64,1152]{1,0:T(8,128)(2,1)} %get-tuple-element.100) | copy-start | bytes 442372
  123.2 12.6 %copy-start.26 = (bf16[64,1152]{1,0:T(8,128)(2,1)S(1)}, bf16[64,1152]{1,0:T(8,128)(2,1)}, u32[]{:S(2)}) copy-start(bf16[64,1152]{1,0:T(8,128)(2,1)} %get-tuple-element.101) | copy-start | bytes 442372
  126.4 14.2 %collective-permute-start.26 = (bf16[64,1152]{1,0:T(8,128)(2,1)}, bf16[64,1152]{1,0:T(8,128)(2,1)S(1)}, u32[]{:S(2)}, u32[]{:S(2)}) collective-permute-start(bf16[64,1152]{1,0:T(8,128)(2,1)} %get-tuple-element.102), channel_id=1, source_target_pairs={{0,0},{1,1},{16,2},{17,3},{8,4},{9,5},{24,6},{25,7},{20,8},{21,9},... | collective-permute-start | bytes 442376 | tf_op jit(solution)/shard_map/ppermute | solution.py:444
  131.8 8.8 %collective-permute-start.27 = (bf16[64,1152]{1,0:T(8,128)(2,1)}, bf16[64,1152]{1,0:T(8,128)(2,1)S(1)}, u32[]{:S(2)}, u32[]{:S(2)}) collective-permute-start(bf16[64,1152]{1,0:T(8,128)(2,1)} %get-tuple-element.103), channel_id=1, source_target_pairs={{8,0},{9,1},{24,2},{25,3},{0,4},{1,5},{16,6},{17,7},{28,8},{29,9},... | collective-permute-start | bytes 442376 | tf_op jit(solution)/shard_map/ppermute | solution.py:444
  133.8 9.0 %collective-permute-start.28 = (bf16[64,1152]{1,0:T(8,128)(2,1)S(1)}, bf16[64,1152]{1,0:T(8,128)(2,1)S(1)}, u32[]{:S(2)}, u32[]{:S(2)}) collective-permute-start(bf16[64,1152]{1,0:T(8,128)(2,1)S(1)} %copy-done.27), channel_id=1, source_target_pairs={{0,0},{1,1},{16,2},{17,3},{8,4},{9,5},{24,6},{25,7},{20,8},{21,9},... | collective-permute-start | bytes 442376 | tf_op jit(solution)/shard_map/ppermute | solution.py:444
  135.7 8.9 %collective-permute-start.29 = (bf16[64,1152]{1,0:T(8,128)(2,1)S(1)}, bf16[64,1152]{1,0:T(8,128)(2,1)S(1)}, u32[]{:S(2)}, u32[]{:S(2)}) collective-permute-start(bf16[64,1152]{1,0:T(8,128)(2,1)S(1)} %copy-done.26), channel_id=1, source_target_pairs={{8,0},{9,1},{24,2},{25,3},{0,4},{1,5},{16,6},{17,7},{28,8},{29,9},... | collective-permute-start | bytes 442376 | tf_op jit(solution)/shard_map/ppermute | solution.py:444
  138.4 11.4 %collective-permute-start.31 = (f32[48,864]{1,0:T(8,128)S(1)}, f32[48,864]{1,0:T(8,128)S(1)}, u32[]{:S(2)}, u32[]{:S(2)}) collective-permute-start(f32[48,864]{1,0:T(8,128)S(1)} %bitcast.26), channel_id=1, source_target_pairs={{0,0},{1,1},{2,8},{3,9},{4,16},{5,17},{6,24},{7,25},{8,4},{9,5},{1... | collective-permute-start | bytes 497672 | tf_op jit(solution)/shard_map/ppermute | solution.py:605

commit v8 on v7

--- a/solution.py
+++ b/solution.py
@@ -493,13 +493,14 @@
     if halves > 1:
         w_pieces += [lax.ppermute(piece, AXES, lay.swap(kc=1)) for piece in w_pieces]
 
+    late_w_out, _ = lax.optimization_barrier((w_out, own))
+    wo_own = lax.ppermute(late_w_out, AXES, lay.rows_to_chip())
+
     pairs = []
     for j in range(nc):
-        pairs += doubling(own[j], lay.chip_bits(j), chip_swap, early if j else info)
-    pairs, _ = lax.optimization_barrier((pairs, [late] + w_pieces[lay.nz : -1]))
-
-    late_w_out, _ = lax.optimization_barrier((w_out, own))
-    wo_own = lax.ppermute(late_w_out, AXES, lay.rows_to_chip())
+        pairs += doubling(own[j], lay.chip_bits(j), chip_swap, info)
+    pairs, _ = lax.optimization_barrier((pairs, [late, wo_own] + w_pieces[lay.nz : -1]))
+
 
     def spread(count, width, patches_at_once):
         return pl.BlockSpec((count, patches_at_once, width), lambda i, *_: (0, i, 0))
@@ -527,7 +528,6 @@
         [struct((lay.frames, half, model))] * 2,
         grid=(few_steps,),
     )(pos, info, *pairs, mod_table)
-    wo_own, _ = lax.optimization_barrier((wo_own, hidden))
     wo_rows = [wo_own, lax.ppermute(wo_own, AXES, lay.swap(kc=1))]
 
     fold = 3 if rows % 24 == 0 else 1
@@ -585,7 +585,10 @@
     cut = cut + first_away
     for bit in lay.bits(lay.nz)[1:]:
         middle = middle // 2
-        cut = cut[:middle] + lax.ppermute(cut[middle:], AXES, lay.swap(kz=bit))
+        away = lax.ppermute(cut[middle:], AXES, lay.swap(kz=bit))
+        away, _ = lax.optimization_barrier((away, out_parts))
+        cut = cut[:middle] + away
+    out_y = from_plane(out_parts)
 
 
     grad_parts = call(
@@ -598,8 +601,6 @@
         grid=(few_steps,),
     )(pos, info, *own, *grad_hidden, mod_table)
     grad_x = from_plane(grad_parts)
-    out_parts, _ = lax.optimization_barrier((out_parts, grad_parts))
-    out_y = from_plane(out_parts)
 
     cut, _ = lax.optimization_barrier((cut, grad_parts))
     grad_w = lax.ppermute(cut[0], AXES, lay.to_owner())

time: 153 us -> 140 us (0.915); the launches traced: 151 us -> 140 us
  starting transfers between devices: 47 us -> 35 us
    ppermute x1, waiting for transfers between devices: 0.01 us -> 7.58 us  [local(): wo_own = lax.ppermute(late_w_out, AXES, lay.rows_to_chip())]
    ppermute x1, starting transfers between devices: 6.06 us -> 0.07 us  [local(): first_away = lax.ppermute(away, AXES, lay.swap(kz=1))]
    ppermute x2, waiting for transfers between devices: 4.45 us -> 0.01 us  [doubling(): return [held, lax.ppermute(held, AXES, swap(bits[-1]))]]
    ppermute x6, waiting for transfers between devices: 10.1 us -> 6.95 us  [over_chips(): got = [lax.ppermute(parts[k], AXES, chip_swap(k)) for k in range(1, chips)]]
    ppermute x4, waiting for transfers between devices: 2.42 us -> 0.01 us  [local(): lax.ppermute(piece, AXES, lay.swap(kc=1))]
    ppermute x2, waiting for transfers between devices: 2.92 us -> 5.13 us  [doubling(): held = jnp.concatenate([held, lax.ppermute(held, AXES, swap(bit))], axis=0)]
    ppermute x2, starting transfers between devices: 2.21 us -> 0.01 us  [local(): w_pieces[bit] = lax.ppermute(w_own, AXES, lay.swap(kz=bit))]
    ppermute x4, starting transfers between devices: 11.9 us -> 9.75 us  [from_plane(): lax.ppermute(part, AXES, lay.from_plane(k))]
  transfers between devices with their start and end apart: 32 -> 32, of which waited for: 18 -> 13; matrix products, arithmetic and copies ran while one was open for 3% -> 3% of each run, Pallas kernels for 14% -> 15%
where the time goes in v8:
time: 140 us
  waiting for transfers between devices  58.3 us (42%)
  Pallas kernels  35.4 us (25%)
  starting transfers between devices  35 us (25%)
  other arithmetic  5.89 us (4%)
  local copies, waits for them, and re-layouts  4.02 us (3%)
    ppermute x2, waiting for transfers between devices, local(): lax.ppermute(pair, AXES, lay.to_plane(k))  16.5 us
    pallas_call x1, Pallas kernels, local(): call(functools.partial(forward_kernel, lay), 'forward', 14 * model * 1000...  11.3 us
    ppermute x4, starting transfers between devices, from_plane(): lax.ppermute(part, AXES, lay.from_plane(k))  9.75 us
    pallas_call x1, Pallas kernels, local(): call(functools.partial(backward_kernel, lay), 'backward', 10 * model * 10...  9.74 us
    ppermute x2, waiting for transfers between devices, local(): w_pieces[bit] = lax.ppermute(w_own, AXES, lay.swap(kz=bit))  9.37 us
    ppermute x1, waiting for transfers between devices, local(): wo_own = lax.ppermute(late_w_out, AXES, lay.rows_to_chip())  7.58 us
    ppermute x6, starting transfers between devices, over_chips(): got = [lax.ppermute(parts[k], AXES, chip_swap(k)) for k in range(1, chips)]  7.04 us
    ppermute x6, waiting for transfers between devices, over_chips(): got = [lax.ppermute(parts[k], AXES, chip_swap(k)) for k in range(1, chips)]  6.95 us
  transfers between devices with their start and end apart: 32, of which 13 were waited for; matrix products, arithmetic and copies ran while one was open for 3% of the time, Pallas kernels for 15%

profile of v8, /device:TPU:4, one launch (start us, length us, event | category | flops | bytes accessed | tf_op | source)
XLA Modules:
  0.0 139.6 jit_solution(12428833614918032090)
XLA Ops:
  0.6 0.6 pad_add_fusion.1.pos_ref
  1.2 3.4 %start.1 = (bf16[1,2,64,1152]{3,2,1,0:T(8,128)(2,1)}, bf16[1,2,64,1152]{3,2,1,0:T(8,128)(2,1)}, bf16[144,432]{1,0:T(8,128)(2,1)}, bf16[144,432]{1,0:T(8,128)(2,1)}) custom-call(s32[4]{0:T(128)} %pad_add_fusion.1.pos_ref, bf16[1,128,1152]{2,1,0:T(8,128)(2,1)} %x_ref.1, bf16[1,128,1152]{2,1,0:T(8,128)(2,1)} %g_ref.1, bf16[144,3456]{1,0:T(8,128)(2,1)} %w_ref.1), custom_call_target="tpu_custom_call" | custom-call | flops 1179648000 | bytes 2359296 | tf_op jit(solution)/shard_map/start/pallas_call | solution.py:462
  4.7 1.5 %collective-permute-start.3 = (bf16[144,432]{1,0:T(8,128)(2,1)}, bf16[144,432]{1,0:T(8,128)(2,1)S(1)}, u32[]{:S(2)}, u32[]{:S(2)}) collective-permute-start(bf16[144,432]{1,0:T(8,128)(2,1)} %get-tuple-element.55), channel_id=1, source_target_pairs={{0,1},{1,0},{2,3},{3,2},{4,5},{5,4},{6,7},{7,6},{8,9},{9,8},{10,11... | collective-permute-start | bytes 373256 | tf_op jit(solution)/shard_map/ppermute | solution.py:474
  6.2 0.1 fusion.7
  6.3 3.4 %collective-permute-start.2 = (bf16[1,2,64,1152]{3,2,1,0:T(8,128)(2,1)}, bf16[1,2,64,1152]{3,2,1,0:T(8,128)(2,1)S(1)}, u32[]{:S(2)}, u32[]{:S(2)}) collective-permute-start(bf16[1,2,64,1152]{3,2,1,0:T(8,128)(2,1)} %get-tuple-element.53), channel_id=1, source_target_pairs={{0,0},{1,1},{2,16},{3,17},{4,8},{5,9},{6,24},{7,25},{8,20},{9,21},... | collective-permute-start | bytes 884744 | tf_op jit(solution)/shard_map/ppermute | solution.py:472
  9.7 1.4 collective-permute-start.4
  11.0 0.9 broadcast_select_fusion.1
  12.0 0.1 pad_maximum_fusion.2.refs_0_
  12.1 16.5 %collective-permute-done.2.refs_0_ = bf16[1,2,64,1152]{3,2,1,0:T(8,128)(2,1)S(1)} collective-permute-done((bf16[1,2,64,1152]{3,2,1,0:T(8,128)(2,1)}, bf16[1,2,64,1152]{3,2,1,0:T(8,128)(2,1)S(1)}, u32[]{:S(2)}, u32[]{:S(2)}) %collective-permute-start.2) | collective-permute-done | bytes 294944 | tf_op jit(solution)/shard_map/ppermute | solution.py:472
  28.6 0.1 collective-permute-start.12
  28.8 0.1 collective-permute-start.1
  28.9 2.0 %collective-permute-start.14 = (bf16[1,2,64,1152]{3,2,1,0:T(8,128)(2,1)S(1)}, bf16[1,2,64,1152]{3,2,1,0:T(8,128)(2,1)S(1)}, u32[]{:S(2)}, u32[]{:S(2)}) collective-permute-start(bf16[1,2,64,1152]{3,2,1,0:T(8,128)(2,1)S(1)} %collective-permute-done.4.refs_1_), channel_id=1, source_target_pairs={{0,16},{1,17},{2,18},{3,19},{4,20},{5,21},{6,22},{7,23},{8,24},{9,... | collective-permute-start | bytes 884744 | tf_op jit(solution)/shard_map/ppermute | solution.py:435
  30.9 1.5 %collective-permute-done.1 = s32[2,16]{1,0:T(2,128)S(1)} collective-permute-done((s32[2,16]{1,0:T(2,128)S(1)}, s32[2,16]{1,0:T(2,128)S(1)}, u32[]{:S(2)}, u32[]{:S(2)}) %collective-permute-start.1) | collective-permute-done | bytes 160 | tf_op jit(solution)/shard_map/ppermute | solution.py:452
  32.4 0.6 fusion.2.info_ref
  33.0 2.3 %collective-permute-done.12 = bf16[1,2,64,1152]{3,2,1,0:T(8,128)(2,1)S(1)} collective-permute-done((bf16[1,2,64,1152]{3,2,1,0:T(8,128)(2,1)S(1)}, bf16[1,2,64,1152]{3,2,1,0:T(8,128)(2,1)S(1)}, u32[]{:S(2)}, u32[]{:S(2)}) %collective-permute-start.12) | collective-permute-done | bytes 294944 | tf_op jit(solution)/shard_map/ppermute | solution.py:435
  35.4 0.1 pad_maximum_fusion.refs_0_
  35.4 2.8 %collective-permute-done.14 = bf16[1,2,64,1152]{3,2,1,0:T(8,128)(2,1)S(1)} collective-permute-done((bf16[1,2,64,1152]{3,2,1,0:T(8,128)(2,1)S(1)}, bf16[1,2,64,1152]{3,2,1,0:T(8,128)(2,1)S(1)}, u32[]{:S(2)}, u32[]{:S(2)}) %collective-permute-start.14) | collective-permute-done | bytes 294944 | tf_op jit(solution)/shard_map/ppermute | solution.py:435
  38.2 0.1 pad_maximum_fusion.1.refs_2_
  38.3 2.5 %collective-permute-start.15 = (bf16[2,2,64,1152]{3,2,1,0:T(8,128)(2,1)S(1)}, bf16[2,2,64,1152]{3,2,1,0:T(8,128)(2,1)S(1)}, u32[]{:S(2)}, u32[]{:S(2)}) collective-permute-start(bf16[2,2,64,1152]{3,2,1,0:T(8,128)(2,1)S(1)} %pad_maximum_fusion.1.refs_2_), channel_id=1, source_target_pairs={{0,1},{1,0},{2,3},{3,2},{4,5},{5,4},{6,7},{7,6},{8,9},{9,8},{10,11... | collective-permute-start | bytes 1769480 | tf_op jit(solution)/shard_map/ppermute | solution.py:437
  40.8 0.3 collective-permute-start.13
  41.1 6.1 %collective-permute-done.6.refs_2_ = bf16[144,864]{1,0:T(8,128)(2,1)S(1)} collective-permute-done((bf16[144,864]{1,0:T(8,128)(2,1)S(1)}, bf16[144,864]{1,0:T(8,128)(2,1)S(1)}, u32[]{:S(2)}, u32[]{:S(2)}) %collective-permute-start.6) | collective-permute-done | bytes 248864 | tf_op jit(solution)/shard_map/ppermute | solution.py:485
  47.2 0.0 collective-permute-start.10
  47.2 2.1 %collective-permute-start.16 = (bf16[144,1152]{1,0:T(8,128)(2,1)S(1)}, bf16[144,1152]{1,0:T(8,128)(2,1)S(1)}, u32[]{:S(2)}, u32[]{:S(2)}) collective-permute-start(bf16[144,1152]{1,0:T(8,128)(2,1)S(1)} %copy-done.10), channel_id=1, source_target_pairs={{0,0},{1,1},{2,18},{3,19},{4,8},{5,9},{6,26},{7,27},{8,4},{9,5},{1... | collective-permute-start | bytes 995336 | tf_op jit(solution)/shard_map/ppermute | solution.py:497
  49.3 3.3 %collective-permute-done.5.refs_1_ = bf16[144,864]{1,0:T(8,128)(2,1)S(1)} collective-permute-done((bf16[144,864]{1,0:T(8,128)(2,1)S(1)}, bf16[144,864]{1,0:T(8,128)(2,1)S(1)}, u32[]{:S(2)}, u32[]{:S(2)}) %collective-permute-start.5) | collective-permute-done | bytes 248864 | tf_op jit(solution)/shard_map/ppermute | solution.py:485
  52.7 0.1 collective-permute-start.9
  52.7 7.6 %collective-permute-done.16.refs_8_ = bf16[144,1152]{1,0:T(8,128)(2,1)S(1)} collective-permute-done((bf16[144,1152]{1,0:T(8,128)(2,1)S(1)}, bf16[144,1152]{1,0:T(8,128)(2,1)S(1)}, u32[]{:S(2)}, u32[]{:S(2)}) %collective-permute-start.16) | collective-permute-done | bytes 331808 | tf_op jit(solution)/shard_map/ppermute | solution.py:497
  60.3 1.3 collective-permute-start.17
  61.6 3.8 %collective-permute-done.7.refs_3_ = bf16[144,864]{1,0:T(8,128)(2,1)S(1)} collective-permute-done((bf16[144,864]{1,0:T(8,128)(2,1)S(1)}, bf16[144,864]{1,0:T(8,128)(2,1)S(1)}, u32[]{:S(2)}, u32[]{:S(2)}) %collective-permute-start.7) | collective-permute-done | bytes 248864 | tf_op jit(solution)/shard_map/ppermute | solution.py:490
  65.4 0.8 copy-done.8
  66.2 0.8 copy-done.9
  67.1 4.4 %prepare.1 = (bf16[8,64,1152]{2,1,0:T(8,128)(2,1)}, bf16[8,64,1152]{2,1,0:T(8,128)(2,1)}) custom-call(s32[4]{0:T(128)} %pad_add_fusion.1.pos_ref, s32[16]{0:T(128)} %fusion.2.info_ref, bf16[2,2,64,1152]{3,2,1,0:T(8,128)(2,1)} %copy-done, bf16[2,2,64,1152]{3,2,1,0:T(8,128)(2,1)} %copy-done.9, bf16[2,2,64,1152]{3,2,1,0:T(8,128)(2,1)} %copy-done.1, ...), custom_call_target="tpu_custom_call" | custom-call | flops 1769472000 | bytes 2359296 | tf_op jit(solution)/shard_map/prepare/pallas_call | solution.py:522
  71.5 0.6 copy-done.25
  72.1 0.1 copy-done.12
  72.3 11.3 %forward.1 = (bf16[2,8,64,144]{3,2,1,0:T(8,128)(2,1)}, bf16[2,8,64,144]{3,2,1,0:T(8,128)(2,1)}, bf16[2,8,64,144]{3,2,1,0:T(8,128)(2,1)}, bf16[2,8,64,144]{3,2,1,...) custom-call(s32[4]{0:T(128)} %pad_add_fusion.1.pos_ref, ...), custom_call_target="tpu_custom_call" | custom-call | flops 8257536000 | bytes 2359296 | tf_op jit(solution)/shard_map/forward/pallas_call | solution.py:535
  83.6 0.5 collective-permute-start.18
  84.1 0.6 collective-permute-start.20
  84.7 0.2 collective-permute-start.21
  84.8 2.8 %collective-permute-start.22 = (bf16[2,64,1152]{2,1,0:T(8,128)(2,1)}, bf16[2,64,1152]{2,1,0:T(8,128)(2,1)S(1)}, u32[]{:S(2)}, u32[]{:S(2)}) collective-permute-start(bf16[2,64,1152]{2,1,0:T(8,128)(2,1)} %get-tuple-element.82), channel_id=1, source_target_pairs={{0,17},{1,16},{2,19},{3,18},{4,21},{5,20},{6,23},{7,22},{8,25},{9,... | collective-permute-start | bytes 884744 | tf_op jit(solution)/shard_map/ppermute | solution.py:440
  87.6 1.2 slice_add_fusion
  88.7 0.1 collective-permute-start.19
  88.8 9.7 %backward.1 = (f32[2,64,1152]{2,1,0:T(8,128)}, bf16[2,64,1152]{2,1,0:T(8,128)(2,1)}, bf16[2,64,1152]{2,1,0:T(8,128)(2,1)}, bf16[2,64,1152]{2,1,0:T(8,128)(2,1)}) custom-call(s32[4]{0:T(128)} %pad_add_fusion.1.pos_ref, s32[16]{0:T(128)} %fusion.2.info_ref, bf16[144,864]{1,0:T(8,128)(2,1)} %copy-done.4, bf16[144,864]{1,0:T(8,128)(2,1)} %copy-done.21, ...), custom_call_target="tpu_custom_call" | custom-call | flops 5898240000 | bytes 2359296 | tf_op jit(solution)/shard_map/backward/pallas_call | solution.py:561
  98.6 1.3 collective-permute-done.21.refs_4_
  99.9 1.5 %collective-permute-start.23 = (bf16[2,64,1152]{2,1,0:T(8,128)(2,1)}, bf16[2,64,1152]{2,1,0:T(8,128)(2,1)S(1)}, u32[]{:S(2)}, u32[]{:S(2)}) collective-permute-start(bf16[2,64,1152]{2,1,0:T(8,128)(2,1)} %get-tuple-element.87), channel_id=1, source_target_pairs={{0,1},{1,0},{2,3},{3,2},{4,5},{5,4},{6,7},{7,6},{8,9},{9,8},{10,11... | collective-permute-start | bytes 884744 | tf_op jit(solution)/shard_map/ppermute | solution.py:440
  101.4 0.2 collective-permute-start.26
  101.6 1.8 %collective-permute-start.27 = (bf16[2,64,1152]{2,1,0:T(8,128)(2,1)}, bf16[2,64,1152]{2,1,0:T(8,128)(2,1)S(1)}, u32[]{:S(2)}, u32[]{:S(2)}) collective-permute-start(bf16[2,64,1152]{2,1,0:T(8,128)(2,1)} %get-tuple-element.96), channel_id=1, source_target_pairs={{0,17},{1,16},{2,19},{3,18},{4,21},{5,20},{6,23},{7,22},{8,25},{9,... | collective-permute-start | bytes 884744 | tf_op jit(solution)/shard_map/ppermute | solution.py:440
  103.5 1.0 collective-permute-start.30
  104.5 5.6 %collective-permute-done.23.refs_3_ = bf16[2,64,1152]{2,1,0:T(8,128)(2,1)S(1)} collective-permute-done((bf16[2,64,1152]{2,1,0:T(8,128)(2,1)}, bf16[2,64,1152]{2,1,0:T(8,128)(2,1)S(1)}, u32[]{:S(2)}, u32[]{:S(2)}) %collective-permute-start.23) | collective-permute-done | bytes 294944 | tf_op jit(solution)/shard_map/ppermute | solution.py:440
  110.1 3.1 %output.1 = (bf16[64,1152]{1,0:T(8,128)(2,1)}, bf16[64,1152]{1,0:T(8,128)(2,1)}) custom-call(s32[4]{0:T(128)} %pad_add_fusion.1.pos_ref, s32[16]{0:T(128)} %fusion.2.info_ref, bf16[1,2,64,1152]{3,2,1,0:T(8,128)(2,1)} %copy-done.2, bf16[1,2,64,1152]{3,2,1,0:T(8,128)(2,1)} %copy-done.3, f32[2,64,1152]{2,1,0:T(8,128)} %get-tuple-element.88.refs_2_, ...), custom_call_target="tpu_custom_call" | custom-call | flops 1769472000 | bytes 2359296 | tf_op jit(solution)/shard_map/output/pallas_call | solution.py:575
  113.3 2.7 %collective-permute-start.24 = (bf16[64,1152]{1,0:T(8,128)(2,1)}, bf16[64,1152]{1,0:T(8,128)(2,1)S(1)}, u32[]{:S(2)}, u32[]{:S(2)}) collective-permute-start(bf16[64,1152]{1,0:T(8,128)(2,1)} %get-tuple-element.92), channel_id=1, source_target_pairs={{0,0},{1,1},{16,2},{17,3},{8,4},{9,5},{24,6},{25,7},{20,8},{21,9},... | collective-permute-start | bytes 442376 | tf_op jit(solution)/shard_map/ppermute | solution.py:444
  115.9 1.7 %collective-permute-start.25 = (bf16[64,1152]{1,0:T(8,128)(2,1)}, bf16[64,1152]{1,0:T(8,128)(2,1)S(1)}, u32[]{:S(2)}, u32[]{:S(2)}) collective-permute-start(bf16[64,1152]{1,0:T(8,128)(2,1)} %get-tuple-element.93), channel_id=1, source_target_pairs={{8,0},{9,1},{24,2},{25,3},{0,4},{1,5},{16,6},{17,7},{28,8},{29,9},... | collective-permute-start | bytes 442376 | tf_op jit(solution)/shard_map/ppermute | solution.py:444
  117.7 0.7 copy-done.17
  118.4 0.7 copy-done.18
  119.1 3.4 %input_grad.1 = (bf16[64,1152]{1,0:T(8,128)(2,1)}, bf16[64,1152]{1,0:T(8,128)(2,1)}) custom-call(s32[4]{0:T(128)} %pad_add_fusion.1.pos_ref, s32[16]{0:T(128)} %fusion.2.info_ref, bf16[1,2,64,1152]{3,2,1,0:T(8,128)(2,1)} %copy-done.2, bf16[1,2,64,1152]{3,2,1,0:T(8,128)(2,1)} %copy-done.3, f32[2,64,1152]{2,1,0:T(8,128)} %get-tuple-element.94.refs_2_, ...), custom_call_target="tpu_custom_call" | custom-call | flops 1769472000 | bytes 2359296 | tf_op jit(solution)/shard_map/input_grad/pallas_call | solution.py:594
  122.5 2.4 %collective-permute-start.28 = (bf16[64,1152]{1,0:T(8,128)(2,1)}, bf16[64,1152]{1,0:T(8,128)(2,1)S(1)}, u32[]{:S(2)}, u32[]{:S(2)}) collective-permute-start(bf16[64,1152]{1,0:T(8,128)(2,1)} %get-tuple-element.97), channel_id=1, source_target_pairs={{0,0},{1,1},{16,2},{17,3},{8,4},{9,5},{24,6},{25,7},{20,8},{21,9},... | collective-permute-start | bytes 442376 | tf_op jit(solution)/shard_map/ppermute | solution.py:444
  124.9 2.9 %collective-permute-start.29 = (bf16[64,1152]{1,0:T(8,128)(2,1)}, bf16[64,1152]{1,0:T(8,128)(2,1)S(1)}, u32[]{:S(2)}, u32[]{:S(2)}) collective-permute-start(bf16[64,1152]{1,0:T(8,128)(2,1)} %get-tuple-element.98), channel_id=1, source_target_pairs={{8,0},{9,1},{24,2},{25,3},{0,4},{1,5},{16,6},{17,7},{28,8},{29,9},... | collective-permute-start | bytes 442376 | tf_op jit(solution)/shard_map/ppermute | solution.py:444
  127.9 1.9 %collective-permute-start.31 = (f32[48,864]{1,0:T(8,128)S(1)}, f32[48,864]{1,0:T(8,128)S(1)}, u32[]{:S(2)}, u32[]{:S(2)}) collective-permute-start(f32[48,864]{1,0:T(8,128)S(1)} %bitcast.26), channel_id=1, source_target_pairs={{0,0},{1,1},{2,8},{3,9},{4,16},{5,17},{6,24},{7,25},{8,4},{9,5},{1... | collective-permute-start | bytes 497672 | tf_op jit(solution)/shard_map/ppermute | solution.py:606
  129.8 2.4 %collective-permute-done.28 = bf16[64,1152]{1,0:T(8,128)(2,1)S(1)} collective-permute-done((bf16[64,1152]{1,0:T(8,128)(2,1)}, bf16[64,1152]{1,0:T(8,128)(2,1)S(1)}, u32[]{:S(2)}, u32[]{:S(2)}) %collective-permute-start.28) | collective-permute-done | bytes 147488 | tf_op jit(solution)/shard_map/ppermute | solution.py:444
  132.2 0.1 collective-permute-done.29
  132.3 0.1 broadcast_select_fusion.3
  132.3 0.7 maximum_bitcast_fusion.1
  133.1 0.7 maximum_bitcast_fusion
  133.8 5.0 %collective-permute-done.31 = f32[48,864]{1,0:T(8,128)S(1)} collective-permute-done((f32[48,864]{1,0:T(8,128)S(1)}, f32[48,864]{1,0:T(8,128)S(1)}, u32[]{:S(2)}, u32[]{:S(2)}) %collective-permute-start.31) | collective-permute-done | bytes 165920 | tf_op jit(solution)/shard_map/ppermute | solution.py:606
  138.8 0.1 fusion.6
  138.9 0.7 maximum_multiply_fusion
  (75 shorter events, 0.2 us)
Async XLA Ops:
  1.2 4.9 %copy-start.5 = (s32[1,4]{1,0:T(1,128)S(1)}, s32[1,4]{1,0:T(1,128)}, u32[]{:S(2)}) copy-start(s32[1,4]{1,0:T(1,128)} %param.12) | copy-start | bytes 52
  1.2 4.9 %copy-start.6 = (s32[1,4]{1,0:T(1,128)S(1)}, s32[1,4]{1,0:T(1,128)}, u32[]{:S(2)}) copy-start(s32[1,4]{1,0:T(1,128)} %param.11) | copy-start | bytes 52
  1.2 4.9 %copy-start.7 = (s32[1,8]{1,0:T(1,128)S(1)}, s32[1,8]{1,0:T(1,128)}, u32[]{:S(2)}) copy-start(s32[1,8]{1,0:T(1,128)} %param.10) | copy-start | bytes 100
  4.7 6.4 %collective-permute-start.3 = (bf16[144,432]{1,0:T(8,128)(2,1)}, bf16[144,432]{1,0:T(8,128)(2,1)S(1)}, u32[]{:S(2)}, u32[]{:S(2)}) collective-permute-start(bf16[144,432]{1,0:T(8,128)(2,1)} %get-tuple-element.55), channel_id=1, source_target_pairs={{0,1},{1,0},{2,3},{3,2},{4,5},{5,4},{6,7},{7,6},{8,9},{9,8},{10,11... | collective-permute-start | bytes 373256 | tf_op jit(solution)/shard_map/ppermute | solution.py:474
  6.2 22.5 %collective-permute-start = (s32[1,16]{1,0:T(1,128)S(1)}, s32[1,16]{1,0:T(1,128)S(1)}, u32[]{:S(2)}, u32[]{:S(2)}) collective-permute-start(s32[1,16]{1,0:T(1,128)S(1)} %fusion.7), channel_id=1, source_target_pairs={{0,8},{1,9},{2,10},{3,11},{4,12},{5,13},{6,14},{7,15},{8,0},{9,1},... | collective-permute-start | bytes 200 | tf_op jit(solution)/shard_map/ppermute | solution.py:450
  6.3 22.4 %collective-permute-start.2 = (bf16[1,2,64,1152]{3,2,1,0:T(8,128)(2,1)}, bf16[1,2,64,1152]{3,2,1,0:T(8,128)(2,1)S(1)}, u32[]{:S(2)}, u32[]{:S(2)}) collective-permute-start(bf16[1,2,64,1152]{3,2,1,0:T(8,128)(2,1)} %get-tuple-element.53), channel_id=1, source_target_pairs={{0,0},{1,1},{2,16},{3,17},{4,8},{5,9},{6,24},{7,25},{8,20},{9,21},... | collective-permute-start | bytes 884744 | tf_op jit(solution)/shard_map/ppermute | solution.py:472
  9.7 19.2 %collective-permute-start.4 = (bf16[1,2,64,1152]{3,2,1,0:T(8,128)(2,1)}, bf16[1,2,64,1152]{3,2,1,0:T(8,128)(2,1)S(1)}, u32[]{:S(2)}, u32[]{:S(2)}) collective-permute-start(bf16[1,2,64,1152]{3,2,1,0:T(8,128)(2,1)} %get-tuple-element.57), channel_id=1, source_target_pairs={{0,8},{1,9},{2,24},{3,25},{4,0},{5,1},{6,16},{7,17},{8,28},{9,29},... | collective-permute-start | bytes 884744 | tf_op jit(solution)/shard_map/ppermute | solution.py:472
  12.1 29.0 %copy-start.4 = (bf16[144,864]{1,0:T(8,128)(2,1)}, bf16[144,864]{1,0:T(8,128)(2,1)S(1)}, u32[]{:S(2)}) copy-start(bf16[144,864]{1,0:T(8,128)(2,1)S(1)} %pad_maximum_fusion.2.refs_0_) | copy-start | bytes 746500
  28.6 9.7 %copy-start.2 = (bf16[1,2,64,1152]{3,2,1,0:T(8,128)(2,1)}, bf16[1,2,64,1152]{3,2,1,0:T(8,128)(2,1)S(1)}, u32[]{:S(2)}) copy-start(bf16[1,2,64,1152]{3,2,1,0:T(8,128)(2,1)S(1)} %collective-permute-done.2.refs_0_) | copy-start | bytes 884740
  28.6 6.7 %collective-permute-start.12 = (bf16[1,2,64,1152]{3,2,1,0:T(8,128)(2,1)S(1)}, bf16[1,2,64,1152]{3,2,1,0:T(8,128)(2,1)S(1)}, u32[]{:S(2)}, u32[]{:S(2)}) collective-permute-start(bf16[1,2,64,1152]{3,2,1,0:T(8,128)(2,1)S(1)} %collective-permute-done.2.refs_0_), channel_id=1, source_target_pairs={{0,1},{1,0},{2,3},{3,2},{4,5},{5,4},{6,7},{7,6},{8,9},{9,8},{10,11... | collective-permute-start | bytes 884744 | tf_op jit(solution)/shard_map/ppermute | solution.py:435
  28.8 3.6 %collective-permute-start.1 = (s32[2,16]{1,0:T(2,128)S(1)}, s32[2,16]{1,0:T(2,128)S(1)}, u32[]{:S(2)}, u32[]{:S(2)}) collective-permute-start(s32[2,16]{1,0:T(2,128)S(1)} %pad_add_fusion), channel_id=1, source_target_pairs={{0,16},{1,17},{2,18},{3,19},{4,20},{5,21},{6,22},{7,23},{8,24},{9,... | collective-permute-start | bytes 392 | tf_op jit(solution)/shard_map/ppermute | solution.py:452
  28.9 9.4 %copy-start.3 = (bf16[1,2,64,1152]{3,2,1,0:T(8,128)(2,1)}, bf16[1,2,64,1152]{3,2,1,0:T(8,128)(2,1)S(1)}, u32[]{:S(2)}) copy-start(bf16[1,2,64,1152]{3,2,1,0:T(8,128)(2,1)S(1)} %collective-permute-done.4.refs_1_) | copy-start | bytes 884740
  28.9 9.4 %collective-permute-start.14 = (bf16[1,2,64,1152]{3,2,1,0:T(8,128)(2,1)S(1)}, bf16[1,2,64,1152]{3,2,1,0:T(8,128)(2,1)S(1)}, u32[]{:S(2)}, u32[]{:S(2)}) collective-permute-start(bf16[1,2,64,1152]{3,2,1,0:T(8,128)(2,1)S(1)} %collective-permute-done.4.refs_1_), channel_id=1, source_target_pairs={{0,16},{1,17},{2,18},{3,19},{4,20},{5,21},{6,22},{7,23},{8,24},{9,... | collective-permute-start | bytes 884744 | tf_op jit(solution)/shard_map/ppermute | solution.py:435
  33.0 14.2 %copy-start.10 = (bf16[144,1152]{1,0:T(8,128)(2,1)S(1)}, bf16[144,1152]{1,0:T(8,128)(2,1)}, u32[]{:S(2)}) copy-start(bf16[144,1152]{1,0:T(8,128)(2,1)} %param.15) | copy-start | bytes 995332
  33.0 14.2 %collective-permute-start.8 = (bf16[144,864]{1,0:T(8,128)(2,1)S(1)}, bf16[144,864]{1,0:T(8,128)(2,1)S(1)}, u32[]{:S(2)}, u32[]{:S(2)}) collective-permute-start(bf16[144,864]{1,0:T(8,128)(2,1)S(1)} %pad_maximum_fusion.2.refs_0_), channel_id=1, source_target_pairs={{0,8},{1,9},{2,10},{3,11},{4,12},{5,13},{6,14},{7,15},{8,0},{9,1},... | collective-permute-start | bytes 746504 | tf_op jit(solution)/shard_map/ppermute | solution.py:494
  33.0 14.2 %collective-permute-start.6 = (bf16[144,864]{1,0:T(8,128)(2,1)S(1)}, bf16[144,864]{1,0:T(8,128)(2,1)S(1)}, u32[]{:S(2)}, u32[]{:S(2)}) collective-permute-start(bf16[144,864]{1,0:T(8,128)(2,1)S(1)} %pad_maximum_fusion.2.refs_0_), channel_id=1, source_target_pairs={{0,4},{1,5},{2,6},{3,7},{4,0},{5,1},{6,2},{7,3},{8,12},{9,13},{10,... | collective-permute-start | bytes 746504 | tf_op jit(solution)/shard_map/ppermute | solution.py:485
  35.4 30.0 %copy-start = (bf16[2,2,64,1152]{3,2,1,0:T(8,128)(2,1)}, bf16[2,2,64,1152]{3,2,1,0:T(8,128)(2,1)S(1)}, u32[]{:S(2)}) copy-start(bf16[2,2,64,1152]{3,2,1,0:T(8,128)(2,1)S(1)} %pad_maximum_fusion.refs_0_) | copy-start | bytes 1769476
  38.3 27.1 %copy-start.1 = (bf16[2,2,64,1152]{3,2,1,0:T(8,128)(2,1)}, bf16[2,2,64,1152]{3,2,1,0:T(8,128)(2,1)S(1)}, u32[]{:S(2)}) copy-start(bf16[2,2,64,1152]{3,2,1,0:T(8,128)(2,1)S(1)} %pad_maximum_fusion.1.refs_2_) | copy-start | bytes 1769476
  38.3 27.0 %collective-permute-start.15 = (bf16[2,2,64,1152]{3,2,1,0:T(8,128)(2,1)S(1)}, bf16[2,2,64,1152]{3,2,1,0:T(8,128)(2,1)S(1)}, u32[]{:S(2)}, u32[]{:S(2)}) collective-permute-start(bf16[2,2,64,1152]{3,2,1,0:T(8,128)(2,1)S(1)} %pad_maximum_fusion.1.refs_2_), channel_id=1, source_target_pairs={{0,1},{1,0},{2,3},{3,2},{4,5},{5,4},{6,7},{7,6},{8,9},{9,8},{10,11... | collective-permute-start | bytes 1769480 | tf_op jit(solution)/shard_map/ppermute | solution.py:437
  40.8 24.5 %collective-permute-start.13 = (bf16[2,2,64,1152]{3,2,1,0:T(8,128)(2,1)S(1)}, bf16[2,2,64,1152]{3,2,1,0:T(8,128)(2,1)S(1)}, u32[]{:S(2)}, u32[]{:S(2)}) collective-permute-start(bf16[2,2,64,1152]{3,2,1,0:T(8,128)(2,1)S(1)} %pad_maximum_fusion.refs_0_), channel_id=1, source_target_pairs={{0,16},{1,17},{2,18},{3,19},{4,20},{5,21},{6,22},{7,23},{8,24},{9,... | collective-permute-start | bytes 1769480 | tf_op jit(solution)/shard_map/ppermute | solution.py:437
  41.1 11.5 %collective-permute-start.5 = (bf16[144,864]{1,0:T(8,128)(2,1)S(1)}, bf16[144,864]{1,0:T(8,128)(2,1)S(1)}, u32[]{:S(2)}, u32[]{:S(2)}) collective-permute-start(bf16[144,864]{1,0:T(8,128)(2,1)S(1)} %pad_maximum_fusion.2.refs_0_), channel_id=1, source_target_pairs={{0,2},{1,3},{2,0},{3,1},{4,6},{5,7},{6,4},{7,5},{8,10},{9,11},{10,... | collective-permute-start | bytes 746504 | tf_op jit(solution)/shard_map/ppermute | solution.py:485
  47.2 24.3 %copy-start.20 = (bf16[144,864]{1,0:T(8,128)(2,1)}, bf16[144,864]{1,0:T(8,128)(2,1)S(1)}, u32[]{:S(2)}) copy-start(bf16[144,864]{1,0:T(8,128)(2,1)S(1)} %collective-permute-done.6.refs_2_) | copy-start | bytes 746500
  47.2 5.4 %collective-permute-start.10 = (bf16[144,864]{1,0:T(8,128)(2,1)S(1)}, bf16[144,864]{1,0:T(8,128)(2,1)S(1)}, u32[]{:S(2)}, u32[]{:S(2)}) collective-permute-start(bf16[144,864]{1,0:T(8,128)(2,1)S(1)} %collective-permute-done.6.refs_2_), channel_id=1, source_target_pairs={{0,8},{1,9},{2,10},{3,11},{4,12},{5,13},{6,14},{7,15},{8,0},{9,1},... | collective-permute-start | bytes 746504 | tf_op jit(solution)/shard_map/ppermute | solution.py:494
  47.2 24.3 %copy-start.19 = (bf16[144,864]{1,0:T(8,128)(2,1)}, bf16[144,864]{1,0:T(8,128)(2,1)S(1)}, u32[]{:S(2)}) copy-start(bf16[144,864]{1,0:T(8,128)(2,1)S(1)} %collective-permute-done.8.refs_4_) | copy-start | bytes 746500
  47.2 13.1 %collective-permute-start.16 = (bf16[144,1152]{1,0:T(8,128)(2,1)S(1)}, bf16[144,1152]{1,0:T(8,128)(2,1)S(1)}, u32[]{:S(2)}, u32[]{:S(2)}) collective-permute-start(bf16[144,1152]{1,0:T(8,128)(2,1)S(1)} %copy-done.10), channel_id=1, source_target_pairs={{0,0},{1,1},{2,18},{3,19},{4,8},{5,9},{6,26},{7,27},{8,4},{9,5},{1... | collective-permute-start | bytes 995336 | tf_op jit(solution)/shard_map/ppermute | solution.py:497
  52.6 18.9 %copy-start.21 = (bf16[144,864]{1,0:T(8,128)(2,1)}, bf16[144,864]{1,0:T(8,128)(2,1)S(1)}, u32[]{:S(2)}) copy-start(bf16[144,864]{1,0:T(8,128)(2,1)S(1)} %collective-permute-done.5.refs_1_) | copy-start | bytes 746500
  52.6 12.7 %collective-permute-start.7 = (bf16[144,864]{1,0:T(8,128)(2,1)S(1)}, bf16[144,864]{1,0:T(8,128)(2,1)S(1)}, u32[]{:S(2)}, u32[]{:S(2)}) collective-permute-start(bf16[144,864]{1,0:T(8,128)(2,1)S(1)} %collective-permute-done.6.refs_2_), channel_id=1, source_target_pairs={{0,2},{1,3},{2,0},{3,1},{4,6},{5,7},{6,4},{7,5},{8,10},{9,11},{10,... | collective-permute-start | bytes 746504 | tf_op jit(solution)/shard_map/ppermute | solution.py:490
  52.6 18.9 %copy-start.22 = (bf16[144,864]{1,0:T(8,128)(2,1)}, bf16[144,864]{1,0:T(8,128)(2,1)S(1)}, u32[]{:S(2)}) copy-start(bf16[144,864]{1,0:T(8,128)(2,1)S(1)} %collective-permute-done.10.refs_6_) | copy-start | bytes 746500
  52.7 12.7 %collective-permute-start.9 = (bf16[144,864]{1,0:T(8,128)(2,1)S(1)}, bf16[144,864]{1,0:T(8,128)(2,1)S(1)}, u32[]{:S(2)}, u32[]{:S(2)}) collective-permute-start(bf16[144,864]{1,0:T(8,128)(2,1)S(1)} %collective-permute-done.5.refs_1_), channel_id=1, source_target_pairs={{0,8},{1,9},{2,10},{3,11},{4,12},{5,13},{6,14},{7,15},{8,0},{9,1},... | collective-permute-start | bytes 746504 | tf_op jit(solution)/shard_map/ppermute | solution.py:494
  60.3 11.2 %copy-start.11 = (bf16[144,1152]{1,0:T(8,128)(2,1)}, bf16[144,1152]{1,0:T(8,128)(2,1)S(1)}, u32[]{:S(2)}) copy-start(bf16[144,1152]{1,0:T(8,128)(2,1)S(1)} %collective-permute-done.16.refs_8_) | copy-start | bytes 995332
  60.3 11.1 %collective-permute-start.17 = (bf16[144,1152]{1,0:T(8,128)(2,1)S(1)}, bf16[144,1152]{1,0:T(8,128)(2,1)S(1)}, u32[]{:S(2)}, u32[]{:S(2)}) collective-permute-start(bf16[144,1152]{1,0:T(8,128)(2,1)S(1)} %collective-permute-done.16.refs_8_), channel_id=1, source_target_pairs={{0,8},{1,9},{2,10},{3,11},{4,12},{5,13},{6,14},{7,15},{8,0},{9,1},... | collective-permute-start | bytes 995336 | tf_op jit(solution)/shard_map/ppermute | solution.py:531
  65.3 6.2 %copy-start.23 = (bf16[144,864]{1,0:T(8,128)(2,1)}, bf16[144,864]{1,0:T(8,128)(2,1)S(1)}, u32[]{:S(2)}) copy-start(bf16[144,864]{1,0:T(8,128)(2,1)S(1)} %collective-permute-done.7.refs_3_) | copy-start | bytes 746500
  65.3 6.1 %collective-permute-start.11 = (bf16[144,864]{1,0:T(8,128)(2,1)S(1)}, bf16[144,864]{1,0:T(8,128)(2,1)S(1)}, u32[]{:S(2)}, u32[]{:S(2)}) collective-permute-start(bf16[144,864]{1,0:T(8,128)(2,1)S(1)} %collective-permute-done.7.refs_3_), channel_id=1, source_target_pairs={{0,8},{1,9},{2,10},{3,11},{4,12},{5,13},{6,14},{7,15},{8,0},{9,1},... | collective-permute-start | bytes 746504 | tf_op jit(solution)/shard_map/ppermute | solution.py:494
  65.3 6.2 %copy-start.24 = (bf16[144,864]{1,0:T(8,128)(2,1)}, bf16[144,864]{1,0:T(8,128)(2,1)S(1)}, u32[]{:S(2)}) copy-start(bf16[144,864]{1,0:T(8,128)(2,1)S(1)} %collective-permute-done.9.refs_5_) | copy-start | bytes 746500
  65.4 0.9 copy-start.8
  66.2 0.8 copy-start.9
  71.4 0.7 copy-start.25
  71.5 0.8 copy-start.12
  83.6 4.0 %collective-permute-start.18 = (f32[4,48,864]{2,1,0:T(8,128)}, f32[4,48,864]{2,1,0:T(8,128)S(1)}, u32[]{:S(2)}, u32[]{:S(2)}) collective-permute-start(f32[4,48,864]{2,1,0:T(8,128)} %get-tuple-element.72), channel_id=1, source_target_pairs={{0,8},{1,9},{2,10},{3,11},{4,12},{5,13},{6,14},{7,15},{8,0},{9,1},... | collective-permute-start | bytes 1990664 | tf_op jit(solution)/shard_map/ppermute | solution.py:553
  84.1 14.5 %collective-permute-start.20 = (bf16[2,64,1152]{2,1,0:T(8,128)(2,1)}, bf16[2,64,1152]{2,1,0:T(8,128)(2,1)S(1)}, u32[]{:S(2)}, u32[]{:S(2)}) collective-permute-start(bf16[2,64,1152]{2,1,0:T(8,128)(2,1)} %get-tuple-element.80), channel_id=1, source_target_pairs={{0,1},{1,0},{2,3},{3,2},{4,5},{5,4},{6,7},{7,6},{8,9},{9,8},{10,11... | collective-permute-start | bytes 884744 | tf_op jit(solution)/shard_map/ppermute | solution.py:440
  84.7 15.2 %collective-permute-start.21 = (bf16[2,64,1152]{2,1,0:T(8,128)(2,1)}, bf16[2,64,1152]{2,1,0:T(8,128)(2,1)S(1)}, u32[]{:S(2)}, u32[]{:S(2)}) collective-permute-start(bf16[2,64,1152]{2,1,0:T(8,128)(2,1)} %get-tuple-element.81), channel_id=1, source_target_pairs={{0,16},{1,17},{2,18},{3,19},{4,20},{5,21},{6,22},{7,23},{8,24},{9,... | collective-permute-start | bytes 884744 | tf_op jit(solution)/shard_map/ppermute | solution.py:440
  84.8 15.1 %collective-permute-start.22 = (bf16[2,64,1152]{2,1,0:T(8,128)(2,1)}, bf16[2,64,1152]{2,1,0:T(8,128)(2,1)S(1)}, u32[]{:S(2)}, u32[]{:S(2)}) collective-permute-start(bf16[2,64,1152]{2,1,0:T(8,128)(2,1)} %get-tuple-element.82), channel_id=1, source_target_pairs={{0,17},{1,16},{2,19},{3,18},{4,21},{5,20},{6,23},{7,22},{8,25},{9,... | collective-permute-start | bytes 884744 | tf_op jit(solution)/shard_map/ppermute | solution.py:440
  88.7 11.2 %collective-permute-start.19 = (f32[2,48,864]{2,1,0:T(8,128)S(1)}, f32[2,48,864]{2,1,0:T(8,128)S(1)}, u32[]{:S(2)}, u32[]{:S(2)}) collective-permute-start(f32[2,48,864]{2,1,0:T(8,128)S(1)} %get-tuple-element.78), channel_id=1, source_target_pairs={{0,2},{1,3},{2,0},{3,1},{4,6},{5,7},{6,4},{7,5},{8,10},{9,11},{10,... | collective-permute-start | bytes 995336 | tf_op jit(solution)/shard_map/ppermute | solution.py:559
  98.6 11.6 %copy-start.13 = (bf16[2,64,1152]{2,1,0:T(8,128)(2,1)}, bf16[2,64,1152]{2,1,0:T(8,128)(2,1)S(1)}, u32[]{:S(2)}) copy-start(bf16[2,64,1152]{2,1,0:T(8,128)(2,1)S(1)} %collective-permute-done.20.refs_3_) | copy-start | bytes 884740
  99.9 10.2 %copy-start.14 = (bf16[2,64,1152]{2,1,0:T(8,128)(2,1)}, bf16[2,64,1152]{2,1,0:T(8,128)(2,1)S(1)}, u32[]{:S(2)}) copy-start(bf16[2,64,1152]{2,1,0:T(8,128)(2,1)S(1)} %collective-permute-done.21.refs_4_) | copy-start | bytes 884740
  99.9 10.2 %copy-start.15 = (bf16[2,64,1152]{2,1,0:T(8,128)(2,1)}, bf16[2,64,1152]{2,1,0:T(8,128)(2,1)S(1)}, u32[]{:S(2)}) copy-start(bf16[2,64,1152]{2,1,0:T(8,128)(2,1)S(1)} %collective-permute-done.22.refs_5_) | copy-start | bytes 884740
  99.9 10.2 %collective-permute-start.23 = (bf16[2,64,1152]{2,1,0:T(8,128)(2,1)}, bf16[2,64,1152]{2,1,0:T(8,128)(2,1)S(1)}, u32[]{:S(2)}, u32[]{:S(2)}) collective-permute-start(bf16[2,64,1152]{2,1,0:T(8,128)(2,1)} %get-tuple-element.87), channel_id=1, source_target_pairs={{0,1},{1,0},{2,3},{3,2},{4,5},{5,4},{6,7},{7,6},{8,9},{9,8},{10,11... | collective-permute-start | bytes 884744 | tf_op jit(solution)/shard_map/ppermute | solution.py:440
  101.4 16.2 %collective-permute-start.26 = (bf16[2,64,1152]{2,1,0:T(8,128)(2,1)}, bf16[2,64,1152]{2,1,0:T(8,128)(2,1)S(1)}, u32[]{:S(2)}, u32[]{:S(2)}) collective-permute-start(bf16[2,64,1152]{2,1,0:T(8,128)(2,1)} %get-tuple-element.95), channel_id=1, source_target_pairs={{0,16},{1,17},{2,18},{3,19},{4,20},{5,21},{6,22},{7,23},{8,24},{9,... | collective-permute-start | bytes 884744 | tf_op jit(solution)/shard_map/ppermute | solution.py:440
  101.6 16.0 %collective-permute-start.27 = (bf16[2,64,1152]{2,1,0:T(8,128)(2,1)}, bf16[2,64,1152]{2,1,0:T(8,128)(2,1)S(1)}, u32[]{:S(2)}, u32[]{:S(2)}) collective-permute-start(bf16[2,64,1152]{2,1,0:T(8,128)(2,1)} %get-tuple-element.96), channel_id=1, source_target_pairs={{0,17},{1,16},{2,19},{3,18},{4,21},{5,20},{6,23},{7,22},{8,25},{9,... | collective-permute-start | bytes 884744 | tf_op jit(solution)/shard_map/ppermute | solution.py:440
  103.5 14.2 %collective-permute-start.30 = (f32[1,48,864]{2,1,0:T(8,128)S(1)}, f32[1,48,864]{2,1,0:T(8,128)S(1)}, u32[]{:S(2)}, u32[]{:S(2)}) collective-permute-start(f32[1,48,864]{2,1,0:T(8,128)S(1)} %slice.47), channel_id=1, source_target_pairs={{0,4},{1,5},{2,6},{3,7},{4,0},{5,1},{6,2},{7,3},{8,12},{9,13},{10,... | collective-permute-start | bytes 497672 | tf_op jit(solution)/shard_map/ppermute | solution.py:588
  110.1 3.1 %copy-start.16 = (bf16[2,64,1152]{2,1,0:T(8,128)(2,1)}, bf16[2,64,1152]{2,1,0:T(8,128)(2,1)S(1)}, u32[]{:S(2)}) copy-start(bf16[2,64,1152]{2,1,0:T(8,128)(2,1)S(1)} %collective-permute-done.23.refs_3_) | copy-start | bytes 884740
  113.3 16.6 %collective-permute-start.24 = (bf16[64,1152]{1,0:T(8,128)(2,1)}, bf16[64,1152]{1,0:T(8,128)(2,1)S(1)}, u32[]{:S(2)}, u32[]{:S(2)}) collective-permute-start(bf16[64,1152]{1,0:T(8,128)(2,1)} %get-tuple-element.92), channel_id=1, source_target_pairs={{0,0},{1,1},{16,2},{17,3},{8,4},{9,5},{24,6},{25,7},{20,8},{21,9},... | collective-permute-start | bytes 442376 | tf_op jit(solution)/shard_map/ppermute | solution.py:444
  115.9 13.9 %collective-permute-start.25 = (bf16[64,1152]{1,0:T(8,128)(2,1)}, bf16[64,1152]{1,0:T(8,128)(2,1)S(1)}, u32[]{:S(2)}, u32[]{:S(2)}) collective-permute-start(bf16[64,1152]{1,0:T(8,128)(2,1)} %get-tuple-element.93), channel_id=1, source_target_pairs={{8,0},{9,1},{24,2},{25,3},{0,4},{1,5},{16,6},{17,7},{28,8},{29,9},... | collective-permute-start | bytes 442376 | tf_op jit(solution)/shard_map/ppermute | solution.py:444
  117.7 0.7 copy-start.17
  118.4 0.7 copy-start.18
  122.5 9.7 %collective-permute-start.28 = (bf16[64,1152]{1,0:T(8,128)(2,1)}, bf16[64,1152]{1,0:T(8,128)(2,1)S(1)}, u32[]{:S(2)}, u32[]{:S(2)}) collective-permute-start(bf16[64,1152]{1,0:T(8,128)(2,1)} %get-tuple-element.97), channel_id=1, source_target_pairs={{0,0},{1,1},{16,2},{17,3},{8,4},{9,5},{24,6},{25,7},{20,8},{21,9},... | collective-permute-start | bytes 442376 | tf_op jit(solution)/shard_map/ppermute | solution.py:444
  124.9 7.3 %collective-permute-start.29 = (bf16[64,1152]{1,0:T(8,128)(2,1)}, bf16[64,1152]{1,0:T(8,128)(2,1)S(1)}, u32[]{:S(2)}, u32[]{:S(2)}) collective-permute-start(bf16[64,1152]{1,0:T(8,128)(2,1)} %get-tuple-element.98), channel_id=1, source_target_pairs={{8,0},{9,1},{24,2},{25,3},{0,4},{1,5},{16,6},{17,7},{28,8},{29,9},... | collective-permute-start | bytes 442376 | tf_op jit(solution)/shard_map/ppermute | solution.py:444
  127.9 10.9 %collective-permute-start.31 = (f32[48,864]{1,0:T(8,128)S(1)}, f32[48,864]{1,0:T(8,128)S(1)}, u32[]{:S(2)}, u32[]{:S(2)}) collective-permute-start(f32[48,864]{1,0:T(8,128)S(1)} %bitcast.26), channel_id=1, source_target_pairs={{0,0},{1,1},{2,8},{3,9},{4,16},{5,17},{6,24},{7,25},{8,4},{9,5},{1... | collective-permute-start | bytes 497672 | tf_op jit(solution)/shard_map/ppermute | solution.py:606

commit v9 on v8

--- a/solution.py
+++ b/solution.py
@@ -61,9 +61,15 @@
         return pairs
 
     def to_plane(self, k):
-        return self.perm(
-            lambda y, c, z, x: ((z % self.ny) ^ c, (z // self.ny) ^ k, c * self.ny + y, x)
-        )
+        def move(y, c, z, x):
+            half = (z // self.ny) ^ k
+            plane = ((y // self.nc) * self.nc + c) * self.nc + half
+            return (z % self.ny) ^ c, y % self.nc, plane, x
+
+        return self.perm(move)
+
+    def unit(self, c, z):
+        return (z // (self.nc * self.nc)) * self.nc + c, (z // self.nc) % self.nc, z % self.nc
 
     def from_plane(self, k):
         return [(target, source) for source, target in self.to_plane(k)]
@@ -120,7 +126,8 @@
 def slot_scalars(lay, pos_ref, info_ref, slot):
     k, j = slot
     ky, kx = lay.chip_of(k)
-    z_frame = (pos_ref[1] ^ j) * lay.ny + (pos_ref[0] ^ ky ^ (pos_ref[2] // lay.ny))
+    _, group_c, half = lay.unit(pos_ref[1], pos_ref[2])
+    z_frame = (half ^ j) * lay.ny + (pos_ref[0] ^ ky ^ group_c)
     frame = z_frame * lay.nx + (pos_ref[3] ^ kx)
     clip = info_ref[frame]
     clips = (info_ref.shape[0] - lay.frames) // 2
@@ -221,7 +228,7 @@
     pair_refs, (mod_ref, hid_ref, gp_ref) = refs[: 2 * lay.nc], refs[2 * lay.nc :]
     _, step_patches, model = hid_ref.shape
     patches = step_patches * pl.num_programs(0)
-    patch_base = pos_ref[1] * patches + pl.program_id(0) * step_patches
+    patch_base = lay.unit(pos_ref[1], pos_ref[2])[2] * patches + pl.program_id(0) * step_patches
     patch = patch_base + lax.broadcasted_iota(jnp.int32, (step_patches, 1), 0)
     for t, (k, j) in enumerate(lay.slots()):
         _, limit, step = slot_scalars(lay, pos_ref, info_ref, (k, j))
@@ -261,7 +268,7 @@
             ref[h] = triple[:, n * cols : (n + 1) * cols].astype(BF16).reshape(ref.shape[1:])
 
     for b in range(step_patches // BLOCK):
-        patch_base = pos_ref[1] * patches + pl.program_id(0) * step_patches + b * BLOCK
+        patch_base = lay.unit(pos_ref[1], pos_ref[2])[2] * patches + pl.program_id(0) * step_patches + b * BLOCK
         allowed = allowed_pairs(lay, pos_ref, info_ref, patch_base)
         outputs = []
         for h in range(lay.halves):
@@ -320,7 +327,7 @@
         fill_weights(lay, pos_ref, w_refs, w_scr)
 
     for b in range(step_patches // BLOCK):
-        patch_base = pos_ref[1] * patches + pl.program_id(0) * step_patches + b * BLOCK
+        patch_base = lay.unit(pos_ref[1], pos_ref[2])[2] * patches + pl.program_id(0) * step_patches + b * BLOCK
         allowed = allowed_pairs(lay, pos_ref, info_ref, patch_base)
         for h in range(lay.halves):
             queries, keys, values = (patch_blocks(ref[h], b) for ref in (q_ref, k_ref, v_ref))
@@ -351,7 +358,7 @@
     mod_ref, *out_refs = refs
     step_patches, model = out_refs[0].shape
     patches = step_patches * pl.num_programs(0)
-    patch_base = pos_ref[1] * patches + pl.program_id(0) * step_patches
+    patch_base = lay.unit(pos_ref[1], pos_ref[2])[2] * patches + pl.program_id(0) * step_patches
     patch = patch_base + lax.broadcasted_iota(jnp.int32, (step_patches, 1), 0)
     for j in range(lay.nc):
         _, limit, step = slot_scalars(lay, pos_ref, info_ref, (0, j))
@@ -451,7 +458,7 @@
     info = [by_core] + [
         lax.ppermute(by_core, AXES, lay.swap(ky=ky)) for ky in range(1, lay.ny)
     ]
-    group_y, group_c = z % lay.ny, z // lay.ny
+    group_y, group_c, _ = lay.unit(c, z)
     info = sum(
         jnp.where((y ^ ky == group_y) & (c ^ kc == group_c), info[ky][kc], 0)
         for ky in range(lay.ny)
@@ -483,15 +490,13 @@
     w_pieces = {0: w_own}
     for bit in lay.bits(lay.nz):
         w_pieces[bit] = lax.ppermute(w_own, AXES, lay.swap(kz=bit))
-    early = [w_pieces[bit] for bit in lay.bits(lay.nz)]
     for k in range(1, lay.nz):
         if k not in w_pieces:
             bit = k & -k
             w_pieces[k] = lax.ppermute(w_pieces[k ^ bit], AXES, lay.swap(kz=bit))
     w_pieces = [w_pieces[k] for k in range(lay.nz)]
-    late = w_pieces[-1]
     if halves > 1:
-        w_pieces += [lax.ppermute(piece, AXES, lay.swap(kc=1)) for piece in w_pieces]
+        w_pieces += [lax.ppermute(piece, AXES, lay.swap(kc=1)) for piece in w_pieces[:-1]]
 
     late_w_out, _ = lax.optimization_barrier((w_out, own))
     wo_own = lax.ppermute(late_w_out, AXES, lay.rows_to_chip())
@@ -499,7 +504,7 @@
     pairs = []
     for j in range(nc):
         pairs += doubling(own[j], lay.chip_bits(j), chip_swap, info)
-    pairs, _ = lax.optimization_barrier((pairs, [late, wo_own] + w_pieces[lay.nz : -1]))
+    pairs, _ = lax.optimization_barrier((pairs, w_pieces[lay.nz :]))
 
 
     def spread(count, width, patches_at_once):
@@ -512,7 +517,7 @@
     few_steps = half // few
     x_spec = pl.BlockSpec((few, model), lambda i, *_: (i, 0))
     triple_spec = pl.BlockSpec((halves, lay.frames, step_patches, cols), lambda i, *_: (0, 0, i, 0))
-    w_specs = [whole_spec(piece.shape) for piece in w_pieces]
+    w_specs = [whole_spec(w_own.shape)] * (halves * lay.nz)
     w_scratch = pltpu.VMEM((halves, model, 3 * cols), BF16)
     mod_spec = whole_spec(mod_table.shape)
     triple_shape = struct((halves, lay.frames, half, cols))
@@ -528,7 +533,11 @@
         [struct((lay.frames, half, model))] * 2,
         grid=(few_steps,),
     )(pos, info, *pairs, mod_table)
+    wo_own, w_last, _ = lax.optimization_barrier((wo_own, w_pieces[lay.nz - 1], hidden))
     wo_rows = [wo_own, lax.ppermute(wo_own, AXES, lay.swap(kc=1))]
+    w_pieces[lay.nz - 1] = w_last
+    if halves > 1:
+        w_pieces.append(lax.ppermute(w_last, AXES, lay.swap(kc=1)))
 
     fold = 3 if rows % 24 == 0 else 1
     piece_shape = (groups, rows // fold, quarter * fold)

time: 140 us -> 144 us (1.029)
  the two profiles are of different devices: /device:TPU:4 before, /device:TPU:1 now
where the time goes in v9:
time: 144 us; the launch traced here: 143 us
  starting transfers between devices  50.4 us (35%)
  waiting for transfers between devices  46.3 us (32%)
  Pallas kernels  35.3 us (25%)
  other arithmetic  5.94 us (4%)
  local copies, waits for them, and re-layouts  4.02 us (3%)
    ppermute x4, starting transfers between devices, from_plane(): lax.ppermute(part, AXES, lay.from_plane(k))  16 us
    pallas_call x1, Pallas kernels, local(): call(functools.partial(forward_kernel, lay), 'forward', 14 * model * 1000...  11.3 us
    ppermute x2, waiting for transfers between devices, local(): w_pieces[bit] = lax.ppermute(w_own, AXES, lay.swap(kz=bit))  10.4 us
    ppermute x6, starting transfers between devices, over_chips(): got = [lax.ppermute(parts[k], AXES, chip_swap(k)) for k in range(1, chips)]  9.85 us
    pallas_call x1, Pallas kernels, local(): call(functools.partial(backward_kernel, lay), 'backward', 10 * model * 10...  9.72 us
    ppermute x2, waiting for transfers between devices, local(): lax.ppermute(pair, AXES, lay.to_plane(k))  9.7 us
    ppermute x2, starting transfers between devices, local(): lax.ppermute(pair, AXES, lay.to_plane(k))  8.43 us
    ppermute x2, waiting for transfers between devices, doubling(): held = jnp.concatenate([held, lax.ppermute(held, AXES, swap(bit))], axis=0)  8.13 us
  transfers between devices with their start and end apart: 32, of which 11 were waited for; matrix products, arithmetic and copies ran while one was open for 3% of the time, Pallas kernels for 14%

profile of v9, /device:TPU:1, one launch (start us, length us, event | category | flops | bytes accessed | tf_op | source)
XLA Modules:
  0.0 143.1 jit_solution(17456832330310888716)
XLA Ops:
  0.6 0.6 pad_add_fusion.1.pos_ref
  1.2 3.4 %start.1 = (bf16[1,2,64,1152]{3,2,1,0:T(8,128)(2,1)}, bf16[1,2,64,1152]{3,2,1,0:T(8,128)(2,1)}, bf16[144,432]{1,0:T(8,128)(2,1)}, bf16[144,432]{1,0:T(8,128)(2,1)}) custom-call(s32[4]{0:T(128)} %pad_add_fusion.1.pos_ref, bf16[1,128,1152]{2,1,0:T(8,128)(2,1)} %x_ref.1, bf16[1,128,1152]{2,1,0:T(8,128)(2,1)} %g_ref.1, bf16[144,3456]{1,0:T(8,128)(2,1)} %w_ref.1), custom_call_target="tpu_custom_call" | custom-call | flops 1179648000 | bytes 2359296 | tf_op jit(solution)/shard_map/start/pallas_call | solution.py:469
  4.7 2.0 %collective-permute-start.3 = (bf16[144,432]{1,0:T(8,128)(2,1)}, bf16[144,432]{1,0:T(8,128)(2,1)S(1)}, u32[]{:S(2)}, u32[]{:S(2)}) collective-permute-start(bf16[144,432]{1,0:T(8,128)(2,1)} %get-tuple-element.57), channel_id=1, source_target_pairs={{0,1},{1,0},{2,3},{3,2},{4,5},{5,4},{6,7},{7,6},{8,9},{9,8},{10,11... | collective-permute-start | bytes 373256 | tf_op jit(solution)/shard_map/ppermute | solution.py:481
  6.7 0.1 fusion.7
  6.8 0.9 collective-permute-start
  7.7 5.1 %collective-permute-start.2 = (bf16[1,2,64,1152]{3,2,1,0:T(8,128)(2,1)}, bf16[1,2,64,1152]{3,2,1,0:T(8,128)(2,1)S(1)}, u32[]{:S(2)}, u32[]{:S(2)}) collective-permute-start(bf16[1,2,64,1152]{3,2,1,0:T(8,128)(2,1)} %get-tuple-element.55), channel_id=1, source_target_pairs={{0,0},{1,1},{2,16},{3,17},{4,2},{5,3},{6,18},{7,19},{8,20},{9,21},... | collective-permute-start | bytes 884744 | tf_op jit(solution)/shard_map/ppermute | solution.py:479
  12.8 3.3 %collective-permute-start.4 = (bf16[1,2,64,1152]{3,2,1,0:T(8,128)(2,1)}, bf16[1,2,64,1152]{3,2,1,0:T(8,128)(2,1)S(1)}, u32[]{:S(2)}, u32[]{:S(2)}) collective-permute-start(bf16[1,2,64,1152]{3,2,1,0:T(8,128)(2,1)} %get-tuple-element.59), channel_id=1, source_target_pairs={{0,2},{1,3},{2,18},{3,19},{4,0},{5,1},{6,16},{7,17},{8,22},{9,23},... | collective-permute-start | bytes 884744 | tf_op jit(solution)/shard_map/ppermute | solution.py:479
  16.2 0.9 broadcast_select_fusion.1
  17.2 0.1 pad_maximum_fusion.2.refs_0_
  17.3 0.7 collective-permute-done.2.refs_0_
  18.0 0.3 collective-permute-start.9
  18.3 0.1 collective-permute-start.1
  18.4 9.0 %collective-permute-done.4.refs_1_ = bf16[1,2,64,1152]{3,2,1,0:T(8,128)(2,1)S(1)} collective-permute-done((bf16[1,2,64,1152]{3,2,1,0:T(8,128)(2,1)}, bf16[1,2,64,1152]{3,2,1,0:T(8,128)(2,1)S(1)}, u32[]{:S(2)}, u32[]{:S(2)}) %collective-permute-start.4) | collective-permute-done | bytes 294944 | tf_op jit(solution)/shard_map/ppermute | solution.py:479
  27.4 0.6 fusion.2.info_ref
  28.0 0.1 pad_maximum_fusion.refs_0_
  28.1 8.1 %collective-permute-done.11 = bf16[1,2,64,1152]{3,2,1,0:T(8,128)(2,1)S(1)} collective-permute-done((bf16[1,2,64,1152]{3,2,1,0:T(8,128)(2,1)S(1)}, bf16[1,2,64,1152]{3,2,1,0:T(8,128)(2,1)S(1)}, u32[]{:S(2)}, u32[]{:S(2)}) %collective-permute-start.11) | collective-permute-done | bytes 294944 | tf_op jit(solution)/shard_map/ppermute | solution.py:442
  36.3 0.3 collective-permute-start.12
  36.6 0.1 collective-permute-start.10
  36.8 1.9 %collective-permute-start.5 = (bf16[144,864]{1,0:T(8,128)(2,1)S(1)}, bf16[144,864]{1,0:T(8,128)(2,1)S(1)}, u32[]{:S(2)}, u32[]{:S(2)}) collective-permute-start(bf16[144,864]{1,0:T(8,128)(2,1)S(1)} %pad_maximum_fusion.2.refs_0_), channel_id=1, source_target_pairs={{0,2},{1,3},{2,0},{3,1},{4,6},{5,7},{6,4},{7,5},{8,10},{9,11},{10,... | collective-permute-start | bytes 746504 | tf_op jit(solution)/shard_map/ppermute | solution.py:492
  38.6 1.6 %collective-permute-start.13 = (bf16[144,864]{1,0:T(8,128)(2,1)S(1)}, bf16[144,864]{1,0:T(8,128)(2,1)S(1)}, u32[]{:S(2)}, u32[]{:S(2)}) collective-permute-start(bf16[144,864]{1,0:T(8,128)(2,1)S(1)} %pad_maximum_fusion.2.refs_0_), channel_id=1, source_target_pairs={{0,8},{1,9},{2,10},{3,11},{4,12},{5,13},{6,14},{7,15},{8,0},{9,1},... | collective-permute-start | bytes 746504 | tf_op jit(solution)/shard_map/ppermute | solution.py:499
  40.2 10.4 %collective-permute-done.6.refs_2_ = bf16[144,864]{1,0:T(8,128)(2,1)S(1)} collective-permute-done((bf16[144,864]{1,0:T(8,128)(2,1)S(1)}, bf16[144,864]{1,0:T(8,128)(2,1)S(1)}, u32[]{:S(2)}, u32[]{:S(2)}) %collective-permute-start.6) | collective-permute-done | bytes 248864 | tf_op jit(solution)/shard_map/ppermute | solution.py:492
  50.6 0.6 collective-permute-start.15
  51.2 0.2 collective-permute-start.14
  51.3 2.1 %collective-permute-start.7 = (bf16[144,1152]{1,0:T(8,128)(2,1)S(1)}, bf16[144,1152]{1,0:T(8,128)(2,1)S(1)}, u32[]{:S(2)}, u32[]{:S(2)}) collective-permute-start(bf16[144,1152]{1,0:T(8,128)(2,1)S(1)} %copy-done.10), channel_id=1, source_target_pairs={{0,0},{1,1},{2,18},{3,19},{4,8},{5,9},{6,26},{7,27},{8,4},{9,5},{1... | collective-permute-start | bytes 995336 | tf_op jit(solution)/shard_map/ppermute | solution.py:502
  53.5 3.3 %collective-permute-start.8 = (bf16[144,864]{1,0:T(8,128)(2,1)S(1)}, bf16[144,864]{1,0:T(8,128)(2,1)S(1)}, u32[]{:S(2)}, u32[]{:S(2)}) collective-permute-start(bf16[144,864]{1,0:T(8,128)(2,1)S(1)} %collective-permute-done.6.refs_2_), channel_id=1, source_target_pairs={{0,2},{1,3},{2,0},{3,1},{4,6},{5,7},{6,4},{7,5},{8,10},{9,11},{10,... | collective-permute-start | bytes 746504 | tf_op jit(solution)/shard_map/ppermute | solution.py:496
  56.8 0.8 copy-done.8
  57.7 0.8 copy-done.9
  58.5 4.4 %prepare.1 = (bf16[8,64,1152]{2,1,0:T(8,128)(2,1)}, bf16[8,64,1152]{2,1,0:T(8,128)(2,1)}) custom-call(s32[4]{0:T(128)} %pad_add_fusion.1.pos_ref, s32[16]{0:T(128)} %fusion.2.info_ref, bf16[2,2,64,1152]{3,2,1,0:T(8,128)(2,1)} %copy-done, bf16[2,2,64,1152]{3,2,1,0:T(8,128)(2,1)} %copy-done.9, bf16[2,2,64,1152]{3,2,1,0:T(8,128)(2,1)} %copy-done.1, ...), custom_call_target="tpu_custom_call" | custom-call | flops 1769472000 | bytes 2359296 | tf_op jit(solution)/shard_map/prepare/pallas_call | solution.py:527
  62.8 2.2 %collective-permute-done.8.refs_3_ = bf16[144,864]{1,0:T(8,128)(2,1)S(1)} collective-permute-done((bf16[144,864]{1,0:T(8,128)(2,1)S(1)}, bf16[144,864]{1,0:T(8,128)(2,1)S(1)}, u32[]{:S(2)}, u32[]{:S(2)}) %collective-permute-start.8) | collective-permute-done | bytes 248864 | tf_op jit(solution)/shard_map/ppermute | solution.py:496
  65.0 0.1 collective-permute-start.17
  65.1 0.5 collective-permute-start.16
  65.6 1.5 %collective-permute-done.16.refs_7_ = bf16[144,864]{1,0:T(8,128)(2,1)S(1)} collective-permute-done((bf16[144,864]{1,0:T(8,128)(2,1)S(1)}, bf16[144,864]{1,0:T(8,128)(2,1)S(1)}, u32[]{:S(2)}, u32[]{:S(2)}) %collective-permute-start.16) | collective-permute-done | bytes 248864 | tf_op jit(solution)/shard_map/ppermute | solution.py:540
  67.2 0.6 copy-done.25
  67.8 0.1 copy-done.12
  67.9 11.3 %forward.1 = (bf16[2,8,64,144]{3,2,1,0:T(8,128)(2,1)}, bf16[2,8,64,144]{3,2,1,0:T(8,128)(2,1)}, bf16[2,8,64,144]{3,2,1,0:T(8,128)(2,1)}, bf16[2,8,64,144]{3,2,1,...) custom-call(s32[4]{0:T(128)} %pad_add_fusion.1.pos_ref, ...), custom_call_target="tpu_custom_call" | custom-call | flops 8257536000 | bytes 2359296 | tf_op jit(solution)/shard_map/forward/pallas_call | solution.py:544
  79.3 0.1 collective-permute-start.18
  79.4 1.2 collective-permute-start.20
  80.6 6.0 %collective-permute-start.21 = (bf16[2,64,1152]{2,1,0:T(8,128)(2,1)}, bf16[2,64,1152]{2,1,0:T(8,128)(2,1)S(1)}, u32[]{:S(2)}, u32[]{:S(2)}) collective-permute-start(bf16[2,64,1152]{2,1,0:T(8,128)(2,1)} %get-tuple-element.85), channel_id=1, source_target_pairs={{0,16},{1,17},{2,18},{3,19},{4,20},{5,21},{6,22},{7,23},{8,24},{9,... | collective-permute-start | bytes 884744 | tf_op jit(solution)/shard_map/ppermute | solution.py:447
  86.6 1.2 slice_add_fusion
  87.8 0.1 collective-permute-start.19
  87.8 9.7 %backward.1 = (f32[2,64,1152]{2,1,0:T(8,128)}, bf16[2,64,1152]{2,1,0:T(8,128)(2,1)}, bf16[2,64,1152]{2,1,0:T(8,128)(2,1)}, bf16[2,64,1152]{2,1,0:T(8,128)(2,1)}) custom-call(s32[4]{0:T(128)} %pad_add_fusion.1.pos_ref, s32[16]{0:T(128)} %fusion.2.info_ref, bf16[144,864]{1,0:T(8,128)(2,1)} %copy-done.4, bf16[144,864]{1,0:T(8,128)(2,1)} %copy-done.20, ...), custom_call_target="tpu_custom_call" | custom-call | flops 5898240000 | bytes 2359296 | tf_op jit(solution)/shard_map/backward/pallas_call | solution.py:570
  97.6 1.6 %collective-permute-done.21.refs_4_ = bf16[2,64,1152]{2,1,0:T(8,128)(2,1)S(1)} collective-permute-done((bf16[2,64,1152]{2,1,0:T(8,128)(2,1)}, bf16[2,64,1152]{2,1,0:T(8,128)(2,1)S(1)}, u32[]{:S(2)}, u32[]{:S(2)}) %collective-permute-start.21) | collective-permute-done | bytes 294944 | tf_op jit(solution)/shard_map/ppermute | solution.py:447
  99.2 0.9 collective-permute-done.22.refs_5_
  100.1 1.2 collective-permute-start.23
  101.3 0.3 collective-permute-start.26
  101.6 1.1 collective-permute-start.27
  102.8 0.1 collective-permute-start.30
  102.9 5.0 %collective-permute-done.23.refs_3_ = bf16[2,64,1152]{2,1,0:T(8,128)(2,1)S(1)} collective-permute-done((bf16[2,64,1152]{2,1,0:T(8,128)(2,1)}, bf16[2,64,1152]{2,1,0:T(8,128)(2,1)S(1)}, u32[]{:S(2)}, u32[]{:S(2)}) %collective-permute-start.23) | collective-permute-done | bytes 294944 | tf_op jit(solution)/shard_map/ppermute | solution.py:447
  107.9 3.1 %output.1 = (bf16[64,1152]{1,0:T(8,128)(2,1)}, bf16[64,1152]{1,0:T(8,128)(2,1)}) custom-call(s32[4]{0:T(128)} %pad_add_fusion.1.pos_ref, s32[16]{0:T(128)} %fusion.2.info_ref, bf16[1,2,64,1152]{3,2,1,0:T(8,128)(2,1)} %copy-done.2, bf16[1,2,64,1152]{3,2,1,0:T(8,128)(2,1)} %copy-done.3, f32[2,64,1152]{2,1,0:T(8,128)} %get-tuple-element.92.refs_2_, ...), custom_call_target="tpu_custom_call" | custom-call | flops 1769472000 | bytes 2359296 | tf_op jit(solution)/shard_map/output/pallas_call | solution.py:584
  111.0 6.7 %collective-permute-start.24 = (bf16[64,1152]{1,0:T(8,128)(2,1)}, bf16[64,1152]{1,0:T(8,128)(2,1)S(1)}, u32[]{:S(2)}, u32[]{:S(2)}) collective-permute-start(bf16[64,1152]{1,0:T(8,128)(2,1)} %get-tuple-element.96), channel_id=1, source_target_pairs={{0,0},{1,1},{16,2},{17,3},{2,4},{3,5},{18,6},{19,7},{20,8},{21,9},... | collective-permute-start | bytes 442376 | tf_op jit(solution)/shard_map/ppermute | solution.py:451
  117.7 1.9 %collective-permute-start.25 = (bf16[64,1152]{1,0:T(8,128)(2,1)}, bf16[64,1152]{1,0:T(8,128)(2,1)S(1)}, u32[]{:S(2)}, u32[]{:S(2)}) collective-permute-start(bf16[64,1152]{1,0:T(8,128)(2,1)} %get-tuple-element.97), channel_id=1, source_target_pairs={{2,0},{3,1},{18,2},{19,3},{0,4},{1,5},{16,6},{17,7},{22,8},{23,9},... | collective-permute-start | bytes 442376 | tf_op jit(solution)/shard_map/ppermute | solution.py:451
  119.7 0.7 copy-done.17
  120.4 0.7 copy-done.18
  121.1 3.4 %input_grad.1 = (bf16[64,1152]{1,0:T(8,128)(2,1)}, bf16[64,1152]{1,0:T(8,128)(2,1)}) custom-call(s32[4]{0:T(128)} %pad_add_fusion.1.pos_ref, s32[16]{0:T(128)} %fusion.2.info_ref, bf16[1,2,64,1152]{3,2,1,0:T(8,128)(2,1)} %copy-done.2, bf16[1,2,64,1152]{3,2,1,0:T(8,128)(2,1)} %copy-done.3, f32[2,64,1152]{2,1,0:T(8,128)} %get-tuple-element.98.refs_2_, ...), custom_call_target="tpu_custom_call" | custom-call | flops 1769472000 | bytes 2359296 | tf_op jit(solution)/shard_map/input_grad/pallas_call | solution.py:603
  124.5 1.9 %collective-permute-start.28 = (bf16[64,1152]{1,0:T(8,128)(2,1)}, bf16[64,1152]{1,0:T(8,128)(2,1)S(1)}, u32[]{:S(2)}, u32[]{:S(2)}) collective-permute-start(bf16[64,1152]{1,0:T(8,128)(2,1)} %get-tuple-element.101), channel_id=1, source_target_pairs={{0,0},{1,1},{16,2},{17,3},{2,4},{3,5},{18,6},{19,7},{20,8},{21,9},... | collective-permute-start | bytes 442376 | tf_op jit(solution)/shard_map/ppermute | solution.py:451
  126.4 5.4 %collective-permute-start.29 = (bf16[64,1152]{1,0:T(8,128)(2,1)}, bf16[64,1152]{1,0:T(8,128)(2,1)S(1)}, u32[]{:S(2)}, u32[]{:S(2)}) collective-permute-start(bf16[64,1152]{1,0:T(8,128)(2,1)} %get-tuple-element.102), channel_id=1, source_target_pairs={{2,0},{3,1},{18,2},{19,3},{0,4},{1,5},{16,6},{17,7},{22,8},{23,9},... | collective-permute-start | bytes 442376 | tf_op jit(solution)/shard_map/ppermute | solution.py:451
  131.9 1.9 %collective-permute-start.31 = (f32[48,864]{1,0:T(8,128)S(1)}, f32[48,864]{1,0:T(8,128)S(1)}, u32[]{:S(2)}, u32[]{:S(2)}) collective-permute-start(f32[48,864]{1,0:T(8,128)S(1)} %bitcast.26), channel_id=1, source_target_pairs={{0,0},{1,1},{2,8},{3,9},{4,16},{5,17},{6,24},{7,25},{8,4},{9,5},{1... | collective-permute-start | bytes 497672 | tf_op jit(solution)/shard_map/ppermute | solution.py:615
  133.8 3.2 %collective-permute-done.29 = bf16[64,1152]{1,0:T(8,128)(2,1)S(1)} collective-permute-done((bf16[64,1152]{1,0:T(8,128)(2,1)}, bf16[64,1152]{1,0:T(8,128)(2,1)S(1)}, u32[]{:S(2)}, u32[]{:S(2)}) %collective-permute-start.29) | collective-permute-done | bytes 147488 | tf_op jit(solution)/shard_map/ppermute | solution.py:451
  137.1 0.1 broadcast_select_fusion.3
  137.1 0.7 maximum_bitcast_fusion.1
  137.9 0.7 maximum_bitcast_fusion
  138.6 3.7 %collective-permute-done.31 = f32[48,864]{1,0:T(8,128)S(1)} collective-permute-done((f32[48,864]{1,0:T(8,128)S(1)}, f32[48,864]{1,0:T(8,128)S(1)}, u32[]{:S(2)}, u32[]{:S(2)}) %collective-permute-start.31) | collective-permute-done | bytes 165920 | tf_op jit(solution)/shard_map/ppermute | solution.py:615
  142.3 0.1 fusion.6
  142.4 0.7 maximum_multiply_fusion
  (75 shorter events, 0.3 us)
Async XLA Ops:
  1.2 5.5 %copy-start.5 = (s32[1,4]{1,0:T(1,128)S(1)}, s32[1,4]{1,0:T(1,128)}, u32[]{:S(2)}) copy-start(s32[1,4]{1,0:T(1,128)} %param.12) | copy-start | bytes 52
  1.2 5.5 %copy-start.6 = (s32[1,4]{1,0:T(1,128)S(1)}, s32[1,4]{1,0:T(1,128)}, u32[]{:S(2)}) copy-start(s32[1,4]{1,0:T(1,128)} %param.11) | copy-start | bytes 52
  1.2 5.5 %copy-start.7 = (s32[1,8]{1,0:T(1,128)S(1)}, s32[1,8]{1,0:T(1,128)}, u32[]{:S(2)}) copy-start(s32[1,8]{1,0:T(1,128)} %param.10) | copy-start | bytes 100
  4.7 11.6 %collective-permute-start.3 = (bf16[144,432]{1,0:T(8,128)(2,1)}, bf16[144,432]{1,0:T(8,128)(2,1)S(1)}, u32[]{:S(2)}, u32[]{:S(2)}) collective-permute-start(bf16[144,432]{1,0:T(8,128)(2,1)} %get-tuple-element.57), channel_id=1, source_target_pairs={{0,1},{1,0},{2,3},{3,2},{4,5},{5,4},{6,7},{7,6},{8,9},{9,8},{10,11... | collective-permute-start | bytes 373256 | tf_op jit(solution)/shard_map/ppermute | solution.py:481
  6.8 11.5 %collective-permute-start = (s32[1,16]{1,0:T(1,128)S(1)}, s32[1,16]{1,0:T(1,128)S(1)}, u32[]{:S(2)}, u32[]{:S(2)}) collective-permute-start(s32[1,16]{1,0:T(1,128)S(1)} %fusion.7), channel_id=1, source_target_pairs={{0,8},{1,9},{2,10},{3,11},{4,12},{5,13},{6,14},{7,15},{8,0},{9,1},... | collective-permute-start | bytes 200 | tf_op jit(solution)/shard_map/ppermute | solution.py:457
  7.7 10.3 %collective-permute-start.2 = (bf16[1,2,64,1152]{3,2,1,0:T(8,128)(2,1)}, bf16[1,2,64,1152]{3,2,1,0:T(8,128)(2,1)S(1)}, u32[]{:S(2)}, u32[]{:S(2)}) collective-permute-start(bf16[1,2,64,1152]{3,2,1,0:T(8,128)(2,1)} %get-tuple-element.55), channel_id=1, source_target_pairs={{0,0},{1,1},{2,16},{3,17},{4,2},{5,3},{6,18},{7,19},{8,20},{9,21},... | collective-permute-start | bytes 884744 | tf_op jit(solution)/shard_map/ppermute | solution.py:479
  12.8 14.5 %collective-permute-start.4 = (bf16[1,2,64,1152]{3,2,1,0:T(8,128)(2,1)}, bf16[1,2,64,1152]{3,2,1,0:T(8,128)(2,1)S(1)}, u32[]{:S(2)}, u32[]{:S(2)}) collective-permute-start(bf16[1,2,64,1152]{3,2,1,0:T(8,128)(2,1)} %get-tuple-element.59), channel_id=1, source_target_pairs={{0,2},{1,3},{2,18},{3,19},{4,0},{5,1},{6,16},{7,17},{8,22},{9,23},... | collective-permute-start | bytes 884744 | tf_op jit(solution)/shard_map/ppermute | solution.py:479
  17.3 21.3 %copy-start.4 = (bf16[144,864]{1,0:T(8,128)(2,1)}, bf16[144,864]{1,0:T(8,128)(2,1)S(1)}, u32[]{:S(2)}) copy-start(bf16[144,864]{1,0:T(8,128)(2,1)S(1)} %pad_maximum_fusion.2.refs_0_) | copy-start | bytes 746500
  18.0 18.2 %copy-start.2 = (bf16[1,2,64,1152]{3,2,1,0:T(8,128)(2,1)}, bf16[1,2,64,1152]{3,2,1,0:T(8,128)(2,1)S(1)}, u32[]{:S(2)}) copy-start(bf16[1,2,64,1152]{3,2,1,0:T(8,128)(2,1)S(1)} %collective-permute-done.2.refs_0_) | copy-start | bytes 884740
  18.0 10.0 %collective-permute-start.9 = (bf16[1,2,64,1152]{3,2,1,0:T(8,128)(2,1)S(1)}, bf16[1,2,64,1152]{3,2,1,0:T(8,128)(2,1)S(1)}, u32[]{:S(2)}, u32[]{:S(2)}) collective-permute-start(bf16[1,2,64,1152]{3,2,1,0:T(8,128)(2,1)S(1)} %collective-permute-done.2.refs_0_), channel_id=1, source_target_pairs={{0,1},{1,0},{2,3},{3,2},{4,5},{5,4},{6,7},{7,6},{8,9},{9,8},{10,11... | collective-permute-start | bytes 884744 | tf_op jit(solution)/shard_map/ppermute | solution.py:442
  18.3 9.1 %collective-permute-start.1 = (s32[2,16]{1,0:T(2,128)S(1)}, s32[2,16]{1,0:T(2,128)S(1)}, u32[]{:S(2)}, u32[]{:S(2)}) collective-permute-start(s32[2,16]{1,0:T(2,128)S(1)} %pad_add_fusion), channel_id=1, source_target_pairs={{0,16},{1,17},{2,18},{3,19},{4,20},{5,21},{6,22},{7,23},{8,24},{9,... | collective-permute-start | bytes 392 | tf_op jit(solution)/shard_map/ppermute | solution.py:459
  27.4 8.9 %copy-start.3 = (bf16[1,2,64,1152]{3,2,1,0:T(8,128)(2,1)}, bf16[1,2,64,1152]{3,2,1,0:T(8,128)(2,1)S(1)}, u32[]{:S(2)}) copy-start(bf16[1,2,64,1152]{3,2,1,0:T(8,128)(2,1)S(1)} %collective-permute-done.4.refs_1_) | copy-start | bytes 884740
  27.4 8.9 %collective-permute-start.11 = (bf16[1,2,64,1152]{3,2,1,0:T(8,128)(2,1)S(1)}, bf16[1,2,64,1152]{3,2,1,0:T(8,128)(2,1)S(1)}, u32[]{:S(2)}, u32[]{:S(2)}) collective-permute-start(bf16[1,2,64,1152]{3,2,1,0:T(8,128)(2,1)S(1)} %collective-permute-done.4.refs_1_), channel_id=1, source_target_pairs={{0,16},{1,17},{2,18},{3,19},{4,20},{5,21},{6,22},{7,23},{8,24},{9,... | collective-permute-start | bytes 884744 | tf_op jit(solution)/shard_map/ppermute | solution.py:442
  28.0 23.3 %copy-start.10 = (bf16[144,1152]{1,0:T(8,128)(2,1)S(1)}, bf16[144,1152]{1,0:T(8,128)(2,1)}, u32[]{:S(2)}) copy-start(bf16[144,1152]{1,0:T(8,128)(2,1)} %param.15) | copy-start | bytes 995332
  28.1 28.7 %copy-start = (bf16[2,2,64,1152]{3,2,1,0:T(8,128)(2,1)}, bf16[2,2,64,1152]{3,2,1,0:T(8,128)(2,1)S(1)}, u32[]{:S(2)}) copy-start(bf16[2,2,64,1152]{3,2,1,0:T(8,128)(2,1)S(1)} %pad_maximum_fusion.refs_0_) | copy-start | bytes 1769476
  36.3 20.5 %copy-start.1 = (bf16[2,2,64,1152]{3,2,1,0:T(8,128)(2,1)}, bf16[2,2,64,1152]{3,2,1,0:T(8,128)(2,1)S(1)}, u32[]{:S(2)}) copy-start(bf16[2,2,64,1152]{3,2,1,0:T(8,128)(2,1)S(1)} %pad_maximum_fusion.1.refs_2_) | copy-start | bytes 1769476
  36.3 20.5 %collective-permute-start.12 = (bf16[2,2,64,1152]{3,2,1,0:T(8,128)(2,1)S(1)}, bf16[2,2,64,1152]{3,2,1,0:T(8,128)(2,1)S(1)}, u32[]{:S(2)}, u32[]{:S(2)}) collective-permute-start(bf16[2,2,64,1152]{3,2,1,0:T(8,128)(2,1)S(1)} %pad_maximum_fusion.1.refs_2_), channel_id=1, source_target_pairs={{0,1},{1,0},{2,3},{3,2},{4,5},{5,4},{6,7},{7,6},{8,9},{9,8},{10,11... | collective-permute-start | bytes 1769480 | tf_op jit(solution)/shard_map/ppermute | solution.py:444
  36.6 20.2 %collective-permute-start.10 = (bf16[2,2,64,1152]{3,2,1,0:T(8,128)(2,1)S(1)}, bf16[2,2,64,1152]{3,2,1,0:T(8,128)(2,1)S(1)}, u32[]{:S(2)}, u32[]{:S(2)}) collective-permute-start(bf16[2,2,64,1152]{3,2,1,0:T(8,128)(2,1)S(1)} %pad_maximum_fusion.refs_0_), channel_id=1, source_target_pairs={{0,16},{1,17},{2,18},{3,19},{4,20},{5,21},{6,22},{7,23},{8,24},{9,... | collective-permute-start | bytes 1769480 | tf_op jit(solution)/shard_map/ppermute | solution.py:444
  36.8 13.8 %collective-permute-start.6 = (bf16[144,864]{1,0:T(8,128)(2,1)S(1)}, bf16[144,864]{1,0:T(8,128)(2,1)S(1)}, u32[]{:S(2)}, u32[]{:S(2)}) collective-permute-start(bf16[144,864]{1,0:T(8,128)(2,1)S(1)} %pad_maximum_fusion.2.refs_0_), channel_id=1, source_target_pairs={{0,4},{1,5},{2,6},{3,7},{4,0},{5,1},{6,2},{7,3},{8,12},{9,13},{10,... | collective-permute-start | bytes 746504 | tf_op jit(solution)/shard_map/ppermute | solution.py:492
  36.8 14.4 %collective-permute-start.5 = (bf16[144,864]{1,0:T(8,128)(2,1)S(1)}, bf16[144,864]{1,0:T(8,128)(2,1)S(1)}, u32[]{:S(2)}, u32[]{:S(2)}) collective-permute-start(bf16[144,864]{1,0:T(8,128)(2,1)S(1)} %pad_maximum_fusion.2.refs_0_), channel_id=1, source_target_pairs={{0,2},{1,3},{2,0},{3,1},{4,6},{5,7},{6,4},{7,5},{8,10},{9,11},{10,... | collective-permute-start | bytes 746504 | tf_op jit(solution)/shard_map/ppermute | solution.py:492
  38.6 12.7 %collective-permute-start.13 = (bf16[144,864]{1,0:T(8,128)(2,1)S(1)}, bf16[144,864]{1,0:T(8,128)(2,1)S(1)}, u32[]{:S(2)}, u32[]{:S(2)}) collective-permute-start(bf16[144,864]{1,0:T(8,128)(2,1)S(1)} %pad_maximum_fusion.2.refs_0_), channel_id=1, source_target_pairs={{0,8},{1,9},{2,10},{3,11},{4,12},{5,13},{6,14},{7,15},{8,0},{9,1},... | collective-permute-start | bytes 746504 | tf_op jit(solution)/shard_map/ppermute | solution.py:499
  50.6 16.5 %copy-start.19 = (bf16[144,864]{1,0:T(8,128)(2,1)}, bf16[144,864]{1,0:T(8,128)(2,1)S(1)}, u32[]{:S(2)}) copy-start(bf16[144,864]{1,0:T(8,128)(2,1)S(1)} %collective-permute-done.6.refs_2_) | copy-start | bytes 746500
  50.6 2.8 %collective-permute-start.15 = (bf16[144,864]{1,0:T(8,128)(2,1)S(1)}, bf16[144,864]{1,0:T(8,128)(2,1)S(1)}, u32[]{:S(2)}, u32[]{:S(2)}) collective-permute-start(bf16[144,864]{1,0:T(8,128)(2,1)S(1)} %collective-permute-done.6.refs_2_), channel_id=1, source_target_pairs={{0,8},{1,9},{2,10},{3,11},{4,12},{5,13},{6,14},{7,15},{8,0},{9,1},... | collective-permute-start | bytes 746504 | tf_op jit(solution)/shard_map/ppermute | solution.py:499
  51.2 16.0 %copy-start.20 = (bf16[144,864]{1,0:T(8,128)(2,1)}, bf16[144,864]{1,0:T(8,128)(2,1)S(1)}, u32[]{:S(2)}) copy-start(bf16[144,864]{1,0:T(8,128)(2,1)S(1)} %collective-permute-done.5.refs_1_) | copy-start | bytes 746500
  51.2 5.6 %collective-permute-start.14 = (bf16[144,864]{1,0:T(8,128)(2,1)S(1)}, bf16[144,864]{1,0:T(8,128)(2,1)S(1)}, u32[]{:S(2)}, u32[]{:S(2)}) collective-permute-start(bf16[144,864]{1,0:T(8,128)(2,1)S(1)} %collective-permute-done.5.refs_1_), channel_id=1, source_target_pairs={{0,8},{1,9},{2,10},{3,11},{4,12},{5,13},{6,14},{7,15},{8,0},{9,1},... | collective-permute-start | bytes 746504 | tf_op jit(solution)/shard_map/ppermute | solution.py:499
  51.3 15.8 %copy-start.21 = (bf16[144,864]{1,0:T(8,128)(2,1)}, bf16[144,864]{1,0:T(8,128)(2,1)S(1)}, u32[]{:S(2)}) copy-start(bf16[144,864]{1,0:T(8,128)(2,1)S(1)} %collective-permute-done.13.refs_4_) | copy-start | bytes 746500
  51.3 13.7 %collective-permute-start.7 = (bf16[144,1152]{1,0:T(8,128)(2,1)S(1)}, bf16[144,1152]{1,0:T(8,128)(2,1)S(1)}, u32[]{:S(2)}, u32[]{:S(2)}) collective-permute-start(bf16[144,1152]{1,0:T(8,128)(2,1)S(1)} %copy-done.10), channel_id=1, source_target_pairs={{0,0},{1,1},{2,18},{3,19},{4,8},{5,9},{6,26},{7,27},{8,4},{9,5},{1... | collective-permute-start | bytes 995336 | tf_op jit(solution)/shard_map/ppermute | solution.py:502
  53.4 13.7 %copy-start.22 = (bf16[144,864]{1,0:T(8,128)(2,1)}, bf16[144,864]{1,0:T(8,128)(2,1)S(1)}, u32[]{:S(2)}) copy-start(bf16[144,864]{1,0:T(8,128)(2,1)S(1)} %collective-permute-done.15.refs_6_) | copy-start | bytes 746500
  53.5 11.6 %collective-permute-start.8 = (bf16[144,864]{1,0:T(8,128)(2,1)S(1)}, bf16[144,864]{1,0:T(8,128)(2,1)S(1)}, u32[]{:S(2)}, u32[]{:S(2)}) collective-permute-start(bf16[144,864]{1,0:T(8,128)(2,1)S(1)} %collective-permute-done.6.refs_2_), channel_id=1, source_target_pairs={{0,2},{1,3},{2,0},{3,1},{4,6},{5,7},{6,4},{7,5},{8,10},{9,11},{10,... | collective-permute-start | bytes 746504 | tf_op jit(solution)/shard_map/ppermute | solution.py:496
  56.8 10.4 %copy-start.23 = (bf16[144,864]{1,0:T(8,128)(2,1)}, bf16[144,864]{1,0:T(8,128)(2,1)S(1)}, u32[]{:S(2)}) copy-start(bf16[144,864]{1,0:T(8,128)(2,1)S(1)} %collective-permute-done.14.refs_5_) | copy-start | bytes 746500
  56.8 0.9 copy-start.8
  57.6 0.8 copy-start.9
  65.0 2.1 %copy-start.24 = (bf16[144,864]{1,0:T(8,128)(2,1)}, bf16[144,864]{1,0:T(8,128)(2,1)S(1)}, u32[]{:S(2)}) copy-start(bf16[144,864]{1,0:T(8,128)(2,1)S(1)} %collective-permute-done.8.refs_3_) | copy-start | bytes 746500
  65.0 2.1 %copy-start.11 = (bf16[144,1152]{1,0:T(8,128)(2,1)}, bf16[144,1152]{1,0:T(8,128)(2,1)S(1)}, u32[]{:S(2)}) copy-start(bf16[144,1152]{1,0:T(8,128)(2,1)S(1)} %collective-permute-done.7.refs_8_) | copy-start | bytes 995332
  65.0 2.1 %collective-permute-start.17 = (bf16[144,1152]{1,0:T(8,128)(2,1)S(1)}, bf16[144,1152]{1,0:T(8,128)(2,1)S(1)}, u32[]{:S(2)}, u32[]{:S(2)}) collective-permute-start(bf16[144,1152]{1,0:T(8,128)(2,1)S(1)} %collective-permute-done.7.refs_8_), channel_id=1, source_target_pairs={{0,8},{1,9},{2,10},{3,11},{4,12},{5,13},{6,14},{7,15},{8,0},{9,1},... | collective-permute-start | bytes 995336 | tf_op jit(solution)/shard_map/ppermute | solution.py:537
  65.1 2.0 %collective-permute-start.16 = (bf16[144,864]{1,0:T(8,128)(2,1)S(1)}, bf16[144,864]{1,0:T(8,128)(2,1)S(1)}, u32[]{:S(2)}, u32[]{:S(2)}) collective-permute-start(bf16[144,864]{1,0:T(8,128)(2,1)S(1)} %collective-permute-done.8.refs_3_), channel_id=1, source_target_pairs={{0,8},{1,9},{2,10},{3,11},{4,12},{5,13},{6,14},{7,15},{8,0},{9,1},... | collective-permute-start | bytes 746504 | tf_op jit(solution)/shard_map/ppermute | solution.py:540
  67.1 0.7 copy-start.25
  67.1 0.8 copy-start.12
  79.3 7.3 %collective-permute-start.18 = (f32[4,48,864]{2,1,0:T(8,128)}, f32[4,48,864]{2,1,0:T(8,128)S(1)}, u32[]{:S(2)}, u32[]{:S(2)}) collective-permute-start(f32[4,48,864]{2,1,0:T(8,128)} %get-tuple-element.76), channel_id=1, source_target_pairs={{0,8},{1,9},{2,10},{3,11},{4,12},{5,13},{6,14},{7,15},{8,0},{9,1},... | collective-permute-start | bytes 1990664 | tf_op jit(solution)/shard_map/ppermute | solution.py:562
  79.4 18.2 %collective-permute-start.20 = (bf16[2,64,1152]{2,1,0:T(8,128)(2,1)}, bf16[2,64,1152]{2,1,0:T(8,128)(2,1)S(1)}, u32[]{:S(2)}, u32[]{:S(2)}) collective-permute-start(bf16[2,64,1152]{2,1,0:T(8,128)(2,1)} %get-tuple-element.84), channel_id=1, source_target_pairs={{0,1},{1,0},{2,3},{3,2},{4,5},{5,4},{6,7},{7,6},{8,9},{9,8},{10,11... | collective-permute-start | bytes 884744 | tf_op jit(solution)/shard_map/ppermute | solution.py:447
  80.6 18.6 %collective-permute-start.21 = (bf16[2,64,1152]{2,1,0:T(8,128)(2,1)}, bf16[2,64,1152]{2,1,0:T(8,128)(2,1)S(1)}, u32[]{:S(2)}, u32[]{:S(2)}) collective-permute-start(bf16[2,64,1152]{2,1,0:T(8,128)(2,1)} %get-tuple-element.85), channel_id=1, source_target_pairs={{0,16},{1,17},{2,18},{3,19},{4,20},{5,21},{6,22},{7,23},{8,24},{9,... | collective-permute-start | bytes 884744 | tf_op jit(solution)/shard_map/ppermute | solution.py:447
  86.6 13.5 %collective-permute-start.22 = (bf16[2,64,1152]{2,1,0:T(8,128)(2,1)}, bf16[2,64,1152]{2,1,0:T(8,128)(2,1)S(1)}, u32[]{:S(2)}, u32[]{:S(2)}) collective-permute-start(bf16[2,64,1152]{2,1,0:T(8,128)(2,1)} %get-tuple-element.86), channel_id=1, source_target_pairs={{0,17},{1,16},{2,19},{3,18},{4,21},{5,20},{6,23},{7,22},{8,25},{9,... | collective-permute-start | bytes 884744 | tf_op jit(solution)/shard_map/ppermute | solution.py:447
  87.8 12.4 %collective-permute-start.19 = (f32[2,48,864]{2,1,0:T(8,128)S(1)}, f32[2,48,864]{2,1,0:T(8,128)S(1)}, u32[]{:S(2)}, u32[]{:S(2)}) collective-permute-start(f32[2,48,864]{2,1,0:T(8,128)S(1)} %get-tuple-element.82), channel_id=1, source_target_pairs={{0,2},{1,3},{2,0},{3,1},{4,6},{5,7},{6,4},{7,5},{8,10},{9,11},{10,... | collective-permute-start | bytes 995336 | tf_op jit(solution)/shard_map/ppermute | solution.py:568
  97.6 10.3 %copy-start.13 = (bf16[2,64,1152]{2,1,0:T(8,128)(2,1)}, bf16[2,64,1152]{2,1,0:T(8,128)(2,1)S(1)}, u32[]{:S(2)}) copy-start(bf16[2,64,1152]{2,1,0:T(8,128)(2,1)S(1)} %collective-permute-done.20.refs_3_) | copy-start | bytes 884740
  99.2 8.7 %copy-start.14 = (bf16[2,64,1152]{2,1,0:T(8,128)(2,1)}, bf16[2,64,1152]{2,1,0:T(8,128)(2,1)S(1)}, u32[]{:S(2)}) copy-start(bf16[2,64,1152]{2,1,0:T(8,128)(2,1)S(1)} %collective-permute-done.21.refs_4_) | copy-start | bytes 884740
  100.1 7.8 %copy-start.15 = (bf16[2,64,1152]{2,1,0:T(8,128)(2,1)}, bf16[2,64,1152]{2,1,0:T(8,128)(2,1)S(1)}, u32[]{:S(2)}) copy-start(bf16[2,64,1152]{2,1,0:T(8,128)(2,1)S(1)} %collective-permute-done.22.refs_5_) | copy-start | bytes 884740
  100.1 7.7 %collective-permute-start.23 = (bf16[2,64,1152]{2,1,0:T(8,128)(2,1)}, bf16[2,64,1152]{2,1,0:T(8,128)(2,1)S(1)}, u32[]{:S(2)}, u32[]{:S(2)}) collective-permute-start(bf16[2,64,1152]{2,1,0:T(8,128)(2,1)} %get-tuple-element.91), channel_id=1, source_target_pairs={{0,1},{1,0},{2,3},{3,2},{4,5},{5,4},{6,7},{7,6},{8,9},{9,8},{10,11... | collective-permute-start | bytes 884744 | tf_op jit(solution)/shard_map/ppermute | solution.py:447
  101.3 18.3 %collective-permute-start.26 = (bf16[2,64,1152]{2,1,0:T(8,128)(2,1)}, bf16[2,64,1152]{2,1,0:T(8,128)(2,1)S(1)}, u32[]{:S(2)}, u32[]{:S(2)}) collective-permute-start(bf16[2,64,1152]{2,1,0:T(8,128)(2,1)} %get-tuple-element.99), channel_id=1, source_target_pairs={{0,16},{1,17},{2,18},{3,19},{4,20},{5,21},{6,22},{7,23},{8,24},{9,... | collective-permute-start | bytes 884744 | tf_op jit(solution)/shard_map/ppermute | solution.py:447
  101.6 18.0 %collective-permute-start.27 = (bf16[2,64,1152]{2,1,0:T(8,128)(2,1)}, bf16[2,64,1152]{2,1,0:T(8,128)(2,1)S(1)}, u32[]{:S(2)}, u32[]{:S(2)}) collective-permute-start(bf16[2,64,1152]{2,1,0:T(8,128)(2,1)} %get-tuple-element.100), channel_id=1, source_target_pairs={{0,17},{1,16},{2,19},{3,18},{4,21},{5,20},{6,23},{7,22},{8,25},{9,... | collective-permute-start | bytes 884744 | tf_op jit(solution)/shard_map/ppermute | solution.py:447
  102.8 16.8 %collective-permute-start.30 = (f32[1,48,864]{2,1,0:T(8,128)S(1)}, f32[1,48,864]{2,1,0:T(8,128)S(1)}, u32[]{:S(2)}, u32[]{:S(2)}) collective-permute-start(f32[1,48,864]{2,1,0:T(8,128)S(1)} %slice.47), channel_id=1, source_target_pairs={{0,4},{1,5},{2,6},{3,7},{4,0},{5,1},{6,2},{7,3},{8,12},{9,13},{10,... | collective-permute-start | bytes 497672 | tf_op jit(solution)/shard_map/ppermute | solution.py:597
  107.9 3.1 %copy-start.16 = (bf16[2,64,1152]{2,1,0:T(8,128)(2,1)}, bf16[2,64,1152]{2,1,0:T(8,128)(2,1)S(1)}, u32[]{:S(2)}) copy-start(bf16[2,64,1152]{2,1,0:T(8,128)(2,1)S(1)} %collective-permute-done.23.refs_3_) | copy-start | bytes 884740
  111.0 22.8 %collective-permute-start.24 = (bf16[64,1152]{1,0:T(8,128)(2,1)}, bf16[64,1152]{1,0:T(8,128)(2,1)S(1)}, u32[]{:S(2)}, u32[]{:S(2)}) collective-permute-start(bf16[64,1152]{1,0:T(8,128)(2,1)} %get-tuple-element.96), channel_id=1, source_target_pairs={{0,0},{1,1},{16,2},{17,3},{2,4},{3,5},{18,6},{19,7},{20,8},{21,9},... | collective-permute-start | bytes 442376 | tf_op jit(solution)/shard_map/ppermute | solution.py:451
  117.7 16.1 %collective-permute-start.25 = (bf16[64,1152]{1,0:T(8,128)(2,1)}, bf16[64,1152]{1,0:T(8,128)(2,1)S(1)}, u32[]{:S(2)}, u32[]{:S(2)}) collective-permute-start(bf16[64,1152]{1,0:T(8,128)(2,1)} %get-tuple-element.97), channel_id=1, source_target_pairs={{2,0},{3,1},{18,2},{19,3},{0,4},{1,5},{16,6},{17,7},{22,8},{23,9},... | collective-permute-start | bytes 442376 | tf_op jit(solution)/shard_map/ppermute | solution.py:451
  119.7 0.7 copy-start.17
  120.4 0.7 copy-start.18
  124.5 9.3 %collective-permute-start.28 = (bf16[64,1152]{1,0:T(8,128)(2,1)}, bf16[64,1152]{1,0:T(8,128)(2,1)S(1)}, u32[]{:S(2)}, u32[]{:S(2)}) collective-permute-start(bf16[64,1152]{1,0:T(8,128)(2,1)} %get-tuple-element.101), channel_id=1, source_target_pairs={{0,0},{1,1},{16,2},{17,3},{2,4},{3,5},{18,6},{19,7},{20,8},{21,9},... | collective-permute-start | bytes 442376 | tf_op jit(solution)/shard_map/ppermute | solution.py:451
  126.4 10.6 %collective-permute-start.29 = (bf16[64,1152]{1,0:T(8,128)(2,1)}, bf16[64,1152]{1,0:T(8,128)(2,1)S(1)}, u32[]{:S(2)}, u32[]{:S(2)}) collective-permute-start(bf16[64,1152]{1,0:T(8,128)(2,1)} %get-tuple-element.102), channel_id=1, source_target_pairs={{2,0},{3,1},{18,2},{19,3},{0,4},{1,5},{16,6},{17,7},{22,8},{23,9},... | collective-permute-start | bytes 442376 | tf_op jit(solution)/shard_map/ppermute | solution.py:451
  131.9 10.4 %collective-permute-start.31 = (f32[48,864]{1,0:T(8,128)S(1)}, f32[48,864]{1,0:T(8,128)S(1)}, u32[]{:S(2)}, u32[]{:S(2)}) collective-permute-start(f32[48,864]{1,0:T(8,128)S(1)} %bitcast.26), channel_id=1, source_target_pairs={{0,0},{1,1},{2,8},{3,9},{4,16},{5,17},{6,24},{7,25},{8,4},{9,5},{1... | collective-permute-start | bytes 497672 | tf_op jit(solution)/shard_map/ppermute | solution.py:615

commit v10 on v9

--- a/solution.py
+++ b/solution.py
@@ -197,14 +197,15 @@
 
 
 def fill_weights(lay, pos_ref, w_refs, w_scr):
+    order = lay.doubled(lay.bits(lay.nz)[::-1])
     block = w_scr.shape[1] // lay.nz
-    rows, width = w_refs[0].shape[0], w_scr.shape[2]
+    rows, width = w_refs[0].shape[1], w_scr.shape[2]
     for h in range(lay.halves):
-        for k in range(lay.nz):
-            ref = w_refs[h * lay.nz + k]
+        for n, k in enumerate(order):
+            ref, place = w_refs[2 * h + (2 * n) // lay.nz], n % (lay.nz // 2)
             for m in range(block // rows):
                 start = pl.multiple_of((pos_ref[2] ^ k) * block + m * rows, 16)
-                w_scr[h, pl.ds(start, rows), :] = ref[:, m * width : (m + 1) * width]
+                w_scr[h, pl.ds(start, rows), :] = ref[place, :, m * width : (m + 1) * width]
 
 
 def heads_stacked(lay, values):
@@ -242,7 +243,7 @@
 
 
 def forward_kernel(lay, pos_ref, info_ref, hid_ref, gp_ref, *refs):
-    w_refs, refs = refs[: lay.halves * lay.nz], refs[lay.halves * lay.nz :]
+    w_refs, refs = refs[: 2 * lay.halves], refs[2 * lay.halves :]
     wo_refs, refs = refs[: lay.nc], refs[lay.nc :]
     q_ref, k_ref, v_ref, ga_ref, kept_ref, sent_ref, *refs = refs
     pr_refs, (w_scr, att_scr, wo_scr, acc_scr, cut_scr) = refs[: lay.chips], refs[lay.chips :]
@@ -314,7 +315,7 @@
 
 
 def backward_kernel(lay, pos_ref, info_ref, *refs):
-    w_refs, refs = refs[: lay.halves * lay.nz], refs[lay.halves * lay.nz :]
+    w_refs, refs = refs[: 2 * lay.halves], refs[2 * lay.halves :]
     q_ref, k_ref, v_ref, ga_ref, *refs = refs
     gh_refs, (w_scr, gt_scr) = refs[: lay.chips], refs[lay.chips :]
     _, frames, step_patches, cols = q_ref.shape
@@ -355,40 +356,32 @@
 def output_kernel(lay, pos_ref, info_ref, *refs):
     pair_refs, refs = refs[: lay.nc], refs[lay.nc :]
     pr_refs, refs = refs[: lay.chips], refs[lay.chips :]
+    gh_refs, refs = refs[: lay.chips], refs[lay.chips :]
     mod_ref, *out_refs = refs
-    step_patches, model = out_refs[0].shape
+    _, _, step_patches, model = out_refs[0].shape
     patches = step_patches * pl.num_programs(0)
     patch_base = lay.unit(pos_ref[1], pos_ref[2])[2] * patches + pl.program_id(0) * step_patches
     patch = patch_base + lax.broadcasted_iota(jnp.int32, (step_patches, 1), 0)
     for j in range(lay.nc):
         _, limit, step = slot_scalars(lay, pos_ref, info_ref, (0, j))
+        values = pair_refs[j][0, 0].astype(F32)
         factor = jnp.where(patch < limit, table_row(mod_ref, step, 2, model), 0.0)
-        projected = pr_refs[0][j]
+        projected, grad_hidden = pr_refs[0][j], gh_refs[0][j]
         for k in range(1, lay.chips):
             projected = projected + pr_refs[k][j].astype(F32)
+            grad_hidden = grad_hidden + gh_refs[k][j].astype(F32)
         projected = projected.astype(BF16).astype(F32)
-        out_refs[j][...] = (pair_refs[j][0, 0].astype(F32) + factor * projected).astype(BF16)
-
-
-def input_grad_kernel(lay, pos_ref, info_ref, *refs):
-    pair_refs, refs = refs[: lay.nc], refs[lay.nc :]
-    gh_refs, refs = refs[: lay.chips], refs[lay.chips :]
-    mod_ref, *out_refs = refs
-    model = out_refs[0].shape[1]
-    for j in range(lay.nc):
-        _, _, step = slot_scalars(lay, pos_ref, info_ref, (0, j))
-        grad_hidden = gh_refs[0][j]
-        for k in range(1, lay.chips):
-            grad_hidden = grad_hidden + gh_refs[k][j].astype(F32)
+        out_refs[j][0, 0] = (values + factor * projected).astype(BF16)
+
         grad_hidden = grad_hidden.astype(BF16).astype(F32)
-        normed, inv_sigma = normalize(pair_refs[j][0, 0].astype(F32))
+        normed, inv_sigma = normalize(values)
         grad_norm = grad_hidden * (1.0 + table_row(mod_ref, step, 1, model))
         first_mean = jnp.mean(grad_norm, axis=-1, keepdims=True)
         second_mean = jnp.mean(grad_norm * normed, axis=-1, keepdims=True)
         grad_x = pair_refs[j][0, 1].astype(F32) + inv_sigma * (
             grad_norm - first_mean - normed * second_mean
         )
-        out_refs[j][...] = grad_x.astype(BF16)
+        out_refs[j][0, 1] = grad_x.astype(BF16)
 
 
 def whole_spec(shape):
@@ -446,12 +439,6 @@
     def over_chips(parts):
         got = [lax.ppermute(parts[k], AXES, chip_swap(k)) for k in range(1, chips)]
         return [parts[0]] + got
-
-    def from_plane(parts):
-        got = [lax.ppermute(part, AXES, lay.from_plane(k)) for k, part in enumerate(parts)]
-        first = jnp.where(z // lay.ny == 0, got[0], got[1])
-        second = jnp.where(z // lay.ny == 0, got[1], got[0])
-        return jnp.concatenate([first, second], axis=0)[None]
 
     info = jnp.concatenate([clip_ids[0], clip_patches[0], clip_step[0]])[None]
     by_core = jnp.concatenate([info, lax.ppermute(info, AXES, lay.swap(kc=1))], axis=0)
@@ -485,26 +472,19 @@
     else:
         stacked = jnp.stack(by_x)
         ordered = [lax.dynamic_index_in_dim(stacked, x ^ i, 0, keepdims=False) for i in range(nx)]
-    w_own = jnp.concatenate(ordered, axis=1 if rows % 16 == 0 else 0)
+    w_own = jnp.concatenate(ordered, axis=1 if rows % 16 == 0 else 0)[None]
     own[0], _ = lax.optimization_barrier((own[0], w_own))
-    w_pieces = {0: w_own}
-    for bit in lay.bits(lay.nz):
-        w_pieces[bit] = lax.ppermute(w_own, AXES, lay.swap(kz=bit))
-    for k in range(1, lay.nz):
-        if k not in w_pieces:
-            bit = k & -k
-            w_pieces[k] = lax.ppermute(w_pieces[k ^ bit], AXES, lay.swap(kz=bit))
-    w_pieces = [w_pieces[k] for k in range(lay.nz)]
+    w_pieces = doubling(w_own, lay.bits(lay.nz)[::-1], lambda kz: lay.swap(kz=kz), [])
     if halves > 1:
-        w_pieces += [lax.ppermute(piece, AXES, lay.swap(kc=1)) for piece in w_pieces[:-1]]
+        w_pieces += [lax.ppermute(piece, AXES, lay.swap(kc=1)) for piece in w_pieces]
 
     late_w_out, _ = lax.optimization_barrier((w_out, own))
     wo_own = lax.ppermute(late_w_out, AXES, lay.rows_to_chip())
 
     pairs = []
     for j in range(nc):
-        pairs += doubling(own[j], lay.chip_bits(j), chip_swap, info)
-    pairs, _ = lax.optimization_barrier((pairs, w_pieces[lay.nz :]))
+        pairs += doubling(own[j], lay.chip_bits(j), chip_swap, [info, w_pieces[0]])
+    pairs, _ = lax.optimization_barrier((pairs, w_pieces[2:]))
 
 
     def spread(count, width, patches_at_once):
@@ -517,7 +497,7 @@
     few_steps = half // few
     x_spec = pl.BlockSpec((few, model), lambda i, *_: (i, 0))
     triple_spec = pl.BlockSpec((halves, lay.frames, step_patches, cols), lambda i, *_: (0, 0, i, 0))
-    w_specs = [whole_spec(w_own.shape)] * (halves * lay.nz)
+    w_specs = [whole_spec(piece.shape) for piece in w_pieces]
     w_scratch = pltpu.VMEM((halves, model, 3 * cols), BF16)
     mod_spec = whole_spec(mod_table.shape)
     triple_shape = struct((halves, lay.frames, half, cols))
@@ -533,11 +513,8 @@
         [struct((lay.frames, half, model))] * 2,
         grid=(few_steps,),
     )(pos, info, *pairs, mod_table)
-    wo_own, w_last, _ = lax.optimization_barrier((wo_own, w_pieces[lay.nz - 1], hidden))
+    wo_own, _ = lax.optimization_barrier((wo_own, hidden))
     wo_rows = [wo_own, lax.ppermute(wo_own, AXES, lay.swap(kc=1))]
-    w_pieces[lay.nz - 1] = w_last
-    if halves > 1:
-        w_pieces.append(lax.ppermute(w_last, AXES, lay.swap(kc=1)))
 
     fold = 3 if rows % 24 == 0 else 1
     piece_shape = (groups, rows // fold, quarter * fold)
@@ -580,38 +557,32 @@
     sums, first_away, projected = lax.optimization_barrier((sums, first_away, projected))
     grad_hidden = over_chips(sums)
 
-    projected, _ = lax.optimization_barrier((projected, grad_hidden[1]))
-    out_parts = call(
+    parts = call(
         functools.partial(output_kernel, lay),
         "output",
         3 * model * 1000,
-        [pair_spec(1, few)] * nc + [spread(nc, model, few)] * chips + [mod_spec],
-        [x_spec] * nc,
-        [struct((half, model))] * nc,
+        [pair_spec(1, few)] * nc + [spread(nc, model, few)] * (2 * chips) + [mod_spec],
+        [pair_spec(1, few)] * nc,
+        [struct(pair_shape)] * nc,
         grid=(few_steps,),
-    )(pos, info, *own, *projected, mod_table)
+    )(pos, info, *own, *projected, *grad_hidden, mod_table)
+    got = [lax.ppermute(part, AXES, lay.from_plane(k)) for k, part in enumerate(parts)]
+    is_first = z // lay.ny == 0
+    out_y, grad_x = (
+        jnp.concatenate(
+            [
+                jnp.where(is_first, got[0][:, n], got[1][:, n]),
+                jnp.where(is_first, got[1][:, n], got[0][:, n]),
+            ],
+            axis=1,
+        )
+        for n in range(2)
+    )
 
     cut = cut + first_away
     for bit in lay.bits(lay.nz)[1:]:
         middle = middle // 2
-        away = lax.ppermute(cut[middle:], AXES, lay.swap(kz=bit))
-        away, _ = lax.optimization_barrier((away, out_parts))
-        cut = cut[:middle] + away
-    out_y = from_plane(out_parts)
-
-
-    grad_parts = call(
-        functools.partial(input_grad_kernel, lay),
-        "input_grad",
-        3 * model * 1000,
-        [pair_spec(1, few)] * nc + [spread(nc, model, few)] * chips + [mod_spec],
-        [x_spec] * nc,
-        [struct((half, model))] * nc,
-        grid=(few_steps,),
-    )(pos, info, *own, *grad_hidden, mod_table)
-    grad_x = from_plane(grad_parts)
-
-    cut, _ = lax.optimization_barrier((cut, grad_parts))
+        cut = cut[:middle] + lax.ppermute(cut[middle:], AXES, lay.swap(kz=bit))
     grad_w = lax.ppermute(cut[0], AXES, lay.to_owner())
     grad_w = jnp.concatenate(
         [grad_w[:, m * quarter : (m + 1) * quarter] for m in range(fold)], axis=0

time: 144 us -> 143 us (level)
  the two profiles are of different devices: /device:TPU:1 before, /device:TPU:4 now
where the time goes in v10:
time: 143 us; the launch traced here: 141 us
  starting transfers between devices  52.2 us (37%)
  waiting for transfers between devices  47.5 us (33%)
  Pallas kernels  32.6 us (23%)
  other arithmetic  5.34 us (4%)
  local copies, waits for them, and re-layouts  2.44 us (2%)
    ppermute x3, starting transfers between devices, doubling(): held = jnp.concatenate([held, lax.ppermute(held, AXES, swap(bit))], axis=0)  11.4 us
    pallas_call x1, Pallas kernels, local(): call(functools.partial(forward_kernel, lay), 'forward', 14 * model * 1000...  11.2 us
    ppermute x3, waiting for transfers between devices, doubling(): return [held, lax.ppermute(held, AXES, swap(bits[-1]))]  10.6 us
    pallas_call x1, Pallas kernels, local(): call(functools.partial(backward_kernel, lay), 'backward', 10 * model * 10...  9.57 us
    ppermute x2, waiting for transfers between devices, local(): lax.ppermute(part, AXES, lay.from_plane(k))  8.89 us
    ppermute x2, starting transfers between devices, local(): lax.ppermute(part, AXES, lay.from_plane(k))  8.66 us
    ppermute x6, waiting for transfers between devices, over_chips(): got = [lax.ppermute(parts[k], AXES, chip_swap(k)) for k in range(1, chips)]  7.35 us
    ppermute x3, waiting for transfers between devices, doubling(): held = jnp.concatenate([held, lax.ppermute(held, AXES, swap(bit))], axis=0)  7.07 us
  transfers between devices with their start and end apart: 27, of which 15 were waited for; matrix products, arithmetic and copies ran while one was open for 3% of the time, Pallas kernels for 13%

profile of v10, /device:TPU:4, one launch (start us, length us, event | category | flops | bytes accessed | tf_op | source)
XLA Modules:
  0.0 141.1 jit_solution(8034905218575489916)
XLA Ops:
  0.6 0.6 pad_add_fusion.1.pos_ref
  1.2 3.4 %start.1 = (bf16[1,2,64,1152]{3,2,1,0:T(8,128)(2,1)}, bf16[1,2,64,1152]{3,2,1,0:T(8,128)(2,1)}, bf16[144,432]{1,0:T(8,128)(2,1)}, bf16[144,432]{1,0:T(8,128)(2,1)}) custom-call(s32[4]{0:T(128)} %pad_add_fusion.1.pos_ref, bf16[1,128,1152]{2,1,0:T(8,128)(2,1)} %x_ref.1, bf16[1,128,1152]{2,1,0:T(8,128)(2,1)} %g_ref.1, bf16[144,3456]{1,0:T(8,128)(2,1)} %w_ref.1), custom_call_target="tpu_custom_call" | custom-call | flops 1179648000 | bytes 2359296 | tf_op jit(solution)/shard_map/start/pallas_call | solution.py:456
  4.7 1.5 %collective-permute-start.3 = (bf16[144,432]{1,0:T(8,128)(2,1)}, bf16[144,432]{1,0:T(8,128)(2,1)S(1)}, u32[]{:S(2)}, u32[]{:S(2)}) collective-permute-start(bf16[144,432]{1,0:T(8,128)(2,1)} %get-tuple-element.48), channel_id=1, source_target_pairs={{0,1},{1,0},{2,3},{3,2},{4,5},{5,4},{6,7},{7,6},{8,9},{9,8},{10,11... | collective-permute-start | bytes 373256 | tf_op jit(solution)/shard_map/ppermute | solution.py:468
  6.2 0.1 fusion.8
  6.2 0.0 collective-permute-start
  6.3 2.5 %collective-permute-start.2 = (bf16[1,2,64,1152]{3,2,1,0:T(8,128)(2,1)}, bf16[1,2,64,1152]{3,2,1,0:T(8,128)(2,1)S(1)}, u32[]{:S(2)}, u32[]{:S(2)}) collective-permute-start(bf16[1,2,64,1152]{3,2,1,0:T(8,128)(2,1)} %get-tuple-element.46), channel_id=1, source_target_pairs={{0,0},{1,1},{2,16},{3,17},{4,2},{5,3},{6,18},{7,19},{8,20},{9,21},... | collective-permute-start | bytes 884744 | tf_op jit(solution)/shard_map/ppermute | solution.py:466
  8.7 4.1 %collective-permute-start.4 = (bf16[1,2,64,1152]{3,2,1,0:T(8,128)(2,1)}, bf16[1,2,64,1152]{3,2,1,0:T(8,128)(2,1)S(1)}, u32[]{:S(2)}, u32[]{:S(2)}) collective-permute-start(bf16[1,2,64,1152]{3,2,1,0:T(8,128)(2,1)} %get-tuple-element.50), channel_id=1, source_target_pairs={{0,2},{1,3},{2,18},{3,19},{4,0},{5,1},{6,16},{7,17},{8,22},{9,23},... | collective-permute-start | bytes 884744 | tf_op jit(solution)/shard_map/ppermute | solution.py:466
  13.0 0.9 broadcast_select_fusion.1
  13.9 0.1 maximum_bitcast_fusion
  14.0 3.4 %collective-permute-start.5 = (bf16[1,144,864]{2,1,0:T(8,128)(2,1)S(1)}, bf16[1,144,864]{2,1,0:T(8,128)(2,1)S(1)}, u32[]{:S(2)}, u32[]{:S(2)}) collective-permute-start(bf16[1,144,864]{2,1,0:T(8,128)(2,1)S(1)} %maximum_bitcast_fusion), channel_id=1, source_target_pairs={{0,4},{1,5},{2,6},{3,7},{4,0},{5,1},{6,2},{7,3},{8,12},{9,13},{10,... | collective-permute-start | bytes 746504 | tf_op jit(solution)/shard_map/ppermute | solution.py:435
  17.4 0.1 collective-permute-start.1
  17.5 0.0 copy-start.3
  17.5 0.6 collective-permute-start.9
  18.1 2.9 %collective-permute-done.1 = s32[2,16]{1,0:T(2,128)S(1)} collective-permute-done((s32[2,16]{1,0:T(2,128)S(1)}, s32[2,16]{1,0:T(2,128)S(1)}, u32[]{:S(2)}, u32[]{:S(2)}) %collective-permute-start.1) | collective-permute-done | bytes 160 | tf_op jit(solution)/shard_map/ppermute | solution.py:446
  21.1 0.6 fusion.3.info_ref
  21.7 4.8 %collective-permute-done.4.refs_1_ = bf16[1,2,64,1152]{3,2,1,0:T(8,128)(2,1)S(1)} collective-permute-done((bf16[1,2,64,1152]{3,2,1,0:T(8,128)(2,1)}, bf16[1,2,64,1152]{3,2,1,0:T(8,128)(2,1)S(1)}, u32[]{:S(2)}, u32[]{:S(2)}) %collective-permute-start.4) | collective-permute-done | bytes 294944 | tf_op jit(solution)/shard_map/ppermute | solution.py:466
  26.5 7.4 %collective-permute-start.11 = (bf16[1,2,64,1152]{3,2,1,0:T(8,128)(2,1)S(1)}, bf16[1,2,64,1152]{3,2,1,0:T(8,128)(2,1)S(1)}, u32[]{:S(2)}, u32[]{:S(2)}) collective-permute-start(bf16[1,2,64,1152]{3,2,1,0:T(8,128)(2,1)S(1)} %collective-permute-done.4.refs_1_), channel_id=1, source_target_pairs={{0,16},{1,17},{2,18},{3,19},{4,20},{5,21},{6,22},{7,23},{8,24},{9,... | collective-permute-start | bytes 884744 | tf_op jit(solution)/shard_map/ppermute | solution.py:435
  33.9 2.8 %collective-permute-done.5 = bf16[1,144,864]{2,1,0:T(8,128)(2,1)S(1)} collective-permute-done((bf16[1,144,864]{2,1,0:T(8,128)(2,1)S(1)}, bf16[1,144,864]{2,1,0:T(8,128)(2,1)S(1)}, u32[]{:S(2)}, u32[]{:S(2)}) %collective-permute-start.5) | collective-permute-done | bytes 248864 | tf_op jit(solution)/shard_map/ppermute | solution.py:435
  36.7 0.1 pad_maximum_fusion.2.refs_0_
  36.7 0.0 copy-start.13
  36.7 0.1 collective-permute-start.6
  36.8 0.1 pad_maximum_fusion.refs_0_
  36.9 4.3 %collective-permute-done.11 = bf16[1,2,64,1152]{3,2,1,0:T(8,128)(2,1)S(1)} collective-permute-done((bf16[1,2,64,1152]{3,2,1,0:T(8,128)(2,1)S(1)}, bf16[1,2,64,1152]{3,2,1,0:T(8,128)(2,1)S(1)}, u32[]{:S(2)}, u32[]{:S(2)}) %collective-permute-start.11) | collective-permute-done | bytes 294944 | tf_op jit(solution)/shard_map/ppermute | solution.py:435
  41.2 0.1 pad_maximum_fusion.1.refs_2_
  41.3 0.6 collective-permute-start.12
  42.0 2.2 %collective-permute-start.10 = (bf16[2,2,64,1152]{3,2,1,0:T(8,128)(2,1)S(1)}, bf16[2,2,64,1152]{3,2,1,0:T(8,128)(2,1)S(1)}, u32[]{:S(2)}, u32[]{:S(2)}) collective-permute-start(bf16[2,2,64,1152]{3,2,1,0:T(8,128)(2,1)S(1)} %pad_maximum_fusion.refs_0_), channel_id=1, source_target_pairs={{0,16},{1,17},{2,18},{3,19},{4,20},{5,21},{6,22},{7,23},{8,24},{9,... | collective-permute-start | bytes 1769480 | tf_op jit(solution)/shard_map/ppermute | solution.py:437
  44.2 4.5 %collective-permute-done.6.refs_1_ = bf16[2,144,864]{2,1,0:T(8,128)(2,1)S(1)} collective-permute-done((bf16[2,144,864]{2,1,0:T(8,128)(2,1)S(1)}, bf16[2,144,864]{2,1,0:T(8,128)(2,1)S(1)}, u32[]{:S(2)}, u32[]{:S(2)}) %collective-permute-start.6) | collective-permute-done | bytes 497696 | tf_op jit(solution)/shard_map/ppermute | solution.py:437
  48.7 3.0 %collective-permute-start.13 = (bf16[144,1152]{1,0:T(8,128)(2,1)S(1)}, bf16[144,1152]{1,0:T(8,128)(2,1)S(1)}, u32[]{:S(2)}, u32[]{:S(2)}) collective-permute-start(bf16[144,1152]{1,0:T(8,128)(2,1)S(1)} %copy-done.13), channel_id=1, source_target_pairs={{0,0},{1,1},{2,18},{3,19},{4,8},{5,9},{6,26},{7,27},{8,4},{9,5},{1... | collective-permute-start | bytes 995336 | tf_op jit(solution)/shard_map/ppermute | solution.py:482
  51.7 5.6 %collective-permute-done.12.refs_3_ = bf16[2,2,64,1152]{3,2,1,0:T(8,128)(2,1)S(1)} collective-permute-done((bf16[2,2,64,1152]{3,2,1,0:T(8,128)(2,1)S(1)}, bf16[2,2,64,1152]{3,2,1,0:T(8,128)(2,1)S(1)}, u32[]{:S(2)}, u32[]{:S(2)}) %collective-permute-start.12) | collective-permute-done | bytes 589856 | tf_op jit(solution)/shard_map/ppermute | solution.py:437
  57.3 0.6 collective-permute-done.10.refs_1_
  57.9 0.2 copy-done.8
  58.1 0.6 copy-done.9
  58.7 4.4 %prepare.1 = (bf16[8,64,1152]{2,1,0:T(8,128)(2,1)}, bf16[8,64,1152]{2,1,0:T(8,128)(2,1)}) custom-call(s32[4]{0:T(128)} %pad_add_fusion.1.pos_ref, s32[16]{0:T(128)} %fusion.3.info_ref, bf16[2,2,64,1152]{3,2,1,0:T(8,128)(2,1)} %copy-done, bf16[2,2,64,1152]{3,2,1,0:T(8,128)(2,1)} %copy-done.9, bf16[2,2,64,1152]{3,2,1,0:T(8,128)(2,1)} %copy-done.1, ...), custom_call_target="tpu_custom_call" | custom-call | flops 1769472000 | bytes 2359296 | tf_op jit(solution)/shard_map/prepare/pallas_call | solution.py:507
  63.0 0.1 collective-permute-start.14
  63.1 1.6 %collective-permute-done.14.refs_5_ = bf16[144,1152]{1,0:T(8,128)(2,1)S(1)} collective-permute-done((bf16[144,1152]{1,0:T(8,128)(2,1)S(1)}, bf16[144,1152]{1,0:T(8,128)(2,1)S(1)}, u32[]{:S(2)}, u32[]{:S(2)}) %collective-permute-start.14) | collective-permute-done | bytes 331808 | tf_op jit(solution)/shard_map/ppermute | solution.py:517
  64.8 0.7 copy-done.15
  65.5 11.2 %forward.1 = (bf16[2,8,64,144]{3,2,1,0:T(8,128)(2,1)}, bf16[2,8,64,144]{3,2,1,0:T(8,128)(2,1)}, bf16[2,8,64,144]{3,2,1,0:T(8,128)(2,1)}, bf16[2,8,64,144]{3,2,1,...) custom-call(s32[4]{0:T(128)} %pad_add_fusion.1.pos_ref, ...), custom_call_target="tpu_custom_call" | custom-call | flops 8257536000 | bytes 2359296 | tf_op jit(solution)/shard_map/forward/pallas_call | solution.py:521
  76.7 0.1 collective-permute-start.15
  76.8 1.5 %collective-permute-start.17 = (bf16[2,64,1152]{2,1,0:T(8,128)(2,1)}, bf16[2,64,1152]{2,1,0:T(8,128)(2,1)S(1)}, u32[]{:S(2)}, u32[]{:S(2)}) collective-permute-start(bf16[2,64,1152]{2,1,0:T(8,128)(2,1)} %get-tuple-element.74), channel_id=1, source_target_pairs={{0,1},{1,0},{2,3},{3,2},{4,5},{5,4},{6,7},{7,6},{8,9},{9,8},{10,11... | collective-permute-start | bytes 884744 | tf_op jit(solution)/shard_map/ppermute | solution.py:440
  78.3 1.7 %collective-permute-start.18 = (bf16[2,64,1152]{2,1,0:T(8,128)(2,1)}, bf16[2,64,1152]{2,1,0:T(8,128)(2,1)S(1)}, u32[]{:S(2)}, u32[]{:S(2)}) collective-permute-start(bf16[2,64,1152]{2,1,0:T(8,128)(2,1)} %get-tuple-element.75), channel_id=1, source_target_pairs={{0,16},{1,17},{2,18},{3,19},{4,20},{5,21},{6,22},{7,23},{8,24},{9,... | collective-permute-start | bytes 884744 | tf_op jit(solution)/shard_map/ppermute | solution.py:440
  80.1 0.3 collective-permute-start.19
  80.3 1.2 slice_add_fusion
  81.5 0.1 collective-permute-start.16
  81.6 9.6 %backward.1 = (f32[2,64,1152]{2,1,0:T(8,128)}, bf16[2,64,1152]{2,1,0:T(8,128)(2,1)}, bf16[2,64,1152]{2,1,0:T(8,128)(2,1)}, bf16[2,64,1152]{2,1,0:T(8,128)(2,1)}) custom-call(s32[4]{0:T(128)} %pad_add_fusion.1.pos_ref, s32[16]{0:T(128)} %fusion.3.info_ref, bf16[2,144,864]{2,1,0:T(8,128)(2,1)} %copy-done.2, bf16[2,144,864]{2,1,0:T(8,128)(2,1)} %copy-done.10, ...), custom_call_target="tpu_custom_call" | custom-call | flops 5898240000 | bytes 2359296 | tf_op jit(solution)/shard_map/backward/pallas_call | solution.py:547
  91.2 2.0 %collective-permute-done.18.refs_4_ = bf16[2,64,1152]{2,1,0:T(8,128)(2,1)S(1)} collective-permute-done((bf16[2,64,1152]{2,1,0:T(8,128)(2,1)}, bf16[2,64,1152]{2,1,0:T(8,128)(2,1)S(1)}, u32[]{:S(2)}, u32[]{:S(2)}) %collective-permute-start.18) | collective-permute-done | bytes 294944 | tf_op jit(solution)/shard_map/ppermute | solution.py:440
  93.2 0.6 collective-permute-done.19.refs_5_
  93.9 6.9 %collective-permute-start.25 = (f32[1,48,864]{2,1,0:T(8,128)S(1)}, f32[1,48,864]{2,1,0:T(8,128)S(1)}, u32[]{:S(2)}, u32[]{:S(2)}) collective-permute-start(f32[1,48,864]{2,1,0:T(8,128)S(1)} %slice.71), channel_id=1, source_target_pairs={{0,4},{1,5},{2,6},{3,7},{4,0},{5,1},{6,2},{7,3},{8,12},{9,13},{10,... | collective-permute-start | bytes 497672 | tf_op jit(solution)/shard_map/ppermute | solution.py:585
  100.8 1.5 %collective-permute-start.20 = (bf16[2,64,1152]{2,1,0:T(8,128)(2,1)S(1)}, bf16[2,64,1152]{2,1,0:T(8,128)(2,1)S(1)}, u32[]{:S(2)}, u32[]{:S(2)}) collective-permute-start(bf16[2,64,1152]{2,1,0:T(8,128)(2,1)S(1)} %copy-done.21), channel_id=1, source_target_pairs={{0,1},{1,0},{2,3},{3,2},{4,5},{5,4},{6,7},{7,6},{8,9},{9,8},{10,11... | collective-permute-start | bytes 884744 | tf_op jit(solution)/shard_map/ppermute | solution.py:440
  102.2 2.0 %collective-permute-start.21 = (bf16[2,64,1152]{2,1,0:T(8,128)(2,1)S(1)}, bf16[2,64,1152]{2,1,0:T(8,128)(2,1)S(1)}, u32[]{:S(2)}, u32[]{:S(2)}) collective-permute-start(bf16[2,64,1152]{2,1,0:T(8,128)(2,1)S(1)} %copy-done.20), channel_id=1, source_target_pairs={{0,16},{1,17},{2,18},{3,19},{4,20},{5,21},{6,22},{7,23},{8,24},{9,... | collective-permute-start | bytes 884744 | tf_op jit(solution)/shard_map/ppermute | solution.py:440
  104.3 0.1 collective-permute-start.22
  104.3 4.2 %collective-permute-done.25 = f32[1,48,864]{2,1,0:T(8,128)S(1)} collective-permute-done((f32[1,48,864]{2,1,0:T(8,128)S(1)}, f32[1,48,864]{2,1,0:T(8,128)S(1)}, u32[]{:S(2)}, u32[]{:S(2)}) %collective-permute-start.25) | collective-permute-done | bytes 165920 | tf_op jit(solution)/shard_map/ppermute | solution.py:585
  108.5 3.8 %collective-permute-start.26 = (f32[48,864]{1,0:T(8,128)S(1)}, f32[48,864]{1,0:T(8,128)S(1)}, u32[]{:S(2)}, u32[]{:S(2)}) collective-permute-start(f32[48,864]{1,0:T(8,128)S(1)} %fusion), channel_id=1, source_target_pairs={{0,0},{1,1},{2,8},{3,9},{4,16},{5,17},{6,24},{7,25},{8,4},{9,5},{1... | collective-permute-start | bytes 497672 | tf_op jit(solution)/shard_map/ppermute | solution.py:586
  112.4 3.3 %collective-permute-done.21.refs_8_ = bf16[2,64,1152]{2,1,0:T(8,128)(2,1)S(1)} collective-permute-done((bf16[2,64,1152]{2,1,0:T(8,128)(2,1)S(1)}, bf16[2,64,1152]{2,1,0:T(8,128)(2,1)S(1)}, u32[]{:S(2)}, u32[]{:S(2)}) %collective-permute-start.21) | collective-permute-done | bytes 294944 | tf_op jit(solution)/shard_map/ppermute | solution.py:440
  115.7 1.3 collective-permute-done.22.refs_9_
  117.1 0.7 copy-done.24
  117.8 4.0 %output.1 = (bf16[1,2,64,1152]{3,2,1,0:T(8,128)(2,1)}, bf16[1,2,64,1152]{3,2,1,0:T(8,128)(2,1)}) custom-call(s32[4]{0:T(128)} %pad_add_fusion.1.pos_ref, s32[16]{0:T(128)} %fusion.3.info_ref, bf16[1,2,64,1152]{3,2,1,0:T(8,128)(2,1)} %copy-done.3, bf16[1,2,64,1152]{3,2,1,0:T(8,128)(2,1)} %copy-done.4, f32[2,64,1152]{2,1,0:T(8,128)} %get-tuple-element.77.refs_2_, ...), custom_call_target="tpu_custom_call" | custom-call | flops 1769472000 | bytes 2359296 | tf_op jit(solution)/shard_map/output/pallas_call | solution.py:560
  121.8 6.7 %collective-permute-start.23 = (bf16[1,2,64,1152]{3,2,1,0:T(8,128)(2,1)}, bf16[1,2,64,1152]{3,2,1,0:T(8,128)(2,1)S(1)}, u32[]{:S(2)}, u32[]{:S(2)}) collective-permute-start(bf16[1,2,64,1152]{3,2,1,0:T(8,128)(2,1)} %get-tuple-element.85), channel_id=1, source_target_pairs={{0,0},{1,1},{16,2},{17,3},{2,4},{3,5},{18,6},{19,7},{20,8},{21,9},... | collective-permute-start | bytes 884744 | tf_op jit(solution)/shard_map/ppermute | solution.py:569
  128.5 1.9 %collective-permute-start.24 = (bf16[1,2,64,1152]{3,2,1,0:T(8,128)(2,1)}, bf16[1,2,64,1152]{3,2,1,0:T(8,128)(2,1)S(1)}, u32[]{:S(2)}, u32[]{:S(2)}) collective-permute-start(bf16[1,2,64,1152]{3,2,1,0:T(8,128)(2,1)} %get-tuple-element.86), channel_id=1, source_target_pairs={{2,0},{3,1},{18,2},{19,3},{0,4},{1,5},{16,6},{17,7},{22,8},{23,9},... | collective-permute-start | bytes 884744 | tf_op jit(solution)/shard_map/ppermute | solution.py:569
  130.5 0.1 fusion.7
  130.6 0.7 maximum_multiply_fusion
  131.3 5.0 %collective-permute-done.23 = bf16[1,2,64,1152]{3,2,1,0:T(8,128)(2,1)S(1)} collective-permute-done((bf16[1,2,64,1152]{3,2,1,0:T(8,128)(2,1)}, bf16[1,2,64,1152]{3,2,1,0:T(8,128)(2,1)S(1)}, u32[]{:S(2)}, u32[]{:S(2)}) %collective-permute-start.23) | collective-permute-done | bytes 294944 | tf_op jit(solution)/shard_map/ppermute | solution.py:569
  136.3 3.9 %collective-permute-done.24 = bf16[1,2,64,1152]{3,2,1,0:T(8,128)(2,1)S(1)} collective-permute-done((bf16[1,2,64,1152]{3,2,1,0:T(8,128)(2,1)}, bf16[1,2,64,1152]{3,2,1,0:T(8,128)(2,1)S(1)}, u32[]{:S(2)}, u32[]{:S(2)}) %collective-permute-start.24) | collective-permute-done | bytes 294944 | tf_op jit(solution)/shard_map/ppermute | solution.py:569
  140.2 0.1 select_bitcast_fusion.1
  140.2 0.9 pad_maximum_fusion.3
  (62 shorter events, 0.2 us)
Async XLA Ops:
  1.2 4.9 %copy-start.5 = (s32[1,4]{1,0:T(1,128)S(1)}, s32[1,4]{1,0:T(1,128)}, u32[]{:S(2)}) copy-start(s32[1,4]{1,0:T(1,128)} %param.12) | copy-start | bytes 52
  1.2 4.9 %copy-start.6 = (s32[1,4]{1,0:T(1,128)S(1)}, s32[1,4]{1,0:T(1,128)}, u32[]{:S(2)}) copy-start(s32[1,4]{1,0:T(1,128)} %param.11) | copy-start | bytes 52
  1.2 4.9 %copy-start.7 = (s32[1,8]{1,0:T(1,128)S(1)}, s32[1,8]{1,0:T(1,128)}, u32[]{:S(2)}) copy-start(s32[1,8]{1,0:T(1,128)} %param.10) | copy-start | bytes 100
  4.7 8.3 %collective-permute-start.3 = (bf16[144,432]{1,0:T(8,128)(2,1)}, bf16[144,432]{1,0:T(8,128)(2,1)S(1)}, u32[]{:S(2)}, u32[]{:S(2)}) collective-permute-start(bf16[144,432]{1,0:T(8,128)(2,1)} %get-tuple-element.48), channel_id=1, source_target_pairs={{0,1},{1,0},{2,3},{3,2},{4,5},{5,4},{6,7},{7,6},{8,9},{9,8},{10,11... | collective-permute-start | bytes 373256 | tf_op jit(solution)/shard_map/ppermute | solution.py:468
  6.2 11.2 %collective-permute-start = (s32[1,16]{1,0:T(1,128)S(1)}, s32[1,16]{1,0:T(1,128)S(1)}, u32[]{:S(2)}, u32[]{:S(2)}) collective-permute-start(s32[1,16]{1,0:T(1,128)S(1)} %fusion.8), channel_id=1, source_target_pairs={{0,8},{1,9},{2,10},{3,11},{4,12},{5,13},{6,14},{7,15},{8,0},{9,1},... | collective-permute-start | bytes 200 | tf_op jit(solution)/shard_map/ppermute | solution.py:444
  6.3 11.2 %collective-permute-start.2 = (bf16[1,2,64,1152]{3,2,1,0:T(8,128)(2,1)}, bf16[1,2,64,1152]{3,2,1,0:T(8,128)(2,1)S(1)}, u32[]{:S(2)}, u32[]{:S(2)}) collective-permute-start(bf16[1,2,64,1152]{3,2,1,0:T(8,128)(2,1)} %get-tuple-element.46), channel_id=1, source_target_pairs={{0,0},{1,1},{2,16},{3,17},{4,2},{5,3},{6,18},{7,19},{8,20},{9,21},... | collective-permute-start | bytes 884744 | tf_op jit(solution)/shard_map/ppermute | solution.py:466
  8.7 17.7 %collective-permute-start.4 = (bf16[1,2,64,1152]{3,2,1,0:T(8,128)(2,1)}, bf16[1,2,64,1152]{3,2,1,0:T(8,128)(2,1)S(1)}, u32[]{:S(2)}, u32[]{:S(2)}) collective-permute-start(bf16[1,2,64,1152]{3,2,1,0:T(8,128)(2,1)} %get-tuple-element.50), channel_id=1, source_target_pairs={{0,2},{1,3},{2,18},{3,19},{4,0},{5,1},{6,16},{7,17},{8,22},{9,23},... | collective-permute-start | bytes 884744 | tf_op jit(solution)/shard_map/ppermute | solution.py:466
  14.0 22.6 %collective-permute-start.5 = (bf16[1,144,864]{2,1,0:T(8,128)(2,1)S(1)}, bf16[1,144,864]{2,1,0:T(8,128)(2,1)S(1)}, u32[]{:S(2)}, u32[]{:S(2)}) collective-permute-start(bf16[1,144,864]{2,1,0:T(8,128)(2,1)S(1)} %maximum_bitcast_fusion), channel_id=1, source_target_pairs={{0,4},{1,5},{2,6},{3,7},{4,0},{5,1},{6,2},{7,3},{8,12},{9,13},{10,... | collective-permute-start | bytes 746504 | tf_op jit(solution)/shard_map/ppermute | solution.py:435
  17.4 3.6 %collective-permute-start.1 = (s32[2,16]{1,0:T(2,128)S(1)}, s32[2,16]{1,0:T(2,128)S(1)}, u32[]{:S(2)}, u32[]{:S(2)}) collective-permute-start(s32[2,16]{1,0:T(2,128)S(1)} %pad_add_fusion), channel_id=1, source_target_pairs={{0,16},{1,17},{2,18},{3,19},{4,20},{5,21},{6,22},{7,23},{8,24},{9,... | collective-permute-start | bytes 392 | tf_op jit(solution)/shard_map/ppermute | solution.py:446
  17.5 23.8 %copy-start.3 = (bf16[1,2,64,1152]{3,2,1,0:T(8,128)(2,1)}, bf16[1,2,64,1152]{3,2,1,0:T(8,128)(2,1)S(1)}, u32[]{:S(2)}) copy-start(bf16[1,2,64,1152]{3,2,1,0:T(8,128)(2,1)S(1)} %collective-permute-done.2.refs_0_) | copy-start | bytes 884740
  17.5 19.3 %collective-permute-start.9 = (bf16[1,2,64,1152]{3,2,1,0:T(8,128)(2,1)S(1)}, bf16[1,2,64,1152]{3,2,1,0:T(8,128)(2,1)S(1)}, u32[]{:S(2)}, u32[]{:S(2)}) collective-permute-start(bf16[1,2,64,1152]{3,2,1,0:T(8,128)(2,1)S(1)} %collective-permute-done.2.refs_0_), channel_id=1, source_target_pairs={{0,1},{1,0},{2,3},{3,2},{4,5},{5,4},{6,7},{7,6},{8,9},{9,8},{10,11... | collective-permute-start | bytes 884744 | tf_op jit(solution)/shard_map/ppermute | solution.py:435
  26.5 14.9 %copy-start.4 = (bf16[1,2,64,1152]{3,2,1,0:T(8,128)(2,1)}, bf16[1,2,64,1152]{3,2,1,0:T(8,128)(2,1)S(1)}, u32[]{:S(2)}) copy-start(bf16[1,2,64,1152]{3,2,1,0:T(8,128)(2,1)S(1)} %collective-permute-done.4.refs_1_) | copy-start | bytes 884740
  26.5 14.8 %collective-permute-start.11 = (bf16[1,2,64,1152]{3,2,1,0:T(8,128)(2,1)S(1)}, bf16[1,2,64,1152]{3,2,1,0:T(8,128)(2,1)S(1)}, u32[]{:S(2)}, u32[]{:S(2)}) collective-permute-start(bf16[1,2,64,1152]{3,2,1,0:T(8,128)(2,1)S(1)} %collective-permute-done.4.refs_1_), channel_id=1, source_target_pairs={{0,16},{1,17},{2,18},{3,19},{4,20},{5,21},{6,22},{7,23},{8,24},{9,... | collective-permute-start | bytes 884744 | tf_op jit(solution)/shard_map/ppermute | solution.py:435
  36.7 7.5 %copy-start.2 = (bf16[2,144,864]{2,1,0:T(8,128)(2,1)}, bf16[2,144,864]{2,1,0:T(8,128)(2,1)S(1)}, u32[]{:S(2)}) copy-start(bf16[2,144,864]{2,1,0:T(8,128)(2,1)S(1)} %pad_maximum_fusion.2.refs_0_) | copy-start | bytes 1492996
  36.7 12.0 %copy-start.13 = (bf16[144,1152]{1,0:T(8,128)(2,1)S(1)}, bf16[144,1152]{1,0:T(8,128)(2,1)}, u32[]{:S(2)}) copy-start(bf16[144,1152]{1,0:T(8,128)(2,1)} %param.15) | copy-start | bytes 995332
  36.7 12.0 %collective-permute-start.6 = (bf16[2,144,864]{2,1,0:T(8,128)(2,1)S(1)}, bf16[2,144,864]{2,1,0:T(8,128)(2,1)S(1)}, u32[]{:S(2)}, u32[]{:S(2)}) collective-permute-start(bf16[2,144,864]{2,1,0:T(8,128)(2,1)S(1)} %pad_maximum_fusion.2.refs_0_), channel_id=1, source_target_pairs={{0,2},{1,3},{2,0},{3,1},{4,6},{5,7},{6,4},{7,5},{8,10},{9,11},{10,... | collective-permute-start | bytes 1493000 | tf_op jit(solution)/shard_map/ppermute | solution.py:437
  36.9 20.9 %copy-start = (bf16[2,2,64,1152]{3,2,1,0:T(8,128)(2,1)}, bf16[2,2,64,1152]{3,2,1,0:T(8,128)(2,1)S(1)}, u32[]{:S(2)}) copy-start(bf16[2,2,64,1152]{3,2,1,0:T(8,128)(2,1)S(1)} %pad_maximum_fusion.refs_0_) | copy-start | bytes 1769476
  41.3 16.5 %copy-start.1 = (bf16[2,2,64,1152]{3,2,1,0:T(8,128)(2,1)}, bf16[2,2,64,1152]{3,2,1,0:T(8,128)(2,1)S(1)}, u32[]{:S(2)}) copy-start(bf16[2,2,64,1152]{3,2,1,0:T(8,128)(2,1)S(1)} %pad_maximum_fusion.1.refs_2_) | copy-start | bytes 1769476
  41.3 15.9 %collective-permute-start.12 = (bf16[2,2,64,1152]{3,2,1,0:T(8,128)(2,1)S(1)}, bf16[2,2,64,1152]{3,2,1,0:T(8,128)(2,1)S(1)}, u32[]{:S(2)}, u32[]{:S(2)}) collective-permute-start(bf16[2,2,64,1152]{3,2,1,0:T(8,128)(2,1)S(1)} %pad_maximum_fusion.1.refs_2_), channel_id=1, source_target_pairs={{0,1},{1,0},{2,3},{3,2},{4,5},{5,4},{6,7},{7,6},{8,9},{9,8},{10,11... | collective-permute-start | bytes 1769480 | tf_op jit(solution)/shard_map/ppermute | solution.py:437
  42.0 15.9 %collective-permute-start.10 = (bf16[2,2,64,1152]{3,2,1,0:T(8,128)(2,1)S(1)}, bf16[2,2,64,1152]{3,2,1,0:T(8,128)(2,1)S(1)}, u32[]{:S(2)}, u32[]{:S(2)}) collective-permute-start(bf16[2,2,64,1152]{3,2,1,0:T(8,128)(2,1)S(1)} %pad_maximum_fusion.refs_0_), channel_id=1, source_target_pairs={{0,16},{1,17},{2,18},{3,19},{4,20},{5,21},{6,22},{7,23},{8,24},{9,... | collective-permute-start | bytes 1769480 | tf_op jit(solution)/shard_map/ppermute | solution.py:437
  44.2 7.5 %collective-permute-start.7 = (bf16[2,144,864]{2,1,0:T(8,128)(2,1)S(1)}, bf16[2,144,864]{2,1,0:T(8,128)(2,1)S(1)}, u32[]{:S(2)}, u32[]{:S(2)}) collective-permute-start(bf16[2,144,864]{2,1,0:T(8,128)(2,1)S(1)} %pad_maximum_fusion.2.refs_0_), channel_id=1, source_target_pairs={{0,8},{1,9},{2,10},{3,11},{4,12},{5,13},{6,14},{7,15},{8,0},{9,1},... | collective-permute-start | bytes 1493000 | tf_op jit(solution)/shard_map/ppermute | solution.py:479
  48.7 16.0 %copy-start.10 = (bf16[2,144,864]{2,1,0:T(8,128)(2,1)}, bf16[2,144,864]{2,1,0:T(8,128)(2,1)S(1)}, u32[]{:S(2)}) copy-start(bf16[2,144,864]{2,1,0:T(8,128)(2,1)S(1)} %collective-permute-done.6.refs_1_) | copy-start | bytes 1492996
  48.7 9.1 %collective-permute-start.8 = (bf16[2,144,864]{2,1,0:T(8,128)(2,1)S(1)}, bf16[2,144,864]{2,1,0:T(8,128)(2,1)S(1)}, u32[]{:S(2)}, u32[]{:S(2)}) collective-permute-start(bf16[2,144,864]{2,1,0:T(8,128)(2,1)S(1)} %collective-permute-done.6.refs_1_), channel_id=1, source_target_pairs={{0,8},{1,9},{2,10},{3,11},{4,12},{5,13},{6,14},{7,15},{8,0},{9,1},... | collective-permute-start | bytes 1493000 | tf_op jit(solution)/shard_map/ppermute | solution.py:479
  48.7 14.3 %collective-permute-start.13 = (bf16[144,1152]{1,0:T(8,128)(2,1)S(1)}, bf16[144,1152]{1,0:T(8,128)(2,1)S(1)}, u32[]{:S(2)}, u32[]{:S(2)}) collective-permute-start(bf16[144,1152]{1,0:T(8,128)(2,1)S(1)} %copy-done.13), channel_id=1, source_target_pairs={{0,0},{1,1},{2,18},{3,19},{4,8},{5,9},{6,26},{7,27},{8,4},{9,5},{1... | collective-permute-start | bytes 995336 | tf_op jit(solution)/shard_map/ppermute | solution.py:482
  51.7 13.1 %copy-start.11 = (bf16[2,144,864]{2,1,0:T(8,128)(2,1)}, bf16[2,144,864]{2,1,0:T(8,128)(2,1)S(1)}, u32[]{:S(2)}) copy-start(bf16[2,144,864]{2,1,0:T(8,128)(2,1)S(1)} %collective-permute-done.7.refs_2_) | copy-start | bytes 1492996
  57.3 0.8 copy-start.8
  57.8 0.8 copy-start.9
  58.7 4.4 %copy-start.12 = (bf16[2,144,864]{2,1,0:T(8,128)(2,1)}, bf16[2,144,864]{2,1,0:T(8,128)(2,1)S(1)}, u32[]{:S(2)}) copy-start(bf16[2,144,864]{2,1,0:T(8,128)(2,1)S(1)} %collective-permute-done.8.refs_3_) | copy-start | bytes 1492996
  63.0 1.7 %copy-start.14 = (bf16[144,1152]{1,0:T(8,128)(2,1)}, bf16[144,1152]{1,0:T(8,128)(2,1)S(1)}, u32[]{:S(2)}) copy-start(bf16[144,1152]{1,0:T(8,128)(2,1)S(1)} %collective-permute-done.13.refs_4_) | copy-start | bytes 995332
  63.0 1.7 %collective-permute-start.14 = (bf16[144,1152]{1,0:T(8,128)(2,1)S(1)}, bf16[144,1152]{1,0:T(8,128)(2,1)S(1)}, u32[]{:S(2)}, u32[]{:S(2)}) collective-permute-start(bf16[144,1152]{1,0:T(8,128)(2,1)S(1)} %collective-permute-done.13.refs_4_), channel_id=1, source_target_pairs={{0,8},{1,9},{2,10},{3,11},{4,12},{5,13},{6,14},{7,15},{8,0},{9,1},... | collective-permute-start | bytes 995336 | tf_op jit(solution)/shard_map/ppermute | solution.py:517
  64.7 0.7 copy-start.15
  76.7 3.6 %collective-permute-start.15 = (f32[4,48,864]{2,1,0:T(8,128)}, f32[4,48,864]{2,1,0:T(8,128)S(1)}, u32[]{:S(2)}, u32[]{:S(2)}) collective-permute-start(f32[4,48,864]{2,1,0:T(8,128)} %get-tuple-element.66), channel_id=1, source_target_pairs={{0,8},{1,9},{2,10},{3,11},{4,12},{5,13},{6,14},{7,15},{8,0},{9,1},... | collective-permute-start | bytes 1990664 | tf_op jit(solution)/shard_map/ppermute | solution.py:539
  76.8 14.3 %collective-permute-start.17 = (bf16[2,64,1152]{2,1,0:T(8,128)(2,1)}, bf16[2,64,1152]{2,1,0:T(8,128)(2,1)S(1)}, u32[]{:S(2)}, u32[]{:S(2)}) collective-permute-start(bf16[2,64,1152]{2,1,0:T(8,128)(2,1)} %get-tuple-element.74), channel_id=1, source_target_pairs={{0,1},{1,0},{2,3},{3,2},{4,5},{5,4},{6,7},{7,6},{8,9},{9,8},{10,11... | collective-permute-start | bytes 884744 | tf_op jit(solution)/shard_map/ppermute | solution.py:440
  78.3 14.9 %collective-permute-start.18 = (bf16[2,64,1152]{2,1,0:T(8,128)(2,1)}, bf16[2,64,1152]{2,1,0:T(8,128)(2,1)S(1)}, u32[]{:S(2)}, u32[]{:S(2)}) collective-permute-start(bf16[2,64,1152]{2,1,0:T(8,128)(2,1)} %get-tuple-element.75), channel_id=1, source_target_pairs={{0,16},{1,17},{2,18},{3,19},{4,20},{5,21},{6,22},{7,23},{8,24},{9,... | collective-permute-start | bytes 884744 | tf_op jit(solution)/shard_map/ppermute | solution.py:440
  80.1 13.8 %collective-permute-start.19 = (bf16[2,64,1152]{2,1,0:T(8,128)(2,1)}, bf16[2,64,1152]{2,1,0:T(8,128)(2,1)S(1)}, u32[]{:S(2)}, u32[]{:S(2)}) collective-permute-start(bf16[2,64,1152]{2,1,0:T(8,128)(2,1)} %get-tuple-element.76), channel_id=1, source_target_pairs={{0,17},{1,16},{2,19},{3,18},{4,21},{5,20},{6,23},{7,22},{8,25},{9,... | collective-permute-start | bytes 884744 | tf_op jit(solution)/shard_map/ppermute | solution.py:440
  81.5 12.4 %collective-permute-start.16 = (f32[2,48,864]{2,1,0:T(8,128)S(1)}, f32[2,48,864]{2,1,0:T(8,128)S(1)}, u32[]{:S(2)}, u32[]{:S(2)}) collective-permute-start(f32[2,48,864]{2,1,0:T(8,128)S(1)} %get-tuple-element.72), channel_id=1, source_target_pairs={{0,2},{1,3},{2,0},{3,1},{4,6},{5,7},{6,4},{7,5},{8,10},{9,11},{10,... | collective-permute-start | bytes 995336 | tf_op jit(solution)/shard_map/ppermute | solution.py:545
  91.1 9.6 %copy-start.21 = (bf16[2,64,1152]{2,1,0:T(8,128)(2,1)S(1)}, bf16[2,64,1152]{2,1,0:T(8,128)(2,1)}, u32[]{:S(2)}) copy-start(bf16[2,64,1152]{2,1,0:T(8,128)(2,1)} %get-tuple-element.82) | copy-start | bytes 884740
  91.1 11.1 %copy-start.20 = (bf16[2,64,1152]{2,1,0:T(8,128)(2,1)S(1)}, bf16[2,64,1152]{2,1,0:T(8,128)(2,1)}, u32[]{:S(2)}) copy-start(bf16[2,64,1152]{2,1,0:T(8,128)(2,1)} %get-tuple-element.83) | copy-start | bytes 884740
  91.1 13.1 %copy-start.19 = (bf16[2,64,1152]{2,1,0:T(8,128)(2,1)S(1)}, bf16[2,64,1152]{2,1,0:T(8,128)(2,1)}, u32[]{:S(2)}) copy-start(bf16[2,64,1152]{2,1,0:T(8,128)(2,1)} %get-tuple-element.84) | copy-start | bytes 884740
  91.2 25.9 %copy-start.16 = (bf16[2,64,1152]{2,1,0:T(8,128)(2,1)}, bf16[2,64,1152]{2,1,0:T(8,128)(2,1)S(1)}, u32[]{:S(2)}) copy-start(bf16[2,64,1152]{2,1,0:T(8,128)(2,1)S(1)} %collective-permute-done.17.refs_3_) | copy-start | bytes 884740
  93.2 23.8 %copy-start.17 = (bf16[2,64,1152]{2,1,0:T(8,128)(2,1)}, bf16[2,64,1152]{2,1,0:T(8,128)(2,1)S(1)}, u32[]{:S(2)}) copy-start(bf16[2,64,1152]{2,1,0:T(8,128)(2,1)S(1)} %collective-permute-done.18.refs_4_) | copy-start | bytes 884740
  93.8 23.2 %copy-start.18 = (bf16[2,64,1152]{2,1,0:T(8,128)(2,1)}, bf16[2,64,1152]{2,1,0:T(8,128)(2,1)S(1)}, u32[]{:S(2)}) copy-start(bf16[2,64,1152]{2,1,0:T(8,128)(2,1)S(1)} %collective-permute-done.19.refs_5_) | copy-start | bytes 884740
  93.9 14.6 %collective-permute-start.25 = (f32[1,48,864]{2,1,0:T(8,128)S(1)}, f32[1,48,864]{2,1,0:T(8,128)S(1)}, u32[]{:S(2)}, u32[]{:S(2)}) collective-permute-start(f32[1,48,864]{2,1,0:T(8,128)S(1)} %slice.71), channel_id=1, source_target_pairs={{0,4},{1,5},{2,6},{3,7},{4,0},{5,1},{6,2},{7,3},{8,12},{9,13},{10,... | collective-permute-start | bytes 497672 | tf_op jit(solution)/shard_map/ppermute | solution.py:585
  100.8 11.6 %collective-permute-start.20 = (bf16[2,64,1152]{2,1,0:T(8,128)(2,1)S(1)}, bf16[2,64,1152]{2,1,0:T(8,128)(2,1)S(1)}, u32[]{:S(2)}, u32[]{:S(2)}) collective-permute-start(bf16[2,64,1152]{2,1,0:T(8,128)(2,1)S(1)} %copy-done.21), channel_id=1, source_target_pairs={{0,1},{1,0},{2,3},{3,2},{4,5},{5,4},{6,7},{7,6},{8,9},{9,8},{10,11... | collective-permute-start | bytes 884744 | tf_op jit(solution)/shard_map/ppermute | solution.py:440
  102.2 13.5 %collective-permute-start.21 = (bf16[2,64,1152]{2,1,0:T(8,128)(2,1)S(1)}, bf16[2,64,1152]{2,1,0:T(8,128)(2,1)S(1)}, u32[]{:S(2)}, u32[]{:S(2)}) collective-permute-start(bf16[2,64,1152]{2,1,0:T(8,128)(2,1)S(1)} %copy-done.20), channel_id=1, source_target_pairs={{0,16},{1,17},{2,18},{3,19},{4,20},{5,21},{6,22},{7,23},{8,24},{9,... | collective-permute-start | bytes 884744 | tf_op jit(solution)/shard_map/ppermute | solution.py:440
  104.3 12.8 %collective-permute-start.22 = (bf16[2,64,1152]{2,1,0:T(8,128)(2,1)S(1)}, bf16[2,64,1152]{2,1,0:T(8,128)(2,1)S(1)}, u32[]{:S(2)}, u32[]{:S(2)}) collective-permute-start(bf16[2,64,1152]{2,1,0:T(8,128)(2,1)S(1)} %copy-done.19), channel_id=1, source_target_pairs={{0,17},{1,16},{2,19},{3,18},{4,21},{5,20},{6,23},{7,22},{8,25},{9,... | collective-permute-start | bytes 884744 | tf_op jit(solution)/shard_map/ppermute | solution.py:440
  108.5 21.9 %collective-permute-start.26 = (f32[48,864]{1,0:T(8,128)S(1)}, f32[48,864]{1,0:T(8,128)S(1)}, u32[]{:S(2)}, u32[]{:S(2)}) collective-permute-start(f32[48,864]{1,0:T(8,128)S(1)} %fusion), channel_id=1, source_target_pairs={{0,0},{1,1},{2,8},{3,9},{4,16},{5,17},{6,24},{7,25},{8,4},{9,5},{1... | collective-permute-start | bytes 497672 | tf_op jit(solution)/shard_map/ppermute | solution.py:586
  112.3 4.7 %copy-start.22 = (bf16[2,64,1152]{2,1,0:T(8,128)(2,1)}, bf16[2,64,1152]{2,1,0:T(8,128)(2,1)S(1)}, u32[]{:S(2)}) copy-start(bf16[2,64,1152]{2,1,0:T(8,128)(2,1)S(1)} %collective-permute-done.20.refs_7_) | copy-start | bytes 884740
  115.7 1.4 copy-start.23
  117.1 0.7 copy-start.24
  121.8 14.5 %collective-permute-start.23 = (bf16[1,2,64,1152]{3,2,1,0:T(8,128)(2,1)}, bf16[1,2,64,1152]{3,2,1,0:T(8,128)(2,1)S(1)}, u32[]{:S(2)}, u32[]{:S(2)}) collective-permute-start(bf16[1,2,64,1152]{3,2,1,0:T(8,128)(2,1)} %get-tuple-element.85), channel_id=1, source_target_pairs={{0,0},{1,1},{16,2},{17,3},{2,4},{3,5},{18,6},{19,7},{20,8},{21,9},... | collective-permute-start | bytes 884744 | tf_op jit(solution)/shard_map/ppermute | solution.py:569
  128.5 11.6 %collective-permute-start.24 = (bf16[1,2,64,1152]{3,2,1,0:T(8,128)(2,1)}, bf16[1,2,64,1152]{3,2,1,0:T(8,128)(2,1)S(1)}, u32[]{:S(2)}, u32[]{:S(2)}) collective-permute-start(bf16[1,2,64,1152]{3,2,1,0:T(8,128)(2,1)} %get-tuple-element.86), channel_id=1, source_target_pairs={{2,0},{3,1},{18,2},{19,3},{0,4},{1,5},{16,6},{17,7},{22,8},{23,9},... | collective-permute-start | bytes 884744 | tf_op jit(solution)/shard_map/ppermute | solution.py:569

commit v11 on v10

--- a/solution.py
+++ b/solution.py
@@ -430,9 +430,10 @@
         ky, kx = lay.chip_of(k)
         return lay.swap(ky=ky, kx=kx)
 
-    def doubling(held, bits, swap, after):
+    def doubling(held, bits, swap, after, first=None):
         for bit in bits[:-1]:
-            held = jnp.concatenate([held, lax.ppermute(held, AXES, swap(bit))], axis=0)
+            got = lax.ppermute(held, AXES, swap(bit)) if first is None else first
+            held, first = jnp.concatenate([held, got], axis=0), None
         held, _ = lax.optimization_barrier((held, after))
         return [held, lax.ppermute(held, AXES, swap(bits[-1]))]
 
@@ -473,18 +474,18 @@
         stacked = jnp.stack(by_x)
         ordered = [lax.dynamic_index_in_dim(stacked, x ^ i, 0, keepdims=False) for i in range(nx)]
     w_own = jnp.concatenate(ordered, axis=1 if rows % 16 == 0 else 0)[None]
-    own[0], _ = lax.optimization_barrier((own[0], w_own))
+    first = lax.ppermute(own[0], AXES, chip_swap(lay.chip_bits(0)[0]))
+    own[1], first = lax.optimization_barrier((own[1], first))
+    w_own, _ = lax.optimization_barrier((w_own, own[1]))
     w_pieces = doubling(w_own, lay.bits(lay.nz)[::-1], lambda kz: lay.swap(kz=kz), [])
-    if halves > 1:
-        w_pieces += [lax.ppermute(piece, AXES, lay.swap(kc=1)) for piece in w_pieces]
-
     late_w_out, _ = lax.optimization_barrier((w_out, own))
     wo_own = lax.ppermute(late_w_out, AXES, lay.rows_to_chip())
 
     pairs = []
     for j in range(nc):
-        pairs += doubling(own[j], lay.chip_bits(j), chip_swap, [info, w_pieces[0]])
-    pairs, _ = lax.optimization_barrier((pairs, w_pieces[2:]))
+        after = ([], None) if j else (info, first)
+        pairs += doubling(own[j], lay.chip_bits(j), chip_swap, *after)
+    pairs, _ = lax.optimization_barrier((pairs, w_pieces))
 
 
     def spread(count, width, patches_at_once):
@@ -497,7 +498,7 @@
     few_steps = half // few
     x_spec = pl.BlockSpec((few, model), lambda i, *_: (i, 0))
     triple_spec = pl.BlockSpec((halves, lay.frames, step_patches, cols), lambda i, *_: (0, 0, i, 0))
-    w_specs = [whole_spec(piece.shape) for piece in w_pieces]
+    w_specs = [whole_spec(w_pieces[0].shape)] * (2 * halves)
     w_scratch = pltpu.VMEM((halves, model, 3 * cols), BF16)
     mod_spec = whole_spec(mod_table.shape)
     triple_shape = struct((halves, lay.frames, half, cols))
@@ -513,7 +514,9 @@
         [struct((lay.frames, half, model))] * 2,
         grid=(few_steps,),
     )(pos, info, *pairs, mod_table)
-    wo_own, _ = lax.optimization_barrier((wo_own, hidden))
+    wo_own, w_pieces, _ = lax.optimization_barrier((wo_own, w_pieces, hidden))
+    if halves > 1:
+        w_pieces += [lax.ppermute(piece, AXES, lay.swap(kc=1)) for piece in w_pieces]
     wo_rows = [wo_own, lax.ppermute(wo_own, AXES, lay.swap(kc=1))]
 
     fold = 3 if rows % 24 == 0 else 1
@@ -579,10 +582,11 @@
         for n in range(2)
     )
 
-    cut = cut + first_away
+    cut, _ = lax.optimization_barrier((cut + first_away, grad_hidden[1]))
     for bit in lay.bits(lay.nz)[1:]:
         middle = middle // 2
         cut = cut[:middle] + lax.ppermute(cut[middle:], AXES, lay.swap(kz=bit))
+    cut, _ = lax.optimization_barrier((cut, parts))
     grad_w = lax.ppermute(cut[0], AXES, lay.to_owner())
     grad_w = jnp.concatenate(
         [grad_w[:, m * quarter : (m + 1) * quarter] for m in range(fold)], axis=0

time: 143 us -> 141 us (0.986)
  the two profiles are of different devices: /device:TPU:4 before, /device:TPU:30 now
where the time goes in v11:
time: 141 us; the launch traced here: 140 us
  waiting for transfers between devices  61.9 us (44%)
  starting transfers between devices  35.5 us (25%)
  Pallas kernels  32.7 us (23%)
  other arithmetic  5.39 us (4%)
  local copies, waits for them, and re-layouts  3.55 us (3%)
    ppermute x3, waiting for transfers between devices, doubling(): return [held, lax.ppermute(held, AXES, swap(bits[-1]))]  14.2 us
    ppermute x6, waiting for transfers between devices, over_chips(): got = [lax.ppermute(parts[k], AXES, chip_swap(k)) for k in range(1, chips)]  14 us
    ppermute x2, waiting for transfers between devices, local(): lax.ppermute(part, AXES, lay.from_plane(k))  11.6 us
    pallas_call x1, Pallas kernels, local(): call(functools.partial(forward_kernel, lay), 'forward', 14 * model * 1000...  11.3 us
    ppermute x2, waiting for transfers between devices, doubling(): got = lax.ppermute(held, AXES, swap(bit)) if first is None else first  10.4 us
    pallas_call x1, Pallas kernels, local(): call(functools.partial(backward_kernel, lay), 'backward', 10 * model * 10...  9.56 us
    ppermute x6, starting transfers between devices, over_chips(): got = [lax.ppermute(parts[k], AXES, chip_swap(k)) for k in range(1, chips)]  7.06 us
    ppermute x2, starting transfers between devices, local(): lax.ppermute(part, AXES, lay.from_plane(k))  5.65 us
  transfers between devices with their start and end apart: 27, of which 14 were waited for; matrix products, arithmetic and copies ran while one was open for 3% of the time, Pallas kernels for 13%

profile of v11, /device:TPU:30, one launch (start us, length us, event | category | flops | bytes accessed | tf_op | source)
XLA Modules:
  0.0 140.2 jit_solution(397667338044173552)
XLA Ops:
  0.6 0.6 pad_add_fusion.1.pos_ref
  1.3 3.4 %start.1 = (bf16[1,2,64,1152]{3,2,1,0:T(8,128)(2,1)}, bf16[1,2,64,1152]{3,2,1,0:T(8,128)(2,1)}, bf16[144,432]{1,0:T(8,128)(2,1)}, bf16[144,432]{1,0:T(8,128)(2,1)}) custom-call(s32[4]{0:T(128)} %pad_add_fusion.1.pos_ref, bf16[1,128,1152]{2,1,0:T(8,128)(2,1)} %x_ref.1, bf16[1,128,1152]{2,1,0:T(8,128)(2,1)} %g_ref.1, bf16[144,3456]{1,0:T(8,128)(2,1)} %w_ref.1), custom_call_target="tpu_custom_call" | custom-call | flops 1179648000 | bytes 2359296 | tf_op jit(solution)/shard_map/start/pallas_call | solution.py:457
  4.7 1.9 %collective-permute-start.2 = (bf16[1,2,64,1152]{3,2,1,0:T(8,128)(2,1)}, bf16[1,2,64,1152]{3,2,1,0:T(8,128)(2,1)S(1)}, u32[]{:S(2)}, u32[]{:S(2)}) collective-permute-start(bf16[1,2,64,1152]{3,2,1,0:T(8,128)(2,1)} %get-tuple-element.51), channel_id=1, source_target_pairs={{0,0},{1,1},{2,16},{3,17},{4,2},{5,3},{6,18},{7,19},{8,20},{9,21},... | collective-permute-start | bytes 884744 | tf_op jit(solution)/shard_map/ppermute | solution.py:467
  6.6 0.1 fusion.7
  6.7 0.1 collective-permute-start
  6.8 0.5 collective-permute-start.6
  7.3 3.6 %collective-permute-start.3 = (bf16[1,2,64,1152]{3,2,1,0:T(8,128)(2,1)}, bf16[1,2,64,1152]{3,2,1,0:T(8,128)(2,1)S(1)}, u32[]{:S(2)}, u32[]{:S(2)}) collective-permute-start(bf16[1,2,64,1152]{3,2,1,0:T(8,128)(2,1)} %get-tuple-element.52), channel_id=1, source_target_pairs={{0,2},{1,3},{2,18},{3,19},{4,0},{5,1},{6,16},{7,17},{8,22},{9,23},... | collective-permute-start | bytes 884744 | tf_op jit(solution)/shard_map/ppermute | solution.py:467
  11.0 2.1 %collective-permute-start.1 = (s32[2,16]{1,0:T(2,128)S(1)}, s32[2,16]{1,0:T(2,128)S(1)}, u32[]{:S(2)}, u32[]{:S(2)}) collective-permute-start(s32[2,16]{1,0:T(2,128)S(1)} %pad_add_fusion), channel_id=1, source_target_pairs={{0,16},{1,17},{2,18},{3,19},{4,20},{5,21},{6,22},{7,23},{8,24},{9,... | collective-permute-start | bytes 392 | tf_op jit(solution)/shard_map/ppermute | solution.py:447
  13.2 0.7 collective-permute-done.2.refs_0_
  13.8 0.8 collective-permute-start.4
  14.6 0.1 collective-permute-done.1
  14.7 0.6 fusion.2.info_ref
  15.3 0.9 broadcast_select_fusion.1
  16.3 4.8 %collective-permute-done.3.refs_1_ = bf16[1,2,64,1152]{3,2,1,0:T(8,128)(2,1)S(1)} collective-permute-done((bf16[1,2,64,1152]{3,2,1,0:T(8,128)(2,1)}, bf16[1,2,64,1152]{3,2,1,0:T(8,128)(2,1)S(1)}, u32[]{:S(2)}, u32[]{:S(2)}) %collective-permute-start.3) | collective-permute-done | bytes 294944 | tf_op jit(solution)/shard_map/ppermute | solution.py:467
  21.0 0.6 collective-permute-done.4
  21.7 1.1 collective-permute-start.10
  22.8 0.1 maximum_bitcast_fusion
  22.9 3.7 %collective-permute-start.7 = (bf16[1,144,864]{2,1,0:T(8,128)(2,1)S(1)}, bf16[1,144,864]{2,1,0:T(8,128)(2,1)S(1)}, u32[]{:S(2)}, u32[]{:S(2)}) collective-permute-start(bf16[1,144,864]{2,1,0:T(8,128)(2,1)S(1)} %maximum_bitcast_fusion), channel_id=1, source_target_pairs={{0,4},{1,5},{2,6},{3,7},{4,0},{5,1},{6,2},{7,3},{8,12},{9,13},{10,... | collective-permute-start | bytes 746504 | tf_op jit(solution)/shard_map/ppermute | solution.py:435
  26.6 0.1 pad_maximum_fusion.refs_0_
  26.7 1.0 collective-permute-start.9
  27.7 3.0 %collective-permute-done.10 = bf16[1,2,64,1152]{3,2,1,0:T(8,128)(2,1)S(1)} collective-permute-done((bf16[1,2,64,1152]{3,2,1,0:T(8,128)(2,1)S(1)}, bf16[1,2,64,1152]{3,2,1,0:T(8,128)(2,1)S(1)}, u32[]{:S(2)}, u32[]{:S(2)}) %collective-permute-start.10) | collective-permute-done | bytes 294944 | tf_op jit(solution)/shard_map/ppermute | solution.py:435
  30.7 0.1 pad_maximum_fusion.1.refs_2_
  30.8 0.8 collective-permute-start.11
  31.6 7.4 %collective-permute-done.7 = bf16[1,144,864]{2,1,0:T(8,128)(2,1)S(1)} collective-permute-done((bf16[1,144,864]{2,1,0:T(8,128)(2,1)S(1)}, bf16[1,144,864]{2,1,0:T(8,128)(2,1)S(1)}, u32[]{:S(2)}, u32[]{:S(2)}) %collective-permute-start.7) | collective-permute-done | bytes 248864 | tf_op jit(solution)/shard_map/ppermute | solution.py:435
  39.0 0.1 pad_maximum_fusion.2.refs_0_
  39.1 0.1 collective-permute-start.8
  39.2 3.1 %collective-permute-start.5 = (bf16[144,1152]{1,0:T(8,128)(2,1)S(1)}, bf16[144,1152]{1,0:T(8,128)(2,1)S(1)}, u32[]{:S(2)}, u32[]{:S(2)}) collective-permute-start(bf16[144,1152]{1,0:T(8,128)(2,1)S(1)} %copy-done.13), channel_id=1, source_target_pairs={{0,0},{1,1},{2,18},{3,19},{4,8},{5,9},{6,26},{7,27},{8,4},{9,5},{1... | collective-permute-start | bytes 995336 | tf_op jit(solution)/shard_map/ppermute | solution.py:482
  42.3 0.5 collective-permute-done.9.refs_1_
  42.8 13.8 %collective-permute-done.8.refs_1_ = bf16[2,144,864]{2,1,0:T(8,128)(2,1)S(1)} collective-permute-done((bf16[2,144,864]{2,1,0:T(8,128)(2,1)S(1)}, bf16[2,144,864]{2,1,0:T(8,128)(2,1)S(1)}, u32[]{:S(2)}, u32[]{:S(2)}) %collective-permute-start.8) | collective-permute-done | bytes 497696 | tf_op jit(solution)/shard_map/ppermute | solution.py:438
  56.6 0.9 copy-done.9
  57.5 4.5 %prepare.1 = (bf16[8,64,1152]{2,1,0:T(8,128)(2,1)}, bf16[8,64,1152]{2,1,0:T(8,128)(2,1)}) custom-call(s32[4]{0:T(128)} %pad_add_fusion.1.pos_ref, s32[16]{0:T(128)} %fusion.2.info_ref, bf16[2,2,64,1152]{3,2,1,0:T(8,128)(2,1)} %copy-done, bf16[2,2,64,1152]{3,2,1,0:T(8,128)(2,1)} %copy-done.8, bf16[2,2,64,1152]{3,2,1,0:T(8,128)(2,1)} %copy-done.1, ...), custom_call_target="tpu_custom_call" | custom-call | flops 1769472000 | bytes 2359296 | tf_op jit(solution)/shard_map/prepare/pallas_call | solution.py:508
  62.1 0.1 collective-permute-start.12
  62.1 0.5 collective-permute-start.13
  62.6 0.1 collective-permute-start.14
  62.7 2.5 %collective-permute-done.14.refs_5_ = bf16[144,1152]{1,0:T(8,128)(2,1)S(1)} collective-permute-done((bf16[144,1152]{1,0:T(8,128)(2,1)S(1)}, bf16[144,1152]{1,0:T(8,128)(2,1)S(1)}, u32[]{:S(2)}, u32[]{:S(2)}) %collective-permute-start.14) | collective-permute-done | bytes 331808 | tf_op jit(solution)/shard_map/ppermute | solution.py:520
  65.3 0.7 copy-done.15
  66.0 0.3 copy-done.11
  66.2 0.1 copy-done.12
  66.4 11.3 %forward.1 = (bf16[2,8,64,144]{3,2,1,0:T(8,128)(2,1)}, bf16[2,8,64,144]{3,2,1,0:T(8,128)(2,1)}, bf16[2,8,64,144]{3,2,1,0:T(8,128)(2,1)}, bf16[2,8,64,144]{3,2,1,...) custom-call(s32[4]{0:T(128)} %pad_add_fusion.1.pos_ref, ...), custom_call_target="tpu_custom_call" | custom-call | flops 8257536000 | bytes 2359296 | tf_op jit(solution)/shard_map/forward/pallas_call | solution.py:524
  77.6 0.1 collective-permute-start.15
  77.8 0.2 collective-permute-start.17
  78.0 3.3 %collective-permute-start.19 = (bf16[2,64,1152]{2,1,0:T(8,128)(2,1)}, bf16[2,64,1152]{2,1,0:T(8,128)(2,1)S(1)}, u32[]{:S(2)}, u32[]{:S(2)}) collective-permute-start(bf16[2,64,1152]{2,1,0:T(8,128)(2,1)} %get-tuple-element.84), channel_id=1, source_target_pairs={{0,17},{1,16},{2,19},{3,18},{4,21},{5,20},{6,23},{7,22},{8,25},{9,... | collective-permute-start | bytes 884744 | tf_op jit(solution)/shard_map/ppermute | solution.py:441
  81.3 1.2 slice_add_fusion
  82.4 0.1 collective-permute-start.16
  82.5 9.6 %backward.1 = (f32[2,64,1152]{2,1,0:T(8,128)}, bf16[2,64,1152]{2,1,0:T(8,128)(2,1)}, bf16[2,64,1152]{2,1,0:T(8,128)(2,1)}, bf16[2,64,1152]{2,1,0:T(8,128)(2,1)}) custom-call(s32[4]{0:T(128)} %pad_add_fusion.1.pos_ref, s32[16]{0:T(128)} %fusion.2.info_ref, bf16[2,144,864]{2,1,0:T(8,128)(2,1)} %copy-done.2, bf16[2,144,864]{2,1,0:T(8,128)(2,1)} %copy-done.10, ...), custom_call_target="tpu_custom_call" | custom-call | flops 5898240000 | bytes 2359296 | tf_op jit(solution)/shard_map/backward/pallas_call | solution.py:550
  92.1 1.5 %collective-permute-done.18.refs_4_ = bf16[2,64,1152]{2,1,0:T(8,128)(2,1)S(1)} collective-permute-done((bf16[2,64,1152]{2,1,0:T(8,128)(2,1)}, bf16[2,64,1152]{2,1,0:T(8,128)(2,1)S(1)}, u32[]{:S(2)}, u32[]{:S(2)}) %collective-permute-start.18) | collective-permute-done | bytes 294944 | tf_op jit(solution)/shard_map/ppermute | solution.py:441
  93.6 1.8 %collective-permute-start.20 = (bf16[2,64,1152]{2,1,0:T(8,128)(2,1)}, bf16[2,64,1152]{2,1,0:T(8,128)(2,1)S(1)}, u32[]{:S(2)}, u32[]{:S(2)}) collective-permute-start(bf16[2,64,1152]{2,1,0:T(8,128)(2,1)} %get-tuple-element.90), channel_id=1, source_target_pairs={{0,1},{1,0},{2,3},{3,2},{4,5},{5,4},{6,7},{7,6},{8,9},{9,8},{10,11... | collective-permute-start | bytes 884744 | tf_op jit(solution)/shard_map/ppermute | solution.py:441
  95.4 0.3 collective-permute-start.21
  95.7 1.5 %collective-permute-start.22 = (bf16[2,64,1152]{2,1,0:T(8,128)(2,1)}, bf16[2,64,1152]{2,1,0:T(8,128)(2,1)S(1)}, u32[]{:S(2)}, u32[]{:S(2)}) collective-permute-start(bf16[2,64,1152]{2,1,0:T(8,128)(2,1)} %get-tuple-element.92), channel_id=1, source_target_pairs={{0,17},{1,16},{2,19},{3,18},{4,21},{5,20},{6,23},{7,22},{8,25},{9,... | collective-permute-start | bytes 884744 | tf_op jit(solution)/shard_map/ppermute | solution.py:441
  97.2 6.6 %collective-permute-done.20.refs_7_ = bf16[2,64,1152]{2,1,0:T(8,128)(2,1)S(1)} collective-permute-done((bf16[2,64,1152]{2,1,0:T(8,128)(2,1)}, bf16[2,64,1152]{2,1,0:T(8,128)(2,1)S(1)}, u32[]{:S(2)}, u32[]{:S(2)}) %collective-permute-start.20) | collective-permute-done | bytes 294944 | tf_op jit(solution)/shard_map/ppermute | solution.py:441
  103.8 0.1 collective-permute-start.25
  103.9 5.9 %collective-permute-done.21.refs_8_ = bf16[2,64,1152]{2,1,0:T(8,128)(2,1)S(1)} collective-permute-done((bf16[2,64,1152]{2,1,0:T(8,128)(2,1)}, bf16[2,64,1152]{2,1,0:T(8,128)(2,1)S(1)}, u32[]{:S(2)}, u32[]{:S(2)}) %collective-permute-start.21) | collective-permute-done | bytes 294944 | tf_op jit(solution)/shard_map/ppermute | solution.py:441
  109.9 0.7 copy-done.20
  110.5 0.7 copy-done.21
  111.3 4.0 %output.1 = (bf16[1,2,64,1152]{3,2,1,0:T(8,128)(2,1)}, bf16[1,2,64,1152]{3,2,1,0:T(8,128)(2,1)}) custom-call(s32[4]{0:T(128)} %pad_add_fusion.1.pos_ref, s32[16]{0:T(128)} %fusion.2.info_ref, bf16[1,2,64,1152]{3,2,1,0:T(8,128)(2,1)} %copy-done.3, bf16[1,2,64,1152]{3,2,1,0:T(8,128)(2,1)} %copy-done.4, f32[2,64,1152]{2,1,0:T(8,128)} %get-tuple-element.85.refs_2_, ...), custom_call_target="tpu_custom_call" | custom-call | flops 1769472000 | bytes 2359296 | tf_op jit(solution)/shard_map/output/pallas_call | solution.py:563
  115.2 1.9 %collective-permute-start.23 = (bf16[1,2,64,1152]{3,2,1,0:T(8,128)(2,1)}, bf16[1,2,64,1152]{3,2,1,0:T(8,128)(2,1)S(1)}, u32[]{:S(2)}, u32[]{:S(2)}) collective-permute-start(bf16[1,2,64,1152]{3,2,1,0:T(8,128)(2,1)} %get-tuple-element.93), channel_id=1, source_target_pairs={{0,0},{1,1},{16,2},{17,3},{2,4},{3,5},{18,6},{19,7},{20,8},{21,9},... | collective-permute-start | bytes 884744 | tf_op jit(solution)/shard_map/ppermute | solution.py:572
  117.2 3.7 %collective-permute-start.24 = (bf16[1,2,64,1152]{3,2,1,0:T(8,128)(2,1)}, bf16[1,2,64,1152]{3,2,1,0:T(8,128)(2,1)S(1)}, u32[]{:S(2)}, u32[]{:S(2)}) collective-permute-start(bf16[1,2,64,1152]{3,2,1,0:T(8,128)(2,1)} %get-tuple-element.94), channel_id=1, source_target_pairs={{2,0},{3,1},{18,2},{19,3},{0,4},{1,5},{16,6},{17,7},{22,8},{23,9},... | collective-permute-start | bytes 884744 | tf_op jit(solution)/shard_map/ppermute | solution.py:572
  120.9 2.9 %collective-permute-start.26 = (f32[48,864]{1,0:T(8,128)S(1)}, f32[48,864]{1,0:T(8,128)S(1)}, u32[]{:S(2)}, u32[]{:S(2)}) collective-permute-start(f32[48,864]{1,0:T(8,128)S(1)} %bitcast.32), channel_id=1, source_target_pairs={{0,0},{1,1},{2,8},{3,9},{4,16},{5,17},{6,24},{7,25},{8,4},{9,5},{1... | collective-permute-start | bytes 497672 | tf_op jit(solution)/shard_map/ppermute | solution.py:590
  123.9 11.6 %collective-permute-done.23 = bf16[1,2,64,1152]{3,2,1,0:T(8,128)(2,1)S(1)} collective-permute-done((bf16[1,2,64,1152]{3,2,1,0:T(8,128)(2,1)}, bf16[1,2,64,1152]{3,2,1,0:T(8,128)(2,1)S(1)}, u32[]{:S(2)}, u32[]{:S(2)}) %collective-permute-start.23) | collective-permute-done | bytes 294944 | tf_op jit(solution)/shard_map/ppermute | solution.py:572
  135.5 0.1 select_bitcast_fusion.1
  135.6 0.9 pad_maximum_fusion.3
  136.4 3.0 %collective-permute-done.26 = f32[48,864]{1,0:T(8,128)S(1)} collective-permute-done((f32[48,864]{1,0:T(8,128)S(1)}, f32[48,864]{1,0:T(8,128)S(1)}, u32[]{:S(2)}, u32[]{:S(2)}) %collective-permute-start.26) | collective-permute-done | bytes 165920 | tf_op jit(solution)/shard_map/ppermute | solution.py:590
  139.4 0.1 fusion.6
  139.5 0.7 maximum_multiply_fusion
  (56 shorter events, 0.2 us)
Async XLA Ops:
  1.3 5.4 %copy-start.5 = (s32[1,4]{1,0:T(1,128)S(1)}, s32[1,4]{1,0:T(1,128)}, u32[]{:S(2)}) copy-start(s32[1,4]{1,0:T(1,128)} %param.12) | copy-start | bytes 52
  1.3 5.4 %copy-start.6 = (s32[1,4]{1,0:T(1,128)S(1)}, s32[1,4]{1,0:T(1,128)}, u32[]{:S(2)}) copy-start(s32[1,4]{1,0:T(1,128)} %param.11) | copy-start | bytes 52
  1.3 5.4 %copy-start.7 = (s32[1,8]{1,0:T(1,128)S(1)}, s32[1,8]{1,0:T(1,128)}, u32[]{:S(2)}) copy-start(s32[1,8]{1,0:T(1,128)} %param.10) | copy-start | bytes 100
  4.7 9.1 %collective-permute-start.2 = (bf16[1,2,64,1152]{3,2,1,0:T(8,128)(2,1)}, bf16[1,2,64,1152]{3,2,1,0:T(8,128)(2,1)S(1)}, u32[]{:S(2)}, u32[]{:S(2)}) collective-permute-start(bf16[1,2,64,1152]{3,2,1,0:T(8,128)(2,1)} %get-tuple-element.51), channel_id=1, source_target_pairs={{0,0},{1,1},{2,16},{3,17},{4,2},{5,3},{6,18},{7,19},{8,20},{9,21},... | collective-permute-start | bytes 884744 | tf_op jit(solution)/shard_map/ppermute | solution.py:467
  6.7 4.3 %collective-permute-start = (s32[1,16]{1,0:T(1,128)S(1)}, s32[1,16]{1,0:T(1,128)S(1)}, u32[]{:S(2)}, u32[]{:S(2)}) collective-permute-start(s32[1,16]{1,0:T(1,128)S(1)} %fusion.7), channel_id=1, source_target_pairs={{0,8},{1,9},{2,10},{3,11},{4,12},{5,13},{6,14},{7,15},{8,0},{9,1},... | collective-permute-start | bytes 200 | tf_op jit(solution)/shard_map/ppermute | solution.py:445
  6.8 8.5 %collective-permute-start.6 = (bf16[144,432]{1,0:T(8,128)(2,1)}, bf16[144,432]{1,0:T(8,128)(2,1)S(1)}, u32[]{:S(2)}, u32[]{:S(2)}) collective-permute-start(bf16[144,432]{1,0:T(8,128)(2,1)} %get-tuple-element.56), channel_id=1, source_target_pairs={{0,1},{1,0},{2,3},{3,2},{4,5},{5,4},{6,7},{7,6},{8,9},{9,8},{10,11... | collective-permute-start | bytes 373256 | tf_op jit(solution)/shard_map/ppermute | solution.py:469
  7.3 13.7 %collective-permute-start.3 = (bf16[1,2,64,1152]{3,2,1,0:T(8,128)(2,1)}, bf16[1,2,64,1152]{3,2,1,0:T(8,128)(2,1)S(1)}, u32[]{:S(2)}, u32[]{:S(2)}) collective-permute-start(bf16[1,2,64,1152]{3,2,1,0:T(8,128)(2,1)} %get-tuple-element.52), channel_id=1, source_target_pairs={{0,2},{1,3},{2,18},{3,19},{4,0},{5,1},{6,16},{7,17},{8,22},{9,23},... | collective-permute-start | bytes 884744 | tf_op jit(solution)/shard_map/ppermute | solution.py:467
  11.0 3.7 %collective-permute-start.1 = (s32[2,16]{1,0:T(2,128)S(1)}, s32[2,16]{1,0:T(2,128)S(1)}, u32[]{:S(2)}, u32[]{:S(2)}) collective-permute-start(s32[2,16]{1,0:T(2,128)S(1)} %pad_add_fusion), channel_id=1, source_target_pairs={{0,16},{1,17},{2,18},{3,19},{4,20},{5,21},{6,22},{7,23},{8,24},{9,... | collective-permute-start | bytes 392 | tf_op jit(solution)/shard_map/ppermute | solution.py:447
  13.8 16.9 %copy-start.3 = (bf16[1,2,64,1152]{3,2,1,0:T(8,128)(2,1)}, bf16[1,2,64,1152]{3,2,1,0:T(8,128)(2,1)S(1)}, u32[]{:S(2)}) copy-start(bf16[1,2,64,1152]{3,2,1,0:T(8,128)(2,1)S(1)} %collective-permute-done.2.refs_0_) | copy-start | bytes 884740
  13.8 7.8 %collective-permute-start.4 = (bf16[1,2,64,1152]{3,2,1,0:T(8,128)(2,1)S(1)}, bf16[1,2,64,1152]{3,2,1,0:T(8,128)(2,1)S(1)}, u32[]{:S(2)}, u32[]{:S(2)}) collective-permute-start(bf16[1,2,64,1152]{3,2,1,0:T(8,128)(2,1)S(1)} %collective-permute-done.2.refs_0_), channel_id=1, source_target_pairs={{0,1},{1,0},{2,3},{3,2},{4,5},{5,4},{6,7},{7,6},{8,9},{9,8},{10,11... | collective-permute-start | bytes 884744 | tf_op jit(solution)/shard_map/ppermute | solution.py:477
  21.0 9.7 %copy-start.4 = (bf16[1,2,64,1152]{3,2,1,0:T(8,128)(2,1)}, bf16[1,2,64,1152]{3,2,1,0:T(8,128)(2,1)S(1)}, u32[]{:S(2)}) copy-start(bf16[1,2,64,1152]{3,2,1,0:T(8,128)(2,1)S(1)} %collective-permute-done.3.refs_1_) | copy-start | bytes 884740
  21.7 9.0 %collective-permute-start.10 = (bf16[1,2,64,1152]{3,2,1,0:T(8,128)(2,1)S(1)}, bf16[1,2,64,1152]{3,2,1,0:T(8,128)(2,1)S(1)}, u32[]{:S(2)}, u32[]{:S(2)}) collective-permute-start(bf16[1,2,64,1152]{3,2,1,0:T(8,128)(2,1)S(1)} %collective-permute-done.3.refs_1_), channel_id=1, source_target_pairs={{0,16},{1,17},{2,18},{3,19},{4,20},{5,21},{6,22},{7,23},{8,24},{9,... | collective-permute-start | bytes 884744 | tf_op jit(solution)/shard_map/ppermute | solution.py:435
  22.9 16.1 %collective-permute-start.7 = (bf16[1,144,864]{2,1,0:T(8,128)(2,1)S(1)}, bf16[1,144,864]{2,1,0:T(8,128)(2,1)S(1)}, u32[]{:S(2)}, u32[]{:S(2)}) collective-permute-start(bf16[1,144,864]{2,1,0:T(8,128)(2,1)S(1)} %maximum_bitcast_fusion), channel_id=1, source_target_pairs={{0,4},{1,5},{2,6},{3,7},{4,0},{5,1},{6,2},{7,3},{8,12},{9,13},{10,... | collective-permute-start | bytes 746504 | tf_op jit(solution)/shard_map/ppermute | solution.py:435
  26.7 29.9 %copy-start = (bf16[2,2,64,1152]{3,2,1,0:T(8,128)(2,1)}, bf16[2,2,64,1152]{3,2,1,0:T(8,128)(2,1)S(1)}, u32[]{:S(2)}) copy-start(bf16[2,2,64,1152]{3,2,1,0:T(8,128)(2,1)S(1)} %pad_maximum_fusion.refs_0_) | copy-start | bytes 1769476
  26.7 12.5 %copy-start.13 = (bf16[144,1152]{1,0:T(8,128)(2,1)S(1)}, bf16[144,1152]{1,0:T(8,128)(2,1)}, u32[]{:S(2)}) copy-start(bf16[144,1152]{1,0:T(8,128)(2,1)} %param.15) | copy-start | bytes 995332
  26.7 16.1 %collective-permute-start.9 = (bf16[2,2,64,1152]{3,2,1,0:T(8,128)(2,1)S(1)}, bf16[2,2,64,1152]{3,2,1,0:T(8,128)(2,1)S(1)}, u32[]{:S(2)}, u32[]{:S(2)}) collective-permute-start(bf16[2,2,64,1152]{3,2,1,0:T(8,128)(2,1)S(1)} %pad_maximum_fusion.refs_0_), channel_id=1, source_target_pairs={{0,16},{1,17},{2,18},{3,19},{4,20},{5,21},{6,22},{7,23},{8,24},{9,... | collective-permute-start | bytes 1769480 | tf_op jit(solution)/shard_map/ppermute | solution.py:438
  30.8 25.8 %copy-start.1 = (bf16[2,2,64,1152]{3,2,1,0:T(8,128)(2,1)}, bf16[2,2,64,1152]{3,2,1,0:T(8,128)(2,1)S(1)}, u32[]{:S(2)}) copy-start(bf16[2,2,64,1152]{3,2,1,0:T(8,128)(2,1)S(1)} %pad_maximum_fusion.1.refs_2_) | copy-start | bytes 1769476
  30.8 25.8 %collective-permute-start.11 = (bf16[2,2,64,1152]{3,2,1,0:T(8,128)(2,1)S(1)}, bf16[2,2,64,1152]{3,2,1,0:T(8,128)(2,1)S(1)}, u32[]{:S(2)}, u32[]{:S(2)}) collective-permute-start(bf16[2,2,64,1152]{3,2,1,0:T(8,128)(2,1)S(1)} %pad_maximum_fusion.1.refs_2_), channel_id=1, source_target_pairs={{0,1},{1,0},{2,3},{3,2},{4,5},{5,4},{6,7},{7,6},{8,9},{9,8},{10,11... | collective-permute-start | bytes 1769480 | tf_op jit(solution)/shard_map/ppermute | solution.py:438
  39.1 23.0 %copy-start.2 = (bf16[2,144,864]{2,1,0:T(8,128)(2,1)}, bf16[2,144,864]{2,1,0:T(8,128)(2,1)S(1)}, u32[]{:S(2)}) copy-start(bf16[2,144,864]{2,1,0:T(8,128)(2,1)S(1)} %pad_maximum_fusion.2.refs_0_) | copy-start | bytes 1492996
  39.1 17.5 %collective-permute-start.8 = (bf16[2,144,864]{2,1,0:T(8,128)(2,1)S(1)}, bf16[2,144,864]{2,1,0:T(8,128)(2,1)S(1)}, u32[]{:S(2)}, u32[]{:S(2)}) collective-permute-start(bf16[2,144,864]{2,1,0:T(8,128)(2,1)S(1)} %pad_maximum_fusion.2.refs_0_), channel_id=1, source_target_pairs={{0,2},{1,3},{2,0},{3,1},{4,6},{5,7},{6,4},{7,5},{8,10},{9,11},{10,... | collective-permute-start | bytes 1493000 | tf_op jit(solution)/shard_map/ppermute | solution.py:438
  39.2 22.9 %collective-permute-start.5 = (bf16[144,1152]{1,0:T(8,128)(2,1)S(1)}, bf16[144,1152]{1,0:T(8,128)(2,1)S(1)}, u32[]{:S(2)}, u32[]{:S(2)}) collective-permute-start(bf16[144,1152]{1,0:T(8,128)(2,1)S(1)} %copy-done.13), channel_id=1, source_target_pairs={{0,0},{1,1},{2,18},{3,19},{4,8},{5,9},{6,26},{7,27},{8,4},{9,5},{1... | collective-permute-start | bytes 995336 | tf_op jit(solution)/shard_map/ppermute | solution.py:482
  42.8 13.8 %copy-start.8 = (bf16[2,2,64,1152]{3,2,1,0:T(8,128)(2,1)}, bf16[2,2,64,1152]{3,2,1,0:T(8,128)(2,1)S(1)}, u32[]{:S(2)}) copy-start(bf16[2,2,64,1152]{3,2,1,0:T(8,128)(2,1)S(1)} %collective-permute-done.9.refs_1_) | copy-start | bytes 1769476
  56.6 8.7 %copy-start.10 = (bf16[2,144,864]{2,1,0:T(8,128)(2,1)}, bf16[2,144,864]{2,1,0:T(8,128)(2,1)S(1)}, u32[]{:S(2)}) copy-start(bf16[2,144,864]{2,1,0:T(8,128)(2,1)S(1)} %collective-permute-done.8.refs_1_) | copy-start | bytes 1492996
  56.6 0.9 copy-start.9
  62.0 3.2 %copy-start.14 = (bf16[144,1152]{1,0:T(8,128)(2,1)}, bf16[144,1152]{1,0:T(8,128)(2,1)S(1)}, u32[]{:S(2)}) copy-start(bf16[144,1152]{1,0:T(8,128)(2,1)S(1)} %collective-permute-done.5.refs_4_) | copy-start | bytes 995332
  62.1 3.2 %collective-permute-start.12 = (bf16[2,144,864]{2,1,0:T(8,128)(2,1)S(1)}, bf16[2,144,864]{2,1,0:T(8,128)(2,1)S(1)}, u32[]{:S(2)}, u32[]{:S(2)}) collective-permute-start(bf16[2,144,864]{2,1,0:T(8,128)(2,1)S(1)} %pad_maximum_fusion.2.refs_0_), channel_id=1, source_target_pairs={{0,8},{1,9},{2,10},{3,11},{4,12},{5,13},{6,14},{7,15},{8,0},{9,1},... | collective-permute-start | bytes 1493000 | tf_op jit(solution)/shard_map/ppermute | solution.py:519
  62.1 3.1 %collective-permute-start.13 = (bf16[2,144,864]{2,1,0:T(8,128)(2,1)S(1)}, bf16[2,144,864]{2,1,0:T(8,128)(2,1)S(1)}, u32[]{:S(2)}, u32[]{:S(2)}) collective-permute-start(bf16[2,144,864]{2,1,0:T(8,128)(2,1)S(1)} %collective-permute-done.8.refs_1_), channel_id=1, source_target_pairs={{0,8},{1,9},{2,10},{3,11},{4,12},{5,13},{6,14},{7,15},{8,0},{9,1},... | collective-permute-start | bytes 1493000 | tf_op jit(solution)/shard_map/ppermute | solution.py:519
  62.6 2.6 %collective-permute-start.14 = (bf16[144,1152]{1,0:T(8,128)(2,1)S(1)}, bf16[144,1152]{1,0:T(8,128)(2,1)S(1)}, u32[]{:S(2)}, u32[]{:S(2)}) collective-permute-start(bf16[144,1152]{1,0:T(8,128)(2,1)S(1)} %collective-permute-done.5.refs_4_), channel_id=1, source_target_pairs={{0,8},{1,9},{2,10},{3,11},{4,12},{5,13},{6,14},{7,15},{8,0},{9,1},... | collective-permute-start | bytes 995336 | tf_op jit(solution)/shard_map/ppermute | solution.py:520
  65.2 0.7 copy-start.15
  65.3 1.0 copy-start.11
  65.3 1.1 copy-start.12
  77.6 3.6 %collective-permute-start.15 = (f32[4,48,864]{2,1,0:T(8,128)}, f32[4,48,864]{2,1,0:T(8,128)S(1)}, u32[]{:S(2)}, u32[]{:S(2)}) collective-permute-start(f32[4,48,864]{2,1,0:T(8,128)} %get-tuple-element.74), channel_id=1, source_target_pairs={{0,8},{1,9},{2,10},{3,11},{4,12},{5,13},{6,14},{7,15},{8,0},{9,1},... | collective-permute-start | bytes 1990664 | tf_op jit(solution)/shard_map/ppermute | solution.py:542
  77.8 14.3 %collective-permute-start.17 = (bf16[2,64,1152]{2,1,0:T(8,128)(2,1)}, bf16[2,64,1152]{2,1,0:T(8,128)(2,1)S(1)}, u32[]{:S(2)}, u32[]{:S(2)}) collective-permute-start(bf16[2,64,1152]{2,1,0:T(8,128)(2,1)} %get-tuple-element.82), channel_id=1, source_target_pairs={{0,1},{1,0},{2,3},{3,2},{4,5},{5,4},{6,7},{7,6},{8,9},{9,8},{10,11... | collective-permute-start | bytes 884744 | tf_op jit(solution)/shard_map/ppermute | solution.py:441
  78.0 15.6 %collective-permute-start.18 = (bf16[2,64,1152]{2,1,0:T(8,128)(2,1)}, bf16[2,64,1152]{2,1,0:T(8,128)(2,1)S(1)}, u32[]{:S(2)}, u32[]{:S(2)}) collective-permute-start(bf16[2,64,1152]{2,1,0:T(8,128)(2,1)} %get-tuple-element.83), channel_id=1, source_target_pairs={{0,16},{1,17},{2,18},{3,19},{4,20},{5,21},{6,22},{7,23},{8,24},{9,... | collective-permute-start | bytes 884744 | tf_op jit(solution)/shard_map/ppermute | solution.py:441
  78.0 15.6 %collective-permute-start.19 = (bf16[2,64,1152]{2,1,0:T(8,128)(2,1)}, bf16[2,64,1152]{2,1,0:T(8,128)(2,1)S(1)}, u32[]{:S(2)}, u32[]{:S(2)}) collective-permute-start(bf16[2,64,1152]{2,1,0:T(8,128)(2,1)} %get-tuple-element.84), channel_id=1, source_target_pairs={{0,17},{1,16},{2,19},{3,18},{4,21},{5,20},{6,23},{7,22},{8,25},{9,... | collective-permute-start | bytes 884744 | tf_op jit(solution)/shard_map/ppermute | solution.py:441
  82.4 11.2 %collective-permute-start.16 = (f32[2,48,864]{2,1,0:T(8,128)S(1)}, f32[2,48,864]{2,1,0:T(8,128)S(1)}, u32[]{:S(2)}, u32[]{:S(2)}) collective-permute-start(f32[2,48,864]{2,1,0:T(8,128)S(1)} %get-tuple-element.80), channel_id=1, source_target_pairs={{0,2},{1,3},{2,0},{3,1},{4,6},{5,7},{6,4},{7,5},{8,10},{9,11},{10,... | collective-permute-start | bytes 995336 | tf_op jit(solution)/shard_map/ppermute | solution.py:548
  92.1 17.8 %copy-start.16 = (bf16[2,64,1152]{2,1,0:T(8,128)(2,1)}, bf16[2,64,1152]{2,1,0:T(8,128)(2,1)S(1)}, u32[]{:S(2)}) copy-start(bf16[2,64,1152]{2,1,0:T(8,128)(2,1)S(1)} %collective-permute-done.17.refs_3_) | copy-start | bytes 884740
  93.6 16.2 %copy-start.17 = (bf16[2,64,1152]{2,1,0:T(8,128)(2,1)}, bf16[2,64,1152]{2,1,0:T(8,128)(2,1)S(1)}, u32[]{:S(2)}) copy-start(bf16[2,64,1152]{2,1,0:T(8,128)(2,1)S(1)} %collective-permute-done.18.refs_4_) | copy-start | bytes 884740
  93.6 16.2 %copy-start.18 = (bf16[2,64,1152]{2,1,0:T(8,128)(2,1)}, bf16[2,64,1152]{2,1,0:T(8,128)(2,1)S(1)}, u32[]{:S(2)}) copy-start(bf16[2,64,1152]{2,1,0:T(8,128)(2,1)S(1)} %collective-permute-done.19.refs_5_) | copy-start | bytes 884740
  93.6 10.2 %collective-permute-start.20 = (bf16[2,64,1152]{2,1,0:T(8,128)(2,1)}, bf16[2,64,1152]{2,1,0:T(8,128)(2,1)S(1)}, u32[]{:S(2)}, u32[]{:S(2)}) collective-permute-start(bf16[2,64,1152]{2,1,0:T(8,128)(2,1)} %get-tuple-element.90), channel_id=1, source_target_pairs={{0,1},{1,0},{2,3},{3,2},{4,5},{5,4},{6,7},{7,6},{8,9},{9,8},{10,11... | collective-permute-start | bytes 884744 | tf_op jit(solution)/shard_map/ppermute | solution.py:441
  95.4 14.4 %collective-permute-start.21 = (bf16[2,64,1152]{2,1,0:T(8,128)(2,1)}, bf16[2,64,1152]{2,1,0:T(8,128)(2,1)S(1)}, u32[]{:S(2)}, u32[]{:S(2)}) collective-permute-start(bf16[2,64,1152]{2,1,0:T(8,128)(2,1)} %get-tuple-element.91), channel_id=1, source_target_pairs={{0,16},{1,17},{2,18},{3,19},{4,20},{5,21},{6,22},{7,23},{8,24},{9,... | collective-permute-start | bytes 884744 | tf_op jit(solution)/shard_map/ppermute | solution.py:441
  95.7 14.1 %collective-permute-start.22 = (bf16[2,64,1152]{2,1,0:T(8,128)(2,1)}, bf16[2,64,1152]{2,1,0:T(8,128)(2,1)S(1)}, u32[]{:S(2)}, u32[]{:S(2)}) collective-permute-start(bf16[2,64,1152]{2,1,0:T(8,128)(2,1)} %get-tuple-element.92), channel_id=1, source_target_pairs={{0,17},{1,16},{2,19},{3,18},{4,21},{5,20},{6,23},{7,22},{8,25},{9,... | collective-permute-start | bytes 884744 | tf_op jit(solution)/shard_map/ppermute | solution.py:441
  103.8 6.0 %copy-start.19 = (bf16[2,64,1152]{2,1,0:T(8,128)(2,1)}, bf16[2,64,1152]{2,1,0:T(8,128)(2,1)S(1)}, u32[]{:S(2)}) copy-start(bf16[2,64,1152]{2,1,0:T(8,128)(2,1)S(1)} %collective-permute-done.20.refs_7_) | copy-start | bytes 884740
  103.8 17.1 %collective-permute-start.25 = (f32[1,48,864]{2,1,0:T(8,128)S(1)}, f32[1,48,864]{2,1,0:T(8,128)S(1)}, u32[]{:S(2)}, u32[]{:S(2)}) collective-permute-start(f32[1,48,864]{2,1,0:T(8,128)S(1)} %slice.60), channel_id=1, source_target_pairs={{0,4},{1,5},{2,6},{3,7},{4,0},{5,1},{6,2},{7,3},{8,12},{9,13},{10,... | collective-permute-start | bytes 497672 | tf_op jit(solution)/shard_map/ppermute | solution.py:588
  109.8 0.7 copy-start.20
  110.5 0.7 copy-start.21
  115.2 20.3 %collective-permute-start.23 = (bf16[1,2,64,1152]{3,2,1,0:T(8,128)(2,1)}, bf16[1,2,64,1152]{3,2,1,0:T(8,128)(2,1)S(1)}, u32[]{:S(2)}, u32[]{:S(2)}) collective-permute-start(bf16[1,2,64,1152]{3,2,1,0:T(8,128)(2,1)} %get-tuple-element.93), channel_id=1, source_target_pairs={{0,0},{1,1},{16,2},{17,3},{2,4},{3,5},{18,6},{19,7},{20,8},{21,9},... | collective-permute-start | bytes 884744 | tf_op jit(solution)/shard_map/ppermute | solution.py:572
  117.2 18.3 %collective-permute-start.24 = (bf16[1,2,64,1152]{3,2,1,0:T(8,128)(2,1)}, bf16[1,2,64,1152]{3,2,1,0:T(8,128)(2,1)S(1)}, u32[]{:S(2)}, u32[]{:S(2)}) collective-permute-start(bf16[1,2,64,1152]{3,2,1,0:T(8,128)(2,1)} %get-tuple-element.94), channel_id=1, source_target_pairs={{2,0},{3,1},{18,2},{19,3},{0,4},{1,5},{16,6},{17,7},{22,8},{23,9},... | collective-permute-start | bytes 884744 | tf_op jit(solution)/shard_map/ppermute | solution.py:572
  120.9 18.5 %collective-permute-start.26 = (f32[48,864]{1,0:T(8,128)S(1)}, f32[48,864]{1,0:T(8,128)S(1)}, u32[]{:S(2)}, u32[]{:S(2)}) collective-permute-start(f32[48,864]{1,0:T(8,128)S(1)} %bitcast.32), channel_id=1, source_target_pairs={{0,0},{1,1},{2,8},{3,9},{4,16},{5,17},{6,24},{7,25},{8,4},{9,5},{1... | collective-permute-start | bytes 497672 | tf_op jit(solution)/shard_map/ppermute | solution.py:590

commit v12 on v9

--- a/solution.py
+++ b/solution.py
@@ -197,14 +197,15 @@
 
 
 def fill_weights(lay, pos_ref, w_refs, w_scr):
+    order = lay.doubled(lay.bits(lay.nz)[::-1])
     block = w_scr.shape[1] // lay.nz
-    rows, width = w_refs[0].shape[0], w_scr.shape[2]
+    rows, width = w_refs[0].shape[1], w_scr.shape[2]
     for h in range(lay.halves):
-        for k in range(lay.nz):
-            ref = w_refs[h * lay.nz + k]
+        for n, k in enumerate(order):
+            ref, place = w_refs[2 * h + (2 * n) // lay.nz], n % (lay.nz // 2)
             for m in range(block // rows):
                 start = pl.multiple_of((pos_ref[2] ^ k) * block + m * rows, 16)
-                w_scr[h, pl.ds(start, rows), :] = ref[:, m * width : (m + 1) * width]
+                w_scr[h, pl.ds(start, rows), :] = ref[place, :, m * width : (m + 1) * width]
 
 
 def heads_stacked(lay, values):
@@ -242,7 +243,7 @@
 
 
 def forward_kernel(lay, pos_ref, info_ref, hid_ref, gp_ref, *refs):
-    w_refs, refs = refs[: lay.halves * lay.nz], refs[lay.halves * lay.nz :]
+    w_refs, refs = refs[: 2 * lay.halves], refs[2 * lay.halves :]
     wo_refs, refs = refs[: lay.nc], refs[lay.nc :]
     q_ref, k_ref, v_ref, ga_ref, kept_ref, sent_ref, *refs = refs
     pr_refs, (w_scr, att_scr, wo_scr, acc_scr, cut_scr) = refs[: lay.chips], refs[lay.chips :]
@@ -314,7 +315,7 @@
 
 
 def backward_kernel(lay, pos_ref, info_ref, *refs):
-    w_refs, refs = refs[: lay.halves * lay.nz], refs[lay.halves * lay.nz :]
+    w_refs, refs = refs[: 2 * lay.halves], refs[2 * lay.halves :]
     q_ref, k_ref, v_ref, ga_ref, *refs = refs
     gh_refs, (w_scr, gt_scr) = refs[: lay.chips], refs[lay.chips :]
     _, frames, step_patches, cols = q_ref.shape
@@ -437,21 +438,22 @@
         ky, kx = lay.chip_of(k)
         return lay.swap(ky=ky, kx=kx)
 
-    def doubling(held, bits, swap, after):
-        for bit in bits[:-1]:
-            held = jnp.concatenate([held, lax.ppermute(held, AXES, swap(bit))], axis=0)
-        held, _ = lax.optimization_barrier((held, after))
-        return [held, lax.ppermute(held, AXES, swap(bits[-1]))]
-
-    def over_chips(parts):
-        got = [lax.ppermute(parts[k], AXES, chip_swap(k)) for k in range(1, chips)]
-        return [parts[0]] + got
-
     def from_plane(parts):
         got = [lax.ppermute(part, AXES, lay.from_plane(k)) for k, part in enumerate(parts)]
         first = jnp.where(z // lay.ny == 0, got[0], got[1])
         second = jnp.where(z // lay.ny == 0, got[1], got[0])
         return jnp.concatenate([first, second], axis=0)[None]
+
+    def doubling(held, bits, swap, after, first=None):
+        for bit in bits[:-1]:
+            got = lax.ppermute(held, AXES, swap(bit)) if first is None else first
+            held, first = jnp.concatenate([held, got], axis=0), None
+        held, _ = lax.optimization_barrier((held, after))
+        return [held, lax.ppermute(held, AXES, swap(bits[-1]))]
+
+    def over_chips(parts):
+        got = [lax.ppermute(parts[k], AXES, chip_swap(k)) for k in range(1, chips)]
+        return [parts[0]] + got
 
     info = jnp.concatenate([clip_ids[0], clip_patches[0], clip_step[0]])[None]
     by_core = jnp.concatenate([info, lax.ppermute(info, AXES, lay.swap(kc=1))], axis=0)
@@ -485,26 +487,22 @@
     else:
         stacked = jnp.stack(by_x)
         ordered = [lax.dynamic_index_in_dim(stacked, x ^ i, 0, keepdims=False) for i in range(nx)]
-    w_own = jnp.concatenate(ordered, axis=1 if rows % 16 == 0 else 0)
-    own[0], _ = lax.optimization_barrier((own[0], w_own))
-    w_pieces = {0: w_own}
-    for bit in lay.bits(lay.nz):
-        w_pieces[bit] = lax.ppermute(w_own, AXES, lay.swap(kz=bit))
-    for k in range(1, lay.nz):
-        if k not in w_pieces:
-            bit = k & -k
-            w_pieces[k] = lax.ppermute(w_pieces[k ^ bit], AXES, lay.swap(kz=bit))
-    w_pieces = [w_pieces[k] for k in range(lay.nz)]
-    if halves > 1:
-        w_pieces += [lax.ppermute(piece, AXES, lay.swap(kc=1)) for piece in w_pieces[:-1]]
-
+    w_own = jnp.concatenate(ordered, axis=1 if rows % 16 == 0 else 0)[None]
+    first = lax.ppermute(own[0], AXES, chip_swap(lay.chip_bits(0)[0]))
+    own[1], first = lax.optimization_barrier((own[1], first))
+    w_own, _ = lax.optimization_barrier((w_own, own[1]))
+    w_pieces = doubling(w_own, lay.bits(lay.nz)[::-1], lambda kz: lay.swap(kz=kz), [])
     late_w_out, _ = lax.optimization_barrier((w_out, own))
     wo_own = lax.ppermute(late_w_out, AXES, lay.rows_to_chip())
 
     pairs = []
     for j in range(nc):
-        pairs += doubling(own[j], lay.chip_bits(j), chip_swap, info)
-    pairs, _ = lax.optimization_barrier((pairs, w_pieces[lay.nz :]))
+        after = ([], None) if j else (info, first)
+        pairs += doubling(own[j], lay.chip_bits(j), chip_swap, *after)
+    pairs, w_pieces, wo_own = lax.optimization_barrier((pairs, w_pieces, wo_own))
+    if halves > 1:
+        w_pieces += [lax.ppermute(piece, AXES, lay.swap(kc=1)) for piece in w_pieces]
+    wo_rows = [wo_own, lax.ppermute(wo_own, AXES, lay.swap(kc=1))]
 
 
     def spread(count, width, patches_at_once):
@@ -517,7 +515,7 @@
     few_steps = half // few
     x_spec = pl.BlockSpec((few, model), lambda i, *_: (i, 0))
     triple_spec = pl.BlockSpec((halves, lay.frames, step_patches, cols), lambda i, *_: (0, 0, i, 0))
-    w_specs = [whole_spec(w_own.shape)] * (halves * lay.nz)
+    w_specs = [whole_spec(w_pieces[0].shape)] * (2 * halves)
     w_scratch = pltpu.VMEM((halves, model, 3 * cols), BF16)
     mod_spec = whole_spec(mod_table.shape)
     triple_shape = struct((halves, lay.frames, half, cols))
@@ -533,11 +531,6 @@
         [struct((lay.frames, half, model))] * 2,
         grid=(few_steps,),
     )(pos, info, *pairs, mod_table)
-    wo_own, w_last, _ = lax.optimization_barrier((wo_own, w_pieces[lay.nz - 1], hidden))
-    wo_rows = [wo_own, lax.ppermute(wo_own, AXES, lay.swap(kc=1))]
-    w_pieces[lay.nz - 1] = w_last
-    if halves > 1:
-        w_pieces.append(lax.ppermute(w_last, AXES, lay.swap(kc=1)))
 
     fold = 3 if rows % 24 == 0 else 1
     piece_shape = (groups, rows // fold, quarter * fold)
@@ -580,26 +573,18 @@
     sums, first_away, projected = lax.optimization_barrier((sums, first_away, projected))
     grad_hidden = over_chips(sums)
 
-    projected, _ = lax.optimization_barrier((projected, grad_hidden[1]))
     out_parts = call(
         functools.partial(output_kernel, lay),
         "output",
-        3 * model * 1000,
+        20 * model * 1000,
         [pair_spec(1, few)] * nc + [spread(nc, model, few)] * chips + [mod_spec],
         [x_spec] * nc,
         [struct((half, model))] * nc,
         grid=(few_steps,),
     )(pos, info, *own, *projected, mod_table)
-
-    cut = cut + first_away
-    for bit in lay.bits(lay.nz)[1:]:
-        middle = middle // 2
-        away = lax.ppermute(cut[middle:], AXES, lay.swap(kz=bit))
-        away, _ = lax.optimization_barrier((away, out_parts))
-        cut = cut[:middle] + away
     out_y = from_plane(out_parts)
 
-
+    grad_hidden, _ = lax.optimization_barrier((grad_hidden, out_parts))
     grad_parts = call(
         functools.partial(input_grad_kernel, lay),
         "input_grad",
@@ -611,6 +596,10 @@
     )(pos, info, *own, *grad_hidden, mod_table)
     grad_x = from_plane(grad_parts)
 
+    cut, _ = lax.optimization_barrier((cut + first_away, out_parts))
+    for bit in lay.bits(lay.nz)[1:]:
+        middle = middle // 2
+        cut = cut[:middle] + lax.ppermute(cut[middle:], AXES, lay.swap(kz=bit))
     cut, _ = lax.optimization_barrier((cut, grad_parts))
     grad_w = lax.ppermute(cut[0], AXES, lay.to_owner())
     grad_w = jnp.concatenate(

time: 144 us -> 136 us (0.944)
  the two profiles are of different devices: /device:TPU:1 before, /device:TPU:4 now
where the time goes in v12:
time: 136 us; the launch traced here: 134 us
  starting transfers between devices  45.8 us (34%)
  waiting for transfers between devices  43.4 us (32%)
  Pallas kernels  35.1 us (26%)
  other arithmetic  5.98 us (4%)
  local copies, waits for them, and re-layouts  2.66 us (2%)
    ppermute x1, waiting for transfers between devices, local(): wo_own = lax.ppermute(late_w_out, AXES, lay.rows_to_chip())  15.2 us
    ppermute x4, starting transfers between devices, from_plane(): lax.ppermute(part, AXES, lay.from_plane(k))  14.7 us
    ppermute x2, waiting for transfers between devices, doubling(): got = lax.ppermute(held, AXES, swap(bit)) if first is None else first  11.4 us
    pallas_call x1, Pallas kernels, local(): call(functools.partial(forward_kernel, lay), 'forward', 14 * model * 1000...  11.2 us
    pallas_call x1, Pallas kernels, local(): call(functools.partial(backward_kernel, lay), 'backward', 10 * model * 10...  9.56 us
    ppermute x6, starting transfers between devices, over_chips(): got = [lax.ppermute(parts[k], AXES, chip_swap(k)) for k in range(1, chips)]  7.04 us
    ppermute x2, waiting for transfers between devices, local(): lax.ppermute(pair, AXES, lay.to_plane(k))  6.1 us
    ppermute x2, starting transfers between devices, doubling(): got = lax.ppermute(held, AXES, swap(bit)) if first is None else first  5.2 us
  transfers between devices with their start and end apart: 29, of which 9 were waited for; matrix products, arithmetic and copies ran while one was open for 3% of the time, Pallas kernels for 15%

profile of v12, /device:TPU:4, one launch (start us, length us, event | category | flops | bytes accessed | tf_op | source)
XLA Modules:
  0.0 134.1 jit_solution(4649698556783630995)
XLA Ops:
  0.6 0.6 pad_add_fusion.1.pos_ref
  1.3 3.4 %start.1 = (bf16[1,2,64,1152]{3,2,1,0:T(8,128)(2,1)}, bf16[1,2,64,1152]{3,2,1,0:T(8,128)(2,1)}, bf16[144,432]{1,0:T(8,128)(2,1)}, bf16[144,432]{1,0:T(8,128)(2,1)}) custom-call(s32[4]{0:T(128)} %pad_add_fusion.1.pos_ref, bf16[1,128,1152]{2,1,0:T(8,128)(2,1)} %x_ref.1, bf16[1,128,1152]{2,1,0:T(8,128)(2,1)} %g_ref.1, bf16[144,3456]{1,0:T(8,128)(2,1)} %w_ref.1), custom_call_target="tpu_custom_call" | custom-call | flops 1179648000 | bytes 2359296 | tf_op jit(solution)/shard_map/start/pallas_call | solution.py:471
  4.7 1.9 %collective-permute-start.2 = (bf16[1,2,64,1152]{3,2,1,0:T(8,128)(2,1)}, bf16[1,2,64,1152]{3,2,1,0:T(8,128)(2,1)S(1)}, u32[]{:S(2)}, u32[]{:S(2)}) collective-permute-start(bf16[1,2,64,1152]{3,2,1,0:T(8,128)(2,1)} %get-tuple-element.57), channel_id=1, source_target_pairs={{0,0},{1,1},{2,16},{3,17},{4,2},{5,3},{6,18},{7,19},{8,20},{9,21},... | collective-permute-start | bytes 884744 | tf_op jit(solution)/shard_map/ppermute | solution.py:481
  6.6 0.1 fusion.7
  6.7 2.2 %collective-permute-start = (s32[1,16]{1,0:T(1,128)S(1)}, s32[1,16]{1,0:T(1,128)S(1)}, u32[]{:S(2)}, u32[]{:S(2)}) collective-permute-start(s32[1,16]{1,0:T(1,128)S(1)} %fusion.7), channel_id=1, source_target_pairs={{0,8},{1,9},{2,10},{3,11},{4,12},{5,13},{6,14},{7,15},{8,0},{9,1},... | collective-permute-start | bytes 200 | tf_op jit(solution)/shard_map/ppermute | solution.py:459
  8.9 1.5 %collective-permute-start.8 = (bf16[144,432]{1,0:T(8,128)(2,1)}, bf16[144,432]{1,0:T(8,128)(2,1)S(1)}, u32[]{:S(2)}, u32[]{:S(2)}) collective-permute-start(bf16[144,432]{1,0:T(8,128)(2,1)} %get-tuple-element.63), channel_id=1, source_target_pairs={{0,1},{1,0},{2,3},{3,2},{4,5},{5,4},{6,7},{7,6},{8,9},{9,8},{10,11... | collective-permute-start | bytes 373256 | tf_op jit(solution)/shard_map/ppermute | solution.py:483
  10.4 2.5 %collective-permute-start.3 = (bf16[1,2,64,1152]{3,2,1,0:T(8,128)(2,1)}, bf16[1,2,64,1152]{3,2,1,0:T(8,128)(2,1)S(1)}, u32[]{:S(2)}, u32[]{:S(2)}) collective-permute-start(bf16[1,2,64,1152]{3,2,1,0:T(8,128)(2,1)} %get-tuple-element.58), channel_id=1, source_target_pairs={{0,2},{1,3},{2,18},{3,19},{4,0},{5,1},{6,16},{7,17},{8,22},{9,23},... | collective-permute-start | bytes 884744 | tf_op jit(solution)/shard_map/ppermute | solution.py:481
  12.9 0.0 collective-permute-done
  12.9 1.5 %collective-permute-start.1 = (s32[2,16]{1,0:T(2,128)S(1)}, s32[2,16]{1,0:T(2,128)S(1)}, u32[]{:S(2)}, u32[]{:S(2)}) collective-permute-start(s32[2,16]{1,0:T(2,128)S(1)} %pad_add_fusion), channel_id=1, source_target_pairs={{0,16},{1,17},{2,18},{3,19},{4,20},{5,21},{6,22},{7,23},{8,24},{9,... | collective-permute-start | bytes 392 | tf_op jit(solution)/shard_map/ppermute | solution.py:461
  14.4 1.5 %collective-permute-start.4 = (bf16[1,2,64,1152]{3,2,1,0:T(8,128)(2,1)S(1)}, bf16[1,2,64,1152]{3,2,1,0:T(8,128)(2,1)S(1)}, u32[]{:S(2)}, u32[]{:S(2)}) collective-permute-start(bf16[1,2,64,1152]{3,2,1,0:T(8,128)(2,1)S(1)} %collective-permute-done.2.refs_0_), channel_id=1, source_target_pairs={{0,1},{1,0},{2,3},{3,2},{4,5},{5,4},{6,7},{7,6},{8,9},{9,8},{10,11... | collective-permute-start | bytes 884744 | tf_op jit(solution)/shard_map/ppermute | solution.py:491
  15.9 0.7 collective-permute-done.1
  16.6 0.6 fusion.2.info_ref
  17.2 0.9 broadcast_select_fusion.1
  18.1 6.1 %collective-permute-done.3.refs_1_ = bf16[1,2,64,1152]{3,2,1,0:T(8,128)(2,1)S(1)} collective-permute-done((bf16[1,2,64,1152]{3,2,1,0:T(8,128)(2,1)}, bf16[1,2,64,1152]{3,2,1,0:T(8,128)(2,1)S(1)}, u32[]{:S(2)}, u32[]{:S(2)}) %collective-permute-start.3) | collective-permute-done | bytes 294944 | tf_op jit(solution)/shard_map/ppermute | solution.py:481
  24.2 1.0 collective-permute-start.6
  25.2 0.1 maximum_bitcast_fusion.2
  25.4 4.2 %collective-permute-start.9 = (bf16[1,144,864]{2,1,0:T(8,128)(2,1)S(1)}, bf16[1,144,864]{2,1,0:T(8,128)(2,1)S(1)}, u32[]{:S(2)}, u32[]{:S(2)}) collective-permute-start(bf16[1,144,864]{2,1,0:T(8,128)(2,1)S(1)} %maximum_bitcast_fusion.2), channel_id=1, source_target_pairs={{0,4},{1,5},{2,6},{3,7},{4,0},{5,1},{6,2},{7,3},{8,12},{9,13},{10,... | collective-permute-start | bytes 746504 | tf_op jit(solution)/shard_map/ppermute | solution.py:449
  29.5 0.1 pad_maximum_fusion.refs_0_
  29.6 0.0 copy-start.13
  29.6 0.1 collective-permute-start.5
  29.7 4.4 %collective-permute-done.6 = bf16[1,2,64,1152]{3,2,1,0:T(8,128)(2,1)S(1)} collective-permute-done((bf16[1,2,64,1152]{3,2,1,0:T(8,128)(2,1)S(1)}, bf16[1,2,64,1152]{3,2,1,0:T(8,128)(2,1)S(1)}, u32[]{:S(2)}, u32[]{:S(2)}) %collective-permute-start.6) | collective-permute-done | bytes 294944 | tf_op jit(solution)/shard_map/ppermute | solution.py:449
  34.1 0.1 pad_maximum_fusion.1.refs_2_
  34.2 0.1 collective-permute-start.7
  34.3 7.0 %collective-permute-done.9 = bf16[1,144,864]{2,1,0:T(8,128)(2,1)S(1)} collective-permute-done((bf16[1,144,864]{2,1,0:T(8,128)(2,1)S(1)}, bf16[1,144,864]{2,1,0:T(8,128)(2,1)S(1)}, u32[]{:S(2)}, u32[]{:S(2)}) %collective-permute-start.9) | collective-permute-done | bytes 248864 | tf_op jit(solution)/shard_map/ppermute | solution.py:449
  41.3 0.1 pad_maximum_fusion.2.refs_0_
  41.4 0.1 collective-permute-start.10
  41.5 3.8 %collective-permute-start.11 = (bf16[144,1152]{1,0:T(8,128)(2,1)S(1)}, bf16[144,1152]{1,0:T(8,128)(2,1)S(1)}, u32[]{:S(2)}, u32[]{:S(2)}) collective-permute-start(bf16[144,1152]{1,0:T(8,128)(2,1)S(1)} %copy-done.13), channel_id=1, source_target_pairs={{0,0},{1,1},{2,18},{3,19},{4,8},{5,9},{6,26},{7,27},{8,4},{9,5},{1... | collective-permute-start | bytes 995336 | tf_op jit(solution)/shard_map/ppermute | solution.py:496
  45.3 15.2 %collective-permute-done.11.refs_4_ = bf16[144,1152]{1,0:T(8,128)(2,1)S(1)} collective-permute-done((bf16[144,1152]{1,0:T(8,128)(2,1)S(1)}, bf16[144,1152]{1,0:T(8,128)(2,1)S(1)}, u32[]{:S(2)}, u32[]{:S(2)}) %collective-permute-start.11) | collective-permute-done | bytes 331808 | tf_op jit(solution)/shard_map/ppermute | solution.py:496
  60.5 0.9 collective-permute-start.12
  61.4 0.1 collective-permute-start.13
  61.5 0.4 collective-permute-start.14
  62.0 4.4 %prepare.1 = (bf16[8,64,1152]{2,1,0:T(8,128)(2,1)}, bf16[8,64,1152]{2,1,0:T(8,128)(2,1)}) custom-call(s32[4]{0:T(128)} %pad_add_fusion.1.pos_ref, s32[16]{0:T(128)} %fusion.2.info_ref, bf16[2,2,64,1152]{3,2,1,0:T(8,128)(2,1)} %copy-done, bf16[2,2,64,1152]{3,2,1,0:T(8,128)(2,1)} %copy-done.8, bf16[2,2,64,1152]{3,2,1,0:T(8,128)(2,1)} %copy-done.1, ...), custom_call_target="tpu_custom_call" | custom-call | flops 1769472000 | bytes 2359296 | tf_op jit(solution)/shard_map/prepare/pallas_call | solution.py:525
  66.4 0.7 copy-done.15
  67.1 0.3 copy-done.11
  67.4 0.2 copy-done.12
  67.5 11.2 %forward.1 = (bf16[2,8,64,144]{3,2,1,0:T(8,128)(2,1)}, bf16[2,8,64,144]{3,2,1,0:T(8,128)(2,1)}, bf16[2,8,64,144]{3,2,1,0:T(8,128)(2,1)}, bf16[2,8,64,144]{3,2,1,...) custom-call(s32[4]{0:T(128)} %pad_add_fusion.1.pos_ref, ...), custom_call_target="tpu_custom_call" | custom-call | flops 8257536000 | bytes 2359296 | tf_op jit(solution)/shard_map/forward/pallas_call | solution.py:537
  78.8 0.4 collective-permute-start.15
  79.2 1.7 %collective-permute-start.17 = (bf16[2,64,1152]{2,1,0:T(8,128)(2,1)}, bf16[2,64,1152]{2,1,0:T(8,128)(2,1)S(1)}, u32[]{:S(2)}, u32[]{:S(2)}) collective-permute-start(bf16[2,64,1152]{2,1,0:T(8,128)(2,1)} %get-tuple-element.88), channel_id=1, source_target_pairs={{0,1},{1,0},{2,3},{3,2},{4,5},{5,4},{6,7},{7,6},{8,9},{9,8},{10,11... | collective-permute-start | bytes 884744 | tf_op jit(solution)/shard_map/ppermute | solution.py:455
  80.9 1.8 %collective-permute-start.19 = (bf16[2,64,1152]{2,1,0:T(8,128)(2,1)}, bf16[2,64,1152]{2,1,0:T(8,128)(2,1)S(1)}, u32[]{:S(2)}, u32[]{:S(2)}) collective-permute-start(bf16[2,64,1152]{2,1,0:T(8,128)(2,1)} %get-tuple-element.90), channel_id=1, source_target_pairs={{0,17},{1,16},{2,19},{3,18},{4,21},{5,20},{6,23},{7,22},{8,25},{9,... | collective-permute-start | bytes 884744 | tf_op jit(solution)/shard_map/ppermute | solution.py:455
  82.7 1.2 slice_add_fusion
  83.8 0.1 collective-permute-start.16
  83.9 9.6 %backward.1 = (f32[2,64,1152]{2,1,0:T(8,128)}, bf16[2,64,1152]{2,1,0:T(8,128)(2,1)}, bf16[2,64,1152]{2,1,0:T(8,128)(2,1)}, bf16[2,64,1152]{2,1,0:T(8,128)(2,1)}) custom-call(s32[4]{0:T(128)} %pad_add_fusion.1.pos_ref, s32[16]{0:T(128)} %fusion.2.info_ref, bf16[2,144,864]{2,1,0:T(8,128)(2,1)} %copy-done.2, bf16[2,144,864]{2,1,0:T(8,128)(2,1)} %copy-done.10, ...), custom_call_target="tpu_custom_call" | custom-call | flops 5898240000 | bytes 2359296 | tf_op jit(solution)/shard_map/backward/pallas_call | solution.py:563
  93.5 2.6 %collective-permute-done.18.refs_4_ = bf16[2,64,1152]{2,1,0:T(8,128)(2,1)S(1)} collective-permute-done((bf16[2,64,1152]{2,1,0:T(8,128)(2,1)}, bf16[2,64,1152]{2,1,0:T(8,128)(2,1)S(1)}, u32[]{:S(2)}, u32[]{:S(2)}) %collective-permute-start.18) | collective-permute-done | bytes 294944 | tf_op jit(solution)/shard_map/ppermute | solution.py:455
  96.2 0.4 collective-permute-start.22
  96.6 1.3 collective-permute-start.23
  97.9 1.8 %collective-permute-start.24 = (bf16[2,64,1152]{2,1,0:T(8,128)(2,1)}, bf16[2,64,1152]{2,1,0:T(8,128)(2,1)S(1)}, u32[]{:S(2)}, u32[]{:S(2)}) collective-permute-start(bf16[2,64,1152]{2,1,0:T(8,128)(2,1)} %get-tuple-element.100), channel_id=1, source_target_pairs={{0,17},{1,16},{2,19},{3,18},{4,21},{5,20},{6,23},{7,22},{8,25},{9,... | collective-permute-start | bytes 884744 | tf_op jit(solution)/shard_map/ppermute | solution.py:455
  99.7 3.1 %output.1 = (bf16[64,1152]{1,0:T(8,128)(2,1)}, bf16[64,1152]{1,0:T(8,128)(2,1)}) custom-call(s32[4]{0:T(128)} %pad_add_fusion.1.pos_ref, s32[16]{0:T(128)} %fusion.2.info_ref, bf16[1,2,64,1152]{3,2,1,0:T(8,128)(2,1)} %copy-done.3, bf16[1,2,64,1152]{3,2,1,0:T(8,128)(2,1)} %copy-done.4, f32[2,64,1152]{2,1,0:T(8,128)} %get-tuple-element.91.refs_2_, ...), custom_call_target="tpu_custom_call" | custom-call | flops 11796480000 | bytes 2359296 | tf_op jit(solution)/shard_map/output/pallas_call | solution.py:576
  102.8 3.3 %collective-permute-start.20 = (bf16[64,1152]{1,0:T(8,128)(2,1)}, bf16[64,1152]{1,0:T(8,128)(2,1)S(1)}, u32[]{:S(2)}, u32[]{:S(2)}) collective-permute-start(bf16[64,1152]{1,0:T(8,128)(2,1)} %get-tuple-element.95), channel_id=1, source_target_pairs={{0,0},{1,1},{16,2},{17,3},{2,4},{3,5},{18,6},{19,7},{20,8},{21,9},... | collective-permute-start | bytes 442376 | tf_op jit(solution)/shard_map/ppermute | solution.py:442
  106.1 3.1 %collective-permute-start.21 = (bf16[64,1152]{1,0:T(8,128)(2,1)}, bf16[64,1152]{1,0:T(8,128)(2,1)S(1)}, u32[]{:S(2)}, u32[]{:S(2)}) collective-permute-start(bf16[64,1152]{1,0:T(8,128)(2,1)} %get-tuple-element.96), channel_id=1, source_target_pairs={{2,0},{3,1},{18,2},{19,3},{0,4},{1,5},{16,6},{17,7},{22,8},{23,9},... | collective-permute-start | bytes 442376 | tf_op jit(solution)/shard_map/ppermute | solution.py:442
  109.4 0.1 collective-permute-start.27
  109.5 1.4 %collective-permute-done.23.refs_4_ = bf16[2,64,1152]{2,1,0:T(8,128)(2,1)S(1)} collective-permute-done((bf16[2,64,1152]{2,1,0:T(8,128)(2,1)}, bf16[2,64,1152]{2,1,0:T(8,128)(2,1)S(1)}, u32[]{:S(2)}, u32[]{:S(2)}) %collective-permute-start.23) | collective-permute-done | bytes 294944 | tf_op jit(solution)/shard_map/ppermute | solution.py:455
  110.9 0.7 copy-done.20
  111.6 0.7 copy-done.21
  112.3 3.4 %input_grad.1 = (bf16[64,1152]{1,0:T(8,128)(2,1)}, bf16[64,1152]{1,0:T(8,128)(2,1)}) custom-call(s32[4]{0:T(128)} %pad_add_fusion.1.pos_ref, s32[16]{0:T(128)} %fusion.2.info_ref, bf16[1,2,64,1152]{3,2,1,0:T(8,128)(2,1)} %copy-done.3, bf16[1,2,64,1152]{3,2,1,0:T(8,128)(2,1)} %copy-done.4, f32[2,64,1152]{2,1,0:T(8,128)} %get-tuple-element.101.refs_2_, ...), custom_call_target="tpu_custom_call" | custom-call | flops 1769472000 | bytes 2359296 | tf_op jit(solution)/shard_map/input_grad/pallas_call | solution.py:588
  115.7 5.4 %collective-permute-start.25 = (bf16[64,1152]{1,0:T(8,128)(2,1)}, bf16[64,1152]{1,0:T(8,128)(2,1)S(1)}, u32[]{:S(2)}, u32[]{:S(2)}) collective-permute-start(bf16[64,1152]{1,0:T(8,128)(2,1)} %get-tuple-element.105), channel_id=1, source_target_pairs={{0,0},{1,1},{16,2},{17,3},{2,4},{3,5},{18,6},{19,7},{20,8},{21,9},... | collective-permute-start | bytes 442376 | tf_op jit(solution)/shard_map/ppermute | solution.py:442
  121.1 2.8 %collective-permute-start.26 = (bf16[64,1152]{1,0:T(8,128)(2,1)}, bf16[64,1152]{1,0:T(8,128)(2,1)S(1)}, u32[]{:S(2)}, u32[]{:S(2)}) collective-permute-start(bf16[64,1152]{1,0:T(8,128)(2,1)} %get-tuple-element.106), channel_id=1, source_target_pairs={{2,0},{3,1},{18,2},{19,3},{0,4},{1,5},{16,6},{17,7},{22,8},{23,9},... | collective-permute-start | bytes 442376 | tf_op jit(solution)/shard_map/ppermute | solution.py:442
  124.0 1.9 %collective-permute-start.28 = (f32[48,864]{1,0:T(8,128)S(1)}, f32[48,864]{1,0:T(8,128)S(1)}, u32[]{:S(2)}, u32[]{:S(2)}) collective-permute-start(f32[48,864]{1,0:T(8,128)S(1)} %bitcast.28), channel_id=1, source_target_pairs={{0,0},{1,1},{2,8},{3,9},{4,16},{5,17},{6,24},{7,25},{8,4},{9,5},{1... | collective-permute-start | bytes 497672 | tf_op jit(solution)/shard_map/ppermute | solution.py:604
  125.9 2.8 %collective-permute-done.26 = bf16[64,1152]{1,0:T(8,128)(2,1)S(1)} collective-permute-done((bf16[64,1152]{1,0:T(8,128)(2,1)}, bf16[64,1152]{1,0:T(8,128)(2,1)S(1)}, u32[]{:S(2)}, u32[]{:S(2)}) %collective-permute-start.26) | collective-permute-done | bytes 147488 | tf_op jit(solution)/shard_map/ppermute | solution.py:442
  128.7 0.1 broadcast_select_fusion.3
  128.8 0.7 maximum_bitcast_fusion.1
  129.5 0.7 maximum_bitcast_fusion
  130.3 3.0 %collective-permute-done.28 = f32[48,864]{1,0:T(8,128)S(1)} collective-permute-done((f32[48,864]{1,0:T(8,128)S(1)}, f32[48,864]{1,0:T(8,128)S(1)}, u32[]{:S(2)}, u32[]{:S(2)}) %collective-permute-start.28) | collective-permute-done | bytes 165920 | tf_op jit(solution)/shard_map/ppermute | solution.py:604
  133.3 0.1 fusion.6
  133.4 0.7 maximum_multiply_fusion
  (62 shorter events, 0.2 us)
Async XLA Ops:
  1.2 5.4 %copy-start.5 = (s32[1,4]{1,0:T(1,128)S(1)}, s32[1,4]{1,0:T(1,128)}, u32[]{:S(2)}) copy-start(s32[1,4]{1,0:T(1,128)} %param.12) | copy-start | bytes 52
  1.3 5.4 %copy-start.6 = (s32[1,4]{1,0:T(1,128)S(1)}, s32[1,4]{1,0:T(1,128)}, u32[]{:S(2)}) copy-start(s32[1,4]{1,0:T(1,128)} %param.11) | copy-start | bytes 52
  1.3 5.4 %copy-start.7 = (s32[1,8]{1,0:T(1,128)S(1)}, s32[1,8]{1,0:T(1,128)}, u32[]{:S(2)}) copy-start(s32[1,8]{1,0:T(1,128)} %param.10) | copy-start | bytes 100
  4.7 9.7 %collective-permute-start.2 = (bf16[1,2,64,1152]{3,2,1,0:T(8,128)(2,1)}, bf16[1,2,64,1152]{3,2,1,0:T(8,128)(2,1)S(1)}, u32[]{:S(2)}, u32[]{:S(2)}) collective-permute-start(bf16[1,2,64,1152]{3,2,1,0:T(8,128)(2,1)} %get-tuple-element.57), channel_id=1, source_target_pairs={{0,0},{1,1},{2,16},{3,17},{4,2},{5,3},{6,18},{7,19},{8,20},{9,21},... | collective-permute-start | bytes 884744 | tf_op jit(solution)/shard_map/ppermute | solution.py:481
  6.7 6.2 %collective-permute-start = (s32[1,16]{1,0:T(1,128)S(1)}, s32[1,16]{1,0:T(1,128)S(1)}, u32[]{:S(2)}, u32[]{:S(2)}) collective-permute-start(s32[1,16]{1,0:T(1,128)S(1)} %fusion.7), channel_id=1, source_target_pairs={{0,8},{1,9},{2,10},{3,11},{4,12},{5,13},{6,14},{7,15},{8,0},{9,1},... | collective-permute-start | bytes 200 | tf_op jit(solution)/shard_map/ppermute | solution.py:459
  8.9 8.3 %collective-permute-start.8 = (bf16[144,432]{1,0:T(8,128)(2,1)}, bf16[144,432]{1,0:T(8,128)(2,1)S(1)}, u32[]{:S(2)}, u32[]{:S(2)}) collective-permute-start(bf16[144,432]{1,0:T(8,128)(2,1)} %get-tuple-element.63), channel_id=1, source_target_pairs={{0,1},{1,0},{2,3},{3,2},{4,5},{5,4},{6,7},{7,6},{8,9},{9,8},{10,11... | collective-permute-start | bytes 373256 | tf_op jit(solution)/shard_map/ppermute | solution.py:483
  10.4 13.9 %collective-permute-start.3 = (bf16[1,2,64,1152]{3,2,1,0:T(8,128)(2,1)}, bf16[1,2,64,1152]{3,2,1,0:T(8,128)(2,1)S(1)}, u32[]{:S(2)}, u32[]{:S(2)}) collective-permute-start(bf16[1,2,64,1152]{3,2,1,0:T(8,128)(2,1)} %get-tuple-element.58), channel_id=1, source_target_pairs={{0,2},{1,3},{2,18},{3,19},{4,0},{5,1},{6,16},{7,17},{8,22},{9,23},... | collective-permute-start | bytes 884744 | tf_op jit(solution)/shard_map/ppermute | solution.py:481
  12.9 3.6 %collective-permute-start.1 = (s32[2,16]{1,0:T(2,128)S(1)}, s32[2,16]{1,0:T(2,128)S(1)}, u32[]{:S(2)}, u32[]{:S(2)}) collective-permute-start(s32[2,16]{1,0:T(2,128)S(1)} %pad_add_fusion), channel_id=1, source_target_pairs={{0,16},{1,17},{2,18},{3,19},{4,20},{5,21},{6,22},{7,23},{8,24},{9,... | collective-permute-start | bytes 392 | tf_op jit(solution)/shard_map/ppermute | solution.py:461
  14.4 19.7 %copy-start.3 = (bf16[1,2,64,1152]{3,2,1,0:T(8,128)(2,1)}, bf16[1,2,64,1152]{3,2,1,0:T(8,128)(2,1)S(1)}, u32[]{:S(2)}) copy-start(bf16[1,2,64,1152]{3,2,1,0:T(8,128)(2,1)S(1)} %collective-permute-done.2.refs_0_) | copy-start | bytes 884740
  14.4 9.8 %collective-permute-start.4 = (bf16[1,2,64,1152]{3,2,1,0:T(8,128)(2,1)S(1)}, bf16[1,2,64,1152]{3,2,1,0:T(8,128)(2,1)S(1)}, u32[]{:S(2)}, u32[]{:S(2)}) collective-permute-start(bf16[1,2,64,1152]{3,2,1,0:T(8,128)(2,1)S(1)} %collective-permute-done.2.refs_0_), channel_id=1, source_target_pairs={{0,1},{1,0},{2,3},{3,2},{4,5},{5,4},{6,7},{7,6},{8,9},{9,8},{10,11... | collective-permute-start | bytes 884744 | tf_op jit(solution)/shard_map/ppermute | solution.py:491
  24.2 10.0 %copy-start.4 = (bf16[1,2,64,1152]{3,2,1,0:T(8,128)(2,1)}, bf16[1,2,64,1152]{3,2,1,0:T(8,128)(2,1)S(1)}, u32[]{:S(2)}) copy-start(bf16[1,2,64,1152]{3,2,1,0:T(8,128)(2,1)S(1)} %collective-permute-done.3.refs_1_) | copy-start | bytes 884740
  24.2 9.9 %collective-permute-start.6 = (bf16[1,2,64,1152]{3,2,1,0:T(8,128)(2,1)S(1)}, bf16[1,2,64,1152]{3,2,1,0:T(8,128)(2,1)S(1)}, u32[]{:S(2)}, u32[]{:S(2)}) collective-permute-start(bf16[1,2,64,1152]{3,2,1,0:T(8,128)(2,1)S(1)} %collective-permute-done.3.refs_1_), channel_id=1, source_target_pairs={{0,16},{1,17},{2,18},{3,19},{4,20},{5,21},{6,22},{7,23},{8,24},{9,... | collective-permute-start | bytes 884744 | tf_op jit(solution)/shard_map/ppermute | solution.py:449
  25.4 15.9 %collective-permute-start.9 = (bf16[1,144,864]{2,1,0:T(8,128)(2,1)S(1)}, bf16[1,144,864]{2,1,0:T(8,128)(2,1)S(1)}, u32[]{:S(2)}, u32[]{:S(2)}) collective-permute-start(bf16[1,144,864]{2,1,0:T(8,128)(2,1)S(1)} %maximum_bitcast_fusion.2), channel_id=1, source_target_pairs={{0,4},{1,5},{2,6},{3,7},{4,0},{5,1},{6,2},{7,3},{8,12},{9,13},{10,... | collective-permute-start | bytes 746504 | tf_op jit(solution)/shard_map/ppermute | solution.py:449
  29.6 32.4 %copy-start = (bf16[2,2,64,1152]{3,2,1,0:T(8,128)(2,1)}, bf16[2,2,64,1152]{3,2,1,0:T(8,128)(2,1)S(1)}, u32[]{:S(2)}) copy-start(bf16[2,2,64,1152]{3,2,1,0:T(8,128)(2,1)S(1)} %pad_maximum_fusion.refs_0_) | copy-start | bytes 1769476
  29.6 11.8 %copy-start.13 = (bf16[144,1152]{1,0:T(8,128)(2,1)S(1)}, bf16[144,1152]{1,0:T(8,128)(2,1)}, u32[]{:S(2)}) copy-start(bf16[144,1152]{1,0:T(8,128)(2,1)} %param.15) | copy-start | bytes 995332
  29.6 30.9 %collective-permute-start.5 = (bf16[2,2,64,1152]{3,2,1,0:T(8,128)(2,1)S(1)}, bf16[2,2,64,1152]{3,2,1,0:T(8,128)(2,1)S(1)}, u32[]{:S(2)}, u32[]{:S(2)}) collective-permute-start(bf16[2,2,64,1152]{3,2,1,0:T(8,128)(2,1)S(1)} %pad_maximum_fusion.refs_0_), channel_id=1, source_target_pairs={{0,16},{1,17},{2,18},{3,19},{4,20},{5,21},{6,22},{7,23},{8,24},{9,... | collective-permute-start | bytes 1769480 | tf_op jit(solution)/shard_map/ppermute | solution.py:452
  34.2 27.8 %copy-start.1 = (bf16[2,2,64,1152]{3,2,1,0:T(8,128)(2,1)}, bf16[2,2,64,1152]{3,2,1,0:T(8,128)(2,1)S(1)}, u32[]{:S(2)}) copy-start(bf16[2,2,64,1152]{3,2,1,0:T(8,128)(2,1)S(1)} %pad_maximum_fusion.1.refs_2_) | copy-start | bytes 1769476
  34.2 26.3 %collective-permute-start.7 = (bf16[2,2,64,1152]{3,2,1,0:T(8,128)(2,1)S(1)}, bf16[2,2,64,1152]{3,2,1,0:T(8,128)(2,1)S(1)}, u32[]{:S(2)}, u32[]{:S(2)}) collective-permute-start(bf16[2,2,64,1152]{3,2,1,0:T(8,128)(2,1)S(1)} %pad_maximum_fusion.1.refs_2_), channel_id=1, source_target_pairs={{0,1},{1,0},{2,3},{3,2},{4,5},{5,4},{6,7},{7,6},{8,9},{9,8},{10,11... | collective-permute-start | bytes 1769480 | tf_op jit(solution)/shard_map/ppermute | solution.py:452
  41.4 25.0 %copy-start.2 = (bf16[2,144,864]{2,1,0:T(8,128)(2,1)}, bf16[2,144,864]{2,1,0:T(8,128)(2,1)S(1)}, u32[]{:S(2)}) copy-start(bf16[2,144,864]{2,1,0:T(8,128)(2,1)S(1)} %pad_maximum_fusion.2.refs_0_) | copy-start | bytes 1492996
  41.4 19.1 %collective-permute-start.10 = (bf16[2,144,864]{2,1,0:T(8,128)(2,1)S(1)}, bf16[2,144,864]{2,1,0:T(8,128)(2,1)S(1)}, u32[]{:S(2)}, u32[]{:S(2)}) collective-permute-start(bf16[2,144,864]{2,1,0:T(8,128)(2,1)S(1)} %pad_maximum_fusion.2.refs_0_), channel_id=1, source_target_pairs={{0,2},{1,3},{2,0},{3,1},{4,6},{5,7},{6,4},{7,5},{8,10},{9,11},{10,... | collective-permute-start | bytes 1493000 | tf_op jit(solution)/shard_map/ppermute | solution.py:452
  41.5 19.0 %collective-permute-start.11 = (bf16[144,1152]{1,0:T(8,128)(2,1)S(1)}, bf16[144,1152]{1,0:T(8,128)(2,1)S(1)}, u32[]{:S(2)}, u32[]{:S(2)}) collective-permute-start(bf16[144,1152]{1,0:T(8,128)(2,1)S(1)} %copy-done.13), channel_id=1, source_target_pairs={{0,0},{1,1},{2,18},{3,19},{4,8},{5,9},{6,26},{7,27},{8,4},{9,5},{1... | collective-permute-start | bytes 995336 | tf_op jit(solution)/shard_map/ppermute | solution.py:496
  60.5 6.0 %copy-start.14 = (bf16[144,1152]{1,0:T(8,128)(2,1)}, bf16[144,1152]{1,0:T(8,128)(2,1)S(1)}, u32[]{:S(2)}) copy-start(bf16[144,1152]{1,0:T(8,128)(2,1)S(1)} %collective-permute-done.11.refs_4_) | copy-start | bytes 995332
  60.5 1.5 %copy-start.8 = (bf16[2,2,64,1152]{3,2,1,0:T(8,128)(2,1)}, bf16[2,2,64,1152]{3,2,1,0:T(8,128)(2,1)S(1)}, u32[]{:S(2)}) copy-start(bf16[2,2,64,1152]{3,2,1,0:T(8,128)(2,1)S(1)} %collective-permute-done.5.refs_1_) | copy-start | bytes 1769476
  60.5 5.9 %copy-start.10 = (bf16[2,144,864]{2,1,0:T(8,128)(2,1)}, bf16[2,144,864]{2,1,0:T(8,128)(2,1)S(1)}, u32[]{:S(2)}) copy-start(bf16[2,144,864]{2,1,0:T(8,128)(2,1)S(1)} %collective-permute-done.10.refs_1_) | copy-start | bytes 1492996
  60.5 1.5 %copy-start.9 = (bf16[2,2,64,1152]{3,2,1,0:T(8,128)(2,1)}, bf16[2,2,64,1152]{3,2,1,0:T(8,128)(2,1)S(1)}, u32[]{:S(2)}) copy-start(bf16[2,2,64,1152]{3,2,1,0:T(8,128)(2,1)S(1)} %collective-permute-done.7.refs_3_) | copy-start | bytes 1769476
  60.5 5.9 %collective-permute-start.12 = (bf16[2,144,864]{2,1,0:T(8,128)(2,1)S(1)}, bf16[2,144,864]{2,1,0:T(8,128)(2,1)S(1)}, u32[]{:S(2)}, u32[]{:S(2)}) collective-permute-start(bf16[2,144,864]{2,1,0:T(8,128)(2,1)S(1)} %pad_maximum_fusion.2.refs_0_), channel_id=1, source_target_pairs={{0,8},{1,9},{2,10},{3,11},{4,12},{5,13},{6,14},{7,15},{8,0},{9,1},... | collective-permute-start | bytes 1493000 | tf_op jit(solution)/shard_map/ppermute | solution.py:504
  61.4 5.0 %collective-permute-start.13 = (bf16[2,144,864]{2,1,0:T(8,128)(2,1)S(1)}, bf16[2,144,864]{2,1,0:T(8,128)(2,1)S(1)}, u32[]{:S(2)}, u32[]{:S(2)}) collective-permute-start(bf16[2,144,864]{2,1,0:T(8,128)(2,1)S(1)} %collective-permute-done.10.refs_1_), channel_id=1, source_target_pairs={{0,8},{1,9},{2,10},{3,11},{4,12},{5,13},{6,14},{7,15},{8,0},{9,1},... | collective-permute-start | bytes 1493000 | tf_op jit(solution)/shard_map/ppermute | solution.py:504
  61.5 4.9 %collective-permute-start.14 = (bf16[144,1152]{1,0:T(8,128)(2,1)S(1)}, bf16[144,1152]{1,0:T(8,128)(2,1)S(1)}, u32[]{:S(2)}, u32[]{:S(2)}) collective-permute-start(bf16[144,1152]{1,0:T(8,128)(2,1)S(1)} %collective-permute-done.11.refs_4_), channel_id=1, source_target_pairs={{0,8},{1,9},{2,10},{3,11},{4,12},{5,13},{6,14},{7,15},{8,0},{9,1},... | collective-permute-start | bytes 995336 | tf_op jit(solution)/shard_map/ppermute | solution.py:505
  66.4 0.7 copy-start.15
  66.4 1.0 copy-start.11
  66.4 1.1 copy-start.12
  78.8 3.9 %collective-permute-start.15 = (f32[4,48,864]{2,1,0:T(8,128)}, f32[4,48,864]{2,1,0:T(8,128)S(1)}, u32[]{:S(2)}, u32[]{:S(2)}) collective-permute-start(f32[4,48,864]{2,1,0:T(8,128)} %get-tuple-element.80), channel_id=1, source_target_pairs={{0,8},{1,9},{2,10},{3,11},{4,12},{5,13},{6,14},{7,15},{8,0},{9,1},... | collective-permute-start | bytes 1990664 | tf_op jit(solution)/shard_map/ppermute | solution.py:555
  79.2 14.3 %collective-permute-start.17 = (bf16[2,64,1152]{2,1,0:T(8,128)(2,1)}, bf16[2,64,1152]{2,1,0:T(8,128)(2,1)S(1)}, u32[]{:S(2)}, u32[]{:S(2)}) collective-permute-start(bf16[2,64,1152]{2,1,0:T(8,128)(2,1)} %get-tuple-element.88), channel_id=1, source_target_pairs={{0,1},{1,0},{2,3},{3,2},{4,5},{5,4},{6,7},{7,6},{8,9},{9,8},{10,11... | collective-permute-start | bytes 884744 | tf_op jit(solution)/shard_map/ppermute | solution.py:455
  80.9 15.2 %collective-permute-start.18 = (bf16[2,64,1152]{2,1,0:T(8,128)(2,1)}, bf16[2,64,1152]{2,1,0:T(8,128)(2,1)S(1)}, u32[]{:S(2)}, u32[]{:S(2)}) collective-permute-start(bf16[2,64,1152]{2,1,0:T(8,128)(2,1)} %get-tuple-element.89), channel_id=1, source_target_pairs={{0,16},{1,17},{2,18},{3,19},{4,20},{5,21},{6,22},{7,23},{8,24},{9,... | collective-permute-start | bytes 884744 | tf_op jit(solution)/shard_map/ppermute | solution.py:455
  80.9 15.2 %collective-permute-start.19 = (bf16[2,64,1152]{2,1,0:T(8,128)(2,1)}, bf16[2,64,1152]{2,1,0:T(8,128)(2,1)S(1)}, u32[]{:S(2)}, u32[]{:S(2)}) collective-permute-start(bf16[2,64,1152]{2,1,0:T(8,128)(2,1)} %get-tuple-element.90), channel_id=1, source_target_pairs={{0,17},{1,16},{2,19},{3,18},{4,21},{5,20},{6,23},{7,22},{8,25},{9,... | collective-permute-start | bytes 884744 | tf_op jit(solution)/shard_map/ppermute | solution.py:455
  83.8 12.3 %collective-permute-start.16 = (f32[2,48,864]{2,1,0:T(8,128)S(1)}, f32[2,48,864]{2,1,0:T(8,128)S(1)}, u32[]{:S(2)}, u32[]{:S(2)}) collective-permute-start(f32[2,48,864]{2,1,0:T(8,128)S(1)} %get-tuple-element.86), channel_id=1, source_target_pairs={{0,2},{1,3},{2,0},{3,1},{4,6},{5,7},{6,4},{7,5},{8,10},{9,11},{10,... | collective-permute-start | bytes 995336 | tf_op jit(solution)/shard_map/ppermute | solution.py:561
  93.5 6.2 %copy-start.16 = (bf16[2,64,1152]{2,1,0:T(8,128)(2,1)}, bf16[2,64,1152]{2,1,0:T(8,128)(2,1)S(1)}, u32[]{:S(2)}) copy-start(bf16[2,64,1152]{2,1,0:T(8,128)(2,1)S(1)} %collective-permute-done.17.refs_3_) | copy-start | bytes 884740
  96.1 3.6 %copy-start.17 = (bf16[2,64,1152]{2,1,0:T(8,128)(2,1)}, bf16[2,64,1152]{2,1,0:T(8,128)(2,1)S(1)}, u32[]{:S(2)}) copy-start(bf16[2,64,1152]{2,1,0:T(8,128)(2,1)S(1)} %collective-permute-done.18.refs_4_) | copy-start | bytes 884740
  96.1 3.6 %copy-start.18 = (bf16[2,64,1152]{2,1,0:T(8,128)(2,1)}, bf16[2,64,1152]{2,1,0:T(8,128)(2,1)S(1)}, u32[]{:S(2)}) copy-start(bf16[2,64,1152]{2,1,0:T(8,128)(2,1)S(1)} %collective-permute-done.19.refs_5_) | copy-start | bytes 884740
  96.2 13.2 %collective-permute-start.22 = (bf16[2,64,1152]{2,1,0:T(8,128)(2,1)}, bf16[2,64,1152]{2,1,0:T(8,128)(2,1)S(1)}, u32[]{:S(2)}, u32[]{:S(2)}) collective-permute-start(bf16[2,64,1152]{2,1,0:T(8,128)(2,1)} %get-tuple-element.98), channel_id=1, source_target_pairs={{0,1},{1,0},{2,3},{3,2},{4,5},{5,4},{6,7},{7,6},{8,9},{9,8},{10,11... | collective-permute-start | bytes 884744 | tf_op jit(solution)/shard_map/ppermute | solution.py:455
  96.6 14.3 %collective-permute-start.23 = (bf16[2,64,1152]{2,1,0:T(8,128)(2,1)}, bf16[2,64,1152]{2,1,0:T(8,128)(2,1)S(1)}, u32[]{:S(2)}, u32[]{:S(2)}) collective-permute-start(bf16[2,64,1152]{2,1,0:T(8,128)(2,1)} %get-tuple-element.99), channel_id=1, source_target_pairs={{0,16},{1,17},{2,18},{3,19},{4,20},{5,21},{6,22},{7,23},{8,24},{9,... | collective-permute-start | bytes 884744 | tf_op jit(solution)/shard_map/ppermute | solution.py:455
  97.9 13.0 %collective-permute-start.24 = (bf16[2,64,1152]{2,1,0:T(8,128)(2,1)}, bf16[2,64,1152]{2,1,0:T(8,128)(2,1)S(1)}, u32[]{:S(2)}, u32[]{:S(2)}) collective-permute-start(bf16[2,64,1152]{2,1,0:T(8,128)(2,1)} %get-tuple-element.100), channel_id=1, source_target_pairs={{0,17},{1,16},{2,19},{3,18},{4,21},{5,20},{6,23},{7,22},{8,25},{9,... | collective-permute-start | bytes 884744 | tf_op jit(solution)/shard_map/ppermute | solution.py:455
  102.8 23.1 %collective-permute-start.20 = (bf16[64,1152]{1,0:T(8,128)(2,1)}, bf16[64,1152]{1,0:T(8,128)(2,1)S(1)}, u32[]{:S(2)}, u32[]{:S(2)}) collective-permute-start(bf16[64,1152]{1,0:T(8,128)(2,1)} %get-tuple-element.95), channel_id=1, source_target_pairs={{0,0},{1,1},{16,2},{17,3},{2,4},{3,5},{18,6},{19,7},{20,8},{21,9},... | collective-permute-start | bytes 442376 | tf_op jit(solution)/shard_map/ppermute | solution.py:442
  106.1 19.8 %collective-permute-start.21 = (bf16[64,1152]{1,0:T(8,128)(2,1)}, bf16[64,1152]{1,0:T(8,128)(2,1)S(1)}, u32[]{:S(2)}, u32[]{:S(2)}) collective-permute-start(bf16[64,1152]{1,0:T(8,128)(2,1)} %get-tuple-element.96), channel_id=1, source_target_pairs={{2,0},{3,1},{18,2},{19,3},{0,4},{1,5},{16,6},{17,7},{22,8},{23,9},... | collective-permute-start | bytes 442376 | tf_op jit(solution)/shard_map/ppermute | solution.py:442
  109.4 1.5 %copy-start.19 = (bf16[2,64,1152]{2,1,0:T(8,128)(2,1)}, bf16[2,64,1152]{2,1,0:T(8,128)(2,1)S(1)}, u32[]{:S(2)}) copy-start(bf16[2,64,1152]{2,1,0:T(8,128)(2,1)S(1)} %collective-permute-done.22.refs_3_) | copy-start | bytes 884740
  109.4 14.5 %collective-permute-start.27 = (f32[1,48,864]{2,1,0:T(8,128)S(1)}, f32[1,48,864]{2,1,0:T(8,128)S(1)}, u32[]{:S(2)}, u32[]{:S(2)}) collective-permute-start(f32[1,48,864]{2,1,0:T(8,128)S(1)} %slice.40), channel_id=1, source_target_pairs={{0,4},{1,5},{2,6},{3,7},{4,0},{5,1},{6,2},{7,3},{8,12},{9,13},{10,... | collective-permute-start | bytes 497672 | tf_op jit(solution)/shard_map/ppermute | solution.py:602
  110.9 0.7 copy-start.20
  111.6 0.7 copy-start.21
  115.7 10.2 %collective-permute-start.25 = (bf16[64,1152]{1,0:T(8,128)(2,1)}, bf16[64,1152]{1,0:T(8,128)(2,1)S(1)}, u32[]{:S(2)}, u32[]{:S(2)}) collective-permute-start(bf16[64,1152]{1,0:T(8,128)(2,1)} %get-tuple-element.105), channel_id=1, source_target_pairs={{0,0},{1,1},{16,2},{17,3},{2,4},{3,5},{18,6},{19,7},{20,8},{21,9},... | collective-permute-start | bytes 442376 | tf_op jit(solution)/shard_map/ppermute | solution.py:442
  121.1 7.6 %collective-permute-start.26 = (bf16[64,1152]{1,0:T(8,128)(2,1)}, bf16[64,1152]{1,0:T(8,128)(2,1)S(1)}, u32[]{:S(2)}, u32[]{:S(2)}) collective-permute-start(bf16[64,1152]{1,0:T(8,128)(2,1)} %get-tuple-element.106), channel_id=1, source_target_pairs={{2,0},{3,1},{18,2},{19,3},{0,4},{1,5},{16,6},{17,7},{22,8},{23,9},... | collective-permute-start | bytes 442376 | tf_op jit(solution)/shard_map/ppermute | solution.py:442
  124.0 9.3 %collective-permute-start.28 = (f32[48,864]{1,0:T(8,128)S(1)}, f32[48,864]{1,0:T(8,128)S(1)}, u32[]{:S(2)}, u32[]{:S(2)}) collective-permute-start(f32[48,864]{1,0:T(8,128)S(1)} %bitcast.28), channel_id=1, source_target_pairs={{0,0},{1,1},{2,8},{3,9},{4,16},{5,17},{6,24},{7,25},{8,4},{9,5},{1... | collective-permute-start | bytes 497672 | tf_op jit(solution)/shard_map/ppermute | solution.py:604

commit v13 on v12

--- a/solution.py
+++ b/solution.py
@@ -244,9 +244,7 @@
 
 def forward_kernel(lay, pos_ref, info_ref, hid_ref, gp_ref, *refs):
     w_refs, refs = refs[: 2 * lay.halves], refs[2 * lay.halves :]
-    wo_refs, refs = refs[: lay.nc], refs[lay.nc :]
-    q_ref, k_ref, v_ref, ga_ref, kept_ref, sent_ref, *refs = refs
-    pr_refs, (w_scr, att_scr, wo_scr, acc_scr, cut_scr) = refs[: lay.chips], refs[lay.chips :]
+    q_ref, k_ref, v_ref, att_ref, kept_ref, sent_ref, w_scr, acc_scr, cut_scr = refs
     _, step_patches, model = hid_ref.shape
     tokens = lay.frames * step_patches
     cols = w_scr.shape[2] // 3
@@ -257,9 +255,6 @@
     @pl.when(pl.program_id(0) == 0)
     def _():
         fill_weights(lay, pos_ref, w_refs, w_scr)
-        own, other = wo_refs[0][...].astype(F32), wo_refs[1][...].astype(F32)
-        both = [jnp.where(is_first, own, other), jnp.where(is_first, other, own)]
-        wo_scr[...] = jnp.concatenate(both, axis=0).astype(BF16)
         acc_scr[...] = jnp.zeros_like(acc_scr)
 
     hidden = hid_ref[...].reshape(lay.frames * step_patches, model)
@@ -282,18 +277,10 @@
             second = jnp.where(pos_ref[1] == 0, outputs[1], outputs[0])
             outputs = [jnp.concatenate([first, second], axis=1)]
         attended = outputs[0].astype(BF16)
-        att_scr[:, b * BLOCK : (b + 1) * BLOCK, :] = attended.reshape(lay.frames, BLOCK, -1)
-
-    attended = att_scr[...].reshape(tokens, -1)
-    grad_proj = gp_ref[...].reshape(tokens, model)
-    acc_scr[...] += t_dot(attended, grad_proj)
-    grad_attn = dot_t(grad_proj, wo_scr[...])
-    part = wo_scr.shape[0] // lay.halves
-    for h in range(lay.halves):
-        ga_ref[h] = grad_attn[:, h * part : (h + 1) * part].astype(BF16).reshape(ga_ref.shape[1:])
-    projected = dot(attended, wo_scr[...]).reshape(lay.chips, lay.nc, step_patches, model)
-    for k in range(lay.chips):
-        pr_refs[k][...] = projected[k].astype(pr_refs[k].dtype)
+        att_ref[:, b * BLOCK : (b + 1) * BLOCK, :] = attended.reshape(lay.frames, BLOCK, -1)
+
+    attended = att_ref[...].reshape(tokens, -1)
+    acc_scr[...] += t_dot(attended, gp_ref[...].reshape(tokens, model))
 
     @pl.when(pl.program_id(0) == pl.num_programs(0) - 1)
     def _():
@@ -312,6 +299,29 @@
                 cut_scr[d] = jnp.concatenate(chunk, axis=1) if len(chunk) > 1 else chunk[0]
             for n, k in enumerate(order):
                 ref[n] = cut_scr[pos_ref[2] ^ k]
+
+
+def projection_kernel(lay, pos_ref, gp_ref, att_ref, *refs):
+    wo_refs, (ga_ref, *refs) = refs[: lay.nc], refs[lay.nc :]
+    pr_refs, (wo_scr,) = refs[: lay.chips], refs[lay.chips :]
+    _, step_patches, model = gp_ref.shape
+    tokens = lay.frames * step_patches
+    is_first = pos_ref[1] == 0
+
+    @pl.when(pl.program_id(0) == 0)
+    def _():
+        own, other = wo_refs[0][...].astype(F32), wo_refs[1][...].astype(F32)
+        both = [jnp.where(is_first, own, other), jnp.where(is_first, other, own)]
+        wo_scr[...] = jnp.concatenate(both, axis=0).astype(BF16)
+
+    grad_attn = dot_t(gp_ref[...].reshape(tokens, model), wo_scr[...])
+    part = wo_scr.shape[0] // lay.halves
+    for h in range(lay.halves):
+        ga_ref[h] = grad_attn[:, h * part : (h + 1) * part].astype(BF16).reshape(ga_ref.shape[1:])
+    attended = att_ref[...].reshape(tokens, -1)
+    projected = dot(attended, wo_scr[...]).reshape(lay.chips, lay.nc, step_patches, model)
+    for k in range(lay.chips):
+        pr_refs[k][...] = projected[k].astype(pr_refs[k].dtype)
 
 
 def backward_kernel(lay, pos_ref, info_ref, *refs):
@@ -492,17 +502,16 @@
     own[1], first = lax.optimization_barrier((own[1], first))
     w_own, _ = lax.optimization_barrier((w_own, own[1]))
     w_pieces = doubling(w_own, lay.bits(lay.nz)[::-1], lambda kz: lay.swap(kz=kz), [])
-    late_w_out, _ = lax.optimization_barrier((w_out, own))
+    late_w_out, _ = lax.optimization_barrier((w_out, w_pieces))
     wo_own = lax.ppermute(late_w_out, AXES, lay.rows_to_chip())
 
     pairs = []
     for j in range(nc):
         after = ([], None) if j else (info, first)
         pairs += doubling(own[j], lay.chip_bits(j), chip_swap, *after)
-    pairs, w_pieces, wo_own = lax.optimization_barrier((pairs, w_pieces, wo_own))
+    pairs, w_pieces = lax.optimization_barrier((pairs, w_pieces))
     if halves > 1:
         w_pieces += [lax.ppermute(piece, AXES, lay.swap(kc=1)) for piece in w_pieces]
-    wo_rows = [wo_own, lax.ppermute(wo_own, AXES, lay.swap(kc=1))]
 
 
     def spread(count, width, patches_at_once):
@@ -531,28 +540,38 @@
         [struct((lay.frames, half, model))] * 2,
         grid=(few_steps,),
     )(pos, info, *pairs, mod_table)
+    wo_own, _ = lax.optimization_barrier((wo_own, hidden))
+    wo_rows = [wo_own, lax.ppermute(wo_own, AXES, lay.swap(kc=1))]
 
     fold = 3 if rows % 24 == 0 else 1
     piece_shape = (groups, rows // fold, quarter * fold)
-    queries, keys, values, grad_attn, kept, sent, *projected = call(
+    token_spec = spread(lay.frames, model, step_patches)
+    att_spec = spread(lay.frames, chip_width, step_patches)
+    queries, keys, values, attended, kept, sent = call(
         functools.partial(forward_kernel, lay),
         "forward",
         14 * model * 1000,
-        [spread(lay.frames, model, step_patches)] * 2
-        + w_specs
-        + [whole_spec(w_out.shape)] * nc,
-        [triple_spec] * 4 + [whole_spec(piece_shape)] * 2 + part_specs,
-        [triple_shape] * 4 + [struct(piece_shape, F32)] * 2 + part_shapes,
-        [
-            w_scratch,
-            pltpu.VMEM((lay.frames, step_patches, chip_width), BF16),
-            pltpu.VMEM((chip_width, model), BF16),
-            pltpu.VMEM((chip_width, model), F32),
-            pltpu.VMEM(piece_shape, F32),
-        ],
+        [token_spec] * 2 + w_specs,
+        [triple_spec] * 3 + [att_spec] + [whole_spec(piece_shape)] * 2,
+        [triple_shape] * 3
+        + [struct((lay.frames, half, chip_width))]
+        + [struct(piece_shape, F32)] * 2,
+        [w_scratch, pltpu.VMEM((chip_width, model), F32), pltpu.VMEM(piece_shape, F32)],
         (steps,),
-    )(pos, info, hidden, grad_proj, *w_pieces, *wo_rows)
+    )(pos, info, hidden, grad_proj, *w_pieces)
     got = lax.ppermute(sent, AXES, lay.swap(kc=1))
+
+    grad_attn, *projected = call(
+        functools.partial(projection_kernel, lay),
+        "projection",
+        6 * model * 1000,
+        [token_spec, att_spec] + [whole_spec(w_out.shape)] * nc,
+        [triple_spec] + part_specs,
+        [triple_shape] + part_shapes,
+        [pltpu.VMEM((chip_width, model), BF16)],
+        (steps,),
+        prefetch=1,
+    )(pos, grad_proj, attended, *wo_rows)
     projected = over_chips(projected)
 
     middle = groups // 2

time: 136 us -> 142 us (1.044)
  waiting for transfers between devices: 43.4 us -> 55.2 us
  starting transfers between devices: 45.8 us -> 36.9 us
  Pallas kernels: 35.1 us -> 38.5 us
    ppermute x3, waiting for transfers between devices: 0.01 us -> 13.3 us  [doubling(): return [held, lax.ppermute(held, AXES, swap(bits[-1]))]]
    ppermute x1, waiting for transfers between devices: 15.2 us -> 6.03 us  [local(): wo_own = lax.ppermute(late_w_out, AXES, lay.rows_to_chip())]
    ppermute x4, starting transfers between devices: 14.7 us -> 9.29 us  [from_plane(): lax.ppermute(part, AXES, lay.from_plane(k))]
    ppermute x6, waiting for transfers between devices: 4.08 us -> 9.44 us  [over_chips(): got = [lax.ppermute(parts[k], AXES, chip_swap(k)) for k in range(1, chips)]]
    pallas_call x0 -> x1, Pallas kernels: none -> 4.93 us  [local(): call(functools.partial(projection_kernel, lay), 'projection', 6 * model *...]
    ppermute x2, waiting for transfers between devices: 6.1 us -> 3.42 us  [local(): lax.ppermute(pair, AXES, lay.to_plane(k))]
    ppermute x1, waiting for transfers between devices: 0.01 us -> 2.5 us  [local(): first = lax.ppermute(own[0], AXES, chip_swap(lay.chip_bits(0)[0]))]
    ppermute x2, starting transfers between devices: 5.2 us -> 3.12 us  [doubling(): got = lax.ppermute(held, AXES, swap(bit)) if first is None else first]
  transfers between devices with their start and end apart: 29 -> 29, of which waited for: 9 -> 13; matrix products, arithmetic and copies ran while one was open for 3% -> 3% of each run, Pallas kernels for 15% -> 25%
where the time goes in v13:
time: 142 us; the launch traced here: 140 us
  waiting for transfers between devices  55.2 us (39%)
  Pallas kernels  38.5 us (27%)
  starting transfers between devices  36.9 us (26%)
  other arithmetic  4.88 us (3%)
  local copies, waits for them, and re-layouts  3.32 us (2%)
    ppermute x3, waiting for transfers between devices, doubling(): return [held, lax.ppermute(held, AXES, swap(bits[-1]))]  13.3 us
    ppermute x2, waiting for transfers between devices, doubling(): got = lax.ppermute(held, AXES, swap(bit)) if first is None else first  11.9 us
    pallas_call x1, Pallas kernels, local(): call(functools.partial(forward_kernel, lay), 'forward', 14 * model * 1000...  9.58 us
    pallas_call x1, Pallas kernels, local(): call(functools.partial(backward_kernel, lay), 'backward', 10 * model * 10...  9.56 us
    ppermute x6, waiting for transfers between devices, over_chips(): got = [lax.ppermute(parts[k], AXES, chip_swap(k)) for k in range(1, chips)]  9.44 us
    ppermute x4, starting transfers between devices, from_plane(): lax.ppermute(part, AXES, lay.from_plane(k))  9.29 us
    ppermute x6, starting transfers between devices, over_chips(): got = [lax.ppermute(parts[k], AXES, chip_swap(k)) for k in range(1, chips)]  7.04 us
    ppermute x2, starting transfers between devices, local(): lax.ppermute(pair, AXES, lay.to_plane(k))  6.31 us
  transfers between devices with their start and end apart: 29, of which 13 were waited for; matrix products, arithmetic and copies ran while one was open for 3% of the time, Pallas kernels for 25%

profile of v13, /device:TPU:4, one launch (start us, length us, event | category | flops | bytes accessed | tf_op | source)
XLA Modules:
  0.0 139.9 jit_solution(5554927272219457170)
XLA Ops:
  0.6 0.6 pad_add_fusion.1.pos_ref
  1.2 3.4 %start.1 = (bf16[1,2,64,1152]{3,2,1,0:T(8,128)(2,1)}, bf16[1,2,64,1152]{3,2,1,0:T(8,128)(2,1)}, bf16[144,432]{1,0:T(8,128)(2,1)}, bf16[144,432]{1,0:T(8,128)(2,1)}) custom-call(s32[4]{0:T(128)} %pad_add_fusion.1.pos_ref, bf16[1,128,1152]{2,1,0:T(8,128)(2,1)} %x_ref.1, bf16[1,128,1152]{2,1,0:T(8,128)(2,1)} %g_ref.1, bf16[144,3456]{1,0:T(8,128)(2,1)} %w_ref.1), custom_call_target="tpu_custom_call" | custom-call | flops 1179648000 | bytes 2359296 | tf_op jit(solution)/shard_map/start/pallas_call | solution.py:481
  4.7 1.9 %collective-permute-start.2 = (bf16[1,2,64,1152]{3,2,1,0:T(8,128)(2,1)}, bf16[1,2,64,1152]{3,2,1,0:T(8,128)(2,1)S(1)}, u32[]{:S(2)}, u32[]{:S(2)}) collective-permute-start(bf16[1,2,64,1152]{3,2,1,0:T(8,128)(2,1)} %get-tuple-element.58), channel_id=1, source_target_pairs={{0,0},{1,1},{2,16},{3,17},{4,2},{5,3},{6,18},{7,19},{8,20},{9,21},... | collective-permute-start | bytes 884744 | tf_op jit(solution)/shard_map/ppermute | solution.py:491
  6.6 1.6 %collective-permute-start.8 = (bf16[144,432]{1,0:T(8,128)(2,1)}, bf16[144,432]{1,0:T(8,128)(2,1)S(1)}, u32[]{:S(2)}, u32[]{:S(2)}) collective-permute-start(bf16[144,432]{1,0:T(8,128)(2,1)} %get-tuple-element.64), channel_id=1, source_target_pairs={{0,1},{1,0},{2,3},{3,2},{4,5},{5,4},{6,7},{7,6},{8,9},{9,8},{10,11... | collective-permute-start | bytes 373256 | tf_op jit(solution)/shard_map/ppermute | solution.py:493
  8.1 4.4 %collective-permute-start.3 = (bf16[1,2,64,1152]{3,2,1,0:T(8,128)(2,1)}, bf16[1,2,64,1152]{3,2,1,0:T(8,128)(2,1)S(1)}, u32[]{:S(2)}, u32[]{:S(2)}) collective-permute-start(bf16[1,2,64,1152]{3,2,1,0:T(8,128)(2,1)} %get-tuple-element.59), channel_id=1, source_target_pairs={{0,2},{1,3},{2,18},{3,19},{4,0},{5,1},{6,16},{7,17},{8,22},{9,23},... | collective-permute-start | bytes 884744 | tf_op jit(solution)/shard_map/ppermute | solution.py:491
  12.6 0.1 fusion.7
  12.6 0.6 collective-permute-start
  13.3 0.8 collective-permute-done
  14.1 2.1 %collective-permute-start.1 = (s32[2,16]{1,0:T(2,128)S(1)}, s32[2,16]{1,0:T(2,128)S(1)}, u32[]{:S(2)}, u32[]{:S(2)}) collective-permute-start(s32[2,16]{1,0:T(2,128)S(1)} %pad_add_fusion), channel_id=1, source_target_pairs={{0,16},{1,17},{2,18},{3,19},{4,20},{5,21},{6,22},{7,23},{8,24},{9,... | collective-permute-start | bytes 392 | tf_op jit(solution)/shard_map/ppermute | solution.py:471
  16.2 0.5 collective-permute-start.4
  16.7 1.0 collective-permute-done.1
  17.7 0.6 fusion.2.info_ref
  18.3 0.9 broadcast_select_fusion.1
  19.2 3.4 %collective-permute-done.3.refs_1_ = bf16[1,2,64,1152]{3,2,1,0:T(8,128)(2,1)S(1)} collective-permute-done((bf16[1,2,64,1152]{3,2,1,0:T(8,128)(2,1)}, bf16[1,2,64,1152]{3,2,1,0:T(8,128)(2,1)S(1)}, u32[]{:S(2)}, u32[]{:S(2)}) %collective-permute-start.3) | collective-permute-done | bytes 294944 | tf_op jit(solution)/shard_map/ppermute | solution.py:491
  22.7 2.5 %collective-permute-done.4 = bf16[1,2,64,1152]{3,2,1,0:T(8,128)(2,1)S(1)} collective-permute-done((bf16[1,2,64,1152]{3,2,1,0:T(8,128)(2,1)S(1)}, bf16[1,2,64,1152]{3,2,1,0:T(8,128)(2,1)S(1)}, u32[]{:S(2)}, u32[]{:S(2)}) %collective-permute-start.4) | collective-permute-done | bytes 294944 | tf_op jit(solution)/shard_map/ppermute | solution.py:501
  25.2 0.4 collective-permute-start.6
  25.5 0.1 maximum_bitcast_fusion.2
  25.6 2.7 %collective-permute-start.9 = (bf16[1,144,864]{2,1,0:T(8,128)(2,1)S(1)}, bf16[1,144,864]{2,1,0:T(8,128)(2,1)S(1)}, u32[]{:S(2)}, u32[]{:S(2)}) collective-permute-start(bf16[1,144,864]{2,1,0:T(8,128)(2,1)S(1)} %maximum_bitcast_fusion.2), channel_id=1, source_target_pairs={{0,4},{1,5},{2,6},{3,7},{4,0},{5,1},{6,2},{7,3},{8,12},{9,13},{10,... | collective-permute-start | bytes 746504 | tf_op jit(solution)/shard_map/ppermute | solution.py:459
  28.5 0.2 collective-permute-start.5
  28.7 6.4 %collective-permute-done.6 = bf16[1,2,64,1152]{3,2,1,0:T(8,128)(2,1)S(1)} collective-permute-done((bf16[1,2,64,1152]{3,2,1,0:T(8,128)(2,1)S(1)}, bf16[1,2,64,1152]{3,2,1,0:T(8,128)(2,1)S(1)}, u32[]{:S(2)}, u32[]{:S(2)}) %collective-permute-start.6) | collective-permute-done | bytes 294944 | tf_op jit(solution)/shard_map/ppermute | solution.py:459
  35.2 0.1 collective-permute-start.7
  35.3 5.5 %collective-permute-done.9 = bf16[1,144,864]{2,1,0:T(8,128)(2,1)S(1)} collective-permute-done((bf16[1,144,864]{2,1,0:T(8,128)(2,1)S(1)}, bf16[1,144,864]{2,1,0:T(8,128)(2,1)S(1)}, u32[]{:S(2)}, u32[]{:S(2)}) %collective-permute-start.9) | collective-permute-done | bytes 248864 | tf_op jit(solution)/shard_map/ppermute | solution.py:459
  40.7 0.1 pad_maximum_fusion.2.refs_0_
  40.8 0.1 collective-permute-start.10
  40.9 5.0 %collective-permute-done.5.refs_1_ = bf16[2,2,64,1152]{3,2,1,0:T(8,128)(2,1)S(1)} collective-permute-done((bf16[2,2,64,1152]{3,2,1,0:T(8,128)(2,1)S(1)}, bf16[2,2,64,1152]{3,2,1,0:T(8,128)(2,1)S(1)}, u32[]{:S(2)}, u32[]{:S(2)}) %collective-permute-start.5) | collective-permute-done | bytes 589856 | tf_op jit(solution)/shard_map/ppermute | solution.py:462
  45.9 8.3 %collective-permute-done.10.refs_1_ = bf16[2,144,864]{2,1,0:T(8,128)(2,1)S(1)} collective-permute-done((bf16[2,144,864]{2,1,0:T(8,128)(2,1)S(1)}, bf16[2,144,864]{2,1,0:T(8,128)(2,1)S(1)}, u32[]{:S(2)}, u32[]{:S(2)}) %collective-permute-start.10) | collective-permute-done | bytes 497696 | tf_op jit(solution)/shard_map/ppermute | solution.py:462
  54.2 0.1 collective-permute-start.11
  54.3 0.5 collective-permute-start.12
  54.8 1.9 %collective-permute-start.13 = (bf16[144,1152]{1,0:T(8,128)(2,1)S(1)}, bf16[144,1152]{1,0:T(8,128)(2,1)S(1)}, u32[]{:S(2)}, u32[]{:S(2)}) collective-permute-start(bf16[144,1152]{1,0:T(8,128)(2,1)S(1)} %copy-done.14), channel_id=1, source_target_pairs={{0,0},{1,1},{2,18},{3,19},{4,8},{5,9},{6,26},{7,27},{8,4},{9,5},{1... | collective-permute-start | bytes 995336 | tf_op jit(solution)/shard_map/ppermute | solution.py:506
  56.8 4.6 %prepare.1 = (bf16[8,64,1152]{2,1,0:T(8,128)(2,1)}, bf16[8,64,1152]{2,1,0:T(8,128)(2,1)}) custom-call(s32[4]{0:T(128)} %pad_add_fusion.1.pos_ref, s32[16]{0:T(128)} %fusion.2.info_ref, bf16[2,2,64,1152]{3,2,1,0:T(8,128)(2,1)} %copy-done.1, bf16[2,2,64,1152]{3,2,1,0:T(8,128)(2,1)} %copy-done.9, bf16[2,2,64,1152]{3,2,1,0:T(8,128)(2,1)} %copy-done.2, ...), custom_call_target="tpu_custom_call" | custom-call | flops 1769472000 | bytes 2359296 | tf_op jit(solution)/shard_map/prepare/pallas_call | solution.py:534
  61.3 6.0 %collective-permute-done.13.refs_0_ = bf16[144,1152]{1,0:T(8,128)(2,1)S(1)} collective-permute-done((bf16[144,1152]{1,0:T(8,128)(2,1)S(1)}, bf16[144,1152]{1,0:T(8,128)(2,1)S(1)}, u32[]{:S(2)}, u32[]{:S(2)}) %collective-permute-start.13) | collective-permute-done | bytes 331808 | tf_op jit(solution)/shard_map/ppermute | solution.py:506
  67.4 0.8 copy-done.12
  68.2 0.2 copy-done.13
  68.4 9.6 %forward.1 = (bf16[2,8,64,144]{3,2,1,0:T(8,128)(2,1)}, bf16[2,8,64,144]{3,2,1,0:T(8,128)(2,1)}, bf16[2,8,64,144]{3,2,1,0:T(8,128)(2,1)}, bf16[8,64,288]{2,1,0:T(...) custom-call(s32[4]{0:T(128)} %pad_add_fusion.1.pos_ref, s32[16]{0:T(128)} %fusion.2.info_ref, ...), custom_call_target="tpu_custom_call" | custom-call | flops 8257536000 | bytes 2359296 | tf_op jit(solution)/shard_map/forward/pallas_call | solution.py:550
  78.0 0.5 collective-permute-start.15
  78.4 0.7 copy-done.16
  79.2 4.9 %projection.1 = (bf16[2,8,64,144]{3,2,1,0:T(8,128)(2,1)}, f32[2,64,1152]{2,1,0:T(8,128)}, bf16[2,64,1152]{2,1,0:T(8,128)(2,1)}, bf16[2,64,1152]{2,1,0:T(8,128)(2,1)}, bf16[2,64,1152]{2,1,0:T(8,128)(2,1)}) custom-call(s32[4]{0:T(128)} %pad_add_fusion.1.pos_ref, bf16[8,64,1152]{2,1,0:T(8,128)(2,1)} %get-tuple-element.73.gp_ref, ...), custom_call_target="tpu_custom_call" | custom-call | flops 3538944000 | bytes 2359296 | tf_op jit(solution)/shard_map/projection/pallas_call | solution.py:564
  84.1 2.0 %collective-permute-start.17 = (bf16[2,64,1152]{2,1,0:T(8,128)(2,1)}, bf16[2,64,1152]{2,1,0:T(8,128)(2,1)S(1)}, u32[]{:S(2)}, u32[]{:S(2)}) collective-permute-start(bf16[2,64,1152]{2,1,0:T(8,128)(2,1)} %get-tuple-element.90), channel_id=1, source_target_pairs={{0,1},{1,0},{2,3},{3,2},{4,5},{5,4},{6,7},{7,6},{8,9},{9,8},{10,11... | collective-permute-start | bytes 884744 | tf_op jit(solution)/shard_map/ppermute | solution.py:465
  86.1 0.4 collective-permute-start.18
  86.5 1.1 collective-permute-start.19
  87.6 0.1 slice_add_fusion
  87.7 0.4 collective-permute-start.16
  88.0 9.6 %backward.1 = (f32[2,64,1152]{2,1,0:T(8,128)}, bf16[2,64,1152]{2,1,0:T(8,128)(2,1)}, bf16[2,64,1152]{2,1,0:T(8,128)(2,1)}, bf16[2,64,1152]{2,1,0:T(8,128)(2,1)}) custom-call(s32[4]{0:T(128)} %pad_add_fusion.1.pos_ref, s32[16]{0:T(128)} %fusion.2.info_ref, bf16[2,144,864]{2,1,0:T(8,128)(2,1)} %copy-done.3, bf16[2,144,864]{2,1,0:T(8,128)(2,1)} %copy-done.11, ...), custom_call_target="tpu_custom_call" | custom-call | flops 5898240000 | bytes 2359296 | tf_op jit(solution)/shard_map/backward/pallas_call | solution.py:582
  97.6 3.7 %collective-permute-done.18.refs_4_ = bf16[2,64,1152]{2,1,0:T(8,128)(2,1)S(1)} collective-permute-done((bf16[2,64,1152]{2,1,0:T(8,128)(2,1)}, bf16[2,64,1152]{2,1,0:T(8,128)(2,1)S(1)}, u32[]{:S(2)}, u32[]{:S(2)}) %collective-permute-start.18) | collective-permute-done | bytes 294944 | tf_op jit(solution)/shard_map/ppermute | solution.py:465
  101.3 0.5 collective-permute-start.22
  101.9 1.2 collective-permute-start.23
  103.1 1.8 %collective-permute-start.24 = (bf16[2,64,1152]{2,1,0:T(8,128)(2,1)}, bf16[2,64,1152]{2,1,0:T(8,128)(2,1)S(1)}, u32[]{:S(2)}, u32[]{:S(2)}) collective-permute-start(bf16[2,64,1152]{2,1,0:T(8,128)(2,1)} %get-tuple-element.102), channel_id=1, source_target_pairs={{0,17},{1,16},{2,19},{3,18},{4,21},{5,20},{6,23},{7,22},{8,25},{9,... | collective-permute-start | bytes 884744 | tf_op jit(solution)/shard_map/ppermute | solution.py:465
  104.9 3.1 %output.1 = (bf16[64,1152]{1,0:T(8,128)(2,1)}, bf16[64,1152]{1,0:T(8,128)(2,1)}) custom-call(s32[4]{0:T(128)} %pad_add_fusion.1.pos_ref, s32[16]{0:T(128)} %fusion.2.info_ref, bf16[1,2,64,1152]{3,2,1,0:T(8,128)(2,1)} %copy-done.4, bf16[1,2,64,1152]{3,2,1,0:T(8,128)(2,1)} %copy-done.5, f32[2,64,1152]{2,1,0:T(8,128)} %get-tuple-element.93.refs_2_, ...), custom_call_target="tpu_custom_call" | custom-call | flops 11796480000 | bytes 2359296 | tf_op jit(solution)/shard_map/output/pallas_call | solution.py:595
  108.0 3.3 %collective-permute-start.20 = (bf16[64,1152]{1,0:T(8,128)(2,1)}, bf16[64,1152]{1,0:T(8,128)(2,1)S(1)}, u32[]{:S(2)}, u32[]{:S(2)}) collective-permute-start(bf16[64,1152]{1,0:T(8,128)(2,1)} %get-tuple-element.97), channel_id=1, source_target_pairs={{0,0},{1,1},{16,2},{17,3},{2,4},{3,5},{18,6},{19,7},{20,8},{21,9},... | collective-permute-start | bytes 442376 | tf_op jit(solution)/shard_map/ppermute | solution.py:452
  111.3 1.9 %collective-permute-start.21 = (bf16[64,1152]{1,0:T(8,128)(2,1)}, bf16[64,1152]{1,0:T(8,128)(2,1)S(1)}, u32[]{:S(2)}, u32[]{:S(2)}) collective-permute-start(bf16[64,1152]{1,0:T(8,128)(2,1)} %get-tuple-element.98), channel_id=1, source_target_pairs={{2,0},{3,1},{18,2},{19,3},{0,4},{1,5},{16,6},{17,7},{22,8},{23,9},... | collective-permute-start | bytes 442376 | tf_op jit(solution)/shard_map/ppermute | solution.py:452
  113.3 0.1 collective-permute-start.27
  113.4 5.7 %collective-permute-done.23.refs_4_ = bf16[2,64,1152]{2,1,0:T(8,128)(2,1)S(1)} collective-permute-done((bf16[2,64,1152]{2,1,0:T(8,128)(2,1)}, bf16[2,64,1152]{2,1,0:T(8,128)(2,1)S(1)}, u32[]{:S(2)}, u32[]{:S(2)}) %collective-permute-start.23) | collective-permute-done | bytes 294944 | tf_op jit(solution)/shard_map/ppermute | solution.py:465
  119.1 0.7 copy-done.21
  119.8 0.7 copy-done.22
  120.5 3.4 %input_grad.1 = (bf16[64,1152]{1,0:T(8,128)(2,1)}, bf16[64,1152]{1,0:T(8,128)(2,1)}) custom-call(s32[4]{0:T(128)} %pad_add_fusion.1.pos_ref, s32[16]{0:T(128)} %fusion.2.info_ref, bf16[1,2,64,1152]{3,2,1,0:T(8,128)(2,1)} %copy-done.4, bf16[1,2,64,1152]{3,2,1,0:T(8,128)(2,1)} %copy-done.5, f32[2,64,1152]{2,1,0:T(8,128)} %get-tuple-element.103.refs_2_, ...), custom_call_target="tpu_custom_call" | custom-call | flops 1769472000 | bytes 2359296 | tf_op jit(solution)/shard_map/input_grad/pallas_call | solution.py:607
  123.9 2.2 %collective-permute-start.25 = (bf16[64,1152]{1,0:T(8,128)(2,1)}, bf16[64,1152]{1,0:T(8,128)(2,1)S(1)}, u32[]{:S(2)}, u32[]{:S(2)}) collective-permute-start(bf16[64,1152]{1,0:T(8,128)(2,1)} %get-tuple-element.107), channel_id=1, source_target_pairs={{0,0},{1,1},{16,2},{17,3},{2,4},{3,5},{18,6},{19,7},{20,8},{21,9},... | collective-permute-start | bytes 442376 | tf_op jit(solution)/shard_map/ppermute | solution.py:452
  126.1 1.9 %collective-permute-start.26 = (bf16[64,1152]{1,0:T(8,128)(2,1)}, bf16[64,1152]{1,0:T(8,128)(2,1)S(1)}, u32[]{:S(2)}, u32[]{:S(2)}) collective-permute-start(bf16[64,1152]{1,0:T(8,128)(2,1)} %get-tuple-element.108), channel_id=1, source_target_pairs={{2,0},{3,1},{18,2},{19,3},{0,4},{1,5},{16,6},{17,7},{22,8},{23,9},... | collective-permute-start | bytes 442376 | tf_op jit(solution)/shard_map/ppermute | solution.py:452
  128.1 2.7 %collective-permute-start.28 = (f32[48,864]{1,0:T(8,128)S(1)}, f32[48,864]{1,0:T(8,128)S(1)}, u32[]{:S(2)}, u32[]{:S(2)}) collective-permute-start(f32[48,864]{1,0:T(8,128)S(1)} %bitcast.28), channel_id=1, source_target_pairs={{0,0},{1,1},{2,8},{3,9},{4,16},{5,17},{6,24},{7,25},{8,4},{9,5},{1... | collective-permute-start | bytes 497672 | tf_op jit(solution)/shard_map/ppermute | solution.py:623
  130.8 2.9 %collective-permute-done.26 = bf16[64,1152]{1,0:T(8,128)(2,1)S(1)} collective-permute-done((bf16[64,1152]{1,0:T(8,128)(2,1)}, bf16[64,1152]{1,0:T(8,128)(2,1)S(1)}, u32[]{:S(2)}, u32[]{:S(2)}) %collective-permute-start.26) | collective-permute-done | bytes 147488 | tf_op jit(solution)/shard_map/ppermute | solution.py:452
  133.7 0.7 maximum_bitcast_fusion.1
  134.5 0.7 maximum_bitcast_fusion
  135.2 3.9 %collective-permute-done.28 = f32[48,864]{1,0:T(8,128)S(1)} collective-permute-done((f32[48,864]{1,0:T(8,128)S(1)}, f32[48,864]{1,0:T(8,128)S(1)}, u32[]{:S(2)}, u32[]{:S(2)}) %collective-permute-start.28) | collective-permute-done | bytes 165920 | tf_op jit(solution)/shard_map/ppermute | solution.py:623
  139.1 0.1 fusion.6
  139.2 0.7 maximum_multiply_fusion
  (65 shorter events, 0.4 us)
Async XLA Ops:
  1.2 11.3 %copy-start.6 = (s32[1,4]{1,0:T(1,128)S(1)}, s32[1,4]{1,0:T(1,128)}, u32[]{:S(2)}) copy-start(s32[1,4]{1,0:T(1,128)} %param.12) | copy-start | bytes 52
  1.2 11.3 %copy-start.7 = (s32[1,4]{1,0:T(1,128)S(1)}, s32[1,4]{1,0:T(1,128)}, u32[]{:S(2)}) copy-start(s32[1,4]{1,0:T(1,128)} %param.11) | copy-start | bytes 52
  1.2 11.3 %copy-start.8 = (s32[1,8]{1,0:T(1,128)S(1)}, s32[1,8]{1,0:T(1,128)}, u32[]{:S(2)}) copy-start(s32[1,8]{1,0:T(1,128)} %param.10) | copy-start | bytes 100
  4.7 11.5 %collective-permute-start.2 = (bf16[1,2,64,1152]{3,2,1,0:T(8,128)(2,1)}, bf16[1,2,64,1152]{3,2,1,0:T(8,128)(2,1)S(1)}, u32[]{:S(2)}, u32[]{:S(2)}) collective-permute-start(bf16[1,2,64,1152]{3,2,1,0:T(8,128)(2,1)} %get-tuple-element.58), channel_id=1, source_target_pairs={{0,0},{1,1},{2,16},{3,17},{4,2},{5,3},{6,18},{7,19},{8,20},{9,21},... | collective-permute-start | bytes 884744 | tf_op jit(solution)/shard_map/ppermute | solution.py:491
  6.6 11.7 %collective-permute-start.8 = (bf16[144,432]{1,0:T(8,128)(2,1)}, bf16[144,432]{1,0:T(8,128)(2,1)S(1)}, u32[]{:S(2)}, u32[]{:S(2)}) collective-permute-start(bf16[144,432]{1,0:T(8,128)(2,1)} %get-tuple-element.64), channel_id=1, source_target_pairs={{0,1},{1,0},{2,3},{3,2},{4,5},{5,4},{6,7},{7,6},{8,9},{9,8},{10,11... | collective-permute-start | bytes 373256 | tf_op jit(solution)/shard_map/ppermute | solution.py:493
  8.1 14.5 %collective-permute-start.3 = (bf16[1,2,64,1152]{3,2,1,0:T(8,128)(2,1)}, bf16[1,2,64,1152]{3,2,1,0:T(8,128)(2,1)S(1)}, u32[]{:S(2)}, u32[]{:S(2)}) collective-permute-start(bf16[1,2,64,1152]{3,2,1,0:T(8,128)(2,1)} %get-tuple-element.59), channel_id=1, source_target_pairs={{0,2},{1,3},{2,18},{3,19},{4,0},{5,1},{6,16},{7,17},{8,22},{9,23},... | collective-permute-start | bytes 884744 | tf_op jit(solution)/shard_map/ppermute | solution.py:491
  12.6 1.4 %collective-permute-start = (s32[1,16]{1,0:T(1,128)S(1)}, s32[1,16]{1,0:T(1,128)S(1)}, u32[]{:S(2)}, u32[]{:S(2)}) collective-permute-start(s32[1,16]{1,0:T(1,128)S(1)} %fusion.7), channel_id=1, source_target_pairs={{0,8},{1,9},{2,10},{3,11},{4,12},{5,13},{6,14},{7,15},{8,0},{9,1},... | collective-permute-start | bytes 200 | tf_op jit(solution)/shard_map/ppermute | solution.py:469
  14.1 3.6 %collective-permute-start.1 = (s32[2,16]{1,0:T(2,128)S(1)}, s32[2,16]{1,0:T(2,128)S(1)}, u32[]{:S(2)}, u32[]{:S(2)}) collective-permute-start(s32[2,16]{1,0:T(2,128)S(1)} %pad_add_fusion), channel_id=1, source_target_pairs={{0,16},{1,17},{2,18},{3,19},{4,20},{5,21},{6,22},{7,23},{8,24},{9,... | collective-permute-start | bytes 392 | tf_op jit(solution)/shard_map/ppermute | solution.py:471
  16.2 19.0 %copy-start.4 = (bf16[1,2,64,1152]{3,2,1,0:T(8,128)(2,1)}, bf16[1,2,64,1152]{3,2,1,0:T(8,128)(2,1)S(1)}, u32[]{:S(2)}) copy-start(bf16[1,2,64,1152]{3,2,1,0:T(8,128)(2,1)S(1)} %collective-permute-done.2.refs_0_) | copy-start | bytes 884740
  16.2 9.0 %collective-permute-start.4 = (bf16[1,2,64,1152]{3,2,1,0:T(8,128)(2,1)S(1)}, bf16[1,2,64,1152]{3,2,1,0:T(8,128)(2,1)S(1)}, u32[]{:S(2)}, u32[]{:S(2)}) collective-permute-start(bf16[1,2,64,1152]{3,2,1,0:T(8,128)(2,1)S(1)} %collective-permute-done.2.refs_0_), channel_id=1, source_target_pairs={{0,1},{1,0},{2,3},{3,2},{4,5},{5,4},{6,7},{7,6},{8,9},{9,8},{10,11... | collective-permute-start | bytes 884744 | tf_op jit(solution)/shard_map/ppermute | solution.py:501
  22.7 12.5 %copy-start.5 = (bf16[1,2,64,1152]{3,2,1,0:T(8,128)(2,1)}, bf16[1,2,64,1152]{3,2,1,0:T(8,128)(2,1)S(1)}, u32[]{:S(2)}) copy-start(bf16[1,2,64,1152]{3,2,1,0:T(8,128)(2,1)S(1)} %collective-permute-done.3.refs_1_) | copy-start | bytes 884740
  25.2 9.9 %collective-permute-start.6 = (bf16[1,2,64,1152]{3,2,1,0:T(8,128)(2,1)S(1)}, bf16[1,2,64,1152]{3,2,1,0:T(8,128)(2,1)S(1)}, u32[]{:S(2)}, u32[]{:S(2)}) collective-permute-start(bf16[1,2,64,1152]{3,2,1,0:T(8,128)(2,1)S(1)} %collective-permute-done.3.refs_1_), channel_id=1, source_target_pairs={{0,16},{1,17},{2,18},{3,19},{4,20},{5,21},{6,22},{7,23},{8,24},{9,... | collective-permute-start | bytes 884744 | tf_op jit(solution)/shard_map/ppermute | solution.py:459
  25.6 15.1 %collective-permute-start.9 = (bf16[1,144,864]{2,1,0:T(8,128)(2,1)S(1)}, bf16[1,144,864]{2,1,0:T(8,128)(2,1)S(1)}, u32[]{:S(2)}, u32[]{:S(2)}) collective-permute-start(bf16[1,144,864]{2,1,0:T(8,128)(2,1)S(1)} %maximum_bitcast_fusion.2), channel_id=1, source_target_pairs={{0,4},{1,5},{2,6},{3,7},{4,0},{5,1},{6,2},{7,3},{8,12},{9,13},{10,... | collective-permute-start | bytes 746504 | tf_op jit(solution)/shard_map/ppermute | solution.py:459
  28.4 28.3 %copy-start.1 = (bf16[2,2,64,1152]{3,2,1,0:T(8,128)(2,1)}, bf16[2,2,64,1152]{3,2,1,0:T(8,128)(2,1)S(1)}, u32[]{:S(2)}) copy-start(bf16[2,2,64,1152]{3,2,1,0:T(8,128)(2,1)S(1)} %pad_maximum_fusion.refs_0_) | copy-start | bytes 1769476
  28.5 26.3 %copy-start.14 = (bf16[144,1152]{1,0:T(8,128)(2,1)S(1)}, bf16[144,1152]{1,0:T(8,128)(2,1)}, u32[]{:S(2)}) copy-start(bf16[144,1152]{1,0:T(8,128)(2,1)} %param.15) | copy-start | bytes 995332
  28.5 17.5 %collective-permute-start.5 = (bf16[2,2,64,1152]{3,2,1,0:T(8,128)(2,1)S(1)}, bf16[2,2,64,1152]{3,2,1,0:T(8,128)(2,1)S(1)}, u32[]{:S(2)}, u32[]{:S(2)}) collective-permute-start(bf16[2,2,64,1152]{3,2,1,0:T(8,128)(2,1)S(1)} %pad_maximum_fusion.refs_0_), channel_id=1, source_target_pairs={{0,16},{1,17},{2,18},{3,19},{4,20},{5,21},{6,22},{7,23},{8,24},{9,... | collective-permute-start | bytes 1769480 | tf_op jit(solution)/shard_map/ppermute | solution.py:462
  35.2 21.5 %copy-start.2 = (bf16[2,2,64,1152]{3,2,1,0:T(8,128)(2,1)}, bf16[2,2,64,1152]{3,2,1,0:T(8,128)(2,1)S(1)}, u32[]{:S(2)}) copy-start(bf16[2,2,64,1152]{3,2,1,0:T(8,128)(2,1)S(1)} %pad_maximum_fusion.1.refs_2_) | copy-start | bytes 1769476
  35.2 19.0 %collective-permute-start.7 = (bf16[2,2,64,1152]{3,2,1,0:T(8,128)(2,1)S(1)}, bf16[2,2,64,1152]{3,2,1,0:T(8,128)(2,1)S(1)}, u32[]{:S(2)}, u32[]{:S(2)}) collective-permute-start(bf16[2,2,64,1152]{3,2,1,0:T(8,128)(2,1)S(1)} %pad_maximum_fusion.1.refs_2_), channel_id=1, source_target_pairs={{0,1},{1,0},{2,3},{3,2},{4,5},{5,4},{6,7},{7,6},{8,9},{9,8},{10,11... | collective-permute-start | bytes 1769480 | tf_op jit(solution)/shard_map/ppermute | solution.py:462
  40.8 20.5 %copy-start.3 = (bf16[2,144,864]{2,1,0:T(8,128)(2,1)}, bf16[2,144,864]{2,1,0:T(8,128)(2,1)S(1)}, u32[]{:S(2)}) copy-start(bf16[2,144,864]{2,1,0:T(8,128)(2,1)S(1)} %pad_maximum_fusion.2.refs_0_) | copy-start | bytes 1492996
  40.8 13.4 %collective-permute-start.10 = (bf16[2,144,864]{2,1,0:T(8,128)(2,1)S(1)}, bf16[2,144,864]{2,1,0:T(8,128)(2,1)S(1)}, u32[]{:S(2)}, u32[]{:S(2)}) collective-permute-start(bf16[2,144,864]{2,1,0:T(8,128)(2,1)S(1)} %pad_maximum_fusion.2.refs_0_), channel_id=1, source_target_pairs={{0,2},{1,3},{2,0},{3,1},{4,6},{5,7},{6,4},{7,5},{8,10},{9,11},{10,... | collective-permute-start | bytes 1493000 | tf_op jit(solution)/shard_map/ppermute | solution.py:462
  45.9 10.8 %copy-start.9 = (bf16[2,2,64,1152]{3,2,1,0:T(8,128)(2,1)}, bf16[2,2,64,1152]{3,2,1,0:T(8,128)(2,1)S(1)}, u32[]{:S(2)}) copy-start(bf16[2,2,64,1152]{3,2,1,0:T(8,128)(2,1)S(1)} %collective-permute-done.5.refs_1_) | copy-start | bytes 1769476
  54.2 13.2 %copy-start.11 = (bf16[2,144,864]{2,1,0:T(8,128)(2,1)}, bf16[2,144,864]{2,1,0:T(8,128)(2,1)S(1)}, u32[]{:S(2)}) copy-start(bf16[2,144,864]{2,1,0:T(8,128)(2,1)S(1)} %collective-permute-done.10.refs_1_) | copy-start | bytes 1492996
  54.2 2.5 %copy-start.10 = (bf16[2,2,64,1152]{3,2,1,0:T(8,128)(2,1)}, bf16[2,2,64,1152]{3,2,1,0:T(8,128)(2,1)S(1)}, u32[]{:S(2)}) copy-start(bf16[2,2,64,1152]{3,2,1,0:T(8,128)(2,1)S(1)} %collective-permute-done.7.refs_3_) | copy-start | bytes 1769476
  54.2 13.1 %collective-permute-start.11 = (bf16[2,144,864]{2,1,0:T(8,128)(2,1)S(1)}, bf16[2,144,864]{2,1,0:T(8,128)(2,1)S(1)}, u32[]{:S(2)}, u32[]{:S(2)}) collective-permute-start(bf16[2,144,864]{2,1,0:T(8,128)(2,1)S(1)} %pad_maximum_fusion.2.refs_0_), channel_id=1, source_target_pairs={{0,8},{1,9},{2,10},{3,11},{4,12},{5,13},{6,14},{7,15},{8,0},{9,1},... | collective-permute-start | bytes 1493000 | tf_op jit(solution)/shard_map/ppermute | solution.py:514
  54.3 13.1 %collective-permute-start.12 = (bf16[2,144,864]{2,1,0:T(8,128)(2,1)S(1)}, bf16[2,144,864]{2,1,0:T(8,128)(2,1)S(1)}, u32[]{:S(2)}, u32[]{:S(2)}) collective-permute-start(bf16[2,144,864]{2,1,0:T(8,128)(2,1)S(1)} %collective-permute-done.10.refs_1_), channel_id=1, source_target_pairs={{0,8},{1,9},{2,10},{3,11},{4,12},{5,13},{6,14},{7,15},{8,0},{9,1},... | collective-permute-start | bytes 1493000 | tf_op jit(solution)/shard_map/ppermute | solution.py:514
  54.8 12.6 %collective-permute-start.13 = (bf16[144,1152]{1,0:T(8,128)(2,1)S(1)}, bf16[144,1152]{1,0:T(8,128)(2,1)S(1)}, u32[]{:S(2)}, u32[]{:S(2)}) collective-permute-start(bf16[144,1152]{1,0:T(8,128)(2,1)S(1)} %copy-done.14), channel_id=1, source_target_pairs={{0,0},{1,1},{2,18},{3,19},{4,8},{5,9},{6,26},{7,27},{8,4},{9,5},{1... | collective-permute-start | bytes 995336 | tf_op jit(solution)/shard_map/ppermute | solution.py:506
  67.4 10.6 %copy-start.15 = (bf16[144,1152]{1,0:T(8,128)(2,1)}, bf16[144,1152]{1,0:T(8,128)(2,1)S(1)}, u32[]{:S(2)}) copy-start(bf16[144,1152]{1,0:T(8,128)(2,1)S(1)} %collective-permute-done.13.refs_0_) | copy-start | bytes 995332
  67.4 11.1 %collective-permute-start.14 = (bf16[144,1152]{1,0:T(8,128)(2,1)S(1)}, bf16[144,1152]{1,0:T(8,128)(2,1)S(1)}, u32[]{:S(2)}, u32[]{:S(2)}) collective-permute-start(bf16[144,1152]{1,0:T(8,128)(2,1)S(1)} %collective-permute-done.13.refs_0_), channel_id=1, source_target_pairs={{0,8},{1,9},{2,10},{3,11},{4,12},{5,13},{6,14},{7,15},{8,0},{9,1},... | collective-permute-start | bytes 995336 | tf_op jit(solution)/shard_map/ppermute | solution.py:544
  67.4 0.8 copy-start.12
  67.4 1.0 copy-start.13
  78.0 9.6 %collective-permute-start.15 = (f32[4,48,864]{2,1,0:T(8,128)}, f32[4,48,864]{2,1,0:T(8,128)S(1)}, u32[]{:S(2)}, u32[]{:S(2)}) collective-permute-start(f32[4,48,864]{2,1,0:T(8,128)} %get-tuple-element.82), channel_id=1, source_target_pairs={{0,8},{1,9},{2,10},{3,11},{4,12},{5,13},{6,14},{7,15},{8,0},{9,1},... | collective-permute-start | bytes 1990664 | tf_op jit(solution)/shard_map/ppermute | solution.py:562
  78.4 0.7 copy-start.16
  79.2 8.4 %copy-start = (f32[4,48,864]{2,1,0:T(8,128)S(1)}, f32[4,48,864]{2,1,0:T(8,128)}, u32[]{:S(2)}) copy-start(f32[4,48,864]{2,1,0:T(8,128)} %get-tuple-element.81) | copy-start | bytes 1990660
  84.1 13.5 %collective-permute-start.17 = (bf16[2,64,1152]{2,1,0:T(8,128)(2,1)}, bf16[2,64,1152]{2,1,0:T(8,128)(2,1)S(1)}, u32[]{:S(2)}, u32[]{:S(2)}) collective-permute-start(bf16[2,64,1152]{2,1,0:T(8,128)(2,1)} %get-tuple-element.90), channel_id=1, source_target_pairs={{0,1},{1,0},{2,3},{3,2},{4,5},{5,4},{6,7},{7,6},{8,9},{9,8},{10,11... | collective-permute-start | bytes 884744 | tf_op jit(solution)/shard_map/ppermute | solution.py:465
  86.1 15.2 %collective-permute-start.18 = (bf16[2,64,1152]{2,1,0:T(8,128)(2,1)}, bf16[2,64,1152]{2,1,0:T(8,128)(2,1)S(1)}, u32[]{:S(2)}, u32[]{:S(2)}) collective-permute-start(bf16[2,64,1152]{2,1,0:T(8,128)(2,1)} %get-tuple-element.91), channel_id=1, source_target_pairs={{0,16},{1,17},{2,18},{3,19},{4,20},{5,21},{6,22},{7,23},{8,24},{9,... | collective-permute-start | bytes 884744 | tf_op jit(solution)/shard_map/ppermute | solution.py:465
  86.5 14.8 %collective-permute-start.19 = (bf16[2,64,1152]{2,1,0:T(8,128)(2,1)}, bf16[2,64,1152]{2,1,0:T(8,128)(2,1)S(1)}, u32[]{:S(2)}, u32[]{:S(2)}) collective-permute-start(bf16[2,64,1152]{2,1,0:T(8,128)(2,1)} %get-tuple-element.92), channel_id=1, source_target_pairs={{0,17},{1,16},{2,19},{3,18},{4,21},{5,20},{6,23},{7,22},{8,25},{9,... | collective-permute-start | bytes 884744 | tf_op jit(solution)/shard_map/ppermute | solution.py:465
  87.7 13.7 %collective-permute-start.16 = (f32[2,48,864]{2,1,0:T(8,128)S(1)}, f32[2,48,864]{2,1,0:T(8,128)S(1)}, u32[]{:S(2)}, u32[]{:S(2)}) collective-permute-start(f32[2,48,864]{2,1,0:T(8,128)S(1)} %get-tuple-element.88), channel_id=1, source_target_pairs={{0,2},{1,3},{2,0},{3,1},{4,6},{5,7},{6,4},{7,5},{8,10},{9,11},{10,... | collective-permute-start | bytes 995336 | tf_op jit(solution)/shard_map/ppermute | solution.py:580
  97.6 7.3 %copy-start.17 = (bf16[2,64,1152]{2,1,0:T(8,128)(2,1)}, bf16[2,64,1152]{2,1,0:T(8,128)(2,1)S(1)}, u32[]{:S(2)}) copy-start(bf16[2,64,1152]{2,1,0:T(8,128)(2,1)S(1)} %collective-permute-done.17.refs_3_) | copy-start | bytes 884740
  101.3 3.6 %copy-start.18 = (bf16[2,64,1152]{2,1,0:T(8,128)(2,1)}, bf16[2,64,1152]{2,1,0:T(8,128)(2,1)S(1)}, u32[]{:S(2)}) copy-start(bf16[2,64,1152]{2,1,0:T(8,128)(2,1)S(1)} %collective-permute-done.18.refs_4_) | copy-start | bytes 884740
  101.3 3.6 %copy-start.19 = (bf16[2,64,1152]{2,1,0:T(8,128)(2,1)}, bf16[2,64,1152]{2,1,0:T(8,128)(2,1)S(1)}, u32[]{:S(2)}) copy-start(bf16[2,64,1152]{2,1,0:T(8,128)(2,1)S(1)} %collective-permute-done.19.refs_5_) | copy-start | bytes 884740
  101.3 11.9 %collective-permute-start.22 = (bf16[2,64,1152]{2,1,0:T(8,128)(2,1)}, bf16[2,64,1152]{2,1,0:T(8,128)(2,1)S(1)}, u32[]{:S(2)}, u32[]{:S(2)}) collective-permute-start(bf16[2,64,1152]{2,1,0:T(8,128)(2,1)} %get-tuple-element.100), channel_id=1, source_target_pairs={{0,1},{1,0},{2,3},{3,2},{4,5},{5,4},{6,7},{7,6},{8,9},{9,8},{10,11... | collective-permute-start | bytes 884744 | tf_op jit(solution)/shard_map/ppermute | solution.py:465
  101.9 17.2 %collective-permute-start.23 = (bf16[2,64,1152]{2,1,0:T(8,128)(2,1)}, bf16[2,64,1152]{2,1,0:T(8,128)(2,1)S(1)}, u32[]{:S(2)}, u32[]{:S(2)}) collective-permute-start(bf16[2,64,1152]{2,1,0:T(8,128)(2,1)} %get-tuple-element.101), channel_id=1, source_target_pairs={{0,16},{1,17},{2,18},{3,19},{4,20},{5,21},{6,22},{7,23},{8,24},{9,... | collective-permute-start | bytes 884744 | tf_op jit(solution)/shard_map/ppermute | solution.py:465
  103.1 16.0 %collective-permute-start.24 = (bf16[2,64,1152]{2,1,0:T(8,128)(2,1)}, bf16[2,64,1152]{2,1,0:T(8,128)(2,1)S(1)}, u32[]{:S(2)}, u32[]{:S(2)}) collective-permute-start(bf16[2,64,1152]{2,1,0:T(8,128)(2,1)} %get-tuple-element.102), channel_id=1, source_target_pairs={{0,17},{1,16},{2,19},{3,18},{4,21},{5,20},{6,23},{7,22},{8,25},{9,... | collective-permute-start | bytes 884744 | tf_op jit(solution)/shard_map/ppermute | solution.py:465
  108.0 22.7 %collective-permute-start.20 = (bf16[64,1152]{1,0:T(8,128)(2,1)}, bf16[64,1152]{1,0:T(8,128)(2,1)S(1)}, u32[]{:S(2)}, u32[]{:S(2)}) collective-permute-start(bf16[64,1152]{1,0:T(8,128)(2,1)} %get-tuple-element.97), channel_id=1, source_target_pairs={{0,0},{1,1},{16,2},{17,3},{2,4},{3,5},{18,6},{19,7},{20,8},{21,9},... | collective-permute-start | bytes 442376 | tf_op jit(solution)/shard_map/ppermute | solution.py:452
  111.3 19.5 %collective-permute-start.21 = (bf16[64,1152]{1,0:T(8,128)(2,1)}, bf16[64,1152]{1,0:T(8,128)(2,1)S(1)}, u32[]{:S(2)}, u32[]{:S(2)}) collective-permute-start(bf16[64,1152]{1,0:T(8,128)(2,1)} %get-tuple-element.98), channel_id=1, source_target_pairs={{2,0},{3,1},{18,2},{19,3},{0,4},{1,5},{16,6},{17,7},{22,8},{23,9},... | collective-permute-start | bytes 442376 | tf_op jit(solution)/shard_map/ppermute | solution.py:452
  113.3 5.8 %copy-start.20 = (bf16[2,64,1152]{2,1,0:T(8,128)(2,1)}, bf16[2,64,1152]{2,1,0:T(8,128)(2,1)S(1)}, u32[]{:S(2)}) copy-start(bf16[2,64,1152]{2,1,0:T(8,128)(2,1)S(1)} %collective-permute-done.22.refs_3_) | copy-start | bytes 884740
  113.3 14.7 %collective-permute-start.27 = (f32[1,48,864]{2,1,0:T(8,128)S(1)}, f32[1,48,864]{2,1,0:T(8,128)S(1)}, u32[]{:S(2)}, u32[]{:S(2)}) collective-permute-start(f32[1,48,864]{2,1,0:T(8,128)S(1)} %slice.40), channel_id=1, source_target_pairs={{0,4},{1,5},{2,6},{3,7},{4,0},{5,1},{6,2},{7,3},{8,12},{9,13},{10,... | collective-permute-start | bytes 497672 | tf_op jit(solution)/shard_map/ppermute | solution.py:621
  119.1 0.7 copy-start.21
  119.8 0.7 copy-start.22
  123.9 6.8 %collective-permute-start.25 = (bf16[64,1152]{1,0:T(8,128)(2,1)}, bf16[64,1152]{1,0:T(8,128)(2,1)S(1)}, u32[]{:S(2)}, u32[]{:S(2)}) collective-permute-start(bf16[64,1152]{1,0:T(8,128)(2,1)} %get-tuple-element.107), channel_id=1, source_target_pairs={{0,0},{1,1},{16,2},{17,3},{2,4},{3,5},{18,6},{19,7},{20,8},{21,9},... | collective-permute-start | bytes 442376 | tf_op jit(solution)/shard_map/ppermute | solution.py:452
  126.1 7.6 %collective-permute-start.26 = (bf16[64,1152]{1,0:T(8,128)(2,1)}, bf16[64,1152]{1,0:T(8,128)(2,1)S(1)}, u32[]{:S(2)}, u32[]{:S(2)}) collective-permute-start(bf16[64,1152]{1,0:T(8,128)(2,1)} %get-tuple-element.108), channel_id=1, source_target_pairs={{2,0},{3,1},{18,2},{19,3},{0,4},{1,5},{16,6},{17,7},{22,8},{23,9},... | collective-permute-start | bytes 442376 | tf_op jit(solution)/shard_map/ppermute | solution.py:452
  128.1 11.0 %collective-permute-start.28 = (f32[48,864]{1,0:T(8,128)S(1)}, f32[48,864]{1,0:T(8,128)S(1)}, u32[]{:S(2)}, u32[]{:S(2)}) collective-permute-start(f32[48,864]{1,0:T(8,128)S(1)} %bitcast.28), channel_id=1, source_target_pairs={{0,0},{1,1},{2,8},{3,9},{4,16},{5,17},{6,24},{7,25},{8,4},{9,5},{1... | collective-permute-start | bytes 497672 | tf_op jit(solution)/shard_map/ppermute | solution.py:623

commit v14 on v12

--- a/solution.py
+++ b/solution.py
@@ -499,10 +499,9 @@
     for j in range(nc):
         after = ([], None) if j else (info, first)
         pairs += doubling(own[j], lay.chip_bits(j), chip_swap, *after)
-    pairs, w_pieces, wo_own = lax.optimization_barrier((pairs, w_pieces, wo_own))
+    pairs, w_pieces = lax.optimization_barrier((pairs, w_pieces))
     if halves > 1:
         w_pieces += [lax.ppermute(piece, AXES, lay.swap(kc=1)) for piece in w_pieces]
-    wo_rows = [wo_own, lax.ppermute(wo_own, AXES, lay.swap(kc=1))]
 
 
     def spread(count, width, patches_at_once):
@@ -531,6 +530,8 @@
         [struct((lay.frames, half, model))] * 2,
         grid=(few_steps,),
     )(pos, info, *pairs, mod_table)
+    wo_own, _ = lax.optimization_barrier((wo_own, hidden))
+    wo_rows = [wo_own, lax.ppermute(wo_own, AXES, lay.swap(kc=1))]
 
     fold = 3 if rows % 24 == 0 else 1
     piece_shape = (groups, rows // fold, quarter * fold)

time: 136 us -> 135 us (level); the launches traced: 134 us -> 135 us
    ppermute x1, waiting for transfers between devices: 15.2 us -> 0.86 us  [local(): wo_own = lax.ppermute(late_w_out, AXES, lay.rows_to_chip())]
    ppermute x3, waiting for transfers between devices: 0.01 us -> 9.1 us  [doubling(): return [held, lax.ppermute(held, AXES, swap(bits[-1]))]]
    ppermute x1, waiting for transfers between devices: 3.02 us -> 5.91 us  [local(): grad_w = lax.ppermute(cut[0], AXES, lay.to_owner())]
    ppermute x6, waiting for transfers between devices: 4.08 us -> 5.68 us  [over_chips(): got = [lax.ppermute(parts[k], AXES, chip_swap(k)) for k in range(1, chips)]]
  transfers between devices with their start and end apart: 29 -> 29, of which waited for: 9 -> 13; matrix products, arithmetic and copies ran while one was open for 3% -> 3% of each run, Pallas kernels for 15% -> 15%
where the time goes in v14:
time: 135 us
  starting transfers between devices  47.1 us (35%)
  waiting for transfers between devices  42.6 us (32%)
  Pallas kernels  35.1 us (26%)
  other arithmetic  5.98 us (4%)
  local copies, waits for them, and re-layouts  2.95 us (2%)
    ppermute x4, starting transfers between devices, from_plane(): lax.ppermute(part, AXES, lay.from_plane(k))  15.4 us
    ppermute x2, waiting for transfers between devices, doubling(): got = lax.ppermute(held, AXES, swap(bit)) if first is None else first  11.4 us
    pallas_call x1, Pallas kernels, local(): call(functools.partial(forward_kernel, lay), 'forward', 14 * model * 1000...  11.2 us
    pallas_call x1, Pallas kernels, local(): call(functools.partial(backward_kernel, lay), 'backward', 10 * model * 10...  9.56 us
    ppermute x3, waiting for transfers between devices, doubling(): return [held, lax.ppermute(held, AXES, swap(bits[-1]))]  9.1 us
    ppermute x6, starting transfers between devices, over_chips(): got = [lax.ppermute(parts[k], AXES, chip_swap(k)) for k in range(1, chips)]  7.63 us
    ppermute x2, waiting for transfers between devices, local(): lax.ppermute(pair, AXES, lay.to_plane(k))  6.1 us
    ppermute x1, waiting for transfers between devices, local(): grad_w = lax.ppermute(cut[0], AXES, lay.to_owner())  5.91 us
  transfers between devices with their start and end apart: 29, of which 13 were waited for; matrix products, arithmetic and copies ran while one was open for 3% of the time, Pallas kernels for 15%

profile of v14, /device:TPU:4, one launch (start us, length us, event | category | flops | bytes accessed | tf_op | source)
XLA Modules:
  0.0 134.9 jit_solution(16876108801394352933)
XLA Ops:
  0.6 0.6 pad_add_fusion.1.pos_ref
  1.3 3.4 %start.1 = (bf16[1,2,64,1152]{3,2,1,0:T(8,128)(2,1)}, bf16[1,2,64,1152]{3,2,1,0:T(8,128)(2,1)}, bf16[144,432]{1,0:T(8,128)(2,1)}, bf16[144,432]{1,0:T(8,128)(2,1)}) custom-call(s32[4]{0:T(128)} %pad_add_fusion.1.pos_ref, bf16[1,128,1152]{2,1,0:T(8,128)(2,1)} %x_ref.1, bf16[1,128,1152]{2,1,0:T(8,128)(2,1)} %g_ref.1, bf16[144,3456]{1,0:T(8,128)(2,1)} %w_ref.1), custom_call_target="tpu_custom_call" | custom-call | flops 1179648000 | bytes 2359296 | tf_op jit(solution)/shard_map/start/pallas_call | solution.py:471
  4.7 1.9 %collective-permute-start.2 = (bf16[1,2,64,1152]{3,2,1,0:T(8,128)(2,1)}, bf16[1,2,64,1152]{3,2,1,0:T(8,128)(2,1)S(1)}, u32[]{:S(2)}, u32[]{:S(2)}) collective-permute-start(bf16[1,2,64,1152]{3,2,1,0:T(8,128)(2,1)} %get-tuple-element.57), channel_id=1, source_target_pairs={{0,0},{1,1},{2,16},{3,17},{4,2},{5,3},{6,18},{7,19},{8,20},{9,21},... | collective-permute-start | bytes 884744 | tf_op jit(solution)/shard_map/ppermute | solution.py:481
  6.6 0.1 fusion.7
  6.7 2.2 %collective-permute-start = (s32[1,16]{1,0:T(1,128)S(1)}, s32[1,16]{1,0:T(1,128)S(1)}, u32[]{:S(2)}, u32[]{:S(2)}) collective-permute-start(s32[1,16]{1,0:T(1,128)S(1)} %fusion.7), channel_id=1, source_target_pairs={{0,8},{1,9},{2,10},{3,11},{4,12},{5,13},{6,14},{7,15},{8,0},{9,1},... | collective-permute-start | bytes 200 | tf_op jit(solution)/shard_map/ppermute | solution.py:459
  8.9 1.5 %collective-permute-start.8 = (bf16[144,432]{1,0:T(8,128)(2,1)}, bf16[144,432]{1,0:T(8,128)(2,1)S(1)}, u32[]{:S(2)}, u32[]{:S(2)}) collective-permute-start(bf16[144,432]{1,0:T(8,128)(2,1)} %get-tuple-element.63), channel_id=1, source_target_pairs={{0,1},{1,0},{2,3},{3,2},{4,5},{5,4},{6,7},{7,6},{8,9},{9,8},{10,11... | collective-permute-start | bytes 373256 | tf_op jit(solution)/shard_map/ppermute | solution.py:483
  10.4 2.5 %collective-permute-start.3 = (bf16[1,2,64,1152]{3,2,1,0:T(8,128)(2,1)}, bf16[1,2,64,1152]{3,2,1,0:T(8,128)(2,1)S(1)}, u32[]{:S(2)}, u32[]{:S(2)}) collective-permute-start(bf16[1,2,64,1152]{3,2,1,0:T(8,128)(2,1)} %get-tuple-element.58), channel_id=1, source_target_pairs={{0,2},{1,3},{2,18},{3,19},{4,0},{5,1},{6,16},{7,17},{8,22},{9,23},... | collective-permute-start | bytes 884744 | tf_op jit(solution)/shard_map/ppermute | solution.py:481
  12.9 1.5 %collective-permute-start.1 = (s32[2,16]{1,0:T(2,128)S(1)}, s32[2,16]{1,0:T(2,128)S(1)}, u32[]{:S(2)}, u32[]{:S(2)}) collective-permute-start(s32[2,16]{1,0:T(2,128)S(1)} %pad_add_fusion), channel_id=1, source_target_pairs={{0,16},{1,17},{2,18},{3,19},{4,20},{5,21},{6,22},{7,23},{8,24},{9,... | collective-permute-start | bytes 392 | tf_op jit(solution)/shard_map/ppermute | solution.py:461
  14.4 1.5 %collective-permute-start.4 = (bf16[1,2,64,1152]{3,2,1,0:T(8,128)(2,1)S(1)}, bf16[1,2,64,1152]{3,2,1,0:T(8,128)(2,1)S(1)}, u32[]{:S(2)}, u32[]{:S(2)}) collective-permute-start(bf16[1,2,64,1152]{3,2,1,0:T(8,128)(2,1)S(1)} %collective-permute-done.2.refs_0_), channel_id=1, source_target_pairs={{0,1},{1,0},{2,3},{3,2},{4,5},{5,4},{6,7},{7,6},{8,9},{9,8},{10,11... | collective-permute-start | bytes 884744 | tf_op jit(solution)/shard_map/ppermute | solution.py:491
  15.9 0.7 collective-permute-done.1
  16.6 0.6 fusion.2.info_ref
  17.2 0.9 broadcast_select_fusion.1
  18.1 6.1 %collective-permute-done.3.refs_1_ = bf16[1,2,64,1152]{3,2,1,0:T(8,128)(2,1)S(1)} collective-permute-done((bf16[1,2,64,1152]{3,2,1,0:T(8,128)(2,1)}, bf16[1,2,64,1152]{3,2,1,0:T(8,128)(2,1)S(1)}, u32[]{:S(2)}, u32[]{:S(2)}) %collective-permute-start.3) | collective-permute-done | bytes 294944 | tf_op jit(solution)/shard_map/ppermute | solution.py:481
  24.2 1.0 collective-permute-start.6
  25.2 0.1 maximum_bitcast_fusion.2
  25.4 4.2 %collective-permute-start.9 = (bf16[1,144,864]{2,1,0:T(8,128)(2,1)S(1)}, bf16[1,144,864]{2,1,0:T(8,128)(2,1)S(1)}, u32[]{:S(2)}, u32[]{:S(2)}) collective-permute-start(bf16[1,144,864]{2,1,0:T(8,128)(2,1)S(1)} %maximum_bitcast_fusion.2), channel_id=1, source_target_pairs={{0,4},{1,5},{2,6},{3,7},{4,0},{5,1},{6,2},{7,3},{8,12},{9,13},{10,... | collective-permute-start | bytes 746504 | tf_op jit(solution)/shard_map/ppermute | solution.py:449
  29.6 0.1 collective-permute-start.5
  29.7 4.4 %collective-permute-done.6 = bf16[1,2,64,1152]{3,2,1,0:T(8,128)(2,1)S(1)} collective-permute-done((bf16[1,2,64,1152]{3,2,1,0:T(8,128)(2,1)S(1)}, bf16[1,2,64,1152]{3,2,1,0:T(8,128)(2,1)S(1)}, u32[]{:S(2)}, u32[]{:S(2)}) %collective-permute-start.6) | collective-permute-done | bytes 294944 | tf_op jit(solution)/shard_map/ppermute | solution.py:449
  34.2 0.1 collective-permute-start.7
  34.3 7.0 %collective-permute-done.9 = bf16[1,144,864]{2,1,0:T(8,128)(2,1)S(1)} collective-permute-done((bf16[1,144,864]{2,1,0:T(8,128)(2,1)S(1)}, bf16[1,144,864]{2,1,0:T(8,128)(2,1)S(1)}, u32[]{:S(2)}, u32[]{:S(2)}) %collective-permute-start.9) | collective-permute-done | bytes 248864 | tf_op jit(solution)/shard_map/ppermute | solution.py:449
  41.3 0.1 pad_maximum_fusion.2.refs_0_
  41.4 0.1 collective-permute-start.10
  41.5 3.8 %collective-permute-start.13 = (bf16[144,1152]{1,0:T(8,128)(2,1)S(1)}, bf16[144,1152]{1,0:T(8,128)(2,1)S(1)}, u32[]{:S(2)}, u32[]{:S(2)}) collective-permute-start(bf16[144,1152]{1,0:T(8,128)(2,1)S(1)} %copy-done.13), channel_id=1, source_target_pairs={{0,0},{1,1},{2,18},{3,19},{4,8},{5,9},{6,26},{7,27},{8,4},{9,5},{1... | collective-permute-start | bytes 995336 | tf_op jit(solution)/shard_map/ppermute | solution.py:496
  45.3 0.4 collective-permute-done.5.refs_1_
  45.7 8.7 %collective-permute-done.10.refs_1_ = bf16[2,144,864]{2,1,0:T(8,128)(2,1)S(1)} collective-permute-done((bf16[2,144,864]{2,1,0:T(8,128)(2,1)S(1)}, bf16[2,144,864]{2,1,0:T(8,128)(2,1)S(1)}, u32[]{:S(2)}, u32[]{:S(2)}) %collective-permute-start.10) | collective-permute-done | bytes 497696 | tf_op jit(solution)/shard_map/ppermute | solution.py:452
  54.4 0.5 collective-permute-start.12
  54.9 0.3 copy-done.9
  55.2 4.4 %prepare.1 = (bf16[8,64,1152]{2,1,0:T(8,128)(2,1)}, bf16[8,64,1152]{2,1,0:T(8,128)(2,1)}) custom-call(s32[4]{0:T(128)} %pad_add_fusion.1.pos_ref, s32[16]{0:T(128)} %fusion.2.info_ref, bf16[2,2,64,1152]{3,2,1,0:T(8,128)(2,1)} %copy-done, bf16[2,2,64,1152]{3,2,1,0:T(8,128)(2,1)} %copy-done.8, bf16[2,2,64,1152]{3,2,1,0:T(8,128)(2,1)} %copy-done.1, ...), custom_call_target="tpu_custom_call" | custom-call | flops 1769472000 | bytes 2359296 | tf_op jit(solution)/shard_map/prepare/pallas_call | solution.py:524
  59.6 0.9 collective-permute-done.13.refs_4_
  60.5 0.9 collective-permute-start.14
  61.3 1.3 collective-permute-done.14.refs_5_
  62.6 0.7 copy-done.15
  63.3 0.3 copy-done.11
  63.6 0.2 copy-done.12
  63.7 11.2 %forward.1 = (bf16[2,8,64,144]{3,2,1,0:T(8,128)(2,1)}, bf16[2,8,64,144]{3,2,1,0:T(8,128)(2,1)}, bf16[2,8,64,144]{3,2,1,0:T(8,128)(2,1)}, bf16[2,8,64,144]{3,2,1,...) custom-call(s32[4]{0:T(128)} %pad_add_fusion.1.pos_ref, ...), custom_call_target="tpu_custom_call" | custom-call | flops 8257536000 | bytes 2359296 | tf_op jit(solution)/shard_map/forward/pallas_call | solution.py:538
  75.0 0.4 collective-permute-start.15
  75.4 1.7 %collective-permute-start.17 = (bf16[2,64,1152]{2,1,0:T(8,128)(2,1)}, bf16[2,64,1152]{2,1,0:T(8,128)(2,1)S(1)}, u32[]{:S(2)}, u32[]{:S(2)}) collective-permute-start(bf16[2,64,1152]{2,1,0:T(8,128)(2,1)} %get-tuple-element.88), channel_id=1, source_target_pairs={{0,1},{1,0},{2,3},{3,2},{4,5},{5,4},{6,7},{7,6},{8,9},{9,8},{10,11... | collective-permute-start | bytes 884744 | tf_op jit(solution)/shard_map/ppermute | solution.py:455
  77.1 2.3 %collective-permute-start.18 = (bf16[2,64,1152]{2,1,0:T(8,128)(2,1)}, bf16[2,64,1152]{2,1,0:T(8,128)(2,1)S(1)}, u32[]{:S(2)}, u32[]{:S(2)}) collective-permute-start(bf16[2,64,1152]{2,1,0:T(8,128)(2,1)} %get-tuple-element.89), channel_id=1, source_target_pairs={{0,16},{1,17},{2,18},{3,19},{4,20},{5,21},{6,22},{7,23},{8,24},{9,... | collective-permute-start | bytes 884744 | tf_op jit(solution)/shard_map/ppermute | solution.py:455
  79.3 0.2 collective-permute-start.19
  79.5 1.2 slice_add_fusion
  80.6 0.1 collective-permute-start.16
  80.7 9.6 %backward.1 = (f32[2,64,1152]{2,1,0:T(8,128)}, bf16[2,64,1152]{2,1,0:T(8,128)(2,1)}, bf16[2,64,1152]{2,1,0:T(8,128)(2,1)}, bf16[2,64,1152]{2,1,0:T(8,128)(2,1)}) custom-call(s32[4]{0:T(128)} %pad_add_fusion.1.pos_ref, s32[16]{0:T(128)} %fusion.2.info_ref, bf16[2,144,864]{2,1,0:T(8,128)(2,1)} %copy-done.2, bf16[2,144,864]{2,1,0:T(8,128)(2,1)} %copy-done.10, ...), custom_call_target="tpu_custom_call" | custom-call | flops 5898240000 | bytes 2359296 | tf_op jit(solution)/shard_map/backward/pallas_call | solution.py:564
  90.3 2.2 %collective-permute-done.18.refs_4_ = bf16[2,64,1152]{2,1,0:T(8,128)(2,1)S(1)} collective-permute-done((bf16[2,64,1152]{2,1,0:T(8,128)(2,1)}, bf16[2,64,1152]{2,1,0:T(8,128)(2,1)S(1)}, u32[]{:S(2)}, u32[]{:S(2)}) %collective-permute-start.18) | collective-permute-done | bytes 294944 | tf_op jit(solution)/shard_map/ppermute | solution.py:455
  92.5 0.8 collective-permute-done.19.refs_5_
  93.3 1.3 collective-permute-start.22
  94.6 1.1 collective-permute-start.23
  95.7 1.1 collective-permute-start.24
  96.8 3.1 %output.1 = (bf16[64,1152]{1,0:T(8,128)(2,1)}, bf16[64,1152]{1,0:T(8,128)(2,1)}) custom-call(s32[4]{0:T(128)} %pad_add_fusion.1.pos_ref, s32[16]{0:T(128)} %fusion.2.info_ref, bf16[1,2,64,1152]{3,2,1,0:T(8,128)(2,1)} %copy-done.3, bf16[1,2,64,1152]{3,2,1,0:T(8,128)(2,1)} %copy-done.4, f32[2,64,1152]{2,1,0:T(8,128)} %get-tuple-element.91.refs_2_, ...), custom_call_target="tpu_custom_call" | custom-call | flops 11796480000 | bytes 2359296 | tf_op jit(solution)/shard_map/output/pallas_call | solution.py:577
  99.9 2.5 %collective-permute-start.20 = (bf16[64,1152]{1,0:T(8,128)(2,1)}, bf16[64,1152]{1,0:T(8,128)(2,1)S(1)}, u32[]{:S(2)}, u32[]{:S(2)}) collective-permute-start(bf16[64,1152]{1,0:T(8,128)(2,1)} %get-tuple-element.95), channel_id=1, source_target_pairs={{0,0},{1,1},{16,2},{17,3},{2,4},{3,5},{18,6},{19,7},{20,8},{21,9},... | collective-permute-start | bytes 442376 | tf_op jit(solution)/shard_map/ppermute | solution.py:442
  102.4 4.5 %collective-permute-start.21 = (bf16[64,1152]{1,0:T(8,128)(2,1)}, bf16[64,1152]{1,0:T(8,128)(2,1)S(1)}, u32[]{:S(2)}, u32[]{:S(2)}) collective-permute-start(bf16[64,1152]{1,0:T(8,128)(2,1)} %get-tuple-element.96), channel_id=1, source_target_pairs={{2,0},{3,1},{18,2},{19,3},{0,4},{1,5},{16,6},{17,7},{22,8},{23,9},... | collective-permute-start | bytes 442376 | tf_op jit(solution)/shard_map/ppermute | solution.py:442
  107.0 0.1 collective-permute-start.27
  107.1 2.7 %collective-permute-done.23.refs_4_ = bf16[2,64,1152]{2,1,0:T(8,128)(2,1)S(1)} collective-permute-done((bf16[2,64,1152]{2,1,0:T(8,128)(2,1)}, bf16[2,64,1152]{2,1,0:T(8,128)(2,1)S(1)}, u32[]{:S(2)}, u32[]{:S(2)}) %collective-permute-start.23) | collective-permute-done | bytes 294944 | tf_op jit(solution)/shard_map/ppermute | solution.py:455
  109.8 0.7 copy-done.20
  110.5 0.7 copy-done.21
  111.2 3.4 %input_grad.1 = (bf16[64,1152]{1,0:T(8,128)(2,1)}, bf16[64,1152]{1,0:T(8,128)(2,1)}) custom-call(s32[4]{0:T(128)} %pad_add_fusion.1.pos_ref, s32[16]{0:T(128)} %fusion.2.info_ref, bf16[1,2,64,1152]{3,2,1,0:T(8,128)(2,1)} %copy-done.3, bf16[1,2,64,1152]{3,2,1,0:T(8,128)(2,1)} %copy-done.4, f32[2,64,1152]{2,1,0:T(8,128)} %get-tuple-element.101.refs_2_, ...), custom_call_target="tpu_custom_call" | custom-call | flops 1769472000 | bytes 2359296 | tf_op jit(solution)/shard_map/input_grad/pallas_call | solution.py:589
  114.6 3.3 %collective-permute-start.25 = (bf16[64,1152]{1,0:T(8,128)(2,1)}, bf16[64,1152]{1,0:T(8,128)(2,1)S(1)}, u32[]{:S(2)}, u32[]{:S(2)}) collective-permute-start(bf16[64,1152]{1,0:T(8,128)(2,1)} %get-tuple-element.105), channel_id=1, source_target_pairs={{0,0},{1,1},{16,2},{17,3},{2,4},{3,5},{18,6},{19,7},{20,8},{21,9},... | collective-permute-start | bytes 442376 | tf_op jit(solution)/shard_map/ppermute | solution.py:442
  117.9 5.1 %collective-permute-start.26 = (bf16[64,1152]{1,0:T(8,128)(2,1)}, bf16[64,1152]{1,0:T(8,128)(2,1)S(1)}, u32[]{:S(2)}, u32[]{:S(2)}) collective-permute-start(bf16[64,1152]{1,0:T(8,128)(2,1)} %get-tuple-element.106), channel_id=1, source_target_pairs={{2,0},{3,1},{18,2},{19,3},{0,4},{1,5},{16,6},{17,7},{22,8},{23,9},... | collective-permute-start | bytes 442376 | tf_op jit(solution)/shard_map/ppermute | solution.py:442
  123.0 1.9 %collective-permute-start.28 = (f32[48,864]{1,0:T(8,128)S(1)}, f32[48,864]{1,0:T(8,128)S(1)}, u32[]{:S(2)}, u32[]{:S(2)}) collective-permute-start(f32[48,864]{1,0:T(8,128)S(1)} %bitcast.28), channel_id=1, source_target_pairs={{0,0},{1,1},{2,8},{3,9},{4,16},{5,17},{6,24},{7,25},{8,4},{9,5},{1... | collective-permute-start | bytes 497672 | tf_op jit(solution)/shard_map/ppermute | solution.py:605
  125.0 1.6 %collective-permute-done.26 = bf16[64,1152]{1,0:T(8,128)(2,1)S(1)} collective-permute-done((bf16[64,1152]{1,0:T(8,128)(2,1)}, bf16[64,1152]{1,0:T(8,128)(2,1)S(1)}, u32[]{:S(2)}, u32[]{:S(2)}) %collective-permute-start.26) | collective-permute-done | bytes 147488 | tf_op jit(solution)/shard_map/ppermute | solution.py:442
  126.7 0.7 maximum_bitcast_fusion.1
  127.4 0.7 maximum_bitcast_fusion
  128.2 5.9 %collective-permute-done.28 = f32[48,864]{1,0:T(8,128)S(1)} collective-permute-done((f32[48,864]{1,0:T(8,128)S(1)}, f32[48,864]{1,0:T(8,128)S(1)}, u32[]{:S(2)}, u32[]{:S(2)}) %collective-permute-start.28) | collective-permute-done | bytes 165920 | tf_op jit(solution)/shard_map/ppermute | solution.py:605
  134.1 0.1 fusion.6
  134.2 0.7 maximum_multiply_fusion
  (62 shorter events, 0.5 us)
Async XLA Ops:
  1.2 5.4 %copy-start.5 = (s32[1,4]{1,0:T(1,128)S(1)}, s32[1,4]{1,0:T(1,128)}, u32[]{:S(2)}) copy-start(s32[1,4]{1,0:T(1,128)} %param.12) | copy-start | bytes 52
  1.3 5.4 %copy-start.6 = (s32[1,4]{1,0:T(1,128)S(1)}, s32[1,4]{1,0:T(1,128)}, u32[]{:S(2)}) copy-start(s32[1,4]{1,0:T(1,128)} %param.11) | copy-start | bytes 52
  1.3 5.4 %copy-start.7 = (s32[1,8]{1,0:T(1,128)S(1)}, s32[1,8]{1,0:T(1,128)}, u32[]{:S(2)}) copy-start(s32[1,8]{1,0:T(1,128)} %param.10) | copy-start | bytes 100
  4.7 9.7 %collective-permute-start.2 = (bf16[1,2,64,1152]{3,2,1,0:T(8,128)(2,1)}, bf16[1,2,64,1152]{3,2,1,0:T(8,128)(2,1)S(1)}, u32[]{:S(2)}, u32[]{:S(2)}) collective-permute-start(bf16[1,2,64,1152]{3,2,1,0:T(8,128)(2,1)} %get-tuple-element.57), channel_id=1, source_target_pairs={{0,0},{1,1},{2,16},{3,17},{4,2},{5,3},{6,18},{7,19},{8,20},{9,21},... | collective-permute-start | bytes 884744 | tf_op jit(solution)/shard_map/ppermute | solution.py:481
  6.7 6.2 %collective-permute-start = (s32[1,16]{1,0:T(1,128)S(1)}, s32[1,16]{1,0:T(1,128)S(1)}, u32[]{:S(2)}, u32[]{:S(2)}) collective-permute-start(s32[1,16]{1,0:T(1,128)S(1)} %fusion.7), channel_id=1, source_target_pairs={{0,8},{1,9},{2,10},{3,11},{4,12},{5,13},{6,14},{7,15},{8,0},{9,1},... | collective-permute-start | bytes 200 | tf_op jit(solution)/shard_map/ppermute | solution.py:459
  8.9 8.3 %collective-permute-start.8 = (bf16[144,432]{1,0:T(8,128)(2,1)}, bf16[144,432]{1,0:T(8,128)(2,1)S(1)}, u32[]{:S(2)}, u32[]{:S(2)}) collective-permute-start(bf16[144,432]{1,0:T(8,128)(2,1)} %get-tuple-element.63), channel_id=1, source_target_pairs={{0,1},{1,0},{2,3},{3,2},{4,5},{5,4},{6,7},{7,6},{8,9},{9,8},{10,11... | collective-permute-start | bytes 373256 | tf_op jit(solution)/shard_map/ppermute | solution.py:483
  10.4 13.9 %collective-permute-start.3 = (bf16[1,2,64,1152]{3,2,1,0:T(8,128)(2,1)}, bf16[1,2,64,1152]{3,2,1,0:T(8,128)(2,1)S(1)}, u32[]{:S(2)}, u32[]{:S(2)}) collective-permute-start(bf16[1,2,64,1152]{3,2,1,0:T(8,128)(2,1)} %get-tuple-element.58), channel_id=1, source_target_pairs={{0,2},{1,3},{2,18},{3,19},{4,0},{5,1},{6,16},{7,17},{8,22},{9,23},... | collective-permute-start | bytes 884744 | tf_op jit(solution)/shard_map/ppermute | solution.py:481
  12.9 3.6 %collective-permute-start.1 = (s32[2,16]{1,0:T(2,128)S(1)}, s32[2,16]{1,0:T(2,128)S(1)}, u32[]{:S(2)}, u32[]{:S(2)}) collective-permute-start(s32[2,16]{1,0:T(2,128)S(1)} %pad_add_fusion), channel_id=1, source_target_pairs={{0,16},{1,17},{2,18},{3,19},{4,20},{5,21},{6,22},{7,23},{8,24},{9,... | collective-permute-start | bytes 392 | tf_op jit(solution)/shard_map/ppermute | solution.py:461
  14.4 19.7 %copy-start.3 = (bf16[1,2,64,1152]{3,2,1,0:T(8,128)(2,1)}, bf16[1,2,64,1152]{3,2,1,0:T(8,128)(2,1)S(1)}, u32[]{:S(2)}) copy-start(bf16[1,2,64,1152]{3,2,1,0:T(8,128)(2,1)S(1)} %collective-permute-done.2.refs_0_) | copy-start | bytes 884740
  14.4 9.8 %collective-permute-start.4 = (bf16[1,2,64,1152]{3,2,1,0:T(8,128)(2,1)S(1)}, bf16[1,2,64,1152]{3,2,1,0:T(8,128)(2,1)S(1)}, u32[]{:S(2)}, u32[]{:S(2)}) collective-permute-start(bf16[1,2,64,1152]{3,2,1,0:T(8,128)(2,1)S(1)} %collective-permute-done.2.refs_0_), channel_id=1, source_target_pairs={{0,1},{1,0},{2,3},{3,2},{4,5},{5,4},{6,7},{7,6},{8,9},{9,8},{10,11... | collective-permute-start | bytes 884744 | tf_op jit(solution)/shard_map/ppermute | solution.py:491
  24.2 10.0 %copy-start.4 = (bf16[1,2,64,1152]{3,2,1,0:T(8,128)(2,1)}, bf16[1,2,64,1152]{3,2,1,0:T(8,128)(2,1)S(1)}, u32[]{:S(2)}) copy-start(bf16[1,2,64,1152]{3,2,1,0:T(8,128)(2,1)S(1)} %collective-permute-done.3.refs_1_) | copy-start | bytes 884740
  24.2 9.9 %collective-permute-start.6 = (bf16[1,2,64,1152]{3,2,1,0:T(8,128)(2,1)S(1)}, bf16[1,2,64,1152]{3,2,1,0:T(8,128)(2,1)S(1)}, u32[]{:S(2)}, u32[]{:S(2)}) collective-permute-start(bf16[1,2,64,1152]{3,2,1,0:T(8,128)(2,1)S(1)} %collective-permute-done.3.refs_1_), channel_id=1, source_target_pairs={{0,16},{1,17},{2,18},{3,19},{4,20},{5,21},{6,22},{7,23},{8,24},{9,... | collective-permute-start | bytes 884744 | tf_op jit(solution)/shard_map/ppermute | solution.py:449
  25.4 15.9 %collective-permute-start.9 = (bf16[1,144,864]{2,1,0:T(8,128)(2,1)S(1)}, bf16[1,144,864]{2,1,0:T(8,128)(2,1)S(1)}, u32[]{:S(2)}, u32[]{:S(2)}) collective-permute-start(bf16[1,144,864]{2,1,0:T(8,128)(2,1)S(1)} %maximum_bitcast_fusion.2), channel_id=1, source_target_pairs={{0,4},{1,5},{2,6},{3,7},{4,0},{5,1},{6,2},{7,3},{8,12},{9,13},{10,... | collective-permute-start | bytes 746504 | tf_op jit(solution)/shard_map/ppermute | solution.py:449
  29.6 25.3 %copy-start = (bf16[2,2,64,1152]{3,2,1,0:T(8,128)(2,1)}, bf16[2,2,64,1152]{3,2,1,0:T(8,128)(2,1)S(1)}, u32[]{:S(2)}) copy-start(bf16[2,2,64,1152]{3,2,1,0:T(8,128)(2,1)S(1)} %pad_maximum_fusion.refs_0_) | copy-start | bytes 1769476
  29.6 11.8 %copy-start.13 = (bf16[144,1152]{1,0:T(8,128)(2,1)S(1)}, bf16[144,1152]{1,0:T(8,128)(2,1)}, u32[]{:S(2)}) copy-start(bf16[144,1152]{1,0:T(8,128)(2,1)} %param.15) | copy-start | bytes 995332
  29.6 16.0 %collective-permute-start.5 = (bf16[2,2,64,1152]{3,2,1,0:T(8,128)(2,1)S(1)}, bf16[2,2,64,1152]{3,2,1,0:T(8,128)(2,1)S(1)}, u32[]{:S(2)}, u32[]{:S(2)}) collective-permute-start(bf16[2,2,64,1152]{3,2,1,0:T(8,128)(2,1)S(1)} %pad_maximum_fusion.refs_0_), channel_id=1, source_target_pairs={{0,16},{1,17},{2,18},{3,19},{4,20},{5,21},{6,22},{7,23},{8,24},{9,... | collective-permute-start | bytes 1769480 | tf_op jit(solution)/shard_map/ppermute | solution.py:452
  34.2 20.8 %copy-start.1 = (bf16[2,2,64,1152]{3,2,1,0:T(8,128)(2,1)}, bf16[2,2,64,1152]{3,2,1,0:T(8,128)(2,1)S(1)}, u32[]{:S(2)}) copy-start(bf16[2,2,64,1152]{3,2,1,0:T(8,128)(2,1)S(1)} %pad_maximum_fusion.1.refs_2_) | copy-start | bytes 1769476
  34.2 20.2 %collective-permute-start.7 = (bf16[2,2,64,1152]{3,2,1,0:T(8,128)(2,1)S(1)}, bf16[2,2,64,1152]{3,2,1,0:T(8,128)(2,1)S(1)}, u32[]{:S(2)}, u32[]{:S(2)}) collective-permute-start(bf16[2,2,64,1152]{3,2,1,0:T(8,128)(2,1)S(1)} %pad_maximum_fusion.1.refs_2_), channel_id=1, source_target_pairs={{0,1},{1,0},{2,3},{3,2},{4,5},{5,4},{6,7},{7,6},{8,9},{9,8},{10,11... | collective-permute-start | bytes 1769480 | tf_op jit(solution)/shard_map/ppermute | solution.py:452
  41.4 18.3 %copy-start.2 = (bf16[2,144,864]{2,1,0:T(8,128)(2,1)}, bf16[2,144,864]{2,1,0:T(8,128)(2,1)S(1)}, u32[]{:S(2)}) copy-start(bf16[2,144,864]{2,1,0:T(8,128)(2,1)S(1)} %pad_maximum_fusion.2.refs_0_) | copy-start | bytes 1492996
  41.4 13.0 %collective-permute-start.10 = (bf16[2,144,864]{2,1,0:T(8,128)(2,1)S(1)}, bf16[2,144,864]{2,1,0:T(8,128)(2,1)S(1)}, u32[]{:S(2)}, u32[]{:S(2)}) collective-permute-start(bf16[2,144,864]{2,1,0:T(8,128)(2,1)S(1)} %pad_maximum_fusion.2.refs_0_), channel_id=1, source_target_pairs={{0,2},{1,3},{2,0},{3,1},{4,6},{5,7},{6,4},{7,5},{8,10},{9,11},{10,... | collective-permute-start | bytes 1493000 | tf_op jit(solution)/shard_map/ppermute | solution.py:452
  41.5 19.0 %collective-permute-start.13 = (bf16[144,1152]{1,0:T(8,128)(2,1)S(1)}, bf16[144,1152]{1,0:T(8,128)(2,1)S(1)}, u32[]{:S(2)}, u32[]{:S(2)}) collective-permute-start(bf16[144,1152]{1,0:T(8,128)(2,1)S(1)} %copy-done.13), channel_id=1, source_target_pairs={{0,0},{1,1},{2,18},{3,19},{4,8},{5,9},{6,26},{7,27},{8,4},{9,5},{1... | collective-permute-start | bytes 995336 | tf_op jit(solution)/shard_map/ppermute | solution.py:496
  45.7 9.3 %copy-start.8 = (bf16[2,2,64,1152]{3,2,1,0:T(8,128)(2,1)}, bf16[2,2,64,1152]{3,2,1,0:T(8,128)(2,1)S(1)}, u32[]{:S(2)}) copy-start(bf16[2,2,64,1152]{3,2,1,0:T(8,128)(2,1)S(1)} %collective-permute-done.5.refs_1_) | copy-start | bytes 1769476
  54.4 8.3 %copy-start.10 = (bf16[2,144,864]{2,1,0:T(8,128)(2,1)}, bf16[2,144,864]{2,1,0:T(8,128)(2,1)S(1)}, u32[]{:S(2)}) copy-start(bf16[2,144,864]{2,1,0:T(8,128)(2,1)S(1)} %collective-permute-done.10.refs_1_) | copy-start | bytes 1492996
  54.4 0.9 copy-start.9
  54.4 8.2 %collective-permute-start.11 = (bf16[2,144,864]{2,1,0:T(8,128)(2,1)S(1)}, bf16[2,144,864]{2,1,0:T(8,128)(2,1)S(1)}, u32[]{:S(2)}, u32[]{:S(2)}) collective-permute-start(bf16[2,144,864]{2,1,0:T(8,128)(2,1)S(1)} %pad_maximum_fusion.2.refs_0_), channel_id=1, source_target_pairs={{0,8},{1,9},{2,10},{3,11},{4,12},{5,13},{6,14},{7,15},{8,0},{9,1},... | collective-permute-start | bytes 1493000 | tf_op jit(solution)/shard_map/ppermute | solution.py:504
  54.4 8.2 %collective-permute-start.12 = (bf16[2,144,864]{2,1,0:T(8,128)(2,1)S(1)}, bf16[2,144,864]{2,1,0:T(8,128)(2,1)S(1)}, u32[]{:S(2)}, u32[]{:S(2)}) collective-permute-start(bf16[2,144,864]{2,1,0:T(8,128)(2,1)S(1)} %collective-permute-done.10.refs_1_), channel_id=1, source_target_pairs={{0,8},{1,9},{2,10},{3,11},{4,12},{5,13},{6,14},{7,15},{8,0},{9,1},... | collective-permute-start | bytes 1493000 | tf_op jit(solution)/shard_map/ppermute | solution.py:504
  60.5 2.2 %copy-start.14 = (bf16[144,1152]{1,0:T(8,128)(2,1)}, bf16[144,1152]{1,0:T(8,128)(2,1)S(1)}, u32[]{:S(2)}) copy-start(bf16[144,1152]{1,0:T(8,128)(2,1)S(1)} %collective-permute-done.13.refs_4_) | copy-start | bytes 995332
  60.5 2.1 %collective-permute-start.14 = (bf16[144,1152]{1,0:T(8,128)(2,1)S(1)}, bf16[144,1152]{1,0:T(8,128)(2,1)S(1)}, u32[]{:S(2)}, u32[]{:S(2)}) collective-permute-start(bf16[144,1152]{1,0:T(8,128)(2,1)S(1)} %collective-permute-done.13.refs_4_), channel_id=1, source_target_pairs={{0,8},{1,9},{2,10},{3,11},{4,12},{5,13},{6,14},{7,15},{8,0},{9,1},... | collective-permute-start | bytes 995336 | tf_op jit(solution)/shard_map/ppermute | solution.py:534
  62.6 0.7 copy-start.15
  62.6 1.0 copy-start.11
  62.6 1.1 copy-start.12
  75.0 4.5 %collective-permute-start.15 = (f32[4,48,864]{2,1,0:T(8,128)}, f32[4,48,864]{2,1,0:T(8,128)S(1)}, u32[]{:S(2)}, u32[]{:S(2)}) collective-permute-start(f32[4,48,864]{2,1,0:T(8,128)} %get-tuple-element.80), channel_id=1, source_target_pairs={{0,8},{1,9},{2,10},{3,11},{4,12},{5,13},{6,14},{7,15},{8,0},{9,1},... | collective-permute-start | bytes 1990664 | tf_op jit(solution)/shard_map/ppermute | solution.py:556
  75.4 14.9 %collective-permute-start.17 = (bf16[2,64,1152]{2,1,0:T(8,128)(2,1)}, bf16[2,64,1152]{2,1,0:T(8,128)(2,1)S(1)}, u32[]{:S(2)}, u32[]{:S(2)}) collective-permute-start(bf16[2,64,1152]{2,1,0:T(8,128)(2,1)} %get-tuple-element.88), channel_id=1, source_target_pairs={{0,1},{1,0},{2,3},{3,2},{4,5},{5,4},{6,7},{7,6},{8,9},{9,8},{10,11... | collective-permute-start | bytes 884744 | tf_op jit(solution)/shard_map/ppermute | solution.py:455
  77.1 15.4 %collective-permute-start.18 = (bf16[2,64,1152]{2,1,0:T(8,128)(2,1)}, bf16[2,64,1152]{2,1,0:T(8,128)(2,1)S(1)}, u32[]{:S(2)}, u32[]{:S(2)}) collective-permute-start(bf16[2,64,1152]{2,1,0:T(8,128)(2,1)} %get-tuple-element.89), channel_id=1, source_target_pairs={{0,16},{1,17},{2,18},{3,19},{4,20},{5,21},{6,22},{7,23},{8,24},{9,... | collective-permute-start | bytes 884744 | tf_op jit(solution)/shard_map/ppermute | solution.py:455
  79.3 13.9 %collective-permute-start.19 = (bf16[2,64,1152]{2,1,0:T(8,128)(2,1)}, bf16[2,64,1152]{2,1,0:T(8,128)(2,1)S(1)}, u32[]{:S(2)}, u32[]{:S(2)}) collective-permute-start(bf16[2,64,1152]{2,1,0:T(8,128)(2,1)} %get-tuple-element.90), channel_id=1, source_target_pairs={{0,17},{1,16},{2,19},{3,18},{4,21},{5,20},{6,23},{7,22},{8,25},{9,... | collective-permute-start | bytes 884744 | tf_op jit(solution)/shard_map/ppermute | solution.py:455
  80.6 12.6 %collective-permute-start.16 = (f32[2,48,864]{2,1,0:T(8,128)S(1)}, f32[2,48,864]{2,1,0:T(8,128)S(1)}, u32[]{:S(2)}, u32[]{:S(2)}) collective-permute-start(f32[2,48,864]{2,1,0:T(8,128)S(1)} %get-tuple-element.86), channel_id=1, source_target_pairs={{0,2},{1,3},{2,0},{3,1},{4,6},{5,7},{6,4},{7,5},{8,10},{9,11},{10,... | collective-permute-start | bytes 995336 | tf_op jit(solution)/shard_map/ppermute | solution.py:562
  90.3 6.5 %copy-start.16 = (bf16[2,64,1152]{2,1,0:T(8,128)(2,1)}, bf16[2,64,1152]{2,1,0:T(8,128)(2,1)S(1)}, u32[]{:S(2)}) copy-start(bf16[2,64,1152]{2,1,0:T(8,128)(2,1)S(1)} %collective-permute-done.17.refs_3_) | copy-start | bytes 884740
  92.5 4.3 %copy-start.17 = (bf16[2,64,1152]{2,1,0:T(8,128)(2,1)}, bf16[2,64,1152]{2,1,0:T(8,128)(2,1)S(1)}, u32[]{:S(2)}) copy-start(bf16[2,64,1152]{2,1,0:T(8,128)(2,1)S(1)} %collective-permute-done.18.refs_4_) | copy-start | bytes 884740
  93.3 3.5 %copy-start.18 = (bf16[2,64,1152]{2,1,0:T(8,128)(2,1)}, bf16[2,64,1152]{2,1,0:T(8,128)(2,1)S(1)}, u32[]{:S(2)}) copy-start(bf16[2,64,1152]{2,1,0:T(8,128)(2,1)S(1)} %collective-permute-done.19.refs_5_) | copy-start | bytes 884740
  93.3 13.7 %collective-permute-start.22 = (bf16[2,64,1152]{2,1,0:T(8,128)(2,1)}, bf16[2,64,1152]{2,1,0:T(8,128)(2,1)S(1)}, u32[]{:S(2)}, u32[]{:S(2)}) collective-permute-start(bf16[2,64,1152]{2,1,0:T(8,128)(2,1)} %get-tuple-element.98), channel_id=1, source_target_pairs={{0,1},{1,0},{2,3},{3,2},{4,5},{5,4},{6,7},{7,6},{8,9},{9,8},{10,11... | collective-permute-start | bytes 884744 | tf_op jit(solution)/shard_map/ppermute | solution.py:455
  94.6 15.2 %collective-permute-start.23 = (bf16[2,64,1152]{2,1,0:T(8,128)(2,1)}, bf16[2,64,1152]{2,1,0:T(8,128)(2,1)S(1)}, u32[]{:S(2)}, u32[]{:S(2)}) collective-permute-start(bf16[2,64,1152]{2,1,0:T(8,128)(2,1)} %get-tuple-element.99), channel_id=1, source_target_pairs={{0,16},{1,17},{2,18},{3,19},{4,20},{5,21},{6,22},{7,23},{8,24},{9,... | collective-permute-start | bytes 884744 | tf_op jit(solution)/shard_map/ppermute | solution.py:455
  95.7 14.1 %collective-permute-start.24 = (bf16[2,64,1152]{2,1,0:T(8,128)(2,1)}, bf16[2,64,1152]{2,1,0:T(8,128)(2,1)S(1)}, u32[]{:S(2)}, u32[]{:S(2)}) collective-permute-start(bf16[2,64,1152]{2,1,0:T(8,128)(2,1)} %get-tuple-element.100), channel_id=1, source_target_pairs={{0,17},{1,16},{2,19},{3,18},{4,21},{5,20},{6,23},{7,22},{8,25},{9,... | collective-permute-start | bytes 884744 | tf_op jit(solution)/shard_map/ppermute | solution.py:455
  99.9 25.1 %collective-permute-start.20 = (bf16[64,1152]{1,0:T(8,128)(2,1)}, bf16[64,1152]{1,0:T(8,128)(2,1)S(1)}, u32[]{:S(2)}, u32[]{:S(2)}) collective-permute-start(bf16[64,1152]{1,0:T(8,128)(2,1)} %get-tuple-element.95), channel_id=1, source_target_pairs={{0,0},{1,1},{16,2},{17,3},{2,4},{3,5},{18,6},{19,7},{20,8},{21,9},... | collective-permute-start | bytes 442376 | tf_op jit(solution)/shard_map/ppermute | solution.py:442
  102.4 22.6 %collective-permute-start.21 = (bf16[64,1152]{1,0:T(8,128)(2,1)}, bf16[64,1152]{1,0:T(8,128)(2,1)S(1)}, u32[]{:S(2)}, u32[]{:S(2)}) collective-permute-start(bf16[64,1152]{1,0:T(8,128)(2,1)} %get-tuple-element.96), channel_id=1, source_target_pairs={{2,0},{3,1},{18,2},{19,3},{0,4},{1,5},{16,6},{17,7},{22,8},{23,9},... | collective-permute-start | bytes 442376 | tf_op jit(solution)/shard_map/ppermute | solution.py:442
  107.0 2.8 %copy-start.19 = (bf16[2,64,1152]{2,1,0:T(8,128)(2,1)}, bf16[2,64,1152]{2,1,0:T(8,128)(2,1)S(1)}, u32[]{:S(2)}) copy-start(bf16[2,64,1152]{2,1,0:T(8,128)(2,1)S(1)} %collective-permute-done.22.refs_3_) | copy-start | bytes 884740
  107.0 16.0 %collective-permute-start.27 = (f32[1,48,864]{2,1,0:T(8,128)S(1)}, f32[1,48,864]{2,1,0:T(8,128)S(1)}, u32[]{:S(2)}, u32[]{:S(2)}) collective-permute-start(f32[1,48,864]{2,1,0:T(8,128)S(1)} %slice.40), channel_id=1, source_target_pairs={{0,4},{1,5},{2,6},{3,7},{4,0},{5,1},{6,2},{7,3},{8,12},{9,13},{10,... | collective-permute-start | bytes 497672 | tf_op jit(solution)/shard_map/ppermute | solution.py:603
  109.8 0.7 copy-start.20
  110.5 0.7 copy-start.21
  114.6 10.4 %collective-permute-start.25 = (bf16[64,1152]{1,0:T(8,128)(2,1)}, bf16[64,1152]{1,0:T(8,128)(2,1)S(1)}, u32[]{:S(2)}, u32[]{:S(2)}) collective-permute-start(bf16[64,1152]{1,0:T(8,128)(2,1)} %get-tuple-element.105), channel_id=1, source_target_pairs={{0,0},{1,1},{16,2},{17,3},{2,4},{3,5},{18,6},{19,7},{20,8},{21,9},... | collective-permute-start | bytes 442376 | tf_op jit(solution)/shard_map/ppermute | solution.py:442
  117.9 8.7 %collective-permute-start.26 = (bf16[64,1152]{1,0:T(8,128)(2,1)}, bf16[64,1152]{1,0:T(8,128)(2,1)S(1)}, u32[]{:S(2)}, u32[]{:S(2)}) collective-permute-start(bf16[64,1152]{1,0:T(8,128)(2,1)} %get-tuple-element.106), channel_id=1, source_target_pairs={{2,0},{3,1},{18,2},{19,3},{0,4},{1,5},{16,6},{17,7},{22,8},{23,9},... | collective-permute-start | bytes 442376 | tf_op jit(solution)/shard_map/ppermute | solution.py:442
  123.0 11.0 %collective-permute-start.28 = (f32[48,864]{1,0:T(8,128)S(1)}, f32[48,864]{1,0:T(8,128)S(1)}, u32[]{:S(2)}, u32[]{:S(2)}) collective-permute-start(f32[48,864]{1,0:T(8,128)S(1)} %bitcast.28), channel_id=1, source_target_pairs={{0,0},{1,1},{2,8},{3,9},{4,16},{5,17},{6,24},{7,25},{8,4},{9,5},{1... | collective-permute-start | bytes 497672 | tf_op jit(solution)/shard_map/ppermute | solution.py:605

commit v15 on v14

--- a/solution.py
+++ b/solution.py
@@ -12,7 +12,7 @@
 CORES = 2
 AXES = ("y", "c", "z", "x")
 BLOCK = 16
-VMEM_LIMIT = 56 * 1024 * 1024
+VMEM_LIMIT = 64 * 1024 * 1024 - 65536
 BF16 = jnp.bfloat16
 F32 = jnp.float32
 
@@ -344,13 +344,12 @@
             grads = jnp.concatenate([grad_queries, grad_keys, grad_values], axis=1).astype(BF16)
             gt_scr[h, :, b * BLOCK : (b + 1) * BLOCK, :] = grads.reshape(frames, BLOCK, 3 * cols)
 
-    rows = lay.nc * step_patches
+    total = jnp.zeros((frames * step_patches, model), F32)
+    for h in range(lay.halves):
+        total = total + dot_t(gt_scr[h].reshape(frames * step_patches, 3 * cols), w_scr[h])
+    total = total.reshape(lay.chips, lay.nc, step_patches, model)
     for k in range(lay.chips):
-        total = jnp.zeros((rows, model), F32)
-        for h in range(lay.halves):
-            part = gt_scr[h, k * lay.nc : (k + 1) * lay.nc].reshape(rows, 3 * cols)
-            total = total + dot_t(part, w_scr[h])
-        gh_refs[k][...] = total.reshape(gh_refs[k].shape).astype(gh_refs[k].dtype)
+        gh_refs[k][...] = total[k].astype(gh_refs[k].dtype)
 
 
 def output_kernel(lay, pos_ref, info_ref, *refs):
@@ -525,10 +524,10 @@
         functools.partial(prepare_kernel, lay),
         "prepare",
         3 * model * 1000,
-        [pair_spec(chips // 2, few)] * (2 * nc) + [mod_spec],
-        [spread(lay.frames, model, few)] * 2,
+        [pair_spec(chips // 2, BLOCK)] * (2 * nc) + [mod_spec],
+        [spread(lay.frames, model, BLOCK)] * 2,
         [struct((lay.frames, half, model))] * 2,
-        grid=(few_steps,),
+        grid=(half // BLOCK,),
     )(pos, info, *pairs, mod_table)
     wo_own, _ = lax.optimization_barrier((wo_own, hidden))
     wo_rows = [wo_own, lax.ppermute(wo_own, AXES, lay.swap(kc=1))]

time: 135 us -> 137 us (1.015)
  other arithmetic: 5.98 us -> 12.2 us
  waiting for transfers between devices: 42.6 us -> 37.1 us
  starting transfers between devices: 47.1 us -> 49 us
    ppermute x6, waiting for transfers between devices: 5.68 us -> 3.23 us  [over_chips(): got = [lax.ppermute(parts[k], AXES, chip_swap(k)) for k in range(1, chips)]]
    ppermute x4, starting transfers between devices: 15.4 us -> 17.1 us  [from_plane(): lax.ppermute(part, AXES, lay.from_plane(k))]
    unnamed x44 -> x14, local copies, waits for them, and re-layouts: 2.85 us -> 1.48 us
  transfers between devices with their start and end apart: 29 -> 29, of which waited for: 13 -> 10; matrix products, arithmetic and copies ran while one was open for 3% -> 8% of each run, Pallas kernels for 15% -> 15%
where the time goes in v15:
time: 137 us; the launch traced here: 136 us
  starting transfers between devices  49 us (36%)
  waiting for transfers between devices  37.1 us (27%)
  Pallas kernels  35.1 us (26%)
  other arithmetic  12.2 us (9%)
  local copies, waits for them, and re-layouts  2.26 us (2%)
    ppermute x4, starting transfers between devices, from_plane(): lax.ppermute(part, AXES, lay.from_plane(k))  17.1 us
    pallas_call x1, Pallas kernels, local(): call(functools.partial(forward_kernel, lay), 'forward', 14 * model * 1000...  11.3 us
    ppermute x2, waiting for transfers between devices, doubling(): got = lax.ppermute(held, AXES, swap(bit)) if first is None else first  10.6 us
    ppermute x6, starting transfers between devices, over_chips(): got = [lax.ppermute(parts[k], AXES, chip_swap(k)) for k in range(1, chips)]  8.59 us
    ppermute x3, waiting for transfers between devices, doubling(): return [held, lax.ppermute(held, AXES, swap(bits[-1]))]  8.45 us
    pallas_call x1, Pallas kernels, local(): call(functools.partial(backward_kernel, lay), 'backward', 10 * model * 10...  8.41 us
    ppermute x1, waiting for transfers between devices, local(): grad_w = lax.ppermute(cut[0], AXES, lay.to_owner())  5.92 us
    pallas_call x1, Pallas kernels, local(): call(functools.partial(prepare_kernel, lay), 'prepare', 3 * model * 1000,...  5.51 us
  transfers between devices with their start and end apart: 29, of which 10 were waited for; matrix products, arithmetic and copies ran while one was open for 8% of the time, Pallas kernels for 15%

profile of v15, /device:TPU:4, one launch (start us, length us, event | category | flops | bytes accessed | tf_op | source)
XLA Modules:
  0.0 136.5 jit_solution(12222782861335609539)
XLA Ops:
  0.6 0.7 pad_add_fusion.1.pos_ref
  1.3 3.3 %start.1 = (bf16[1,2,64,1152]{3,2,1,0:T(8,128)(2,1)}, bf16[1,2,64,1152]{3,2,1,0:T(8,128)(2,1)}, bf16[144,432]{1,0:T(8,128)(2,1)}, bf16[144,432]{1,0:T(8,128)(2,1)}) custom-call(s32[4]{0:T(128)} %pad_add_fusion.1.pos_ref, bf16[1,128,1152]{2,1,0:T(8,128)(2,1)} %x_ref.1, bf16[1,128,1152]{2,1,0:T(8,128)(2,1)} %g_ref.1, bf16[144,3456]{1,0:T(8,128)(2,1)} %w_ref.1), custom_call_target="tpu_custom_call" | custom-call | flops 1179648000 | bytes 2359296 | tf_op jit(solution)/shard_map/start/pallas_call | solution.py:470
  4.6 1.9 %collective-permute-start.2 = (bf16[1,2,64,1152]{3,2,1,0:T(8,128)(2,1)}, bf16[1,2,64,1152]{3,2,1,0:T(8,128)(2,1)S(1)}, u32[]{:S(2)}, u32[]{:S(2)}) collective-permute-start(bf16[1,2,64,1152]{3,2,1,0:T(8,128)(2,1)} %get-tuple-element.57), channel_id=1, source_target_pairs={{0,0},{1,1},{2,16},{3,17},{4,2},{5,3},{6,18},{7,19},{8,20},{9,21},... | collective-permute-start | bytes 884744 | tf_op jit(solution)/shard_map/ppermute | solution.py:480
  6.5 0.8 fusion.7
  7.3 2.2 %collective-permute-start = (s32[1,16]{1,0:T(1,128)S(1)}, s32[1,16]{1,0:T(1,128)S(1)}, u32[]{:S(2)}, u32[]{:S(2)}) collective-permute-start(s32[1,16]{1,0:T(1,128)S(1)} %fusion.7), channel_id=1, source_target_pairs={{0,8},{1,9},{2,10},{3,11},{4,12},{5,13},{6,14},{7,15},{8,0},{9,1},... | collective-permute-start | bytes 200 | tf_op jit(solution)/shard_map/ppermute | solution.py:458
  9.4 1.5 %collective-permute-start.8 = (bf16[144,432]{1,0:T(8,128)(2,1)}, bf16[144,432]{1,0:T(8,128)(2,1)S(1)}, u32[]{:S(2)}, u32[]{:S(2)}) collective-permute-start(bf16[144,432]{1,0:T(8,128)(2,1)} %get-tuple-element.63), channel_id=1, source_target_pairs={{0,1},{1,0},{2,3},{3,2},{4,5},{5,4},{6,7},{7,6},{8,9},{9,8},{10,11... | collective-permute-start | bytes 373256 | tf_op jit(solution)/shard_map/ppermute | solution.py:482
  10.9 2.5 %collective-permute-start.3 = (bf16[1,2,64,1152]{3,2,1,0:T(8,128)(2,1)}, bf16[1,2,64,1152]{3,2,1,0:T(8,128)(2,1)S(1)}, u32[]{:S(2)}, u32[]{:S(2)}) collective-permute-start(bf16[1,2,64,1152]{3,2,1,0:T(8,128)(2,1)} %get-tuple-element.58), channel_id=1, source_target_pairs={{0,2},{1,3},{2,18},{3,19},{4,0},{5,1},{6,16},{7,17},{8,22},{9,23},... | collective-permute-start | bytes 884744 | tf_op jit(solution)/shard_map/ppermute | solution.py:480
  13.5 0.0 collective-permute-done
  13.5 1.5 %collective-permute-start.1 = (s32[2,16]{1,0:T(2,128)S(1)}, s32[2,16]{1,0:T(2,128)S(1)}, u32[]{:S(2)}, u32[]{:S(2)}) collective-permute-start(s32[2,16]{1,0:T(2,128)S(1)} %pad_add_fusion), channel_id=1, source_target_pairs={{0,16},{1,17},{2,18},{3,19},{4,20},{5,21},{6,22},{7,23},{8,24},{9,... | collective-permute-start | bytes 392 | tf_op jit(solution)/shard_map/ppermute | solution.py:460
  15.0 0.8 collective-permute-start.4
  15.8 1.3 collective-permute-done.1
  17.1 1.3 fusion.2.info_ref
  18.5 0.0 collective-permute-done.8
  18.5 0.9 broadcast_select_fusion.1
  19.4 5.4 %collective-permute-done.3.refs_1_ = bf16[1,2,64,1152]{3,2,1,0:T(8,128)(2,1)S(1)} collective-permute-done((bf16[1,2,64,1152]{3,2,1,0:T(8,128)(2,1)}, bf16[1,2,64,1152]{3,2,1,0:T(8,128)(2,1)S(1)}, u32[]{:S(2)}, u32[]{:S(2)}) %collective-permute-start.3) | collective-permute-done | bytes 294944 | tf_op jit(solution)/shard_map/ppermute | solution.py:480
  24.8 1.0 collective-permute-start.6
  25.8 0.1 maximum_bitcast_fusion.2
  25.9 2.9 %collective-permute-start.9 = (bf16[1,144,864]{2,1,0:T(8,128)(2,1)S(1)}, bf16[1,144,864]{2,1,0:T(8,128)(2,1)S(1)}, u32[]{:S(2)}, u32[]{:S(2)}) collective-permute-start(bf16[1,144,864]{2,1,0:T(8,128)(2,1)S(1)} %maximum_bitcast_fusion.2), channel_id=1, source_target_pairs={{0,4},{1,5},{2,6},{3,7},{4,0},{5,1},{6,2},{7,3},{8,12},{9,13},{10,... | collective-permute-start | bytes 746504 | tf_op jit(solution)/shard_map/ppermute | solution.py:448
  28.9 0.1 pad_maximum_fusion.refs_0_
  28.9 0.1 collective-permute-start.5
  29.0 5.7 %collective-permute-done.6 = bf16[1,2,64,1152]{3,2,1,0:T(8,128)(2,1)S(1)} collective-permute-done((bf16[1,2,64,1152]{3,2,1,0:T(8,128)(2,1)S(1)}, bf16[1,2,64,1152]{3,2,1,0:T(8,128)(2,1)S(1)}, u32[]{:S(2)}, u32[]{:S(2)}) %collective-permute-start.6) | collective-permute-done | bytes 294944 | tf_op jit(solution)/shard_map/ppermute | solution.py:448
  34.7 0.1 pad_maximum_fusion.1.refs_2_
  34.8 0.6 collective-permute-start.7
  35.4 4.9 %collective-permute-done.9 = bf16[1,144,864]{2,1,0:T(8,128)(2,1)S(1)} collective-permute-done((bf16[1,144,864]{2,1,0:T(8,128)(2,1)S(1)}, bf16[1,144,864]{2,1,0:T(8,128)(2,1)S(1)}, u32[]{:S(2)}, u32[]{:S(2)}) %collective-permute-start.9) | collective-permute-done | bytes 248864 | tf_op jit(solution)/shard_map/ppermute | solution.py:448
  40.3 0.9 pad_maximum_fusion.2.refs_0_
  41.2 4.4 %collective-permute-start.13 = (bf16[144,1152]{1,0:T(8,128)(2,1)}, bf16[144,1152]{1,0:T(8,128)(2,1)}, u32[]{:S(2)}, u32[]{:S(2)}) collective-permute-start(bf16[144,1152]{1,0:T(8,128)(2,1)} %param.15), channel_id=1, source_target_pairs={{0,0},{1,1},{2,18},{3,19},{4,8},{5,9},{6,26},{7,27},{8,4},{9,5},{1... | collective-permute-start | bytes 995336 | tf_op jit(solution)/shard_map/ppermute | solution.py:495
  45.6 0.7 collective-permute-done.5.refs_1_
  46.2 7.8 %collective-permute-done.10.refs_1_ = bf16[2,144,864]{2,1,0:T(8,128)(2,1)} collective-permute-done((bf16[2,144,864]{2,1,0:T(8,128)(2,1)}, bf16[2,144,864]{2,1,0:T(8,128)(2,1)}, u32[]{:S(2)}, u32[]{:S(2)}) %collective-permute-start.10) | collective-permute-done | bytes 497696 | tf_op jit(solution)/shard_map/ppermute | solution.py:451
  54.0 0.0 collective-permute-done.7.refs_3_
  54.0 0.1 collective-permute-start.11
  54.1 0.7 copy-done.6
  54.9 0.0 collective-permute-start.12
  54.9 5.5 %prepare.1 = (bf16[8,64,1152]{2,1,0:T(8,128)(2,1)}, bf16[8,64,1152]{2,1,0:T(8,128)(2,1)}) custom-call(s32[4]{0:T(128)} %pad_add_fusion.1.pos_ref, s32[16]{0:T(128)} %fusion.2.info_ref, bf16[2,2,64,1152]{3,2,1,0:T(8,128)(2,1)} %copy-done.1, bf16[2,2,64,1152]{3,2,1,0:T(8,128)(2,1)} %copy-done.5, bf16[2,2,64,1152]{3,2,1,0:T(8,128)(2,1)} %copy-done.2, ...), custom_call_target="tpu_custom_call" | custom-call | flops 1769472000 | bytes 2359296 | tf_op jit(solution)/shard_map/prepare/pallas_call | solution.py:523
  60.4 1.5 %collective-permute-start.14 = (bf16[144,1152]{1,0:T(8,128)(2,1)}, bf16[144,1152]{1,0:T(8,128)(2,1)}, u32[]{:S(2)}, u32[]{:S(2)}) collective-permute-start(bf16[144,1152]{1,0:T(8,128)(2,1)} %collective-permute-done.13.refs_4_), channel_id=1, source_target_pairs={{0,8},{1,9},{2,10},{3,11},{4,12},{5,13},{6,14},{7,15},{8,0},{9,1},... | collective-permute-start | bytes 995336 | tf_op jit(solution)/shard_map/ppermute | solution.py:533
  61.9 1.6 %collective-permute-done.14.refs_5_ = bf16[144,1152]{1,0:T(8,128)(2,1)} collective-permute-done((bf16[144,1152]{1,0:T(8,128)(2,1)}, bf16[144,1152]{1,0:T(8,128)(2,1)}, u32[]{:S(2)}, u32[]{:S(2)}) %collective-permute-start.14) | collective-permute-done | bytes 331808 | tf_op jit(solution)/shard_map/ppermute | solution.py:533
  63.5 0.0 collective-permute-done.12.refs_3_
  63.5 11.3 %forward.1 = (bf16[2,8,64,144]{3,2,1,0:T(8,128)(2,1)}, bf16[2,8,64,144]{3,2,1,0:T(8,128)(2,1)}, bf16[2,8,64,144]{3,2,1,0:T(8,128)(2,1)}, bf16[2,8,64,144]{3,2,1,...) custom-call(s32[4]{0:T(128)} %pad_add_fusion.1.pos_ref, ...), custom_call_target="tpu_custom_call" | custom-call | flops 8257536000 | bytes 2359296 | tf_op jit(solution)/shard_map/forward/pallas_call | solution.py:537
  74.8 0.4 collective-permute-start.15
  75.2 1.6 %collective-permute-start.17 = (bf16[2,64,1152]{2,1,0:T(8,128)(2,1)}, bf16[2,64,1152]{2,1,0:T(8,128)(2,1)}, u32[]{:S(2)}, u32[]{:S(2)}) collective-permute-start(bf16[2,64,1152]{2,1,0:T(8,128)(2,1)} %get-tuple-element.88), channel_id=1, source_target_pairs={{0,1},{1,0},{2,3},{3,2},{4,5},{5,4},{6,7},{7,6},{8,9},{9,8},{10,11... | collective-permute-start | bytes 884744 | tf_op jit(solution)/shard_map/ppermute | solution.py:454
  76.8 3.5 %collective-permute-start.18 = (bf16[2,64,1152]{2,1,0:T(8,128)(2,1)}, bf16[2,64,1152]{2,1,0:T(8,128)(2,1)}, u32[]{:S(2)}, u32[]{:S(2)}) collective-permute-start(bf16[2,64,1152]{2,1,0:T(8,128)(2,1)} %get-tuple-element.89), channel_id=1, source_target_pairs={{0,16},{1,17},{2,18},{3,19},{4,20},{5,21},{6,22},{7,23},{8,24},{9,... | collective-permute-start | bytes 884744 | tf_op jit(solution)/shard_map/ppermute | solution.py:454
  80.3 2.0 %slice_add_fusion = (f32[2,48,864]{2,1,0:T(8,128)}, f32[2,48,864]{2,1,0:T(8,128)}) fusion(f32[4,48,864]{2,1,0:T(8,128)S(1)} %collective-permute-done.15, f32[4,48,864]{2,1,0:T(8,128)} %get-tuple-element.79), kind=kLoop, calls=%fused_computation.3 | loop fusion | flops 165888 | bytes 1990656 | tf_op jit(solution)/shard_map/add | solution.py:559
  82.3 8.4 %backward.1 = (f32[2,64,1152]{2,1,0:T(8,128)}, bf16[2,64,1152]{2,1,0:T(8,128)(2,1)}, bf16[2,64,1152]{2,1,0:T(8,128)(2,1)}, bf16[2,64,1152]{2,1,0:T(8,128)(2,1)}) custom-call(s32[4]{0:T(128)} %pad_add_fusion.1.pos_ref, s32[16]{0:T(128)} %fusion.2.info_ref, bf16[2,144,864]{2,1,0:T(8,128)(2,1)} %pad_maximum_fusion.2.refs_0_, ...), custom_call_target="tpu_custom_call" | custom-call | flops 5898240000 | bytes 2359296 | tf_op jit(solution)/shard_map/backward/pallas_call | solution.py:563
  90.8 3.2 %collective-permute-done.18.refs_4_ = bf16[2,64,1152]{2,1,0:T(8,128)(2,1)} collective-permute-done((bf16[2,64,1152]{2,1,0:T(8,128)(2,1)}, bf16[2,64,1152]{2,1,0:T(8,128)(2,1)}, u32[]{:S(2)}, u32[]{:S(2)}) %collective-permute-start.18) | collective-permute-done | bytes 294944 | tf_op jit(solution)/shard_map/ppermute | solution.py:454
  94.0 1.5 %collective-permute-start.22 = (bf16[2,64,1152]{2,1,0:T(8,128)(2,1)}, bf16[2,64,1152]{2,1,0:T(8,128)(2,1)}, u32[]{:S(2)}, u32[]{:S(2)}) collective-permute-start(bf16[2,64,1152]{2,1,0:T(8,128)(2,1)} %get-tuple-element.98), channel_id=1, source_target_pairs={{0,1},{1,0},{2,3},{3,2},{4,5},{5,4},{6,7},{7,6},{8,9},{9,8},{10,11... | collective-permute-start | bytes 884744 | tf_op jit(solution)/shard_map/ppermute | solution.py:454
  95.4 0.6 collective-permute-start.23
  96.0 1.4 %collective-permute-start.24 = (bf16[2,64,1152]{2,1,0:T(8,128)(2,1)}, bf16[2,64,1152]{2,1,0:T(8,128)(2,1)}, u32[]{:S(2)}, u32[]{:S(2)}) collective-permute-start(bf16[2,64,1152]{2,1,0:T(8,128)(2,1)} %get-tuple-element.100), channel_id=1, source_target_pairs={{0,17},{1,16},{2,19},{3,18},{4,21},{5,20},{6,23},{7,22},{8,25},{9,... | collective-permute-start | bytes 884744 | tf_op jit(solution)/shard_map/ppermute | solution.py:454
  97.5 3.1 %output.1 = (bf16[64,1152]{1,0:T(8,128)(2,1)}, bf16[64,1152]{1,0:T(8,128)(2,1)}) custom-call(s32[4]{0:T(128)} %pad_add_fusion.1.pos_ref, s32[16]{0:T(128)} %fusion.2.info_ref, bf16[1,2,64,1152]{3,2,1,0:T(8,128)(2,1)} %copy-done.3, bf16[1,2,64,1152]{3,2,1,0:T(8,128)(2,1)} %copy-done.4, f32[2,64,1152]{2,1,0:T(8,128)} %get-tuple-element.91.refs_2_, ...), custom_call_target="tpu_custom_call" | custom-call | flops 11796480000 | bytes 2359296 | tf_op jit(solution)/shard_map/output/pallas_call | solution.py:576
  100.6 2.6 %collective-permute-start.20 = (bf16[64,1152]{1,0:T(8,128)(2,1)}, bf16[64,1152]{1,0:T(8,128)(2,1)}, u32[]{:S(2)}, u32[]{:S(2)}) collective-permute-start(bf16[64,1152]{1,0:T(8,128)(2,1)} %get-tuple-element.95), channel_id=1, source_target_pairs={{0,0},{1,1},{16,2},{17,3},{2,4},{3,5},{18,6},{19,7},{20,8},{21,9},... | collective-permute-start | bytes 442376 | tf_op jit(solution)/shard_map/ppermute | solution.py:441
  103.2 6.1 %collective-permute-start.21 = (bf16[64,1152]{1,0:T(8,128)(2,1)}, bf16[64,1152]{1,0:T(8,128)(2,1)}, u32[]{:S(2)}, u32[]{:S(2)}) collective-permute-start(bf16[64,1152]{1,0:T(8,128)(2,1)} %get-tuple-element.96), channel_id=1, source_target_pairs={{2,0},{3,1},{18,2},{19,3},{0,4},{1,5},{16,6},{17,7},{22,8},{23,9},... | collective-permute-start | bytes 442376 | tf_op jit(solution)/shard_map/ppermute | solution.py:441
  109.3 1.1 add.37
  110.4 0.7 copy-done
  111.1 0.7 slice.40
  111.8 3.4 %input_grad.1 = (bf16[64,1152]{1,0:T(8,128)(2,1)}, bf16[64,1152]{1,0:T(8,128)(2,1)}) custom-call(s32[4]{0:T(128)} %pad_add_fusion.1.pos_ref, s32[16]{0:T(128)} %fusion.2.info_ref, bf16[1,2,64,1152]{3,2,1,0:T(8,128)(2,1)} %copy-done.3, bf16[1,2,64,1152]{3,2,1,0:T(8,128)(2,1)} %copy-done.4, f32[2,64,1152]{2,1,0:T(8,128)} %get-tuple-element.101.refs_2_, ...), custom_call_target="tpu_custom_call" | custom-call | flops 1769472000 | bytes 2359296 | tf_op jit(solution)/shard_map/input_grad/pallas_call | solution.py:588
  115.2 4.0 %collective-permute-start.25 = (bf16[64,1152]{1,0:T(8,128)(2,1)}, bf16[64,1152]{1,0:T(8,128)(2,1)S(1)}, u32[]{:S(2)}, u32[]{:S(2)}) collective-permute-start(bf16[64,1152]{1,0:T(8,128)(2,1)} %get-tuple-element.105), channel_id=1, source_target_pairs={{0,0},{1,1},{16,2},{17,3},{2,4},{3,5},{18,6},{19,7},{20,8},{21,9},... | collective-permute-start | bytes 442376 | tf_op jit(solution)/shard_map/ppermute | solution.py:441
  119.2 4.5 %collective-permute-start.26 = (bf16[64,1152]{1,0:T(8,128)(2,1)}, bf16[64,1152]{1,0:T(8,128)(2,1)S(1)}, u32[]{:S(2)}, u32[]{:S(2)}) collective-permute-start(bf16[64,1152]{1,0:T(8,128)(2,1)} %get-tuple-element.106), channel_id=1, source_target_pairs={{2,0},{3,1},{18,2},{19,3},{0,4},{1,5},{16,6},{17,7},{22,8},{23,9},... | collective-permute-start | bytes 442376 | tf_op jit(solution)/shard_map/ppermute | solution.py:441
  123.7 1.0 slice_add_fusion.2
  124.7 1.9 %collective-permute-start.28 = (f32[48,864]{1,0:T(8,128)S(1)}, f32[48,864]{1,0:T(8,128)S(1)}, u32[]{:S(2)}, u32[]{:S(2)}) collective-permute-start(f32[48,864]{1,0:T(8,128)S(1)} %bitcast.28), channel_id=1, source_target_pairs={{0,0},{1,1},{2,8},{3,9},{4,16},{5,17},{6,24},{7,25},{8,4},{9,5},{1... | collective-permute-start | bytes 497672 | tf_op jit(solution)/shard_map/ppermute | solution.py:604
  126.7 0.5 collective-permute-done.26
  127.2 1.0 broadcast_select_fusion.3
  128.3 0.7 maximum_bitcast_fusion.1
  129.0 0.7 maximum_bitcast_fusion
  129.8 5.9 %collective-permute-done.28 = f32[48,864]{1,0:T(8,128)S(1)} collective-permute-done((f32[48,864]{1,0:T(8,128)S(1)}, f32[48,864]{1,0:T(8,128)S(1)}, u32[]{:S(2)}, u32[]{:S(2)}) %collective-permute-start.28) | collective-permute-done | bytes 165920 | tf_op jit(solution)/shard_map/ppermute | solution.py:604
  135.7 0.1 fusion.6
  135.8 0.7 maximum_multiply_fusion
  (32 shorter events, 0.1 us)
Async XLA Ops:
  4.6 10.4 %collective-permute-start.2 = (bf16[1,2,64,1152]{3,2,1,0:T(8,128)(2,1)}, bf16[1,2,64,1152]{3,2,1,0:T(8,128)(2,1)S(1)}, u32[]{:S(2)}, u32[]{:S(2)}) collective-permute-start(bf16[1,2,64,1152]{3,2,1,0:T(8,128)(2,1)} %get-tuple-element.57), channel_id=1, source_target_pairs={{0,0},{1,1},{2,16},{3,17},{4,2},{5,3},{6,18},{7,19},{8,20},{9,21},... | collective-permute-start | bytes 884744 | tf_op jit(solution)/shard_map/ppermute | solution.py:480
  7.3 6.2 %collective-permute-start = (s32[1,16]{1,0:T(1,128)S(1)}, s32[1,16]{1,0:T(1,128)S(1)}, u32[]{:S(2)}, u32[]{:S(2)}) collective-permute-start(s32[1,16]{1,0:T(1,128)S(1)} %fusion.7), channel_id=1, source_target_pairs={{0,8},{1,9},{2,10},{3,11},{4,12},{5,13},{6,14},{7,15},{8,0},{9,1},... | collective-permute-start | bytes 200 | tf_op jit(solution)/shard_map/ppermute | solution.py:458
  9.4 9.0 %collective-permute-start.8 = (bf16[144,432]{1,0:T(8,128)(2,1)}, bf16[144,432]{1,0:T(8,128)(2,1)S(1)}, u32[]{:S(2)}, u32[]{:S(2)}) collective-permute-start(bf16[144,432]{1,0:T(8,128)(2,1)} %get-tuple-element.63), channel_id=1, source_target_pairs={{0,1},{1,0},{2,3},{3,2},{4,5},{5,4},{6,7},{7,6},{8,9},{9,8},{10,11... | collective-permute-start | bytes 373256 | tf_op jit(solution)/shard_map/ppermute | solution.py:482
  10.9 13.9 %collective-permute-start.3 = (bf16[1,2,64,1152]{3,2,1,0:T(8,128)(2,1)}, bf16[1,2,64,1152]{3,2,1,0:T(8,128)(2,1)S(1)}, u32[]{:S(2)}, u32[]{:S(2)}) collective-permute-start(bf16[1,2,64,1152]{3,2,1,0:T(8,128)(2,1)} %get-tuple-element.58), channel_id=1, source_target_pairs={{0,2},{1,3},{2,18},{3,19},{4,0},{5,1},{6,16},{7,17},{8,22},{9,23},... | collective-permute-start | bytes 884744 | tf_op jit(solution)/shard_map/ppermute | solution.py:480
  13.5 3.6 %collective-permute-start.1 = (s32[2,16]{1,0:T(2,128)S(1)}, s32[2,16]{1,0:T(2,128)S(1)}, u32[]{:S(2)}, u32[]{:S(2)}) collective-permute-start(s32[2,16]{1,0:T(2,128)S(1)} %pad_add_fusion), channel_id=1, source_target_pairs={{0,16},{1,17},{2,18},{3,19},{4,20},{5,21},{6,22},{7,23},{8,24},{9,... | collective-permute-start | bytes 392 | tf_op jit(solution)/shard_map/ppermute | solution.py:460
  15.0 19.7 %copy-start.3 = (bf16[1,2,64,1152]{3,2,1,0:T(8,128)(2,1)}, bf16[1,2,64,1152]{3,2,1,0:T(8,128)(2,1)S(1)}, u32[]{:S(2)}) copy-start(bf16[1,2,64,1152]{3,2,1,0:T(8,128)(2,1)S(1)} %collective-permute-done.2.refs_0_) | copy-start | bytes 884740
  15.0 9.8 %collective-permute-start.4 = (bf16[1,2,64,1152]{3,2,1,0:T(8,128)(2,1)S(1)}, bf16[1,2,64,1152]{3,2,1,0:T(8,128)(2,1)S(1)}, u32[]{:S(2)}, u32[]{:S(2)}) collective-permute-start(bf16[1,2,64,1152]{3,2,1,0:T(8,128)(2,1)S(1)} %collective-permute-done.2.refs_0_), channel_id=1, source_target_pairs={{0,1},{1,0},{2,3},{3,2},{4,5},{5,4},{6,7},{7,6},{8,9},{9,8},{10,11... | collective-permute-start | bytes 884744 | tf_op jit(solution)/shard_map/ppermute | solution.py:490
  24.8 10.0 %copy-start.4 = (bf16[1,2,64,1152]{3,2,1,0:T(8,128)(2,1)}, bf16[1,2,64,1152]{3,2,1,0:T(8,128)(2,1)S(1)}, u32[]{:S(2)}) copy-start(bf16[1,2,64,1152]{3,2,1,0:T(8,128)(2,1)S(1)} %collective-permute-done.3.refs_1_) | copy-start | bytes 884740
  24.8 9.9 %collective-permute-start.6 = (bf16[1,2,64,1152]{3,2,1,0:T(8,128)(2,1)S(1)}, bf16[1,2,64,1152]{3,2,1,0:T(8,128)(2,1)S(1)}, u32[]{:S(2)}, u32[]{:S(2)}) collective-permute-start(bf16[1,2,64,1152]{3,2,1,0:T(8,128)(2,1)S(1)} %collective-permute-done.3.refs_1_), channel_id=1, source_target_pairs={{0,16},{1,17},{2,18},{3,19},{4,20},{5,21},{6,22},{7,23},{8,24},{9,... | collective-permute-start | bytes 884744 | tf_op jit(solution)/shard_map/ppermute | solution.py:448
  25.9 14.4 %collective-permute-start.9 = (bf16[1,144,864]{2,1,0:T(8,128)(2,1)S(1)}, bf16[1,144,864]{2,1,0:T(8,128)(2,1)S(1)}, u32[]{:S(2)}, u32[]{:S(2)}) collective-permute-start(bf16[1,144,864]{2,1,0:T(8,128)(2,1)S(1)} %maximum_bitcast_fusion.2), channel_id=1, source_target_pairs={{0,4},{1,5},{2,6},{3,7},{4,0},{5,1},{6,2},{7,3},{8,12},{9,13},{10,... | collective-permute-start | bytes 746504 | tf_op jit(solution)/shard_map/ppermute | solution.py:448
  28.9 12.3 %copy-start.1 = (bf16[2,2,64,1152]{3,2,1,0:T(8,128)(2,1)}, bf16[2,2,64,1152]{3,2,1,0:T(8,128)(2,1)S(1)}, u32[]{:S(2)}) copy-start(bf16[2,2,64,1152]{3,2,1,0:T(8,128)(2,1)S(1)} %pad_maximum_fusion.refs_0_) | copy-start | bytes 1769476
  28.9 17.3 %collective-permute-start.5 = (bf16[2,2,64,1152]{3,2,1,0:T(8,128)(2,1)S(1)}, bf16[2,2,64,1152]{3,2,1,0:T(8,128)(2,1)S(1)}, u32[]{:S(2)}, u32[]{:S(2)}) collective-permute-start(bf16[2,2,64,1152]{3,2,1,0:T(8,128)(2,1)S(1)} %pad_maximum_fusion.refs_0_), channel_id=1, source_target_pairs={{0,16},{1,17},{2,18},{3,19},{4,20},{5,21},{6,22},{7,23},{8,24},{9,... | collective-permute-start | bytes 1769480 | tf_op jit(solution)/shard_map/ppermute | solution.py:451
  34.8 11.5 %copy-start.2 = (bf16[2,2,64,1152]{3,2,1,0:T(8,128)(2,1)}, bf16[2,2,64,1152]{3,2,1,0:T(8,128)(2,1)S(1)}, u32[]{:S(2)}) copy-start(bf16[2,2,64,1152]{3,2,1,0:T(8,128)(2,1)S(1)} %pad_maximum_fusion.1.refs_2_) | copy-start | bytes 1769476
  34.8 19.3 %collective-permute-start.7 = (bf16[2,2,64,1152]{3,2,1,0:T(8,128)(2,1)S(1)}, bf16[2,2,64,1152]{3,2,1,0:T(8,128)(2,1)S(1)}, u32[]{:S(2)}, u32[]{:S(2)}) collective-permute-start(bf16[2,2,64,1152]{3,2,1,0:T(8,128)(2,1)S(1)} %pad_maximum_fusion.1.refs_2_), channel_id=1, source_target_pairs={{0,1},{1,0},{2,3},{3,2},{4,5},{5,4},{6,7},{7,6},{8,9},{9,8},{10,11... | collective-permute-start | bytes 1769480 | tf_op jit(solution)/shard_map/ppermute | solution.py:451
  41.2 12.9 %collective-permute-start.10 = (bf16[2,144,864]{2,1,0:T(8,128)(2,1)}, bf16[2,144,864]{2,1,0:T(8,128)(2,1)}, u32[]{:S(2)}, u32[]{:S(2)}) collective-permute-start(bf16[2,144,864]{2,1,0:T(8,128)(2,1)} %pad_maximum_fusion.2.refs_0_), channel_id=1, source_target_pairs={{0,2},{1,3},{2,0},{3,1},{4,6},{5,7},{6,4},{7,5},{8,10},{9,11},{10,... | collective-permute-start | bytes 1493000 | tf_op jit(solution)/shard_map/ppermute | solution.py:451
  41.2 19.2 %collective-permute-start.13 = (bf16[144,1152]{1,0:T(8,128)(2,1)}, bf16[144,1152]{1,0:T(8,128)(2,1)}, u32[]{:S(2)}, u32[]{:S(2)}) collective-permute-start(bf16[144,1152]{1,0:T(8,128)(2,1)} %param.15), channel_id=1, source_target_pairs={{0,0},{1,1},{2,18},{3,19},{4,8},{5,9},{6,26},{7,27},{8,4},{9,5},{1... | collective-permute-start | bytes 995336 | tf_op jit(solution)/shard_map/ppermute | solution.py:495
  46.2 7.8 %copy-start.5 = (bf16[2,2,64,1152]{3,2,1,0:T(8,128)(2,1)}, bf16[2,2,64,1152]{3,2,1,0:T(8,128)(2,1)S(1)}, u32[]{:S(2)}) copy-start(bf16[2,2,64,1152]{3,2,1,0:T(8,128)(2,1)S(1)} %collective-permute-done.5.refs_1_) | copy-start | bytes 1769476
  54.0 0.8 copy-start.6
  54.0 9.5 %collective-permute-start.11 = (bf16[2,144,864]{2,1,0:T(8,128)(2,1)}, bf16[2,144,864]{2,1,0:T(8,128)(2,1)}, u32[]{:S(2)}, u32[]{:S(2)}) collective-permute-start(bf16[2,144,864]{2,1,0:T(8,128)(2,1)} %pad_maximum_fusion.2.refs_0_), channel_id=1, source_target_pairs={{0,8},{1,9},{2,10},{3,11},{4,12},{5,13},{6,14},{7,15},{8,0},{9,1},... | collective-permute-start | bytes 1493000 | tf_op jit(solution)/shard_map/ppermute | solution.py:503
  54.9 8.6 %collective-permute-start.12 = (bf16[2,144,864]{2,1,0:T(8,128)(2,1)}, bf16[2,144,864]{2,1,0:T(8,128)(2,1)}, u32[]{:S(2)}, u32[]{:S(2)}) collective-permute-start(bf16[2,144,864]{2,1,0:T(8,128)(2,1)} %collective-permute-done.10.refs_1_), channel_id=1, source_target_pairs={{0,8},{1,9},{2,10},{3,11},{4,12},{5,13},{6,14},{7,15},{8,0},{9,1},... | collective-permute-start | bytes 1493000 | tf_op jit(solution)/shard_map/ppermute | solution.py:503
  60.4 3.1 %collective-permute-start.14 = (bf16[144,1152]{1,0:T(8,128)(2,1)}, bf16[144,1152]{1,0:T(8,128)(2,1)}, u32[]{:S(2)}, u32[]{:S(2)}) collective-permute-start(bf16[144,1152]{1,0:T(8,128)(2,1)} %collective-permute-done.13.refs_4_), channel_id=1, source_target_pairs={{0,8},{1,9},{2,10},{3,11},{4,12},{5,13},{6,14},{7,15},{8,0},{9,1},... | collective-permute-start | bytes 995336 | tf_op jit(solution)/shard_map/ppermute | solution.py:533
  74.8 5.5 %collective-permute-start.15 = (f32[4,48,864]{2,1,0:T(8,128)}, f32[4,48,864]{2,1,0:T(8,128)S(1)}, u32[]{:S(2)}, u32[]{:S(2)}) collective-permute-start(f32[4,48,864]{2,1,0:T(8,128)} %get-tuple-element.80), channel_id=1, source_target_pairs={{0,8},{1,9},{2,10},{3,11},{4,12},{5,13},{6,14},{7,15},{8,0},{9,1},... | collective-permute-start | bytes 1990664 | tf_op jit(solution)/shard_map/ppermute | solution.py:555
  75.2 15.5 %collective-permute-start.17 = (bf16[2,64,1152]{2,1,0:T(8,128)(2,1)}, bf16[2,64,1152]{2,1,0:T(8,128)(2,1)}, u32[]{:S(2)}, u32[]{:S(2)}) collective-permute-start(bf16[2,64,1152]{2,1,0:T(8,128)(2,1)} %get-tuple-element.88), channel_id=1, source_target_pairs={{0,1},{1,0},{2,3},{3,2},{4,5},{5,4},{6,7},{7,6},{8,9},{9,8},{10,11... | collective-permute-start | bytes 884744 | tf_op jit(solution)/shard_map/ppermute | solution.py:454
  76.8 17.2 %collective-permute-start.18 = (bf16[2,64,1152]{2,1,0:T(8,128)(2,1)}, bf16[2,64,1152]{2,1,0:T(8,128)(2,1)}, u32[]{:S(2)}, u32[]{:S(2)}) collective-permute-start(bf16[2,64,1152]{2,1,0:T(8,128)(2,1)} %get-tuple-element.89), channel_id=1, source_target_pairs={{0,16},{1,17},{2,18},{3,19},{4,20},{5,21},{6,22},{7,23},{8,24},{9,... | collective-permute-start | bytes 884744 | tf_op jit(solution)/shard_map/ppermute | solution.py:454
  80.3 13.7 %collective-permute-start.19 = (bf16[2,64,1152]{2,1,0:T(8,128)(2,1)}, bf16[2,64,1152]{2,1,0:T(8,128)(2,1)}, u32[]{:S(2)}, u32[]{:S(2)}) collective-permute-start(bf16[2,64,1152]{2,1,0:T(8,128)(2,1)} %get-tuple-element.90), channel_id=1, source_target_pairs={{0,17},{1,16},{2,19},{3,18},{4,21},{5,20},{6,23},{7,22},{8,25},{9,... | collective-permute-start | bytes 884744 | tf_op jit(solution)/shard_map/ppermute | solution.py:454
  82.3 11.6 %collective-permute-start.16 = (f32[2,48,864]{2,1,0:T(8,128)}, f32[2,48,864]{2,1,0:T(8,128)}, u32[]{:S(2)}, u32[]{:S(2)}) collective-permute-start(f32[2,48,864]{2,1,0:T(8,128)} %get-tuple-element.86), channel_id=1, source_target_pairs={{0,2},{1,3},{2,0},{3,1},{4,6},{5,7},{6,4},{7,5},{8,10},{9,11},{10,... | collective-permute-start | bytes 995336 | tf_op jit(solution)/shard_map/ppermute | solution.py:561
  94.0 17.8 %collective-permute-start.22 = (bf16[2,64,1152]{2,1,0:T(8,128)(2,1)}, bf16[2,64,1152]{2,1,0:T(8,128)(2,1)}, u32[]{:S(2)}, u32[]{:S(2)}) collective-permute-start(bf16[2,64,1152]{2,1,0:T(8,128)(2,1)} %get-tuple-element.98), channel_id=1, source_target_pairs={{0,1},{1,0},{2,3},{3,2},{4,5},{5,4},{6,7},{7,6},{8,9},{9,8},{10,11... | collective-permute-start | bytes 884744 | tf_op jit(solution)/shard_map/ppermute | solution.py:454
  95.4 16.4 %collective-permute-start.23 = (bf16[2,64,1152]{2,1,0:T(8,128)(2,1)}, bf16[2,64,1152]{2,1,0:T(8,128)(2,1)}, u32[]{:S(2)}, u32[]{:S(2)}) collective-permute-start(bf16[2,64,1152]{2,1,0:T(8,128)(2,1)} %get-tuple-element.99), channel_id=1, source_target_pairs={{0,16},{1,17},{2,18},{3,19},{4,20},{5,21},{6,22},{7,23},{8,24},{9,... | collective-permute-start | bytes 884744 | tf_op jit(solution)/shard_map/ppermute | solution.py:454
  96.0 15.8 %collective-permute-start.24 = (bf16[2,64,1152]{2,1,0:T(8,128)(2,1)}, bf16[2,64,1152]{2,1,0:T(8,128)(2,1)}, u32[]{:S(2)}, u32[]{:S(2)}) collective-permute-start(bf16[2,64,1152]{2,1,0:T(8,128)(2,1)} %get-tuple-element.100), channel_id=1, source_target_pairs={{0,17},{1,16},{2,19},{3,18},{4,21},{5,20},{6,23},{7,22},{8,25},{9,... | collective-permute-start | bytes 884744 | tf_op jit(solution)/shard_map/ppermute | solution.py:454
  100.6 26.1 %collective-permute-start.20 = (bf16[64,1152]{1,0:T(8,128)(2,1)}, bf16[64,1152]{1,0:T(8,128)(2,1)}, u32[]{:S(2)}, u32[]{:S(2)}) collective-permute-start(bf16[64,1152]{1,0:T(8,128)(2,1)} %get-tuple-element.95), channel_id=1, source_target_pairs={{0,0},{1,1},{16,2},{17,3},{2,4},{3,5},{18,6},{19,7},{20,8},{21,9},... | collective-permute-start | bytes 442376 | tf_op jit(solution)/shard_map/ppermute | solution.py:441
  103.2 23.5 %collective-permute-start.21 = (bf16[64,1152]{1,0:T(8,128)(2,1)}, bf16[64,1152]{1,0:T(8,128)(2,1)}, u32[]{:S(2)}, u32[]{:S(2)}) collective-permute-start(bf16[64,1152]{1,0:T(8,128)(2,1)} %get-tuple-element.96), channel_id=1, source_target_pairs={{2,0},{3,1},{18,2},{19,3},{0,4},{1,5},{16,6},{17,7},{22,8},{23,9},... | collective-permute-start | bytes 442376 | tf_op jit(solution)/shard_map/ppermute | solution.py:441
  110.4 0.7 copy-start
  111.8 11.9 %collective-permute-start.27 = (f32[1,48,864]{2,1,0:T(8,128)}, f32[1,48,864]{2,1,0:T(8,128)}, u32[]{:S(2)}, u32[]{:S(2)}) collective-permute-start(f32[1,48,864]{2,1,0:T(8,128)} %slice.40), channel_id=1, source_target_pairs={{0,4},{1,5},{2,6},{3,7},{4,0},{5,1},{6,2},{7,3},{8,12},{9,13},{10,... | collective-permute-start | bytes 497672 | tf_op jit(solution)/shard_map/ppermute | solution.py:602
  115.2 11.5 %collective-permute-start.25 = (bf16[64,1152]{1,0:T(8,128)(2,1)}, bf16[64,1152]{1,0:T(8,128)(2,1)S(1)}, u32[]{:S(2)}, u32[]{:S(2)}) collective-permute-start(bf16[64,1152]{1,0:T(8,128)(2,1)} %get-tuple-element.105), channel_id=1, source_target_pairs={{0,0},{1,1},{16,2},{17,3},{2,4},{3,5},{18,6},{19,7},{20,8},{21,9},... | collective-permute-start | bytes 442376 | tf_op jit(solution)/shard_map/ppermute | solution.py:441
  119.2 8.0 %collective-permute-start.26 = (bf16[64,1152]{1,0:T(8,128)(2,1)}, bf16[64,1152]{1,0:T(8,128)(2,1)S(1)}, u32[]{:S(2)}, u32[]{:S(2)}) collective-permute-start(bf16[64,1152]{1,0:T(8,128)(2,1)} %get-tuple-element.106), channel_id=1, source_target_pairs={{2,0},{3,1},{18,2},{19,3},{0,4},{1,5},{16,6},{17,7},{22,8},{23,9},... | collective-permute-start | bytes 442376 | tf_op jit(solution)/shard_map/ppermute | solution.py:441
  124.7 10.9 %collective-permute-start.28 = (f32[48,864]{1,0:T(8,128)S(1)}, f32[48,864]{1,0:T(8,128)S(1)}, u32[]{:S(2)}, u32[]{:S(2)}) collective-permute-start(f32[48,864]{1,0:T(8,128)S(1)} %bitcast.28), channel_id=1, source_target_pairs={{0,0},{1,1},{2,8},{3,9},{4,16},{5,17},{6,24},{7,25},{8,4},{9,5},{1... | collective-permute-start | bytes 497672 | tf_op jit(solution)/shard_map/ppermute | solution.py:604

commit v16 on v15

--- a/solution.py
+++ b/solution.py
@@ -12,7 +12,7 @@
 CORES = 2
 AXES = ("y", "c", "z", "x")
 BLOCK = 16
-VMEM_LIMIT = 64 * 1024 * 1024 - 65536
+VMEM_LIMIT = 56 * 1024 * 1024
 BF16 = jnp.bfloat16
 F32 = jnp.float32
 
@@ -225,8 +225,7 @@
     return exponent * (1.0 / jnp.sum(exponent, axis=1, keepdims=True))
 
 
-def prepare_kernel(lay, pos_ref, info_ref, *refs):
-    pair_refs, (mod_ref, hid_ref, gp_ref) = refs[: 2 * lay.nc], refs[2 * lay.nc :]
+def modulate(lay, pos_ref, info_ref, pair_refs, mod_ref, hid_ref, gp_ref):
     _, step_patches, model = hid_ref.shape
     patches = step_patches * pl.num_programs(0)
     patch_base = lay.unit(pos_ref[1], pos_ref[2])[2] * patches + pl.program_id(0) * step_patches
@@ -242,11 +241,13 @@
         gp_ref[t] = (factor * ref[place, 1].astype(F32)).astype(BF16)
 
 
-def forward_kernel(lay, pos_ref, info_ref, hid_ref, gp_ref, *refs):
+def forward_kernel(lay, pos_ref, info_ref, *refs):
+    pair_refs, refs = refs[: 2 * lay.nc], refs[2 * lay.nc :]
     w_refs, refs = refs[: 2 * lay.halves], refs[2 * lay.halves :]
     wo_refs, refs = refs[: lay.nc], refs[lay.nc :]
-    q_ref, k_ref, v_ref, ga_ref, kept_ref, sent_ref, *refs = refs
-    pr_refs, (w_scr, att_scr, wo_scr, acc_scr, cut_scr) = refs[: lay.chips], refs[lay.chips :]
+    mod_ref, q_ref, k_ref, v_ref, ga_ref, kept_ref, sent_ref, *refs = refs
+    pr_refs, refs = refs[: lay.chips], refs[lay.chips :]
+    hid_ref, gp_ref, w_scr, att_scr, wo_scr, acc_scr, cut_scr = refs
     _, step_patches, model = hid_ref.shape
     tokens = lay.frames * step_patches
     cols = w_scr.shape[2] // 3
@@ -262,6 +263,7 @@
         wo_scr[...] = jnp.concatenate(both, axis=0).astype(BF16)
         acc_scr[...] = jnp.zeros_like(acc_scr)
 
+    modulate(lay, pos_ref, info_ref, pair_refs, mod_ref, hid_ref, gp_ref)
     hidden = hid_ref[...].reshape(lay.frames * step_patches, model)
     for h in range(lay.halves):
         triple = dot(hidden, w_scr[h])
@@ -520,16 +522,6 @@
     part_specs = [spread(nc, model, step_patches)] * chips
     part_shapes = [struct((nc, half, model), F32)] + [struct((nc, half, model))] * (chips - 1)
 
-    hidden, grad_proj = call(
-        functools.partial(prepare_kernel, lay),
-        "prepare",
-        3 * model * 1000,
-        [pair_spec(chips // 2, BLOCK)] * (2 * nc) + [mod_spec],
-        [spread(lay.frames, model, BLOCK)] * 2,
-        [struct((lay.frames, half, model))] * 2,
-        grid=(half // BLOCK,),
-    )(pos, info, *pairs, mod_table)
-    wo_own, _ = lax.optimization_barrier((wo_own, hidden))
     wo_rows = [wo_own, lax.ppermute(wo_own, AXES, lay.swap(kc=1))]
 
     fold = 3 if rows % 24 == 0 else 1
@@ -538,12 +530,14 @@
         functools.partial(forward_kernel, lay),
         "forward",
         14 * model * 1000,
-        [spread(lay.frames, model, step_patches)] * 2
+        [pair_spec(chips // 2, step_patches)] * (2 * nc)
         + w_specs
-        + [whole_spec(w_out.shape)] * nc,
+        + [whole_spec(w_out.shape)] * nc
+        + [mod_spec],
         [triple_spec] * 4 + [whole_spec(piece_shape)] * 2 + part_specs,
         [triple_shape] * 4 + [struct(piece_shape, F32)] * 2 + part_shapes,
-        [
+        [pltpu.VMEM((lay.frames, step_patches, model), BF16)] * 2
+        + [
             w_scratch,
             pltpu.VMEM((lay.frames, step_patches, chip_width), BF16),
             pltpu.VMEM((chip_width, model), BF16),
@@ -551,7 +545,7 @@
             pltpu.VMEM(piece_shape, F32),
         ],
         (steps,),
-    )(pos, info, hidden, grad_proj, *w_pieces, *wo_rows)
+    )(pos, info, *pairs, *w_pieces, *wo_rows, mod_table)
     got = lax.ppermute(sent, AXES, lay.swap(kc=1))
     projected = over_chips(projected)
 

time: 137 us -> 134 us (0.978); the launches traced: 136 us -> 132 us
  other arithmetic: 12.2 us -> 6 us
  waiting for transfers between devices: 37.1 us -> 42.8 us
  Pallas kernels: 35.1 us -> 30.1 us
  local copies, waits for them, and re-layouts: 2.26 us -> 4.01 us
  starting transfers between devices: 49 us -> 47.5 us
    pallas_call x1 -> x0, Pallas kernels: 5.51 us -> none  [local(): call(functools.partial(prepare_kernel, lay), 'prepare', 3 * model * 1000,...]
    ppermute x1, waiting for transfers between devices: 0.01 us -> 4.34 us  [local(): wo_own = lax.ppermute(late_w_out, AXES, lay.rows_to_chip())]
    ppermute x1, waiting for transfers between devices: 5.92 us -> 2.62 us  [local(): grad_w = lax.ppermute(cut[0], AXES, lay.to_owner())]
    ppermute x4, waiting for transfers between devices: 0.55 us -> 3.24 us  [from_plane(): lax.ppermute(part, AXES, lay.from_plane(k))]
    unnamed x14 -> x44, local copies, waits for them, and re-layouts: 1.48 us -> 3.9 us
    ppermute x4, starting transfers between devices: 17.1 us -> 15.1 us  [from_plane(): lax.ppermute(part, AXES, lay.from_plane(k))]
    ppermute x6, waiting for transfers between devices: 3.23 us -> 5.26 us  [over_chips(): got = [lax.ppermute(parts[k], AXES, chip_swap(k)) for k in range(1, chips)]]
    ppermute x6, starting transfers between devices: 8.59 us -> 7.04 us  [over_chips(): got = [lax.ppermute(parts[k], AXES, chip_swap(k)) for k in range(1, chips)]]
  transfers between devices with their start and end apart: 29 -> 29, of which waited for: 10 -> 12; matrix products, arithmetic and copies ran while one was open for 8% -> 4% of each run, Pallas kernels for 15% -> 11%
where the time goes in v16:
time: 134 us; the launch traced here: 132 us
  starting transfers between devices  47.5 us (35%)
  waiting for transfers between devices  42.8 us (32%)
  Pallas kernels  30.1 us (22%)
  other arithmetic  6 us (4%)
  local copies, waits for them, and re-layouts  4.01 us (3%)
    ppermute x4, starting transfers between devices, from_plane(): lax.ppermute(part, AXES, lay.from_plane(k))  15.1 us
    pallas_call x1, Pallas kernels, local(): call(functools.partial(forward_kernel, lay), 'forward', 14 * model * 1000...  11.9 us
    ppermute x2, waiting for transfers between devices, doubling(): got = lax.ppermute(held, AXES, swap(bit)) if first is None else first  10.6 us
    pallas_call x1, Pallas kernels, local(): call(functools.partial(backward_kernel, lay), 'backward', 10 * model * 10...  8.39 us
    ppermute x3, waiting for transfers between devices, doubling(): return [held, lax.ppermute(held, AXES, swap(bits[-1]))]  8.11 us
    ppermute x6, starting transfers between devices, over_chips(): got = [lax.ppermute(parts[k], AXES, chip_swap(k)) for k in range(1, chips)]  7.04 us
    ppermute x2, waiting for transfers between devices, local(): lax.ppermute(pair, AXES, lay.to_plane(k))  6.08 us
    ppermute x6, waiting for transfers between devices, over_chips(): got = [lax.ppermute(parts[k], AXES, chip_swap(k)) for k in range(1, chips)]  5.26 us
  transfers between devices with their start and end apart: 29, of which 12 were waited for; matrix products, arithmetic and copies ran while one was open for 4% of the time, Pallas kernels for 11%

profile of v16, /device:TPU:4, one launch (start us, length us, event | category | flops | bytes accessed | tf_op | source)
XLA Modules:
  0.0 131.5 jit_solution(1426802886516248881)
XLA Ops:
  0.6 0.6 pad_add_fusion.1.pos_ref
  1.2 3.3 %start.1 = (bf16[1,2,64,1152]{3,2,1,0:T(8,128)(2,1)}, bf16[1,2,64,1152]{3,2,1,0:T(8,128)(2,1)}, bf16[144,432]{1,0:T(8,128)(2,1)}, bf16[144,432]{1,0:T(8,128)(2,1)}) custom-call(s32[4]{0:T(128)} %pad_add_fusion.1.pos_ref, bf16[1,128,1152]{2,1,0:T(8,128)(2,1)} %x_ref.1, bf16[1,128,1152]{2,1,0:T(8,128)(2,1)} %g_ref.1, bf16[144,3456]{1,0:T(8,128)(2,1)} %w_ref.1), custom_call_target="tpu_custom_call" | custom-call | flops 1179648000 | bytes 2359296 | tf_op jit(solution)/shard_map/start/pallas_call | solution.py:472
  4.5 1.9 %collective-permute-start.2 = (bf16[1,2,64,1152]{3,2,1,0:T(8,128)(2,1)}, bf16[1,2,64,1152]{3,2,1,0:T(8,128)(2,1)S(1)}, u32[]{:S(2)}, u32[]{:S(2)}) collective-permute-start(bf16[1,2,64,1152]{3,2,1,0:T(8,128)(2,1)} %get-tuple-element.54), channel_id=1, source_target_pairs={{0,0},{1,1},{2,16},{3,17},{4,2},{5,3},{6,18},{7,19},{8,20},{9,21},... | collective-permute-start | bytes 884744 | tf_op jit(solution)/shard_map/ppermute | solution.py:482
  6.5 0.6 copy-done.5
  7.2 0.1 fusion.7
  7.2 2.2 %collective-permute-start = (s32[1,16]{1,0:T(1,128)S(1)}, s32[1,16]{1,0:T(1,128)S(1)}, u32[]{:S(2)}, u32[]{:S(2)}) collective-permute-start(s32[1,16]{1,0:T(1,128)S(1)} %fusion.7), channel_id=1, source_target_pairs={{0,8},{1,9},{2,10},{3,11},{4,12},{5,13},{6,14},{7,15},{8,0},{9,1},... | collective-permute-start | bytes 200 | tf_op jit(solution)/shard_map/ppermute | solution.py:460
  9.4 1.5 %collective-permute-start.8 = (bf16[144,432]{1,0:T(8,128)(2,1)}, bf16[144,432]{1,0:T(8,128)(2,1)S(1)}, u32[]{:S(2)}, u32[]{:S(2)}) collective-permute-start(bf16[144,432]{1,0:T(8,128)(2,1)} %get-tuple-element.60), channel_id=1, source_target_pairs={{0,1},{1,0},{2,3},{3,2},{4,5},{5,4},{6,7},{7,6},{8,9},{9,8},{10,11... | collective-permute-start | bytes 373256 | tf_op jit(solution)/shard_map/ppermute | solution.py:484
  10.9 2.5 %collective-permute-start.3 = (bf16[1,2,64,1152]{3,2,1,0:T(8,128)(2,1)}, bf16[1,2,64,1152]{3,2,1,0:T(8,128)(2,1)S(1)}, u32[]{:S(2)}, u32[]{:S(2)}) collective-permute-start(bf16[1,2,64,1152]{3,2,1,0:T(8,128)(2,1)} %get-tuple-element.55), channel_id=1, source_target_pairs={{0,2},{1,3},{2,18},{3,19},{4,0},{5,1},{6,16},{7,17},{8,22},{9,23},... | collective-permute-start | bytes 884744 | tf_op jit(solution)/shard_map/ppermute | solution.py:482
  13.5 1.5 %collective-permute-start.1 = (s32[2,16]{1,0:T(2,128)S(1)}, s32[2,16]{1,0:T(2,128)S(1)}, u32[]{:S(2)}, u32[]{:S(2)}) collective-permute-start(s32[2,16]{1,0:T(2,128)S(1)} %pad_add_fusion), channel_id=1, source_target_pairs={{0,16},{1,17},{2,18},{3,19},{4,20},{5,21},{6,22},{7,23},{8,24},{9,... | collective-permute-start | bytes 392 | tf_op jit(solution)/shard_map/ppermute | solution.py:462
  14.9 0.8 collective-permute-start.4
  15.8 1.3 %collective-permute-done.1 = s32[2,16]{1,0:T(2,128)S(1)} collective-permute-done((s32[2,16]{1,0:T(2,128)S(1)}, s32[2,16]{1,0:T(2,128)S(1)}, u32[]{:S(2)}, u32[]{:S(2)}) %collective-permute-start.1) | collective-permute-done | bytes 160 | tf_op jit(solution)/shard_map/ppermute | solution.py:462
  17.1 0.6 fusion.2.info_ref
  17.7 0.9 broadcast_select_fusion.1
  18.6 6.1 %collective-permute-done.3.refs_1_ = bf16[1,2,64,1152]{3,2,1,0:T(8,128)(2,1)S(1)} collective-permute-done((bf16[1,2,64,1152]{3,2,1,0:T(8,128)(2,1)}, bf16[1,2,64,1152]{3,2,1,0:T(8,128)(2,1)S(1)}, u32[]{:S(2)}, u32[]{:S(2)}) %collective-permute-start.3) | collective-permute-done | bytes 294944 | tf_op jit(solution)/shard_map/ppermute | solution.py:482
  24.7 1.0 collective-permute-start.6
  25.8 0.1 maximum_bitcast_fusion.2
  25.9 2.9 %collective-permute-start.9 = (bf16[1,144,864]{2,1,0:T(8,128)(2,1)S(1)}, bf16[1,144,864]{2,1,0:T(8,128)(2,1)S(1)}, u32[]{:S(2)}, u32[]{:S(2)}) collective-permute-start(bf16[1,144,864]{2,1,0:T(8,128)(2,1)S(1)} %maximum_bitcast_fusion.2), channel_id=1, source_target_pairs={{0,4},{1,5},{2,6},{3,7},{4,0},{5,1},{6,2},{7,3},{8,12},{9,13},{10,... | collective-permute-start | bytes 746504 | tf_op jit(solution)/shard_map/ppermute | solution.py:450
  28.8 0.1 pad_maximum_fusion.refs_0_
  28.9 0.1 collective-permute-start.5
  29.0 5.7 %collective-permute-done.6 = bf16[1,2,64,1152]{3,2,1,0:T(8,128)(2,1)S(1)} collective-permute-done((bf16[1,2,64,1152]{3,2,1,0:T(8,128)(2,1)S(1)}, bf16[1,2,64,1152]{3,2,1,0:T(8,128)(2,1)S(1)}, u32[]{:S(2)}, u32[]{:S(2)}) %collective-permute-start.6) | collective-permute-done | bytes 294944 | tf_op jit(solution)/shard_map/ppermute | solution.py:450
  34.6 0.1 pad_maximum_fusion.1.refs_2_
  34.7 0.6 collective-permute-start.7
  35.3 4.9 %collective-permute-done.9 = bf16[1,144,864]{2,1,0:T(8,128)(2,1)S(1)} collective-permute-done((bf16[1,144,864]{2,1,0:T(8,128)(2,1)S(1)}, bf16[1,144,864]{2,1,0:T(8,128)(2,1)S(1)}, u32[]{:S(2)}, u32[]{:S(2)}) %collective-permute-start.9) | collective-permute-done | bytes 248864 | tf_op jit(solution)/shard_map/ppermute | solution.py:450
  40.2 0.1 pad_maximum_fusion.2.refs_4_.refs_0_
  40.3 0.1 collective-permute-start.10
  40.4 4.4 %collective-permute-start.13 = (bf16[144,1152]{1,0:T(8,128)(2,1)S(1)}, bf16[144,1152]{1,0:T(8,128)(2,1)S(1)}, u32[]{:S(2)}, u32[]{:S(2)}) collective-permute-start(bf16[144,1152]{1,0:T(8,128)(2,1)S(1)} %copy-done.13), channel_id=1, source_target_pairs={{0,0},{1,1},{2,18},{3,19},{4,8},{5,9},{6,26},{7,27},{8,4},{9,5},{1... | collective-permute-start | bytes 995336 | tf_op jit(solution)/shard_map/ppermute | solution.py:497
  44.8 1.4 %collective-permute-done.5.refs_1_ = bf16[2,2,64,1152]{3,2,1,0:T(8,128)(2,1)S(1)} collective-permute-done((bf16[2,2,64,1152]{3,2,1,0:T(8,128)(2,1)S(1)}, bf16[2,2,64,1152]{3,2,1,0:T(8,128)(2,1)S(1)}, u32[]{:S(2)}, u32[]{:S(2)}) %collective-permute-start.5) | collective-permute-done | bytes 589856 | tf_op jit(solution)/shard_map/ppermute | solution.py:453
  46.2 6.7 %collective-permute-done.10.refs_5_.refs_1_ = bf16[2,144,864]{2,1,0:T(8,128)(2,1)S(1)} collective-permute-done((bf16[2,144,864]{2,1,0:T(8,128)(2,1)S(1)}, bf16[2,144,864]{2,1,0:T(8,128)(2,1)S(1)}, u32[]{:S(2)}, u32[]{:S(2)}) %collective-permute-start.10) | collective-permute-done | bytes 497696 | tf_op jit(solution)/shard_map/ppermute | solution.py:453
  52.9 0.1 collective-permute-start.11
  53.0 0.5 collective-permute-start.12
  53.5 4.3 %collective-permute-done.13.refs_8_ = bf16[144,1152]{1,0:T(8,128)(2,1)S(1)} collective-permute-done((bf16[144,1152]{1,0:T(8,128)(2,1)S(1)}, bf16[144,1152]{1,0:T(8,128)(2,1)S(1)}, u32[]{:S(2)}, u32[]{:S(2)}) %collective-permute-start.13) | collective-permute-done | bytes 331808 | tf_op jit(solution)/shard_map/ppermute | solution.py:497
  57.8 3.0 %collective-permute-start.14 = (bf16[144,1152]{1,0:T(8,128)(2,1)S(1)}, bf16[144,1152]{1,0:T(8,128)(2,1)S(1)}, u32[]{:S(2)}, u32[]{:S(2)}) collective-permute-start(bf16[144,1152]{1,0:T(8,128)(2,1)S(1)} %collective-permute-done.13.refs_8_), channel_id=1, source_target_pairs={{0,8},{1,9},{2,10},{3,11},{4,12},{5,13},{6,14},{7,15},{8,0},{9,1},... | collective-permute-start | bytes 995336 | tf_op jit(solution)/shard_map/ppermute | solution.py:525
  60.8 1.3 collective-permute-done.14.refs_9_
  62.1 0.7 copy-done.15
  62.8 0.2 copy-done.11
  63.0 0.8 copy-done.12
  63.9 11.9 %forward.1 = (bf16[2,8,64,144]{3,2,1,0:T(8,128)(2,1)}, bf16[2,8,64,144]{3,2,1,0:T(8,128)(2,1)}, bf16[2,8,64,144]{3,2,1,0:T(8,128)(2,1)}, bf16[2,8,64,144]{3,2,1,...) custom-call(s32[4]{0:T(128)} %pad_add_fusion.1.pos_ref, ...), custom_call_target="tpu_custom_call" | custom-call | flops 8257536000 | bytes 2359296 | tf_op jit(solution)/shard_map/forward/pallas_call | solution.py:529
  75.8 0.4 collective-permute-start.15
  76.2 1.6 %collective-permute-start.17 = (bf16[2,64,1152]{2,1,0:T(8,128)(2,1)}, bf16[2,64,1152]{2,1,0:T(8,128)(2,1)S(1)}, u32[]{:S(2)}, u32[]{:S(2)}) collective-permute-start(bf16[2,64,1152]{2,1,0:T(8,128)(2,1)} %get-tuple-element.82), channel_id=1, source_target_pairs={{0,1},{1,0},{2,3},{3,2},{4,5},{5,4},{6,7},{7,6},{8,9},{9,8},{10,11... | collective-permute-start | bytes 884744 | tf_op jit(solution)/shard_map/ppermute | solution.py:456
  77.8 1.9 %collective-permute-start.19 = (bf16[2,64,1152]{2,1,0:T(8,128)(2,1)}, bf16[2,64,1152]{2,1,0:T(8,128)(2,1)S(1)}, u32[]{:S(2)}, u32[]{:S(2)}) collective-permute-start(bf16[2,64,1152]{2,1,0:T(8,128)(2,1)} %get-tuple-element.84), channel_id=1, source_target_pairs={{0,17},{1,16},{2,19},{3,18},{4,21},{5,20},{6,23},{7,22},{8,25},{9,... | collective-permute-start | bytes 884744 | tf_op jit(solution)/shard_map/ppermute | solution.py:456
  79.7 1.2 slice_add_fusion
  80.8 0.1 collective-permute-start.16
  80.9 8.4 %backward.1 = (f32[2,64,1152]{2,1,0:T(8,128)}, bf16[2,64,1152]{2,1,0:T(8,128)(2,1)}, bf16[2,64,1152]{2,1,0:T(8,128)(2,1)}, bf16[2,64,1152]{2,1,0:T(8,128)(2,1)}) custom-call(s32[4]{0:T(128)} %pad_add_fusion.1.pos_ref, s32[16]{0:T(128)} %fusion.2.info_ref, bf16[2,144,864]{2,1,0:T(8,128)(2,1)} %copy-done.2, bf16[2,144,864]{2,1,0:T(8,128)(2,1)} %copy-done.10, ...), custom_call_target="tpu_custom_call" | custom-call | flops 5898240000 | bytes 2359296 | tf_op jit(solution)/shard_map/backward/pallas_call | solution.py:557
  89.3 3.7 %collective-permute-done.18.refs_4_ = bf16[2,64,1152]{2,1,0:T(8,128)(2,1)S(1)} collective-permute-done((bf16[2,64,1152]{2,1,0:T(8,128)(2,1)}, bf16[2,64,1152]{2,1,0:T(8,128)(2,1)S(1)}, u32[]{:S(2)}, u32[]{:S(2)}) %collective-permute-start.18) | collective-permute-done | bytes 294944 | tf_op jit(solution)/shard_map/ppermute | solution.py:456
  93.1 0.5 collective-permute-start.22
  93.6 1.2 collective-permute-start.23
  94.8 1.8 %collective-permute-start.24 = (bf16[2,64,1152]{2,1,0:T(8,128)(2,1)}, bf16[2,64,1152]{2,1,0:T(8,128)(2,1)S(1)}, u32[]{:S(2)}, u32[]{:S(2)}) collective-permute-start(bf16[2,64,1152]{2,1,0:T(8,128)(2,1)} %get-tuple-element.94), channel_id=1, source_target_pairs={{0,17},{1,16},{2,19},{3,18},{4,21},{5,20},{6,23},{7,22},{8,25},{9,... | collective-permute-start | bytes 884744 | tf_op jit(solution)/shard_map/ppermute | solution.py:456
  96.6 3.1 %output.1 = (bf16[64,1152]{1,0:T(8,128)(2,1)}, bf16[64,1152]{1,0:T(8,128)(2,1)}) custom-call(s32[4]{0:T(128)} %pad_add_fusion.1.pos_ref, s32[16]{0:T(128)} %fusion.2.info_ref, bf16[1,2,64,1152]{3,2,1,0:T(8,128)(2,1)} %copy-done.3, bf16[1,2,64,1152]{3,2,1,0:T(8,128)(2,1)} %copy-done.4, f32[2,64,1152]{2,1,0:T(8,128)} %get-tuple-element.85.refs_2_, ...), custom_call_target="tpu_custom_call" | custom-call | flops 11796480000 | bytes 2359296 | tf_op jit(solution)/shard_map/output/pallas_call | solution.py:570
  99.7 3.0 %collective-permute-start.20 = (bf16[64,1152]{1,0:T(8,128)(2,1)}, bf16[64,1152]{1,0:T(8,128)(2,1)S(1)}, u32[]{:S(2)}, u32[]{:S(2)}) collective-permute-start(bf16[64,1152]{1,0:T(8,128)(2,1)} %get-tuple-element.89), channel_id=1, source_target_pairs={{0,0},{1,1},{16,2},{17,3},{2,4},{3,5},{18,6},{19,7},{20,8},{21,9},... | collective-permute-start | bytes 442376 | tf_op jit(solution)/shard_map/ppermute | solution.py:443
  102.7 3.4 %collective-permute-start.21 = (bf16[64,1152]{1,0:T(8,128)(2,1)}, bf16[64,1152]{1,0:T(8,128)(2,1)S(1)}, u32[]{:S(2)}, u32[]{:S(2)}) collective-permute-start(bf16[64,1152]{1,0:T(8,128)(2,1)} %get-tuple-element.90), channel_id=1, source_target_pairs={{2,0},{3,1},{18,2},{19,3},{0,4},{1,5},{16,6},{17,7},{22,8},{23,9},... | collective-permute-start | bytes 442376 | tf_op jit(solution)/shard_map/ppermute | solution.py:443
  106.3 0.1 collective-permute-start.27
  106.4 1.5 %collective-permute-done.23.refs_4_ = bf16[2,64,1152]{2,1,0:T(8,128)(2,1)S(1)} collective-permute-done((bf16[2,64,1152]{2,1,0:T(8,128)(2,1)}, bf16[2,64,1152]{2,1,0:T(8,128)(2,1)S(1)}, u32[]{:S(2)}, u32[]{:S(2)}) %collective-permute-start.23) | collective-permute-done | bytes 294944 | tf_op jit(solution)/shard_map/ppermute | solution.py:456
  107.9 0.7 copy-done.20
  108.6 0.7 copy-done.21
  109.3 3.4 %input_grad.1 = (bf16[64,1152]{1,0:T(8,128)(2,1)}, bf16[64,1152]{1,0:T(8,128)(2,1)}) custom-call(s32[4]{0:T(128)} %pad_add_fusion.1.pos_ref, s32[16]{0:T(128)} %fusion.2.info_ref, bf16[1,2,64,1152]{3,2,1,0:T(8,128)(2,1)} %copy-done.3, bf16[1,2,64,1152]{3,2,1,0:T(8,128)(2,1)} %copy-done.4, f32[2,64,1152]{2,1,0:T(8,128)} %get-tuple-element.95.refs_2_, ...), custom_call_target="tpu_custom_call" | custom-call | flops 1769472000 | bytes 2359296 | tf_op jit(solution)/shard_map/input_grad/pallas_call | solution.py:582
  112.7 4.7 %collective-permute-start.25 = (bf16[64,1152]{1,0:T(8,128)(2,1)}, bf16[64,1152]{1,0:T(8,128)(2,1)S(1)}, u32[]{:S(2)}, u32[]{:S(2)}) collective-permute-start(bf16[64,1152]{1,0:T(8,128)(2,1)} %get-tuple-element.99), channel_id=1, source_target_pairs={{0,0},{1,1},{16,2},{17,3},{2,4},{3,5},{18,6},{19,7},{20,8},{21,9},... | collective-permute-start | bytes 442376 | tf_op jit(solution)/shard_map/ppermute | solution.py:443
  117.4 3.9 %collective-permute-start.26 = (bf16[64,1152]{1,0:T(8,128)(2,1)}, bf16[64,1152]{1,0:T(8,128)(2,1)S(1)}, u32[]{:S(2)}, u32[]{:S(2)}) collective-permute-start(bf16[64,1152]{1,0:T(8,128)(2,1)} %get-tuple-element.100), channel_id=1, source_target_pairs={{2,0},{3,1},{18,2},{19,3},{0,4},{1,5},{16,6},{17,7},{22,8},{23,9},... | collective-permute-start | bytes 442376 | tf_op jit(solution)/shard_map/ppermute | solution.py:443
  121.4 1.9 %collective-permute-start.28 = (f32[48,864]{1,0:T(8,128)S(1)}, f32[48,864]{1,0:T(8,128)S(1)}, u32[]{:S(2)}, u32[]{:S(2)}) collective-permute-start(f32[48,864]{1,0:T(8,128)S(1)} %bitcast.28), channel_id=1, source_target_pairs={{0,0},{1,1},{2,8},{3,9},{4,16},{5,17},{6,24},{7,25},{8,4},{9,5},{1... | collective-permute-start | bytes 497672 | tf_op jit(solution)/shard_map/ppermute | solution.py:598
  123.3 3.2 %collective-permute-done.26 = bf16[64,1152]{1,0:T(8,128)(2,1)S(1)} collective-permute-done((bf16[64,1152]{1,0:T(8,128)(2,1)}, bf16[64,1152]{1,0:T(8,128)(2,1)S(1)}, u32[]{:S(2)}, u32[]{:S(2)}) %collective-permute-start.26) | collective-permute-done | bytes 147488 | tf_op jit(solution)/shard_map/ppermute | solution.py:443
  126.6 0.7 maximum_bitcast_fusion.1
  127.4 0.7 maximum_bitcast_fusion
  128.1 2.6 %collective-permute-done.28 = f32[48,864]{1,0:T(8,128)S(1)} collective-permute-done((f32[48,864]{1,0:T(8,128)S(1)}, f32[48,864]{1,0:T(8,128)S(1)}, u32[]{:S(2)}, u32[]{:S(2)}) %collective-permute-start.28) | collective-permute-done | bytes 165920 | tf_op jit(solution)/shard_map/ppermute | solution.py:598
  130.7 0.1 fusion.6
  130.8 0.7 maximum_multiply_fusion
  (61 shorter events, 0.3 us)
Async XLA Ops:
  4.5 10.4 %collective-permute-start.2 = (bf16[1,2,64,1152]{3,2,1,0:T(8,128)(2,1)}, bf16[1,2,64,1152]{3,2,1,0:T(8,128)(2,1)S(1)}, u32[]{:S(2)}, u32[]{:S(2)}) collective-permute-start(bf16[1,2,64,1152]{3,2,1,0:T(8,128)(2,1)} %get-tuple-element.54), channel_id=1, source_target_pairs={{0,0},{1,1},{2,16},{3,17},{4,2},{5,3},{6,18},{7,19},{8,20},{9,21},... | collective-permute-start | bytes 884744 | tf_op jit(solution)/shard_map/ppermute | solution.py:482
  6.5 0.7 copy-start.5
  6.5 0.7 copy-start.6
  6.5 0.7 copy-start.7
  7.2 6.2 %collective-permute-start = (s32[1,16]{1,0:T(1,128)S(1)}, s32[1,16]{1,0:T(1,128)S(1)}, u32[]{:S(2)}, u32[]{:S(2)}) collective-permute-start(s32[1,16]{1,0:T(1,128)S(1)} %fusion.7), channel_id=1, source_target_pairs={{0,8},{1,9},{2,10},{3,11},{4,12},{5,13},{6,14},{7,15},{8,0},{9,1},... | collective-permute-start | bytes 200 | tf_op jit(solution)/shard_map/ppermute | solution.py:460
  9.4 8.3 %collective-permute-start.8 = (bf16[144,432]{1,0:T(8,128)(2,1)}, bf16[144,432]{1,0:T(8,128)(2,1)S(1)}, u32[]{:S(2)}, u32[]{:S(2)}) collective-permute-start(bf16[144,432]{1,0:T(8,128)(2,1)} %get-tuple-element.60), channel_id=1, source_target_pairs={{0,1},{1,0},{2,3},{3,2},{4,5},{5,4},{6,7},{7,6},{8,9},{9,8},{10,11... | collective-permute-start | bytes 373256 | tf_op jit(solution)/shard_map/ppermute | solution.py:484
  10.9 13.9 %collective-permute-start.3 = (bf16[1,2,64,1152]{3,2,1,0:T(8,128)(2,1)}, bf16[1,2,64,1152]{3,2,1,0:T(8,128)(2,1)S(1)}, u32[]{:S(2)}, u32[]{:S(2)}) collective-permute-start(bf16[1,2,64,1152]{3,2,1,0:T(8,128)(2,1)} %get-tuple-element.55), channel_id=1, source_target_pairs={{0,2},{1,3},{2,18},{3,19},{4,0},{5,1},{6,16},{7,17},{8,22},{9,23},... | collective-permute-start | bytes 884744 | tf_op jit(solution)/shard_map/ppermute | solution.py:482
  13.5 3.6 %collective-permute-start.1 = (s32[2,16]{1,0:T(2,128)S(1)}, s32[2,16]{1,0:T(2,128)S(1)}, u32[]{:S(2)}, u32[]{:S(2)}) collective-permute-start(s32[2,16]{1,0:T(2,128)S(1)} %pad_add_fusion), channel_id=1, source_target_pairs={{0,16},{1,17},{2,18},{3,19},{4,20},{5,21},{6,22},{7,23},{8,24},{9,... | collective-permute-start | bytes 392 | tf_op jit(solution)/shard_map/ppermute | solution.py:462
  14.9 13.9 %copy-start.3 = (bf16[1,2,64,1152]{3,2,1,0:T(8,128)(2,1)}, bf16[1,2,64,1152]{3,2,1,0:T(8,128)(2,1)S(1)}, u32[]{:S(2)}) copy-start(bf16[1,2,64,1152]{3,2,1,0:T(8,128)(2,1)S(1)} %collective-permute-done.2.refs_0_) | copy-start | bytes 884740
  14.9 9.8 %collective-permute-start.4 = (bf16[1,2,64,1152]{3,2,1,0:T(8,128)(2,1)S(1)}, bf16[1,2,64,1152]{3,2,1,0:T(8,128)(2,1)S(1)}, u32[]{:S(2)}, u32[]{:S(2)}) collective-permute-start(bf16[1,2,64,1152]{3,2,1,0:T(8,128)(2,1)S(1)} %collective-permute-done.2.refs_0_), channel_id=1, source_target_pairs={{0,1},{1,0},{2,3},{3,2},{4,5},{5,4},{6,7},{7,6},{8,9},{9,8},{10,11... | collective-permute-start | bytes 884744 | tf_op jit(solution)/shard_map/ppermute | solution.py:492
  24.7 9.9 %copy-start.4 = (bf16[1,2,64,1152]{3,2,1,0:T(8,128)(2,1)}, bf16[1,2,64,1152]{3,2,1,0:T(8,128)(2,1)S(1)}, u32[]{:S(2)}) copy-start(bf16[1,2,64,1152]{3,2,1,0:T(8,128)(2,1)S(1)} %collective-permute-done.3.refs_1_) | copy-start | bytes 884740
  24.7 9.9 %collective-permute-start.6 = (bf16[1,2,64,1152]{3,2,1,0:T(8,128)(2,1)S(1)}, bf16[1,2,64,1152]{3,2,1,0:T(8,128)(2,1)S(1)}, u32[]{:S(2)}, u32[]{:S(2)}) collective-permute-start(bf16[1,2,64,1152]{3,2,1,0:T(8,128)(2,1)S(1)} %collective-permute-done.3.refs_1_), channel_id=1, source_target_pairs={{0,16},{1,17},{2,18},{3,19},{4,20},{5,21},{6,22},{7,23},{8,24},{9,... | collective-permute-start | bytes 884744 | tf_op jit(solution)/shard_map/ppermute | solution.py:450
  25.9 14.4 %collective-permute-start.9 = (bf16[1,144,864]{2,1,0:T(8,128)(2,1)S(1)}, bf16[1,144,864]{2,1,0:T(8,128)(2,1)S(1)}, u32[]{:S(2)}, u32[]{:S(2)}) collective-permute-start(bf16[1,144,864]{2,1,0:T(8,128)(2,1)S(1)} %maximum_bitcast_fusion.2), channel_id=1, source_target_pairs={{0,4},{1,5},{2,6},{3,7},{4,0},{5,1},{6,2},{7,3},{8,12},{9,13},{10,... | collective-permute-start | bytes 746504 | tf_op jit(solution)/shard_map/ppermute | solution.py:450
  28.9 5.8 %copy-start = (bf16[2,2,64,1152]{3,2,1,0:T(8,128)(2,1)}, bf16[2,2,64,1152]{3,2,1,0:T(8,128)(2,1)S(1)}, u32[]{:S(2)}) copy-start(bf16[2,2,64,1152]{3,2,1,0:T(8,128)(2,1)S(1)} %pad_maximum_fusion.refs_0_) | copy-start | bytes 1769476
  28.9 17.3 %collective-permute-start.5 = (bf16[2,2,64,1152]{3,2,1,0:T(8,128)(2,1)S(1)}, bf16[2,2,64,1152]{3,2,1,0:T(8,128)(2,1)S(1)}, u32[]{:S(2)}, u32[]{:S(2)}) collective-permute-start(bf16[2,2,64,1152]{3,2,1,0:T(8,128)(2,1)S(1)} %pad_maximum_fusion.refs_0_), channel_id=1, source_target_pairs={{0,16},{1,17},{2,18},{3,19},{4,20},{5,21},{6,22},{7,23},{8,24},{9,... | collective-permute-start | bytes 1769480 | tf_op jit(solution)/shard_map/ppermute | solution.py:453
  34.7 27.4 %copy-start.1 = (bf16[2,2,64,1152]{3,2,1,0:T(8,128)(2,1)}, bf16[2,2,64,1152]{3,2,1,0:T(8,128)(2,1)S(1)}, u32[]{:S(2)}) copy-start(bf16[2,2,64,1152]{3,2,1,0:T(8,128)(2,1)S(1)} %pad_maximum_fusion.1.refs_2_) | copy-start | bytes 1769476
  34.7 5.7 %copy-start.13 = (bf16[144,1152]{1,0:T(8,128)(2,1)S(1)}, bf16[144,1152]{1,0:T(8,128)(2,1)}, u32[]{:S(2)}) copy-start(bf16[144,1152]{1,0:T(8,128)(2,1)} %param.15) | copy-start | bytes 995332
  34.7 18.2 %collective-permute-start.7 = (bf16[2,2,64,1152]{3,2,1,0:T(8,128)(2,1)S(1)}, bf16[2,2,64,1152]{3,2,1,0:T(8,128)(2,1)S(1)}, u32[]{:S(2)}, u32[]{:S(2)}) collective-permute-start(bf16[2,2,64,1152]{3,2,1,0:T(8,128)(2,1)S(1)} %pad_maximum_fusion.1.refs_2_), channel_id=1, source_target_pairs={{0,1},{1,0},{2,3},{3,2},{4,5},{5,4},{6,7},{7,6},{8,9},{9,8},{10,11... | collective-permute-start | bytes 1769480 | tf_op jit(solution)/shard_map/ppermute | solution.py:453
  40.3 21.8 %copy-start.2 = (bf16[2,144,864]{2,1,0:T(8,128)(2,1)}, bf16[2,144,864]{2,1,0:T(8,128)(2,1)S(1)}, u32[]{:S(2)}) copy-start(bf16[2,144,864]{2,1,0:T(8,128)(2,1)S(1)} %pad_maximum_fusion.2.refs_4_.refs_0_) | copy-start | bytes 1492996
  40.3 12.6 %collective-permute-start.10 = (bf16[2,144,864]{2,1,0:T(8,128)(2,1)S(1)}, bf16[2,144,864]{2,1,0:T(8,128)(2,1)S(1)}, u32[]{:S(2)}, u32[]{:S(2)}) collective-permute-start(bf16[2,144,864]{2,1,0:T(8,128)(2,1)S(1)} %pad_maximum_fusion.2.refs_4_.refs_0_), channel_id=1, source_target_pairs={{0,2},{1,3},{2,0},{3,1},{4,6},{5,7},{6,4},{7,5},{8,10},{9,11},{10,... | collective-permute-start | bytes 1493000 | tf_op jit(solution)/shard_map/ppermute | solution.py:453
  40.4 17.4 %collective-permute-start.13 = (bf16[144,1152]{1,0:T(8,128)(2,1)S(1)}, bf16[144,1152]{1,0:T(8,128)(2,1)S(1)}, u32[]{:S(2)}, u32[]{:S(2)}) collective-permute-start(bf16[144,1152]{1,0:T(8,128)(2,1)S(1)} %copy-done.13), channel_id=1, source_target_pairs={{0,0},{1,1},{2,18},{3,19},{4,8},{5,9},{6,26},{7,27},{8,4},{9,5},{1... | collective-permute-start | bytes 995336 | tf_op jit(solution)/shard_map/ppermute | solution.py:497
  46.2 15.9 %copy-start.8 = (bf16[2,2,64,1152]{3,2,1,0:T(8,128)(2,1)}, bf16[2,2,64,1152]{3,2,1,0:T(8,128)(2,1)S(1)}, u32[]{:S(2)}) copy-start(bf16[2,2,64,1152]{3,2,1,0:T(8,128)(2,1)S(1)} %collective-permute-done.5.refs_1_) | copy-start | bytes 1769476
  52.9 9.2 %copy-start.10 = (bf16[2,144,864]{2,1,0:T(8,128)(2,1)}, bf16[2,144,864]{2,1,0:T(8,128)(2,1)S(1)}, u32[]{:S(2)}) copy-start(bf16[2,144,864]{2,1,0:T(8,128)(2,1)S(1)} %collective-permute-done.10.refs_5_.refs_1_) | copy-start | bytes 1492996
  52.9 9.2 %copy-start.9 = (bf16[2,2,64,1152]{3,2,1,0:T(8,128)(2,1)}, bf16[2,2,64,1152]{3,2,1,0:T(8,128)(2,1)S(1)}, u32[]{:S(2)}) copy-start(bf16[2,2,64,1152]{3,2,1,0:T(8,128)(2,1)S(1)} %collective-permute-done.7.refs_3_) | copy-start | bytes 1769476
  52.9 9.1 %collective-permute-start.11 = (bf16[2,144,864]{2,1,0:T(8,128)(2,1)S(1)}, bf16[2,144,864]{2,1,0:T(8,128)(2,1)S(1)}, u32[]{:S(2)}, u32[]{:S(2)}) collective-permute-start(bf16[2,144,864]{2,1,0:T(8,128)(2,1)S(1)} %pad_maximum_fusion.2.refs_4_.refs_0_), channel_id=1, source_target_pairs={{0,8},{1,9},{2,10},{3,11},{4,12},{5,13},{6,14},{7,15},{8,0},{9,1},... | collective-permute-start | bytes 1493000 | tf_op jit(solution)/shard_map/ppermute | solution.py:505
  53.0 9.1 %collective-permute-start.12 = (bf16[2,144,864]{2,1,0:T(8,128)(2,1)S(1)}, bf16[2,144,864]{2,1,0:T(8,128)(2,1)S(1)}, u32[]{:S(2)}, u32[]{:S(2)}) collective-permute-start(bf16[2,144,864]{2,1,0:T(8,128)(2,1)S(1)} %collective-permute-done.10.refs_5_.refs_1_), channel_id=1, source_target_pairs={{0,8},{1,9},{2,10},{3,11},{4,12},{5,13},{6,14},{7,15},{8,0},{9,1},... | collective-permute-start | bytes 1493000 | tf_op jit(solution)/shard_map/ppermute | solution.py:505
  57.8 4.3 %copy-start.14 = (bf16[144,1152]{1,0:T(8,128)(2,1)}, bf16[144,1152]{1,0:T(8,128)(2,1)S(1)}, u32[]{:S(2)}) copy-start(bf16[144,1152]{1,0:T(8,128)(2,1)S(1)} %collective-permute-done.13.refs_8_) | copy-start | bytes 995332
  57.8 4.2 %collective-permute-start.14 = (bf16[144,1152]{1,0:T(8,128)(2,1)S(1)}, bf16[144,1152]{1,0:T(8,128)(2,1)S(1)}, u32[]{:S(2)}, u32[]{:S(2)}) collective-permute-start(bf16[144,1152]{1,0:T(8,128)(2,1)S(1)} %collective-permute-done.13.refs_8_), channel_id=1, source_target_pairs={{0,8},{1,9},{2,10},{3,11},{4,12},{5,13},{6,14},{7,15},{8,0},{9,1},... | collective-permute-start | bytes 995336 | tf_op jit(solution)/shard_map/ppermute | solution.py:525
  62.1 0.7 copy-start.15
  62.1 1.0 copy-start.11
  63.0 0.8 copy-start.12
  75.8 3.9 %collective-permute-start.15 = (f32[4,48,864]{2,1,0:T(8,128)}, f32[4,48,864]{2,1,0:T(8,128)S(1)}, u32[]{:S(2)}, u32[]{:S(2)}) collective-permute-start(f32[4,48,864]{2,1,0:T(8,128)} %get-tuple-element.74), channel_id=1, source_target_pairs={{0,8},{1,9},{2,10},{3,11},{4,12},{5,13},{6,14},{7,15},{8,0},{9,1},... | collective-permute-start | bytes 1990664 | tf_op jit(solution)/shard_map/ppermute | solution.py:549
  76.2 13.1 %collective-permute-start.17 = (bf16[2,64,1152]{2,1,0:T(8,128)(2,1)}, bf16[2,64,1152]{2,1,0:T(8,128)(2,1)S(1)}, u32[]{:S(2)}, u32[]{:S(2)}) collective-permute-start(bf16[2,64,1152]{2,1,0:T(8,128)(2,1)} %get-tuple-element.82), channel_id=1, source_target_pairs={{0,1},{1,0},{2,3},{3,2},{4,5},{5,4},{6,7},{7,6},{8,9},{9,8},{10,11... | collective-permute-start | bytes 884744 | tf_op jit(solution)/shard_map/ppermute | solution.py:456
  77.8 15.3 %collective-permute-start.18 = (bf16[2,64,1152]{2,1,0:T(8,128)(2,1)}, bf16[2,64,1152]{2,1,0:T(8,128)(2,1)S(1)}, u32[]{:S(2)}, u32[]{:S(2)}) collective-permute-start(bf16[2,64,1152]{2,1,0:T(8,128)(2,1)} %get-tuple-element.83), channel_id=1, source_target_pairs={{0,16},{1,17},{2,18},{3,19},{4,20},{5,21},{6,22},{7,23},{8,24},{9,... | collective-permute-start | bytes 884744 | tf_op jit(solution)/shard_map/ppermute | solution.py:456
  77.8 15.3 %collective-permute-start.19 = (bf16[2,64,1152]{2,1,0:T(8,128)(2,1)}, bf16[2,64,1152]{2,1,0:T(8,128)(2,1)S(1)}, u32[]{:S(2)}, u32[]{:S(2)}) collective-permute-start(bf16[2,64,1152]{2,1,0:T(8,128)(2,1)} %get-tuple-element.84), channel_id=1, source_target_pairs={{0,17},{1,16},{2,19},{3,18},{4,21},{5,20},{6,23},{7,22},{8,25},{9,... | collective-permute-start | bytes 884744 | tf_op jit(solution)/shard_map/ppermute | solution.py:456
  80.8 12.2 %collective-permute-start.16 = (f32[2,48,864]{2,1,0:T(8,128)S(1)}, f32[2,48,864]{2,1,0:T(8,128)S(1)}, u32[]{:S(2)}, u32[]{:S(2)}) collective-permute-start(f32[2,48,864]{2,1,0:T(8,128)S(1)} %get-tuple-element.80), channel_id=1, source_target_pairs={{0,2},{1,3},{2,0},{3,1},{4,6},{5,7},{6,4},{7,5},{8,10},{9,11},{10,... | collective-permute-start | bytes 995336 | tf_op jit(solution)/shard_map/ppermute | solution.py:555
  89.3 7.3 %copy-start.16 = (bf16[2,64,1152]{2,1,0:T(8,128)(2,1)}, bf16[2,64,1152]{2,1,0:T(8,128)(2,1)S(1)}, u32[]{:S(2)}) copy-start(bf16[2,64,1152]{2,1,0:T(8,128)(2,1)S(1)} %collective-permute-done.17.refs_3_) | copy-start | bytes 884740
  93.1 3.6 %copy-start.17 = (bf16[2,64,1152]{2,1,0:T(8,128)(2,1)}, bf16[2,64,1152]{2,1,0:T(8,128)(2,1)S(1)}, u32[]{:S(2)}) copy-start(bf16[2,64,1152]{2,1,0:T(8,128)(2,1)S(1)} %collective-permute-done.18.refs_4_) | copy-start | bytes 884740
  93.1 3.6 %copy-start.18 = (bf16[2,64,1152]{2,1,0:T(8,128)(2,1)}, bf16[2,64,1152]{2,1,0:T(8,128)(2,1)S(1)}, u32[]{:S(2)}) copy-start(bf16[2,64,1152]{2,1,0:T(8,128)(2,1)S(1)} %collective-permute-done.19.refs_5_) | copy-start | bytes 884740
  93.1 13.2 %collective-permute-start.22 = (bf16[2,64,1152]{2,1,0:T(8,128)(2,1)}, bf16[2,64,1152]{2,1,0:T(8,128)(2,1)S(1)}, u32[]{:S(2)}, u32[]{:S(2)}) collective-permute-start(bf16[2,64,1152]{2,1,0:T(8,128)(2,1)} %get-tuple-element.92), channel_id=1, source_target_pairs={{0,1},{1,0},{2,3},{3,2},{4,5},{5,4},{6,7},{7,6},{8,9},{9,8},{10,11... | collective-permute-start | bytes 884744 | tf_op jit(solution)/shard_map/ppermute | solution.py:456
  93.6 14.3 %collective-permute-start.23 = (bf16[2,64,1152]{2,1,0:T(8,128)(2,1)}, bf16[2,64,1152]{2,1,0:T(8,128)(2,1)S(1)}, u32[]{:S(2)}, u32[]{:S(2)}) collective-permute-start(bf16[2,64,1152]{2,1,0:T(8,128)(2,1)} %get-tuple-element.93), channel_id=1, source_target_pairs={{0,16},{1,17},{2,18},{3,19},{4,20},{5,21},{6,22},{7,23},{8,24},{9,... | collective-permute-start | bytes 884744 | tf_op jit(solution)/shard_map/ppermute | solution.py:456
  94.8 13.1 %collective-permute-start.24 = (bf16[2,64,1152]{2,1,0:T(8,128)(2,1)}, bf16[2,64,1152]{2,1,0:T(8,128)(2,1)S(1)}, u32[]{:S(2)}, u32[]{:S(2)}) collective-permute-start(bf16[2,64,1152]{2,1,0:T(8,128)(2,1)} %get-tuple-element.94), channel_id=1, source_target_pairs={{0,17},{1,16},{2,19},{3,18},{4,21},{5,20},{6,23},{7,22},{8,25},{9,... | collective-permute-start | bytes 884744 | tf_op jit(solution)/shard_map/ppermute | solution.py:456
  99.7 23.6 %collective-permute-start.20 = (bf16[64,1152]{1,0:T(8,128)(2,1)}, bf16[64,1152]{1,0:T(8,128)(2,1)S(1)}, u32[]{:S(2)}, u32[]{:S(2)}) collective-permute-start(bf16[64,1152]{1,0:T(8,128)(2,1)} %get-tuple-element.89), channel_id=1, source_target_pairs={{0,0},{1,1},{16,2},{17,3},{2,4},{3,5},{18,6},{19,7},{20,8},{21,9},... | collective-permute-start | bytes 442376 | tf_op jit(solution)/shard_map/ppermute | solution.py:443
  102.7 20.6 %collective-permute-start.21 = (bf16[64,1152]{1,0:T(8,128)(2,1)}, bf16[64,1152]{1,0:T(8,128)(2,1)S(1)}, u32[]{:S(2)}, u32[]{:S(2)}) collective-permute-start(bf16[64,1152]{1,0:T(8,128)(2,1)} %get-tuple-element.90), channel_id=1, source_target_pairs={{2,0},{3,1},{18,2},{19,3},{0,4},{1,5},{16,6},{17,7},{22,8},{23,9},... | collective-permute-start | bytes 442376 | tf_op jit(solution)/shard_map/ppermute | solution.py:443
  106.3 1.6 %copy-start.19 = (bf16[2,64,1152]{2,1,0:T(8,128)(2,1)}, bf16[2,64,1152]{2,1,0:T(8,128)(2,1)S(1)}, u32[]{:S(2)}) copy-start(bf16[2,64,1152]{2,1,0:T(8,128)(2,1)S(1)} %collective-permute-done.22.refs_3_) | copy-start | bytes 884740
  106.3 15.1 %collective-permute-start.27 = (f32[1,48,864]{2,1,0:T(8,128)S(1)}, f32[1,48,864]{2,1,0:T(8,128)S(1)}, u32[]{:S(2)}, u32[]{:S(2)}) collective-permute-start(f32[1,48,864]{2,1,0:T(8,128)S(1)} %slice.40), channel_id=1, source_target_pairs={{0,4},{1,5},{2,6},{3,7},{4,0},{5,1},{6,2},{7,3},{8,12},{9,13},{10,... | collective-permute-start | bytes 497672 | tf_op jit(solution)/shard_map/ppermute | solution.py:596
  107.9 0.7 copy-start.20
  108.6 0.7 copy-start.21
  112.7 10.6 %collective-permute-start.25 = (bf16[64,1152]{1,0:T(8,128)(2,1)}, bf16[64,1152]{1,0:T(8,128)(2,1)S(1)}, u32[]{:S(2)}, u32[]{:S(2)}) collective-permute-start(bf16[64,1152]{1,0:T(8,128)(2,1)} %get-tuple-element.99), channel_id=1, source_target_pairs={{0,0},{1,1},{16,2},{17,3},{2,4},{3,5},{18,6},{19,7},{20,8},{21,9},... | collective-permute-start | bytes 442376 | tf_op jit(solution)/shard_map/ppermute | solution.py:443
  117.4 9.1 %collective-permute-start.26 = (bf16[64,1152]{1,0:T(8,128)(2,1)}, bf16[64,1152]{1,0:T(8,128)(2,1)S(1)}, u32[]{:S(2)}, u32[]{:S(2)}) collective-permute-start(bf16[64,1152]{1,0:T(8,128)(2,1)} %get-tuple-element.100), channel_id=1, source_target_pairs={{2,0},{3,1},{18,2},{19,3},{0,4},{1,5},{16,6},{17,7},{22,8},{23,9},... | collective-permute-start | bytes 442376 | tf_op jit(solution)/shard_map/ppermute | solution.py:443
  121.4 9.3 %collective-permute-start.28 = (f32[48,864]{1,0:T(8,128)S(1)}, f32[48,864]{1,0:T(8,128)S(1)}, u32[]{:S(2)}, u32[]{:S(2)}) collective-permute-start(f32[48,864]{1,0:T(8,128)S(1)} %bitcast.28), channel_id=1, source_target_pairs={{0,0},{1,1},{2,8},{3,9},{4,16},{5,17},{6,24},{7,25},{8,4},{9,5},{1... | collective-permute-start | bytes 497672 | tf_op jit(solution)/shard_map/ppermute | solution.py:598

commit v17 on v16

--- a/solution.py
+++ b/solution.py
@@ -171,13 +171,15 @@
     return part.reshape(part.shape[0] * BLOCK, part.shape[2])
 
 
-def start_kernel(lay, cols, pos_ref, x_ref, g_ref, w_ref, *refs):
-    pair_refs, out_refs = refs[: lay.nc], refs[lay.nc :]
+def halves_kernel(lay, pos_ref, x_ref, g_ref, *pair_refs):
     half = x_ref.shape[1] // lay.nc
     for k, ref in enumerate(pair_refs):
         first = pl.multiple_of(((pos_ref[2] // lay.ny) ^ k) * half, 16)
         ref[0, 0] = x_ref[0, pl.ds(first, half), :]
         ref[0, 1] = g_ref[0, pl.ds(first, half), :]
+
+
+def pick_kernel(lay, cols, pos_ref, w_ref, *out_refs):
     model = w_ref.shape[1] // 3
     for k, out_ref in enumerate(out_refs):
         chip_x = pos_ref[3] ^ k
@@ -456,6 +458,18 @@
         got = [lax.ppermute(parts[k], AXES, chip_swap(k)) for k in range(1, chips)]
         return [parts[0]] + got
 
+    pos = jnp.stack([y, c, z, x]).astype(jnp.int32)
+    pair_shape = (1, 2, half, model)
+    pairs = call(
+        functools.partial(halves_kernel, lay),
+        "halves",
+        model,
+        [whole_spec(frames_x.shape)] * 2,
+        [whole_spec(pair_shape)] * nc,
+        [struct(pair_shape)] * nc,
+        prefetch=1,
+    )(pos, frames_x, grad_y)
+    w_qkv, clip_ids, _ = lax.optimization_barrier((w_qkv, clip_ids, pairs))
     info = jnp.concatenate([clip_ids[0], clip_patches[0], clip_step[0]])[None]
     by_core = jnp.concatenate([info, lax.ppermute(info, AXES, lay.swap(kc=1))], axis=0)
     info = [by_core] + [
@@ -467,18 +481,15 @@
         for ky in range(lay.ny)
         for kc in range(nc)
     )
-    pos = jnp.stack([y, c, z, x]).astype(jnp.int32)
-    pair_shape = (1, 2, half, model)
-    outputs = call(
-        functools.partial(start_kernel, lay, cols),
-        "start",
-        2 * model * 1000,
-        [whole_spec(frames_x.shape)] * 2 + [whole_spec(w_qkv.shape)],
-        [whole_spec(pair_shape)] * nc + [whole_spec((rows, 3 * cols))] * nx,
-        [struct(pair_shape)] * nc + [struct((rows, 3 * cols))] * nx,
+    picked = call(
+        functools.partial(pick_kernel, lay, cols),
+        "pick",
+        20 * model * 1000,
+        [whole_spec(w_qkv.shape)],
+        [whole_spec((rows, 3 * cols))] * nx,
+        [struct((rows, 3 * cols))] * nx,
         prefetch=1,
-    )(pos, frames_x, grad_y, w_qkv)
-    pairs, picked = outputs[:nc], outputs[nc:]
+    )(pos, w_qkv)
     own = [lax.ppermute(pair, AXES, lay.to_plane(k)) for k, pair in enumerate(pairs)]
     by_x = [picked[0]] + [
         lax.ppermute(picked[kx], AXES, lay.swap(kx=kx)) for kx in range(1, nx)
@@ -578,7 +589,11 @@
     )(pos, info, *own, *projected, mod_table)
     out_y = from_plane(out_parts)
 
-    grad_hidden, _ = lax.optimization_barrier((grad_hidden, out_parts))
+    cut = cut + first_away
+    for bit in lay.bits(lay.nz)[1:]:
+        middle = middle // 2
+        cut = cut[:middle] + lax.ppermute(cut[middle:], AXES, lay.swap(kz=bit))
+    grad_hidden, cut, _ = lax.optimization_barrier((grad_hidden, cut, out_parts))
     grad_parts = call(
         functools.partial(input_grad_kernel, lay),
         "input_grad",
@@ -590,10 +605,6 @@
     )(pos, info, *own, *grad_hidden, mod_table)
     grad_x = from_plane(grad_parts)
 
-    cut, _ = lax.optimization_barrier((cut + first_away, out_parts))
-    for bit in lay.bits(lay.nz)[1:]:
-        middle = middle // 2
-        cut = cut[:middle] + lax.ppermute(cut[middle:], AXES, lay.swap(kz=bit))
     cut, _ = lax.optimization_barrier((cut, grad_parts))
     grad_w = lax.ppermute(cut[0], AXES, lay.to_owner())
     grad_w = jnp.concatenate(

time: 134 us -> 138 us (1.030)
  Pallas kernels: 30.1 us -> 32.2 us
    ppermute x2, waiting for transfers between devices: 6.08 us -> 0.01 us  [local(): lax.ppermute(pair, AXES, lay.to_plane(k))]
    ppermute x1, waiting for transfers between devices: 0.01 us -> 4.88 us  [local(): first = lax.ppermute(own[0], AXES, chip_swap(lay.chip_bits(0)[0]))]
    ppermute x1, starting transfers between devices: 2.97 us -> 0.01 us  [local(): wo_rows = [wo_own, lax.ppermute(wo_own, AXES, lay.swap(kc=1))]]
    ppermute x3, starting transfers between devices: 0.77 us -> 3.7 us  [doubling(): return [held, lax.ppermute(held, AXES, swap(bits[-1]))]]
    ppermute x2, waiting for transfers between devices: 10.6 us -> 8.21 us  [doubling(): got = lax.ppermute(held, AXES, swap(bit)) if first is None else first]
    ppermute x2, starting transfers between devices: 4.4 us -> 6.62 us  [local(): lax.ppermute(pair, AXES, lay.to_plane(k))]
    ppermute x1, waiting for transfers between devices: 4.34 us -> 6.53 us  [local(): wo_own = lax.ppermute(late_w_out, AXES, lay.rows_to_chip())]
    pallas_call x1 -> x2, Pallas kernels: 3.3 us -> 5.44 us  [the longest x1 2.87 us: local(): call(functools.partial(pick_kernel, lay, cols), 'pick', 20 * model * 1000...]
  transfers between devices with their start and end apart: 29 -> 29, of which waited for: 12 -> 13; matrix products, arithmetic and copies ran while one was open for 4% -> 3% of each run, Pallas kernels for 11% -> 13%
where the time goes in v17:
time: 138 us; the launch traced here: 136 us
  starting transfers between devices  48.3 us (35%)
  waiting for transfers between devices  43.3 us (31%)
  Pallas kernels  32.2 us (23%)
  other arithmetic  6.04 us (4%)
  local copies, waits for them, and re-layouts  4.95 us (4%)
    ppermute x4, starting transfers between devices, from_plane(): lax.ppermute(part, AXES, lay.from_plane(k))  15.1 us
    pallas_call x1, Pallas kernels, local(): call(functools.partial(forward_kernel, lay), 'forward', 14 * model * 1000...  11.9 us
    ppermute x3, waiting for transfers between devices, doubling(): return [held, lax.ppermute(held, AXES, swap(bits[-1]))]  8.64 us
    pallas_call x1, Pallas kernels, local(): call(functools.partial(backward_kernel, lay), 'backward', 10 * model * 10...  8.38 us
    ppermute x2, waiting for transfers between devices, doubling(): got = lax.ppermute(held, AXES, swap(bit)) if first is None else first  8.21 us
    ppermute x6, starting transfers between devices, over_chips(): got = [lax.ppermute(parts[k], AXES, chip_swap(k)) for k in range(1, chips)]  6.99 us
    ppermute x2, starting transfers between devices, local(): lax.ppermute(pair, AXES, lay.to_plane(k))  6.62 us
    ppermute x1, waiting for transfers between devices, local(): wo_own = lax.ppermute(late_w_out, AXES, lay.rows_to_chip())  6.53 us
  transfers between devices with their start and end apart: 29, of which 13 were waited for; matrix products, arithmetic and copies ran while one was open for 3% of the time, Pallas kernels for 13%

profile of v17, /device:TPU:4, one launch (start us, length us, event | category | flops | bytes accessed | tf_op | source)
XLA Modules:
  0.0 135.9 jit_solution(13505203197338632545)
XLA Ops:
  0.6 0.6 pad_add_fusion.1.pos_ref
  1.3 2.6 %halves.1 = (bf16[1,2,64,1152]{3,2,1,0:T(8,128)(2,1)}, bf16[1,2,64,1152]{3,2,1,0:T(8,128)(2,1)}) custom-call(s32[4]{0:T(128)} %pad_add_fusion.1.pos_ref, bf16[1,128,1152]{2,1,0:T(8,128)(2,1)} %x_ref.1, bf16[1,128,1152]{2,1,0:T(8,128)(2,1)} %g_ref.1), custom_call_target="tpu_custom_call" | custom-call | flops 589824 | bytes 2359296 | tf_op jit(solution)/shard_map/halves/pallas_call | solution.py:463
  3.8 1.9 %collective-permute-start.2 = (bf16[1,2,64,1152]{3,2,1,0:T(8,128)(2,1)}, bf16[1,2,64,1152]{3,2,1,0:T(8,128)(2,1)S(1)}, u32[]{:S(2)}, u32[]{:S(2)}) collective-permute-start(bf16[1,2,64,1152]{3,2,1,0:T(8,128)(2,1)} %get-tuple-element.56), channel_id=1, source_target_pairs={{0,0},{1,1},{2,16},{3,17},{4,2},{5,3},{6,18},{7,19},{8,20},{9,21},... | collective-permute-start | bytes 884744 | tf_op jit(solution)/shard_map/ppermute | solution.py:493
  5.7 4.7 %collective-permute-start.3 = (bf16[1,2,64,1152]{3,2,1,0:T(8,128)(2,1)}, bf16[1,2,64,1152]{3,2,1,0:T(8,128)(2,1)S(1)}, u32[]{:S(2)}, u32[]{:S(2)}) collective-permute-start(bf16[1,2,64,1152]{3,2,1,0:T(8,128)(2,1)} %get-tuple-element.57), channel_id=1, source_target_pairs={{0,2},{1,3},{2,18},{3,19},{4,0},{5,1},{6,16},{7,17},{8,22},{9,23},... | collective-permute-start | bytes 884744 | tf_op jit(solution)/shard_map/ppermute | solution.py:493
  10.5 0.6 copy-done.5
  11.1 0.1 fusion.7
  11.2 0.6 collective-permute-start
  11.8 2.9 %pick.1 = (bf16[144,432]{1,0:T(8,128)(2,1)}, bf16[144,432]{1,0:T(8,128)(2,1)}) custom-call(s32[4]{0:T(128)} %pad_add_fusion.1.pos_ref, bf16[144,3456]{1,0:T(8,128)(2,1)} %w_ref), custom_call_target="tpu_custom_call" | custom-call | flops 11796480000 | bytes 2359296 | tf_op jit(solution)/shard_map/pick/pallas_call | solution.py:484
  14.7 1.5 %collective-permute-start.8 = (bf16[144,432]{1,0:T(8,128)(2,1)}, bf16[144,432]{1,0:T(8,128)(2,1)S(1)}, u32[]{:S(2)}, u32[]{:S(2)}) collective-permute-start(bf16[144,432]{1,0:T(8,128)(2,1)} %get-tuple-element.64), channel_id=1, source_target_pairs={{0,1},{1,0},{2,3},{3,2},{4,5},{5,4},{6,7},{7,6},{8,9},{9,8},{10,11... | collective-permute-start | bytes 373256 | tf_op jit(solution)/shard_map/ppermute | solution.py:495
  16.2 1.9 %collective-permute-start.1 = (s32[2,16]{1,0:T(2,128)S(1)}, s32[2,16]{1,0:T(2,128)S(1)}, u32[]{:S(2)}, u32[]{:S(2)}) collective-permute-start(s32[2,16]{1,0:T(2,128)S(1)} %pad_add_fusion), channel_id=1, source_target_pairs={{0,16},{1,17},{2,18},{3,19},{4,20},{5,21},{6,22},{7,23},{8,24},{9,... | collective-permute-start | bytes 392 | tf_op jit(solution)/shard_map/ppermute | solution.py:476
  18.0 0.5 collective-permute-start.4
  18.6 1.3 collective-permute-done.1
  19.9 0.7 fusion.2.info_ref
  20.6 0.6 collective-permute-done.8
  21.1 0.9 broadcast_select_fusion.1
  22.1 4.9 %collective-permute-done.4 = bf16[1,2,64,1152]{3,2,1,0:T(8,128)(2,1)S(1)} collective-permute-done((bf16[1,2,64,1152]{3,2,1,0:T(8,128)(2,1)S(1)}, bf16[1,2,64,1152]{3,2,1,0:T(8,128)(2,1)S(1)}, u32[]{:S(2)}, u32[]{:S(2)}) %collective-permute-start.4) | collective-permute-done | bytes 294944 | tf_op jit(solution)/shard_map/ppermute | solution.py:503
  27.0 1.8 %collective-permute-start.6 = (bf16[1,2,64,1152]{3,2,1,0:T(8,128)(2,1)S(1)}, bf16[1,2,64,1152]{3,2,1,0:T(8,128)(2,1)S(1)}, u32[]{:S(2)}, u32[]{:S(2)}) collective-permute-start(bf16[1,2,64,1152]{3,2,1,0:T(8,128)(2,1)S(1)} %collective-permute-done.3.refs_1_), channel_id=1, source_target_pairs={{0,16},{1,17},{2,18},{3,19},{4,20},{5,21},{6,22},{7,23},{8,24},{9,... | collective-permute-start | bytes 884744 | tf_op jit(solution)/shard_map/ppermute | solution.py:452
  28.8 0.1 maximum_bitcast_fusion.2
  28.9 1.5 %collective-permute-start.9 = (bf16[1,144,864]{2,1,0:T(8,128)(2,1)S(1)}, bf16[1,144,864]{2,1,0:T(8,128)(2,1)S(1)}, u32[]{:S(2)}, u32[]{:S(2)}) collective-permute-start(bf16[1,144,864]{2,1,0:T(8,128)(2,1)S(1)} %maximum_bitcast_fusion.2), channel_id=1, source_target_pairs={{0,4},{1,5},{2,6},{3,7},{4,0},{5,1},{6,2},{7,3},{8,12},{9,13},{10,... | collective-permute-start | bytes 746504 | tf_op jit(solution)/shard_map/ppermute | solution.py:452
  30.5 2.1 %collective-permute-start.5 = (bf16[2,2,64,1152]{3,2,1,0:T(8,128)(2,1)S(1)}, bf16[2,2,64,1152]{3,2,1,0:T(8,128)(2,1)S(1)}, u32[]{:S(2)}, u32[]{:S(2)}) collective-permute-start(bf16[2,2,64,1152]{3,2,1,0:T(8,128)(2,1)S(1)} %pad_maximum_fusion.refs_0_), channel_id=1, source_target_pairs={{0,16},{1,17},{2,18},{3,19},{4,20},{5,21},{6,22},{7,23},{8,24},{9,... | collective-permute-start | bytes 1769480 | tf_op jit(solution)/shard_map/ppermute | solution.py:455
  32.6 4.4 %collective-permute-done.6 = bf16[1,2,64,1152]{3,2,1,0:T(8,128)(2,1)S(1)} collective-permute-done((bf16[1,2,64,1152]{3,2,1,0:T(8,128)(2,1)S(1)}, bf16[1,2,64,1152]{3,2,1,0:T(8,128)(2,1)S(1)}, u32[]{:S(2)}, u32[]{:S(2)}) %collective-permute-start.6) | collective-permute-done | bytes 294944 | tf_op jit(solution)/shard_map/ppermute | solution.py:452
  37.0 1.5 %collective-permute-start.7 = (bf16[2,2,64,1152]{3,2,1,0:T(8,128)(2,1)S(1)}, bf16[2,2,64,1152]{3,2,1,0:T(8,128)(2,1)S(1)}, u32[]{:S(2)}, u32[]{:S(2)}) collective-permute-start(bf16[2,2,64,1152]{3,2,1,0:T(8,128)(2,1)S(1)} %pad_maximum_fusion.1.refs_2_), channel_id=1, source_target_pairs={{0,1},{1,0},{2,3},{3,2},{4,5},{5,4},{6,7},{7,6},{8,9},{9,8},{10,11... | collective-permute-start | bytes 1769480 | tf_op jit(solution)/shard_map/ppermute | solution.py:455
  38.6 3.9 %collective-permute-done.9 = bf16[1,144,864]{2,1,0:T(8,128)(2,1)S(1)} collective-permute-done((bf16[1,144,864]{2,1,0:T(8,128)(2,1)S(1)}, bf16[1,144,864]{2,1,0:T(8,128)(2,1)S(1)}, u32[]{:S(2)}, u32[]{:S(2)}) %collective-permute-start.9) | collective-permute-done | bytes 248864 | tf_op jit(solution)/shard_map/ppermute | solution.py:452
  42.5 0.1 collective-permute-start.10
  42.6 4.4 %collective-permute-start.13 = (bf16[144,1152]{1,0:T(8,128)(2,1)S(1)}, bf16[144,1152]{1,0:T(8,128)(2,1)S(1)}, u32[]{:S(2)}, u32[]{:S(2)}) collective-permute-start(bf16[144,1152]{1,0:T(8,128)(2,1)S(1)} %copy-done.13), channel_id=1, source_target_pairs={{0,0},{1,1},{2,18},{3,19},{4,8},{5,9},{6,26},{7,27},{8,4},{9,5},{1... | collective-permute-start | bytes 995336 | tf_op jit(solution)/shard_map/ppermute | solution.py:508
  47.0 0.8 collective-permute-done.5.refs_1_
  47.8 7.8 %collective-permute-done.10.refs_5_.refs_1_ = bf16[2,144,864]{2,1,0:T(8,128)(2,1)S(1)} collective-permute-done((bf16[2,144,864]{2,1,0:T(8,128)(2,1)S(1)}, bf16[2,144,864]{2,1,0:T(8,128)(2,1)S(1)}, u32[]{:S(2)}, u32[]{:S(2)}) %collective-permute-start.10) | collective-permute-done | bytes 497696 | tf_op jit(solution)/shard_map/ppermute | solution.py:455
  55.7 0.5 collective-permute-start.12
  56.2 6.5 %collective-permute-done.13.refs_8_ = bf16[144,1152]{1,0:T(8,128)(2,1)S(1)} collective-permute-done((bf16[144,1152]{1,0:T(8,128)(2,1)S(1)}, bf16[144,1152]{1,0:T(8,128)(2,1)S(1)}, u32[]{:S(2)}, u32[]{:S(2)}) %collective-permute-start.13) | collective-permute-done | bytes 331808 | tf_op jit(solution)/shard_map/ppermute | solution.py:508
  62.7 1.6 %collective-permute-done.14.refs_9_ = bf16[144,1152]{1,0:T(8,128)(2,1)S(1)} collective-permute-done((bf16[144,1152]{1,0:T(8,128)(2,1)S(1)}, bf16[144,1152]{1,0:T(8,128)(2,1)S(1)}, u32[]{:S(2)}, u32[]{:S(2)}) %collective-permute-start.14) | collective-permute-done | bytes 331808 | tf_op jit(solution)/shard_map/ppermute | solution.py:536
  64.4 0.7 copy-done.15
  65.1 0.2 copy-done.11
  65.3 0.8 copy-done.12
  66.1 11.9 %forward.1 = (bf16[2,8,64,144]{3,2,1,0:T(8,128)(2,1)}, bf16[2,8,64,144]{3,2,1,0:T(8,128)(2,1)}, bf16[2,8,64,144]{3,2,1,0:T(8,128)(2,1)}, bf16[2,8,64,144]{3,2,1,...) custom-call(s32[4]{0:T(128)} %pad_add_fusion.1.pos_ref, ...), custom_call_target="tpu_custom_call" | custom-call | flops 8257536000 | bytes 2359296 | tf_op jit(solution)/shard_map/forward/pallas_call | solution.py:540
  78.1 0.1 collective-permute-start.15
  78.2 1.5 %collective-permute-start.17 = (bf16[2,64,1152]{2,1,0:T(8,128)(2,1)}, bf16[2,64,1152]{2,1,0:T(8,128)(2,1)S(1)}, u32[]{:S(2)}, u32[]{:S(2)}) collective-permute-start(bf16[2,64,1152]{2,1,0:T(8,128)(2,1)} %get-tuple-element.86), channel_id=1, source_target_pairs={{0,1},{1,0},{2,3},{3,2},{4,5},{5,4},{6,7},{7,6},{8,9},{9,8},{10,11... | collective-permute-start | bytes 884744 | tf_op jit(solution)/shard_map/ppermute | solution.py:458
  79.7 2.0 %collective-permute-start.19 = (bf16[2,64,1152]{2,1,0:T(8,128)(2,1)}, bf16[2,64,1152]{2,1,0:T(8,128)(2,1)S(1)}, u32[]{:S(2)}, u32[]{:S(2)}) collective-permute-start(bf16[2,64,1152]{2,1,0:T(8,128)(2,1)} %get-tuple-element.88), channel_id=1, source_target_pairs={{0,17},{1,16},{2,19},{3,18},{4,21},{5,20},{6,23},{7,22},{8,25},{9,... | collective-permute-start | bytes 884744 | tf_op jit(solution)/shard_map/ppermute | solution.py:458
  81.7 1.2 slice_add_fusion
  82.9 0.1 collective-permute-start.16
  83.0 8.4 %backward.1 = (f32[2,64,1152]{2,1,0:T(8,128)}, bf16[2,64,1152]{2,1,0:T(8,128)(2,1)}, bf16[2,64,1152]{2,1,0:T(8,128)(2,1)}, bf16[2,64,1152]{2,1,0:T(8,128)(2,1)}) custom-call(s32[4]{0:T(128)} %pad_add_fusion.1.pos_ref, s32[16]{0:T(128)} %fusion.2.info_ref, bf16[2,144,864]{2,1,0:T(8,128)(2,1)} %copy-done.2, bf16[2,144,864]{2,1,0:T(8,128)(2,1)} %copy-done.10, ...), custom_call_target="tpu_custom_call" | custom-call | flops 5898240000 | bytes 2359296 | tf_op jit(solution)/shard_map/backward/pallas_call | solution.py:568
  91.3 3.9 %collective-permute-done.18.refs_4_ = bf16[2,64,1152]{2,1,0:T(8,128)(2,1)S(1)} collective-permute-done((bf16[2,64,1152]{2,1,0:T(8,128)(2,1)}, bf16[2,64,1152]{2,1,0:T(8,128)(2,1)S(1)}, u32[]{:S(2)}, u32[]{:S(2)}) %collective-permute-start.18) | collective-permute-done | bytes 294944 | tf_op jit(solution)/shard_map/ppermute | solution.py:458
  95.3 0.6 copy-done.19
  95.9 0.1 copy-done.21
  96.1 0.1 collective-permute-start.25
  96.1 0.3 copy-done.20
  96.4 0.6 collective-permute-start.22
  97.0 1.1 collective-permute-start.23
  98.0 1.9 %collective-permute-start.24 = (bf16[2,64,1152]{2,1,0:T(8,128)(2,1)S(1)}, bf16[2,64,1152]{2,1,0:T(8,128)(2,1)S(1)}, u32[]{:S(2)}, u32[]{:S(2)}) collective-permute-start(bf16[2,64,1152]{2,1,0:T(8,128)(2,1)S(1)} %copy-done.16), channel_id=1, source_target_pairs={{0,17},{1,16},{2,19},{3,18},{4,21},{5,20},{6,23},{7,22},{8,25},{9,... | collective-permute-start | bytes 884744 | tf_op jit(solution)/shard_map/ppermute | solution.py:458
  99.9 3.1 %output.1 = (bf16[64,1152]{1,0:T(8,128)(2,1)}, bf16[64,1152]{1,0:T(8,128)(2,1)}) custom-call(s32[4]{0:T(128)} %pad_add_fusion.1.pos_ref, s32[16]{0:T(128)} %fusion.2.info_ref, bf16[1,2,64,1152]{3,2,1,0:T(8,128)(2,1)} %copy-done.3, bf16[1,2,64,1152]{3,2,1,0:T(8,128)(2,1)} %copy-done.4, f32[2,64,1152]{2,1,0:T(8,128)} %get-tuple-element.89.refs_2_, ...), custom_call_target="tpu_custom_call" | custom-call | flops 11796480000 | bytes 2359296 | tf_op jit(solution)/shard_map/output/pallas_call | solution.py:581
  103.0 3.8 %collective-permute-start.20 = (bf16[64,1152]{1,0:T(8,128)(2,1)}, bf16[64,1152]{1,0:T(8,128)(2,1)S(1)}, u32[]{:S(2)}, u32[]{:S(2)}) collective-permute-start(bf16[64,1152]{1,0:T(8,128)(2,1)} %get-tuple-element.93), channel_id=1, source_target_pairs={{0,0},{1,1},{16,2},{17,3},{2,4},{3,5},{18,6},{19,7},{20,8},{21,9},... | collective-permute-start | bytes 442376 | tf_op jit(solution)/shard_map/ppermute | solution.py:445
  106.8 3.3 %collective-permute-start.21 = (bf16[64,1152]{1,0:T(8,128)(2,1)}, bf16[64,1152]{1,0:T(8,128)(2,1)S(1)}, u32[]{:S(2)}, u32[]{:S(2)}) collective-permute-start(bf16[64,1152]{1,0:T(8,128)(2,1)} %get-tuple-element.94), channel_id=1, source_target_pairs={{2,0},{3,1},{18,2},{19,3},{0,4},{1,5},{16,6},{17,7},{22,8},{23,9},... | collective-permute-start | bytes 442376 | tf_op jit(solution)/shard_map/ppermute | solution.py:445
  110.2 1.2 collective-permute-done.23.refs_4_
  111.4 0.7 copy-done.23
  112.1 0.7 copy-done.24
  112.8 3.4 %input_grad.1 = (bf16[64,1152]{1,0:T(8,128)(2,1)}, bf16[64,1152]{1,0:T(8,128)(2,1)}) custom-call(s32[4]{0:T(128)} %pad_add_fusion.1.pos_ref, s32[16]{0:T(128)} %fusion.2.info_ref, bf16[1,2,64,1152]{3,2,1,0:T(8,128)(2,1)} %copy-done.3, bf16[1,2,64,1152]{3,2,1,0:T(8,128)(2,1)} %copy-done.4, f32[2,64,1152]{2,1,0:T(8,128)} %get-tuple-element.101.refs_2_, ...), custom_call_target="tpu_custom_call" | custom-call | flops 1769472000 | bytes 2359296 | tf_op jit(solution)/shard_map/input_grad/pallas_call | solution.py:597
  116.2 5.2 %collective-permute-start.26 = (bf16[64,1152]{1,0:T(8,128)(2,1)}, bf16[64,1152]{1,0:T(8,128)(2,1)S(1)}, u32[]{:S(2)}, u32[]{:S(2)}) collective-permute-start(bf16[64,1152]{1,0:T(8,128)(2,1)} %get-tuple-element.105), channel_id=1, source_target_pairs={{0,0},{1,1},{16,2},{17,3},{2,4},{3,5},{18,6},{19,7},{20,8},{21,9},... | collective-permute-start | bytes 442376 | tf_op jit(solution)/shard_map/ppermute | solution.py:445
  121.4 2.8 %collective-permute-start.27 = (bf16[64,1152]{1,0:T(8,128)(2,1)}, bf16[64,1152]{1,0:T(8,128)(2,1)S(1)}, u32[]{:S(2)}, u32[]{:S(2)}) collective-permute-start(bf16[64,1152]{1,0:T(8,128)(2,1)} %get-tuple-element.106), channel_id=1, source_target_pairs={{2,0},{3,1},{18,2},{19,3},{0,4},{1,5},{16,6},{17,7},{22,8},{23,9},... | collective-permute-start | bytes 442376 | tf_op jit(solution)/shard_map/ppermute | solution.py:445
  124.2 2.8 %collective-permute-start.28 = (f32[48,864]{1,0:T(8,128)S(1)}, f32[48,864]{1,0:T(8,128)S(1)}, u32[]{:S(2)}, u32[]{:S(2)}) collective-permute-start(f32[48,864]{1,0:T(8,128)S(1)} %bitcast.28), channel_id=1, source_target_pairs={{0,0},{1,1},{2,8},{3,9},{4,16},{5,17},{6,24},{7,25},{8,4},{9,5},{1... | collective-permute-start | bytes 497672 | tf_op jit(solution)/shard_map/ppermute | solution.py:609
  127.1 2.9 %collective-permute-done.27 = bf16[64,1152]{1,0:T(8,128)(2,1)S(1)} collective-permute-done((bf16[64,1152]{1,0:T(8,128)(2,1)}, bf16[64,1152]{1,0:T(8,128)(2,1)S(1)}, u32[]{:S(2)}, u32[]{:S(2)}) %collective-permute-start.27) | collective-permute-done | bytes 147488 | tf_op jit(solution)/shard_map/ppermute | solution.py:445
  130.1 0.7 maximum_bitcast_fusion.1
  130.8 0.7 maximum_bitcast_fusion
  131.6 3.5 %collective-permute-done.28 = f32[48,864]{1,0:T(8,128)S(1)} collective-permute-done((f32[48,864]{1,0:T(8,128)S(1)}, f32[48,864]{1,0:T(8,128)S(1)}, u32[]{:S(2)}, u32[]{:S(2)}) %collective-permute-start.28) | collective-permute-done | bytes 165920 | tf_op jit(solution)/shard_map/ppermute | solution.py:609
  135.1 0.1 fusion.6
  135.2 0.7 maximum_multiply_fusion
  (68 shorter events, 0.6 us)
Async XLA Ops:
  3.8 14.2 %collective-permute-start.2 = (bf16[1,2,64,1152]{3,2,1,0:T(8,128)(2,1)}, bf16[1,2,64,1152]{3,2,1,0:T(8,128)(2,1)S(1)}, u32[]{:S(2)}, u32[]{:S(2)}) collective-permute-start(bf16[1,2,64,1152]{3,2,1,0:T(8,128)(2,1)} %get-tuple-element.56), channel_id=1, source_target_pairs={{0,0},{1,1},{2,16},{3,17},{4,2},{5,3},{6,18},{7,19},{8,20},{9,21},... | collective-permute-start | bytes 884744 | tf_op jit(solution)/shard_map/ppermute | solution.py:493
  5.7 16.3 %collective-permute-start.3 = (bf16[1,2,64,1152]{3,2,1,0:T(8,128)(2,1)}, bf16[1,2,64,1152]{3,2,1,0:T(8,128)(2,1)S(1)}, u32[]{:S(2)}, u32[]{:S(2)}) collective-permute-start(bf16[1,2,64,1152]{3,2,1,0:T(8,128)(2,1)} %get-tuple-element.57), channel_id=1, source_target_pairs={{0,2},{1,3},{2,18},{3,19},{4,0},{5,1},{6,16},{7,17},{8,22},{9,23},... | collective-permute-start | bytes 884744 | tf_op jit(solution)/shard_map/ppermute | solution.py:493
  10.5 0.7 copy-start.5
  10.5 0.7 copy-start.6
  10.5 0.7 copy-start.7
  11.2 4.9 %collective-permute-start = (s32[1,16]{1,0:T(1,128)S(1)}, s32[1,16]{1,0:T(1,128)S(1)}, u32[]{:S(2)}, u32[]{:S(2)}) collective-permute-start(s32[1,16]{1,0:T(1,128)S(1)} %fusion.7), channel_id=1, source_target_pairs={{0,8},{1,9},{2,10},{3,11},{4,12},{5,13},{6,14},{7,15},{8,0},{9,1},... | collective-permute-start | bytes 200 | tf_op jit(solution)/shard_map/ppermute | solution.py:474
  14.7 6.5 %collective-permute-start.8 = (bf16[144,432]{1,0:T(8,128)(2,1)}, bf16[144,432]{1,0:T(8,128)(2,1)S(1)}, u32[]{:S(2)}, u32[]{:S(2)}) collective-permute-start(bf16[144,432]{1,0:T(8,128)(2,1)} %get-tuple-element.64), channel_id=1, source_target_pairs={{0,1},{1,0},{2,3},{3,2},{4,5},{5,4},{6,7},{7,6},{8,9},{9,8},{10,11... | collective-permute-start | bytes 373256 | tf_op jit(solution)/shard_map/ppermute | solution.py:495
  16.2 3.7 %collective-permute-start.1 = (s32[2,16]{1,0:T(2,128)S(1)}, s32[2,16]{1,0:T(2,128)S(1)}, u32[]{:S(2)}, u32[]{:S(2)}) collective-permute-start(s32[2,16]{1,0:T(2,128)S(1)} %pad_add_fusion), channel_id=1, source_target_pairs={{0,16},{1,17},{2,18},{3,19},{4,20},{5,21},{6,22},{7,23},{8,24},{9,... | collective-permute-start | bytes 392 | tf_op jit(solution)/shard_map/ppermute | solution.py:476
  18.0 12.4 %copy-start.3 = (bf16[1,2,64,1152]{3,2,1,0:T(8,128)(2,1)}, bf16[1,2,64,1152]{3,2,1,0:T(8,128)(2,1)S(1)}, u32[]{:S(2)}) copy-start(bf16[1,2,64,1152]{3,2,1,0:T(8,128)(2,1)S(1)} %collective-permute-done.2.refs_0_) | copy-start | bytes 884740
  18.0 8.9 %collective-permute-start.4 = (bf16[1,2,64,1152]{3,2,1,0:T(8,128)(2,1)S(1)}, bf16[1,2,64,1152]{3,2,1,0:T(8,128)(2,1)S(1)}, u32[]{:S(2)}, u32[]{:S(2)}) collective-permute-start(bf16[1,2,64,1152]{3,2,1,0:T(8,128)(2,1)S(1)} %collective-permute-done.2.refs_0_), channel_id=1, source_target_pairs={{0,1},{1,0},{2,3},{3,2},{4,5},{5,4},{6,7},{7,6},{8,9},{9,8},{10,11... | collective-permute-start | bytes 884744 | tf_op jit(solution)/shard_map/ppermute | solution.py:503
  22.1 14.8 %copy-start.4 = (bf16[1,2,64,1152]{3,2,1,0:T(8,128)(2,1)}, bf16[1,2,64,1152]{3,2,1,0:T(8,128)(2,1)S(1)}, u32[]{:S(2)}) copy-start(bf16[1,2,64,1152]{3,2,1,0:T(8,128)(2,1)S(1)} %collective-permute-done.3.refs_1_) | copy-start | bytes 884740
  27.0 9.9 %collective-permute-start.6 = (bf16[1,2,64,1152]{3,2,1,0:T(8,128)(2,1)S(1)}, bf16[1,2,64,1152]{3,2,1,0:T(8,128)(2,1)S(1)}, u32[]{:S(2)}, u32[]{:S(2)}) collective-permute-start(bf16[1,2,64,1152]{3,2,1,0:T(8,128)(2,1)S(1)} %collective-permute-done.3.refs_1_), channel_id=1, source_target_pairs={{0,16},{1,17},{2,18},{3,19},{4,20},{5,21},{6,22},{7,23},{8,24},{9,... | collective-permute-start | bytes 884744 | tf_op jit(solution)/shard_map/ppermute | solution.py:452
  28.9 13.5 %collective-permute-start.9 = (bf16[1,144,864]{2,1,0:T(8,128)(2,1)S(1)}, bf16[1,144,864]{2,1,0:T(8,128)(2,1)S(1)}, u32[]{:S(2)}, u32[]{:S(2)}) collective-permute-start(bf16[1,144,864]{2,1,0:T(8,128)(2,1)S(1)} %maximum_bitcast_fusion.2), channel_id=1, source_target_pairs={{0,4},{1,5},{2,6},{3,7},{4,0},{5,1},{6,2},{7,3},{8,12},{9,13},{10,... | collective-permute-start | bytes 746504 | tf_op jit(solution)/shard_map/ppermute | solution.py:452
  30.5 6.5 %copy-start = (bf16[2,2,64,1152]{3,2,1,0:T(8,128)(2,1)}, bf16[2,2,64,1152]{3,2,1,0:T(8,128)(2,1)S(1)}, u32[]{:S(2)}) copy-start(bf16[2,2,64,1152]{3,2,1,0:T(8,128)(2,1)S(1)} %pad_maximum_fusion.refs_0_) | copy-start | bytes 1769476
  30.5 17.3 %collective-permute-start.5 = (bf16[2,2,64,1152]{3,2,1,0:T(8,128)(2,1)S(1)}, bf16[2,2,64,1152]{3,2,1,0:T(8,128)(2,1)S(1)}, u32[]{:S(2)}, u32[]{:S(2)}) collective-permute-start(bf16[2,2,64,1152]{3,2,1,0:T(8,128)(2,1)S(1)} %pad_maximum_fusion.refs_0_), channel_id=1, source_target_pairs={{0,16},{1,17},{2,18},{3,19},{4,20},{5,21},{6,22},{7,23},{8,24},{9,... | collective-permute-start | bytes 1769480 | tf_op jit(solution)/shard_map/ppermute | solution.py:455
  37.0 27.4 %copy-start.1 = (bf16[2,2,64,1152]{3,2,1,0:T(8,128)(2,1)}, bf16[2,2,64,1152]{3,2,1,0:T(8,128)(2,1)S(1)}, u32[]{:S(2)}) copy-start(bf16[2,2,64,1152]{3,2,1,0:T(8,128)(2,1)S(1)} %pad_maximum_fusion.1.refs_2_) | copy-start | bytes 1769476
  37.0 5.6 %copy-start.13 = (bf16[144,1152]{1,0:T(8,128)(2,1)S(1)}, bf16[144,1152]{1,0:T(8,128)(2,1)}, u32[]{:S(2)}) copy-start(bf16[144,1152]{1,0:T(8,128)(2,1)} %param.15) | copy-start | bytes 995332
  37.0 18.6 %collective-permute-start.7 = (bf16[2,2,64,1152]{3,2,1,0:T(8,128)(2,1)S(1)}, bf16[2,2,64,1152]{3,2,1,0:T(8,128)(2,1)S(1)}, u32[]{:S(2)}, u32[]{:S(2)}) collective-permute-start(bf16[2,2,64,1152]{3,2,1,0:T(8,128)(2,1)S(1)} %pad_maximum_fusion.1.refs_2_), channel_id=1, source_target_pairs={{0,1},{1,0},{2,3},{3,2},{4,5},{5,4},{6,7},{7,6},{8,9},{9,8},{10,11... | collective-permute-start | bytes 1769480 | tf_op jit(solution)/shard_map/ppermute | solution.py:455
  42.5 21.9 %copy-start.2 = (bf16[2,144,864]{2,1,0:T(8,128)(2,1)}, bf16[2,144,864]{2,1,0:T(8,128)(2,1)S(1)}, u32[]{:S(2)}) copy-start(bf16[2,144,864]{2,1,0:T(8,128)(2,1)S(1)} %pad_maximum_fusion.2.refs_4_.refs_0_) | copy-start | bytes 1492996
  42.5 13.1 %collective-permute-start.10 = (bf16[2,144,864]{2,1,0:T(8,128)(2,1)S(1)}, bf16[2,144,864]{2,1,0:T(8,128)(2,1)S(1)}, u32[]{:S(2)}, u32[]{:S(2)}) collective-permute-start(bf16[2,144,864]{2,1,0:T(8,128)(2,1)S(1)} %pad_maximum_fusion.2.refs_4_.refs_0_), channel_id=1, source_target_pairs={{0,2},{1,3},{2,0},{3,1},{4,6},{5,7},{6,4},{7,5},{8,10},{9,11},{10,... | collective-permute-start | bytes 1493000 | tf_op jit(solution)/shard_map/ppermute | solution.py:455
  42.6 20.1 %collective-permute-start.13 = (bf16[144,1152]{1,0:T(8,128)(2,1)S(1)}, bf16[144,1152]{1,0:T(8,128)(2,1)S(1)}, u32[]{:S(2)}, u32[]{:S(2)}) collective-permute-start(bf16[144,1152]{1,0:T(8,128)(2,1)S(1)} %copy-done.13), channel_id=1, source_target_pairs={{0,0},{1,1},{2,18},{3,19},{4,8},{5,9},{6,26},{7,27},{8,4},{9,5},{1... | collective-permute-start | bytes 995336 | tf_op jit(solution)/shard_map/ppermute | solution.py:508
  47.8 16.6 %copy-start.8 = (bf16[2,2,64,1152]{3,2,1,0:T(8,128)(2,1)}, bf16[2,2,64,1152]{3,2,1,0:T(8,128)(2,1)S(1)}, u32[]{:S(2)}) copy-start(bf16[2,2,64,1152]{3,2,1,0:T(8,128)(2,1)S(1)} %collective-permute-done.5.refs_1_) | copy-start | bytes 1769476
  55.6 8.8 %copy-start.10 = (bf16[2,144,864]{2,1,0:T(8,128)(2,1)}, bf16[2,144,864]{2,1,0:T(8,128)(2,1)S(1)}, u32[]{:S(2)}) copy-start(bf16[2,144,864]{2,1,0:T(8,128)(2,1)S(1)} %collective-permute-done.10.refs_5_.refs_1_) | copy-start | bytes 1492996
  55.6 8.8 %copy-start.9 = (bf16[2,2,64,1152]{3,2,1,0:T(8,128)(2,1)}, bf16[2,2,64,1152]{3,2,1,0:T(8,128)(2,1)S(1)}, u32[]{:S(2)}) copy-start(bf16[2,2,64,1152]{3,2,1,0:T(8,128)(2,1)S(1)} %collective-permute-done.7.refs_3_) | copy-start | bytes 1769476
  55.6 8.7 %collective-permute-start.11 = (bf16[2,144,864]{2,1,0:T(8,128)(2,1)S(1)}, bf16[2,144,864]{2,1,0:T(8,128)(2,1)S(1)}, u32[]{:S(2)}, u32[]{:S(2)}) collective-permute-start(bf16[2,144,864]{2,1,0:T(8,128)(2,1)S(1)} %pad_maximum_fusion.2.refs_4_.refs_0_), channel_id=1, source_target_pairs={{0,8},{1,9},{2,10},{3,11},{4,12},{5,13},{6,14},{7,15},{8,0},{9,1},... | collective-permute-start | bytes 1493000 | tf_op jit(solution)/shard_map/ppermute | solution.py:516
  55.7 8.7 %collective-permute-start.12 = (bf16[2,144,864]{2,1,0:T(8,128)(2,1)S(1)}, bf16[2,144,864]{2,1,0:T(8,128)(2,1)S(1)}, u32[]{:S(2)}, u32[]{:S(2)}) collective-permute-start(bf16[2,144,864]{2,1,0:T(8,128)(2,1)S(1)} %collective-permute-done.10.refs_5_.refs_1_), channel_id=1, source_target_pairs={{0,8},{1,9},{2,10},{3,11},{4,12},{5,13},{6,14},{7,15},{8,0},{9,1},... | collective-permute-start | bytes 1493000 | tf_op jit(solution)/shard_map/ppermute | solution.py:516
  62.7 1.7 %copy-start.14 = (bf16[144,1152]{1,0:T(8,128)(2,1)}, bf16[144,1152]{1,0:T(8,128)(2,1)S(1)}, u32[]{:S(2)}) copy-start(bf16[144,1152]{1,0:T(8,128)(2,1)S(1)} %collective-permute-done.13.refs_8_) | copy-start | bytes 995332
  62.7 1.6 %collective-permute-start.14 = (bf16[144,1152]{1,0:T(8,128)(2,1)S(1)}, bf16[144,1152]{1,0:T(8,128)(2,1)S(1)}, u32[]{:S(2)}, u32[]{:S(2)}) collective-permute-start(bf16[144,1152]{1,0:T(8,128)(2,1)S(1)} %collective-permute-done.13.refs_8_), channel_id=1, source_target_pairs={{0,8},{1,9},{2,10},{3,11},{4,12},{5,13},{6,14},{7,15},{8,0},{9,1},... | collective-permute-start | bytes 995336 | tf_op jit(solution)/shard_map/ppermute | solution.py:536
  64.4 0.7 copy-start.15
  64.4 0.9 copy-start.11
  65.3 0.8 copy-start.12
  78.1 3.6 %collective-permute-start.15 = (f32[4,48,864]{2,1,0:T(8,128)}, f32[4,48,864]{2,1,0:T(8,128)S(1)}, u32[]{:S(2)}, u32[]{:S(2)}) collective-permute-start(f32[4,48,864]{2,1,0:T(8,128)} %get-tuple-element.78), channel_id=1, source_target_pairs={{0,8},{1,9},{2,10},{3,11},{4,12},{5,13},{6,14},{7,15},{8,0},{9,1},... | collective-permute-start | bytes 1990664 | tf_op jit(solution)/shard_map/ppermute | solution.py:560
  78.2 13.1 %collective-permute-start.17 = (bf16[2,64,1152]{2,1,0:T(8,128)(2,1)}, bf16[2,64,1152]{2,1,0:T(8,128)(2,1)S(1)}, u32[]{:S(2)}, u32[]{:S(2)}) collective-permute-start(bf16[2,64,1152]{2,1,0:T(8,128)(2,1)} %get-tuple-element.86), channel_id=1, source_target_pairs={{0,1},{1,0},{2,3},{3,2},{4,5},{5,4},{6,7},{7,6},{8,9},{9,8},{10,11... | collective-permute-start | bytes 884744 | tf_op jit(solution)/shard_map/ppermute | solution.py:458
  79.7 15.5 %collective-permute-start.18 = (bf16[2,64,1152]{2,1,0:T(8,128)(2,1)}, bf16[2,64,1152]{2,1,0:T(8,128)(2,1)S(1)}, u32[]{:S(2)}, u32[]{:S(2)}) collective-permute-start(bf16[2,64,1152]{2,1,0:T(8,128)(2,1)} %get-tuple-element.87), channel_id=1, source_target_pairs={{0,16},{1,17},{2,18},{3,19},{4,20},{5,21},{6,22},{7,23},{8,24},{9,... | collective-permute-start | bytes 884744 | tf_op jit(solution)/shard_map/ppermute | solution.py:458
  79.7 15.5 %collective-permute-start.19 = (bf16[2,64,1152]{2,1,0:T(8,128)(2,1)}, bf16[2,64,1152]{2,1,0:T(8,128)(2,1)S(1)}, u32[]{:S(2)}, u32[]{:S(2)}) collective-permute-start(bf16[2,64,1152]{2,1,0:T(8,128)(2,1)} %get-tuple-element.88), channel_id=1, source_target_pairs={{0,17},{1,16},{2,19},{3,18},{4,21},{5,20},{6,23},{7,22},{8,25},{9,... | collective-permute-start | bytes 884744 | tf_op jit(solution)/shard_map/ppermute | solution.py:458
  82.9 12.4 %collective-permute-start.16 = (f32[2,48,864]{2,1,0:T(8,128)S(1)}, f32[2,48,864]{2,1,0:T(8,128)S(1)}, u32[]{:S(2)}, u32[]{:S(2)}) collective-permute-start(f32[2,48,864]{2,1,0:T(8,128)S(1)} %get-tuple-element.84), channel_id=1, source_target_pairs={{0,2},{1,3},{2,0},{3,1},{4,6},{5,7},{6,4},{7,5},{8,10},{9,11},{10,... | collective-permute-start | bytes 995336 | tf_op jit(solution)/shard_map/ppermute | solution.py:566
  91.3 4.0 %copy-start.17 = (bf16[2,64,1152]{2,1,0:T(8,128)(2,1)}, bf16[2,64,1152]{2,1,0:T(8,128)(2,1)S(1)}, u32[]{:S(2)}) copy-start(bf16[2,64,1152]{2,1,0:T(8,128)(2,1)S(1)} %collective-permute-done.17.refs_3_) | copy-start | bytes 884740
  95.2 0.7 copy-start.19
  95.2 0.8 copy-start.21
  95.2 1.2 copy-start.20
  95.2 1.7 %copy-start.18 = (bf16[2,64,1152]{2,1,0:T(8,128)(2,1)S(1)}, bf16[2,64,1152]{2,1,0:T(8,128)(2,1)}, u32[]{:S(2)}) copy-start(bf16[2,64,1152]{2,1,0:T(8,128)(2,1)} %get-tuple-element.97) | copy-start | bytes 884740
  96.0 2.0 %copy-start.16 = (bf16[2,64,1152]{2,1,0:T(8,128)(2,1)S(1)}, bf16[2,64,1152]{2,1,0:T(8,128)(2,1)}, u32[]{:S(2)}) copy-start(bf16[2,64,1152]{2,1,0:T(8,128)(2,1)} %get-tuple-element.98) | copy-start | bytes 884740
  96.1 10.8 %collective-permute-start.25 = (f32[1,48,864]{2,1,0:T(8,128)S(1)}, f32[1,48,864]{2,1,0:T(8,128)S(1)}, u32[]{:S(2)}, u32[]{:S(2)}) collective-permute-start(f32[1,48,864]{2,1,0:T(8,128)S(1)} %slice.47), channel_id=1, source_target_pairs={{0,4},{1,5},{2,6},{3,7},{4,0},{5,1},{6,2},{7,3},{8,12},{9,13},{10,... | collective-permute-start | bytes 497672 | tf_op jit(solution)/shard_map/ppermute | solution.py:595
  96.4 13.7 %collective-permute-start.22 = (bf16[2,64,1152]{2,1,0:T(8,128)(2,1)S(1)}, bf16[2,64,1152]{2,1,0:T(8,128)(2,1)S(1)}, u32[]{:S(2)}, u32[]{:S(2)}) collective-permute-start(bf16[2,64,1152]{2,1,0:T(8,128)(2,1)S(1)} %copy-done.20), channel_id=1, source_target_pairs={{0,1},{1,0},{2,3},{3,2},{4,5},{5,4},{6,7},{7,6},{8,9},{9,8},{10,11... | collective-permute-start | bytes 884744 | tf_op jit(solution)/shard_map/ppermute | solution.py:458
  97.0 14.4 %collective-permute-start.23 = (bf16[2,64,1152]{2,1,0:T(8,128)(2,1)S(1)}, bf16[2,64,1152]{2,1,0:T(8,128)(2,1)S(1)}, u32[]{:S(2)}, u32[]{:S(2)}) collective-permute-start(bf16[2,64,1152]{2,1,0:T(8,128)(2,1)S(1)} %copy-done.18), channel_id=1, source_target_pairs={{0,16},{1,17},{2,18},{3,19},{4,20},{5,21},{6,22},{7,23},{8,24},{9,... | collective-permute-start | bytes 884744 | tf_op jit(solution)/shard_map/ppermute | solution.py:458
  98.0 13.3 %collective-permute-start.24 = (bf16[2,64,1152]{2,1,0:T(8,128)(2,1)S(1)}, bf16[2,64,1152]{2,1,0:T(8,128)(2,1)S(1)}, u32[]{:S(2)}, u32[]{:S(2)}) collective-permute-start(bf16[2,64,1152]{2,1,0:T(8,128)(2,1)S(1)} %copy-done.16), channel_id=1, source_target_pairs={{0,17},{1,16},{2,19},{3,18},{4,21},{5,20},{6,23},{7,22},{8,25},{9,... | collective-permute-start | bytes 884744 | tf_op jit(solution)/shard_map/ppermute | solution.py:458
  103.0 24.1 %collective-permute-start.20 = (bf16[64,1152]{1,0:T(8,128)(2,1)}, bf16[64,1152]{1,0:T(8,128)(2,1)S(1)}, u32[]{:S(2)}, u32[]{:S(2)}) collective-permute-start(bf16[64,1152]{1,0:T(8,128)(2,1)} %get-tuple-element.93), channel_id=1, source_target_pairs={{0,0},{1,1},{16,2},{17,3},{2,4},{3,5},{18,6},{19,7},{20,8},{21,9},... | collective-permute-start | bytes 442376 | tf_op jit(solution)/shard_map/ppermute | solution.py:445
  106.8 20.2 %collective-permute-start.21 = (bf16[64,1152]{1,0:T(8,128)(2,1)}, bf16[64,1152]{1,0:T(8,128)(2,1)S(1)}, u32[]{:S(2)}, u32[]{:S(2)}) collective-permute-start(bf16[64,1152]{1,0:T(8,128)(2,1)} %get-tuple-element.94), channel_id=1, source_target_pairs={{2,0},{3,1},{18,2},{19,3},{0,4},{1,5},{16,6},{17,7},{22,8},{23,9},... | collective-permute-start | bytes 442376 | tf_op jit(solution)/shard_map/ppermute | solution.py:445
  110.2 1.2 copy-start.22
  111.3 0.7 copy-start.23
  112.1 0.7 copy-start.24
  116.2 10.9 %collective-permute-start.26 = (bf16[64,1152]{1,0:T(8,128)(2,1)}, bf16[64,1152]{1,0:T(8,128)(2,1)S(1)}, u32[]{:S(2)}, u32[]{:S(2)}) collective-permute-start(bf16[64,1152]{1,0:T(8,128)(2,1)} %get-tuple-element.105), channel_id=1, source_target_pairs={{0,0},{1,1},{16,2},{17,3},{2,4},{3,5},{18,6},{19,7},{20,8},{21,9},... | collective-permute-start | bytes 442376 | tf_op jit(solution)/shard_map/ppermute | solution.py:445
  121.4 8.6 %collective-permute-start.27 = (bf16[64,1152]{1,0:T(8,128)(2,1)}, bf16[64,1152]{1,0:T(8,128)(2,1)S(1)}, u32[]{:S(2)}, u32[]{:S(2)}) collective-permute-start(bf16[64,1152]{1,0:T(8,128)(2,1)} %get-tuple-element.106), channel_id=1, source_target_pairs={{2,0},{3,1},{18,2},{19,3},{0,4},{1,5},{16,6},{17,7},{22,8},{23,9},... | collective-permute-start | bytes 442376 | tf_op jit(solution)/shard_map/ppermute | solution.py:445
  124.2 10.8 %collective-permute-start.28 = (f32[48,864]{1,0:T(8,128)S(1)}, f32[48,864]{1,0:T(8,128)S(1)}, u32[]{:S(2)}, u32[]{:S(2)}) collective-permute-start(f32[48,864]{1,0:T(8,128)S(1)} %bitcast.28), channel_id=1, source_target_pairs={{0,0},{1,1},{2,8},{3,9},{4,16},{5,17},{6,24},{7,25},{8,4},{9,5},{1... | collective-permute-start | bytes 497672 | tf_op jit(solution)/shard_map/ppermute | solution.py:609

commit v18 on v16

--- a/solution.py
+++ b/solution.py
@@ -491,18 +491,19 @@
     w_own = jnp.concatenate(ordered, axis=1 if rows % 16 == 0 else 0)[None]
     first = lax.ppermute(own[0], AXES, chip_swap(lay.chip_bits(0)[0]))
     own[1], first = lax.optimization_barrier((own[1], first))
-    w_own, _ = lax.optimization_barrier((w_own, own[1]))
+    late_w_out, _ = lax.optimization_barrier((w_out, own[0]))
+    wo_own = lax.ppermute(late_w_out, AXES, lay.rows_to_chip())
+    wo_rows = [wo_own, lax.ppermute(wo_own, AXES, lay.swap(kc=1))]
+    w_own, _ = lax.optimization_barrier((w_own, (own[1], wo_own)))
     w_pieces = doubling(w_own, lay.bits(lay.nz)[::-1], lambda kz: lay.swap(kz=kz), [])
-    late_w_out, _ = lax.optimization_barrier((w_out, own))
-    wo_own = lax.ppermute(late_w_out, AXES, lay.rows_to_chip())
-
     pairs = []
     for j in range(nc):
         after = ([], None) if j else (info, first)
         pairs += doubling(own[j], lay.chip_bits(j), chip_swap, *after)
-    pairs, w_pieces = lax.optimization_barrier((pairs, w_pieces))
+    early = [lax.ppermute(w_pieces[0], AXES, lay.swap(kc=1))] if halves > 1 else []
+    pairs, w_pieces, early, wo_rows = lax.optimization_barrier((pairs, w_pieces, early, wo_rows))
     if halves > 1:
-        w_pieces += [lax.ppermute(piece, AXES, lay.swap(kc=1)) for piece in w_pieces]
+        w_pieces += early + [lax.ppermute(w_pieces[1], AXES, lay.swap(kc=1))]
 
 
     def spread(count, width, patches_at_once):
@@ -521,8 +522,6 @@
     triple_shape = struct((halves, lay.frames, half, cols))
     part_specs = [spread(nc, model, step_patches)] * chips
     part_shapes = [struct((nc, half, model), F32)] + [struct((nc, half, model))] * (chips - 1)
-
-    wo_rows = [wo_own, lax.ppermute(wo_own, AXES, lay.swap(kc=1))]
 
     fold = 3 if rows % 24 == 0 else 1
     piece_shape = (groups, rows // fold, quarter * fold)

time: 134 us -> 133 us (level)
  waiting for transfers between devices: 42.8 us -> 48.4 us
  starting transfers between devices: 47.5 us -> 43.1 us
    ppermute x2, waiting for transfers between devices: 6.08 us -> 1.73 us  [local(): lax.ppermute(pair, AXES, lay.to_plane(k))]
    ppermute x3, waiting for transfers between devices: 8.11 us -> 11.8 us  [doubling(): return [held, lax.ppermute(held, AXES, swap(bits[-1]))]]
    ppermute x2, starting transfers between devices: 3.95 us -> 1.22 us  [doubling(): got = lax.ppermute(held, AXES, swap(bit)) if first is None else first]
    ppermute x1, starting transfers between devices: 2.97 us -> 0.28 us  [local(): wo_rows = [wo_own, lax.ppermute(wo_own, AXES, lay.swap(kc=1))]]
    ppermute x1, waiting for transfers between devices: 2.62 us -> 5.09 us  [local(): grad_w = lax.ppermute(cut[0], AXES, lay.to_owner())]
    ppermute x2, waiting for transfers between devices: 0.01 us -> 1.89 us  [the longest x1 1.89 us: local(): w_pieces += early + [lax.ppermute(w_pieces[1], AXES, lay.swap(kc=1))]]
where the time goes in v18:
time: 133 us; the launch traced here: 132 us
  waiting for transfers between devices  48.4 us (36%)
  starting transfers between devices  43.1 us (32%)
  Pallas kernels  30.1 us (23%)
  other arithmetic  6 us (5%)
  local copies, waits for them, and re-layouts  3.1 us (2%)
    ppermute x4, starting transfers between devices, from_plane(): lax.ppermute(part, AXES, lay.from_plane(k))  15.4 us
    pallas_call x1, Pallas kernels, local(): call(functools.partial(forward_kernel, lay), 'forward', 14 * model * 1000...  11.9 us
    ppermute x3, waiting for transfers between devices, doubling(): return [held, lax.ppermute(held, AXES, swap(bits[-1]))]  11.8 us
    ppermute x2, waiting for transfers between devices, doubling(): got = lax.ppermute(held, AXES, swap(bit)) if first is None else first  11.7 us
    pallas_call x1, Pallas kernels, local(): call(functools.partial(backward_kernel, lay), 'backward', 10 * model * 10...  8.39 us
    ppermute x6, starting transfers between devices, over_chips(): got = [lax.ppermute(parts[k], AXES, chip_swap(k)) for k in range(1, chips)]  7.06 us
    ppermute x1, waiting for transfers between devices, local(): wo_own = lax.ppermute(late_w_out, AXES, lay.rows_to_chip())  5.28 us
    ppermute x6, waiting for transfers between devices, over_chips(): got = [lax.ppermute(parts[k], AXES, chip_swap(k)) for k in range(1, chips)]  5.26 us
  transfers between devices with their start and end apart: 29, of which 12 were waited for; matrix products, arithmetic and copies ran while one was open for 4% of the time, Pallas kernels for 11%

profile of v18, /device:TPU:4, one launch (start us, length us, event | category | flops | bytes accessed | tf_op | source)
XLA Modules:
  0.0 131.8 jit_solution(1791316784782249615)
XLA Ops:
  0.6 0.6 pad_add_fusion.1.pos_ref
  1.2 3.3 %start.1 = (bf16[1,2,64,1152]{3,2,1,0:T(8,128)(2,1)}, bf16[1,2,64,1152]{3,2,1,0:T(8,128)(2,1)}, bf16[144,432]{1,0:T(8,128)(2,1)}, bf16[144,432]{1,0:T(8,128)(2,1)}) custom-call(s32[4]{0:T(128)} %pad_add_fusion.1.pos_ref, bf16[1,128,1152]{2,1,0:T(8,128)(2,1)} %x_ref.1, bf16[1,128,1152]{2,1,0:T(8,128)(2,1)} %g_ref.1, bf16[144,3456]{1,0:T(8,128)(2,1)} %w_ref.1), custom_call_target="tpu_custom_call" | custom-call | flops 1179648000 | bytes 2359296 | tf_op jit(solution)/shard_map/start/pallas_call | solution.py:472
  4.5 1.9 %collective-permute-start.2 = (bf16[1,2,64,1152]{3,2,1,0:T(8,128)(2,1)}, bf16[1,2,64,1152]{3,2,1,0:T(8,128)(2,1)S(1)}, u32[]{:S(2)}, u32[]{:S(2)}) collective-permute-start(bf16[1,2,64,1152]{3,2,1,0:T(8,128)(2,1)} %get-tuple-element.57), channel_id=1, source_target_pairs={{0,0},{1,1},{2,16},{3,17},{4,2},{5,3},{6,18},{7,19},{8,20},{9,21},... | collective-permute-start | bytes 884744 | tf_op jit(solution)/shard_map/ppermute | solution.py:482
  6.5 0.6 copy-done.5
  7.2 0.1 fusion.7
  7.2 2.2 %collective-permute-start = (s32[1,16]{1,0:T(1,128)S(1)}, s32[1,16]{1,0:T(1,128)S(1)}, u32[]{:S(2)}, u32[]{:S(2)}) collective-permute-start(s32[1,16]{1,0:T(1,128)S(1)} %fusion.7), channel_id=1, source_target_pairs={{0,8},{1,9},{2,10},{3,11},{4,12},{5,13},{6,14},{7,15},{8,0},{9,1},... | collective-permute-start | bytes 200 | tf_op jit(solution)/shard_map/ppermute | solution.py:460
  9.4 1.5 %collective-permute-start.8 = (bf16[144,432]{1,0:T(8,128)(2,1)}, bf16[144,432]{1,0:T(8,128)(2,1)S(1)}, u32[]{:S(2)}, u32[]{:S(2)}) collective-permute-start(bf16[144,432]{1,0:T(8,128)(2,1)} %get-tuple-element.63), channel_id=1, source_target_pairs={{0,1},{1,0},{2,3},{3,2},{4,5},{5,4},{6,7},{7,6},{8,9},{9,8},{10,11... | collective-permute-start | bytes 373256 | tf_op jit(solution)/shard_map/ppermute | solution.py:484
  10.9 2.5 %collective-permute-start.3 = (bf16[1,2,64,1152]{3,2,1,0:T(8,128)(2,1)}, bf16[1,2,64,1152]{3,2,1,0:T(8,128)(2,1)S(1)}, u32[]{:S(2)}, u32[]{:S(2)}) collective-permute-start(bf16[1,2,64,1152]{3,2,1,0:T(8,128)(2,1)} %get-tuple-element.58), channel_id=1, source_target_pairs={{0,2},{1,3},{2,18},{3,19},{4,0},{5,1},{6,16},{7,17},{8,22},{9,23},... | collective-permute-start | bytes 884744 | tf_op jit(solution)/shard_map/ppermute | solution.py:482
  13.5 1.5 %collective-permute-start.1 = (s32[2,16]{1,0:T(2,128)S(1)}, s32[2,16]{1,0:T(2,128)S(1)}, u32[]{:S(2)}, u32[]{:S(2)}) collective-permute-start(s32[2,16]{1,0:T(2,128)S(1)} %pad_add_fusion), channel_id=1, source_target_pairs={{0,16},{1,17},{2,18},{3,19},{4,20},{5,21},{6,22},{7,23},{8,24},{9,... | collective-permute-start | bytes 392 | tf_op jit(solution)/shard_map/ppermute | solution.py:462
  15.0 0.8 collective-permute-start.4
  15.8 1.4 %collective-permute-done.1 = s32[2,16]{1,0:T(2,128)S(1)} collective-permute-done((s32[2,16]{1,0:T(2,128)S(1)}, s32[2,16]{1,0:T(2,128)S(1)}, u32[]{:S(2)}, u32[]{:S(2)}) %collective-permute-start.1) | collective-permute-done | bytes 160 | tf_op jit(solution)/shard_map/ppermute | solution.py:462
  17.1 0.6 fusion.2.info_ref
  17.7 0.9 broadcast_select_fusion.1
  18.7 4.3 %collective-permute-start.9 = (bf16[144,1152]{1,0:T(8,128)(2,1)S(1)}, bf16[144,1152]{1,0:T(8,128)(2,1)S(1)}, u32[]{:S(2)}, u32[]{:S(2)}) collective-permute-start(bf16[144,1152]{1,0:T(8,128)(2,1)S(1)} %copy-done.13), channel_id=1, source_target_pairs={{0,0},{1,1},{2,18},{3,19},{4,8},{5,9},{6,26},{7,27},{8,4},{9,5},{1... | collective-permute-start | bytes 995336 | tf_op jit(solution)/shard_map/ppermute | solution.py:495
  23.0 1.7 %collective-permute-done.3.refs_1_ = bf16[1,2,64,1152]{3,2,1,0:T(8,128)(2,1)S(1)} collective-permute-done((bf16[1,2,64,1152]{3,2,1,0:T(8,128)(2,1)}, bf16[1,2,64,1152]{3,2,1,0:T(8,128)(2,1)S(1)}, u32[]{:S(2)}, u32[]{:S(2)}) %collective-permute-start.3) | collective-permute-done | bytes 294944 | tf_op jit(solution)/shard_map/ppermute | solution.py:482
  24.7 1.0 collective-permute-start.6
  25.8 0.1 maximum_bitcast_fusion.2
  25.9 0.1 pad_maximum_fusion.refs_0_
  26.0 1.1 collective-permute-start.5
  27.0 5.3 %collective-permute-done.9.refs_8_ = bf16[144,1152]{1,0:T(8,128)(2,1)S(1)} collective-permute-done((bf16[144,1152]{1,0:T(8,128)(2,1)S(1)}, bf16[144,1152]{1,0:T(8,128)(2,1)S(1)}, u32[]{:S(2)}, u32[]{:S(2)}) %collective-permute-start.9) | collective-permute-done | bytes 331808 | tf_op jit(solution)/shard_map/ppermute | solution.py:495
  32.3 0.2 collective-permute-start.10
  32.5 2.1 %collective-permute-done.6 = bf16[1,2,64,1152]{3,2,1,0:T(8,128)(2,1)S(1)} collective-permute-done((bf16[1,2,64,1152]{3,2,1,0:T(8,128)(2,1)S(1)}, bf16[1,2,64,1152]{3,2,1,0:T(8,128)(2,1)S(1)}, u32[]{:S(2)}, u32[]{:S(2)}) %collective-permute-start.6) | collective-permute-done | bytes 294944 | tf_op jit(solution)/shard_map/ppermute | solution.py:450
  34.6 0.1 pad_maximum_fusion.1.refs_2_
  34.7 0.6 collective-permute-start.7
  35.3 9.6 %collective-permute-done.10 = bf16[1,144,864]{2,1,0:T(8,128)(2,1)S(1)} collective-permute-done((bf16[1,144,864]{2,1,0:T(8,128)(2,1)S(1)}, bf16[1,144,864]{2,1,0:T(8,128)(2,1)S(1)}, u32[]{:S(2)}, u32[]{:S(2)}) %collective-permute-start.10) | collective-permute-done | bytes 248864 | tf_op jit(solution)/shard_map/ppermute | solution.py:450
  44.9 0.1 pad_maximum_fusion.2.refs_4_.refs_0_
  45.0 0.1 collective-permute-start.12
  45.0 0.2 collective-permute-start.11
  45.3 0.3 collective-permute-start.13
  45.5 1.9 %collective-permute-done.13.refs_9_ = bf16[144,1152]{1,0:T(8,128)(2,1)S(1)} collective-permute-done((bf16[144,1152]{1,0:T(8,128)(2,1)S(1)}, bf16[144,1152]{1,0:T(8,128)(2,1)S(1)}, u32[]{:S(2)}, u32[]{:S(2)}) %collective-permute-start.13) | collective-permute-done | bytes 331808 | tf_op jit(solution)/shard_map/ppermute | solution.py:496
  47.4 11.8 %collective-permute-done.11.refs_5_.refs_1_ = bf16[2,144,864]{2,1,0:T(8,128)(2,1)S(1)} collective-permute-done((bf16[2,144,864]{2,1,0:T(8,128)(2,1)S(1)}, bf16[2,144,864]{2,1,0:T(8,128)(2,1)S(1)}, u32[]{:S(2)}, u32[]{:S(2)}) %collective-permute-start.11) | collective-permute-done | bytes 497696 | tf_op jit(solution)/shard_map/ppermute | solution.py:453
  59.2 0.1 collective-permute-start.14
  59.3 1.9 %collective-permute-done.14.refs_7_.refs_3_ = bf16[2,144,864]{2,1,0:T(8,128)(2,1)S(1)} collective-permute-done((bf16[2,144,864]{2,1,0:T(8,128)(2,1)S(1)}, bf16[2,144,864]{2,1,0:T(8,128)(2,1)S(1)}, u32[]{:S(2)}, u32[]{:S(2)}) %collective-permute-start.14) | collective-permute-done | bytes 497696 | tf_op jit(solution)/shard_map/ppermute | solution.py:506
  61.2 0.8 copy-done.12
  62.1 11.9 %forward.1 = (bf16[2,8,64,144]{3,2,1,0:T(8,128)(2,1)}, bf16[2,8,64,144]{3,2,1,0:T(8,128)(2,1)}, bf16[2,8,64,144]{3,2,1,0:T(8,128)(2,1)}, bf16[2,8,64,144]{3,2,1,...) custom-call(s32[4]{0:T(128)} %pad_add_fusion.1.pos_ref, ...), custom_call_target="tpu_custom_call" | custom-call | flops 8257536000 | bytes 2359296 | tf_op jit(solution)/shard_map/forward/pallas_call | solution.py:528
  74.0 0.1 collective-permute-start.15
  74.1 0.6 collective-permute-start.17
  74.7 0.1 collective-permute-start.18
  74.9 2.8 %collective-permute-start.19 = (bf16[2,64,1152]{2,1,0:T(8,128)(2,1)}, bf16[2,64,1152]{2,1,0:T(8,128)(2,1)S(1)}, u32[]{:S(2)}, u32[]{:S(2)}) collective-permute-start(bf16[2,64,1152]{2,1,0:T(8,128)(2,1)} %get-tuple-element.90), channel_id=1, source_target_pairs={{0,17},{1,16},{2,19},{3,18},{4,21},{5,20},{6,23},{7,22},{8,25},{9,... | collective-permute-start | bytes 884744 | tf_op jit(solution)/shard_map/ppermute | solution.py:456
  77.6 1.2 slice_add_fusion
  78.8 0.3 collective-permute-start.16
  79.1 8.4 %backward.1 = (f32[2,64,1152]{2,1,0:T(8,128)}, bf16[2,64,1152]{2,1,0:T(8,128)(2,1)}, bf16[2,64,1152]{2,1,0:T(8,128)(2,1)}, bf16[2,64,1152]{2,1,0:T(8,128)(2,1)}) custom-call(s32[4]{0:T(128)} %pad_add_fusion.1.pos_ref, s32[16]{0:T(128)} %fusion.2.info_ref, bf16[2,144,864]{2,1,0:T(8,128)(2,1)} %copy-done.2, bf16[2,144,864]{2,1,0:T(8,128)(2,1)} %copy-done.11, ...), custom_call_target="tpu_custom_call" | custom-call | flops 5898240000 | bytes 2359296 | tf_op jit(solution)/shard_map/backward/pallas_call | solution.py:556
  87.5 2.7 %collective-permute-done.18.refs_4_ = bf16[2,64,1152]{2,1,0:T(8,128)(2,1)S(1)} collective-permute-done((bf16[2,64,1152]{2,1,0:T(8,128)(2,1)}, bf16[2,64,1152]{2,1,0:T(8,128)(2,1)S(1)}, u32[]{:S(2)}, u32[]{:S(2)}) %collective-permute-start.18) | collective-permute-done | bytes 294944 | tf_op jit(solution)/shard_map/ppermute | solution.py:456
  90.3 1.5 %collective-permute-start.22 = (bf16[2,64,1152]{2,1,0:T(8,128)(2,1)}, bf16[2,64,1152]{2,1,0:T(8,128)(2,1)S(1)}, u32[]{:S(2)}, u32[]{:S(2)}) collective-permute-start(bf16[2,64,1152]{2,1,0:T(8,128)(2,1)} %get-tuple-element.98), channel_id=1, source_target_pairs={{0,1},{1,0},{2,3},{3,2},{4,5},{5,4},{6,7},{7,6},{8,9},{9,8},{10,11... | collective-permute-start | bytes 884744 | tf_op jit(solution)/shard_map/ppermute | solution.py:456
  91.8 0.2 collective-permute-start.23
  92.0 1.8 %collective-permute-start.24 = (bf16[2,64,1152]{2,1,0:T(8,128)(2,1)}, bf16[2,64,1152]{2,1,0:T(8,128)(2,1)S(1)}, u32[]{:S(2)}, u32[]{:S(2)}) collective-permute-start(bf16[2,64,1152]{2,1,0:T(8,128)(2,1)} %get-tuple-element.100), channel_id=1, source_target_pairs={{0,17},{1,16},{2,19},{3,18},{4,21},{5,20},{6,23},{7,22},{8,25},{9,... | collective-permute-start | bytes 884744 | tf_op jit(solution)/shard_map/ppermute | solution.py:456
  93.8 3.1 %output.1 = (bf16[64,1152]{1,0:T(8,128)(2,1)}, bf16[64,1152]{1,0:T(8,128)(2,1)}) custom-call(s32[4]{0:T(128)} %pad_add_fusion.1.pos_ref, s32[16]{0:T(128)} %fusion.2.info_ref, bf16[1,2,64,1152]{3,2,1,0:T(8,128)(2,1)} %copy-done.3, bf16[1,2,64,1152]{3,2,1,0:T(8,128)(2,1)} %copy-done.4, f32[2,64,1152]{2,1,0:T(8,128)} %get-tuple-element.91.refs_2_, ...), custom_call_target="tpu_custom_call" | custom-call | flops 11796480000 | bytes 2359296 | tf_op jit(solution)/shard_map/output/pallas_call | solution.py:569
  96.9 2.7 %collective-permute-start.20 = (bf16[64,1152]{1,0:T(8,128)(2,1)}, bf16[64,1152]{1,0:T(8,128)(2,1)S(1)}, u32[]{:S(2)}, u32[]{:S(2)}) collective-permute-start(bf16[64,1152]{1,0:T(8,128)(2,1)} %get-tuple-element.95), channel_id=1, source_target_pairs={{0,0},{1,1},{16,2},{17,3},{2,4},{3,5},{18,6},{19,7},{20,8},{21,9},... | collective-permute-start | bytes 442376 | tf_op jit(solution)/shard_map/ppermute | solution.py:443
  99.6 4.7 %collective-permute-start.21 = (bf16[64,1152]{1,0:T(8,128)(2,1)}, bf16[64,1152]{1,0:T(8,128)(2,1)S(1)}, u32[]{:S(2)}, u32[]{:S(2)}) collective-permute-start(bf16[64,1152]{1,0:T(8,128)(2,1)} %get-tuple-element.96), channel_id=1, source_target_pairs={{2,0},{3,1},{18,2},{19,3},{0,4},{1,5},{16,6},{17,7},{22,8},{23,9},... | collective-permute-start | bytes 442376 | tf_op jit(solution)/shard_map/ppermute | solution.py:443
  104.5 0.1 collective-permute-start.27
  104.5 2.5 %collective-permute-done.23.refs_4_ = bf16[2,64,1152]{2,1,0:T(8,128)(2,1)S(1)} collective-permute-done((bf16[2,64,1152]{2,1,0:T(8,128)(2,1)}, bf16[2,64,1152]{2,1,0:T(8,128)(2,1)S(1)}, u32[]{:S(2)}, u32[]{:S(2)}) %collective-permute-start.23) | collective-permute-done | bytes 294944 | tf_op jit(solution)/shard_map/ppermute | solution.py:456
  107.1 0.7 copy-done.20
  107.8 0.7 copy-done.21
  108.5 3.4 %input_grad.1 = (bf16[64,1152]{1,0:T(8,128)(2,1)}, bf16[64,1152]{1,0:T(8,128)(2,1)}) custom-call(s32[4]{0:T(128)} %pad_add_fusion.1.pos_ref, s32[16]{0:T(128)} %fusion.2.info_ref, bf16[1,2,64,1152]{3,2,1,0:T(8,128)(2,1)} %copy-done.3, bf16[1,2,64,1152]{3,2,1,0:T(8,128)(2,1)} %copy-done.4, f32[2,64,1152]{2,1,0:T(8,128)} %get-tuple-element.101.refs_2_, ...), custom_call_target="tpu_custom_call" | custom-call | flops 1769472000 | bytes 2359296 | tf_op jit(solution)/shard_map/input_grad/pallas_call | solution.py:581
  111.9 3.4 %collective-permute-start.25 = (bf16[64,1152]{1,0:T(8,128)(2,1)}, bf16[64,1152]{1,0:T(8,128)(2,1)S(1)}, u32[]{:S(2)}, u32[]{:S(2)}) collective-permute-start(bf16[64,1152]{1,0:T(8,128)(2,1)} %get-tuple-element.105), channel_id=1, source_target_pairs={{0,0},{1,1},{16,2},{17,3},{2,4},{3,5},{18,6},{19,7},{20,8},{21,9},... | collective-permute-start | bytes 442376 | tf_op jit(solution)/shard_map/ppermute | solution.py:443
  115.3 4.6 %collective-permute-start.26 = (bf16[64,1152]{1,0:T(8,128)(2,1)}, bf16[64,1152]{1,0:T(8,128)(2,1)S(1)}, u32[]{:S(2)}, u32[]{:S(2)}) collective-permute-start(bf16[64,1152]{1,0:T(8,128)(2,1)} %get-tuple-element.106), channel_id=1, source_target_pairs={{2,0},{3,1},{18,2},{19,3},{0,4},{1,5},{16,6},{17,7},{22,8},{23,9},... | collective-permute-start | bytes 442376 | tf_op jit(solution)/shard_map/ppermute | solution.py:443
  120.0 1.9 %collective-permute-start.28 = (f32[48,864]{1,0:T(8,128)S(1)}, f32[48,864]{1,0:T(8,128)S(1)}, u32[]{:S(2)}, u32[]{:S(2)}) collective-permute-start(f32[48,864]{1,0:T(8,128)S(1)} %bitcast.28), channel_id=1, source_target_pairs={{0,0},{1,1},{2,8},{3,9},{4,16},{5,17},{6,24},{7,25},{8,4},{9,5},{1... | collective-permute-start | bytes 497672 | tf_op jit(solution)/shard_map/ppermute | solution.py:597
  121.9 2.4 %collective-permute-done.26 = bf16[64,1152]{1,0:T(8,128)(2,1)S(1)} collective-permute-done((bf16[64,1152]{1,0:T(8,128)(2,1)}, bf16[64,1152]{1,0:T(8,128)(2,1)S(1)}, u32[]{:S(2)}, u32[]{:S(2)}) %collective-permute-start.26) | collective-permute-done | bytes 147488 | tf_op jit(solution)/shard_map/ppermute | solution.py:443
  124.4 0.1 broadcast_select_fusion.3
  124.4 0.7 maximum_bitcast_fusion.1
  125.2 0.7 maximum_bitcast_fusion
  125.9 5.1 %collective-permute-done.28 = f32[48,864]{1,0:T(8,128)S(1)} collective-permute-done((f32[48,864]{1,0:T(8,128)S(1)}, f32[48,864]{1,0:T(8,128)S(1)}, u32[]{:S(2)}, u32[]{:S(2)}) %collective-permute-start.28) | collective-permute-done | bytes 165920 | tf_op jit(solution)/shard_map/ppermute | solution.py:597
  131.0 0.1 fusion.6
  131.1 0.7 maximum_multiply_fusion
  (61 shorter events, 0.2 us)
Async XLA Ops:
  4.5 10.4 %collective-permute-start.2 = (bf16[1,2,64,1152]{3,2,1,0:T(8,128)(2,1)}, bf16[1,2,64,1152]{3,2,1,0:T(8,128)(2,1)S(1)}, u32[]{:S(2)}, u32[]{:S(2)}) collective-permute-start(bf16[1,2,64,1152]{3,2,1,0:T(8,128)(2,1)} %get-tuple-element.57), channel_id=1, source_target_pairs={{0,0},{1,1},{2,16},{3,17},{4,2},{5,3},{6,18},{7,19},{8,20},{9,21},... | collective-permute-start | bytes 884744 | tf_op jit(solution)/shard_map/ppermute | solution.py:482
  6.5 0.7 copy-start.5
  6.5 0.7 copy-start.6
  6.5 0.7 copy-start.7
  7.2 6.2 %collective-permute-start = (s32[1,16]{1,0:T(1,128)S(1)}, s32[1,16]{1,0:T(1,128)S(1)}, u32[]{:S(2)}, u32[]{:S(2)}) collective-permute-start(s32[1,16]{1,0:T(1,128)S(1)} %fusion.7), channel_id=1, source_target_pairs={{0,8},{1,9},{2,10},{3,11},{4,12},{5,13},{6,14},{7,15},{8,0},{9,1},... | collective-permute-start | bytes 200 | tf_op jit(solution)/shard_map/ppermute | solution.py:460
  9.4 8.3 %collective-permute-start.8 = (bf16[144,432]{1,0:T(8,128)(2,1)}, bf16[144,432]{1,0:T(8,128)(2,1)S(1)}, u32[]{:S(2)}, u32[]{:S(2)}) collective-permute-start(bf16[144,432]{1,0:T(8,128)(2,1)} %get-tuple-element.63), channel_id=1, source_target_pairs={{0,1},{1,0},{2,3},{3,2},{4,5},{5,4},{6,7},{7,6},{8,9},{9,8},{10,11... | collective-permute-start | bytes 373256 | tf_op jit(solution)/shard_map/ppermute | solution.py:484
  10.9 13.9 %collective-permute-start.3 = (bf16[1,2,64,1152]{3,2,1,0:T(8,128)(2,1)}, bf16[1,2,64,1152]{3,2,1,0:T(8,128)(2,1)S(1)}, u32[]{:S(2)}, u32[]{:S(2)}) collective-permute-start(bf16[1,2,64,1152]{3,2,1,0:T(8,128)(2,1)} %get-tuple-element.58), channel_id=1, source_target_pairs={{0,2},{1,3},{2,18},{3,19},{4,0},{5,1},{6,16},{7,17},{8,22},{9,23},... | collective-permute-start | bytes 884744 | tf_op jit(solution)/shard_map/ppermute | solution.py:482
  13.4 5.3 %copy-start.13 = (bf16[144,1152]{1,0:T(8,128)(2,1)S(1)}, bf16[144,1152]{1,0:T(8,128)(2,1)}, u32[]{:S(2)}) copy-start(bf16[144,1152]{1,0:T(8,128)(2,1)} %param.15) | copy-start | bytes 995332
  13.5 3.6 %collective-permute-start.1 = (s32[2,16]{1,0:T(2,128)S(1)}, s32[2,16]{1,0:T(2,128)S(1)}, u32[]{:S(2)}, u32[]{:S(2)}) collective-permute-start(s32[2,16]{1,0:T(2,128)S(1)} %pad_add_fusion), channel_id=1, source_target_pairs={{0,16},{1,17},{2,18},{3,19},{4,20},{5,21},{6,22},{7,23},{8,24},{9,... | collective-permute-start | bytes 392 | tf_op jit(solution)/shard_map/ppermute | solution.py:462
  15.0 10.9 %copy-start.3 = (bf16[1,2,64,1152]{3,2,1,0:T(8,128)(2,1)}, bf16[1,2,64,1152]{3,2,1,0:T(8,128)(2,1)S(1)}, u32[]{:S(2)}) copy-start(bf16[1,2,64,1152]{3,2,1,0:T(8,128)(2,1)S(1)} %collective-permute-done.2.refs_0_) | copy-start | bytes 884740
  15.0 9.8 %collective-permute-start.4 = (bf16[1,2,64,1152]{3,2,1,0:T(8,128)(2,1)S(1)}, bf16[1,2,64,1152]{3,2,1,0:T(8,128)(2,1)S(1)}, u32[]{:S(2)}, u32[]{:S(2)}) collective-permute-start(bf16[1,2,64,1152]{3,2,1,0:T(8,128)(2,1)S(1)} %collective-permute-done.2.refs_0_), channel_id=1, source_target_pairs={{0,1},{1,0},{2,3},{3,2},{4,5},{5,4},{6,7},{7,6},{8,9},{9,8},{10,11... | collective-permute-start | bytes 884744 | tf_op jit(solution)/shard_map/ppermute | solution.py:492
  18.7 13.6 %collective-permute-start.9 = (bf16[144,1152]{1,0:T(8,128)(2,1)S(1)}, bf16[144,1152]{1,0:T(8,128)(2,1)S(1)}, u32[]{:S(2)}, u32[]{:S(2)}) collective-permute-start(bf16[144,1152]{1,0:T(8,128)(2,1)S(1)} %copy-done.13), channel_id=1, source_target_pairs={{0,0},{1,1},{2,18},{3,19},{4,8},{5,9},{6,26},{7,27},{8,4},{9,5},{1... | collective-permute-start | bytes 995336 | tf_op jit(solution)/shard_map/ppermute | solution.py:495
  24.7 9.9 %copy-start.4 = (bf16[1,2,64,1152]{3,2,1,0:T(8,128)(2,1)}, bf16[1,2,64,1152]{3,2,1,0:T(8,128)(2,1)S(1)}, u32[]{:S(2)}) copy-start(bf16[1,2,64,1152]{3,2,1,0:T(8,128)(2,1)S(1)} %collective-permute-done.3.refs_1_) | copy-start | bytes 884740
  24.7 9.8 %collective-permute-start.6 = (bf16[1,2,64,1152]{3,2,1,0:T(8,128)(2,1)S(1)}, bf16[1,2,64,1152]{3,2,1,0:T(8,128)(2,1)S(1)}, u32[]{:S(2)}, u32[]{:S(2)}) collective-permute-start(bf16[1,2,64,1152]{3,2,1,0:T(8,128)(2,1)S(1)} %collective-permute-done.3.refs_1_), channel_id=1, source_target_pairs={{0,16},{1,17},{2,18},{3,19},{4,20},{5,21},{6,22},{7,23},{8,24},{9,... | collective-permute-start | bytes 884744 | tf_op jit(solution)/shard_map/ppermute | solution.py:450
  26.0 8.7 %copy-start = (bf16[2,2,64,1152]{3,2,1,0:T(8,128)(2,1)}, bf16[2,2,64,1152]{3,2,1,0:T(8,128)(2,1)S(1)}, u32[]{:S(2)}) copy-start(bf16[2,2,64,1152]{3,2,1,0:T(8,128)(2,1)S(1)} %pad_maximum_fusion.refs_0_) | copy-start | bytes 1769476
  26.0 21.4 %collective-permute-start.5 = (bf16[2,2,64,1152]{3,2,1,0:T(8,128)(2,1)S(1)}, bf16[2,2,64,1152]{3,2,1,0:T(8,128)(2,1)S(1)}, u32[]{:S(2)}, u32[]{:S(2)}) collective-permute-start(bf16[2,2,64,1152]{3,2,1,0:T(8,128)(2,1)S(1)} %pad_maximum_fusion.refs_0_), channel_id=1, source_target_pairs={{0,16},{1,17},{2,18},{3,19},{4,20},{5,21},{6,22},{7,23},{8,24},{9,... | collective-permute-start | bytes 1769480 | tf_op jit(solution)/shard_map/ppermute | solution.py:453
  32.3 13.0 %copy-start.14 = (bf16[144,1152]{1,0:T(8,128)(2,1)}, bf16[144,1152]{1,0:T(8,128)(2,1)S(1)}, u32[]{:S(2)}) copy-start(bf16[144,1152]{1,0:T(8,128)(2,1)S(1)} %collective-permute-done.9.refs_8_) | copy-start | bytes 995332
  32.3 12.6 %collective-permute-start.10 = (bf16[1,144,864]{2,1,0:T(8,128)(2,1)S(1)}, bf16[1,144,864]{2,1,0:T(8,128)(2,1)S(1)}, u32[]{:S(2)}, u32[]{:S(2)}) collective-permute-start(bf16[1,144,864]{2,1,0:T(8,128)(2,1)S(1)} %maximum_bitcast_fusion.2), channel_id=1, source_target_pairs={{0,4},{1,5},{2,6},{3,7},{4,0},{5,1},{6,2},{7,3},{8,12},{9,13},{10,... | collective-permute-start | bytes 746504 | tf_op jit(solution)/shard_map/ppermute | solution.py:450
  34.7 26.5 %copy-start.1 = (bf16[2,2,64,1152]{3,2,1,0:T(8,128)(2,1)}, bf16[2,2,64,1152]{3,2,1,0:T(8,128)(2,1)S(1)}, u32[]{:S(2)}) copy-start(bf16[2,2,64,1152]{3,2,1,0:T(8,128)(2,1)S(1)} %pad_maximum_fusion.1.refs_2_) | copy-start | bytes 1769476
  34.7 24.5 %collective-permute-start.7 = (bf16[2,2,64,1152]{3,2,1,0:T(8,128)(2,1)S(1)}, bf16[2,2,64,1152]{3,2,1,0:T(8,128)(2,1)S(1)}, u32[]{:S(2)}, u32[]{:S(2)}) collective-permute-start(bf16[2,2,64,1152]{3,2,1,0:T(8,128)(2,1)S(1)} %pad_maximum_fusion.1.refs_2_), channel_id=1, source_target_pairs={{0,1},{1,0},{2,3},{3,2},{4,5},{5,4},{6,7},{7,6},{8,9},{9,8},{10,11... | collective-permute-start | bytes 1769480 | tf_op jit(solution)/shard_map/ppermute | solution.py:453
  45.0 16.2 %copy-start.2 = (bf16[2,144,864]{2,1,0:T(8,128)(2,1)}, bf16[2,144,864]{2,1,0:T(8,128)(2,1)S(1)}, u32[]{:S(2)}) copy-start(bf16[2,144,864]{2,1,0:T(8,128)(2,1)S(1)} %pad_maximum_fusion.2.refs_4_.refs_0_) | copy-start | bytes 1492996
  45.0 2.4 %collective-permute-start.12 = (bf16[2,144,864]{2,1,0:T(8,128)(2,1)S(1)}, bf16[2,144,864]{2,1,0:T(8,128)(2,1)S(1)}, u32[]{:S(2)}, u32[]{:S(2)}) collective-permute-start(bf16[2,144,864]{2,1,0:T(8,128)(2,1)S(1)} %pad_maximum_fusion.2.refs_4_.refs_0_), channel_id=1, source_target_pairs={{0,8},{1,9},{2,10},{3,11},{4,12},{5,13},{6,14},{7,15},{8,0},{9,1},... | collective-permute-start | bytes 1493000 | tf_op jit(solution)/shard_map/ppermute | solution.py:503
  45.0 14.2 %collective-permute-start.11 = (bf16[2,144,864]{2,1,0:T(8,128)(2,1)S(1)}, bf16[2,144,864]{2,1,0:T(8,128)(2,1)S(1)}, u32[]{:S(2)}, u32[]{:S(2)}) collective-permute-start(bf16[2,144,864]{2,1,0:T(8,128)(2,1)S(1)} %pad_maximum_fusion.2.refs_4_.refs_0_), channel_id=1, source_target_pairs={{0,2},{1,3},{2,0},{3,1},{4,6},{5,7},{6,4},{7,5},{8,10},{9,11},{10,... | collective-permute-start | bytes 1493000 | tf_op jit(solution)/shard_map/ppermute | solution.py:453
  45.3 2.1 %collective-permute-start.13 = (bf16[144,1152]{1,0:T(8,128)(2,1)S(1)}, bf16[144,1152]{1,0:T(8,128)(2,1)S(1)}, u32[]{:S(2)}, u32[]{:S(2)}) collective-permute-start(bf16[144,1152]{1,0:T(8,128)(2,1)S(1)} %collective-permute-done.9.refs_8_), channel_id=1, source_target_pairs={{0,8},{1,9},{2,10},{3,11},{4,12},{5,13},{6,14},{7,15},{8,0},{9,1},... | collective-permute-start | bytes 995336 | tf_op jit(solution)/shard_map/ppermute | solution.py:496
  47.4 13.8 %copy-start.15 = (bf16[144,1152]{1,0:T(8,128)(2,1)}, bf16[144,1152]{1,0:T(8,128)(2,1)S(1)}, u32[]{:S(2)}) copy-start(bf16[144,1152]{1,0:T(8,128)(2,1)S(1)} %collective-permute-done.13.refs_9_) | copy-start | bytes 995332
  47.4 13.8 %copy-start.8 = (bf16[2,2,64,1152]{3,2,1,0:T(8,128)(2,1)}, bf16[2,2,64,1152]{3,2,1,0:T(8,128)(2,1)S(1)}, u32[]{:S(2)}) copy-start(bf16[2,2,64,1152]{3,2,1,0:T(8,128)(2,1)S(1)} %collective-permute-done.5.refs_1_) | copy-start | bytes 1769476
  47.4 13.8 %copy-start.10 = (bf16[2,144,864]{2,1,0:T(8,128)(2,1)}, bf16[2,144,864]{2,1,0:T(8,128)(2,1)S(1)}, u32[]{:S(2)}) copy-start(bf16[2,144,864]{2,1,0:T(8,128)(2,1)S(1)} %collective-permute-done.12.refs_6_.refs_2_) | copy-start | bytes 1492996
  59.2 2.0 %copy-start.11 = (bf16[2,144,864]{2,1,0:T(8,128)(2,1)}, bf16[2,144,864]{2,1,0:T(8,128)(2,1)S(1)}, u32[]{:S(2)}) copy-start(bf16[2,144,864]{2,1,0:T(8,128)(2,1)S(1)} %collective-permute-done.11.refs_5_.refs_1_) | copy-start | bytes 1492996
  59.2 2.0 %copy-start.9 = (bf16[2,2,64,1152]{3,2,1,0:T(8,128)(2,1)}, bf16[2,2,64,1152]{3,2,1,0:T(8,128)(2,1)S(1)}, u32[]{:S(2)}) copy-start(bf16[2,2,64,1152]{3,2,1,0:T(8,128)(2,1)S(1)} %collective-permute-done.7.refs_3_) | copy-start | bytes 1769476
  59.2 2.0 %collective-permute-start.14 = (bf16[2,144,864]{2,1,0:T(8,128)(2,1)S(1)}, bf16[2,144,864]{2,1,0:T(8,128)(2,1)S(1)}, u32[]{:S(2)}, u32[]{:S(2)}) collective-permute-start(bf16[2,144,864]{2,1,0:T(8,128)(2,1)S(1)} %collective-permute-done.11.refs_5_.refs_1_), channel_id=1, source_target_pairs={{0,8},{1,9},{2,10},{3,11},{4,12},{5,13},{6,14},{7,15},{8,0},{9,1},... | collective-permute-start | bytes 1493000 | tf_op jit(solution)/shard_map/ppermute | solution.py:506
  61.2 0.8 copy-start.12
  74.0 3.6 %collective-permute-start.15 = (f32[4,48,864]{2,1,0:T(8,128)}, f32[4,48,864]{2,1,0:T(8,128)S(1)}, u32[]{:S(2)}, u32[]{:S(2)}) collective-permute-start(f32[4,48,864]{2,1,0:T(8,128)} %get-tuple-element.80), channel_id=1, source_target_pairs={{0,8},{1,9},{2,10},{3,11},{4,12},{5,13},{6,14},{7,15},{8,0},{9,1},... | collective-permute-start | bytes 1990664 | tf_op jit(solution)/shard_map/ppermute | solution.py:548
  74.1 13.4 %collective-permute-start.17 = (bf16[2,64,1152]{2,1,0:T(8,128)(2,1)}, bf16[2,64,1152]{2,1,0:T(8,128)(2,1)S(1)}, u32[]{:S(2)}, u32[]{:S(2)}) collective-permute-start(bf16[2,64,1152]{2,1,0:T(8,128)(2,1)} %get-tuple-element.88), channel_id=1, source_target_pairs={{0,1},{1,0},{2,3},{3,2},{4,5},{5,4},{6,7},{7,6},{8,9},{9,8},{10,11... | collective-permute-start | bytes 884744 | tf_op jit(solution)/shard_map/ppermute | solution.py:456
  74.7 15.5 %collective-permute-start.18 = (bf16[2,64,1152]{2,1,0:T(8,128)(2,1)}, bf16[2,64,1152]{2,1,0:T(8,128)(2,1)S(1)}, u32[]{:S(2)}, u32[]{:S(2)}) collective-permute-start(bf16[2,64,1152]{2,1,0:T(8,128)(2,1)} %get-tuple-element.89), channel_id=1, source_target_pairs={{0,16},{1,17},{2,18},{3,19},{4,20},{5,21},{6,22},{7,23},{8,24},{9,... | collective-permute-start | bytes 884744 | tf_op jit(solution)/shard_map/ppermute | solution.py:456
  74.9 15.4 %collective-permute-start.19 = (bf16[2,64,1152]{2,1,0:T(8,128)(2,1)}, bf16[2,64,1152]{2,1,0:T(8,128)(2,1)S(1)}, u32[]{:S(2)}, u32[]{:S(2)}) collective-permute-start(bf16[2,64,1152]{2,1,0:T(8,128)(2,1)} %get-tuple-element.90), channel_id=1, source_target_pairs={{0,17},{1,16},{2,19},{3,18},{4,21},{5,20},{6,23},{7,22},{8,25},{9,... | collective-permute-start | bytes 884744 | tf_op jit(solution)/shard_map/ppermute | solution.py:456
  78.8 11.5 %collective-permute-start.16 = (f32[2,48,864]{2,1,0:T(8,128)S(1)}, f32[2,48,864]{2,1,0:T(8,128)S(1)}, u32[]{:S(2)}, u32[]{:S(2)}) collective-permute-start(f32[2,48,864]{2,1,0:T(8,128)S(1)} %get-tuple-element.86), channel_id=1, source_target_pairs={{0,2},{1,3},{2,0},{3,1},{4,6},{5,7},{6,4},{7,5},{8,10},{9,11},{10,... | collective-permute-start | bytes 995336 | tf_op jit(solution)/shard_map/ppermute | solution.py:554
  87.5 6.3 %copy-start.16 = (bf16[2,64,1152]{2,1,0:T(8,128)(2,1)}, bf16[2,64,1152]{2,1,0:T(8,128)(2,1)S(1)}, u32[]{:S(2)}) copy-start(bf16[2,64,1152]{2,1,0:T(8,128)(2,1)S(1)} %collective-permute-done.17.refs_3_) | copy-start | bytes 884740
  90.3 3.6 %copy-start.17 = (bf16[2,64,1152]{2,1,0:T(8,128)(2,1)}, bf16[2,64,1152]{2,1,0:T(8,128)(2,1)S(1)}, u32[]{:S(2)}) copy-start(bf16[2,64,1152]{2,1,0:T(8,128)(2,1)S(1)} %collective-permute-done.18.refs_4_) | copy-start | bytes 884740
  90.3 3.6 %copy-start.18 = (bf16[2,64,1152]{2,1,0:T(8,128)(2,1)}, bf16[2,64,1152]{2,1,0:T(8,128)(2,1)S(1)}, u32[]{:S(2)}) copy-start(bf16[2,64,1152]{2,1,0:T(8,128)(2,1)S(1)} %collective-permute-done.19.refs_5_) | copy-start | bytes 884740
  90.3 14.2 %collective-permute-start.22 = (bf16[2,64,1152]{2,1,0:T(8,128)(2,1)}, bf16[2,64,1152]{2,1,0:T(8,128)(2,1)S(1)}, u32[]{:S(2)}, u32[]{:S(2)}) collective-permute-start(bf16[2,64,1152]{2,1,0:T(8,128)(2,1)} %get-tuple-element.98), channel_id=1, source_target_pairs={{0,1},{1,0},{2,3},{3,2},{4,5},{5,4},{6,7},{7,6},{8,9},{9,8},{10,11... | collective-permute-start | bytes 884744 | tf_op jit(solution)/shard_map/ppermute | solution.py:456
  91.8 15.3 %collective-permute-start.23 = (bf16[2,64,1152]{2,1,0:T(8,128)(2,1)}, bf16[2,64,1152]{2,1,0:T(8,128)(2,1)S(1)}, u32[]{:S(2)}, u32[]{:S(2)}) collective-permute-start(bf16[2,64,1152]{2,1,0:T(8,128)(2,1)} %get-tuple-element.99), channel_id=1, source_target_pairs={{0,16},{1,17},{2,18},{3,19},{4,20},{5,21},{6,22},{7,23},{8,24},{9,... | collective-permute-start | bytes 884744 | tf_op jit(solution)/shard_map/ppermute | solution.py:456
  92.0 15.1 %collective-permute-start.24 = (bf16[2,64,1152]{2,1,0:T(8,128)(2,1)}, bf16[2,64,1152]{2,1,0:T(8,128)(2,1)S(1)}, u32[]{:S(2)}, u32[]{:S(2)}) collective-permute-start(bf16[2,64,1152]{2,1,0:T(8,128)(2,1)} %get-tuple-element.100), channel_id=1, source_target_pairs={{0,17},{1,16},{2,19},{3,18},{4,21},{5,20},{6,23},{7,22},{8,25},{9,... | collective-permute-start | bytes 884744 | tf_op jit(solution)/shard_map/ppermute | solution.py:456
  96.9 25.0 %collective-permute-start.20 = (bf16[64,1152]{1,0:T(8,128)(2,1)}, bf16[64,1152]{1,0:T(8,128)(2,1)S(1)}, u32[]{:S(2)}, u32[]{:S(2)}) collective-permute-start(bf16[64,1152]{1,0:T(8,128)(2,1)} %get-tuple-element.95), channel_id=1, source_target_pairs={{0,0},{1,1},{16,2},{17,3},{2,4},{3,5},{18,6},{19,7},{20,8},{21,9},... | collective-permute-start | bytes 442376 | tf_op jit(solution)/shard_map/ppermute | solution.py:443
  99.6 22.3 %collective-permute-start.21 = (bf16[64,1152]{1,0:T(8,128)(2,1)}, bf16[64,1152]{1,0:T(8,128)(2,1)S(1)}, u32[]{:S(2)}, u32[]{:S(2)}) collective-permute-start(bf16[64,1152]{1,0:T(8,128)(2,1)} %get-tuple-element.96), channel_id=1, source_target_pairs={{2,0},{3,1},{18,2},{19,3},{0,4},{1,5},{16,6},{17,7},{22,8},{23,9},... | collective-permute-start | bytes 442376 | tf_op jit(solution)/shard_map/ppermute | solution.py:443
  104.5 2.6 %copy-start.19 = (bf16[2,64,1152]{2,1,0:T(8,128)(2,1)}, bf16[2,64,1152]{2,1,0:T(8,128)(2,1)S(1)}, u32[]{:S(2)}) copy-start(bf16[2,64,1152]{2,1,0:T(8,128)(2,1)S(1)} %collective-permute-done.22.refs_3_) | copy-start | bytes 884740
  104.5 15.5 %collective-permute-start.27 = (f32[1,48,864]{2,1,0:T(8,128)S(1)}, f32[1,48,864]{2,1,0:T(8,128)S(1)}, u32[]{:S(2)}, u32[]{:S(2)}) collective-permute-start(f32[1,48,864]{2,1,0:T(8,128)S(1)} %slice.40), channel_id=1, source_target_pairs={{0,4},{1,5},{2,6},{3,7},{4,0},{5,1},{6,2},{7,3},{8,12},{9,13},{10,... | collective-permute-start | bytes 497672 | tf_op jit(solution)/shard_map/ppermute | solution.py:595
  107.1 0.7 copy-start.20
  107.8 0.7 copy-start.21
  111.9 10.0 %collective-permute-start.25 = (bf16[64,1152]{1,0:T(8,128)(2,1)}, bf16[64,1152]{1,0:T(8,128)(2,1)S(1)}, u32[]{:S(2)}, u32[]{:S(2)}) collective-permute-start(bf16[64,1152]{1,0:T(8,128)(2,1)} %get-tuple-element.105), channel_id=1, source_target_pairs={{0,0},{1,1},{16,2},{17,3},{2,4},{3,5},{18,6},{19,7},{20,8},{21,9},... | collective-permute-start | bytes 442376 | tf_op jit(solution)/shard_map/ppermute | solution.py:443
  115.3 9.1 %collective-permute-start.26 = (bf16[64,1152]{1,0:T(8,128)(2,1)}, bf16[64,1152]{1,0:T(8,128)(2,1)S(1)}, u32[]{:S(2)}, u32[]{:S(2)}) collective-permute-start(bf16[64,1152]{1,0:T(8,128)(2,1)} %get-tuple-element.106), channel_id=1, source_target_pairs={{2,0},{3,1},{18,2},{19,3},{0,4},{1,5},{16,6},{17,7},{22,8},{23,9},... | collective-permute-start | bytes 442376 | tf_op jit(solution)/shard_map/ppermute | solution.py:443
  120.0 11.0 %collective-permute-start.28 = (f32[48,864]{1,0:T(8,128)S(1)}, f32[48,864]{1,0:T(8,128)S(1)}, u32[]{:S(2)}, u32[]{:S(2)}) collective-permute-start(f32[48,864]{1,0:T(8,128)S(1)} %bitcast.28), channel_id=1, source_target_pairs={{0,0},{1,1},{2,8},{3,9},{4,16},{5,17},{6,24},{7,25},{8,4},{9,5},{1... | collective-permute-start | bytes 497672 | tf_op jit(solution)/shard_map/ppermute | solution.py:597

commit v19 on v18

--- a/solution.py
+++ b/solution.py
@@ -197,15 +197,14 @@
 
 
 def fill_weights(lay, pos_ref, w_refs, w_scr):
-    order = lay.doubled(lay.bits(lay.nz)[::-1])
     block = w_scr.shape[1] // lay.nz
     rows, width = w_refs[0].shape[1], w_scr.shape[2]
     for h in range(lay.halves):
-        for n, k in enumerate(order):
-            ref, place = w_refs[2 * h + (2 * n) // lay.nz], n % (lay.nz // 2)
+        for k in range(lay.nz):
+            ref = w_refs[h * lay.nz + k]
             for m in range(block // rows):
                 start = pl.multiple_of((pos_ref[2] ^ k) * block + m * rows, 16)
-                w_scr[h, pl.ds(start, rows), :] = ref[place, :, m * width : (m + 1) * width]
+                w_scr[h, pl.ds(start, rows), :] = ref[0, :, m * width : (m + 1) * width]
 
 
 def heads_stacked(lay, values):
@@ -243,7 +242,7 @@
 
 def forward_kernel(lay, pos_ref, info_ref, *refs):
     pair_refs, refs = refs[: 2 * lay.nc], refs[2 * lay.nc :]
-    w_refs, refs = refs[: 2 * lay.halves], refs[2 * lay.halves :]
+    w_refs, refs = refs[: lay.halves * lay.nz], refs[lay.halves * lay.nz :]
     wo_refs, refs = refs[: lay.nc], refs[lay.nc :]
     mod_ref, q_ref, k_ref, v_ref, ga_ref, kept_ref, sent_ref, *refs = refs
     pr_refs, refs = refs[: lay.chips], refs[lay.chips :]
@@ -317,7 +316,7 @@
 
 
 def backward_kernel(lay, pos_ref, info_ref, *refs):
-    w_refs, refs = refs[: 2 * lay.halves], refs[2 * lay.halves :]
+    w_refs, refs = refs[: lay.halves * lay.nz], refs[lay.halves * lay.nz :]
     q_ref, k_ref, v_ref, ga_ref, *refs = refs
     gh_refs, (w_scr, gt_scr) = refs[: lay.chips], refs[lay.chips :]
     _, frames, step_patches, cols = q_ref.shape
@@ -495,15 +494,24 @@
     wo_own = lax.ppermute(late_w_out, AXES, lay.rows_to_chip())
     wo_rows = [wo_own, lax.ppermute(wo_own, AXES, lay.swap(kc=1))]
     w_own, _ = lax.optimization_barrier((w_own, (own[1], wo_own)))
-    w_pieces = doubling(w_own, lay.bits(lay.nz)[::-1], lambda kz: lay.swap(kz=kz), [])
+    by_z = {0: w_own}
+    for bit in lay.bits(lay.nz):
+        by_z[bit] = lax.ppermute(w_own, AXES, lay.swap(kz=bit))
+    for k in range(1, lay.nz):
+        if k not in by_z:
+            forwarded = jnp.where(z < lay.nz, by_z[k ^ (k & -k)], w_own)
+            by_z[k] = lax.ppermute(forwarded, AXES, lay.swap(kz=k & -k))
+    w_pieces = [by_z[k] for k in range(lay.nz)]
+
     pairs = []
     for j in range(nc):
         after = ([], None) if j else (info, first)
         pairs += doubling(own[j], lay.chip_bits(j), chip_swap, *after)
-    early = [lax.ppermute(w_pieces[0], AXES, lay.swap(kc=1))] if halves > 1 else []
+    early = [lax.ppermute(piece, AXES, lay.swap(kc=1)) for piece in w_pieces[:2]]
+    early = early if halves > 1 else []
     pairs, w_pieces, early, wo_rows = lax.optimization_barrier((pairs, w_pieces, early, wo_rows))
     if halves > 1:
-        w_pieces += early + [lax.ppermute(w_pieces[1], AXES, lay.swap(kc=1))]
+        w_pieces += early + [lax.ppermute(piece, AXES, lay.swap(kc=1)) for piece in w_pieces[2:]]
 
 
     def spread(count, width, patches_at_once):
@@ -516,7 +524,7 @@
     few_steps = half // few
     x_spec = pl.BlockSpec((few, model), lambda i, *_: (i, 0))
     triple_spec = pl.BlockSpec((halves, lay.frames, step_patches, cols), lambda i, *_: (0, 0, i, 0))
-    w_specs = [whole_spec(w_pieces[0].shape)] * (2 * halves)
+    w_specs = [whole_spec(w_own.shape)] * (halves * lay.nz)
     w_scratch = pltpu.VMEM((halves, model, 3 * cols), BF16)
     mod_spec = whole_spec(mod_table.shape)
     triple_shape = struct((halves, lay.frames, half, cols))

time: 133 us -> 130 us (0.977)
  waiting for transfers between devices: 48.4 us -> 33.8 us
  starting transfers between devices: 43.1 us -> 54.5 us
    ppermute x2 -> x7, starting transfers between devices: 0.14 us -> 12.1 us  [the longest x2 9.93 us: local(): by_z[bit] = lax.ppermute(w_own, AXES, lay.swap(kz=bit))]
    ppermute x3 -> x2, waiting for transfers between devices: 11.8 us -> 0.01 us  [doubling(): return [held, lax.ppermute(held, AXES, swap(bits[-1]))]]
    ppermute x2 -> x7, waiting for transfers between devices: 1.89 us -> 11.8 us  [the longest x1 5.23 us: local(): by_z[k] = lax.ppermute(forwarded, AXES, lay.swap(kz=k & -k))]
    ppermute x2 -> x1, waiting for transfers between devices: 11.7 us -> 2.09 us  [doubling(): got = lax.ppermute(held, AXES, swap(bit)) if first is None else first]
    ppermute x1, waiting for transfers between devices: 5.09 us -> 2.45 us  [local(): grad_w = lax.ppermute(cut[0], AXES, lay.to_owner())]
    ppermute x4, waiting for transfers between devices: 2.45 us -> 5.01 us  [from_plane(): lax.ppermute(part, AXES, lay.from_plane(k))]
    ppermute x4, starting transfers between devices: 15.4 us -> 13.1 us  [from_plane(): lax.ppermute(part, AXES, lay.from_plane(k))]
    ppermute x1, waiting for transfers between devices: 1.86 us -> 0.01 us  [local(): wo_rows = [wo_own, lax.ppermute(wo_own, AXES, lay.swap(kc=1))]]
  transfers between devices with their start and end apart: 29 -> 32, of which waited for: 12 -> 13; matrix products, arithmetic and copies ran while one was open for 4% -> 4% of each run, Pallas kernels for 11% -> 12%
where the time goes in v19:
time: 130 us; the launch traced here: 129 us
  starting transfers between devices  54.5 us (42%)
  waiting for transfers between devices  33.8 us (26%)
  Pallas kernels  30.3 us (23%)
  other arithmetic  6 us (5%)
  local copies, waits for them, and re-layouts  3.25 us (2%)
    ppermute x4, starting transfers between devices, from_plane(): lax.ppermute(part, AXES, lay.from_plane(k))  13.1 us
    pallas_call x1, Pallas kernels, local(): call(functools.partial(forward_kernel, lay), 'forward', 14 * model * 1000...  12 us
    ppermute x2, starting transfers between devices, local(): by_z[bit] = lax.ppermute(w_own, AXES, lay.swap(kz=bit))  9.93 us
    pallas_call x1, Pallas kernels, local(): call(functools.partial(backward_kernel, lay), 'backward', 10 * model * 10...  8.59 us
    ppermute x6, starting transfers between devices, over_chips(): got = [lax.ppermute(parts[k], AXES, chip_swap(k)) for k in range(1, chips)]  7.06 us
    ppermute x1, waiting for transfers between devices, local(): wo_own = lax.ppermute(late_w_out, AXES, lay.rows_to_chip())  5.25 us
    ppermute x1, waiting for transfers between devices, local(): by_z[k] = lax.ppermute(forwarded, AXES, lay.swap(kz=k & -k))  5.23 us
    ppermute x2, waiting for transfers between devices, local(): by_z[bit] = lax.ppermute(w_own, AXES, lay.swap(kz=bit))  5.16 us
  transfers between devices with their start and end apart: 32, of which 13 were waited for; matrix products, arithmetic and copies ran while one was open for 4% of the time, Pallas kernels for 12%

profile of v19, /device:TPU:4, one launch (start us, length us, event | category | flops | bytes accessed | tf_op | source)
XLA Modules:
  0.0 129.0 jit_solution(12682137947652077450)
XLA Ops:
  0.6 0.7 pad_add_fusion.1.pos_ref
  1.3 3.3 %start.1 = (bf16[1,2,64,1152]{3,2,1,0:T(8,128)(2,1)}, bf16[1,2,64,1152]{3,2,1,0:T(8,128)(2,1)}, bf16[144,432]{1,0:T(8,128)(2,1)}, bf16[144,432]{1,0:T(8,128)(2,1)}) custom-call(s32[4]{0:T(128)} %pad_add_fusion.1.pos_ref, bf16[1,128,1152]{2,1,0:T(8,128)(2,1)} %x_ref.1, bf16[1,128,1152]{2,1,0:T(8,128)(2,1)} %g_ref.1, bf16[144,3456]{1,0:T(8,128)(2,1)} %w_ref.1), custom_call_target="tpu_custom_call" | custom-call | flops 1179648000 | bytes 2359296 | tf_op jit(solution)/shard_map/start/pallas_call | solution.py:471
  4.6 1.9 %collective-permute-start.2 = (bf16[1,2,64,1152]{3,2,1,0:T(8,128)(2,1)}, bf16[1,2,64,1152]{3,2,1,0:T(8,128)(2,1)S(1)}, u32[]{:S(2)}, u32[]{:S(2)}) collective-permute-start(bf16[1,2,64,1152]{3,2,1,0:T(8,128)(2,1)} %get-tuple-element.60), channel_id=1, source_target_pairs={{0,0},{1,1},{2,16},{3,17},{4,2},{5,3},{6,18},{7,19},{8,20},{9,21},... | collective-permute-start | bytes 884744 | tf_op jit(solution)/shard_map/ppermute | solution.py:481
  6.5 0.6 copy-done.6
  7.2 0.1 fusion.7
  7.3 2.2 %collective-permute-start = (s32[1,16]{1,0:T(1,128)S(1)}, s32[1,16]{1,0:T(1,128)S(1)}, u32[]{:S(2)}, u32[]{:S(2)}) collective-permute-start(s32[1,16]{1,0:T(1,128)S(1)} %fusion.7), channel_id=1, source_target_pairs={{0,8},{1,9},{2,10},{3,11},{4,12},{5,13},{6,14},{7,15},{8,0},{9,1},... | collective-permute-start | bytes 200 | tf_op jit(solution)/shard_map/ppermute | solution.py:459
  9.4 1.5 %collective-permute-start.8 = (bf16[144,432]{1,0:T(8,128)(2,1)}, bf16[144,432]{1,0:T(8,128)(2,1)S(1)}, u32[]{:S(2)}, u32[]{:S(2)}) collective-permute-start(bf16[144,432]{1,0:T(8,128)(2,1)} %get-tuple-element.66), channel_id=1, source_target_pairs={{0,1},{1,0},{2,3},{3,2},{4,5},{5,4},{6,7},{7,6},{8,9},{9,8},{10,11... | collective-permute-start | bytes 373256 | tf_op jit(solution)/shard_map/ppermute | solution.py:483
  10.9 2.5 %collective-permute-start.3 = (bf16[1,2,64,1152]{3,2,1,0:T(8,128)(2,1)}, bf16[1,2,64,1152]{3,2,1,0:T(8,128)(2,1)S(1)}, u32[]{:S(2)}, u32[]{:S(2)}) collective-permute-start(bf16[1,2,64,1152]{3,2,1,0:T(8,128)(2,1)} %get-tuple-element.61), channel_id=1, source_target_pairs={{0,2},{1,3},{2,18},{3,19},{4,0},{5,1},{6,16},{7,17},{8,22},{9,23},... | collective-permute-start | bytes 884744 | tf_op jit(solution)/shard_map/ppermute | solution.py:481
  13.5 1.5 %collective-permute-start.1 = (s32[2,16]{1,0:T(2,128)S(1)}, s32[2,16]{1,0:T(2,128)S(1)}, u32[]{:S(2)}, u32[]{:S(2)}) collective-permute-start(s32[2,16]{1,0:T(2,128)S(1)} %pad_add_fusion), channel_id=1, source_target_pairs={{0,16},{1,17},{2,18},{3,19},{4,20},{5,21},{6,22},{7,23},{8,24},{9,... | collective-permute-start | bytes 392 | tf_op jit(solution)/shard_map/ppermute | solution.py:461
  15.0 0.8 collective-permute-start.4
  15.8 1.4 %collective-permute-done.1 = s32[2,16]{1,0:T(2,128)S(1)} collective-permute-done((s32[2,16]{1,0:T(2,128)S(1)}, s32[2,16]{1,0:T(2,128)S(1)}, u32[]{:S(2)}, u32[]{:S(2)}) %collective-permute-start.1) | collective-permute-done | bytes 160 | tf_op jit(solution)/shard_map/ppermute | solution.py:461
  17.1 0.6 fusion.2.info_ref
  17.7 0.9 broadcast_select_fusion.2
  18.7 4.3 %collective-permute-start.9 = (bf16[144,1152]{1,0:T(8,128)(2,1)S(1)}, bf16[144,1152]{1,0:T(8,128)(2,1)S(1)}, u32[]{:S(2)}, u32[]{:S(2)}) collective-permute-start(bf16[144,1152]{1,0:T(8,128)(2,1)S(1)} %copy-done.11), channel_id=1, source_target_pairs={{0,0},{1,1},{2,18},{3,19},{4,8},{5,9},{6,26},{7,27},{8,4},{9,5},{1... | collective-permute-start | bytes 995336 | tf_op jit(solution)/shard_map/ppermute | solution.py:494
  23.0 1.7 %collective-permute-done.3.refs_1_ = bf16[1,2,64,1152]{3,2,1,0:T(8,128)(2,1)S(1)} collective-permute-done((bf16[1,2,64,1152]{3,2,1,0:T(8,128)(2,1)}, bf16[1,2,64,1152]{3,2,1,0:T(8,128)(2,1)S(1)}, u32[]{:S(2)}, u32[]{:S(2)}) %collective-permute-start.3) | collective-permute-done | bytes 294944 | tf_op jit(solution)/shard_map/ppermute | solution.py:481
  24.8 1.0 collective-permute-start.6
  25.8 0.1 maximum_bitcast_fusion.2.refs_4_.refs_0_
  25.9 0.1 pad_maximum_fusion.refs_0_
  26.0 1.1 collective-permute-start.5
  27.1 5.2 %collective-permute-done.9.refs_12_ = bf16[144,1152]{1,0:T(8,128)(2,1)S(1)} collective-permute-done((bf16[144,1152]{1,0:T(8,128)(2,1)S(1)}, bf16[144,1152]{1,0:T(8,128)(2,1)S(1)}, u32[]{:S(2)}, u32[]{:S(2)}) %collective-permute-start.9) | collective-permute-done | bytes 331808 | tf_op jit(solution)/shard_map/ppermute | solution.py:494
  32.3 0.2 collective-permute-start.11
  32.5 2.1 %collective-permute-done.6 = bf16[1,2,64,1152]{3,2,1,0:T(8,128)(2,1)S(1)} collective-permute-done((bf16[1,2,64,1152]{3,2,1,0:T(8,128)(2,1)S(1)}, bf16[1,2,64,1152]{3,2,1,0:T(8,128)(2,1)S(1)}, u32[]{:S(2)}, u32[]{:S(2)}) %collective-permute-start.6) | collective-permute-done | bytes 294944 | tf_op jit(solution)/shard_map/ppermute | solution.py:449
  34.6 0.1 pad_maximum_fusion.1.refs_2_
  34.7 0.6 collective-permute-start.7
  35.3 9.7 %collective-permute-start.10 = (bf16[1,144,864]{2,1,0:T(8,128)(2,1)S(1)}, bf16[1,144,864]{2,1,0:T(8,128)(2,1)}, u32[]{:S(2)}, u32[]{:S(2)}) collective-permute-start(bf16[1,144,864]{2,1,0:T(8,128)(2,1)S(1)} %maximum_bitcast_fusion.2.refs_4_.refs_0_), channel_id=1, source_target_pairs={{0,2},{1,3},{2,0},{3,1},{4,6},{5,7},{6,4},{7,5},{8,10},{9,11},{10,... | collective-permute-start | bytes 746504 | tf_op jit(solution)/shard_map/ppermute | solution.py:499
  45.1 0.3 collective-permute-start.15
  45.4 1.6 %collective-permute-start.12 = (bf16[1,144,864]{2,1,0:T(8,128)(2,1)S(1)}, bf16[1,144,864]{2,1,0:T(8,128)(2,1)S(1)}, u32[]{:S(2)}, u32[]{:S(2)}) collective-permute-start(bf16[1,144,864]{2,1,0:T(8,128)(2,1)S(1)} %broadcast_select_fusion), channel_id=1, source_target_pairs={{0,2},{1,3},{2,0},{3,1},{4,6},{5,7},{6,4},{7,5},{8,10},{9,11},{10,... | collective-permute-start | bytes 746504 | tf_op jit(solution)/shard_map/ppermute | solution.py:503
  47.1 5.2 %collective-permute-done.10.refs_5_.refs_1_ = bf16[1,144,864]{2,1,0:T(8,128)(2,1)} collective-permute-done((bf16[1,144,864]{2,1,0:T(8,128)(2,1)S(1)}, bf16[1,144,864]{2,1,0:T(8,128)(2,1)}, u32[]{:S(2)}, u32[]{:S(2)}) %collective-permute-start.10) | collective-permute-done | bytes 248864 | tf_op jit(solution)/shard_map/ppermute | solution.py:499
  52.2 5.2 %collective-permute-done.12.refs_7_.refs_3_ = bf16[1,144,864]{2,1,0:T(8,128)(2,1)S(1)} collective-permute-done((bf16[1,144,864]{2,1,0:T(8,128)(2,1)S(1)}, bf16[1,144,864]{2,1,0:T(8,128)(2,1)S(1)}, u32[]{:S(2)}, u32[]{:S(2)}) %collective-permute-start.12) | collective-permute-done | bytes 248864 | tf_op jit(solution)/shard_map/ppermute | solution.py:503
  57.5 0.1 collective-permute-start.16
  57.6 0.5 collective-permute-start.17
  58.1 1.0 collective-permute-done.16.refs_10_.refs_6_
  59.1 0.4 collective-permute-done.17.refs_11_.refs_7_
  59.5 0.3 copy-done.22
  59.8 0.7 copy-done.23
  60.5 12.0 %forward.1 = (bf16[2,8,64,144]{3,2,1,0:T(8,128)(2,1)}, bf16[2,8,64,144]{3,2,1,0:T(8,128)(2,1)}, bf16[2,8,64,144]{3,2,1,0:T(8,128)(2,1)}, bf16[2,8,64,144]{3,2,1,...) custom-call(s32[4]{0:T(128)} %pad_add_fusion.1.pos_ref, ...), custom_call_target="tpu_custom_call" | custom-call | flops 8257536000 | bytes 2359296 | tf_op jit(solution)/shard_map/forward/pallas_call | solution.py:536
  72.5 0.2 collective-permute-start.18
  72.6 1.2 collective-permute-start.20
  73.8 2.3 %collective-permute-start.22 = (bf16[2,64,1152]{2,1,0:T(8,128)(2,1)}, bf16[2,64,1152]{2,1,0:T(8,128)(2,1)S(1)}, u32[]{:S(2)}, u32[]{:S(2)}) collective-permute-start(bf16[2,64,1152]{2,1,0:T(8,128)(2,1)} %get-tuple-element.96), channel_id=1, source_target_pairs={{0,17},{1,16},{2,19},{3,18},{4,21},{5,20},{6,23},{7,22},{8,25},{9,... | collective-permute-start | bytes 884744 | tf_op jit(solution)/shard_map/ppermute | solution.py:455
  76.1 1.2 slice_add_fusion
  77.3 1.8 %collective-permute-start.19 = (f32[2,48,864]{2,1,0:T(8,128)S(1)}, f32[2,48,864]{2,1,0:T(8,128)S(1)}, u32[]{:S(2)}, u32[]{:S(2)}) collective-permute-start(f32[2,48,864]{2,1,0:T(8,128)S(1)} %get-tuple-element.92), channel_id=1, source_target_pairs={{0,2},{1,3},{2,0},{3,1},{4,6},{5,7},{6,4},{7,5},{8,10},{9,11},{10,... | collective-permute-start | bytes 995336 | tf_op jit(solution)/shard_map/ppermute | solution.py:562
  79.1 8.6 %backward.1 = (f32[2,64,1152]{2,1,0:T(8,128)}, bf16[2,64,1152]{2,1,0:T(8,128)(2,1)}, bf16[2,64,1152]{2,1,0:T(8,128)(2,1)}, bf16[2,64,1152]{2,1,0:T(8,128)(2,1)}) custom-call(s32[4]{0:T(128)} %pad_add_fusion.1.pos_ref, s32[16]{0:T(128)} %fusion.2.info_ref, bf16[1,144,864]{2,1,0:T(8,128)(2,1)} %copy-done, ...), custom_call_target="tpu_custom_call" | custom-call | flops 5898240000 | bytes 2359296 | tf_op jit(solution)/shard_map/backward/pallas_call | solution.py:564
  87.7 1.6 %collective-permute-done.21.refs_4_ = bf16[2,64,1152]{2,1,0:T(8,128)(2,1)S(1)} collective-permute-done((bf16[2,64,1152]{2,1,0:T(8,128)(2,1)}, bf16[2,64,1152]{2,1,0:T(8,128)(2,1)S(1)}, u32[]{:S(2)}, u32[]{:S(2)}) %collective-permute-start.21) | collective-permute-done | bytes 294944 | tf_op jit(solution)/shard_map/ppermute | solution.py:455
  89.4 0.9 collective-permute-start.25
  90.3 0.8 collective-permute-start.26
  91.1 1.8 %collective-permute-start.27 = (bf16[2,64,1152]{2,1,0:T(8,128)(2,1)}, bf16[2,64,1152]{2,1,0:T(8,128)(2,1)S(1)}, u32[]{:S(2)}, u32[]{:S(2)}) collective-permute-start(bf16[2,64,1152]{2,1,0:T(8,128)(2,1)} %get-tuple-element.106), channel_id=1, source_target_pairs={{0,17},{1,16},{2,19},{3,18},{4,21},{5,20},{6,23},{7,22},{8,25},{9,... | collective-permute-start | bytes 884744 | tf_op jit(solution)/shard_map/ppermute | solution.py:455
  92.9 3.1 %output.1 = (bf16[64,1152]{1,0:T(8,128)(2,1)}, bf16[64,1152]{1,0:T(8,128)(2,1)}) custom-call(s32[4]{0:T(128)} %pad_add_fusion.1.pos_ref, s32[16]{0:T(128)} %fusion.2.info_ref, bf16[1,2,64,1152]{3,2,1,0:T(8,128)(2,1)} %copy-done.3, bf16[1,2,64,1152]{3,2,1,0:T(8,128)(2,1)} %copy-done.4, f32[2,64,1152]{2,1,0:T(8,128)} %get-tuple-element.97.refs_2_, ...), custom_call_target="tpu_custom_call" | custom-call | flops 11796480000 | bytes 2359296 | tf_op jit(solution)/shard_map/output/pallas_call | solution.py:577
  96.0 3.6 %collective-permute-start.23 = (bf16[64,1152]{1,0:T(8,128)(2,1)}, bf16[64,1152]{1,0:T(8,128)(2,1)S(1)}, u32[]{:S(2)}, u32[]{:S(2)}) collective-permute-start(bf16[64,1152]{1,0:T(8,128)(2,1)} %get-tuple-element.101), channel_id=1, source_target_pairs={{0,0},{1,1},{16,2},{17,3},{2,4},{3,5},{18,6},{19,7},{20,8},{21,9},... | collective-permute-start | bytes 442376 | tf_op jit(solution)/shard_map/ppermute | solution.py:442
  99.6 1.9 %collective-permute-start.24 = (bf16[64,1152]{1,0:T(8,128)(2,1)}, bf16[64,1152]{1,0:T(8,128)(2,1)S(1)}, u32[]{:S(2)}, u32[]{:S(2)}) collective-permute-start(bf16[64,1152]{1,0:T(8,128)(2,1)} %get-tuple-element.102), channel_id=1, source_target_pairs={{2,0},{3,1},{18,2},{19,3},{0,4},{1,5},{16,6},{17,7},{22,8},{23,9},... | collective-permute-start | bytes 442376 | tf_op jit(solution)/shard_map/ppermute | solution.py:442
  101.6 0.8 collective-permute-start.30
  102.4 2.5 %collective-permute-done.26.refs_4_ = bf16[2,64,1152]{2,1,0:T(8,128)(2,1)S(1)} collective-permute-done((bf16[2,64,1152]{2,1,0:T(8,128)(2,1)}, bf16[2,64,1152]{2,1,0:T(8,128)(2,1)S(1)}, u32[]{:S(2)}, u32[]{:S(2)}) %collective-permute-start.26) | collective-permute-done | bytes 294944 | tf_op jit(solution)/shard_map/ppermute | solution.py:455
  104.8 0.7 copy-done.18
  105.6 0.7 copy-done.19
  106.3 3.4 %input_grad.1 = (bf16[64,1152]{1,0:T(8,128)(2,1)}, bf16[64,1152]{1,0:T(8,128)(2,1)}) custom-call(s32[4]{0:T(128)} %pad_add_fusion.1.pos_ref, s32[16]{0:T(128)} %fusion.2.info_ref, bf16[1,2,64,1152]{3,2,1,0:T(8,128)(2,1)} %copy-done.3, bf16[1,2,64,1152]{3,2,1,0:T(8,128)(2,1)} %copy-done.4, f32[2,64,1152]{2,1,0:T(8,128)} %get-tuple-element.107.refs_2_, ...), custom_call_target="tpu_custom_call" | custom-call | flops 1769472000 | bytes 2359296 | tf_op jit(solution)/shard_map/input_grad/pallas_call | solution.py:589
  109.7 5.6 %collective-permute-start.28 = (bf16[64,1152]{1,0:T(8,128)(2,1)}, bf16[64,1152]{1,0:T(8,128)(2,1)S(1)}, u32[]{:S(2)}, u32[]{:S(2)}) collective-permute-start(bf16[64,1152]{1,0:T(8,128)(2,1)} %get-tuple-element.111), channel_id=1, source_target_pairs={{0,0},{1,1},{16,2},{17,3},{2,4},{3,5},{18,6},{19,7},{20,8},{21,9},... | collective-permute-start | bytes 442376 | tf_op jit(solution)/shard_map/ppermute | solution.py:442
  115.3 1.9 %collective-permute-start.29 = (bf16[64,1152]{1,0:T(8,128)(2,1)}, bf16[64,1152]{1,0:T(8,128)(2,1)S(1)}, u32[]{:S(2)}, u32[]{:S(2)}) collective-permute-start(bf16[64,1152]{1,0:T(8,128)(2,1)} %get-tuple-element.112), channel_id=1, source_target_pairs={{2,0},{3,1},{18,2},{19,3},{0,4},{1,5},{16,6},{17,7},{22,8},{23,9},... | collective-permute-start | bytes 442376 | tf_op jit(solution)/shard_map/ppermute | solution.py:442
  117.3 1.9 %collective-permute-start.31 = (f32[48,864]{1,0:T(8,128)S(1)}, f32[48,864]{1,0:T(8,128)S(1)}, u32[]{:S(2)}, u32[]{:S(2)}) collective-permute-start(f32[48,864]{1,0:T(8,128)S(1)} %bitcast.28), channel_id=1, source_target_pairs={{0,0},{1,1},{2,8},{3,9},{4,16},{5,17},{6,24},{7,25},{8,4},{9,5},{1... | collective-permute-start | bytes 497672 | tf_op jit(solution)/shard_map/ppermute | solution.py:605
  119.2 0.3 collective-permute-done.28
  119.5 4.7 %collective-permute-done.29 = bf16[64,1152]{1,0:T(8,128)(2,1)S(1)} collective-permute-done((bf16[64,1152]{1,0:T(8,128)(2,1)}, bf16[64,1152]{1,0:T(8,128)(2,1)S(1)}, u32[]{:S(2)}, u32[]{:S(2)}) %collective-permute-start.29) | collective-permute-done | bytes 147488 | tf_op jit(solution)/shard_map/ppermute | solution.py:442
  124.3 0.7 maximum_bitcast_fusion.1
  125.0 0.7 maximum_bitcast_fusion
  125.8 2.5 %collective-permute-done.31 = f32[48,864]{1,0:T(8,128)S(1)} collective-permute-done((f32[48,864]{1,0:T(8,128)S(1)}, f32[48,864]{1,0:T(8,128)S(1)}, u32[]{:S(2)}, u32[]{:S(2)}) %collective-permute-start.31) | collective-permute-done | bytes 165920 | tf_op jit(solution)/shard_map/ppermute | solution.py:605
  128.2 0.1 fusion.6
  128.3 0.7 maximum_multiply_fusion
  (71 shorter events, 0.4 us)
Async XLA Ops:
  4.6 10.4 %collective-permute-start.2 = (bf16[1,2,64,1152]{3,2,1,0:T(8,128)(2,1)}, bf16[1,2,64,1152]{3,2,1,0:T(8,128)(2,1)S(1)}, u32[]{:S(2)}, u32[]{:S(2)}) collective-permute-start(bf16[1,2,64,1152]{3,2,1,0:T(8,128)(2,1)} %get-tuple-element.60), channel_id=1, source_target_pairs={{0,0},{1,1},{2,16},{3,17},{4,2},{5,3},{6,18},{7,19},{8,20},{9,21},... | collective-permute-start | bytes 884744 | tf_op jit(solution)/shard_map/ppermute | solution.py:481
  6.5 0.7 copy-start.6
  6.5 0.7 copy-start.7
  6.5 0.7 copy-start.8
  7.3 6.2 %collective-permute-start = (s32[1,16]{1,0:T(1,128)S(1)}, s32[1,16]{1,0:T(1,128)S(1)}, u32[]{:S(2)}, u32[]{:S(2)}) collective-permute-start(s32[1,16]{1,0:T(1,128)S(1)} %fusion.7), channel_id=1, source_target_pairs={{0,8},{1,9},{2,10},{3,11},{4,12},{5,13},{6,14},{7,15},{8,0},{9,1},... | collective-permute-start | bytes 200 | tf_op jit(solution)/shard_map/ppermute | solution.py:459
  9.4 8.3 %collective-permute-start.8 = (bf16[144,432]{1,0:T(8,128)(2,1)}, bf16[144,432]{1,0:T(8,128)(2,1)S(1)}, u32[]{:S(2)}, u32[]{:S(2)}) collective-permute-start(bf16[144,432]{1,0:T(8,128)(2,1)} %get-tuple-element.66), channel_id=1, source_target_pairs={{0,1},{1,0},{2,3},{3,2},{4,5},{5,4},{6,7},{7,6},{8,9},{9,8},{10,11... | collective-permute-start | bytes 373256 | tf_op jit(solution)/shard_map/ppermute | solution.py:483
  10.9 13.9 %collective-permute-start.3 = (bf16[1,2,64,1152]{3,2,1,0:T(8,128)(2,1)}, bf16[1,2,64,1152]{3,2,1,0:T(8,128)(2,1)S(1)}, u32[]{:S(2)}, u32[]{:S(2)}) collective-permute-start(bf16[1,2,64,1152]{3,2,1,0:T(8,128)(2,1)} %get-tuple-element.61), channel_id=1, source_target_pairs={{0,2},{1,3},{2,18},{3,19},{4,0},{5,1},{6,16},{7,17},{8,22},{9,23},... | collective-permute-start | bytes 884744 | tf_op jit(solution)/shard_map/ppermute | solution.py:481
  13.4 5.2 %copy-start.11 = (bf16[144,1152]{1,0:T(8,128)(2,1)S(1)}, bf16[144,1152]{1,0:T(8,128)(2,1)}, u32[]{:S(2)}) copy-start(bf16[144,1152]{1,0:T(8,128)(2,1)} %param.15) | copy-start | bytes 995332
  13.5 3.6 %collective-permute-start.1 = (s32[2,16]{1,0:T(2,128)S(1)}, s32[2,16]{1,0:T(2,128)S(1)}, u32[]{:S(2)}, u32[]{:S(2)}) collective-permute-start(s32[2,16]{1,0:T(2,128)S(1)} %pad_add_fusion), channel_id=1, source_target_pairs={{0,16},{1,17},{2,18},{3,19},{4,20},{5,21},{6,22},{7,23},{8,24},{9,... | collective-permute-start | bytes 392 | tf_op jit(solution)/shard_map/ppermute | solution.py:461
  15.0 10.9 %copy-start.3 = (bf16[1,2,64,1152]{3,2,1,0:T(8,128)(2,1)}, bf16[1,2,64,1152]{3,2,1,0:T(8,128)(2,1)S(1)}, u32[]{:S(2)}) copy-start(bf16[1,2,64,1152]{3,2,1,0:T(8,128)(2,1)S(1)} %collective-permute-done.2.refs_0_) | copy-start | bytes 884740
  15.0 9.8 %collective-permute-start.4 = (bf16[1,2,64,1152]{3,2,1,0:T(8,128)(2,1)S(1)}, bf16[1,2,64,1152]{3,2,1,0:T(8,128)(2,1)S(1)}, u32[]{:S(2)}, u32[]{:S(2)}) collective-permute-start(bf16[1,2,64,1152]{3,2,1,0:T(8,128)(2,1)S(1)} %collective-permute-done.2.refs_0_), channel_id=1, source_target_pairs={{0,1},{1,0},{2,3},{3,2},{4,5},{5,4},{6,7},{7,6},{8,9},{9,8},{10,11... | collective-permute-start | bytes 884744 | tf_op jit(solution)/shard_map/ppermute | solution.py:491
  18.7 13.6 %collective-permute-start.9 = (bf16[144,1152]{1,0:T(8,128)(2,1)S(1)}, bf16[144,1152]{1,0:T(8,128)(2,1)S(1)}, u32[]{:S(2)}, u32[]{:S(2)}) collective-permute-start(bf16[144,1152]{1,0:T(8,128)(2,1)S(1)} %copy-done.11), channel_id=1, source_target_pairs={{0,0},{1,1},{2,18},{3,19},{4,8},{5,9},{6,26},{7,27},{8,4},{9,5},{1... | collective-permute-start | bytes 995336 | tf_op jit(solution)/shard_map/ppermute | solution.py:494
  24.8 9.9 %copy-start.4 = (bf16[1,2,64,1152]{3,2,1,0:T(8,128)(2,1)}, bf16[1,2,64,1152]{3,2,1,0:T(8,128)(2,1)S(1)}, u32[]{:S(2)}) copy-start(bf16[1,2,64,1152]{3,2,1,0:T(8,128)(2,1)S(1)} %collective-permute-done.3.refs_1_) | copy-start | bytes 884740
  24.8 9.8 %collective-permute-start.6 = (bf16[1,2,64,1152]{3,2,1,0:T(8,128)(2,1)S(1)}, bf16[1,2,64,1152]{3,2,1,0:T(8,128)(2,1)S(1)}, u32[]{:S(2)}, u32[]{:S(2)}) collective-permute-start(bf16[1,2,64,1152]{3,2,1,0:T(8,128)(2,1)S(1)} %collective-permute-done.3.refs_1_), channel_id=1, source_target_pairs={{0,16},{1,17},{2,18},{3,19},{4,20},{5,21},{6,22},{7,23},{8,24},{9,... | collective-permute-start | bytes 884744 | tf_op jit(solution)/shard_map/ppermute | solution.py:449
  25.9 19.4 %copy-start = (bf16[1,144,864]{2,1,0:T(8,128)(2,1)}, bf16[1,144,864]{2,1,0:T(8,128)(2,1)S(1)}, u32[]{:S(2)}) copy-start(bf16[1,144,864]{2,1,0:T(8,128)(2,1)S(1)} %maximum_bitcast_fusion.2.refs_4_.refs_0_) | copy-start | bytes 746500
  26.0 19.0 %copy-start.1 = (bf16[2,2,64,1152]{3,2,1,0:T(8,128)(2,1)}, bf16[2,2,64,1152]{3,2,1,0:T(8,128)(2,1)S(1)}, u32[]{:S(2)}) copy-start(bf16[2,2,64,1152]{3,2,1,0:T(8,128)(2,1)S(1)} %pad_maximum_fusion.refs_0_) | copy-start | bytes 1769476
  26.0 31.5 %collective-permute-start.5 = (bf16[2,2,64,1152]{3,2,1,0:T(8,128)(2,1)S(1)}, bf16[2,2,64,1152]{3,2,1,0:T(8,128)(2,1)S(1)}, u32[]{:S(2)}, u32[]{:S(2)}) collective-permute-start(bf16[2,2,64,1152]{3,2,1,0:T(8,128)(2,1)S(1)} %pad_maximum_fusion.refs_0_), channel_id=1, source_target_pairs={{0,16},{1,17},{2,18},{3,19},{4,20},{5,21},{6,22},{7,23},{8,24},{9,... | collective-permute-start | bytes 1769480 | tf_op jit(solution)/shard_map/ppermute | solution.py:452
  32.3 12.7 %copy-start.12 = (bf16[144,1152]{1,0:T(8,128)(2,1)}, bf16[144,1152]{1,0:T(8,128)(2,1)S(1)}, u32[]{:S(2)}) copy-start(bf16[144,1152]{1,0:T(8,128)(2,1)S(1)} %collective-permute-done.9.refs_12_) | copy-start | bytes 995332
  32.3 12.7 %collective-permute-start.11 = (bf16[1,144,864]{2,1,0:T(8,128)(2,1)S(1)}, bf16[1,144,864]{2,1,0:T(8,128)(2,1)S(1)}, u32[]{:S(2)}, u32[]{:S(2)}) collective-permute-start(bf16[1,144,864]{2,1,0:T(8,128)(2,1)S(1)} %maximum_bitcast_fusion.2.refs_4_.refs_0_), channel_id=1, source_target_pairs={{0,4},{1,5},{2,6},{3,7},{4,0},{5,1},{6,2},{7,3},{8,12},{9,13},{10,... | collective-permute-start | bytes 746504 | tf_op jit(solution)/shard_map/ppermute | solution.py:499
  34.7 24.8 %copy-start.2 = (bf16[2,2,64,1152]{3,2,1,0:T(8,128)(2,1)}, bf16[2,2,64,1152]{3,2,1,0:T(8,128)(2,1)S(1)}, u32[]{:S(2)}) copy-start(bf16[2,2,64,1152]{3,2,1,0:T(8,128)(2,1)S(1)} %pad_maximum_fusion.1.refs_2_) | copy-start | bytes 1769476
  34.7 22.8 %collective-permute-start.7 = (bf16[2,2,64,1152]{3,2,1,0:T(8,128)(2,1)S(1)}, bf16[2,2,64,1152]{3,2,1,0:T(8,128)(2,1)S(1)}, u32[]{:S(2)}, u32[]{:S(2)}) collective-permute-start(bf16[2,2,64,1152]{3,2,1,0:T(8,128)(2,1)S(1)} %pad_maximum_fusion.1.refs_2_), channel_id=1, source_target_pairs={{0,1},{1,0},{2,3},{3,2},{4,5},{5,4},{6,7},{7,6},{8,9},{9,8},{10,11... | collective-permute-start | bytes 1769480 | tf_op jit(solution)/shard_map/ppermute | solution.py:452
  35.3 10.1 %collective-permute-start.13 = (bf16[1,144,864]{2,1,0:T(8,128)(2,1)S(1)}, bf16[1,144,864]{2,1,0:T(8,128)(2,1)}, u32[]{:S(2)}, u32[]{:S(2)}) collective-permute-start(bf16[1,144,864]{2,1,0:T(8,128)(2,1)S(1)} %maximum_bitcast_fusion.2.refs_4_.refs_0_), channel_id=1, source_target_pairs={{0,8},{1,9},{2,10},{3,11},{4,12},{5,13},{6,14},{7,15},{8,0},{9,1},... | collective-permute-start | bytes 746504 | tf_op jit(solution)/shard_map/ppermute | solution.py:510
  35.3 16.9 %collective-permute-start.10 = (bf16[1,144,864]{2,1,0:T(8,128)(2,1)S(1)}, bf16[1,144,864]{2,1,0:T(8,128)(2,1)}, u32[]{:S(2)}, u32[]{:S(2)}) collective-permute-start(bf16[1,144,864]{2,1,0:T(8,128)(2,1)S(1)} %maximum_bitcast_fusion.2.refs_4_.refs_0_), channel_id=1, source_target_pairs={{0,2},{1,3},{2,0},{3,1},{4,6},{5,7},{6,4},{7,5},{8,10},{9,11},{10,... | collective-permute-start | bytes 746504 | tf_op jit(solution)/shard_map/ppermute | solution.py:499
  45.0 14.4 %copy-start.5 = (bf16[1,144,864]{2,1,0:T(8,128)(2,1)}, bf16[1,144,864]{2,1,0:T(8,128)(2,1)S(1)}, u32[]{:S(2)}) copy-start(bf16[1,144,864]{2,1,0:T(8,128)(2,1)S(1)} %collective-permute-done.11.refs_6_.refs_2_) | copy-start | bytes 746500
  45.1 7.2 %collective-permute-start.15 = (bf16[144,1152]{1,0:T(8,128)(2,1)S(1)}, bf16[144,1152]{1,0:T(8,128)(2,1)S(1)}, u32[]{:S(2)}, u32[]{:S(2)}) collective-permute-start(bf16[144,1152]{1,0:T(8,128)(2,1)S(1)} %collective-permute-done.9.refs_12_), channel_id=1, source_target_pairs={{0,8},{1,9},{2,10},{3,11},{4,12},{5,13},{6,14},{7,15},{8,0},{9,1},... | collective-permute-start | bytes 995336 | tf_op jit(solution)/shard_map/ppermute | solution.py:495
  45.4 12.0 %collective-permute-start.12 = (bf16[1,144,864]{2,1,0:T(8,128)(2,1)S(1)}, bf16[1,144,864]{2,1,0:T(8,128)(2,1)S(1)}, u32[]{:S(2)}, u32[]{:S(2)}) collective-permute-start(bf16[1,144,864]{2,1,0:T(8,128)(2,1)S(1)} %broadcast_select_fusion), channel_id=1, source_target_pairs={{0,2},{1,3},{2,0},{3,1},{4,6},{5,7},{6,4},{7,5},{8,10},{9,11},{10,... | collective-permute-start | bytes 746504 | tf_op jit(solution)/shard_map/ppermute | solution.py:503
  52.2 5.2 %collective-permute-start.14 = (bf16[1,144,864]{2,1,0:T(8,128)(2,1)}, bf16[1,144,864]{2,1,0:T(8,128)(2,1)S(1)}, u32[]{:S(2)}, u32[]{:S(2)}) collective-permute-start(bf16[1,144,864]{2,1,0:T(8,128)(2,1)} %collective-permute-done.10.refs_5_.refs_1_), channel_id=1, source_target_pairs={{0,8},{1,9},{2,10},{3,11},{4,12},{5,13},{6,14},{7,15},{8,0},{9,1},... | collective-permute-start | bytes 746504 | tf_op jit(solution)/shard_map/ppermute | solution.py:510
  52.2 7.3 %copy-start.13 = (bf16[144,1152]{1,0:T(8,128)(2,1)}, bf16[144,1152]{1,0:T(8,128)(2,1)S(1)}, u32[]{:S(2)}) copy-start(bf16[144,1152]{1,0:T(8,128)(2,1)S(1)} %collective-permute-done.15.refs_13_) | copy-start | bytes 995332
  57.5 2.0 %copy-start.20 = (bf16[1,144,864]{2,1,0:T(8,128)(2,1)}, bf16[1,144,864]{2,1,0:T(8,128)(2,1)S(1)}, u32[]{:S(2)}) copy-start(bf16[1,144,864]{2,1,0:T(8,128)(2,1)S(1)} %collective-permute-done.12.refs_7_.refs_3_) | copy-start | bytes 746500
  57.5 2.0 %copy-start.21 = (bf16[1,144,864]{2,1,0:T(8,128)(2,1)}, bf16[1,144,864]{2,1,0:T(8,128)(2,1)S(1)}, u32[]{:S(2)}) copy-start(bf16[1,144,864]{2,1,0:T(8,128)(2,1)S(1)} %collective-permute-done.14.refs_9_.refs_5_) | copy-start | bytes 746500
  57.5 2.0 %copy-start.9 = (bf16[2,2,64,1152]{3,2,1,0:T(8,128)(2,1)}, bf16[2,2,64,1152]{3,2,1,0:T(8,128)(2,1)S(1)}, u32[]{:S(2)}) copy-start(bf16[2,2,64,1152]{3,2,1,0:T(8,128)(2,1)S(1)} %collective-permute-done.5.refs_1_) | copy-start | bytes 1769476
  57.5 2.0 %copy-start.10 = (bf16[2,2,64,1152]{3,2,1,0:T(8,128)(2,1)}, bf16[2,2,64,1152]{3,2,1,0:T(8,128)(2,1)S(1)}, u32[]{:S(2)}) copy-start(bf16[2,2,64,1152]{3,2,1,0:T(8,128)(2,1)S(1)} %collective-permute-done.7.refs_3_) | copy-start | bytes 1769476
  57.5 1.6 %collective-permute-start.16 = (bf16[1,144,864]{2,1,0:T(8,128)(2,1)S(1)}, bf16[1,144,864]{2,1,0:T(8,128)(2,1)S(1)}, u32[]{:S(2)}, u32[]{:S(2)}) collective-permute-start(bf16[1,144,864]{2,1,0:T(8,128)(2,1)S(1)} %collective-permute-done.11.refs_6_.refs_2_), channel_id=1, source_target_pairs={{0,8},{1,9},{2,10},{3,11},{4,12},{5,13},{6,14},{7,15},{8,0},{9,1},... | collective-permute-start | bytes 746504 | tf_op jit(solution)/shard_map/ppermute | solution.py:514
  57.6 1.9 %collective-permute-start.17 = (bf16[1,144,864]{2,1,0:T(8,128)(2,1)S(1)}, bf16[1,144,864]{2,1,0:T(8,128)(2,1)S(1)}, u32[]{:S(2)}, u32[]{:S(2)}) collective-permute-start(bf16[1,144,864]{2,1,0:T(8,128)(2,1)S(1)} %collective-permute-done.12.refs_7_.refs_3_), channel_id=1, source_target_pairs={{0,8},{1,9},{2,10},{3,11},{4,12},{5,13},{6,14},{7,15},{8,0},{9,1},... | collective-permute-start | bytes 746504 | tf_op jit(solution)/shard_map/ppermute | solution.py:514
  59.1 0.7 copy-start.22
  59.8 0.7 copy-start.23
  72.5 3.7 %collective-permute-start.18 = (f32[4,48,864]{2,1,0:T(8,128)}, f32[4,48,864]{2,1,0:T(8,128)S(1)}, u32[]{:S(2)}, u32[]{:S(2)}) collective-permute-start(f32[4,48,864]{2,1,0:T(8,128)} %get-tuple-element.86), channel_id=1, source_target_pairs={{0,8},{1,9},{2,10},{3,11},{4,12},{5,13},{6,14},{7,15},{8,0},{9,1},... | collective-permute-start | bytes 1990664 | tf_op jit(solution)/shard_map/ppermute | solution.py:556
  72.6 15.1 %collective-permute-start.20 = (bf16[2,64,1152]{2,1,0:T(8,128)(2,1)}, bf16[2,64,1152]{2,1,0:T(8,128)(2,1)S(1)}, u32[]{:S(2)}, u32[]{:S(2)}) collective-permute-start(bf16[2,64,1152]{2,1,0:T(8,128)(2,1)} %get-tuple-element.94), channel_id=1, source_target_pairs={{0,1},{1,0},{2,3},{3,2},{4,5},{5,4},{6,7},{7,6},{8,9},{9,8},{10,11... | collective-permute-start | bytes 884744 | tf_op jit(solution)/shard_map/ppermute | solution.py:455
  73.8 15.5 %collective-permute-start.21 = (bf16[2,64,1152]{2,1,0:T(8,128)(2,1)}, bf16[2,64,1152]{2,1,0:T(8,128)(2,1)S(1)}, u32[]{:S(2)}, u32[]{:S(2)}) collective-permute-start(bf16[2,64,1152]{2,1,0:T(8,128)(2,1)} %get-tuple-element.95), channel_id=1, source_target_pairs={{0,16},{1,17},{2,18},{3,19},{4,20},{5,21},{6,22},{7,23},{8,24},{9,... | collective-permute-start | bytes 884744 | tf_op jit(solution)/shard_map/ppermute | solution.py:455
  73.8 15.5 %collective-permute-start.22 = (bf16[2,64,1152]{2,1,0:T(8,128)(2,1)}, bf16[2,64,1152]{2,1,0:T(8,128)(2,1)S(1)}, u32[]{:S(2)}, u32[]{:S(2)}) collective-permute-start(bf16[2,64,1152]{2,1,0:T(8,128)(2,1)} %get-tuple-element.96), channel_id=1, source_target_pairs={{0,17},{1,16},{2,19},{3,18},{4,21},{5,20},{6,23},{7,22},{8,25},{9,... | collective-permute-start | bytes 884744 | tf_op jit(solution)/shard_map/ppermute | solution.py:455
  77.3 12.1 %collective-permute-start.19 = (f32[2,48,864]{2,1,0:T(8,128)S(1)}, f32[2,48,864]{2,1,0:T(8,128)S(1)}, u32[]{:S(2)}, u32[]{:S(2)}) collective-permute-start(f32[2,48,864]{2,1,0:T(8,128)S(1)} %get-tuple-element.92), channel_id=1, source_target_pairs={{0,2},{1,3},{2,0},{3,1},{4,6},{5,7},{6,4},{7,5},{8,10},{9,11},{10,... | collective-permute-start | bytes 995336 | tf_op jit(solution)/shard_map/ppermute | solution.py:562
  87.7 5.2 %copy-start.14 = (bf16[2,64,1152]{2,1,0:T(8,128)(2,1)}, bf16[2,64,1152]{2,1,0:T(8,128)(2,1)S(1)}, u32[]{:S(2)}) copy-start(bf16[2,64,1152]{2,1,0:T(8,128)(2,1)S(1)} %collective-permute-done.20.refs_3_) | copy-start | bytes 884740
  89.3 3.6 %copy-start.15 = (bf16[2,64,1152]{2,1,0:T(8,128)(2,1)}, bf16[2,64,1152]{2,1,0:T(8,128)(2,1)S(1)}, u32[]{:S(2)}) copy-start(bf16[2,64,1152]{2,1,0:T(8,128)(2,1)S(1)} %collective-permute-done.21.refs_4_) | copy-start | bytes 884740
  89.3 3.6 %copy-start.16 = (bf16[2,64,1152]{2,1,0:T(8,128)(2,1)}, bf16[2,64,1152]{2,1,0:T(8,128)(2,1)S(1)}, u32[]{:S(2)}) copy-start(bf16[2,64,1152]{2,1,0:T(8,128)(2,1)S(1)} %collective-permute-done.22.refs_5_) | copy-start | bytes 884740
  89.4 12.2 %collective-permute-start.25 = (bf16[2,64,1152]{2,1,0:T(8,128)(2,1)}, bf16[2,64,1152]{2,1,0:T(8,128)(2,1)S(1)}, u32[]{:S(2)}, u32[]{:S(2)}) collective-permute-start(bf16[2,64,1152]{2,1,0:T(8,128)(2,1)} %get-tuple-element.104), channel_id=1, source_target_pairs={{0,1},{1,0},{2,3},{3,2},{4,5},{5,4},{6,7},{7,6},{8,9},{9,8},{10,11... | collective-permute-start | bytes 884744 | tf_op jit(solution)/shard_map/ppermute | solution.py:455
  90.3 14.6 %collective-permute-start.26 = (bf16[2,64,1152]{2,1,0:T(8,128)(2,1)}, bf16[2,64,1152]{2,1,0:T(8,128)(2,1)S(1)}, u32[]{:S(2)}, u32[]{:S(2)}) collective-permute-start(bf16[2,64,1152]{2,1,0:T(8,128)(2,1)} %get-tuple-element.105), channel_id=1, source_target_pairs={{0,16},{1,17},{2,18},{3,19},{4,20},{5,21},{6,22},{7,23},{8,24},{9,... | collective-permute-start | bytes 884744 | tf_op jit(solution)/shard_map/ppermute | solution.py:455
  91.1 13.7 %collective-permute-start.27 = (bf16[2,64,1152]{2,1,0:T(8,128)(2,1)}, bf16[2,64,1152]{2,1,0:T(8,128)(2,1)S(1)}, u32[]{:S(2)}, u32[]{:S(2)}) collective-permute-start(bf16[2,64,1152]{2,1,0:T(8,128)(2,1)} %get-tuple-element.106), channel_id=1, source_target_pairs={{0,17},{1,16},{2,19},{3,18},{4,21},{5,20},{6,23},{7,22},{8,25},{9,... | collective-permute-start | bytes 884744 | tf_op jit(solution)/shard_map/ppermute | solution.py:455
  96.0 23.2 %collective-permute-start.23 = (bf16[64,1152]{1,0:T(8,128)(2,1)}, bf16[64,1152]{1,0:T(8,128)(2,1)S(1)}, u32[]{:S(2)}, u32[]{:S(2)}) collective-permute-start(bf16[64,1152]{1,0:T(8,128)(2,1)} %get-tuple-element.101), channel_id=1, source_target_pairs={{0,0},{1,1},{16,2},{17,3},{2,4},{3,5},{18,6},{19,7},{20,8},{21,9},... | collective-permute-start | bytes 442376 | tf_op jit(solution)/shard_map/ppermute | solution.py:442
  99.6 19.6 %collective-permute-start.24 = (bf16[64,1152]{1,0:T(8,128)(2,1)}, bf16[64,1152]{1,0:T(8,128)(2,1)S(1)}, u32[]{:S(2)}, u32[]{:S(2)}) collective-permute-start(bf16[64,1152]{1,0:T(8,128)(2,1)} %get-tuple-element.102), channel_id=1, source_target_pairs={{2,0},{3,1},{18,2},{19,3},{0,4},{1,5},{16,6},{17,7},{22,8},{23,9},... | collective-permute-start | bytes 442376 | tf_op jit(solution)/shard_map/ppermute | solution.py:442
  101.6 3.2 %copy-start.17 = (bf16[2,64,1152]{2,1,0:T(8,128)(2,1)}, bf16[2,64,1152]{2,1,0:T(8,128)(2,1)S(1)}, u32[]{:S(2)}) copy-start(bf16[2,64,1152]{2,1,0:T(8,128)(2,1)S(1)} %collective-permute-done.25.refs_3_) | copy-start | bytes 884740
  101.6 15.6 %collective-permute-start.30 = (f32[1,48,864]{2,1,0:T(8,128)S(1)}, f32[1,48,864]{2,1,0:T(8,128)S(1)}, u32[]{:S(2)}, u32[]{:S(2)}) collective-permute-start(f32[1,48,864]{2,1,0:T(8,128)S(1)} %slice.40), channel_id=1, source_target_pairs={{0,4},{1,5},{2,6},{3,7},{4,0},{5,1},{6,2},{7,3},{8,12},{9,13},{10,... | collective-permute-start | bytes 497672 | tf_op jit(solution)/shard_map/ppermute | solution.py:603
  104.8 0.7 copy-start.18
  105.6 0.7 copy-start.19
  109.7 9.9 %collective-permute-start.28 = (bf16[64,1152]{1,0:T(8,128)(2,1)}, bf16[64,1152]{1,0:T(8,128)(2,1)S(1)}, u32[]{:S(2)}, u32[]{:S(2)}) collective-permute-start(bf16[64,1152]{1,0:T(8,128)(2,1)} %get-tuple-element.111), channel_id=1, source_target_pairs={{0,0},{1,1},{16,2},{17,3},{2,4},{3,5},{18,6},{19,7},{20,8},{21,9},... | collective-permute-start | bytes 442376 | tf_op jit(solution)/shard_map/ppermute | solution.py:442
  115.3 8.9 %collective-permute-start.29 = (bf16[64,1152]{1,0:T(8,128)(2,1)}, bf16[64,1152]{1,0:T(8,128)(2,1)S(1)}, u32[]{:S(2)}, u32[]{:S(2)}) collective-permute-start(bf16[64,1152]{1,0:T(8,128)(2,1)} %get-tuple-element.112), channel_id=1, source_target_pairs={{2,0},{3,1},{18,2},{19,3},{0,4},{1,5},{16,6},{17,7},{22,8},{23,9},... | collective-permute-start | bytes 442376 | tf_op jit(solution)/shard_map/ppermute | solution.py:442
  117.3 10.9 %collective-permute-start.31 = (f32[48,864]{1,0:T(8,128)S(1)}, f32[48,864]{1,0:T(8,128)S(1)}, u32[]{:S(2)}, u32[]{:S(2)}) collective-permute-start(f32[48,864]{1,0:T(8,128)S(1)} %bitcast.28), channel_id=1, source_target_pairs={{0,0},{1,1},{2,8},{3,9},{4,16},{5,17},{6,24},{7,25},{8,4},{9,5},{1... | collective-permute-start | bytes 497672 | tf_op jit(solution)/shard_map/ppermute | solution.py:605

commit v20 on v19

--- a/solution.py
+++ b/solution.py
@@ -507,7 +507,8 @@
     for j in range(nc):
         after = ([], None) if j else (info, first)
         pairs += doubling(own[j], lay.chip_bits(j), chip_swap, *after)
-    early = [lax.ppermute(piece, AXES, lay.swap(kc=1)) for piece in w_pieces[:2]]
+    near = jnp.where(z < lay.nz, w_pieces[1], w_own)
+    early = [lax.ppermute(piece, AXES, lay.swap(kc=1)) for piece in (w_own, near)]
     early = early if halves > 1 else []
     pairs, w_pieces, early, wo_rows = lax.optimization_barrier((pairs, w_pieces, early, wo_rows))
     if halves > 1:

time: 130 us -> 130 us (level)
  starting transfers between devices: 54.5 us -> 51.6 us
  waiting for transfers between devices: 33.8 us -> 36.5 us
    ppermute x4, starting transfers between devices: 13.1 us -> 17.8 us  [from_plane(): lax.ppermute(part, AXES, lay.from_plane(k))]
    ppermute x2, starting transfers between devices: 9.93 us -> 5.4 us  [local(): by_z[bit] = lax.ppermute(w_own, AXES, lay.swap(kz=bit))]
    ppermute x1, waiting for transfers between devices: 2.45 us -> 5.2 us  [local(): grad_w = lax.ppermute(cut[0], AXES, lay.to_owner())]
    ppermute x4, waiting for transfers between devices: 5.01 us -> 2.52 us  [from_plane(): lax.ppermute(part, AXES, lay.from_plane(k))]
    ppermute x2, waiting for transfers between devices: 5.16 us -> 7.58 us  [local(): by_z[bit] = lax.ppermute(w_own, AXES, lay.swap(kz=bit))]
    ppermute x1, waiting for transfers between devices: 2.09 us -> 0.01 us  [doubling(): got = lax.ppermute(held, AXES, swap(bit)) if first is None else first]
    ppermute x1, waiting for transfers between devices: 5.23 us -> 7.11 us  [local(): by_z[k] = lax.ppermute(forwarded, AXES, lay.swap(kz=k & -k))]
    ppermute x1, starting transfers between devices: 1.81 us -> 0.43 us  [local(): first_away = lax.ppermute(away, AXES, lay.swap(kz=1))]
where the time goes in v20:
time: 130 us; the launch traced here: 129 us
  starting transfers between devices  51.6 us (40%)
  waiting for transfers between devices  36.5 us (28%)
  Pallas kernels  30.4 us (23%)
  other arithmetic  5.98 us (5%)
  local copies, waits for them, and re-layouts  3.88 us (3%)
    ppermute x4, starting transfers between devices, from_plane(): lax.ppermute(part, AXES, lay.from_plane(k))  17.8 us
    pallas_call x1, Pallas kernels, local(): call(functools.partial(forward_kernel, lay), 'forward', 14 * model * 1000...  12 us
    pallas_call x1, Pallas kernels, local(): call(functools.partial(backward_kernel, lay), 'backward', 10 * model * 10...  8.62 us
    ppermute x2, waiting for transfers between devices, local(): by_z[bit] = lax.ppermute(w_own, AXES, lay.swap(kz=bit))  7.58 us
    ppermute x1, waiting for transfers between devices, local(): by_z[k] = lax.ppermute(forwarded, AXES, lay.swap(kz=k & -k))  7.11 us
    ppermute x6, starting transfers between devices, over_chips(): got = [lax.ppermute(parts[k], AXES, chip_swap(k)) for k in range(1, chips)]  7.06 us
    ppermute x2, starting transfers between devices, local(): by_z[bit] = lax.ppermute(w_own, AXES, lay.swap(kz=bit))  5.4 us
    ppermute x1, waiting for transfers between devices, local(): wo_own = lax.ppermute(late_w_out, AXES, lay.rows_to_chip())  5.26 us
  transfers between devices with their start and end apart: 32, of which 13 were waited for; matrix products, arithmetic and copies ran while one was open for 4% of the time, Pallas kernels for 12%

profile of v20, /device:TPU:4, one launch (start us, length us, event | category | flops | bytes accessed | tf_op | source)
XLA Modules:
  0.0 129.4 jit_solution(11803060355586554020)
XLA Ops:
  0.6 0.6 pad_add_fusion.1.pos_ref
  1.2 3.3 %start.1 = (bf16[1,2,64,1152]{3,2,1,0:T(8,128)(2,1)}, bf16[1,2,64,1152]{3,2,1,0:T(8,128)(2,1)}, bf16[144,432]{1,0:T(8,128)(2,1)}, bf16[144,432]{1,0:T(8,128)(2,1)}) custom-call(s32[4]{0:T(128)} %pad_add_fusion.1.pos_ref, bf16[1,128,1152]{2,1,0:T(8,128)(2,1)} %x_ref.1, bf16[1,128,1152]{2,1,0:T(8,128)(2,1)} %g_ref.1, bf16[144,3456]{1,0:T(8,128)(2,1)} %w_ref.1), custom_call_target="tpu_custom_call" | custom-call | flops 1179648000 | bytes 2359296 | tf_op jit(solution)/shard_map/start/pallas_call | solution.py:471
  4.5 1.9 %collective-permute-start.2 = (bf16[1,2,64,1152]{3,2,1,0:T(8,128)(2,1)}, bf16[1,2,64,1152]{3,2,1,0:T(8,128)(2,1)S(1)}, u32[]{:S(2)}, u32[]{:S(2)}) collective-permute-start(bf16[1,2,64,1152]{3,2,1,0:T(8,128)(2,1)} %get-tuple-element.60), channel_id=1, source_target_pairs={{0,0},{1,1},{2,16},{3,17},{4,2},{5,3},{6,18},{7,19},{8,20},{9,21},... | collective-permute-start | bytes 884744 | tf_op jit(solution)/shard_map/ppermute | solution.py:481
  6.5 0.6 copy-done.7
  7.1 0.1 fusion.7
  7.2 2.2 %collective-permute-start = (s32[1,16]{1,0:T(1,128)S(1)}, s32[1,16]{1,0:T(1,128)S(1)}, u32[]{:S(2)}, u32[]{:S(2)}) collective-permute-start(s32[1,16]{1,0:T(1,128)S(1)} %fusion.7), channel_id=1, source_target_pairs={{0,8},{1,9},{2,10},{3,11},{4,12},{5,13},{6,14},{7,15},{8,0},{9,1},... | collective-permute-start | bytes 200 | tf_op jit(solution)/shard_map/ppermute | solution.py:459
  9.4 1.5 %collective-permute-start.8 = (bf16[144,432]{1,0:T(8,128)(2,1)}, bf16[144,432]{1,0:T(8,128)(2,1)S(1)}, u32[]{:S(2)}, u32[]{:S(2)}) collective-permute-start(bf16[144,432]{1,0:T(8,128)(2,1)} %get-tuple-element.66), channel_id=1, source_target_pairs={{0,1},{1,0},{2,3},{3,2},{4,5},{5,4},{6,7},{7,6},{8,9},{9,8},{10,11... | collective-permute-start | bytes 373256 | tf_op jit(solution)/shard_map/ppermute | solution.py:483
  10.8 2.5 %collective-permute-start.3 = (bf16[1,2,64,1152]{3,2,1,0:T(8,128)(2,1)}, bf16[1,2,64,1152]{3,2,1,0:T(8,128)(2,1)S(1)}, u32[]{:S(2)}, u32[]{:S(2)}) collective-permute-start(bf16[1,2,64,1152]{3,2,1,0:T(8,128)(2,1)} %get-tuple-element.61), channel_id=1, source_target_pairs={{0,2},{1,3},{2,18},{3,19},{4,0},{5,1},{6,16},{7,17},{8,22},{9,23},... | collective-permute-start | bytes 884744 | tf_op jit(solution)/shard_map/ppermute | solution.py:481
  13.4 1.5 %collective-permute-start.1 = (s32[2,16]{1,0:T(2,128)S(1)}, s32[2,16]{1,0:T(2,128)S(1)}, u32[]{:S(2)}, u32[]{:S(2)}) collective-permute-start(s32[2,16]{1,0:T(2,128)S(1)} %pad_add_fusion), channel_id=1, source_target_pairs={{0,16},{1,17},{2,18},{3,19},{4,20},{5,21},{6,22},{7,23},{8,24},{9,... | collective-permute-start | bytes 392 | tf_op jit(solution)/shard_map/ppermute | solution.py:461
  14.9 0.8 collective-permute-start.4
  15.7 1.4 %collective-permute-done.1 = s32[2,16]{1,0:T(2,128)S(1)} collective-permute-done((s32[2,16]{1,0:T(2,128)S(1)}, s32[2,16]{1,0:T(2,128)S(1)}, u32[]{:S(2)}, u32[]{:S(2)}) %collective-permute-start.1) | collective-permute-done | bytes 160 | tf_op jit(solution)/shard_map/ppermute | solution.py:461
  17.1 0.6 fusion.2.info_ref
  17.7 0.9 broadcast_select_fusion.3
  18.6 4.3 %collective-permute-start.9 = (bf16[144,1152]{1,0:T(8,128)(2,1)S(1)}, bf16[144,1152]{1,0:T(8,128)(2,1)S(1)}, u32[]{:S(2)}, u32[]{:S(2)}) collective-permute-start(bf16[144,1152]{1,0:T(8,128)(2,1)S(1)} %copy-done.12), channel_id=1, source_target_pairs={{0,0},{1,1},{2,18},{3,19},{4,8},{5,9},{6,26},{7,27},{8,4},{9,5},{1... | collective-permute-start | bytes 995336 | tf_op jit(solution)/shard_map/ppermute | solution.py:494
  23.0 1.7 %collective-permute-done.3.refs_1_ = bf16[1,2,64,1152]{3,2,1,0:T(8,128)(2,1)S(1)} collective-permute-done((bf16[1,2,64,1152]{3,2,1,0:T(8,128)(2,1)}, bf16[1,2,64,1152]{3,2,1,0:T(8,128)(2,1)S(1)}, u32[]{:S(2)}, u32[]{:S(2)}) %collective-permute-start.3) | collective-permute-done | bytes 294944 | tf_op jit(solution)/shard_map/ppermute | solution.py:481
  24.7 1.0 collective-permute-start.6
  25.7 0.1 maximum_bitcast_fusion.2.refs_4_.refs_0_
  25.9 0.1 pad_maximum_fusion.refs_0_
  25.9 1.1 collective-permute-start.5
  27.0 5.3 %collective-permute-done.9.refs_12_ = bf16[144,1152]{1,0:T(8,128)(2,1)S(1)} collective-permute-done((bf16[144,1152]{1,0:T(8,128)(2,1)S(1)}, bf16[144,1152]{1,0:T(8,128)(2,1)S(1)}, u32[]{:S(2)}, u32[]{:S(2)}) %collective-permute-start.9) | collective-permute-done | bytes 331808 | tf_op jit(solution)/shard_map/ppermute | solution.py:494
  32.3 0.2 collective-permute-start.11
  32.5 5.2 %collective-permute-start.10 = (bf16[1,144,864]{2,1,0:T(8,128)(2,1)S(1)}, bf16[1,144,864]{2,1,0:T(8,128)(2,1)S(1)}, u32[]{:S(2)}, u32[]{:S(2)}) collective-permute-start(bf16[1,144,864]{2,1,0:T(8,128)(2,1)S(1)} %maximum_bitcast_fusion.2.refs_4_.refs_0_), channel_id=1, source_target_pairs={{0,2},{1,3},{2,0},{3,1},{4,6},{5,7},{6,4},{7,5},{8,10},{9,11},{10,... | collective-permute-start | bytes 746504 | tf_op jit(solution)/shard_map/ppermute | solution.py:499
  37.8 0.9 collective-permute-start.7
  38.7 6.3 %collective-permute-done.11.refs_6_.refs_2_ = bf16[1,144,864]{2,1,0:T(8,128)(2,1)S(1)} collective-permute-done((bf16[1,144,864]{2,1,0:T(8,128)(2,1)S(1)}, bf16[1,144,864]{2,1,0:T(8,128)(2,1)S(1)}, u32[]{:S(2)}, u32[]{:S(2)}) %collective-permute-start.11) | collective-permute-done | bytes 248864 | tf_op jit(solution)/shard_map/ppermute | solution.py:499
  45.0 1.3 collective-permute-done.10.refs_5_.refs_1_
  46.3 0.1 broadcast_select_fusion
  46.4 0.6 copy-done.6
  47.0 0.4 collective-permute-start.12
  47.4 1.1 collective-permute-done.14.refs_9_.refs_5_
  48.5 7.1 %collective-permute-done.12.refs_7_.refs_3_ = bf16[1,144,864]{2,1,0:T(8,128)(2,1)S(1)} collective-permute-done((bf16[1,144,864]{2,1,0:T(8,128)(2,1)S(1)}, bf16[1,144,864]{2,1,0:T(8,128)(2,1)S(1)}, u32[]{:S(2)}, u32[]{:S(2)}) %collective-permute-start.12) | collective-permute-done | bytes 248864 | tf_op jit(solution)/shard_map/ppermute | solution.py:503
  55.7 0.1 collective-permute-start.16
  55.7 0.5 collective-permute-start.17
  56.2 1.0 collective-permute-done.16.refs_10_.refs_6_
  57.3 0.4 collective-permute-done.17.refs_11_.refs_7_
  57.7 0.3 copy-done.24
  58.0 0.7 copy-done.25
  58.7 12.0 %forward.1 = (bf16[2,8,64,144]{3,2,1,0:T(8,128)(2,1)}, bf16[2,8,64,144]{3,2,1,0:T(8,128)(2,1)}, bf16[2,8,64,144]{3,2,1,0:T(8,128)(2,1)}, bf16[2,8,64,144]{3,2,1,...) custom-call(s32[4]{0:T(128)} %pad_add_fusion.1.pos_ref, ...), custom_call_target="tpu_custom_call" | custom-call | flops 8257536000 | bytes 2359296 | tf_op jit(solution)/shard_map/forward/pallas_call | solution.py:537
  70.7 0.2 collective-permute-start.18
  70.8 0.8 collective-permute-start.20
  71.7 2.7 %collective-permute-start.22 = (bf16[2,64,1152]{2,1,0:T(8,128)(2,1)}, bf16[2,64,1152]{2,1,0:T(8,128)(2,1)S(1)}, u32[]{:S(2)}, u32[]{:S(2)}) collective-permute-start(bf16[2,64,1152]{2,1,0:T(8,128)(2,1)} %get-tuple-element.96), channel_id=1, source_target_pairs={{0,17},{1,16},{2,19},{3,18},{4,21},{5,20},{6,23},{7,22},{8,25},{9,... | collective-permute-start | bytes 884744 | tf_op jit(solution)/shard_map/ppermute | solution.py:455
  74.3 1.2 slice_add_fusion
  75.5 0.4 collective-permute-start.19
  75.9 8.6 %backward.1 = (f32[2,64,1152]{2,1,0:T(8,128)}, bf16[2,64,1152]{2,1,0:T(8,128)(2,1)}, bf16[2,64,1152]{2,1,0:T(8,128)(2,1)}, bf16[2,64,1152]{2,1,0:T(8,128)(2,1)}) custom-call(s32[4]{0:T(128)} %pad_add_fusion.1.pos_ref, s32[16]{0:T(128)} %fusion.2.info_ref, bf16[1,144,864]{2,1,0:T(8,128)(2,1)} %copy-done, bf16[1,144,864]{2,1,0:T(8,128)(2,1)} %copy-done.6, ...), custom_call_target="tpu_custom_call" | custom-call | flops 5898240000 | bytes 2359296 | tf_op jit(solution)/shard_map/backward/pallas_call | solution.py:565
  84.6 2.6 %collective-permute-done.21.refs_4_ = bf16[2,64,1152]{2,1,0:T(8,128)(2,1)S(1)} collective-permute-done((bf16[2,64,1152]{2,1,0:T(8,128)(2,1)}, bf16[2,64,1152]{2,1,0:T(8,128)(2,1)S(1)}, u32[]{:S(2)}, u32[]{:S(2)}) %collective-permute-start.21) | collective-permute-done | bytes 294944 | tf_op jit(solution)/shard_map/ppermute | solution.py:455
  87.2 1.3 collective-permute-start.25
  88.5 0.5 collective-permute-start.26
  88.9 1.8 %collective-permute-start.27 = (bf16[2,64,1152]{2,1,0:T(8,128)(2,1)}, bf16[2,64,1152]{2,1,0:T(8,128)(2,1)S(1)}, u32[]{:S(2)}, u32[]{:S(2)}) collective-permute-start(bf16[2,64,1152]{2,1,0:T(8,128)(2,1)} %get-tuple-element.106), channel_id=1, source_target_pairs={{0,17},{1,16},{2,19},{3,18},{4,21},{5,20},{6,23},{7,22},{8,25},{9,... | collective-permute-start | bytes 884744 | tf_op jit(solution)/shard_map/ppermute | solution.py:455
  90.7 3.1 %output.1 = (bf16[64,1152]{1,0:T(8,128)(2,1)}, bf16[64,1152]{1,0:T(8,128)(2,1)}) custom-call(s32[4]{0:T(128)} %pad_add_fusion.1.pos_ref, s32[16]{0:T(128)} %fusion.2.info_ref, bf16[1,2,64,1152]{3,2,1,0:T(8,128)(2,1)} %copy-done.3, bf16[1,2,64,1152]{3,2,1,0:T(8,128)(2,1)} %copy-done.4, f32[2,64,1152]{2,1,0:T(8,128)} %get-tuple-element.97.refs_2_, ...), custom_call_target="tpu_custom_call" | custom-call | flops 11796480000 | bytes 2359296 | tf_op jit(solution)/shard_map/output/pallas_call | solution.py:578
  93.8 2.7 %collective-permute-start.23 = (bf16[64,1152]{1,0:T(8,128)(2,1)}, bf16[64,1152]{1,0:T(8,128)(2,1)S(1)}, u32[]{:S(2)}, u32[]{:S(2)}) collective-permute-start(bf16[64,1152]{1,0:T(8,128)(2,1)} %get-tuple-element.101), channel_id=1, source_target_pairs={{0,0},{1,1},{16,2},{17,3},{2,4},{3,5},{18,6},{19,7},{20,8},{21,9},... | collective-permute-start | bytes 442376 | tf_op jit(solution)/shard_map/ppermute | solution.py:442
  96.5 5.7 %collective-permute-start.24 = (bf16[64,1152]{1,0:T(8,128)(2,1)}, bf16[64,1152]{1,0:T(8,128)(2,1)S(1)}, u32[]{:S(2)}, u32[]{:S(2)}) collective-permute-start(bf16[64,1152]{1,0:T(8,128)(2,1)} %get-tuple-element.102), channel_id=1, source_target_pairs={{2,0},{3,1},{18,2},{19,3},{0,4},{1,5},{16,6},{17,7},{22,8},{23,9},... | collective-permute-start | bytes 442376 | tf_op jit(solution)/shard_map/ppermute | solution.py:442
  102.3 0.1 collective-permute-start.30
  102.3 0.7 collective-permute-done.26.refs_4_
  103.0 0.7 copy-done.19
  103.7 0.7 copy-done.20
  104.4 3.4 %input_grad.1 = (bf16[64,1152]{1,0:T(8,128)(2,1)}, bf16[64,1152]{1,0:T(8,128)(2,1)}) custom-call(s32[4]{0:T(128)} %pad_add_fusion.1.pos_ref, s32[16]{0:T(128)} %fusion.2.info_ref, bf16[1,2,64,1152]{3,2,1,0:T(8,128)(2,1)} %copy-done.3, bf16[1,2,64,1152]{3,2,1,0:T(8,128)(2,1)} %copy-done.4, f32[2,64,1152]{2,1,0:T(8,128)} %get-tuple-element.107.refs_2_, ...), custom_call_target="tpu_custom_call" | custom-call | flops 1769472000 | bytes 2359296 | tf_op jit(solution)/shard_map/input_grad/pallas_call | solution.py:590
  107.8 3.9 %collective-permute-start.28 = (bf16[64,1152]{1,0:T(8,128)(2,1)}, bf16[64,1152]{1,0:T(8,128)(2,1)S(1)}, u32[]{:S(2)}, u32[]{:S(2)}) collective-permute-start(bf16[64,1152]{1,0:T(8,128)(2,1)} %get-tuple-element.111), channel_id=1, source_target_pairs={{0,0},{1,1},{16,2},{17,3},{2,4},{3,5},{18,6},{19,7},{20,8},{21,9},... | collective-permute-start | bytes 442376 | tf_op jit(solution)/shard_map/ppermute | solution.py:442
  111.8 5.6 %collective-permute-start.29 = (bf16[64,1152]{1,0:T(8,128)(2,1)}, bf16[64,1152]{1,0:T(8,128)(2,1)S(1)}, u32[]{:S(2)}, u32[]{:S(2)}) collective-permute-start(bf16[64,1152]{1,0:T(8,128)(2,1)} %get-tuple-element.112), channel_id=1, source_target_pairs={{2,0},{3,1},{18,2},{19,3},{0,4},{1,5},{16,6},{17,7},{22,8},{23,9},... | collective-permute-start | bytes 442376 | tf_op jit(solution)/shard_map/ppermute | solution.py:442
  117.4 1.9 %collective-permute-start.31 = (f32[48,864]{1,0:T(8,128)S(1)}, f32[48,864]{1,0:T(8,128)S(1)}, u32[]{:S(2)}, u32[]{:S(2)}) collective-permute-start(f32[48,864]{1,0:T(8,128)S(1)} %bitcast.28), channel_id=1, source_target_pairs={{0,0},{1,1},{2,8},{3,9},{4,16},{5,17},{6,24},{7,25},{8,4},{9,5},{1... | collective-permute-start | bytes 497672 | tf_op jit(solution)/shard_map/ppermute | solution.py:606
  119.4 2.5 %collective-permute-done.29 = bf16[64,1152]{1,0:T(8,128)(2,1)S(1)} collective-permute-done((bf16[64,1152]{1,0:T(8,128)(2,1)}, bf16[64,1152]{1,0:T(8,128)(2,1)S(1)}, u32[]{:S(2)}, u32[]{:S(2)}) %collective-permute-start.29) | collective-permute-done | bytes 147488 | tf_op jit(solution)/shard_map/ppermute | solution.py:442
  122.0 0.7 maximum_bitcast_fusion.1
  122.7 0.7 maximum_bitcast_fusion
  123.4 5.2 %collective-permute-done.31 = f32[48,864]{1,0:T(8,128)S(1)} collective-permute-done((f32[48,864]{1,0:T(8,128)S(1)}, f32[48,864]{1,0:T(8,128)S(1)}, u32[]{:S(2)}, u32[]{:S(2)}) %collective-permute-start.31) | collective-permute-done | bytes 165920 | tf_op jit(solution)/shard_map/ppermute | solution.py:606
  128.6 0.1 fusion.6
  128.7 0.7 maximum_multiply_fusion
  (75 shorter events, 0.4 us)
Async XLA Ops:
  4.5 10.4 %collective-permute-start.2 = (bf16[1,2,64,1152]{3,2,1,0:T(8,128)(2,1)}, bf16[1,2,64,1152]{3,2,1,0:T(8,128)(2,1)S(1)}, u32[]{:S(2)}, u32[]{:S(2)}) collective-permute-start(bf16[1,2,64,1152]{3,2,1,0:T(8,128)(2,1)} %get-tuple-element.60), channel_id=1, source_target_pairs={{0,0},{1,1},{2,16},{3,17},{4,2},{5,3},{6,18},{7,19},{8,20},{9,21},... | collective-permute-start | bytes 884744 | tf_op jit(solution)/shard_map/ppermute | solution.py:481
  6.4 0.7 copy-start.7
  6.5 0.7 copy-start.8
  6.5 0.7 copy-start.9
  7.2 6.2 %collective-permute-start = (s32[1,16]{1,0:T(1,128)S(1)}, s32[1,16]{1,0:T(1,128)S(1)}, u32[]{:S(2)}, u32[]{:S(2)}) collective-permute-start(s32[1,16]{1,0:T(1,128)S(1)} %fusion.7), channel_id=1, source_target_pairs={{0,8},{1,9},{2,10},{3,11},{4,12},{5,13},{6,14},{7,15},{8,0},{9,1},... | collective-permute-start | bytes 200 | tf_op jit(solution)/shard_map/ppermute | solution.py:459
  9.4 8.3 %collective-permute-start.8 = (bf16[144,432]{1,0:T(8,128)(2,1)}, bf16[144,432]{1,0:T(8,128)(2,1)S(1)}, u32[]{:S(2)}, u32[]{:S(2)}) collective-permute-start(bf16[144,432]{1,0:T(8,128)(2,1)} %get-tuple-element.66), channel_id=1, source_target_pairs={{0,1},{1,0},{2,3},{3,2},{4,5},{5,4},{6,7},{7,6},{8,9},{9,8},{10,11... | collective-permute-start | bytes 373256 | tf_op jit(solution)/shard_map/ppermute | solution.py:483
  10.8 13.9 %collective-permute-start.3 = (bf16[1,2,64,1152]{3,2,1,0:T(8,128)(2,1)}, bf16[1,2,64,1152]{3,2,1,0:T(8,128)(2,1)S(1)}, u32[]{:S(2)}, u32[]{:S(2)}) collective-permute-start(bf16[1,2,64,1152]{3,2,1,0:T(8,128)(2,1)} %get-tuple-element.61), channel_id=1, source_target_pairs={{0,2},{1,3},{2,18},{3,19},{4,0},{5,1},{6,16},{7,17},{8,22},{9,23},... | collective-permute-start | bytes 884744 | tf_op jit(solution)/shard_map/ppermute | solution.py:481
  13.4 5.3 %copy-start.12 = (bf16[144,1152]{1,0:T(8,128)(2,1)S(1)}, bf16[144,1152]{1,0:T(8,128)(2,1)}, u32[]{:S(2)}) copy-start(bf16[144,1152]{1,0:T(8,128)(2,1)} %param.15) | copy-start | bytes 995332
  13.4 3.6 %collective-permute-start.1 = (s32[2,16]{1,0:T(2,128)S(1)}, s32[2,16]{1,0:T(2,128)S(1)}, u32[]{:S(2)}, u32[]{:S(2)}) collective-permute-start(s32[2,16]{1,0:T(2,128)S(1)} %pad_add_fusion), channel_id=1, source_target_pairs={{0,16},{1,17},{2,18},{3,19},{4,20},{5,21},{6,22},{7,23},{8,24},{9,... | collective-permute-start | bytes 392 | tf_op jit(solution)/shard_map/ppermute | solution.py:461
  14.9 10.9 %copy-start.3 = (bf16[1,2,64,1152]{3,2,1,0:T(8,128)(2,1)}, bf16[1,2,64,1152]{3,2,1,0:T(8,128)(2,1)S(1)}, u32[]{:S(2)}) copy-start(bf16[1,2,64,1152]{3,2,1,0:T(8,128)(2,1)S(1)} %collective-permute-done.2.refs_0_) | copy-start | bytes 884740
  14.9 9.8 %collective-permute-start.4 = (bf16[1,2,64,1152]{3,2,1,0:T(8,128)(2,1)S(1)}, bf16[1,2,64,1152]{3,2,1,0:T(8,128)(2,1)S(1)}, u32[]{:S(2)}, u32[]{:S(2)}) collective-permute-start(bf16[1,2,64,1152]{3,2,1,0:T(8,128)(2,1)S(1)} %collective-permute-done.2.refs_0_), channel_id=1, source_target_pairs={{0,1},{1,0},{2,3},{3,2},{4,5},{5,4},{6,7},{7,6},{8,9},{9,8},{10,11... | collective-permute-start | bytes 884744 | tf_op jit(solution)/shard_map/ppermute | solution.py:491
  18.6 13.6 %collective-permute-start.9 = (bf16[144,1152]{1,0:T(8,128)(2,1)S(1)}, bf16[144,1152]{1,0:T(8,128)(2,1)S(1)}, u32[]{:S(2)}, u32[]{:S(2)}) collective-permute-start(bf16[144,1152]{1,0:T(8,128)(2,1)S(1)} %copy-done.12), channel_id=1, source_target_pairs={{0,0},{1,1},{2,18},{3,19},{4,8},{5,9},{6,26},{7,27},{8,4},{9,5},{1... | collective-permute-start | bytes 995336 | tf_op jit(solution)/shard_map/ppermute | solution.py:494
  24.7 13.0 %copy-start.4 = (bf16[1,2,64,1152]{3,2,1,0:T(8,128)(2,1)}, bf16[1,2,64,1152]{3,2,1,0:T(8,128)(2,1)S(1)}, u32[]{:S(2)}) copy-start(bf16[1,2,64,1152]{3,2,1,0:T(8,128)(2,1)S(1)} %collective-permute-done.3.refs_1_) | copy-start | bytes 884740
  24.7 13.0 %collective-permute-start.6 = (bf16[1,2,64,1152]{3,2,1,0:T(8,128)(2,1)S(1)}, bf16[1,2,64,1152]{3,2,1,0:T(8,128)(2,1)S(1)}, u32[]{:S(2)}, u32[]{:S(2)}) collective-permute-start(bf16[1,2,64,1152]{3,2,1,0:T(8,128)(2,1)S(1)} %collective-permute-done.3.refs_1_), channel_id=1, source_target_pairs={{0,16},{1,17},{2,18},{3,19},{4,20},{5,21},{6,22},{7,23},{8,24},{9,... | collective-permute-start | bytes 884744 | tf_op jit(solution)/shard_map/ppermute | solution.py:449
  25.9 20.4 %copy-start = (bf16[1,144,864]{2,1,0:T(8,128)(2,1)}, bf16[1,144,864]{2,1,0:T(8,128)(2,1)S(1)}, u32[]{:S(2)}) copy-start(bf16[1,144,864]{2,1,0:T(8,128)(2,1)S(1)} %maximum_bitcast_fusion.2.refs_4_.refs_0_) | copy-start | bytes 746500
  25.9 12.7 %copy-start.1 = (bf16[2,2,64,1152]{3,2,1,0:T(8,128)(2,1)}, bf16[2,2,64,1152]{3,2,1,0:T(8,128)(2,1)S(1)}, u32[]{:S(2)}) copy-start(bf16[2,2,64,1152]{3,2,1,0:T(8,128)(2,1)S(1)} %pad_maximum_fusion.refs_0_) | copy-start | bytes 1769476
  25.9 29.7 %collective-permute-start.5 = (bf16[2,2,64,1152]{3,2,1,0:T(8,128)(2,1)S(1)}, bf16[2,2,64,1152]{3,2,1,0:T(8,128)(2,1)S(1)}, u32[]{:S(2)}, u32[]{:S(2)}) collective-permute-start(bf16[2,2,64,1152]{3,2,1,0:T(8,128)(2,1)S(1)} %pad_maximum_fusion.refs_0_), channel_id=1, source_target_pairs={{0,16},{1,17},{2,18},{3,19},{4,20},{5,21},{6,22},{7,23},{8,24},{9,... | collective-permute-start | bytes 1769480 | tf_op jit(solution)/shard_map/ppermute | solution.py:452
  32.3 5.4 %copy-start.13 = (bf16[144,1152]{1,0:T(8,128)(2,1)}, bf16[144,1152]{1,0:T(8,128)(2,1)S(1)}, u32[]{:S(2)}) copy-start(bf16[144,1152]{1,0:T(8,128)(2,1)S(1)} %collective-permute-done.9.refs_12_) | copy-start | bytes 995332
  32.3 12.7 %collective-permute-start.11 = (bf16[1,144,864]{2,1,0:T(8,128)(2,1)S(1)}, bf16[1,144,864]{2,1,0:T(8,128)(2,1)S(1)}, u32[]{:S(2)}, u32[]{:S(2)}) collective-permute-start(bf16[1,144,864]{2,1,0:T(8,128)(2,1)S(1)} %maximum_bitcast_fusion.2.refs_4_.refs_0_), channel_id=1, source_target_pairs={{0,4},{1,5},{2,6},{3,7},{4,0},{5,1},{6,2},{7,3},{8,12},{9,13},{10,... | collective-permute-start | bytes 746504 | tf_op jit(solution)/shard_map/ppermute | solution.py:499
  32.5 13.8 %collective-permute-start.10 = (bf16[1,144,864]{2,1,0:T(8,128)(2,1)S(1)}, bf16[1,144,864]{2,1,0:T(8,128)(2,1)S(1)}, u32[]{:S(2)}, u32[]{:S(2)}) collective-permute-start(bf16[1,144,864]{2,1,0:T(8,128)(2,1)S(1)} %maximum_bitcast_fusion.2.refs_4_.refs_0_), channel_id=1, source_target_pairs={{0,2},{1,3},{2,0},{3,1},{4,6},{5,7},{6,4},{7,5},{8,10},{9,11},{10,... | collective-permute-start | bytes 746504 | tf_op jit(solution)/shard_map/ppermute | solution.py:499
  37.8 8.6 %copy-start.2 = (bf16[2,2,64,1152]{3,2,1,0:T(8,128)(2,1)}, bf16[2,2,64,1152]{3,2,1,0:T(8,128)(2,1)S(1)}, u32[]{:S(2)}) copy-start(bf16[2,2,64,1152]{3,2,1,0:T(8,128)(2,1)S(1)} %pad_maximum_fusion.1.refs_2_) | copy-start | bytes 1769476
  37.8 17.9 %collective-permute-start.7 = (bf16[2,2,64,1152]{3,2,1,0:T(8,128)(2,1)S(1)}, bf16[2,2,64,1152]{3,2,1,0:T(8,128)(2,1)S(1)}, u32[]{:S(2)}, u32[]{:S(2)}) collective-permute-start(bf16[2,2,64,1152]{3,2,1,0:T(8,128)(2,1)S(1)} %pad_maximum_fusion.1.refs_2_), channel_id=1, source_target_pairs={{0,1},{1,0},{2,3},{3,2},{4,5},{5,4},{6,7},{7,6},{8,9},{9,8},{10,11... | collective-permute-start | bytes 1769480 | tf_op jit(solution)/shard_map/ppermute | solution.py:452
  38.7 8.3 %collective-permute-start.13 = (bf16[1,144,864]{2,1,0:T(8,128)(2,1)S(1)}, bf16[1,144,864]{2,1,0:T(8,128)(2,1)S(1)}, u32[]{:S(2)}, u32[]{:S(2)}) collective-permute-start(bf16[1,144,864]{2,1,0:T(8,128)(2,1)S(1)} %maximum_bitcast_fusion.2.refs_4_.refs_0_), channel_id=1, source_target_pairs={{0,8},{1,9},{2,10},{3,11},{4,12},{5,13},{6,14},{7,15},{8,0},{9,1},... | collective-permute-start | bytes 746504 | tf_op jit(solution)/shard_map/ppermute | solution.py:511
  45.0 10.6 %copy-start.5 = (bf16[1,144,864]{2,1,0:T(8,128)(2,1)}, bf16[1,144,864]{2,1,0:T(8,128)(2,1)S(1)}, u32[]{:S(2)}) copy-start(bf16[1,144,864]{2,1,0:T(8,128)(2,1)S(1)} %collective-permute-done.11.refs_6_.refs_2_) | copy-start | bytes 746500
  45.0 2.4 %collective-permute-start.15 = (bf16[144,1152]{1,0:T(8,128)(2,1)}, bf16[144,1152]{1,0:T(8,128)(2,1)S(1)}, u32[]{:S(2)}, u32[]{:S(2)}) collective-permute-start(bf16[144,1152]{1,0:T(8,128)(2,1)} %copy-done.13), channel_id=1, source_target_pairs={{0,8},{1,9},{2,10},{3,11},{4,12},{5,13},{6,14},{7,15},{8,0},{9,1},... | collective-permute-start | bytes 995336 | tf_op jit(solution)/shard_map/ppermute | solution.py:495
  46.3 0.7 copy-start.6
  47.0 1.5 %collective-permute-start.14 = (bf16[1,144,864]{2,1,0:T(8,128)(2,1)S(1)}, bf16[1,144,864]{2,1,0:T(8,128)(2,1)S(1)}, u32[]{:S(2)}, u32[]{:S(2)}) collective-permute-start(bf16[1,144,864]{2,1,0:T(8,128)(2,1)S(1)} %get-tuple-element.125), channel_id=1, source_target_pairs={{0,8},{1,9},{2,10},{3,11},{4,12},{5,13},{6,14},{7,15},{8,0},{9,1},... | collective-permute-start | bytes 746504 | tf_op jit(solution)/shard_map/ppermute | solution.py:511
  47.0 10.6 %copy-start.21 = (bf16[1,144,864]{2,1,0:T(8,128)(2,1)}, bf16[1,144,864]{2,1,0:T(8,128)(2,1)S(1)}, u32[]{:S(2)}) copy-start(bf16[1,144,864]{2,1,0:T(8,128)(2,1)S(1)} %collective-permute-done.13.refs_8_.refs_4_) | copy-start | bytes 746500
  47.0 8.6 %collective-permute-start.12 = (bf16[1,144,864]{2,1,0:T(8,128)(2,1)S(1)}, bf16[1,144,864]{2,1,0:T(8,128)(2,1)S(1)}, u32[]{:S(2)}, u32[]{:S(2)}) collective-permute-start(bf16[1,144,864]{2,1,0:T(8,128)(2,1)S(1)} %get-tuple-element.126), channel_id=1, source_target_pairs={{0,2},{1,3},{2,0},{3,1},{4,6},{5,7},{6,4},{7,5},{8,10},{9,11},{10,... | collective-permute-start | bytes 746504 | tf_op jit(solution)/shard_map/ppermute | solution.py:503
  47.4 10.2 %copy-start.14 = (bf16[144,1152]{1,0:T(8,128)(2,1)}, bf16[144,1152]{1,0:T(8,128)(2,1)S(1)}, u32[]{:S(2)}) copy-start(bf16[144,1152]{1,0:T(8,128)(2,1)S(1)} %collective-permute-done.15.refs_13_) | copy-start | bytes 995332
  48.5 9.1 %copy-start.22 = (bf16[1,144,864]{2,1,0:T(8,128)(2,1)}, bf16[1,144,864]{2,1,0:T(8,128)(2,1)S(1)}, u32[]{:S(2)}) copy-start(bf16[1,144,864]{2,1,0:T(8,128)(2,1)S(1)} %collective-permute-done.14.refs_9_.refs_5_) | copy-start | bytes 746500
  55.6 2.0 %copy-start.23 = (bf16[1,144,864]{2,1,0:T(8,128)(2,1)}, bf16[1,144,864]{2,1,0:T(8,128)(2,1)S(1)}, u32[]{:S(2)}) copy-start(bf16[1,144,864]{2,1,0:T(8,128)(2,1)S(1)} %collective-permute-done.12.refs_7_.refs_3_) | copy-start | bytes 746500
  55.6 2.0 %copy-start.10 = (bf16[2,2,64,1152]{3,2,1,0:T(8,128)(2,1)}, bf16[2,2,64,1152]{3,2,1,0:T(8,128)(2,1)S(1)}, u32[]{:S(2)}) copy-start(bf16[2,2,64,1152]{3,2,1,0:T(8,128)(2,1)S(1)} %collective-permute-done.5.refs_1_) | copy-start | bytes 1769476
  55.7 2.0 %copy-start.11 = (bf16[2,2,64,1152]{3,2,1,0:T(8,128)(2,1)}, bf16[2,2,64,1152]{3,2,1,0:T(8,128)(2,1)S(1)}, u32[]{:S(2)}) copy-start(bf16[2,2,64,1152]{3,2,1,0:T(8,128)(2,1)S(1)} %collective-permute-done.7.refs_3_) | copy-start | bytes 1769476
  55.7 1.6 %collective-permute-start.16 = (bf16[1,144,864]{2,1,0:T(8,128)(2,1)S(1)}, bf16[1,144,864]{2,1,0:T(8,128)(2,1)S(1)}, u32[]{:S(2)}, u32[]{:S(2)}) collective-permute-start(bf16[1,144,864]{2,1,0:T(8,128)(2,1)S(1)} %collective-permute-done.11.refs_6_.refs_2_), channel_id=1, source_target_pairs={{0,8},{1,9},{2,10},{3,11},{4,12},{5,13},{6,14},{7,15},{8,0},{9,1},... | collective-permute-start | bytes 746504 | tf_op jit(solution)/shard_map/ppermute | solution.py:515
  55.7 1.9 %collective-permute-start.17 = (bf16[1,144,864]{2,1,0:T(8,128)(2,1)S(1)}, bf16[1,144,864]{2,1,0:T(8,128)(2,1)S(1)}, u32[]{:S(2)}, u32[]{:S(2)}) collective-permute-start(bf16[1,144,864]{2,1,0:T(8,128)(2,1)S(1)} %collective-permute-done.12.refs_7_.refs_3_), channel_id=1, source_target_pairs={{0,8},{1,9},{2,10},{3,11},{4,12},{5,13},{6,14},{7,15},{8,0},{9,1},... | collective-permute-start | bytes 746504 | tf_op jit(solution)/shard_map/ppermute | solution.py:515
  57.3 0.7 copy-start.24
  58.0 0.7 copy-start.25
  70.7 3.7 %collective-permute-start.18 = (f32[4,48,864]{2,1,0:T(8,128)}, f32[4,48,864]{2,1,0:T(8,128)S(1)}, u32[]{:S(2)}, u32[]{:S(2)}) collective-permute-start(f32[4,48,864]{2,1,0:T(8,128)} %get-tuple-element.86), channel_id=1, source_target_pairs={{0,8},{1,9},{2,10},{3,11},{4,12},{5,13},{6,14},{7,15},{8,0},{9,1},... | collective-permute-start | bytes 1990664 | tf_op jit(solution)/shard_map/ppermute | solution.py:557
  70.8 13.7 %collective-permute-start.20 = (bf16[2,64,1152]{2,1,0:T(8,128)(2,1)}, bf16[2,64,1152]{2,1,0:T(8,128)(2,1)S(1)}, u32[]{:S(2)}, u32[]{:S(2)}) collective-permute-start(bf16[2,64,1152]{2,1,0:T(8,128)(2,1)} %get-tuple-element.94), channel_id=1, source_target_pairs={{0,1},{1,0},{2,3},{3,2},{4,5},{5,4},{6,7},{7,6},{8,9},{9,8},{10,11... | collective-permute-start | bytes 884744 | tf_op jit(solution)/shard_map/ppermute | solution.py:455
  71.7 15.5 %collective-permute-start.21 = (bf16[2,64,1152]{2,1,0:T(8,128)(2,1)}, bf16[2,64,1152]{2,1,0:T(8,128)(2,1)S(1)}, u32[]{:S(2)}, u32[]{:S(2)}) collective-permute-start(bf16[2,64,1152]{2,1,0:T(8,128)(2,1)} %get-tuple-element.95), channel_id=1, source_target_pairs={{0,16},{1,17},{2,18},{3,19},{4,20},{5,21},{6,22},{7,23},{8,24},{9,... | collective-permute-start | bytes 884744 | tf_op jit(solution)/shard_map/ppermute | solution.py:455
  71.7 15.5 %collective-permute-start.22 = (bf16[2,64,1152]{2,1,0:T(8,128)(2,1)}, bf16[2,64,1152]{2,1,0:T(8,128)(2,1)S(1)}, u32[]{:S(2)}, u32[]{:S(2)}) collective-permute-start(bf16[2,64,1152]{2,1,0:T(8,128)(2,1)} %get-tuple-element.96), channel_id=1, source_target_pairs={{0,17},{1,16},{2,19},{3,18},{4,21},{5,20},{6,23},{7,22},{8,25},{9,... | collective-permute-start | bytes 884744 | tf_op jit(solution)/shard_map/ppermute | solution.py:455
  75.5 11.7 %collective-permute-start.19 = (f32[2,48,864]{2,1,0:T(8,128)S(1)}, f32[2,48,864]{2,1,0:T(8,128)S(1)}, u32[]{:S(2)}, u32[]{:S(2)}) collective-permute-start(f32[2,48,864]{2,1,0:T(8,128)S(1)} %get-tuple-element.92), channel_id=1, source_target_pairs={{0,2},{1,3},{2,0},{3,1},{4,6},{5,7},{6,4},{7,5},{8,10},{9,11},{10,... | collective-permute-start | bytes 995336 | tf_op jit(solution)/shard_map/ppermute | solution.py:563
  84.6 6.2 %copy-start.15 = (bf16[2,64,1152]{2,1,0:T(8,128)(2,1)}, bf16[2,64,1152]{2,1,0:T(8,128)(2,1)S(1)}, u32[]{:S(2)}) copy-start(bf16[2,64,1152]{2,1,0:T(8,128)(2,1)S(1)} %collective-permute-done.20.refs_3_) | copy-start | bytes 884740
  87.2 3.6 %copy-start.16 = (bf16[2,64,1152]{2,1,0:T(8,128)(2,1)}, bf16[2,64,1152]{2,1,0:T(8,128)(2,1)S(1)}, u32[]{:S(2)}) copy-start(bf16[2,64,1152]{2,1,0:T(8,128)(2,1)S(1)} %collective-permute-done.21.refs_4_) | copy-start | bytes 884740
  87.2 3.6 %copy-start.17 = (bf16[2,64,1152]{2,1,0:T(8,128)(2,1)}, bf16[2,64,1152]{2,1,0:T(8,128)(2,1)S(1)}, u32[]{:S(2)}) copy-start(bf16[2,64,1152]{2,1,0:T(8,128)(2,1)S(1)} %collective-permute-done.22.refs_5_) | copy-start | bytes 884740
  87.2 15.1 %collective-permute-start.25 = (bf16[2,64,1152]{2,1,0:T(8,128)(2,1)}, bf16[2,64,1152]{2,1,0:T(8,128)(2,1)S(1)}, u32[]{:S(2)}, u32[]{:S(2)}) collective-permute-start(bf16[2,64,1152]{2,1,0:T(8,128)(2,1)} %get-tuple-element.104), channel_id=1, source_target_pairs={{0,1},{1,0},{2,3},{3,2},{4,5},{5,4},{6,7},{7,6},{8,9},{9,8},{10,11... | collective-permute-start | bytes 884744 | tf_op jit(solution)/shard_map/ppermute | solution.py:455
  88.5 14.5 %collective-permute-start.26 = (bf16[2,64,1152]{2,1,0:T(8,128)(2,1)}, bf16[2,64,1152]{2,1,0:T(8,128)(2,1)S(1)}, u32[]{:S(2)}, u32[]{:S(2)}) collective-permute-start(bf16[2,64,1152]{2,1,0:T(8,128)(2,1)} %get-tuple-element.105), channel_id=1, source_target_pairs={{0,16},{1,17},{2,18},{3,19},{4,20},{5,21},{6,22},{7,23},{8,24},{9,... | collective-permute-start | bytes 884744 | tf_op jit(solution)/shard_map/ppermute | solution.py:455
  88.9 14.1 %collective-permute-start.27 = (bf16[2,64,1152]{2,1,0:T(8,128)(2,1)}, bf16[2,64,1152]{2,1,0:T(8,128)(2,1)S(1)}, u32[]{:S(2)}, u32[]{:S(2)}) collective-permute-start(bf16[2,64,1152]{2,1,0:T(8,128)(2,1)} %get-tuple-element.106), channel_id=1, source_target_pairs={{0,17},{1,16},{2,19},{3,18},{4,21},{5,20},{6,23},{7,22},{8,25},{9,... | collective-permute-start | bytes 884744 | tf_op jit(solution)/shard_map/ppermute | solution.py:455
  93.8 25.5 %collective-permute-start.23 = (bf16[64,1152]{1,0:T(8,128)(2,1)}, bf16[64,1152]{1,0:T(8,128)(2,1)S(1)}, u32[]{:S(2)}, u32[]{:S(2)}) collective-permute-start(bf16[64,1152]{1,0:T(8,128)(2,1)} %get-tuple-element.101), channel_id=1, source_target_pairs={{0,0},{1,1},{16,2},{17,3},{2,4},{3,5},{18,6},{19,7},{20,8},{21,9},... | collective-permute-start | bytes 442376 | tf_op jit(solution)/shard_map/ppermute | solution.py:442
  96.5 22.9 %collective-permute-start.24 = (bf16[64,1152]{1,0:T(8,128)(2,1)}, bf16[64,1152]{1,0:T(8,128)(2,1)S(1)}, u32[]{:S(2)}, u32[]{:S(2)}) collective-permute-start(bf16[64,1152]{1,0:T(8,128)(2,1)} %get-tuple-element.102), channel_id=1, source_target_pairs={{2,0},{3,1},{18,2},{19,3},{0,4},{1,5},{16,6},{17,7},{22,8},{23,9},... | collective-permute-start | bytes 442376 | tf_op jit(solution)/shard_map/ppermute | solution.py:442
  102.3 0.8 copy-start.18
  102.3 15.1 %collective-permute-start.30 = (f32[1,48,864]{2,1,0:T(8,128)S(1)}, f32[1,48,864]{2,1,0:T(8,128)S(1)}, u32[]{:S(2)}, u32[]{:S(2)}) collective-permute-start(f32[1,48,864]{2,1,0:T(8,128)S(1)} %slice.40), channel_id=1, source_target_pairs={{0,4},{1,5},{2,6},{3,7},{4,0},{5,1},{6,2},{7,3},{8,12},{9,13},{10,... | collective-permute-start | bytes 497672 | tf_op jit(solution)/shard_map/ppermute | solution.py:604
  103.0 0.7 copy-start.19
  103.7 0.7 copy-start.20
  107.8 11.5 %collective-permute-start.28 = (bf16[64,1152]{1,0:T(8,128)(2,1)}, bf16[64,1152]{1,0:T(8,128)(2,1)S(1)}, u32[]{:S(2)}, u32[]{:S(2)}) collective-permute-start(bf16[64,1152]{1,0:T(8,128)(2,1)} %get-tuple-element.111), channel_id=1, source_target_pairs={{0,0},{1,1},{16,2},{17,3},{2,4},{3,5},{18,6},{19,7},{20,8},{21,9},... | collective-permute-start | bytes 442376 | tf_op jit(solution)/shard_map/ppermute | solution.py:442
  111.8 10.1 %collective-permute-start.29 = (bf16[64,1152]{1,0:T(8,128)(2,1)}, bf16[64,1152]{1,0:T(8,128)(2,1)S(1)}, u32[]{:S(2)}, u32[]{:S(2)}) collective-permute-start(bf16[64,1152]{1,0:T(8,128)(2,1)} %get-tuple-element.112), channel_id=1, source_target_pairs={{2,0},{3,1},{18,2},{19,3},{0,4},{1,5},{16,6},{17,7},{22,8},{23,9},... | collective-permute-start | bytes 442376 | tf_op jit(solution)/shard_map/ppermute | solution.py:442
  117.4 11.2 %collective-permute-start.31 = (f32[48,864]{1,0:T(8,128)S(1)}, f32[48,864]{1,0:T(8,128)S(1)}, u32[]{:S(2)}, u32[]{:S(2)}) collective-permute-start(f32[48,864]{1,0:T(8,128)S(1)} %bitcast.28), channel_id=1, source_target_pairs={{0,0},{1,1},{2,8},{3,9},{4,16},{5,17},{6,24},{7,25},{8,4},{9,5},{1... | collective-permute-start | bytes 497672 | tf_op jit(solution)/shard_map/ppermute | solution.py:606

commit v21 on v20

--- a/solution.py
+++ b/solution.py
@@ -572,7 +572,8 @@
         [w_scratch, pltpu.VMEM((halves, lay.frames, step_patches, 3 * cols), BF16)],
         (steps,),
     )(pos, info, *w_pieces, queries, keys, values, grad_attn)
-    sums, first_away, projected = lax.optimization_barrier((sums, first_away, projected))
+    sums, first_away, projected[1] = lax.optimization_barrier((sums, first_away, projected[1]))
+    projected, _ = lax.optimization_barrier((projected, sums))
     grad_hidden = over_chips(sums)
 
     out_parts = call(

time: 130 us -> 128 us (0.985)
  waiting for transfers between devices: 36.5 us -> 33 us
    ppermute x6, waiting for transfers between devices: 3.28 us -> 0.02 us  [over_chips(): got = [lax.ppermute(parts[k], AXES, chip_swap(k)) for k in range(1, chips)]]
    ppermute x1, starting transfers between devices: 1.92 us -> 4.27 us  [local(): grad_w = lax.ppermute(cut[0], AXES, lay.to_owner())]
    ppermute x4, starting transfers between devices: 17.8 us -> 15.5 us  [from_plane(): lax.ppermute(part, AXES, lay.from_plane(k))]
  transfers between devices with their start and end apart: 32 -> 32, of which waited for: 13 -> 12; matrix products, arithmetic and copies ran while one was open for 4% -> 4% of each run, Pallas kernels for 12% -> 12%
where the time goes in v21:
time: 128 us; the launch traced here: 127 us
  starting transfers between devices  51.5 us (40%)
  waiting for transfers between devices  33 us (26%)
  Pallas kernels  30.4 us (24%)
  other arithmetic  5.98 us (5%)
  local copies, waits for them, and re-layouts  4.65 us (4%)
    ppermute x4, starting transfers between devices, from_plane(): lax.ppermute(part, AXES, lay.from_plane(k))  15.5 us
    pallas_call x1, Pallas kernels, local(): call(functools.partial(forward_kernel, lay), 'forward', 14 * model * 1000...  12 us
    pallas_call x1, Pallas kernels, local(): call(functools.partial(backward_kernel, lay), 'backward', 10 * model * 10...  8.62 us
    ppermute x2, waiting for transfers between devices, local(): by_z[bit] = lax.ppermute(w_own, AXES, lay.swap(kz=bit))  7.58 us
    ppermute x1, waiting for transfers between devices, local(): by_z[k] = lax.ppermute(forwarded, AXES, lay.swap(kz=k & -k))  7.11 us
    ppermute x6, starting transfers between devices, over_chips(): got = [lax.ppermute(parts[k], AXES, chip_swap(k)) for k in range(1, chips)]  6.98 us
    ppermute x2, starting transfers between devices, local(): by_z[bit] = lax.ppermute(w_own, AXES, lay.swap(kz=bit))  5.4 us
    ppermute x1, waiting for transfers between devices, local(): wo_own = lax.ppermute(late_w_out, AXES, lay.rows_to_chip())  5.26 us
  transfers between devices with their start and end apart: 32, of which 12 were waited for; matrix products, arithmetic and copies ran while one was open for 4% of the time, Pallas kernels for 12%

profile of v21, /device:TPU:4, one launch (start us, length us, event | category | flops | bytes accessed | tf_op | source)
XLA Modules:
  0.0 126.7 jit_solution(1473816943276797705)
XLA Ops:
  0.6 0.6 pad_add_fusion.1.pos_ref
  1.2 3.3 %start.1 = (bf16[1,2,64,1152]{3,2,1,0:T(8,128)(2,1)}, bf16[1,2,64,1152]{3,2,1,0:T(8,128)(2,1)}, bf16[144,432]{1,0:T(8,128)(2,1)}, bf16[144,432]{1,0:T(8,128)(2,1)}) custom-call(s32[4]{0:T(128)} %pad_add_fusion.1.pos_ref, bf16[1,128,1152]{2,1,0:T(8,128)(2,1)} %x_ref.1, bf16[1,128,1152]{2,1,0:T(8,128)(2,1)} %g_ref.1, bf16[144,3456]{1,0:T(8,128)(2,1)} %w_ref.1), custom_call_target="tpu_custom_call" | custom-call | flops 1179648000 | bytes 2359296 | tf_op jit(solution)/shard_map/start/pallas_call | solution.py:471
  4.5 1.9 %collective-permute-start.2 = (bf16[1,2,64,1152]{3,2,1,0:T(8,128)(2,1)}, bf16[1,2,64,1152]{3,2,1,0:T(8,128)(2,1)S(1)}, u32[]{:S(2)}, u32[]{:S(2)}) collective-permute-start(bf16[1,2,64,1152]{3,2,1,0:T(8,128)(2,1)} %get-tuple-element.61), channel_id=1, source_target_pairs={{0,0},{1,1},{2,16},{3,17},{4,2},{5,3},{6,18},{7,19},{8,20},{9,21},... | collective-permute-start | bytes 884744 | tf_op jit(solution)/shard_map/ppermute | solution.py:481
  6.5 0.6 copy-done.7
  7.1 0.1 fusion.7
  7.2 2.2 %collective-permute-start = (s32[1,16]{1,0:T(1,128)S(1)}, s32[1,16]{1,0:T(1,128)S(1)}, u32[]{:S(2)}, u32[]{:S(2)}) collective-permute-start(s32[1,16]{1,0:T(1,128)S(1)} %fusion.7), channel_id=1, source_target_pairs={{0,8},{1,9},{2,10},{3,11},{4,12},{5,13},{6,14},{7,15},{8,0},{9,1},... | collective-permute-start | bytes 200 | tf_op jit(solution)/shard_map/ppermute | solution.py:459
  9.4 1.5 %collective-permute-start.8 = (bf16[144,432]{1,0:T(8,128)(2,1)}, bf16[144,432]{1,0:T(8,128)(2,1)S(1)}, u32[]{:S(2)}, u32[]{:S(2)}) collective-permute-start(bf16[144,432]{1,0:T(8,128)(2,1)} %get-tuple-element.67), channel_id=1, source_target_pairs={{0,1},{1,0},{2,3},{3,2},{4,5},{5,4},{6,7},{7,6},{8,9},{9,8},{10,11... | collective-permute-start | bytes 373256 | tf_op jit(solution)/shard_map/ppermute | solution.py:483
  10.8 2.5 %collective-permute-start.3 = (bf16[1,2,64,1152]{3,2,1,0:T(8,128)(2,1)}, bf16[1,2,64,1152]{3,2,1,0:T(8,128)(2,1)S(1)}, u32[]{:S(2)}, u32[]{:S(2)}) collective-permute-start(bf16[1,2,64,1152]{3,2,1,0:T(8,128)(2,1)} %get-tuple-element.62), channel_id=1, source_target_pairs={{0,2},{1,3},{2,18},{3,19},{4,0},{5,1},{6,16},{7,17},{8,22},{9,23},... | collective-permute-start | bytes 884744 | tf_op jit(solution)/shard_map/ppermute | solution.py:481
  13.4 1.5 %collective-permute-start.1 = (s32[2,16]{1,0:T(2,128)S(1)}, s32[2,16]{1,0:T(2,128)S(1)}, u32[]{:S(2)}, u32[]{:S(2)}) collective-permute-start(s32[2,16]{1,0:T(2,128)S(1)} %pad_add_fusion), channel_id=1, source_target_pairs={{0,16},{1,17},{2,18},{3,19},{4,20},{5,21},{6,22},{7,23},{8,24},{9,... | collective-permute-start | bytes 392 | tf_op jit(solution)/shard_map/ppermute | solution.py:461
  14.9 0.8 collective-permute-start.4
  15.7 1.4 %collective-permute-done.1 = s32[2,16]{1,0:T(2,128)S(1)} collective-permute-done((s32[2,16]{1,0:T(2,128)S(1)}, s32[2,16]{1,0:T(2,128)S(1)}, u32[]{:S(2)}, u32[]{:S(2)}) %collective-permute-start.1) | collective-permute-done | bytes 160 | tf_op jit(solution)/shard_map/ppermute | solution.py:461
  17.1 0.6 fusion.2.info_ref
  17.7 0.9 broadcast_select_fusion.3
  18.6 4.3 %collective-permute-start.9 = (bf16[144,1152]{1,0:T(8,128)(2,1)S(1)}, bf16[144,1152]{1,0:T(8,128)(2,1)S(1)}, u32[]{:S(2)}, u32[]{:S(2)}) collective-permute-start(bf16[144,1152]{1,0:T(8,128)(2,1)S(1)} %copy-done.12), channel_id=1, source_target_pairs={{0,0},{1,1},{2,18},{3,19},{4,8},{5,9},{6,26},{7,27},{8,4},{9,5},{1... | collective-permute-start | bytes 995336 | tf_op jit(solution)/shard_map/ppermute | solution.py:494
  23.0 1.7 %collective-permute-done.3.refs_1_ = bf16[1,2,64,1152]{3,2,1,0:T(8,128)(2,1)S(1)} collective-permute-done((bf16[1,2,64,1152]{3,2,1,0:T(8,128)(2,1)}, bf16[1,2,64,1152]{3,2,1,0:T(8,128)(2,1)S(1)}, u32[]{:S(2)}, u32[]{:S(2)}) %collective-permute-start.3) | collective-permute-done | bytes 294944 | tf_op jit(solution)/shard_map/ppermute | solution.py:481
  24.7 1.0 collective-permute-start.6
  25.7 0.1 maximum_bitcast_fusion.2.refs_4_.refs_0_
  25.9 1.1 collective-permute-start.5
  27.0 5.3 %collective-permute-done.9.refs_12_ = bf16[144,1152]{1,0:T(8,128)(2,1)S(1)} collective-permute-done((bf16[144,1152]{1,0:T(8,128)(2,1)S(1)}, bf16[144,1152]{1,0:T(8,128)(2,1)S(1)}, u32[]{:S(2)}, u32[]{:S(2)}) %collective-permute-start.9) | collective-permute-done | bytes 331808 | tf_op jit(solution)/shard_map/ppermute | solution.py:494
  32.3 0.2 collective-permute-start.11
  32.5 5.2 %collective-permute-start.10 = (bf16[1,144,864]{2,1,0:T(8,128)(2,1)S(1)}, bf16[1,144,864]{2,1,0:T(8,128)(2,1)S(1)}, u32[]{:S(2)}, u32[]{:S(2)}) collective-permute-start(bf16[1,144,864]{2,1,0:T(8,128)(2,1)S(1)} %maximum_bitcast_fusion.2.refs_4_.refs_0_), channel_id=1, source_target_pairs={{0,2},{1,3},{2,0},{3,1},{4,6},{5,7},{6,4},{7,5},{8,10},{9,11},{10,... | collective-permute-start | bytes 746504 | tf_op jit(solution)/shard_map/ppermute | solution.py:499
  37.8 0.9 collective-permute-start.7
  38.7 6.3 %collective-permute-done.11.refs_6_.refs_2_ = bf16[1,144,864]{2,1,0:T(8,128)(2,1)S(1)} collective-permute-done((bf16[1,144,864]{2,1,0:T(8,128)(2,1)S(1)}, bf16[1,144,864]{2,1,0:T(8,128)(2,1)S(1)}, u32[]{:S(2)}, u32[]{:S(2)}) %collective-permute-start.11) | collective-permute-done | bytes 248864 | tf_op jit(solution)/shard_map/ppermute | solution.py:499
  45.0 1.3 %collective-permute-done.10.refs_5_.refs_1_ = bf16[1,144,864]{2,1,0:T(8,128)(2,1)S(1)} collective-permute-done((bf16[1,144,864]{2,1,0:T(8,128)(2,1)S(1)}, bf16[1,144,864]{2,1,0:T(8,128)(2,1)S(1)}, u32[]{:S(2)}, u32[]{:S(2)}) %collective-permute-start.10) | collective-permute-done | bytes 248864 | tf_op jit(solution)/shard_map/ppermute | solution.py:499
  46.3 0.1 broadcast_select_fusion
  46.4 0.6 copy-done.6
  47.0 0.4 collective-permute-start.12
  47.4 1.1 collective-permute-done.14.refs_9_.refs_5_
  48.5 7.1 %collective-permute-done.12.refs_7_.refs_3_ = bf16[1,144,864]{2,1,0:T(8,128)(2,1)S(1)} collective-permute-done((bf16[1,144,864]{2,1,0:T(8,128)(2,1)S(1)}, bf16[1,144,864]{2,1,0:T(8,128)(2,1)S(1)}, u32[]{:S(2)}, u32[]{:S(2)}) %collective-permute-start.12) | collective-permute-done | bytes 248864 | tf_op jit(solution)/shard_map/ppermute | solution.py:503
  55.7 0.1 collective-permute-start.16
  55.7 0.5 collective-permute-start.17
  56.2 1.0 collective-permute-done.16.refs_10_.refs_6_
  57.3 0.4 collective-permute-done.17.refs_11_.refs_7_
  57.7 0.3 copy-done.24
  58.0 0.7 copy-done.25
  58.7 12.0 %forward.1 = (bf16[2,8,64,144]{3,2,1,0:T(8,128)(2,1)}, bf16[2,8,64,144]{3,2,1,0:T(8,128)(2,1)}, bf16[2,8,64,144]{3,2,1,0:T(8,128)(2,1)}, bf16[2,8,64,144]{3,2,1,...) custom-call(s32[4]{0:T(128)} %pad_add_fusion.1.pos_ref, ...), custom_call_target="tpu_custom_call" | custom-call | flops 8257536000 | bytes 2359296 | tf_op jit(solution)/shard_map/forward/pallas_call | solution.py:537
  70.7 0.2 collective-permute-start.18
  70.8 0.8 collective-permute-start.20
  71.7 2.7 %collective-permute-start.22 = (bf16[2,64,1152]{2,1,0:T(8,128)(2,1)}, bf16[2,64,1152]{2,1,0:T(8,128)(2,1)S(1)}, u32[]{:S(2)}, u32[]{:S(2)}) collective-permute-start(bf16[2,64,1152]{2,1,0:T(8,128)(2,1)} %get-tuple-element.98), channel_id=1, source_target_pairs={{0,17},{1,16},{2,19},{3,18},{4,21},{5,20},{6,23},{7,22},{8,25},{9,... | collective-permute-start | bytes 884744 | tf_op jit(solution)/shard_map/ppermute | solution.py:455
  74.3 1.2 slice_add_fusion
  75.5 0.4 collective-permute-start.19
  75.9 8.6 %backward.1 = (f32[2,64,1152]{2,1,0:T(8,128)}, bf16[2,64,1152]{2,1,0:T(8,128)(2,1)}, bf16[2,64,1152]{2,1,0:T(8,128)(2,1)}, bf16[2,64,1152]{2,1,0:T(8,128)(2,1)}) custom-call(s32[4]{0:T(128)} %pad_add_fusion.1.pos_ref, s32[16]{0:T(128)} %fusion.2.info_ref, bf16[1,144,864]{2,1,0:T(8,128)(2,1)} %copy-done, bf16[1,144,864]{2,1,0:T(8,128)(2,1)} %copy-done.6, ...), custom_call_target="tpu_custom_call" | custom-call | flops 5898240000 | bytes 2359296 | tf_op jit(solution)/shard_map/backward/pallas_call | solution.py:565
  84.6 0.5 collective-permute-done.19
  85.0 0.8 collective-permute-start.25
  85.8 0.6 collective-permute-start.26
  86.5 2.0 %collective-permute-start.27 = (bf16[2,64,1152]{2,1,0:T(8,128)(2,1)}, bf16[2,64,1152]{2,1,0:T(8,128)(2,1)S(1)}, u32[]{:S(2)}, u32[]{:S(2)}) collective-permute-start(bf16[2,64,1152]{2,1,0:T(8,128)(2,1)} %get-tuple-element.102), channel_id=1, source_target_pairs={{0,17},{1,16},{2,19},{3,18},{4,21},{5,20},{6,23},{7,22},{8,25},{9,... | collective-permute-start | bytes 884744 | tf_op jit(solution)/shard_map/ppermute | solution.py:455
  88.6 0.7 copy-done.16
  89.3 0.1 copy-done.17
  89.3 3.1 %output.1 = (bf16[64,1152]{1,0:T(8,128)(2,1)}, bf16[64,1152]{1,0:T(8,128)(2,1)}) custom-call(s32[4]{0:T(128)} %pad_add_fusion.1.pos_ref, s32[16]{0:T(128)} %fusion.2.info_ref, bf16[1,2,64,1152]{3,2,1,0:T(8,128)(2,1)} %copy-done.3, bf16[1,2,64,1152]{3,2,1,0:T(8,128)(2,1)} %copy-done.4, f32[2,64,1152]{2,1,0:T(8,128)} %get-tuple-element.103.refs_2_, ...), custom_call_target="tpu_custom_call" | custom-call | flops 11796480000 | bytes 2359296 | tf_op jit(solution)/shard_map/output/pallas_call | solution.py:579
  92.4 2.6 %collective-permute-start.23 = (bf16[64,1152]{1,0:T(8,128)(2,1)}, bf16[64,1152]{1,0:T(8,128)(2,1)S(1)}, u32[]{:S(2)}, u32[]{:S(2)}) collective-permute-start(bf16[64,1152]{1,0:T(8,128)(2,1)} %get-tuple-element.107), channel_id=1, source_target_pairs={{0,0},{1,1},{16,2},{17,3},{2,4},{3,5},{18,6},{19,7},{20,8},{21,9},... | collective-permute-start | bytes 442376 | tf_op jit(solution)/shard_map/ppermute | solution.py:442
  95.0 5.8 %collective-permute-start.24 = (bf16[64,1152]{1,0:T(8,128)(2,1)}, bf16[64,1152]{1,0:T(8,128)(2,1)S(1)}, u32[]{:S(2)}, u32[]{:S(2)}) collective-permute-start(bf16[64,1152]{1,0:T(8,128)(2,1)} %get-tuple-element.108), channel_id=1, source_target_pairs={{2,0},{3,1},{18,2},{19,3},{0,4},{1,5},{16,6},{17,7},{22,8},{23,9},... | collective-permute-start | bytes 442376 | tf_op jit(solution)/shard_map/ppermute | solution.py:442
  101.0 0.6 copy-done.18
  101.6 0.1 copy-done.19
  101.7 0.7 copy-done.20
  102.4 3.4 %input_grad.1 = (bf16[64,1152]{1,0:T(8,128)(2,1)}, bf16[64,1152]{1,0:T(8,128)(2,1)}) custom-call(s32[4]{0:T(128)} %pad_add_fusion.1.pos_ref, s32[16]{0:T(128)} %fusion.2.info_ref, bf16[1,2,64,1152]{3,2,1,0:T(8,128)(2,1)} %copy-done.3, bf16[1,2,64,1152]{3,2,1,0:T(8,128)(2,1)} %copy-done.4, f32[2,64,1152]{2,1,0:T(8,128)} %get-tuple-element.109.refs_2_, ...), custom_call_target="tpu_custom_call" | custom-call | flops 1769472000 | bytes 2359296 | tf_op jit(solution)/shard_map/input_grad/pallas_call | solution.py:591
  105.8 4.3 %collective-permute-start.28 = (bf16[64,1152]{1,0:T(8,128)(2,1)}, bf16[64,1152]{1,0:T(8,128)(2,1)S(1)}, u32[]{:S(2)}, u32[]{:S(2)}) collective-permute-start(bf16[64,1152]{1,0:T(8,128)(2,1)} %get-tuple-element.113), channel_id=1, source_target_pairs={{0,0},{1,1},{16,2},{17,3},{2,4},{3,5},{18,6},{19,7},{20,8},{21,9},... | collective-permute-start | bytes 442376 | tf_op jit(solution)/shard_map/ppermute | solution.py:442
  110.1 2.9 %collective-permute-start.29 = (bf16[64,1152]{1,0:T(8,128)(2,1)}, bf16[64,1152]{1,0:T(8,128)(2,1)S(1)}, u32[]{:S(2)}, u32[]{:S(2)}) collective-permute-start(bf16[64,1152]{1,0:T(8,128)(2,1)} %get-tuple-element.114), channel_id=1, source_target_pairs={{2,0},{3,1},{18,2},{19,3},{0,4},{1,5},{16,6},{17,7},{22,8},{23,9},... | collective-permute-start | bytes 442376 | tf_op jit(solution)/shard_map/ppermute | solution.py:442
  113.0 4.3 %collective-permute-start.31 = (f32[48,864]{1,0:T(8,128)S(1)}, f32[48,864]{1,0:T(8,128)S(1)}, u32[]{:S(2)}, u32[]{:S(2)}) collective-permute-start(f32[48,864]{1,0:T(8,128)S(1)} %bitcast.28), channel_id=1, source_target_pairs={{0,0},{1,1},{2,8},{3,9},{4,16},{5,17},{6,24},{7,25},{8,4},{9,5},{1... | collective-permute-start | bytes 497672 | tf_op jit(solution)/shard_map/ppermute | solution.py:607
  117.3 2.9 %collective-permute-done.29 = bf16[64,1152]{1,0:T(8,128)(2,1)S(1)} collective-permute-done((bf16[64,1152]{1,0:T(8,128)(2,1)}, bf16[64,1152]{1,0:T(8,128)(2,1)S(1)}, u32[]{:S(2)}, u32[]{:S(2)}) %collective-permute-start.29) | collective-permute-done | bytes 147488 | tf_op jit(solution)/shard_map/ppermute | solution.py:442
  120.3 0.7 maximum_bitcast_fusion.1
  121.0 0.7 maximum_bitcast_fusion
  121.8 4.1 %collective-permute-done.31 = f32[48,864]{1,0:T(8,128)S(1)} collective-permute-done((f32[48,864]{1,0:T(8,128)S(1)}, f32[48,864]{1,0:T(8,128)S(1)}, u32[]{:S(2)}, u32[]{:S(2)}) %collective-permute-start.31) | collective-permute-done | bytes 165920 | tf_op jit(solution)/shard_map/ppermute | solution.py:607
  125.9 0.1 fusion.6
  126.0 0.7 maximum_multiply_fusion
  (75 shorter events, 0.5 us)
Async XLA Ops:
  4.5 10.4 %collective-permute-start.2 = (bf16[1,2,64,1152]{3,2,1,0:T(8,128)(2,1)}, bf16[1,2,64,1152]{3,2,1,0:T(8,128)(2,1)S(1)}, u32[]{:S(2)}, u32[]{:S(2)}) collective-permute-start(bf16[1,2,64,1152]{3,2,1,0:T(8,128)(2,1)} %get-tuple-element.61), channel_id=1, source_target_pairs={{0,0},{1,1},{2,16},{3,17},{4,2},{5,3},{6,18},{7,19},{8,20},{9,21},... | collective-permute-start | bytes 884744 | tf_op jit(solution)/shard_map/ppermute | solution.py:481
  6.4 0.7 copy-start.7
  6.5 0.7 copy-start.8
  6.5 0.7 copy-start.9
  7.2 6.2 %collective-permute-start = (s32[1,16]{1,0:T(1,128)S(1)}, s32[1,16]{1,0:T(1,128)S(1)}, u32[]{:S(2)}, u32[]{:S(2)}) collective-permute-start(s32[1,16]{1,0:T(1,128)S(1)} %fusion.7), channel_id=1, source_target_pairs={{0,8},{1,9},{2,10},{3,11},{4,12},{5,13},{6,14},{7,15},{8,0},{9,1},... | collective-permute-start | bytes 200 | tf_op jit(solution)/shard_map/ppermute | solution.py:459
  9.4 8.3 %collective-permute-start.8 = (bf16[144,432]{1,0:T(8,128)(2,1)}, bf16[144,432]{1,0:T(8,128)(2,1)S(1)}, u32[]{:S(2)}, u32[]{:S(2)}) collective-permute-start(bf16[144,432]{1,0:T(8,128)(2,1)} %get-tuple-element.67), channel_id=1, source_target_pairs={{0,1},{1,0},{2,3},{3,2},{4,5},{5,4},{6,7},{7,6},{8,9},{9,8},{10,11... | collective-permute-start | bytes 373256 | tf_op jit(solution)/shard_map/ppermute | solution.py:483
  10.8 13.9 %collective-permute-start.3 = (bf16[1,2,64,1152]{3,2,1,0:T(8,128)(2,1)}, bf16[1,2,64,1152]{3,2,1,0:T(8,128)(2,1)S(1)}, u32[]{:S(2)}, u32[]{:S(2)}) collective-permute-start(bf16[1,2,64,1152]{3,2,1,0:T(8,128)(2,1)} %get-tuple-element.62), channel_id=1, source_target_pairs={{0,2},{1,3},{2,18},{3,19},{4,0},{5,1},{6,16},{7,17},{8,22},{9,23},... | collective-permute-start | bytes 884744 | tf_op jit(solution)/shard_map/ppermute | solution.py:481
  13.4 5.3 %copy-start.12 = (bf16[144,1152]{1,0:T(8,128)(2,1)S(1)}, bf16[144,1152]{1,0:T(8,128)(2,1)}, u32[]{:S(2)}) copy-start(bf16[144,1152]{1,0:T(8,128)(2,1)} %param.15) | copy-start | bytes 995332
  13.4 3.6 %collective-permute-start.1 = (s32[2,16]{1,0:T(2,128)S(1)}, s32[2,16]{1,0:T(2,128)S(1)}, u32[]{:S(2)}, u32[]{:S(2)}) collective-permute-start(s32[2,16]{1,0:T(2,128)S(1)} %pad_add_fusion), channel_id=1, source_target_pairs={{0,16},{1,17},{2,18},{3,19},{4,20},{5,21},{6,22},{7,23},{8,24},{9,... | collective-permute-start | bytes 392 | tf_op jit(solution)/shard_map/ppermute | solution.py:461
  14.9 10.9 %copy-start.3 = (bf16[1,2,64,1152]{3,2,1,0:T(8,128)(2,1)}, bf16[1,2,64,1152]{3,2,1,0:T(8,128)(2,1)S(1)}, u32[]{:S(2)}) copy-start(bf16[1,2,64,1152]{3,2,1,0:T(8,128)(2,1)S(1)} %collective-permute-done.2.refs_0_) | copy-start | bytes 884740
  14.9 9.8 %collective-permute-start.4 = (bf16[1,2,64,1152]{3,2,1,0:T(8,128)(2,1)S(1)}, bf16[1,2,64,1152]{3,2,1,0:T(8,128)(2,1)S(1)}, u32[]{:S(2)}, u32[]{:S(2)}) collective-permute-start(bf16[1,2,64,1152]{3,2,1,0:T(8,128)(2,1)S(1)} %collective-permute-done.2.refs_0_), channel_id=1, source_target_pairs={{0,1},{1,0},{2,3},{3,2},{4,5},{5,4},{6,7},{7,6},{8,9},{9,8},{10,11... | collective-permute-start | bytes 884744 | tf_op jit(solution)/shard_map/ppermute | solution.py:491
  18.6 13.6 %collective-permute-start.9 = (bf16[144,1152]{1,0:T(8,128)(2,1)S(1)}, bf16[144,1152]{1,0:T(8,128)(2,1)S(1)}, u32[]{:S(2)}, u32[]{:S(2)}) collective-permute-start(bf16[144,1152]{1,0:T(8,128)(2,1)S(1)} %copy-done.12), channel_id=1, source_target_pairs={{0,0},{1,1},{2,18},{3,19},{4,8},{5,9},{6,26},{7,27},{8,4},{9,5},{1... | collective-permute-start | bytes 995336 | tf_op jit(solution)/shard_map/ppermute | solution.py:494
  24.7 13.0 %copy-start.4 = (bf16[1,2,64,1152]{3,2,1,0:T(8,128)(2,1)}, bf16[1,2,64,1152]{3,2,1,0:T(8,128)(2,1)S(1)}, u32[]{:S(2)}) copy-start(bf16[1,2,64,1152]{3,2,1,0:T(8,128)(2,1)S(1)} %collective-permute-done.3.refs_1_) | copy-start | bytes 884740
  24.7 13.0 %collective-permute-start.6 = (bf16[1,2,64,1152]{3,2,1,0:T(8,128)(2,1)S(1)}, bf16[1,2,64,1152]{3,2,1,0:T(8,128)(2,1)S(1)}, u32[]{:S(2)}, u32[]{:S(2)}) collective-permute-start(bf16[1,2,64,1152]{3,2,1,0:T(8,128)(2,1)S(1)} %collective-permute-done.3.refs_1_), channel_id=1, source_target_pairs={{0,16},{1,17},{2,18},{3,19},{4,20},{5,21},{6,22},{7,23},{8,24},{9,... | collective-permute-start | bytes 884744 | tf_op jit(solution)/shard_map/ppermute | solution.py:449
  25.9 20.4 %copy-start = (bf16[1,144,864]{2,1,0:T(8,128)(2,1)}, bf16[1,144,864]{2,1,0:T(8,128)(2,1)S(1)}, u32[]{:S(2)}) copy-start(bf16[1,144,864]{2,1,0:T(8,128)(2,1)S(1)} %maximum_bitcast_fusion.2.refs_4_.refs_0_) | copy-start | bytes 746500
  25.9 12.7 %copy-start.1 = (bf16[2,2,64,1152]{3,2,1,0:T(8,128)(2,1)}, bf16[2,2,64,1152]{3,2,1,0:T(8,128)(2,1)S(1)}, u32[]{:S(2)}) copy-start(bf16[2,2,64,1152]{3,2,1,0:T(8,128)(2,1)S(1)} %pad_maximum_fusion.refs_0_) | copy-start | bytes 1769476
  25.9 29.7 %collective-permute-start.5 = (bf16[2,2,64,1152]{3,2,1,0:T(8,128)(2,1)S(1)}, bf16[2,2,64,1152]{3,2,1,0:T(8,128)(2,1)S(1)}, u32[]{:S(2)}, u32[]{:S(2)}) collective-permute-start(bf16[2,2,64,1152]{3,2,1,0:T(8,128)(2,1)S(1)} %pad_maximum_fusion.refs_0_), channel_id=1, source_target_pairs={{0,16},{1,17},{2,18},{3,19},{4,20},{5,21},{6,22},{7,23},{8,24},{9,... | collective-permute-start | bytes 1769480 | tf_op jit(solution)/shard_map/ppermute | solution.py:452
  32.3 5.4 %copy-start.13 = (bf16[144,1152]{1,0:T(8,128)(2,1)}, bf16[144,1152]{1,0:T(8,128)(2,1)S(1)}, u32[]{:S(2)}) copy-start(bf16[144,1152]{1,0:T(8,128)(2,1)S(1)} %collective-permute-done.9.refs_12_) | copy-start | bytes 995332
  32.3 12.7 %collective-permute-start.11 = (bf16[1,144,864]{2,1,0:T(8,128)(2,1)S(1)}, bf16[1,144,864]{2,1,0:T(8,128)(2,1)S(1)}, u32[]{:S(2)}, u32[]{:S(2)}) collective-permute-start(bf16[1,144,864]{2,1,0:T(8,128)(2,1)S(1)} %maximum_bitcast_fusion.2.refs_4_.refs_0_), channel_id=1, source_target_pairs={{0,4},{1,5},{2,6},{3,7},{4,0},{5,1},{6,2},{7,3},{8,12},{9,13},{10,... | collective-permute-start | bytes 746504 | tf_op jit(solution)/shard_map/ppermute | solution.py:499
  32.5 13.8 %collective-permute-start.10 = (bf16[1,144,864]{2,1,0:T(8,128)(2,1)S(1)}, bf16[1,144,864]{2,1,0:T(8,128)(2,1)S(1)}, u32[]{:S(2)}, u32[]{:S(2)}) collective-permute-start(bf16[1,144,864]{2,1,0:T(8,128)(2,1)S(1)} %maximum_bitcast_fusion.2.refs_4_.refs_0_), channel_id=1, source_target_pairs={{0,2},{1,3},{2,0},{3,1},{4,6},{5,7},{6,4},{7,5},{8,10},{9,11},{10,... | collective-permute-start | bytes 746504 | tf_op jit(solution)/shard_map/ppermute | solution.py:499
  37.8 8.6 %copy-start.2 = (bf16[2,2,64,1152]{3,2,1,0:T(8,128)(2,1)}, bf16[2,2,64,1152]{3,2,1,0:T(8,128)(2,1)S(1)}, u32[]{:S(2)}) copy-start(bf16[2,2,64,1152]{3,2,1,0:T(8,128)(2,1)S(1)} %pad_maximum_fusion.1.refs_2_) | copy-start | bytes 1769476
  37.8 17.9 %collective-permute-start.7 = (bf16[2,2,64,1152]{3,2,1,0:T(8,128)(2,1)S(1)}, bf16[2,2,64,1152]{3,2,1,0:T(8,128)(2,1)S(1)}, u32[]{:S(2)}, u32[]{:S(2)}) collective-permute-start(bf16[2,2,64,1152]{3,2,1,0:T(8,128)(2,1)S(1)} %pad_maximum_fusion.1.refs_2_), channel_id=1, source_target_pairs={{0,1},{1,0},{2,3},{3,2},{4,5},{5,4},{6,7},{7,6},{8,9},{9,8},{10,11... | collective-permute-start | bytes 1769480 | tf_op jit(solution)/shard_map/ppermute | solution.py:452
  38.7 8.3 %collective-permute-start.13 = (bf16[1,144,864]{2,1,0:T(8,128)(2,1)S(1)}, bf16[1,144,864]{2,1,0:T(8,128)(2,1)S(1)}, u32[]{:S(2)}, u32[]{:S(2)}) collective-permute-start(bf16[1,144,864]{2,1,0:T(8,128)(2,1)S(1)} %maximum_bitcast_fusion.2.refs_4_.refs_0_), channel_id=1, source_target_pairs={{0,8},{1,9},{2,10},{3,11},{4,12},{5,13},{6,14},{7,15},{8,0},{9,1},... | collective-permute-start | bytes 746504 | tf_op jit(solution)/shard_map/ppermute | solution.py:511
  45.0 10.6 %copy-start.5 = (bf16[1,144,864]{2,1,0:T(8,128)(2,1)}, bf16[1,144,864]{2,1,0:T(8,128)(2,1)S(1)}, u32[]{:S(2)}) copy-start(bf16[1,144,864]{2,1,0:T(8,128)(2,1)S(1)} %collective-permute-done.11.refs_6_.refs_2_) | copy-start | bytes 746500
  45.0 2.4 %collective-permute-start.15 = (bf16[144,1152]{1,0:T(8,128)(2,1)}, bf16[144,1152]{1,0:T(8,128)(2,1)S(1)}, u32[]{:S(2)}, u32[]{:S(2)}) collective-permute-start(bf16[144,1152]{1,0:T(8,128)(2,1)} %copy-done.13), channel_id=1, source_target_pairs={{0,8},{1,9},{2,10},{3,11},{4,12},{5,13},{6,14},{7,15},{8,0},{9,1},... | collective-permute-start | bytes 995336 | tf_op jit(solution)/shard_map/ppermute | solution.py:495
  46.3 0.7 copy-start.6
  47.0 1.5 %collective-permute-start.14 = (bf16[1,144,864]{2,1,0:T(8,128)(2,1)S(1)}, bf16[1,144,864]{2,1,0:T(8,128)(2,1)S(1)}, u32[]{:S(2)}, u32[]{:S(2)}) collective-permute-start(bf16[1,144,864]{2,1,0:T(8,128)(2,1)S(1)} %get-tuple-element.127), channel_id=1, source_target_pairs={{0,8},{1,9},{2,10},{3,11},{4,12},{5,13},{6,14},{7,15},{8,0},{9,1},... | collective-permute-start | bytes 746504 | tf_op jit(solution)/shard_map/ppermute | solution.py:511
  47.0 10.6 %copy-start.21 = (bf16[1,144,864]{2,1,0:T(8,128)(2,1)}, bf16[1,144,864]{2,1,0:T(8,128)(2,1)S(1)}, u32[]{:S(2)}) copy-start(bf16[1,144,864]{2,1,0:T(8,128)(2,1)S(1)} %collective-permute-done.13.refs_8_.refs_4_) | copy-start | bytes 746500
  47.0 8.6 %collective-permute-start.12 = (bf16[1,144,864]{2,1,0:T(8,128)(2,1)S(1)}, bf16[1,144,864]{2,1,0:T(8,128)(2,1)S(1)}, u32[]{:S(2)}, u32[]{:S(2)}) collective-permute-start(bf16[1,144,864]{2,1,0:T(8,128)(2,1)S(1)} %get-tuple-element.128), channel_id=1, source_target_pairs={{0,2},{1,3},{2,0},{3,1},{4,6},{5,7},{6,4},{7,5},{8,10},{9,11},{10,... | collective-permute-start | bytes 746504 | tf_op jit(solution)/shard_map/ppermute | solution.py:503
  47.4 10.2 %copy-start.14 = (bf16[144,1152]{1,0:T(8,128)(2,1)}, bf16[144,1152]{1,0:T(8,128)(2,1)S(1)}, u32[]{:S(2)}) copy-start(bf16[144,1152]{1,0:T(8,128)(2,1)S(1)} %collective-permute-done.15.refs_13_) | copy-start | bytes 995332
  48.5 9.1 %copy-start.22 = (bf16[1,144,864]{2,1,0:T(8,128)(2,1)}, bf16[1,144,864]{2,1,0:T(8,128)(2,1)S(1)}, u32[]{:S(2)}) copy-start(bf16[1,144,864]{2,1,0:T(8,128)(2,1)S(1)} %collective-permute-done.14.refs_9_.refs_5_) | copy-start | bytes 746500
  55.6 2.0 %copy-start.23 = (bf16[1,144,864]{2,1,0:T(8,128)(2,1)}, bf16[1,144,864]{2,1,0:T(8,128)(2,1)S(1)}, u32[]{:S(2)}) copy-start(bf16[1,144,864]{2,1,0:T(8,128)(2,1)S(1)} %collective-permute-done.12.refs_7_.refs_3_) | copy-start | bytes 746500
  55.6 2.0 %copy-start.10 = (bf16[2,2,64,1152]{3,2,1,0:T(8,128)(2,1)}, bf16[2,2,64,1152]{3,2,1,0:T(8,128)(2,1)S(1)}, u32[]{:S(2)}) copy-start(bf16[2,2,64,1152]{3,2,1,0:T(8,128)(2,1)S(1)} %collective-permute-done.5.refs_1_) | copy-start | bytes 1769476
  55.7 2.0 %copy-start.11 = (bf16[2,2,64,1152]{3,2,1,0:T(8,128)(2,1)}, bf16[2,2,64,1152]{3,2,1,0:T(8,128)(2,1)S(1)}, u32[]{:S(2)}) copy-start(bf16[2,2,64,1152]{3,2,1,0:T(8,128)(2,1)S(1)} %collective-permute-done.7.refs_3_) | copy-start | bytes 1769476
  55.7 1.6 %collective-permute-start.16 = (bf16[1,144,864]{2,1,0:T(8,128)(2,1)S(1)}, bf16[1,144,864]{2,1,0:T(8,128)(2,1)S(1)}, u32[]{:S(2)}, u32[]{:S(2)}) collective-permute-start(bf16[1,144,864]{2,1,0:T(8,128)(2,1)S(1)} %collective-permute-done.11.refs_6_.refs_2_), channel_id=1, source_target_pairs={{0,8},{1,9},{2,10},{3,11},{4,12},{5,13},{6,14},{7,15},{8,0},{9,1},... | collective-permute-start | bytes 746504 | tf_op jit(solution)/shard_map/ppermute | solution.py:515
  55.7 1.9 %collective-permute-start.17 = (bf16[1,144,864]{2,1,0:T(8,128)(2,1)S(1)}, bf16[1,144,864]{2,1,0:T(8,128)(2,1)S(1)}, u32[]{:S(2)}, u32[]{:S(2)}) collective-permute-start(bf16[1,144,864]{2,1,0:T(8,128)(2,1)S(1)} %collective-permute-done.12.refs_7_.refs_3_), channel_id=1, source_target_pairs={{0,8},{1,9},{2,10},{3,11},{4,12},{5,13},{6,14},{7,15},{8,0},{9,1},... | collective-permute-start | bytes 746504 | tf_op jit(solution)/shard_map/ppermute | solution.py:515
  57.3 0.7 copy-start.24
  58.0 0.7 copy-start.25
  70.7 3.7 %collective-permute-start.18 = (f32[4,48,864]{2,1,0:T(8,128)}, f32[4,48,864]{2,1,0:T(8,128)S(1)}, u32[]{:S(2)}, u32[]{:S(2)}) collective-permute-start(f32[4,48,864]{2,1,0:T(8,128)} %get-tuple-element.88), channel_id=1, source_target_pairs={{0,8},{1,9},{2,10},{3,11},{4,12},{5,13},{6,14},{7,15},{8,0},{9,1},... | collective-permute-start | bytes 1990664 | tf_op jit(solution)/shard_map/ppermute | solution.py:557
  70.8 13.7 %collective-permute-start.20 = (bf16[2,64,1152]{2,1,0:T(8,128)(2,1)}, bf16[2,64,1152]{2,1,0:T(8,128)(2,1)S(1)}, u32[]{:S(2)}, u32[]{:S(2)}) collective-permute-start(bf16[2,64,1152]{2,1,0:T(8,128)(2,1)} %get-tuple-element.95), channel_id=1, source_target_pairs={{0,1},{1,0},{2,3},{3,2},{4,5},{5,4},{6,7},{7,6},{8,9},{9,8},{10,11... | collective-permute-start | bytes 884744 | tf_op jit(solution)/shard_map/ppermute | solution.py:455
  71.7 16.9 %collective-permute-start.21 = (bf16[2,64,1152]{2,1,0:T(8,128)(2,1)}, bf16[2,64,1152]{2,1,0:T(8,128)(2,1)S(1)}, u32[]{:S(2)}, u32[]{:S(2)}) collective-permute-start(bf16[2,64,1152]{2,1,0:T(8,128)(2,1)} %get-tuple-element.97), channel_id=1, source_target_pairs={{0,16},{1,17},{2,18},{3,19},{4,20},{5,21},{6,22},{7,23},{8,24},{9,... | collective-permute-start | bytes 884744 | tf_op jit(solution)/shard_map/ppermute | solution.py:455
  71.7 16.9 %collective-permute-start.22 = (bf16[2,64,1152]{2,1,0:T(8,128)(2,1)}, bf16[2,64,1152]{2,1,0:T(8,128)(2,1)S(1)}, u32[]{:S(2)}, u32[]{:S(2)}) collective-permute-start(bf16[2,64,1152]{2,1,0:T(8,128)(2,1)} %get-tuple-element.98), channel_id=1, source_target_pairs={{0,17},{1,16},{2,19},{3,18},{4,21},{5,20},{6,23},{7,22},{8,25},{9,... | collective-permute-start | bytes 884744 | tf_op jit(solution)/shard_map/ppermute | solution.py:455
  75.5 9.5 %collective-permute-start.19 = (f32[2,48,864]{2,1,0:T(8,128)S(1)}, f32[2,48,864]{2,1,0:T(8,128)S(1)}, u32[]{:S(2)}, u32[]{:S(2)}) collective-permute-start(f32[2,48,864]{2,1,0:T(8,128)S(1)} %get-tuple-element.94), channel_id=1, source_target_pairs={{0,2},{1,3},{2,0},{3,1},{4,6},{5,7},{6,4},{7,5},{8,10},{9,11},{10,... | collective-permute-start | bytes 995336 | tf_op jit(solution)/shard_map/ppermute | solution.py:563
  84.6 4.0 %copy-start.15 = (bf16[2,64,1152]{2,1,0:T(8,128)(2,1)}, bf16[2,64,1152]{2,1,0:T(8,128)(2,1)S(1)}, u32[]{:S(2)}) copy-start(bf16[2,64,1152]{2,1,0:T(8,128)(2,1)S(1)} %collective-permute-done.20.refs_3_) | copy-start | bytes 884740
  85.0 15.8 %collective-permute-start.25 = (bf16[2,64,1152]{2,1,0:T(8,128)(2,1)}, bf16[2,64,1152]{2,1,0:T(8,128)(2,1)S(1)}, u32[]{:S(2)}, u32[]{:S(2)}) collective-permute-start(bf16[2,64,1152]{2,1,0:T(8,128)(2,1)} %get-tuple-element.100), channel_id=1, source_target_pairs={{0,1},{1,0},{2,3},{3,2},{4,5},{5,4},{6,7},{7,6},{8,9},{9,8},{10,11... | collective-permute-start | bytes 884744 | tf_op jit(solution)/shard_map/ppermute | solution.py:455
  85.8 15.1 %collective-permute-start.26 = (bf16[2,64,1152]{2,1,0:T(8,128)(2,1)}, bf16[2,64,1152]{2,1,0:T(8,128)(2,1)S(1)}, u32[]{:S(2)}, u32[]{:S(2)}) collective-permute-start(bf16[2,64,1152]{2,1,0:T(8,128)(2,1)} %get-tuple-element.101), channel_id=1, source_target_pairs={{0,16},{1,17},{2,18},{3,19},{4,20},{5,21},{6,22},{7,23},{8,24},{9,... | collective-permute-start | bytes 884744 | tf_op jit(solution)/shard_map/ppermute | solution.py:455
  86.5 14.5 %collective-permute-start.27 = (bf16[2,64,1152]{2,1,0:T(8,128)(2,1)}, bf16[2,64,1152]{2,1,0:T(8,128)(2,1)S(1)}, u32[]{:S(2)}, u32[]{:S(2)}) collective-permute-start(bf16[2,64,1152]{2,1,0:T(8,128)(2,1)} %get-tuple-element.102), channel_id=1, source_target_pairs={{0,17},{1,16},{2,19},{3,18},{4,21},{5,20},{6,23},{7,22},{8,25},{9,... | collective-permute-start | bytes 884744 | tf_op jit(solution)/shard_map/ppermute | solution.py:455
  88.5 0.7 copy-start.16
  88.5 0.8 copy-start.17
  92.4 24.9 %collective-permute-start.23 = (bf16[64,1152]{1,0:T(8,128)(2,1)}, bf16[64,1152]{1,0:T(8,128)(2,1)S(1)}, u32[]{:S(2)}, u32[]{:S(2)}) collective-permute-start(bf16[64,1152]{1,0:T(8,128)(2,1)} %get-tuple-element.107), channel_id=1, source_target_pairs={{0,0},{1,1},{16,2},{17,3},{2,4},{3,5},{18,6},{19,7},{20,8},{21,9},... | collective-permute-start | bytes 442376 | tf_op jit(solution)/shard_map/ppermute | solution.py:442
  95.0 22.3 %collective-permute-start.24 = (bf16[64,1152]{1,0:T(8,128)(2,1)}, bf16[64,1152]{1,0:T(8,128)(2,1)S(1)}, u32[]{:S(2)}, u32[]{:S(2)}) collective-permute-start(bf16[64,1152]{1,0:T(8,128)(2,1)} %get-tuple-element.108), channel_id=1, source_target_pairs={{2,0},{3,1},{18,2},{19,3},{0,4},{1,5},{16,6},{17,7},{22,8},{23,9},... | collective-permute-start | bytes 442376 | tf_op jit(solution)/shard_map/ppermute | solution.py:442
  100.9 0.7 copy-start.18
  100.9 12.1 %collective-permute-start.30 = (f32[1,48,864]{2,1,0:T(8,128)S(1)}, f32[1,48,864]{2,1,0:T(8,128)S(1)}, u32[]{:S(2)}, u32[]{:S(2)}) collective-permute-start(f32[1,48,864]{2,1,0:T(8,128)S(1)} %slice.40), channel_id=1, source_target_pairs={{0,4},{1,5},{2,6},{3,7},{4,0},{5,1},{6,2},{7,3},{8,12},{9,13},{10,... | collective-permute-start | bytes 497672 | tf_op jit(solution)/shard_map/ppermute | solution.py:605
  101.0 0.7 copy-start.19
  101.7 0.7 copy-start.20
  105.8 11.5 %collective-permute-start.28 = (bf16[64,1152]{1,0:T(8,128)(2,1)}, bf16[64,1152]{1,0:T(8,128)(2,1)S(1)}, u32[]{:S(2)}, u32[]{:S(2)}) collective-permute-start(bf16[64,1152]{1,0:T(8,128)(2,1)} %get-tuple-element.113), channel_id=1, source_target_pairs={{0,0},{1,1},{16,2},{17,3},{2,4},{3,5},{18,6},{19,7},{20,8},{21,9},... | collective-permute-start | bytes 442376 | tf_op jit(solution)/shard_map/ppermute | solution.py:442
  110.1 10.1 %collective-permute-start.29 = (bf16[64,1152]{1,0:T(8,128)(2,1)}, bf16[64,1152]{1,0:T(8,128)(2,1)S(1)}, u32[]{:S(2)}, u32[]{:S(2)}) collective-permute-start(bf16[64,1152]{1,0:T(8,128)(2,1)} %get-tuple-element.114), channel_id=1, source_target_pairs={{2,0},{3,1},{18,2},{19,3},{0,4},{1,5},{16,6},{17,7},{22,8},{23,9},... | collective-permute-start | bytes 442376 | tf_op jit(solution)/shard_map/ppermute | solution.py:442
  113.0 12.8 %collective-permute-start.31 = (f32[48,864]{1,0:T(8,128)S(1)}, f32[48,864]{1,0:T(8,128)S(1)}, u32[]{:S(2)}, u32[]{:S(2)}) collective-permute-start(f32[48,864]{1,0:T(8,128)S(1)} %bitcast.28), channel_id=1, source_target_pairs={{0,0},{1,1},{2,8},{3,9},{4,16},{5,17},{6,24},{7,25},{8,4},{9,5},{1... | collective-permute-start | bytes 497672 | tf_op jit(solution)/shard_map/ppermute | solution.py:607

commit v22 on v21

--- a/solution.py
+++ b/solution.py
@@ -558,8 +558,7 @@
     projected = over_chips(projected)
 
     middle = groups // 2
-    cut, away = kept[:middle] + got[:middle], kept[middle:] + got[middle:]
-    grad_attn, cut, away = lax.optimization_barrier((grad_attn, cut, away))
+    grad_attn, away = lax.optimization_barrier((grad_attn, kept[middle:] + got[middle:]))
     first_away = lax.ppermute(away, AXES, lay.swap(kz=1))
 
     sums = call(
@@ -599,7 +598,8 @@
     )(pos, info, *own, *grad_hidden, mod_table)
     grad_x = from_plane(grad_parts)
 
-    cut, _ = lax.optimization_barrier((cut + first_away, out_parts))
+    cut = kept[:middle] + got[:middle] + first_away
+    cut, _ = lax.optimization_barrier((cut, out_parts))
     for bit in lay.bits(lay.nz)[1:]:
         middle = middle // 2
         cut = cut[:middle] + lax.ppermute(cut[middle:], AXES, lay.swap(kz=bit))

time: 128 us -> 128 us (level)
    unnamed x52 -> x54, local copies, waits for them, and re-layouts: 4.55 us -> 4.57 us
where the time goes in v22:
time: 128 us; the launch traced here: 126 us
  starting transfers between devices  51.2 us (40%)
  waiting for transfers between devices  32.8 us (26%)
  Pallas kernels  30.5 us (24%)
  other arithmetic  5.86 us (5%)
  local copies, waits for them, and re-layouts  4.67 us (4%)
    ppermute x4, starting transfers between devices, from_plane(): lax.ppermute(part, AXES, lay.from_plane(k))  15.4 us
    pallas_call x1, Pallas kernels, local(): call(functools.partial(forward_kernel, lay), 'forward', 14 * model * 1000...  12 us
    pallas_call x1, Pallas kernels, local(): call(functools.partial(backward_kernel, lay), 'backward', 10 * model * 10...  8.54 us
    ppermute x2, waiting for transfers between devices, local(): by_z[bit] = lax.ppermute(w_own, AXES, lay.swap(kz=bit))  7.58 us
    ppermute x1, waiting for transfers between devices, local(): by_z[k] = lax.ppermute(forwarded, AXES, lay.swap(kz=k & -k))  7.11 us
    ppermute x6, starting transfers between devices, over_chips(): got = [lax.ppermute(parts[k], AXES, chip_swap(k)) for k in range(1, chips)]  6.99 us
    ppermute x2, starting transfers between devices, local(): by_z[bit] = lax.ppermute(w_own, AXES, lay.swap(kz=bit))  5.4 us
    ppermute x1, waiting for transfers between devices, local(): wo_own = lax.ppermute(late_w_out, AXES, lay.rows_to_chip())  5.26 us
  transfers between devices with their start and end apart: 32, of which 12 were waited for; matrix products, arithmetic and copies ran while one was open for 4% of the time, Pallas kernels for 12%

profile of v22, /device:TPU:4, one launch (start us, length us, event | category | flops | bytes accessed | tf_op | source)
XLA Modules:
  0.0 126.1 jit_solution(2167682572636268523)
XLA Ops:
  0.6 0.6 pad_add_fusion.1.pos_ref
  1.2 3.3 %start.1 = (bf16[1,2,64,1152]{3,2,1,0:T(8,128)(2,1)}, bf16[1,2,64,1152]{3,2,1,0:T(8,128)(2,1)}, bf16[144,432]{1,0:T(8,128)(2,1)}, bf16[144,432]{1,0:T(8,128)(2,1)}) custom-call(s32[4]{0:T(128)} %pad_add_fusion.1.pos_ref, bf16[1,128,1152]{2,1,0:T(8,128)(2,1)} %x_ref.1, bf16[1,128,1152]{2,1,0:T(8,128)(2,1)} %g_ref.1, bf16[144,3456]{1,0:T(8,128)(2,1)} %w_ref.1), custom_call_target="tpu_custom_call" | custom-call | flops 1179648000 | bytes 2359296 | tf_op jit(solution)/shard_map/start/pallas_call | solution.py:471
  4.5 1.9 %collective-permute-start.2 = (bf16[1,2,64,1152]{3,2,1,0:T(8,128)(2,1)}, bf16[1,2,64,1152]{3,2,1,0:T(8,128)(2,1)S(1)}, u32[]{:S(2)}, u32[]{:S(2)}) collective-permute-start(bf16[1,2,64,1152]{3,2,1,0:T(8,128)(2,1)} %get-tuple-element.60), channel_id=1, source_target_pairs={{0,0},{1,1},{2,16},{3,17},{4,2},{5,3},{6,18},{7,19},{8,20},{9,21},... | collective-permute-start | bytes 884744 | tf_op jit(solution)/shard_map/ppermute | solution.py:481
  6.5 0.6 copy-done.8
  7.1 0.1 fusion.8
  7.2 2.2 %collective-permute-start = (s32[1,16]{1,0:T(1,128)S(1)}, s32[1,16]{1,0:T(1,128)S(1)}, u32[]{:S(2)}, u32[]{:S(2)}) collective-permute-start(s32[1,16]{1,0:T(1,128)S(1)} %fusion.8), channel_id=1, source_target_pairs={{0,8},{1,9},{2,10},{3,11},{4,12},{5,13},{6,14},{7,15},{8,0},{9,1},... | collective-permute-start | bytes 200 | tf_op jit(solution)/shard_map/ppermute | solution.py:459
  9.4 1.5 %collective-permute-start.8 = (bf16[144,432]{1,0:T(8,128)(2,1)}, bf16[144,432]{1,0:T(8,128)(2,1)S(1)}, u32[]{:S(2)}, u32[]{:S(2)}) collective-permute-start(bf16[144,432]{1,0:T(8,128)(2,1)} %get-tuple-element.66), channel_id=1, source_target_pairs={{0,1},{1,0},{2,3},{3,2},{4,5},{5,4},{6,7},{7,6},{8,9},{9,8},{10,11... | collective-permute-start | bytes 373256 | tf_op jit(solution)/shard_map/ppermute | solution.py:483
  10.8 2.5 %collective-permute-start.3 = (bf16[1,2,64,1152]{3,2,1,0:T(8,128)(2,1)}, bf16[1,2,64,1152]{3,2,1,0:T(8,128)(2,1)S(1)}, u32[]{:S(2)}, u32[]{:S(2)}) collective-permute-start(bf16[1,2,64,1152]{3,2,1,0:T(8,128)(2,1)} %get-tuple-element.61), channel_id=1, source_target_pairs={{0,2},{1,3},{2,18},{3,19},{4,0},{5,1},{6,16},{7,17},{8,22},{9,23},... | collective-permute-start | bytes 884744 | tf_op jit(solution)/shard_map/ppermute | solution.py:481
  13.4 1.5 %collective-permute-start.1 = (s32[2,16]{1,0:T(2,128)S(1)}, s32[2,16]{1,0:T(2,128)S(1)}, u32[]{:S(2)}, u32[]{:S(2)}) collective-permute-start(s32[2,16]{1,0:T(2,128)S(1)} %pad_add_fusion), channel_id=1, source_target_pairs={{0,16},{1,17},{2,18},{3,19},{4,20},{5,21},{6,22},{7,23},{8,24},{9,... | collective-permute-start | bytes 392 | tf_op jit(solution)/shard_map/ppermute | solution.py:461
  14.9 0.8 collective-permute-start.4
  15.7 1.4 %collective-permute-done.1 = s32[2,16]{1,0:T(2,128)S(1)} collective-permute-done((s32[2,16]{1,0:T(2,128)S(1)}, s32[2,16]{1,0:T(2,128)S(1)}, u32[]{:S(2)}, u32[]{:S(2)}) %collective-permute-start.1) | collective-permute-done | bytes 160 | tf_op jit(solution)/shard_map/ppermute | solution.py:461
  17.1 0.6 fusion.3.info_ref
  17.7 0.9 broadcast_select_fusion.3
  18.6 4.3 %collective-permute-start.9 = (bf16[144,1152]{1,0:T(8,128)(2,1)S(1)}, bf16[144,1152]{1,0:T(8,128)(2,1)S(1)}, u32[]{:S(2)}, u32[]{:S(2)}) collective-permute-start(bf16[144,1152]{1,0:T(8,128)(2,1)S(1)} %copy-done.13), channel_id=1, source_target_pairs={{0,0},{1,1},{2,18},{3,19},{4,8},{5,9},{6,26},{7,27},{8,4},{9,5},{1... | collective-permute-start | bytes 995336 | tf_op jit(solution)/shard_map/ppermute | solution.py:494
  23.0 1.7 %collective-permute-done.3.refs_1_ = bf16[1,2,64,1152]{3,2,1,0:T(8,128)(2,1)S(1)} collective-permute-done((bf16[1,2,64,1152]{3,2,1,0:T(8,128)(2,1)}, bf16[1,2,64,1152]{3,2,1,0:T(8,128)(2,1)S(1)}, u32[]{:S(2)}, u32[]{:S(2)}) %collective-permute-start.3) | collective-permute-done | bytes 294944 | tf_op jit(solution)/shard_map/ppermute | solution.py:481
  24.7 1.0 collective-permute-start.6
  25.7 0.1 maximum_bitcast_fusion.2.refs_4_.refs_0_
  25.9 1.1 collective-permute-start.5
  27.0 5.3 %collective-permute-done.9.refs_12_ = bf16[144,1152]{1,0:T(8,128)(2,1)S(1)} collective-permute-done((bf16[144,1152]{1,0:T(8,128)(2,1)S(1)}, bf16[144,1152]{1,0:T(8,128)(2,1)S(1)}, u32[]{:S(2)}, u32[]{:S(2)}) %collective-permute-start.9) | collective-permute-done | bytes 331808 | tf_op jit(solution)/shard_map/ppermute | solution.py:494
  32.3 0.2 collective-permute-start.11
  32.5 5.2 %collective-permute-start.10 = (bf16[1,144,864]{2,1,0:T(8,128)(2,1)S(1)}, bf16[1,144,864]{2,1,0:T(8,128)(2,1)S(1)}, u32[]{:S(2)}, u32[]{:S(2)}) collective-permute-start(bf16[1,144,864]{2,1,0:T(8,128)(2,1)S(1)} %maximum_bitcast_fusion.2.refs_4_.refs_0_), channel_id=1, source_target_pairs={{0,2},{1,3},{2,0},{3,1},{4,6},{5,7},{6,4},{7,5},{8,10},{9,11},{10,... | collective-permute-start | bytes 746504 | tf_op jit(solution)/shard_map/ppermute | solution.py:499
  37.8 0.9 collective-permute-start.7
  38.7 6.3 %collective-permute-done.11.refs_6_.refs_2_ = bf16[1,144,864]{2,1,0:T(8,128)(2,1)S(1)} collective-permute-done((bf16[1,144,864]{2,1,0:T(8,128)(2,1)S(1)}, bf16[1,144,864]{2,1,0:T(8,128)(2,1)S(1)}, u32[]{:S(2)}, u32[]{:S(2)}) %collective-permute-start.11) | collective-permute-done | bytes 248864 | tf_op jit(solution)/shard_map/ppermute | solution.py:499
  45.0 1.3 %collective-permute-done.10.refs_5_.refs_1_ = bf16[1,144,864]{2,1,0:T(8,128)(2,1)S(1)} collective-permute-done((bf16[1,144,864]{2,1,0:T(8,128)(2,1)S(1)}, bf16[1,144,864]{2,1,0:T(8,128)(2,1)S(1)}, u32[]{:S(2)}, u32[]{:S(2)}) %collective-permute-start.10) | collective-permute-done | bytes 248864 | tf_op jit(solution)/shard_map/ppermute | solution.py:499
  46.3 0.1 broadcast_select_fusion
  46.4 0.6 copy-done.7
  47.0 0.4 collective-permute-start.12
  47.4 1.1 collective-permute-done.14.refs_9_.refs_5_
  48.5 7.1 %collective-permute-done.12.refs_7_.refs_3_ = bf16[1,144,864]{2,1,0:T(8,128)(2,1)S(1)} collective-permute-done((bf16[1,144,864]{2,1,0:T(8,128)(2,1)S(1)}, bf16[1,144,864]{2,1,0:T(8,128)(2,1)S(1)}, u32[]{:S(2)}, u32[]{:S(2)}) %collective-permute-start.12) | collective-permute-done | bytes 248864 | tf_op jit(solution)/shard_map/ppermute | solution.py:503
  55.7 0.1 collective-permute-start.16
  55.7 0.5 collective-permute-start.17
  56.2 1.0 collective-permute-done.16.refs_10_.refs_6_
  57.3 0.4 collective-permute-done.17.refs_11_.refs_7_
  57.7 0.3 copy-done.25
  58.0 0.7 copy-done.26
  58.7 12.0 %forward.1 = (bf16[2,8,64,144]{3,2,1,0:T(8,128)(2,1)}, bf16[2,8,64,144]{3,2,1,0:T(8,128)(2,1)}, bf16[2,8,64,144]{3,2,1,0:T(8,128)(2,1)}, bf16[2,8,64,144]{3,2,1,...) custom-call(s32[4]{0:T(128)} %pad_add_fusion.1.pos_ref, ...), custom_call_target="tpu_custom_call" | custom-call | flops 8257536000 | bytes 2359296 | tf_op jit(solution)/shard_map/forward/pallas_call | solution.py:537
  70.7 0.1 collective-permute-start.18
  70.8 0.8 collective-permute-start.20
  71.7 2.7 %collective-permute-start.22 = (bf16[2,64,1152]{2,1,0:T(8,128)(2,1)}, bf16[2,64,1152]{2,1,0:T(8,128)(2,1)S(1)}, u32[]{:S(2)}, u32[]{:S(2)}) collective-permute-start(bf16[2,64,1152]{2,1,0:T(8,128)(2,1)} %get-tuple-element.97), channel_id=1, source_target_pairs={{0,17},{1,16},{2,19},{3,18},{4,21},{5,20},{6,23},{7,22},{8,25},{9,... | collective-permute-start | bytes 884744 | tf_op jit(solution)/shard_map/ppermute | solution.py:455
  74.3 1.0 slice_add_fusion.1
  75.4 0.4 collective-permute-start.19
  75.8 8.5 %backward.1 = (f32[2,64,1152]{2,1,0:T(8,128)}, bf16[2,64,1152]{2,1,0:T(8,128)(2,1)}, bf16[2,64,1152]{2,1,0:T(8,128)(2,1)}, bf16[2,64,1152]{2,1,0:T(8,128)(2,1)}) custom-call(s32[4]{0:T(128)} %pad_add_fusion.1.pos_ref, s32[16]{0:T(128)} %fusion.3.info_ref, bf16[1,144,864]{2,1,0:T(8,128)(2,1)} %copy-done, bf16[1,144,864]{2,1,0:T(8,128)(2,1)} %copy-done.7, ...), custom_call_target="tpu_custom_call" | custom-call | flops 5898240000 | bytes 2359296 | tf_op jit(solution)/shard_map/backward/pallas_call | solution.py:564
  84.3 0.6 collective-permute-done.19
  84.9 0.8 collective-permute-start.25
  85.7 0.5 collective-permute-start.26
  86.3 2.1 %collective-permute-start.27 = (bf16[2,64,1152]{2,1,0:T(8,128)(2,1)}, bf16[2,64,1152]{2,1,0:T(8,128)(2,1)S(1)}, u32[]{:S(2)}, u32[]{:S(2)}) collective-permute-start(bf16[2,64,1152]{2,1,0:T(8,128)(2,1)} %get-tuple-element.101), channel_id=1, source_target_pairs={{0,17},{1,16},{2,19},{3,18},{4,21},{5,20},{6,23},{7,22},{8,25},{9,... | collective-permute-start | bytes 884744 | tf_op jit(solution)/shard_map/ppermute | solution.py:455
  88.4 0.7 copy-done.17
  89.1 0.1 copy-done.18
  89.2 3.2 %output.1 = (bf16[64,1152]{1,0:T(8,128)(2,1)}, bf16[64,1152]{1,0:T(8,128)(2,1)}) custom-call(s32[4]{0:T(128)} %pad_add_fusion.1.pos_ref, s32[16]{0:T(128)} %fusion.3.info_ref, bf16[1,2,64,1152]{3,2,1,0:T(8,128)(2,1)} %copy-done.4, bf16[1,2,64,1152]{3,2,1,0:T(8,128)(2,1)} %copy-done.5, f32[2,64,1152]{2,1,0:T(8,128)} %get-tuple-element.102.refs_2_, ...), custom_call_target="tpu_custom_call" | custom-call | flops 11796480000 | bytes 2359296 | tf_op jit(solution)/shard_map/output/pallas_call | solution.py:578
  92.4 2.5 %collective-permute-start.23 = (bf16[64,1152]{1,0:T(8,128)(2,1)}, bf16[64,1152]{1,0:T(8,128)(2,1)S(1)}, u32[]{:S(2)}, u32[]{:S(2)}) collective-permute-start(bf16[64,1152]{1,0:T(8,128)(2,1)} %get-tuple-element.106), channel_id=1, source_target_pairs={{0,0},{1,1},{16,2},{17,3},{2,4},{3,5},{18,6},{19,7},{20,8},{21,9},... | collective-permute-start | bytes 442376 | tf_op jit(solution)/shard_map/ppermute | solution.py:442
  95.0 5.8 %collective-permute-start.24 = (bf16[64,1152]{1,0:T(8,128)(2,1)}, bf16[64,1152]{1,0:T(8,128)(2,1)S(1)}, u32[]{:S(2)}, u32[]{:S(2)}) collective-permute-start(bf16[64,1152]{1,0:T(8,128)(2,1)} %get-tuple-element.107), channel_id=1, source_target_pairs={{2,0},{3,1},{18,2},{19,3},{0,4},{1,5},{16,6},{17,7},{22,8},{23,9},... | collective-permute-start | bytes 442376 | tf_op jit(solution)/shard_map/ppermute | solution.py:442
  101.0 0.6 copy-done.19
  101.6 0.1 copy-done.20
  101.7 0.7 copy-done.21
  102.4 3.4 %input_grad.1 = (bf16[64,1152]{1,0:T(8,128)(2,1)}, bf16[64,1152]{1,0:T(8,128)(2,1)}) custom-call(s32[4]{0:T(128)} %pad_add_fusion.1.pos_ref, s32[16]{0:T(128)} %fusion.3.info_ref, bf16[1,2,64,1152]{3,2,1,0:T(8,128)(2,1)} %copy-done.4, bf16[1,2,64,1152]{3,2,1,0:T(8,128)(2,1)} %copy-done.5, f32[2,64,1152]{2,1,0:T(8,128)} %get-tuple-element.108.refs_2_, ...), custom_call_target="tpu_custom_call" | custom-call | flops 1769472000 | bytes 2359296 | tf_op jit(solution)/shard_map/input_grad/pallas_call | solution.py:590
  105.8 4.2 %collective-permute-start.28 = (bf16[64,1152]{1,0:T(8,128)(2,1)}, bf16[64,1152]{1,0:T(8,128)(2,1)S(1)}, u32[]{:S(2)}, u32[]{:S(2)}) collective-permute-start(bf16[64,1152]{1,0:T(8,128)(2,1)} %get-tuple-element.112), channel_id=1, source_target_pairs={{0,0},{1,1},{16,2},{17,3},{2,4},{3,5},{18,6},{19,7},{20,8},{21,9},... | collective-permute-start | bytes 442376 | tf_op jit(solution)/shard_map/ppermute | solution.py:442
  110.0 2.9 %collective-permute-start.29 = (bf16[64,1152]{1,0:T(8,128)(2,1)}, bf16[64,1152]{1,0:T(8,128)(2,1)S(1)}, u32[]{:S(2)}, u32[]{:S(2)}) collective-permute-start(bf16[64,1152]{1,0:T(8,128)(2,1)} %get-tuple-element.113), channel_id=1, source_target_pairs={{2,0},{3,1},{18,2},{19,3},{0,4},{1,5},{16,6},{17,7},{22,8},{23,9},... | collective-permute-start | bytes 442376 | tf_op jit(solution)/shard_map/ppermute | solution.py:442
  113.0 4.1 %collective-permute-start.31 = (f32[48,864]{1,0:T(8,128)S(1)}, f32[48,864]{1,0:T(8,128)S(1)}, u32[]{:S(2)}, u32[]{:S(2)}) collective-permute-start(f32[48,864]{1,0:T(8,128)S(1)} %bitcast.28), channel_id=1, source_target_pairs={{0,0},{1,1},{2,8},{3,9},{4,16},{5,17},{6,24},{7,25},{8,4},{9,5},{1... | collective-permute-start | bytes 497672 | tf_op jit(solution)/shard_map/ppermute | solution.py:607
  117.1 2.9 %collective-permute-done.29 = bf16[64,1152]{1,0:T(8,128)(2,1)S(1)} collective-permute-done((bf16[64,1152]{1,0:T(8,128)(2,1)}, bf16[64,1152]{1,0:T(8,128)(2,1)S(1)}, u32[]{:S(2)}, u32[]{:S(2)}) %collective-permute-start.29) | collective-permute-done | bytes 147488 | tf_op jit(solution)/shard_map/ppermute | solution.py:442
  120.1 0.7 maximum_bitcast_fusion.1
  120.8 0.7 maximum_bitcast_fusion
  121.6 3.7 %collective-permute-done.31 = f32[48,864]{1,0:T(8,128)S(1)} collective-permute-done((f32[48,864]{1,0:T(8,128)S(1)}, f32[48,864]{1,0:T(8,128)S(1)}, u32[]{:S(2)}, u32[]{:S(2)}) %collective-permute-start.31) | collective-permute-done | bytes 165920 | tf_op jit(solution)/shard_map/ppermute | solution.py:607
  125.3 0.1 fusion.7
  125.4 0.7 maximum_multiply_fusion
  (77 shorter events, 0.5 us)
Async XLA Ops:
  4.5 10.4 %collective-permute-start.2 = (bf16[1,2,64,1152]{3,2,1,0:T(8,128)(2,1)}, bf16[1,2,64,1152]{3,2,1,0:T(8,128)(2,1)S(1)}, u32[]{:S(2)}, u32[]{:S(2)}) collective-permute-start(bf16[1,2,64,1152]{3,2,1,0:T(8,128)(2,1)} %get-tuple-element.60), channel_id=1, source_target_pairs={{0,0},{1,1},{2,16},{3,17},{4,2},{5,3},{6,18},{7,19},{8,20},{9,21},... | collective-permute-start | bytes 884744 | tf_op jit(solution)/shard_map/ppermute | solution.py:481
  6.4 0.7 copy-start.8
  6.5 0.7 copy-start.9
  6.5 0.7 copy-start.10
  7.2 6.2 %collective-permute-start = (s32[1,16]{1,0:T(1,128)S(1)}, s32[1,16]{1,0:T(1,128)S(1)}, u32[]{:S(2)}, u32[]{:S(2)}) collective-permute-start(s32[1,16]{1,0:T(1,128)S(1)} %fusion.8), channel_id=1, source_target_pairs={{0,8},{1,9},{2,10},{3,11},{4,12},{5,13},{6,14},{7,15},{8,0},{9,1},... | collective-permute-start | bytes 200 | tf_op jit(solution)/shard_map/ppermute | solution.py:459
  9.4 8.3 %collective-permute-start.8 = (bf16[144,432]{1,0:T(8,128)(2,1)}, bf16[144,432]{1,0:T(8,128)(2,1)S(1)}, u32[]{:S(2)}, u32[]{:S(2)}) collective-permute-start(bf16[144,432]{1,0:T(8,128)(2,1)} %get-tuple-element.66), channel_id=1, source_target_pairs={{0,1},{1,0},{2,3},{3,2},{4,5},{5,4},{6,7},{7,6},{8,9},{9,8},{10,11... | collective-permute-start | bytes 373256 | tf_op jit(solution)/shard_map/ppermute | solution.py:483
  10.8 13.9 %collective-permute-start.3 = (bf16[1,2,64,1152]{3,2,1,0:T(8,128)(2,1)}, bf16[1,2,64,1152]{3,2,1,0:T(8,128)(2,1)S(1)}, u32[]{:S(2)}, u32[]{:S(2)}) collective-permute-start(bf16[1,2,64,1152]{3,2,1,0:T(8,128)(2,1)} %get-tuple-element.61), channel_id=1, source_target_pairs={{0,2},{1,3},{2,18},{3,19},{4,0},{5,1},{6,16},{7,17},{8,22},{9,23},... | collective-permute-start | bytes 884744 | tf_op jit(solution)/shard_map/ppermute | solution.py:481
  13.4 5.3 %copy-start.13 = (bf16[144,1152]{1,0:T(8,128)(2,1)S(1)}, bf16[144,1152]{1,0:T(8,128)(2,1)}, u32[]{:S(2)}) copy-start(bf16[144,1152]{1,0:T(8,128)(2,1)} %param.15) | copy-start | bytes 995332
  13.4 3.6 %collective-permute-start.1 = (s32[2,16]{1,0:T(2,128)S(1)}, s32[2,16]{1,0:T(2,128)S(1)}, u32[]{:S(2)}, u32[]{:S(2)}) collective-permute-start(s32[2,16]{1,0:T(2,128)S(1)} %pad_add_fusion), channel_id=1, source_target_pairs={{0,16},{1,17},{2,18},{3,19},{4,20},{5,21},{6,22},{7,23},{8,24},{9,... | collective-permute-start | bytes 392 | tf_op jit(solution)/shard_map/ppermute | solution.py:461
  14.9 10.9 %copy-start.4 = (bf16[1,2,64,1152]{3,2,1,0:T(8,128)(2,1)}, bf16[1,2,64,1152]{3,2,1,0:T(8,128)(2,1)S(1)}, u32[]{:S(2)}) copy-start(bf16[1,2,64,1152]{3,2,1,0:T(8,128)(2,1)S(1)} %collective-permute-done.2.refs_0_) | copy-start | bytes 884740
  14.9 9.8 %collective-permute-start.4 = (bf16[1,2,64,1152]{3,2,1,0:T(8,128)(2,1)S(1)}, bf16[1,2,64,1152]{3,2,1,0:T(8,128)(2,1)S(1)}, u32[]{:S(2)}, u32[]{:S(2)}) collective-permute-start(bf16[1,2,64,1152]{3,2,1,0:T(8,128)(2,1)S(1)} %collective-permute-done.2.refs_0_), channel_id=1, source_target_pairs={{0,1},{1,0},{2,3},{3,2},{4,5},{5,4},{6,7},{7,6},{8,9},{9,8},{10,11... | collective-permute-start | bytes 884744 | tf_op jit(solution)/shard_map/ppermute | solution.py:491
  18.6 13.6 %collective-permute-start.9 = (bf16[144,1152]{1,0:T(8,128)(2,1)S(1)}, bf16[144,1152]{1,0:T(8,128)(2,1)S(1)}, u32[]{:S(2)}, u32[]{:S(2)}) collective-permute-start(bf16[144,1152]{1,0:T(8,128)(2,1)S(1)} %copy-done.13), channel_id=1, source_target_pairs={{0,0},{1,1},{2,18},{3,19},{4,8},{5,9},{6,26},{7,27},{8,4},{9,5},{1... | collective-permute-start | bytes 995336 | tf_op jit(solution)/shard_map/ppermute | solution.py:494
  24.7 13.0 %copy-start.5 = (bf16[1,2,64,1152]{3,2,1,0:T(8,128)(2,1)}, bf16[1,2,64,1152]{3,2,1,0:T(8,128)(2,1)S(1)}, u32[]{:S(2)}) copy-start(bf16[1,2,64,1152]{3,2,1,0:T(8,128)(2,1)S(1)} %collective-permute-done.3.refs_1_) | copy-start | bytes 884740
  24.7 13.0 %collective-permute-start.6 = (bf16[1,2,64,1152]{3,2,1,0:T(8,128)(2,1)S(1)}, bf16[1,2,64,1152]{3,2,1,0:T(8,128)(2,1)S(1)}, u32[]{:S(2)}, u32[]{:S(2)}) collective-permute-start(bf16[1,2,64,1152]{3,2,1,0:T(8,128)(2,1)S(1)} %collective-permute-done.3.refs_1_), channel_id=1, source_target_pairs={{0,16},{1,17},{2,18},{3,19},{4,20},{5,21},{6,22},{7,23},{8,24},{9,... | collective-permute-start | bytes 884744 | tf_op jit(solution)/shard_map/ppermute | solution.py:449
  25.9 20.4 %copy-start = (bf16[1,144,864]{2,1,0:T(8,128)(2,1)}, bf16[1,144,864]{2,1,0:T(8,128)(2,1)S(1)}, u32[]{:S(2)}) copy-start(bf16[1,144,864]{2,1,0:T(8,128)(2,1)S(1)} %maximum_bitcast_fusion.2.refs_4_.refs_0_) | copy-start | bytes 746500
  25.9 12.7 %copy-start.2 = (bf16[2,2,64,1152]{3,2,1,0:T(8,128)(2,1)}, bf16[2,2,64,1152]{3,2,1,0:T(8,128)(2,1)S(1)}, u32[]{:S(2)}) copy-start(bf16[2,2,64,1152]{3,2,1,0:T(8,128)(2,1)S(1)} %pad_maximum_fusion.refs_0_) | copy-start | bytes 1769476
  25.9 29.7 %collective-permute-start.5 = (bf16[2,2,64,1152]{3,2,1,0:T(8,128)(2,1)S(1)}, bf16[2,2,64,1152]{3,2,1,0:T(8,128)(2,1)S(1)}, u32[]{:S(2)}, u32[]{:S(2)}) collective-permute-start(bf16[2,2,64,1152]{3,2,1,0:T(8,128)(2,1)S(1)} %pad_maximum_fusion.refs_0_), channel_id=1, source_target_pairs={{0,16},{1,17},{2,18},{3,19},{4,20},{5,21},{6,22},{7,23},{8,24},{9,... | collective-permute-start | bytes 1769480 | tf_op jit(solution)/shard_map/ppermute | solution.py:452
  32.3 5.4 %copy-start.14 = (bf16[144,1152]{1,0:T(8,128)(2,1)}, bf16[144,1152]{1,0:T(8,128)(2,1)S(1)}, u32[]{:S(2)}) copy-start(bf16[144,1152]{1,0:T(8,128)(2,1)S(1)} %collective-permute-done.9.refs_12_) | copy-start | bytes 995332
  32.3 12.7 %collective-permute-start.11 = (bf16[1,144,864]{2,1,0:T(8,128)(2,1)S(1)}, bf16[1,144,864]{2,1,0:T(8,128)(2,1)S(1)}, u32[]{:S(2)}, u32[]{:S(2)}) collective-permute-start(bf16[1,144,864]{2,1,0:T(8,128)(2,1)S(1)} %maximum_bitcast_fusion.2.refs_4_.refs_0_), channel_id=1, source_target_pairs={{0,4},{1,5},{2,6},{3,7},{4,0},{5,1},{6,2},{7,3},{8,12},{9,13},{10,... | collective-permute-start | bytes 746504 | tf_op jit(solution)/shard_map/ppermute | solution.py:499
  32.5 13.8 %collective-permute-start.10 = (bf16[1,144,864]{2,1,0:T(8,128)(2,1)S(1)}, bf16[1,144,864]{2,1,0:T(8,128)(2,1)S(1)}, u32[]{:S(2)}, u32[]{:S(2)}) collective-permute-start(bf16[1,144,864]{2,1,0:T(8,128)(2,1)S(1)} %maximum_bitcast_fusion.2.refs_4_.refs_0_), channel_id=1, source_target_pairs={{0,2},{1,3},{2,0},{3,1},{4,6},{5,7},{6,4},{7,5},{8,10},{9,11},{10,... | collective-permute-start | bytes 746504 | tf_op jit(solution)/shard_map/ppermute | solution.py:499
  37.8 8.6 %copy-start.3 = (bf16[2,2,64,1152]{3,2,1,0:T(8,128)(2,1)}, bf16[2,2,64,1152]{3,2,1,0:T(8,128)(2,1)S(1)}, u32[]{:S(2)}) copy-start(bf16[2,2,64,1152]{3,2,1,0:T(8,128)(2,1)S(1)} %pad_maximum_fusion.1.refs_2_) | copy-start | bytes 1769476
  37.8 17.9 %collective-permute-start.7 = (bf16[2,2,64,1152]{3,2,1,0:T(8,128)(2,1)S(1)}, bf16[2,2,64,1152]{3,2,1,0:T(8,128)(2,1)S(1)}, u32[]{:S(2)}, u32[]{:S(2)}) collective-permute-start(bf16[2,2,64,1152]{3,2,1,0:T(8,128)(2,1)S(1)} %pad_maximum_fusion.1.refs_2_), channel_id=1, source_target_pairs={{0,1},{1,0},{2,3},{3,2},{4,5},{5,4},{6,7},{7,6},{8,9},{9,8},{10,11... | collective-permute-start | bytes 1769480 | tf_op jit(solution)/shard_map/ppermute | solution.py:452
  38.7 8.3 %collective-permute-start.13 = (bf16[1,144,864]{2,1,0:T(8,128)(2,1)S(1)}, bf16[1,144,864]{2,1,0:T(8,128)(2,1)S(1)}, u32[]{:S(2)}, u32[]{:S(2)}) collective-permute-start(bf16[1,144,864]{2,1,0:T(8,128)(2,1)S(1)} %maximum_bitcast_fusion.2.refs_4_.refs_0_), channel_id=1, source_target_pairs={{0,8},{1,9},{2,10},{3,11},{4,12},{5,13},{6,14},{7,15},{8,0},{9,1},... | collective-permute-start | bytes 746504 | tf_op jit(solution)/shard_map/ppermute | solution.py:511
  45.0 10.6 %copy-start.6 = (bf16[1,144,864]{2,1,0:T(8,128)(2,1)}, bf16[1,144,864]{2,1,0:T(8,128)(2,1)S(1)}, u32[]{:S(2)}) copy-start(bf16[1,144,864]{2,1,0:T(8,128)(2,1)S(1)} %collective-permute-done.11.refs_6_.refs_2_) | copy-start | bytes 746500
  45.0 2.4 %collective-permute-start.15 = (bf16[144,1152]{1,0:T(8,128)(2,1)}, bf16[144,1152]{1,0:T(8,128)(2,1)S(1)}, u32[]{:S(2)}, u32[]{:S(2)}) collective-permute-start(bf16[144,1152]{1,0:T(8,128)(2,1)} %copy-done.14), channel_id=1, source_target_pairs={{0,8},{1,9},{2,10},{3,11},{4,12},{5,13},{6,14},{7,15},{8,0},{9,1},... | collective-permute-start | bytes 995336 | tf_op jit(solution)/shard_map/ppermute | solution.py:495
  46.3 0.7 copy-start.7
  47.0 1.5 %collective-permute-start.14 = (bf16[1,144,864]{2,1,0:T(8,128)(2,1)S(1)}, bf16[1,144,864]{2,1,0:T(8,128)(2,1)S(1)}, u32[]{:S(2)}, u32[]{:S(2)}) collective-permute-start(bf16[1,144,864]{2,1,0:T(8,128)(2,1)S(1)} %get-tuple-element.123), channel_id=1, source_target_pairs={{0,8},{1,9},{2,10},{3,11},{4,12},{5,13},{6,14},{7,15},{8,0},{9,1},... | collective-permute-start | bytes 746504 | tf_op jit(solution)/shard_map/ppermute | solution.py:511
  47.0 10.6 %copy-start.22 = (bf16[1,144,864]{2,1,0:T(8,128)(2,1)}, bf16[1,144,864]{2,1,0:T(8,128)(2,1)S(1)}, u32[]{:S(2)}) copy-start(bf16[1,144,864]{2,1,0:T(8,128)(2,1)S(1)} %collective-permute-done.13.refs_8_.refs_4_) | copy-start | bytes 746500
  47.0 8.6 %collective-permute-start.12 = (bf16[1,144,864]{2,1,0:T(8,128)(2,1)S(1)}, bf16[1,144,864]{2,1,0:T(8,128)(2,1)S(1)}, u32[]{:S(2)}, u32[]{:S(2)}) collective-permute-start(bf16[1,144,864]{2,1,0:T(8,128)(2,1)S(1)} %get-tuple-element.124), channel_id=1, source_target_pairs={{0,2},{1,3},{2,0},{3,1},{4,6},{5,7},{6,4},{7,5},{8,10},{9,11},{10,... | collective-permute-start | bytes 746504 | tf_op jit(solution)/shard_map/ppermute | solution.py:503
  47.4 10.2 %copy-start.15 = (bf16[144,1152]{1,0:T(8,128)(2,1)}, bf16[144,1152]{1,0:T(8,128)(2,1)S(1)}, u32[]{:S(2)}) copy-start(bf16[144,1152]{1,0:T(8,128)(2,1)S(1)} %collective-permute-done.15.refs_13_) | copy-start | bytes 995332
  48.5 9.1 %copy-start.23 = (bf16[1,144,864]{2,1,0:T(8,128)(2,1)}, bf16[1,144,864]{2,1,0:T(8,128)(2,1)S(1)}, u32[]{:S(2)}) copy-start(bf16[1,144,864]{2,1,0:T(8,128)(2,1)S(1)} %collective-permute-done.14.refs_9_.refs_5_) | copy-start | bytes 746500
  55.6 2.0 %copy-start.24 = (bf16[1,144,864]{2,1,0:T(8,128)(2,1)}, bf16[1,144,864]{2,1,0:T(8,128)(2,1)S(1)}, u32[]{:S(2)}) copy-start(bf16[1,144,864]{2,1,0:T(8,128)(2,1)S(1)} %collective-permute-done.12.refs_7_.refs_3_) | copy-start | bytes 746500
  55.6 2.0 %copy-start.11 = (bf16[2,2,64,1152]{3,2,1,0:T(8,128)(2,1)}, bf16[2,2,64,1152]{3,2,1,0:T(8,128)(2,1)S(1)}, u32[]{:S(2)}) copy-start(bf16[2,2,64,1152]{3,2,1,0:T(8,128)(2,1)S(1)} %collective-permute-done.5.refs_1_) | copy-start | bytes 1769476
  55.7 2.0 %copy-start.12 = (bf16[2,2,64,1152]{3,2,1,0:T(8,128)(2,1)}, bf16[2,2,64,1152]{3,2,1,0:T(8,128)(2,1)S(1)}, u32[]{:S(2)}) copy-start(bf16[2,2,64,1152]{3,2,1,0:T(8,128)(2,1)S(1)} %collective-permute-done.7.refs_3_) | copy-start | bytes 1769476
  55.7 1.6 %collective-permute-start.16 = (bf16[1,144,864]{2,1,0:T(8,128)(2,1)S(1)}, bf16[1,144,864]{2,1,0:T(8,128)(2,1)S(1)}, u32[]{:S(2)}, u32[]{:S(2)}) collective-permute-start(bf16[1,144,864]{2,1,0:T(8,128)(2,1)S(1)} %collective-permute-done.11.refs_6_.refs_2_), channel_id=1, source_target_pairs={{0,8},{1,9},{2,10},{3,11},{4,12},{5,13},{6,14},{7,15},{8,0},{9,1},... | collective-permute-start | bytes 746504 | tf_op jit(solution)/shard_map/ppermute | solution.py:515
  55.7 1.9 %collective-permute-start.17 = (bf16[1,144,864]{2,1,0:T(8,128)(2,1)S(1)}, bf16[1,144,864]{2,1,0:T(8,128)(2,1)S(1)}, u32[]{:S(2)}, u32[]{:S(2)}) collective-permute-start(bf16[1,144,864]{2,1,0:T(8,128)(2,1)S(1)} %collective-permute-done.12.refs_7_.refs_3_), channel_id=1, source_target_pairs={{0,8},{1,9},{2,10},{3,11},{4,12},{5,13},{6,14},{7,15},{8,0},{9,1},... | collective-permute-start | bytes 746504 | tf_op jit(solution)/shard_map/ppermute | solution.py:515
  57.3 0.7 copy-start.25
  58.0 0.7 copy-start.26
  70.7 3.6 %collective-permute-start.18 = (f32[4,48,864]{2,1,0:T(8,128)}, f32[4,48,864]{2,1,0:T(8,128)S(1)}, u32[]{:S(2)}, u32[]{:S(2)}) collective-permute-start(f32[4,48,864]{2,1,0:T(8,128)} %get-tuple-element.87), channel_id=1, source_target_pairs={{0,8},{1,9},{2,10},{3,11},{4,12},{5,13},{6,14},{7,15},{8,0},{9,1},... | collective-permute-start | bytes 1990664 | tf_op jit(solution)/shard_map/ppermute | solution.py:557
  70.8 13.5 %collective-permute-start.20 = (bf16[2,64,1152]{2,1,0:T(8,128)(2,1)}, bf16[2,64,1152]{2,1,0:T(8,128)(2,1)S(1)}, u32[]{:S(2)}, u32[]{:S(2)}) collective-permute-start(bf16[2,64,1152]{2,1,0:T(8,128)(2,1)} %get-tuple-element.94), channel_id=1, source_target_pairs={{0,1},{1,0},{2,3},{3,2},{4,5},{5,4},{6,7},{7,6},{8,9},{9,8},{10,11... | collective-permute-start | bytes 884744 | tf_op jit(solution)/shard_map/ppermute | solution.py:455
  71.7 16.7 %collective-permute-start.21 = (bf16[2,64,1152]{2,1,0:T(8,128)(2,1)}, bf16[2,64,1152]{2,1,0:T(8,128)(2,1)S(1)}, u32[]{:S(2)}, u32[]{:S(2)}) collective-permute-start(bf16[2,64,1152]{2,1,0:T(8,128)(2,1)} %get-tuple-element.96), channel_id=1, source_target_pairs={{0,16},{1,17},{2,18},{3,19},{4,20},{5,21},{6,22},{7,23},{8,24},{9,... | collective-permute-start | bytes 884744 | tf_op jit(solution)/shard_map/ppermute | solution.py:455
  71.7 16.7 %collective-permute-start.22 = (bf16[2,64,1152]{2,1,0:T(8,128)(2,1)}, bf16[2,64,1152]{2,1,0:T(8,128)(2,1)S(1)}, u32[]{:S(2)}, u32[]{:S(2)}) collective-permute-start(bf16[2,64,1152]{2,1,0:T(8,128)(2,1)} %get-tuple-element.97), channel_id=1, source_target_pairs={{0,17},{1,16},{2,19},{3,18},{4,21},{5,20},{6,23},{7,22},{8,25},{9,... | collective-permute-start | bytes 884744 | tf_op jit(solution)/shard_map/ppermute | solution.py:455
  75.4 9.6 %collective-permute-start.19 = (f32[2,48,864]{2,1,0:T(8,128)S(1)}, f32[2,48,864]{2,1,0:T(8,128)S(1)}, u32[]{:S(2)}, u32[]{:S(2)}) collective-permute-start(f32[2,48,864]{2,1,0:T(8,128)S(1)} %slice_add_fusion.1), channel_id=1, source_target_pairs={{0,2},{1,3},{2,0},{3,1},{4,6},{5,7},{6,4},{7,5},{8,10},{9,11},{10,... | collective-permute-start | bytes 995336 | tf_op jit(solution)/shard_map/ppermute | solution.py:562
  84.3 4.1 %copy-start.16 = (bf16[2,64,1152]{2,1,0:T(8,128)(2,1)}, bf16[2,64,1152]{2,1,0:T(8,128)(2,1)S(1)}, u32[]{:S(2)}) copy-start(bf16[2,64,1152]{2,1,0:T(8,128)(2,1)S(1)} %collective-permute-done.20.refs_3_) | copy-start | bytes 884740
  84.9 16.0 %collective-permute-start.25 = (bf16[2,64,1152]{2,1,0:T(8,128)(2,1)}, bf16[2,64,1152]{2,1,0:T(8,128)(2,1)S(1)}, u32[]{:S(2)}, u32[]{:S(2)}) collective-permute-start(bf16[2,64,1152]{2,1,0:T(8,128)(2,1)} %get-tuple-element.99), channel_id=1, source_target_pairs={{0,1},{1,0},{2,3},{3,2},{4,5},{5,4},{6,7},{7,6},{8,9},{9,8},{10,11... | collective-permute-start | bytes 884744 | tf_op jit(solution)/shard_map/ppermute | solution.py:455
  85.7 15.3 %collective-permute-start.26 = (bf16[2,64,1152]{2,1,0:T(8,128)(2,1)}, bf16[2,64,1152]{2,1,0:T(8,128)(2,1)S(1)}, u32[]{:S(2)}, u32[]{:S(2)}) collective-permute-start(bf16[2,64,1152]{2,1,0:T(8,128)(2,1)} %get-tuple-element.100), channel_id=1, source_target_pairs={{0,16},{1,17},{2,18},{3,19},{4,20},{5,21},{6,22},{7,23},{8,24},{9,... | collective-permute-start | bytes 884744 | tf_op jit(solution)/shard_map/ppermute | solution.py:455
  86.3 14.7 %collective-permute-start.27 = (bf16[2,64,1152]{2,1,0:T(8,128)(2,1)}, bf16[2,64,1152]{2,1,0:T(8,128)(2,1)S(1)}, u32[]{:S(2)}, u32[]{:S(2)}) collective-permute-start(bf16[2,64,1152]{2,1,0:T(8,128)(2,1)} %get-tuple-element.101), channel_id=1, source_target_pairs={{0,17},{1,16},{2,19},{3,18},{4,21},{5,20},{6,23},{7,22},{8,25},{9,... | collective-permute-start | bytes 884744 | tf_op jit(solution)/shard_map/ppermute | solution.py:455
  88.4 0.7 copy-start.17
  88.4 0.8 copy-start.18
  89.2 11.6 %copy-start.1 = (f32[4,48,864]{2,1,0:T(8,128)S(1)}, f32[4,48,864]{2,1,0:T(8,128)}, u32[]{:S(2)}) copy-start(f32[4,48,864]{2,1,0:T(8,128)} %get-tuple-element.86) | copy-start | bytes 1990660
  92.4 24.6 %collective-permute-start.23 = (bf16[64,1152]{1,0:T(8,128)(2,1)}, bf16[64,1152]{1,0:T(8,128)(2,1)S(1)}, u32[]{:S(2)}, u32[]{:S(2)}) collective-permute-start(bf16[64,1152]{1,0:T(8,128)(2,1)} %get-tuple-element.106), channel_id=1, source_target_pairs={{0,0},{1,1},{16,2},{17,3},{2,4},{3,5},{18,6},{19,7},{20,8},{21,9},... | collective-permute-start | bytes 442376 | tf_op jit(solution)/shard_map/ppermute | solution.py:442
  95.0 22.1 %collective-permute-start.24 = (bf16[64,1152]{1,0:T(8,128)(2,1)}, bf16[64,1152]{1,0:T(8,128)(2,1)S(1)}, u32[]{:S(2)}, u32[]{:S(2)}) collective-permute-start(bf16[64,1152]{1,0:T(8,128)(2,1)} %get-tuple-element.107), channel_id=1, source_target_pairs={{2,0},{3,1},{18,2},{19,3},{0,4},{1,5},{16,6},{17,7},{22,8},{23,9},... | collective-permute-start | bytes 442376 | tf_op jit(solution)/shard_map/ppermute | solution.py:442
  100.9 0.7 copy-start.19
  100.9 12.1 %collective-permute-start.30 = (f32[1,48,864]{2,1,0:T(8,128)S(1)}, f32[1,48,864]{2,1,0:T(8,128)S(1)}, u32[]{:S(2)}, u32[]{:S(2)}) collective-permute-start(f32[1,48,864]{2,1,0:T(8,128)S(1)} %slice.40), channel_id=1, source_target_pairs={{0,4},{1,5},{2,6},{3,7},{4,0},{5,1},{6,2},{7,3},{8,12},{9,13},{10,... | collective-permute-start | bytes 497672 | tf_op jit(solution)/shard_map/ppermute | solution.py:605
  101.0 0.7 copy-start.20
  101.7 0.7 copy-start.21
  105.8 11.3 %collective-permute-start.28 = (bf16[64,1152]{1,0:T(8,128)(2,1)}, bf16[64,1152]{1,0:T(8,128)(2,1)S(1)}, u32[]{:S(2)}, u32[]{:S(2)}) collective-permute-start(bf16[64,1152]{1,0:T(8,128)(2,1)} %get-tuple-element.112), channel_id=1, source_target_pairs={{0,0},{1,1},{16,2},{17,3},{2,4},{3,5},{18,6},{19,7},{20,8},{21,9},... | collective-permute-start | bytes 442376 | tf_op jit(solution)/shard_map/ppermute | solution.py:442
  110.0 10.0 %collective-permute-start.29 = (bf16[64,1152]{1,0:T(8,128)(2,1)}, bf16[64,1152]{1,0:T(8,128)(2,1)S(1)}, u32[]{:S(2)}, u32[]{:S(2)}) collective-permute-start(bf16[64,1152]{1,0:T(8,128)(2,1)} %get-tuple-element.113), channel_id=1, source_target_pairs={{2,0},{3,1},{18,2},{19,3},{0,4},{1,5},{16,6},{17,7},{22,8},{23,9},... | collective-permute-start | bytes 442376 | tf_op jit(solution)/shard_map/ppermute | solution.py:442
  113.0 12.3 %collective-permute-start.31 = (f32[48,864]{1,0:T(8,128)S(1)}, f32[48,864]{1,0:T(8,128)S(1)}, u32[]{:S(2)}, u32[]{:S(2)}) collective-permute-start(f32[48,864]{1,0:T(8,128)S(1)} %bitcast.28), channel_id=1, source_target_pairs={{0,0},{1,1},{2,8},{3,9},{4,16},{5,17},{6,24},{7,25},{8,4},{9,5},{1... | collective-permute-start | bytes 497672 | tf_op jit(solution)/shard_map/ppermute | solution.py:607

commit v23 on v22

--- a/solution.py
+++ b/solution.py
@@ -455,17 +455,6 @@
         got = [lax.ppermute(parts[k], AXES, chip_swap(k)) for k in range(1, chips)]
         return [parts[0]] + got
 
-    info = jnp.concatenate([clip_ids[0], clip_patches[0], clip_step[0]])[None]
-    by_core = jnp.concatenate([info, lax.ppermute(info, AXES, lay.swap(kc=1))], axis=0)
-    info = [by_core] + [
-        lax.ppermute(by_core, AXES, lay.swap(ky=ky)) for ky in range(1, lay.ny)
-    ]
-    group_y, group_c, _ = lay.unit(c, z)
-    info = sum(
-        jnp.where((y ^ ky == group_y) & (c ^ kc == group_c), info[ky][kc], 0)
-        for ky in range(lay.ny)
-        for kc in range(nc)
-    )
     pos = jnp.stack([y, c, z, x]).astype(jnp.int32)
     pair_shape = (1, 2, half, model)
     outputs = call(
@@ -479,6 +468,18 @@
     )(pos, frames_x, grad_y, w_qkv)
     pairs, picked = outputs[:nc], outputs[nc:]
     own = [lax.ppermute(pair, AXES, lay.to_plane(k)) for k, pair in enumerate(pairs)]
+    clip_ids, own[0] = lax.optimization_barrier((clip_ids, own[0]))
+    info = jnp.concatenate([clip_ids[0], clip_patches[0], clip_step[0]])[None]
+    by_core = jnp.concatenate([info, lax.ppermute(info, AXES, lay.swap(kc=1))], axis=0)
+    info = [by_core] + [
+        lax.ppermute(by_core, AXES, lay.swap(ky=ky)) for ky in range(1, lay.ny)
+    ]
+    group_y, group_c, _ = lay.unit(c, z)
+    info = sum(
+        jnp.where((y ^ ky == group_y) & (c ^ kc == group_c), info[ky][kc], 0)
+        for ky in range(lay.ny)
+        for kc in range(nc)
+    )
     by_x = [picked[0]] + [
         lax.ppermute(picked[kx], AXES, lay.swap(kx=kx)) for kx in range(1, nx)
     ]

time: 128 us -> 131 us (1.023)
  starting transfers between devices: 51.2 us -> 58.7 us
  waiting for transfers between devices: 32.8 us -> 28.6 us
    ppermute x4, starting transfers between devices: 15.4 us -> 19.2 us  [from_plane(): lax.ppermute(part, AXES, lay.from_plane(k))]
    ppermute x1, starting transfers between devices: 4.32 us -> 7.71 us  [local(): wo_own = lax.ppermute(late_w_out, AXES, lay.rows_to_chip())]
    ppermute x1, waiting for transfers between devices: 5.26 us -> 2.67 us  [local(): wo_own = lax.ppermute(late_w_out, AXES, lay.rows_to_chip())]
    ppermute x2, starting transfers between devices: 4.4 us -> 6.6 us  [local(): lax.ppermute(pair, AXES, lay.to_plane(k))]
    ppermute x1, starting transfers between devices: 2.16 us -> 0.01 us  [local(): lax.ppermute(info, AXES, lay.swap(kc=1))]
    ppermute x2, waiting for transfers between devices: 7.58 us -> 5.74 us  [local(): by_z[bit] = lax.ppermute(w_own, AXES, lay.swap(kz=bit))]
    ppermute x1, starting transfers between devices: 0.43 us -> 2.2 us  [local(): first_away = lax.ppermute(away, AXES, lay.swap(kz=1))]
    ppermute x1, starting transfers between devices: 4.06 us -> 2.58 us  [local(): grad_w = lax.ppermute(cut[0], AXES, lay.to_owner())]
  transfers between devices with their start and end apart: 32 -> 32, of which waited for: 12 -> 10; matrix products, arithmetic and copies ran while one was open for 4% -> 4% of each run, Pallas kernels for 12% -> 12%
where the time goes in v23:
time: 131 us; the launch traced here: 130 us
  starting transfers between devices  58.7 us (45%)
  Pallas kernels  30.5 us (23%)
  waiting for transfers between devices  28.6 us (22%)
  other arithmetic  5.85 us (4%)
  local copies, waits for them, and re-layouts  4.79 us (4%)
    ppermute x4, starting transfers between devices, from_plane(): lax.ppermute(part, AXES, lay.from_plane(k))  19.2 us
    pallas_call x1, Pallas kernels, local(): call(functools.partial(forward_kernel, lay), 'forward', 14 * model * 1000...  12 us
    pallas_call x1, Pallas kernels, local(): call(functools.partial(backward_kernel, lay), 'backward', 10 * model * 10...  8.55 us
    ppermute x1, starting transfers between devices, local(): wo_own = lax.ppermute(late_w_out, AXES, lay.rows_to_chip())  7.71 us
    ppermute x6, starting transfers between devices, over_chips(): got = [lax.ppermute(parts[k], AXES, chip_swap(k)) for k in range(1, chips)]  7.06 us
    ppermute x1, waiting for transfers between devices, local(): by_z[k] = lax.ppermute(forwarded, AXES, lay.swap(kz=k & -k))  7.04 us
    ppermute x2, starting transfers between devices, local(): lax.ppermute(pair, AXES, lay.to_plane(k))  6.6 us
    ppermute x2, waiting for transfers between devices, local(): by_z[bit] = lax.ppermute(w_own, AXES, lay.swap(kz=bit))  5.74 us
  transfers between devices with their start and end apart: 32, of which 10 were waited for; matrix products, arithmetic and copies ran while one was open for 4% of the time, Pallas kernels for 12%

profile of v23, /device:TPU:4, one launch (start us, length us, event | category | flops | bytes accessed | tf_op | source)
XLA Modules:
  0.0 129.6 jit_solution(594685784493131652)
XLA Ops:
  0.6 0.6 pad_add_fusion.1.pos_ref
  1.2 3.3 %start.1 = (bf16[1,2,64,1152]{3,2,1,0:T(8,128)(2,1)}, bf16[1,2,64,1152]{3,2,1,0:T(8,128)(2,1)}, bf16[144,432]{1,0:T(8,128)(2,1)}, bf16[144,432]{1,0:T(8,128)(2,1)}) custom-call(s32[4]{0:T(128)} %pad_add_fusion.1.pos_ref, bf16[1,128,1152]{2,1,0:T(8,128)(2,1)} %x_ref.1, bf16[1,128,1152]{2,1,0:T(8,128)(2,1)} %g_ref.1, bf16[144,3456]{1,0:T(8,128)(2,1)} %w_ref.1), custom_call_target="tpu_custom_call" | custom-call | flops 1179648000 | bytes 2359296 | tf_op jit(solution)/shard_map/start/pallas_call | solution.py:460
  4.5 1.5 %collective-permute-start.8 = (bf16[144,432]{1,0:T(8,128)(2,1)}, bf16[144,432]{1,0:T(8,128)(2,1)S(1)}, u32[]{:S(2)}, u32[]{:S(2)}) collective-permute-start(bf16[144,432]{1,0:T(8,128)(2,1)} %get-tuple-element.70), channel_id=1, source_target_pairs={{0,1},{1,0},{2,3},{3,2},{4,5},{5,4},{6,7},{7,6},{8,9},{9,8},{10,11... | collective-permute-start | bytes 373256 | tf_op jit(solution)/shard_map/ppermute | solution.py:484
  6.0 1.9 %collective-permute-start = (bf16[1,2,64,1152]{3,2,1,0:T(8,128)(2,1)}, bf16[1,2,64,1152]{3,2,1,0:T(8,128)(2,1)S(1)}, u32[]{:S(2)}, u32[]{:S(2)}) collective-permute-start(bf16[1,2,64,1152]{3,2,1,0:T(8,128)(2,1)} %get-tuple-element.62), channel_id=1, source_target_pairs={{0,0},{1,1},{2,16},{3,17},{4,2},{5,3},{6,18},{7,19},{8,20},{9,21},... | collective-permute-start | bytes 884744 | tf_op jit(solution)/shard_map/ppermute | solution.py:470
  7.9 4.7 %collective-permute-start.3 = (bf16[1,2,64,1152]{3,2,1,0:T(8,128)(2,1)}, bf16[1,2,64,1152]{3,2,1,0:T(8,128)(2,1)S(1)}, u32[]{:S(2)}, u32[]{:S(2)}) collective-permute-start(bf16[1,2,64,1152]{3,2,1,0:T(8,128)(2,1)} %get-tuple-element.65), channel_id=1, source_target_pairs={{0,2},{1,3},{2,18},{3,19},{4,0},{5,1},{6,16},{7,17},{8,22},{9,23},... | collective-permute-start | bytes 884744 | tf_op jit(solution)/shard_map/ppermute | solution.py:470
  12.7 0.9 broadcast_select_fusion.3
  13.7 2.1 %collective-permute-done.refs_0_ = bf16[1,2,64,1152]{3,2,1,0:T(8,128)(2,1)S(1)} collective-permute-done((bf16[1,2,64,1152]{3,2,1,0:T(8,128)(2,1)}, bf16[1,2,64,1152]{3,2,1,0:T(8,128)(2,1)S(1)}, u32[]{:S(2)}, u32[]{:S(2)}) %collective-permute-start) | collective-permute-done | bytes 294944 | tf_op jit(solution)/shard_map/ppermute | solution.py:470
  15.7 0.5 collective-permute-start.4
  16.3 0.1 maximum_bitcast_fusion.2.refs_4_.refs_0_
  16.4 0.6 copy-done.8
  17.1 0.1 copy-done.9
  17.2 0.1 fusion.8
  17.3 7.7 %collective-permute-start.9 = (bf16[144,1152]{1,0:T(8,128)(2,1)S(1)}, bf16[144,1152]{1,0:T(8,128)(2,1)S(1)}, u32[]{:S(2)}, u32[]{:S(2)}) collective-permute-start(bf16[144,1152]{1,0:T(8,128)(2,1)S(1)} %copy-done.13), channel_id=1, source_target_pairs={{0,0},{1,1},{2,18},{3,19},{4,8},{5,9},{6,26},{7,27},{8,4},{9,5},{1... | collective-permute-start | bytes 995336 | tf_op jit(solution)/shard_map/ppermute | solution.py:495
  25.0 0.1 collective-permute-start.2
  25.1 2.1 %collective-permute-start.6 = (bf16[1,2,64,1152]{3,2,1,0:T(8,128)(2,1)S(1)}, bf16[1,2,64,1152]{3,2,1,0:T(8,128)(2,1)S(1)}, u32[]{:S(2)}, u32[]{:S(2)}) collective-permute-start(bf16[1,2,64,1152]{3,2,1,0:T(8,128)(2,1)S(1)} %collective-permute-done.3.refs_1_), channel_id=1, source_target_pairs={{0,16},{1,17},{2,18},{3,19},{4,20},{5,21},{6,22},{7,23},{8,24},{9,... | collective-permute-start | bytes 884744 | tf_op jit(solution)/shard_map/ppermute | solution.py:449
  27.2 1.5 %collective-permute-done.2 = s32[2,16]{1,0:T(2,128)S(1)} collective-permute-done((s32[2,16]{1,0:T(2,128)S(1)}, s32[2,16]{1,0:T(2,128)S(1)}, u32[]{:S(2)}, u32[]{:S(2)}) %collective-permute-start.2) | collective-permute-done | bytes 160 | tf_op jit(solution)/shard_map/ppermute | solution.py:475
  28.7 0.6 fusion.3.info_ref
  29.3 0.1 collective-permute-start.5
  29.4 2.7 %collective-permute-done.9.refs_12_ = bf16[144,1152]{1,0:T(8,128)(2,1)S(1)} collective-permute-done((bf16[144,1152]{1,0:T(8,128)(2,1)S(1)}, bf16[144,1152]{1,0:T(8,128)(2,1)S(1)}, u32[]{:S(2)}, u32[]{:S(2)}) %collective-permute-start.9) | collective-permute-done | bytes 331808 | tf_op jit(solution)/shard_map/ppermute | solution.py:495
  32.1 1.7 %collective-permute-start.11 = (bf16[1,144,864]{2,1,0:T(8,128)(2,1)S(1)}, bf16[1,144,864]{2,1,0:T(8,128)(2,1)S(1)}, u32[]{:S(2)}, u32[]{:S(2)}) collective-permute-start(bf16[1,144,864]{2,1,0:T(8,128)(2,1)S(1)} %maximum_bitcast_fusion.2.refs_4_.refs_0_), channel_id=1, source_target_pairs={{0,4},{1,5},{2,6},{3,7},{4,0},{5,1},{6,2},{7,3},{8,12},{9,13},{10,... | collective-permute-start | bytes 746504 | tf_op jit(solution)/shard_map/ppermute | solution.py:500
  33.8 3.2 %collective-permute-start.10 = (bf16[1,144,864]{2,1,0:T(8,128)(2,1)S(1)}, bf16[1,144,864]{2,1,0:T(8,128)(2,1)S(1)}, u32[]{:S(2)}, u32[]{:S(2)}) collective-permute-start(bf16[1,144,864]{2,1,0:T(8,128)(2,1)S(1)} %maximum_bitcast_fusion.2.refs_4_.refs_0_), channel_id=1, source_target_pairs={{0,2},{1,3},{2,0},{3,1},{4,6},{5,7},{6,4},{7,5},{8,10},{9,11},{10,... | collective-permute-start | bytes 746504 | tf_op jit(solution)/shard_map/ppermute | solution.py:500
  37.1 2.2 %collective-permute-start.7 = (bf16[2,2,64,1152]{3,2,1,0:T(8,128)(2,1)S(1)}, bf16[2,2,64,1152]{3,2,1,0:T(8,128)(2,1)S(1)}, u32[]{:S(2)}, u32[]{:S(2)}) collective-permute-start(bf16[2,2,64,1152]{3,2,1,0:T(8,128)(2,1)S(1)} %pad_maximum_fusion.1.refs_2_), channel_id=1, source_target_pairs={{0,1},{1,0},{2,3},{3,2},{4,5},{5,4},{6,7},{7,6},{8,9},{9,8},{10,11... | collective-permute-start | bytes 1769480 | tf_op jit(solution)/shard_map/ppermute | solution.py:452
  39.3 5.7 %collective-permute-done.11.refs_6_.refs_2_ = bf16[1,144,864]{2,1,0:T(8,128)(2,1)S(1)} collective-permute-done((bf16[1,144,864]{2,1,0:T(8,128)(2,1)S(1)}, bf16[1,144,864]{2,1,0:T(8,128)(2,1)S(1)}, u32[]{:S(2)}, u32[]{:S(2)}) %collective-permute-start.11) | collective-permute-done | bytes 248864 | tf_op jit(solution)/shard_map/ppermute | solution.py:500
  45.1 0.1 broadcast_select_fusion
  45.2 0.6 copy-done.7
  45.8 0.5 collective-permute-start.14
  46.3 0.7 collective-permute-start.12
  46.9 0.5 collective-permute-done.14.refs_9_.refs_5_
  47.4 7.0 %collective-permute-done.12.refs_7_.refs_3_ = bf16[1,144,864]{2,1,0:T(8,128)(2,1)S(1)} collective-permute-done((bf16[1,144,864]{2,1,0:T(8,128)(2,1)S(1)}, bf16[1,144,864]{2,1,0:T(8,128)(2,1)S(1)}, u32[]{:S(2)}, u32[]{:S(2)}) %collective-permute-start.12) | collective-permute-done | bytes 248864 | tf_op jit(solution)/shard_map/ppermute | solution.py:504
  54.5 0.1 collective-permute-start.16
  54.6 0.5 collective-permute-start.17
  55.1 1.0 collective-permute-done.16.refs_10_.refs_6_
  56.1 0.4 collective-permute-done.17.refs_11_.refs_7_
  56.5 0.3 copy-done.25
  56.8 0.7 copy-done.26
  57.5 12.0 %forward.1 = (bf16[2,8,64,144]{3,2,1,0:T(8,128)(2,1)}, bf16[2,8,64,144]{3,2,1,0:T(8,128)(2,1)}, bf16[2,8,64,144]{3,2,1,0:T(8,128)(2,1)}, bf16[2,8,64,144]{3,2,1,...) custom-call(s32[4]{0:T(128)} %pad_add_fusion.1.pos_ref, ...), custom_call_target="tpu_custom_call" | custom-call | flops 8257536000 | bytes 2359296 | tf_op jit(solution)/shard_map/forward/pallas_call | solution.py:538
  69.5 0.1 collective-permute-start.18
  69.7 1.4 %collective-permute-start.20 = (bf16[2,64,1152]{2,1,0:T(8,128)(2,1)}, bf16[2,64,1152]{2,1,0:T(8,128)(2,1)S(1)}, u32[]{:S(2)}, u32[]{:S(2)}) collective-permute-start(bf16[2,64,1152]{2,1,0:T(8,128)(2,1)} %get-tuple-element.98), channel_id=1, source_target_pairs={{0,1},{1,0},{2,3},{3,2},{4,5},{5,4},{6,7},{7,6},{8,9},{9,8},{10,11... | collective-permute-start | bytes 884744 | tf_op jit(solution)/shard_map/ppermute | solution.py:455
  71.1 2.0 %collective-permute-start.21 = (bf16[2,64,1152]{2,1,0:T(8,128)(2,1)}, bf16[2,64,1152]{2,1,0:T(8,128)(2,1)S(1)}, u32[]{:S(2)}, u32[]{:S(2)}) collective-permute-start(bf16[2,64,1152]{2,1,0:T(8,128)(2,1)} %get-tuple-element.100), channel_id=1, source_target_pairs={{0,16},{1,17},{2,18},{3,19},{4,20},{5,21},{6,22},{7,23},{8,24},{9,... | collective-permute-start | bytes 884744 | tf_op jit(solution)/shard_map/ppermute | solution.py:455
  73.1 0.1 collective-permute-start.22
  73.2 1.0 slice_add_fusion.1
  74.2 2.2 %collective-permute-start.19 = (f32[2,48,864]{2,1,0:T(8,128)S(1)}, f32[2,48,864]{2,1,0:T(8,128)S(1)}, u32[]{:S(2)}, u32[]{:S(2)}) collective-permute-start(f32[2,48,864]{2,1,0:T(8,128)S(1)} %slice_add_fusion.1), channel_id=1, source_target_pairs={{0,2},{1,3},{2,0},{3,1},{4,6},{5,7},{6,4},{7,5},{8,10},{9,11},{10,... | collective-permute-start | bytes 995336 | tf_op jit(solution)/shard_map/ppermute | solution.py:563
  76.4 8.5 %backward.1 = (f32[2,64,1152]{2,1,0:T(8,128)}, bf16[2,64,1152]{2,1,0:T(8,128)(2,1)}, bf16[2,64,1152]{2,1,0:T(8,128)(2,1)}, bf16[2,64,1152]{2,1,0:T(8,128)(2,1)}) custom-call(s32[4]{0:T(128)} %pad_add_fusion.1.pos_ref, s32[16]{0:T(128)} %fusion.3.info_ref, bf16[1,144,864]{2,1,0:T(8,128)(2,1)} %copy-done, bf16[1,144,864]{2,1,0:T(8,128)(2,1)} %copy-done.7, ...), custom_call_target="tpu_custom_call" | custom-call | flops 5898240000 | bytes 2359296 | tf_op jit(solution)/shard_map/backward/pallas_call | solution.py:565
  85.0 1.5 %collective-permute-start.25 = (bf16[2,64,1152]{2,1,0:T(8,128)(2,1)}, bf16[2,64,1152]{2,1,0:T(8,128)(2,1)S(1)}, u32[]{:S(2)}, u32[]{:S(2)}) collective-permute-start(bf16[2,64,1152]{2,1,0:T(8,128)(2,1)} %get-tuple-element.103), channel_id=1, source_target_pairs={{0,1},{1,0},{2,3},{3,2},{4,5},{5,4},{6,7},{7,6},{8,9},{9,8},{10,11... | collective-permute-start | bytes 884744 | tf_op jit(solution)/shard_map/ppermute | solution.py:455
  86.5 2.0 %collective-permute-start.26 = (bf16[2,64,1152]{2,1,0:T(8,128)(2,1)}, bf16[2,64,1152]{2,1,0:T(8,128)(2,1)S(1)}, u32[]{:S(2)}, u32[]{:S(2)}) collective-permute-start(bf16[2,64,1152]{2,1,0:T(8,128)(2,1)} %get-tuple-element.104), channel_id=1, source_target_pairs={{0,16},{1,17},{2,18},{3,19},{4,20},{5,21},{6,22},{7,23},{8,24},{9,... | collective-permute-start | bytes 884744 | tf_op jit(solution)/shard_map/ppermute | solution.py:455
  88.6 0.7 copy-done.17
  89.2 0.1 copy-done.18
  89.4 3.2 %output.1 = (bf16[64,1152]{1,0:T(8,128)(2,1)}, bf16[64,1152]{1,0:T(8,128)(2,1)}) custom-call(s32[4]{0:T(128)} %pad_add_fusion.1.pos_ref, s32[16]{0:T(128)} %fusion.3.info_ref, bf16[1,2,64,1152]{3,2,1,0:T(8,128)(2,1)} %copy-done.4, bf16[1,2,64,1152]{3,2,1,0:T(8,128)(2,1)} %copy-done.5, f32[2,64,1152]{2,1,0:T(8,128)} %get-tuple-element.106.refs_2_, ...), custom_call_target="tpu_custom_call" | custom-call | flops 11796480000 | bytes 2359296 | tf_op jit(solution)/shard_map/output/pallas_call | solution.py:579
  92.6 4.2 %collective-permute-start.23 = (bf16[64,1152]{1,0:T(8,128)(2,1)}, bf16[64,1152]{1,0:T(8,128)(2,1)S(1)}, u32[]{:S(2)}, u32[]{:S(2)}) collective-permute-start(bf16[64,1152]{1,0:T(8,128)(2,1)} %get-tuple-element.110), channel_id=1, source_target_pairs={{0,0},{1,1},{16,2},{17,3},{2,4},{3,5},{18,6},{19,7},{20,8},{21,9},... | collective-permute-start | bytes 442376 | tf_op jit(solution)/shard_map/ppermute | solution.py:442
  96.7 5.6 %collective-permute-start.24 = (bf16[64,1152]{1,0:T(8,128)(2,1)}, bf16[64,1152]{1,0:T(8,128)(2,1)S(1)}, u32[]{:S(2)}, u32[]{:S(2)}) collective-permute-start(bf16[64,1152]{1,0:T(8,128)(2,1)} %get-tuple-element.111), channel_id=1, source_target_pairs={{2,0},{3,1},{18,2},{19,3},{0,4},{1,5},{16,6},{17,7},{22,8},{23,9},... | collective-permute-start | bytes 442376 | tf_op jit(solution)/shard_map/ppermute | solution.py:442
  102.5 0.1 collective-permute-start.30
  102.6 0.6 copy-done.19
  103.2 0.1 copy-done.20
  103.3 0.7 copy-done.21
  104.0 3.4 %input_grad.1 = (bf16[64,1152]{1,0:T(8,128)(2,1)}, bf16[64,1152]{1,0:T(8,128)(2,1)}) custom-call(s32[4]{0:T(128)} %pad_add_fusion.1.pos_ref, s32[16]{0:T(128)} %fusion.3.info_ref, bf16[1,2,64,1152]{3,2,1,0:T(8,128)(2,1)} %copy-done.4, bf16[1,2,64,1152]{3,2,1,0:T(8,128)(2,1)} %copy-done.5, f32[2,64,1152]{2,1,0:T(8,128)} %get-tuple-element.112.refs_2_, ...), custom_call_target="tpu_custom_call" | custom-call | flops 1769472000 | bytes 2359296 | tf_op jit(solution)/shard_map/input_grad/pallas_call | solution.py:591
  107.4 4.4 %collective-permute-start.28 = (bf16[64,1152]{1,0:T(8,128)(2,1)}, bf16[64,1152]{1,0:T(8,128)(2,1)S(1)}, u32[]{:S(2)}, u32[]{:S(2)}) collective-permute-start(bf16[64,1152]{1,0:T(8,128)(2,1)} %get-tuple-element.116), channel_id=1, source_target_pairs={{0,0},{1,1},{16,2},{17,3},{2,4},{3,5},{18,6},{19,7},{20,8},{21,9},... | collective-permute-start | bytes 442376 | tf_op jit(solution)/shard_map/ppermute | solution.py:442
  111.8 5.1 %collective-permute-start.29 = (bf16[64,1152]{1,0:T(8,128)(2,1)}, bf16[64,1152]{1,0:T(8,128)(2,1)S(1)}, u32[]{:S(2)}, u32[]{:S(2)}) collective-permute-start(bf16[64,1152]{1,0:T(8,128)(2,1)} %get-tuple-element.117), channel_id=1, source_target_pairs={{2,0},{3,1},{18,2},{19,3},{0,4},{1,5},{16,6},{17,7},{22,8},{23,9},... | collective-permute-start | bytes 442376 | tf_op jit(solution)/shard_map/ppermute | solution.py:442
  117.0 2.6 %collective-permute-start.31 = (f32[48,864]{1,0:T(8,128)S(1)}, f32[48,864]{1,0:T(8,128)S(1)}, u32[]{:S(2)}, u32[]{:S(2)}) collective-permute-start(f32[48,864]{1,0:T(8,128)S(1)} %bitcast.28), channel_id=1, source_target_pairs={{0,0},{1,1},{2,8},{3,9},{4,16},{5,17},{6,24},{7,25},{8,4},{9,5},{1... | collective-permute-start | bytes 497672 | tf_op jit(solution)/shard_map/ppermute | solution.py:608
  119.6 2.9 %collective-permute-done.29 = bf16[64,1152]{1,0:T(8,128)(2,1)S(1)} collective-permute-done((bf16[64,1152]{1,0:T(8,128)(2,1)}, bf16[64,1152]{1,0:T(8,128)(2,1)S(1)}, u32[]{:S(2)}, u32[]{:S(2)}) %collective-permute-start.29) | collective-permute-done | bytes 147488 | tf_op jit(solution)/shard_map/ppermute | solution.py:442
  122.5 0.7 maximum_bitcast_fusion.1
  123.3 0.7 maximum_bitcast_fusion
  124.0 4.8 %collective-permute-done.31 = f32[48,864]{1,0:T(8,128)S(1)} collective-permute-done((f32[48,864]{1,0:T(8,128)S(1)}, f32[48,864]{1,0:T(8,128)S(1)}, u32[]{:S(2)}, u32[]{:S(2)}) %collective-permute-start.31) | collective-permute-done | bytes 165920 | tf_op jit(solution)/shard_map/ppermute | solution.py:608
  128.8 0.1 fusion.7
  128.9 0.7 maximum_multiply_fusion
  (77 shorter events, 0.5 us)
Async XLA Ops:
  4.5 8.2 %collective-permute-start.8 = (bf16[144,432]{1,0:T(8,128)(2,1)}, bf16[144,432]{1,0:T(8,128)(2,1)S(1)}, u32[]{:S(2)}, u32[]{:S(2)}) collective-permute-start(bf16[144,432]{1,0:T(8,128)(2,1)} %get-tuple-element.70), channel_id=1, source_target_pairs={{0,1},{1,0},{2,3},{3,2},{4,5},{5,4},{6,7},{7,6},{8,9},{9,8},{10,11... | collective-permute-start | bytes 373256 | tf_op jit(solution)/shard_map/ppermute | solution.py:484
  6.0 9.7 %collective-permute-start = (bf16[1,2,64,1152]{3,2,1,0:T(8,128)(2,1)}, bf16[1,2,64,1152]{3,2,1,0:T(8,128)(2,1)S(1)}, u32[]{:S(2)}, u32[]{:S(2)}) collective-permute-start(bf16[1,2,64,1152]{3,2,1,0:T(8,128)(2,1)} %get-tuple-element.62), channel_id=1, source_target_pairs={{0,0},{1,1},{2,16},{3,17},{4,2},{5,3},{6,18},{7,19},{8,20},{9,21},... | collective-permute-start | bytes 884744 | tf_op jit(solution)/shard_map/ppermute | solution.py:470
  7.9 17.2 %collective-permute-start.3 = (bf16[1,2,64,1152]{3,2,1,0:T(8,128)(2,1)}, bf16[1,2,64,1152]{3,2,1,0:T(8,128)(2,1)S(1)}, u32[]{:S(2)}, u32[]{:S(2)}) collective-permute-start(bf16[1,2,64,1152]{3,2,1,0:T(8,128)(2,1)} %get-tuple-element.65), channel_id=1, source_target_pairs={{0,2},{1,3},{2,18},{3,19},{4,0},{5,1},{6,16},{7,17},{8,22},{9,23},... | collective-permute-start | bytes 884744 | tf_op jit(solution)/shard_map/ppermute | solution.py:470
  13.6 3.6 %copy-start.13 = (bf16[144,1152]{1,0:T(8,128)(2,1)S(1)}, bf16[144,1152]{1,0:T(8,128)(2,1)}, u32[]{:S(2)}) copy-start(bf16[144,1152]{1,0:T(8,128)(2,1)} %param.15) | copy-start | bytes 995332
  15.7 13.6 %copy-start.4 = (bf16[1,2,64,1152]{3,2,1,0:T(8,128)(2,1)}, bf16[1,2,64,1152]{3,2,1,0:T(8,128)(2,1)S(1)}, u32[]{:S(2)}) copy-start(bf16[1,2,64,1152]{3,2,1,0:T(8,128)(2,1)S(1)} %collective-permute-done.refs_0_) | copy-start | bytes 884740
  15.7 9.4 %collective-permute-start.4 = (bf16[1,2,64,1152]{3,2,1,0:T(8,128)(2,1)S(1)}, bf16[1,2,64,1152]{3,2,1,0:T(8,128)(2,1)S(1)}, u32[]{:S(2)}, u32[]{:S(2)}) collective-permute-start(bf16[1,2,64,1152]{3,2,1,0:T(8,128)(2,1)S(1)} %collective-permute-done.refs_0_), channel_id=1, source_target_pairs={{0,1},{1,0},{2,3},{3,2},{4,5},{5,4},{6,7},{7,6},{8,9},{9,8},{10,11... | collective-permute-start | bytes 884744 | tf_op jit(solution)/shard_map/ppermute | solution.py:492
  16.4 28.7 %copy-start = (bf16[1,144,864]{2,1,0:T(8,128)(2,1)}, bf16[1,144,864]{2,1,0:T(8,128)(2,1)S(1)}, u32[]{:S(2)}) copy-start(bf16[1,144,864]{2,1,0:T(8,128)(2,1)S(1)} %maximum_bitcast_fusion.2.refs_4_.refs_0_) | copy-start | bytes 746500
  16.4 0.7 copy-start.8
  16.4 0.7 copy-start.9
  16.4 0.8 copy-start.10
  17.2 7.7 %collective-permute-start.1 = (s32[1,16]{1,0:T(1,128)S(1)}, s32[1,16]{1,0:T(1,128)S(1)}, u32[]{:S(2)}, u32[]{:S(2)}) collective-permute-start(s32[1,16]{1,0:T(1,128)S(1)} %fusion.8), channel_id=1, source_target_pairs={{0,8},{1,9},{2,10},{3,11},{4,12},{5,13},{6,14},{7,15},{8,0},{9,1},... | collective-permute-start | bytes 200 | tf_op jit(solution)/shard_map/ppermute | solution.py:473
  17.3 14.8 %collective-permute-start.9 = (bf16[144,1152]{1,0:T(8,128)(2,1)S(1)}, bf16[144,1152]{1,0:T(8,128)(2,1)S(1)}, u32[]{:S(2)}, u32[]{:S(2)}) collective-permute-start(bf16[144,1152]{1,0:T(8,128)(2,1)S(1)} %copy-done.13), channel_id=1, source_target_pairs={{0,0},{1,1},{2,18},{3,19},{4,8},{5,9},{6,26},{7,27},{8,4},{9,5},{1... | collective-permute-start | bytes 995336 | tf_op jit(solution)/shard_map/ppermute | solution.py:495
  25.0 3.6 %collective-permute-start.2 = (s32[2,16]{1,0:T(2,128)S(1)}, s32[2,16]{1,0:T(2,128)S(1)}, u32[]{:S(2)}, u32[]{:S(2)}) collective-permute-start(s32[2,16]{1,0:T(2,128)S(1)} %pad_add_fusion), channel_id=1, source_target_pairs={{0,16},{1,17},{2,18},{3,19},{4,20},{5,21},{6,22},{7,23},{8,24},{9,... | collective-permute-start | bytes 392 | tf_op jit(solution)/shard_map/ppermute | solution.py:475
  25.1 11.9 %copy-start.5 = (bf16[1,2,64,1152]{3,2,1,0:T(8,128)(2,1)}, bf16[1,2,64,1152]{3,2,1,0:T(8,128)(2,1)S(1)}, u32[]{:S(2)}) copy-start(bf16[1,2,64,1152]{3,2,1,0:T(8,128)(2,1)S(1)} %collective-permute-done.3.refs_1_) | copy-start | bytes 884740
  25.1 11.9 %collective-permute-start.6 = (bf16[1,2,64,1152]{3,2,1,0:T(8,128)(2,1)S(1)}, bf16[1,2,64,1152]{3,2,1,0:T(8,128)(2,1)S(1)}, u32[]{:S(2)}, u32[]{:S(2)}) collective-permute-start(bf16[1,2,64,1152]{3,2,1,0:T(8,128)(2,1)S(1)} %collective-permute-done.3.refs_1_), channel_id=1, source_target_pairs={{0,16},{1,17},{2,18},{3,19},{4,20},{5,21},{6,22},{7,23},{8,24},{9,... | collective-permute-start | bytes 884744 | tf_op jit(solution)/shard_map/ppermute | solution.py:449
  29.3 10.0 %copy-start.2 = (bf16[2,2,64,1152]{3,2,1,0:T(8,128)(2,1)}, bf16[2,2,64,1152]{3,2,1,0:T(8,128)(2,1)S(1)}, u32[]{:S(2)}) copy-start(bf16[2,2,64,1152]{3,2,1,0:T(8,128)(2,1)S(1)} %pad_maximum_fusion.refs_0_) | copy-start | bytes 1769476
  29.3 25.1 %collective-permute-start.5 = (bf16[2,2,64,1152]{3,2,1,0:T(8,128)(2,1)S(1)}, bf16[2,2,64,1152]{3,2,1,0:T(8,128)(2,1)S(1)}, u32[]{:S(2)}, u32[]{:S(2)}) collective-permute-start(bf16[2,2,64,1152]{3,2,1,0:T(8,128)(2,1)S(1)} %pad_maximum_fusion.refs_0_), channel_id=1, source_target_pairs={{0,16},{1,17},{2,18},{3,19},{4,20},{5,21},{6,22},{7,23},{8,24},{9,... | collective-permute-start | bytes 1769480 | tf_op jit(solution)/shard_map/ppermute | solution.py:452
  32.1 5.0 %copy-start.14 = (bf16[144,1152]{1,0:T(8,128)(2,1)}, bf16[144,1152]{1,0:T(8,128)(2,1)S(1)}, u32[]{:S(2)}) copy-start(bf16[144,1152]{1,0:T(8,128)(2,1)S(1)} %collective-permute-done.9.refs_12_) | copy-start | bytes 995332
  32.1 13.0 %collective-permute-start.11 = (bf16[1,144,864]{2,1,0:T(8,128)(2,1)S(1)}, bf16[1,144,864]{2,1,0:T(8,128)(2,1)S(1)}, u32[]{:S(2)}, u32[]{:S(2)}) collective-permute-start(bf16[1,144,864]{2,1,0:T(8,128)(2,1)S(1)} %maximum_bitcast_fusion.2.refs_4_.refs_0_), channel_id=1, source_target_pairs={{0,4},{1,5},{2,6},{3,7},{4,0},{5,1},{6,2},{7,3},{8,12},{9,13},{10,... | collective-permute-start | bytes 746504 | tf_op jit(solution)/shard_map/ppermute | solution.py:500
  33.8 11.3 %collective-permute-start.10 = (bf16[1,144,864]{2,1,0:T(8,128)(2,1)S(1)}, bf16[1,144,864]{2,1,0:T(8,128)(2,1)S(1)}, u32[]{:S(2)}, u32[]{:S(2)}) collective-permute-start(bf16[1,144,864]{2,1,0:T(8,128)(2,1)S(1)} %maximum_bitcast_fusion.2.refs_4_.refs_0_), channel_id=1, source_target_pairs={{0,2},{1,3},{2,0},{3,1},{4,6},{5,7},{6,4},{7,5},{8,10},{9,11},{10,... | collective-permute-start | bytes 746504 | tf_op jit(solution)/shard_map/ppermute | solution.py:500
  37.1 8.1 %copy-start.3 = (bf16[2,2,64,1152]{3,2,1,0:T(8,128)(2,1)}, bf16[2,2,64,1152]{3,2,1,0:T(8,128)(2,1)S(1)}, u32[]{:S(2)}) copy-start(bf16[2,2,64,1152]{3,2,1,0:T(8,128)(2,1)S(1)} %pad_maximum_fusion.1.refs_2_) | copy-start | bytes 1769476
  37.1 17.4 %collective-permute-start.7 = (bf16[2,2,64,1152]{3,2,1,0:T(8,128)(2,1)S(1)}, bf16[2,2,64,1152]{3,2,1,0:T(8,128)(2,1)S(1)}, u32[]{:S(2)}, u32[]{:S(2)}) collective-permute-start(bf16[2,2,64,1152]{3,2,1,0:T(8,128)(2,1)S(1)} %pad_maximum_fusion.1.refs_2_), channel_id=1, source_target_pairs={{0,1},{1,0},{2,3},{3,2},{4,5},{5,4},{6,7},{7,6},{8,9},{9,8},{10,11... | collective-permute-start | bytes 1769480 | tf_op jit(solution)/shard_map/ppermute | solution.py:452
  39.3 7.0 %collective-permute-start.13 = (bf16[1,144,864]{2,1,0:T(8,128)(2,1)S(1)}, bf16[1,144,864]{2,1,0:T(8,128)(2,1)S(1)}, u32[]{:S(2)}, u32[]{:S(2)}) collective-permute-start(bf16[1,144,864]{2,1,0:T(8,128)(2,1)S(1)} %maximum_bitcast_fusion.2.refs_4_.refs_0_), channel_id=1, source_target_pairs={{0,8},{1,9},{2,10},{3,11},{4,12},{5,13},{6,14},{7,15},{8,0},{9,1},... | collective-permute-start | bytes 746504 | tf_op jit(solution)/shard_map/ppermute | solution.py:512
  45.0 9.4 %copy-start.6 = (bf16[1,144,864]{2,1,0:T(8,128)(2,1)}, bf16[1,144,864]{2,1,0:T(8,128)(2,1)S(1)}, u32[]{:S(2)}) copy-start(bf16[1,144,864]{2,1,0:T(8,128)(2,1)S(1)} %collective-permute-done.11.refs_6_.refs_2_) | copy-start | bytes 746500
  45.1 1.9 %collective-permute-start.15 = (bf16[144,1152]{1,0:T(8,128)(2,1)}, bf16[144,1152]{1,0:T(8,128)(2,1)S(1)}, u32[]{:S(2)}, u32[]{:S(2)}) collective-permute-start(bf16[144,1152]{1,0:T(8,128)(2,1)} %copy-done.14), channel_id=1, source_target_pairs={{0,8},{1,9},{2,10},{3,11},{4,12},{5,13},{6,14},{7,15},{8,0},{9,1},... | collective-permute-start | bytes 995336 | tf_op jit(solution)/shard_map/ppermute | solution.py:496
  45.1 0.7 copy-start.7
  45.8 1.6 %collective-permute-start.14 = (bf16[1,144,864]{2,1,0:T(8,128)(2,1)S(1)}, bf16[1,144,864]{2,1,0:T(8,128)(2,1)S(1)}, u32[]{:S(2)}, u32[]{:S(2)}) collective-permute-start(bf16[1,144,864]{2,1,0:T(8,128)(2,1)S(1)} %get-tuple-element.127), channel_id=1, source_target_pairs={{0,8},{1,9},{2,10},{3,11},{4,12},{5,13},{6,14},{7,15},{8,0},{9,1},... | collective-permute-start | bytes 746504 | tf_op jit(solution)/shard_map/ppermute | solution.py:512
  46.3 10.2 %copy-start.22 = (bf16[1,144,864]{2,1,0:T(8,128)(2,1)}, bf16[1,144,864]{2,1,0:T(8,128)(2,1)S(1)}, u32[]{:S(2)}) copy-start(bf16[1,144,864]{2,1,0:T(8,128)(2,1)S(1)} %collective-permute-done.13.refs_8_.refs_4_) | copy-start | bytes 746500
  46.3 8.2 %collective-permute-start.12 = (bf16[1,144,864]{2,1,0:T(8,128)(2,1)S(1)}, bf16[1,144,864]{2,1,0:T(8,128)(2,1)S(1)}, u32[]{:S(2)}, u32[]{:S(2)}) collective-permute-start(bf16[1,144,864]{2,1,0:T(8,128)(2,1)S(1)} %get-tuple-element.128), channel_id=1, source_target_pairs={{0,2},{1,3},{2,0},{3,1},{4,6},{5,7},{6,4},{7,5},{8,10},{9,11},{10,... | collective-permute-start | bytes 746504 | tf_op jit(solution)/shard_map/ppermute | solution.py:504
  46.9 9.5 %copy-start.15 = (bf16[144,1152]{1,0:T(8,128)(2,1)}, bf16[144,1152]{1,0:T(8,128)(2,1)S(1)}, u32[]{:S(2)}) copy-start(bf16[144,1152]{1,0:T(8,128)(2,1)S(1)} %collective-permute-done.15.refs_13_) | copy-start | bytes 995332
  47.4 9.0 %copy-start.23 = (bf16[1,144,864]{2,1,0:T(8,128)(2,1)}, bf16[1,144,864]{2,1,0:T(8,128)(2,1)S(1)}, u32[]{:S(2)}) copy-start(bf16[1,144,864]{2,1,0:T(8,128)(2,1)S(1)} %collective-permute-done.14.refs_9_.refs_5_) | copy-start | bytes 746500
  54.5 2.0 %copy-start.24 = (bf16[1,144,864]{2,1,0:T(8,128)(2,1)}, bf16[1,144,864]{2,1,0:T(8,128)(2,1)S(1)}, u32[]{:S(2)}) copy-start(bf16[1,144,864]{2,1,0:T(8,128)(2,1)S(1)} %collective-permute-done.12.refs_7_.refs_3_) | copy-start | bytes 746500
  54.5 2.0 %copy-start.11 = (bf16[2,2,64,1152]{3,2,1,0:T(8,128)(2,1)}, bf16[2,2,64,1152]{3,2,1,0:T(8,128)(2,1)S(1)}, u32[]{:S(2)}) copy-start(bf16[2,2,64,1152]{3,2,1,0:T(8,128)(2,1)S(1)} %collective-permute-done.5.refs_1_) | copy-start | bytes 1769476
  54.5 2.0 %copy-start.12 = (bf16[2,2,64,1152]{3,2,1,0:T(8,128)(2,1)}, bf16[2,2,64,1152]{3,2,1,0:T(8,128)(2,1)S(1)}, u32[]{:S(2)}) copy-start(bf16[2,2,64,1152]{3,2,1,0:T(8,128)(2,1)S(1)} %collective-permute-done.7.refs_3_) | copy-start | bytes 1769476
  54.5 1.6 %collective-permute-start.16 = (bf16[1,144,864]{2,1,0:T(8,128)(2,1)S(1)}, bf16[1,144,864]{2,1,0:T(8,128)(2,1)S(1)}, u32[]{:S(2)}, u32[]{:S(2)}) collective-permute-start(bf16[1,144,864]{2,1,0:T(8,128)(2,1)S(1)} %collective-permute-done.11.refs_6_.refs_2_), channel_id=1, source_target_pairs={{0,8},{1,9},{2,10},{3,11},{4,12},{5,13},{6,14},{7,15},{8,0},{9,1},... | collective-permute-start | bytes 746504 | tf_op jit(solution)/shard_map/ppermute | solution.py:516
  54.6 1.9 %collective-permute-start.17 = (bf16[1,144,864]{2,1,0:T(8,128)(2,1)S(1)}, bf16[1,144,864]{2,1,0:T(8,128)(2,1)S(1)}, u32[]{:S(2)}, u32[]{:S(2)}) collective-permute-start(bf16[1,144,864]{2,1,0:T(8,128)(2,1)S(1)} %collective-permute-done.12.refs_7_.refs_3_), channel_id=1, source_target_pairs={{0,8},{1,9},{2,10},{3,11},{4,12},{5,13},{6,14},{7,15},{8,0},{9,1},... | collective-permute-start | bytes 746504 | tf_op jit(solution)/shard_map/ppermute | solution.py:516
  56.1 0.7 copy-start.25
  56.8 0.7 copy-start.26
  69.5 3.7 %collective-permute-start.18 = (f32[4,48,864]{2,1,0:T(8,128)}, f32[4,48,864]{2,1,0:T(8,128)S(1)}, u32[]{:S(2)}, u32[]{:S(2)}) collective-permute-start(f32[4,48,864]{2,1,0:T(8,128)} %get-tuple-element.91), channel_id=1, source_target_pairs={{0,8},{1,9},{2,10},{3,11},{4,12},{5,13},{6,14},{7,15},{8,0},{9,1},... | collective-permute-start | bytes 1990664 | tf_op jit(solution)/shard_map/ppermute | solution.py:558
  69.7 15.3 %collective-permute-start.20 = (bf16[2,64,1152]{2,1,0:T(8,128)(2,1)}, bf16[2,64,1152]{2,1,0:T(8,128)(2,1)S(1)}, u32[]{:S(2)}, u32[]{:S(2)}) collective-permute-start(bf16[2,64,1152]{2,1,0:T(8,128)(2,1)} %get-tuple-element.98), channel_id=1, source_target_pairs={{0,1},{1,0},{2,3},{3,2},{4,5},{5,4},{6,7},{7,6},{8,9},{9,8},{10,11... | collective-permute-start | bytes 884744 | tf_op jit(solution)/shard_map/ppermute | solution.py:455
  71.1 17.4 %collective-permute-start.21 = (bf16[2,64,1152]{2,1,0:T(8,128)(2,1)}, bf16[2,64,1152]{2,1,0:T(8,128)(2,1)S(1)}, u32[]{:S(2)}, u32[]{:S(2)}) collective-permute-start(bf16[2,64,1152]{2,1,0:T(8,128)(2,1)} %get-tuple-element.100), channel_id=1, source_target_pairs={{0,16},{1,17},{2,18},{3,19},{4,20},{5,21},{6,22},{7,23},{8,24},{9,... | collective-permute-start | bytes 884744 | tf_op jit(solution)/shard_map/ppermute | solution.py:455
  73.1 15.5 %collective-permute-start.22 = (bf16[2,64,1152]{2,1,0:T(8,128)(2,1)}, bf16[2,64,1152]{2,1,0:T(8,128)(2,1)S(1)}, u32[]{:S(2)}, u32[]{:S(2)}) collective-permute-start(bf16[2,64,1152]{2,1,0:T(8,128)(2,1)} %get-tuple-element.101), channel_id=1, source_target_pairs={{0,17},{1,16},{2,19},{3,18},{4,21},{5,20},{6,23},{7,22},{8,25},{9,... | collective-permute-start | bytes 884744 | tf_op jit(solution)/shard_map/ppermute | solution.py:455
  74.2 10.8 %collective-permute-start.19 = (f32[2,48,864]{2,1,0:T(8,128)S(1)}, f32[2,48,864]{2,1,0:T(8,128)S(1)}, u32[]{:S(2)}, u32[]{:S(2)}) collective-permute-start(f32[2,48,864]{2,1,0:T(8,128)S(1)} %slice_add_fusion.1), channel_id=1, source_target_pairs={{0,2},{1,3},{2,0},{3,1},{4,6},{5,7},{6,4},{7,5},{8,10},{9,11},{10,... | collective-permute-start | bytes 995336 | tf_op jit(solution)/shard_map/ppermute | solution.py:563
  85.0 3.6 %copy-start.16 = (bf16[2,64,1152]{2,1,0:T(8,128)(2,1)}, bf16[2,64,1152]{2,1,0:T(8,128)(2,1)S(1)}, u32[]{:S(2)}) copy-start(bf16[2,64,1152]{2,1,0:T(8,128)(2,1)S(1)} %collective-permute-done.20.refs_3_) | copy-start | bytes 884740
  85.0 17.5 %collective-permute-start.25 = (bf16[2,64,1152]{2,1,0:T(8,128)(2,1)}, bf16[2,64,1152]{2,1,0:T(8,128)(2,1)S(1)}, u32[]{:S(2)}, u32[]{:S(2)}) collective-permute-start(bf16[2,64,1152]{2,1,0:T(8,128)(2,1)} %get-tuple-element.103), channel_id=1, source_target_pairs={{0,1},{1,0},{2,3},{3,2},{4,5},{5,4},{6,7},{7,6},{8,9},{9,8},{10,11... | collective-permute-start | bytes 884744 | tf_op jit(solution)/shard_map/ppermute | solution.py:455
  86.5 16.0 %collective-permute-start.26 = (bf16[2,64,1152]{2,1,0:T(8,128)(2,1)}, bf16[2,64,1152]{2,1,0:T(8,128)(2,1)S(1)}, u32[]{:S(2)}, u32[]{:S(2)}) collective-permute-start(bf16[2,64,1152]{2,1,0:T(8,128)(2,1)} %get-tuple-element.104), channel_id=1, source_target_pairs={{0,16},{1,17},{2,18},{3,19},{4,20},{5,21},{6,22},{7,23},{8,24},{9,... | collective-permute-start | bytes 884744 | tf_op jit(solution)/shard_map/ppermute | solution.py:455
  88.5 14.0 %collective-permute-start.27 = (bf16[2,64,1152]{2,1,0:T(8,128)(2,1)}, bf16[2,64,1152]{2,1,0:T(8,128)(2,1)S(1)}, u32[]{:S(2)}, u32[]{:S(2)}) collective-permute-start(bf16[2,64,1152]{2,1,0:T(8,128)(2,1)} %get-tuple-element.105), channel_id=1, source_target_pairs={{0,17},{1,16},{2,19},{3,18},{4,21},{5,20},{6,23},{7,22},{8,25},{9,... | collective-permute-start | bytes 884744 | tf_op jit(solution)/shard_map/ppermute | solution.py:455
  88.5 0.7 copy-start.17
  88.5 0.8 copy-start.18
  89.4 13.0 %copy-start.1 = (f32[4,48,864]{2,1,0:T(8,128)S(1)}, f32[4,48,864]{2,1,0:T(8,128)}, u32[]{:S(2)}) copy-start(f32[4,48,864]{2,1,0:T(8,128)} %get-tuple-element.90) | copy-start | bytes 1990660
  92.6 27.0 %collective-permute-start.23 = (bf16[64,1152]{1,0:T(8,128)(2,1)}, bf16[64,1152]{1,0:T(8,128)(2,1)S(1)}, u32[]{:S(2)}, u32[]{:S(2)}) collective-permute-start(bf16[64,1152]{1,0:T(8,128)(2,1)} %get-tuple-element.110), channel_id=1, source_target_pairs={{0,0},{1,1},{16,2},{17,3},{2,4},{3,5},{18,6},{19,7},{20,8},{21,9},... | collective-permute-start | bytes 442376 | tf_op jit(solution)/shard_map/ppermute | solution.py:442
  96.7 22.8 %collective-permute-start.24 = (bf16[64,1152]{1,0:T(8,128)(2,1)}, bf16[64,1152]{1,0:T(8,128)(2,1)S(1)}, u32[]{:S(2)}, u32[]{:S(2)}) collective-permute-start(bf16[64,1152]{1,0:T(8,128)(2,1)} %get-tuple-element.111), channel_id=1, source_target_pairs={{2,0},{3,1},{18,2},{19,3},{0,4},{1,5},{16,6},{17,7},{22,8},{23,9},... | collective-permute-start | bytes 442376 | tf_op jit(solution)/shard_map/ppermute | solution.py:442
  102.4 0.7 copy-start.19
  102.5 14.5 %collective-permute-start.30 = (f32[1,48,864]{2,1,0:T(8,128)S(1)}, f32[1,48,864]{2,1,0:T(8,128)S(1)}, u32[]{:S(2)}, u32[]{:S(2)}) collective-permute-start(f32[1,48,864]{2,1,0:T(8,128)S(1)} %slice.40), channel_id=1, source_target_pairs={{0,4},{1,5},{2,6},{3,7},{4,0},{5,1},{6,2},{7,3},{8,12},{9,13},{10,... | collective-permute-start | bytes 497672 | tf_op jit(solution)/shard_map/ppermute | solution.py:606
  102.5 0.7 copy-start.20
  103.3 0.7 copy-start.21
  107.4 12.2 %collective-permute-start.28 = (bf16[64,1152]{1,0:T(8,128)(2,1)}, bf16[64,1152]{1,0:T(8,128)(2,1)S(1)}, u32[]{:S(2)}, u32[]{:S(2)}) collective-permute-start(bf16[64,1152]{1,0:T(8,128)(2,1)} %get-tuple-element.116), channel_id=1, source_target_pairs={{0,0},{1,1},{16,2},{17,3},{2,4},{3,5},{18,6},{19,7},{20,8},{21,9},... | collective-permute-start | bytes 442376 | tf_op jit(solution)/shard_map/ppermute | solution.py:442
  111.8 10.6 %collective-permute-start.29 = (bf16[64,1152]{1,0:T(8,128)(2,1)}, bf16[64,1152]{1,0:T(8,128)(2,1)S(1)}, u32[]{:S(2)}, u32[]{:S(2)}) collective-permute-start(bf16[64,1152]{1,0:T(8,128)(2,1)} %get-tuple-element.117), channel_id=1, source_target_pairs={{2,0},{3,1},{18,2},{19,3},{0,4},{1,5},{16,6},{17,7},{22,8},{23,9},... | collective-permute-start | bytes 442376 | tf_op jit(solution)/shard_map/ppermute | solution.py:442
  117.0 11.9 %collective-permute-start.31 = (f32[48,864]{1,0:T(8,128)S(1)}, f32[48,864]{1,0:T(8,128)S(1)}, u32[]{:S(2)}, u32[]{:S(2)}) collective-permute-start(f32[48,864]{1,0:T(8,128)S(1)} %bitcast.28), channel_id=1, source_target_pairs={{0,0},{1,1},{2,8},{3,9},{4,16},{5,17},{6,24},{7,25},{8,4},{9,5},{1... | collective-permute-start | bytes 497672 | tf_op jit(solution)/shard_map/ppermute | solution.py:608
